TPU v7x, 32 devices: a whole 2x2x4 slice. The times are simulated.
32 devices in a mesh: rep: 4 (over y, core), dom: 8 (over z, x).
Axes of the slice: x: 2, y: 2, z: 4, core: 2. Of those that a mesh axis runs over, the one named last changes fastest.
Arguments:
- features: bfloat16 [32768, 768], P(('rep', 'dom')), may hold values from -6 to 6
- cotangent: bfloat16 [32768, 1024], P(('rep', 'dom')), may hold values from -0.032958984 to 0.032958984
- w_self: bfloat16 [768, 1024], P('dom'), may hold values from -0.21875 to 0.21875
- w_neigh: bfloat16 [768, 1024], P('dom'), may hold values from -0.21875 to 0.21875
- tile_vals: bfloat16 [1024, 128, 128], P(('rep', 'dom')), may hold values from 0 to 0.088378906
- tile_src: int32 [1024], P(('rep', 'dom')), may hold values from 0 to 7
- tile_peer: int32 [1024], P(('rep', 'dom')), may hold values from 0 to 7
- in_block: int32 [256], P(('rep', 'dom')), may hold values from 0 to 7
Outputs:
- grad_self: float32 [768, 1024], P('dom')
- grad_neigh: float32 [768, 1024], P('dom')
Inputs may be any that keep to these rules, and one draw needn't show every extreme that they name: `in_block`: all tiles that one partition sends to one receiving partition land in the same receiver block.
All inputs are finite; a program needn't handle non-finite values.
Results may differ from a plain program's by a relative error of at most 0.023.
Values may be sent and summed in bfloat16 or wider, within the bound.
No kernel may reach another device: no remote copies, remote signals or barrier semaphores. Data moves between devices by JAX's collectives and lax.ppermute only.
A program may use at most 128 MiB of HBM per device.

v0:
```python
import jax
import jax.numpy as jnp
from jax import lax
from jax.sharding import PartitionSpec as P


def gelu_tanh(value):
    return jax.nn.gelu(value, approximate=True)


def add_product(left, total, piece):
    return total + jnp.dot(left, piece, preferred_element_type=jnp.float32)


def shards(features, cotangent, w_self, w_neigh, tile_vals, tile_src, tile_peer, in_block):
    dom_size = lax.axis_size("dom")
    block = tile_vals.shape[1]
    width = features.shape[1]
    hidden = w_self.shape[1]
    block_count = features.shape[0] // block
    blocks = features.reshape(block_count, block, width)
    picked = blocks[tile_src]
    product = jnp.einsum("tij,tjf->tif", tile_vals, picked, preferred_element_type=jnp.float32)
    to_peer = (tile_peer[:, None] == jnp.arange(dom_size, dtype=jnp.int32)[None, :]).astype(
        jnp.float32
    )
    slots = jnp.einsum("tp,tif->pif", to_peer, product, precision=lax.Precision.HIGH).astype(
        jnp.bfloat16
    )
    empty = jnp.zeros((features.shape[0], hidden), jnp.float32)
    into_block = (in_block[:, None] == jnp.arange(block_count, dtype=jnp.int32)[None, :]).astype(
        jnp.bfloat16
    )
    aggregate = jnp.einsum(
        "sk,sif->kif",
        into_block,
        lax.all_to_all(slots, "dom", split_axis=0, concat_axis=0, tiled=True),
        preferred_element_type=jnp.float32,
    )
    aggregate = aggregate.reshape(features.shape[0], width).astype(jnp.bfloat16)
    total = empty
    total = add_product(features, total, lax.all_gather(w_self, "dom", axis=0, tiled=True))
    preact = add_product(aggregate, total, lax.all_gather(w_neigh, "dom", axis=0, tiled=True))
    _, pull = jax.vjp(gelu_tanh, preact)
    grad_pre = pull(cotangent.astype(jnp.float32))[0].astype(jnp.bfloat16)
    contract = (((0,), (0,)), ((), ()))
    self_term = lax.dot_general(features, grad_pre, contract, preferred_element_type=jnp.float32)
    neigh_term = lax.dot_general(aggregate, grad_pre, contract, preferred_element_type=jnp.float32)
    shares = lax.psum_scatter(
        jnp.concatenate([self_term, neigh_term], axis=1).astype(jnp.bfloat16),
        "dom",
        scatter_dimension=0,
        tiled=True,
    )
    totals = lax.psum(shares, "rep").astype(jnp.float32)
    return (totals[:, :hidden], totals[:, hidden:])


def solution(mesh):
    in_specs = (
        P(("rep", "dom"), None),
        P(("rep", "dom"), None),
        P("dom", None),
        P("dom", None),
        P(("rep", "dom"), None, None),
        P(("rep", "dom")),
        P(("rep", "dom")),
        P(("rep", "dom")),
    )
    out_specs = (P("dom", None), P("dom", None))
    return jax.shard_map(shards, mesh=mesh, in_specs=in_specs, out_specs=out_specs, check_vma=False)
```

profile of v0, /device:TPU:0, one launch (start us, length us, event | category | flops | bytes accessed | tf_op | source)
XLA Modules:
  0.0 254.5 jit_solution(12654657185070146056)
XLA Ops:
  7.2 0.0 all-gather.3.cloned.1.call-start
  7.2 0.7 all-gather.3.cloned.1.call-update
  7.9 0.7 compare_select_fusion
  8.6 3.5 %gather_fusion = bf16[32,128,768]{2,1,0:T(8,128)(2,1)} fusion(bf16[8,128,768]{2,1,0:T(8,128)(2,1)S(1)} %bitcast.24, s32[1024]{0:T(1024)S(1)} %pad_clamp_fusion), kind=kCustom, calls=%fused_computation | custom fusion | bytes 12583040 | tf_op jit(solution)/shard_map/gather | solution.py:22
  12.1 9.2 %convolution_bitcast_fusion = f32[32,128,768]{1,2,0:T(8,128)} fusion(bf16[32,128,768]{2,1,0:T(8,128)(2,1)} %gather_fusion, bf16[32,128,128]{2,1,0:T(8,128)(2,1)S(1)} %copy-done.1), kind=kOutput, calls=%fused_computation.5 | convolution fusion | flops 805306368 | bytes 19922944 | tf_op jit(solution)/shard_map/tij,tjf->tif/dot_general | solution.py:23
  21.3 13.0 %copy.25 = f32[32,128,768]{2,0,1:T(8,128)} copy(f32[32,128,768]{1,2,0:T(8,128)} %convolution_bitcast_fusion) | data formatting | bytes 25165824 | tf_op jit(solution)/shard_map/tij,tjf->tif/dot_general | solution.py:23
  34.3 6.8 %convolution_convert_fusion = bf16[8,128,768]{2,0,1:T(8,128)(2,1)S(1)} fusion(f32[32,128,768]{2,0,1:T(8,128)} %copy.25, s32[32]{0:T(128)S(1)} %copy-done.2), kind=kOutput, calls=%fused_computation.17 | convolution fusion | flops 151781632 | bytes 14155904 | tf_op jit(solution)/shard_map/tp,tif->pif/dot_general | solution.py:27
  41.1 1.4 copy.26
  42.6 7.5 %all-to-all-start = ((bf16[8,128,768]{2,1,0:T(8,128)(2,1)}), bf16[8,128,768]{2,1,0:T(8,128)(2,1)S(1)}, u32[]{:S(2)}, u32[]{:S(2)}) async-start(bf16[8,128,768]{2,1,0:T(8,128)(2,1)} %copy.26), calls=%async_computation | async-start | bytes 3145728 | tf_op jit(solution)/shard_map/all_to_all | solution.py:37
  50.0 0.0 all-gather.5.cloned.1.call-start
  50.1 0.7 all-gather.5.cloned.1.call-update
  50.8 0.2 reduce-scatter.4.cloned.1.call-start
  51.0 46.4 %all-to-all-done = bf16[8,128,768]{2,1,0:T(8,128)(2,1)S(1)} async-done(((bf16[8,128,768]{2,1,0:T(8,128)(2,1)}), bf16[8,128,768]{2,1,0:T(8,128)(2,1)S(1)}, u32[]{:S(2)}, u32[]{:S(2)}) %all-to-all-start) | async-done | bytes 1572896 | tf_op jit(solution)/shard_map/all_to_all | solution.py:37
  97.4 1.0 convolution_convert_fusion.3
  98.4 0.3 copy.28
  98.7 0.0 all-gather.3.cloned.1.call-done
  98.7 5.1 %fusion.19 = f32[1024,1024]{1,0:T(8,128)} fusion(bf16[1024,768]{1,0:T(8,128)(2,1)S(1)} %copy-done, bf16[768,1024]{1,0:T(8,128)(2,1)} %all-gather.3.cloned.1.call-done), kind=kOutput, calls=%fused_computation.32 | convolution fusion | flops 1610612736 | bytes 7340032 | tf_op jit(solution)/shard_map/dot_general | solution.py:12
  103.9 15.5 %all-gather.5.cloned.1.call-done = bf16[768,1024]{1,0:T(8,128)(2,1)} async-done(((bf16[96,1024]{1,0:T(8,128)(2,1)}), bf16[768,1024]{1,0:T(8,128)(2,1)}) %all-gather.5.cloned.1.call-update) | async-done | bytes 1572880 | tf_op jit(solution)/shard_map/all_gather | solution.py:43
  119.4 7.1 %fusion.2 = bf16[1024,1024]{1,0:T(8,128)(2,1)S(1)} fusion(bf16[1024,1024]{1,0:T(8,128)(2,1)} %param.9, f32[1024,1024]{1,0:T(8,128)} %fusion.19, bf16[1024,768]{1,0:T(8,128)(2,1)S(1)} %bitcast.25, bf16[768,1024]{1,0:T(8,128)(2,1)} %all-gather.5.cloned.1.call-done), kind=kOutput, calls=%fused_computation.8 | convolution fusion | flops 1633681408 | bytes 11534336 | tf_op jit(solution)/shard_map/dot_general | solution.py:12
  126.5 1.8 convolution_convert_fusion.1
  128.3 1.9 fusion.11
  130.2 1.9 pad_maximum_fusion
  132.1 4.8 %copy.34 = bf16[768,2048]{1,0:T(8,128)(2,1)} copy(bf16[768,2048]{0,1:T(8,128)(2,1)} %pad_maximum_fusion) | data formatting | bytes 6291456
  136.8 0.0 reduce-scatter.4.cloned.1.call-update
  136.9 0.0 all-reduce.2.cloned.1.call-start
  136.9 73.5 %reduce-scatter.4.cloned.1.call-done = bf16[96,2048]{1,0:T(8,128)(2,1)} async-done(((bf16[768,2048]{1,0:T(8,128)(2,1)}), bf16[96,2048]{1,0:T(8,128)(2,1)}) %reduce-scatter.4.cloned.1.call-update) | async-done | bytes 393232
  210.4 2.0 copy.35
  212.4 0.0 all-reduce.2.cloned.1.call-update
  212.5 32.5 %all-reduce.2.cloned.1.call-done = bf16[96,2048]{0,1:T(8,128)(2,1)} async-done(((bf16[96,2048]{0,1:T(8,128)(2,1)}), bf16[96,2048]{0,1:T(8,128)(2,1)}) %all-reduce.2.cloned.1.call-update) | async-done | bytes 393232 | tf_op jit(solution)/shard_map/psum | solution.py:55
  244.9 1.1 fusion.18
  246.0 0.9 copy.30
  247.0 0.9 copy.31
  (9 shorter events, 0.0 us)
Async XLA Ops:
  7.2 1.4 copy-start
  7.2 91.5 %all-gather.3.cloned.1.call-start = ((), (), s32[]{:S(2)}) async-start(), calls=%async_computation.2 | async-start | bytes 1769472 | tf_op jit(solution)/shard_map/all_gather | solution.py:42
  8.6 3.5 %copy-start.1 = (bf16[32,128,128]{2,1,0:T(8,128)(2,1)S(1)}, bf16[32,128,128]{2,1,0:T(8,128)(2,1)}, u32[]{:S(2)}) copy-start(bf16[32,128,128]{2,1,0:T(8,128)(2,1)} %param.12) | copy-start | bytes 3145732
  21.3 13.0 %copy-start.2 = (s32[32]{0:T(128)S(1)}, s32[32]{0:T(128)}, u32[]{:S(2)}) copy-start(s32[32]{0:T(128)} %param.14) | copy-start | bytes 388
  41.1 56.3 %copy-start.3 = (s32[8]{0:T(128)S(1)}, s32[8]{0:T(128)}, u32[]{:S(2)}) copy-start(s32[8]{0:T(128)} %param.15) | copy-start | bytes 100
  42.6 54.8 %all-to-all-start = ((bf16[8,128,768]{2,1,0:T(8,128)(2,1)}), bf16[8,128,768]{2,1,0:T(8,128)(2,1)S(1)}, u32[]{:S(2)}, u32[]{:S(2)}) async-start(bf16[8,128,768]{2,1,0:T(8,128)(2,1)} %copy.26), calls=%async_computation | async-start | bytes 3145728 | tf_op jit(solution)/shard_map/all_to_all | solution.py:37
  50.0 69.4 %all-gather.5.cloned.1.call-start = ((), (), s32[]{:S(2)}) async-start(), calls=%async_computation.3 | async-start | bytes 1769472 | tf_op jit(solution)/shard_map/all_gather | solution.py:43
  50.8 159.7 %reduce-scatter.4.cloned.1.call-start = ((), (), s32[]{:S(2)}) async-start(), calls=%async_computation.5 | async-start | bytes 3538944
  136.9 108.1 %all-reduce.2.cloned.1.call-start = ((), (), s32[]{:S(2)}) async-start(), calls=%async_computation.4 | async-start | bytes 1048576 | tf_op jit(solution)/shard_map/psum | solution.py:55
Sparse Core Ops, SparseCore 0:
  10.2 49.0 all-gather.2
  61.5 57.9 all-gather.4
  137.0 73.3 reduce-scatter.3
  212.6 32.2 all-reduce.1
where the time goes:
time: 255 us; the launch traced here: 254 us
  waiting for transfers between devices  169 us (66%)
  matrix products  32.9 us (13%)
  local copies, waits for them, and re-layouts  28 us (11%)
  between operations  13.8 us (5%)
  starting transfers between devices  7.79 us (3%)
    unnamed x5, waiting for transfers between devices  74.9 us
    all_to_all x1, waiting for transfers between devices, shards(): lax.all_to_all(slots, 'dom', split_axis=0, concat_axis=0, tiled=True)  46.4 us
    psum x1, waiting for transfers between devices, shards(): totals = lax.psum(shares, 'rep').astype(jnp.float32)  32.5 us
    all_gather x1, waiting for transfers between devices, shards(): lax.all_gather(w_neigh, 'dom', axis=0, tiled=True)  15.5 us
    dot_general x1, local copies, waits for them, and re-layouts, shards(): jnp.einsum('tij,tjf->tif', tile_vals, picked, preferred_element_type=jnp....  13 us
    dot_general x2, matrix products, add_product(): return total + jnp.dot(left, piece, preferred_element_type=jnp.float32)  12.2 us
    dot_general x1, matrix products, shards(): jnp.einsum('tij,tjf->tif', tile_vals, picked, preferred_element_type=jnp....  9.17 us
    unnamed x12, local copies, waits for them, and re-layouts  8.68 us
  transfers between devices with their start and end apart: 5, of which 4 were waited for; matrix products, arithmetic and copies ran while one was open for 16% of the time, Pallas kernels for 0%

commit v1 on v0

v1 whole, which is shorter than its diff:
```python
import functools

import jax
import jax.numpy as jnp
from jax import lax
from jax.experimental import pallas as pl
from jax.experimental.pallas import tpu as pltpu
from jax.sharding import PartitionSpec as P

F32 = jnp.float32
BF16 = jnp.bfloat16
SCALE = 0.7978845608
CUBIC = 0.044715
MIB = 1 << 20
SMEM = pl.BlockSpec(memory_space=pltpu.SMEM)
VMEM = pl.BlockSpec(memory_space=pltpu.VMEM)


def swap(value, axis, step):
    size = lax.axis_size(axis)
    return lax.ppermute(value, axis, [(index, index ^ step) for index in range(size)])


def slots_kernel(me_ref, src_ref, peer_ref, tiles_ref, features_ref, *refs):
    out_refs, dense = refs[:-1], refs[-1]
    count, block, _ = tiles_ref.shape
    dense[...] = jnp.zeros_like(dense)
    me = me_ref[0]

    def place(tile, carry):
        row = pl.multiple_of((peer_ref[tile] ^ me) * block, block)
        column = pl.multiple_of(src_ref[tile] * block, block)
        at = (pl.ds(row, block), pl.ds(column, block))
        dense[at] = dense[at] + tiles_ref[tile].astype(F32)
        return carry

    lax.fori_loop(0, count, place, 0)
    group = 4
    for first in range(0, len(out_refs), group):
        rows = dense[first * block : (first + group) * block, :].astype(BF16)
        product = jnp.dot(rows, features_ref[...], preferred_element_type=F32).astype(BF16)
        for offset in range(group):
            out_refs[first + offset][...] = product[offset * block : (offset + 1) * block, :]


def self_kernel(core_ref, features_ref, mine_ref, other_ref, out_ref):
    rows = features_ref.shape[0]
    chunk = 256

    def product(weight_ref):
        def body():
            for first in range(0, rows, chunk):
                at = slice(first, first + chunk)
                out_ref[at, :] = jnp.dot(features_ref[at, :], weight_ref[...], preferred_element_type=F32)

        return body

    pl.when(core_ref[0] == 0)(product(mine_ref))
    pl.when(core_ref[0] != 0)(product(other_ref))


def layer_kernel(me_ref, core_ref, into_ref, cotangent_ref, total_ref, mine_ref, other_ref, *refs):
    slot_refs, (aggregate_ref, grad_ref, summed) = refs[:-3], refs[-3:]
    block = slot_refs[0].shape[0]
    rows = aggregate_ref.shape[0]
    me = me_ref[0]
    summed[...] = jnp.zeros_like(summed)
    for step, slot_ref in enumerate(slot_refs):
        at = pl.ds(pl.multiple_of(into_ref[me ^ step] * block, block), block)
        summed[at, :] = summed[at, :] + slot_ref[...].astype(F32)
    aggregate_ref[...] = summed[...].astype(BF16)
    chunk = 256

    def product(weight_ref):
        def body():
            for first in range(0, rows, chunk):
                at = slice(first, first + chunk)
                value = total_ref[at, :] + jnp.dot(
                    aggregate_ref[at, :], weight_ref[...], preferred_element_type=F32
                )
                square = value * value
                bend = jnp.tanh(SCALE * value * (1.0 + CUBIC * square))
                slope = 0.5 * (1.0 + bend) + (0.5 * SCALE) * value * (1.0 - bend * bend) * (
                    1.0 + 3.0 * CUBIC * square
                )
                grad_ref[at, :] = (cotangent_ref[at, :].astype(F32) * slope).astype(BF16)

        return body

    pl.when(core_ref[0] == 0)(product(other_ref))
    pl.when(core_ref[0] != 0)(product(mine_ref))


def term_kernel(use_ref, features_ref, aggregate_ref, grad_ref, out_ref):
    contract = (((0,), (0,)), ((), ()))

    def product(left_ref):
        def body():
            out_ref[...] = lax.dot_general(
                left_ref[...], grad_ref[...], contract, preferred_element_type=F32
            ).astype(BF16)

        return body

    pl.when(use_ref[0] == 0)(product(features_ref))
    pl.when(use_ref[0] != 0)(product(aggregate_ref))


def call(kernel, outs, places, scratch=(), flops=0, moved=0, vmem=48):
    return pl.pallas_call(
        kernel,
        out_shape=outs,
        in_specs=places,
        out_specs=jax.tree.map(lambda _: VMEM, outs),
        scratch_shapes=list(scratch),
        compiler_params=pltpu.CompilerParams(vmem_limit_bytes=vmem * MIB),
        cost_estimate=pl.CostEstimate(flops=flops, bytes_accessed=moved, transcendentals=0),
    )


def gather_weights(w_self, w_neigh, core, high):
    dom_size = lax.axis_size("dom")
    parts = lax.axis_size("rep") // 2
    hidden = w_self.shape[1]
    share = hidden // parts
    own = jnp.where(core == 0, w_self, w_neigh)
    held = lax.dynamic_slice_in_dim(own, high * share, share, 1)[None]
    step = dom_size // 2
    me = lax.axis_index("dom")
    while step:
        other = swap(held, "dom", step)
        upper = (me & step) != 0
        held = jnp.stack([jnp.where(upper, other, held), jnp.where(upper, held, other)], axis=1)
        held = held.reshape((-1,) + held.shape[2:])
        step //= 2
    held = held.reshape(-1, share)
    step = 1
    while step < parts:
        other = swap(held, "rep", 2 * step)
        upper = (high & step) != 0
        held = jnp.concatenate([jnp.where(upper, other, held), jnp.where(upper, held, other)], axis=1)
        step *= 2
    return held, swap(held, "rep", 1)


def added(left, right):
    return (left.astype(F32) + right.astype(F32)).astype(BF16)


def half(value, axis, which):
    size = value.shape[axis] // 2
    return lax.dynamic_slice_in_dim(value, which * size, size, axis)


def reduce_high(value, high):
    parts = lax.axis_size("rep") // 2
    step = parts // 2
    while step:
        upper = (high // step) % 2
        value = added(half(value, 2, upper), swap(half(value, 2, 1 - upper), "rep", 2 * step))
        step //= 2
    return value


def reduce_low(value, low):
    value = value.reshape(value.shape[0] // 2, 2, *value.shape[1:])
    sent = lax.dynamic_index_in_dim(value, 1 - low, 1, keepdims=False)
    kept = lax.dynamic_index_in_dim(value, low, 1, keepdims=False)
    return added(kept, swap(sent, "dom", 1))


def shards(features, cotangent, w_self, w_neigh, tile_vals, tile_src, tile_peer, in_block):
    dom_size = lax.axis_size("dom")
    rows, width = features.shape
    hidden = w_self.shape[1]
    block = tile_vals.shape[1]
    me = lax.axis_index("dom")
    rep = lax.axis_index("rep")
    core, high = rep % 2, rep // 2
    low, place = me % 2, me // 2
    me_arg = me.astype(jnp.int32).reshape(1)
    core_arg = core.astype(jnp.int32).reshape(1)

    mine, other = gather_weights(w_self, w_neigh, core, high)
    slots = call(
        slots_kernel,
        [jax.ShapeDtypeStruct((block, width), BF16)] * dom_size,
        [SMEM, SMEM, SMEM, VMEM, VMEM],
        [pltpu.VMEM((dom_size * block, rows), F32)],
        flops=2 * dom_size * block * rows * width,
        moved=tile_vals.size * 2 + rows * width * 4,
    )(me_arg, tile_src, tile_peer, tile_vals, features)
    received = [slots[0]] + [swap(slots[step], "dom", step) for step in range(1, dom_size)]

    total = call(
        self_kernel,
        jax.ShapeDtypeStruct((rows, hidden), F32),
        [SMEM, VMEM, VMEM, VMEM],
        flops=2 * rows * width * hidden,
        moved=4 * rows * hidden,
    )(core_arg, features, mine, other)
    aggregate, grad = call(
        layer_kernel,
        [jax.ShapeDtypeStruct((rows, width), BF16), jax.ShapeDtypeStruct((rows, hidden), BF16)],
        [SMEM, SMEM, SMEM] + [VMEM] * (4 + dom_size),
        [pltpu.VMEM((rows, width), F32)],
        flops=2 * rows * width * hidden,
        moved=4 * rows * hidden,
    )(me_arg, core_arg, in_block, cotangent, total, mine, other, *received)

    def term(use):
        return call(
            term_kernel,
            jax.ShapeDtypeStruct((width, hidden), BF16),
            [SMEM, VMEM, VMEM, VMEM],
            flops=2 * rows * width * hidden,
            moved=2 * width * hidden,
        )(use, features, aggregate, grad)

    sent = term(1 - core_arg)
    kept = term(core_arg)
    chip = added(kept, swap(sent, "rep", 1)).reshape(dom_size, width // dom_size, hidden)
    first, second = chip[:, :, : hidden // 2], chip[:, :, hidden // 2 :]
    first = reduce_low(first, low)
    second = reduce_high(second, high)
    first = reduce_high(first, high)
    second = reduce_low(second, low)
    both = jnp.concatenate([first, second], axis=2)
    total = lax.dynamic_index_in_dim(both, place, 0, keepdims=False).astype(F32)
    for step in range(1, dom_size // 2):
        total = total + swap(
            lax.dynamic_index_in_dim(both, place ^ step, 0, keepdims=False), "dom", 2 * step
        ).astype(F32)
    share = total.astype(BF16)
    size = share.shape[1] // 2
    step = 1
    parts = [share[:, :size], share[:, size:]]
    while step < lax.axis_size("rep") // 2:
        upper = (high & step) != 0
        others = swap(jnp.concatenate(parts, axis=1), "rep", 2 * step)
        width_now = parts[0].shape[1]
        others = [others[:, :width_now], others[:, width_now:]]
        parts = [
            jnp.concatenate([jnp.where(upper, b, a), jnp.where(upper, a, b)], axis=1)
            for a, b in zip(parts, others)
        ]
        step *= 2
    whole = jnp.concatenate(parts, axis=1)
    opposite = swap(whole, "rep", 1)
    return (
        jnp.where(core == 0, whole, opposite).astype(F32),
        jnp.where(core == 0, opposite, whole).astype(F32),
    )


def solution(mesh):
    in_specs = (
        P(("rep", "dom"), None),
        P(("rep", "dom"), None),
        P("dom", None),
        P("dom", None),
        P(("rep", "dom"), None, None),
        P(("rep", "dom")),
        P(("rep", "dom")),
        P(("rep", "dom")),
    )
    out_specs = (P("dom", None), P("dom", None))
    return jax.shard_map(shards, mesh=mesh, in_specs=in_specs, out_specs=out_specs, check_vma=False)
```

time: 255 us -> 147 us (0.58)
  waiting for transfers between devices: 169 us -> 70.6 us
  starting transfers between devices: 7.79 us -> 44 us
  matrix products: 32.9 us -> 0 us
  local copies, waits for them, and re-layouts: 28 us -> 1.65 us
  Pallas kernels: 0 us -> 24.6 us
  between operations: 13.8 us -> 0.9 us
  other arithmetic: 2.54 us -> 5.13 us
    unnamed x5 -> x0, waiting for transfers between devices: 74.9 us -> none
    ppermute x0 -> x22, waiting for transfers between devices: none -> 70.6 us  [swap(): lax.ppermute(value, axis, [(index, index ^ step) for index in range(size)])]
    all_to_all x1 -> x0, waiting for transfers between devices: 46.4 us -> none  [shards(): lax.all_to_all(slots, 'dom', split_axis=0, concat_axis=0, tiled=True)]
    ppermute x0 -> x22, starting transfers between devices: none -> 44 us  [swap(): lax.ppermute(value, axis, [(index, index ^ step) for index in range(size)])]
    dot_general x7 -> x0, matrix products: 32.9 us -> none  [the longest x2 12.2 us: add_product(): return total + jnp.dot(left, piece, preferred_element_type=jnp.float32)]
    psum x1 -> x0, waiting for transfers between devices: 32.5 us -> none  [shards(): totals = lax.psum(shares, 'rep').astype(jnp.float32)]
    pallas_call x0 -> x5, Pallas kernels: none -> 24.6 us  [the longest x1 9.65 us: shards(): call(layer_kernel, [jax.ShapeDtypeStruct((rows, width), BF16), jax.ShapeD...]
    all_gather x2 -> x0, waiting for transfers between devices: 15.6 us -> none  [the longest x1 15.5 us: shards(): lax.all_gather(w_neigh, 'dom', axis=0, tiled=True)]
  transfers between devices with their start and end apart: 5 -> 22, of which waited for: 4 -> 16; matrix products, arithmetic and copies ran while one was open for 16% -> 0% of each run, Pallas kernels for 0% -> 7%
where the time goes in v1:
time: 147 us
  waiting for transfers between devices  70.6 us (48%)
  starting transfers between devices  44 us (30%)
  Pallas kernels  24.6 us (17%)
  other arithmetic  5.13 us (3%)
  local copies, waits for them, and re-layouts  1.65 us (1%)
    ppermute x22, waiting for transfers between devices, swap(): lax.ppermute(value, axis, [(index, index ^ step) for index in range(size)])  70.6 us
    ppermute x22, starting transfers between devices, swap(): lax.ppermute(value, axis, [(index, index ^ step) for index in range(size)])  44 us
    pallas_call x1, Pallas kernels, shards(): call(layer_kernel, [jax.ShapeDtypeStruct((rows, width), BF16), jax.ShapeD...  9.65 us
    pallas_call x2, Pallas kernels, term(): call(term_kernel, jax.ShapeDtypeStruct((width, hidden), BF16), [SMEM, VME...  8 us
    pallas_call x1, Pallas kernels, shards(): call(self_kernel, jax.ShapeDtypeStruct((rows, hidden), F32), [SMEM, VMEM,...  3.83 us
    pallas_call x1, Pallas kernels, shards(): call(slots_kernel, [jax.ShapeDtypeStruct((block, width), BF16)] * dom_siz...  3.12 us
  transfers between devices with their start and end apart: 22, of which 16 were waited for; matrix products, arithmetic and copies ran while one was open for 0% of the time, Pallas kernels for 7%

profile of v1, /device:TPU:0, one launch (start us, length us, event | category | flops | bytes accessed | tf_op | source)
XLA Modules:
  0.0 146.8 jit_solution(12662600072458284417)
XLA Ops:
  1.6 4.1 %collective-permute-start = (bf16[1,96,512]{2,1,0:T(8,128)(2,1)S(1)}, bf16[1,96,512]{2,1,0:T(8,128)(2,1)S(1)}, u32[]{:S(2)}, u32[]{:S(2)}) collective-permute-start(bf16[1,96,512]{2,1,0:T(8,128)(2,1)S(1)} %fusion.13), channel_id=1, source_target_pairs={{0,4},{1,5},{2,6},{3,7},{4,0},{5,1},{6,2},{7,3},{8,12},{9,13},{10,... | collective-permute-start | bytes 294920 | tf_op jit(solution)/shard_map/ppermute | solution.py:21
  5.7 4.9 %collective-permute-done = bf16[1,96,512]{2,1,0:T(8,128)(2,1)S(1)} collective-permute-done((bf16[1,96,512]{2,1,0:T(8,128)(2,1)S(1)}, bf16[1,96,512]{2,1,0:T(8,128)(2,1)S(1)}, u32[]{:S(2)}, u32[]{:S(2)}) %collective-permute-start) | collective-permute-done | bytes 98336 | tf_op jit(solution)/shard_map/ppermute | solution.py:21
  11.5 5.4 %collective-permute-done.1 = bf16[2,96,512]{2,1,0:T(8,128)(2,1)S(1)} collective-permute-done((bf16[2,96,512]{2,1,0:T(8,128)(2,1)S(1)}, bf16[2,96,512]{2,1,0:T(8,128)(2,1)S(1)}, u32[]{:S(2)}, u32[]{:S(2)}) %collective-permute-start.1) | collective-permute-done | bytes 196640 | tf_op jit(solution)/shard_map/ppermute | solution.py:21
  16.9 1.3 collective-permute-start.2
  18.2 8.2 %collective-permute-done.2 = bf16[4,96,512]{2,1,0:T(8,128)(2,1)S(1)} collective-permute-done((bf16[4,96,512]{2,1,0:T(8,128)(2,1)S(1)}, bf16[4,96,512]{2,1,0:T(8,128)(2,1)S(1)}, u32[]{:S(2)}, u32[]{:S(2)}) %collective-permute-start.2) | collective-permute-done | bytes 393248 | tf_op jit(solution)/shard_map/ppermute | solution.py:21
  26.5 1.4 collective-permute-start.3
  27.9 15.6 %collective-permute-done.3 = bf16[768,512]{1,0:T(8,128)(2,1)S(1)} collective-permute-done((bf16[768,512]{1,0:T(8,128)(2,1)S(1)}, bf16[768,512]{1,0:T(8,128)(2,1)S(1)}, u32[]{:S(2)}, u32[]{:S(2)}) %collective-permute-start.3) | collective-permute-done | bytes 786464 | tf_op jit(solution)/shard_map/ppermute | solution.py:21
  45.3 3.1 %shard_map.96 = (bf16[128,768]{1,0:T(8,128)(2,1)S(1)}, bf16[128,768]{1,0:T(8,128)(2,1)S(1)}, bf16[128,768]{1,0:T(8,128)(2,1)S(1)}, bf16[128,768]{1,0:T(8,128)(2,...) custom-call(s32[1]{0:T(128)} %bitcast.1.me_ref, ...), custom_call_target="tpu_custom_call" | custom-call | flops 1610612736 | bytes 4194304 | tf_op jit(solution)/shard_map/pallas_call | solution.py:185
  48.5 6.0 %collective-permute-start.10 = (bf16[128,768]{1,0:T(8,128)(2,1)S(1)}, bf16[128,768]{1,0:T(8,128)(2,1)S(1)}, u32[]{:S(2)}, u32[]{:S(2)}) collective-permute-start(bf16[128,768]{1,0:T(8,128)(2,1)S(1)} %get-tuple-element.18), channel_id=1, source_target_pairs={{0,6},{1,7},{2,4},{3,5},{4,2},{5,3},{6,0},{7,1},{8,14},{9,15},{10,... | collective-permute-start | bytes 589832 | tf_op jit(solution)/shard_map/ppermute | solution.py:21
  56.0 3.8 %collective-permute-done.10.refs_6_ = bf16[128,768]{1,0:T(8,128)(2,1)S(1)} collective-permute-done((bf16[128,768]{1,0:T(8,128)(2,1)S(1)}, bf16[128,768]{1,0:T(8,128)(2,1)S(1)}, u32[]{:S(2)}, u32[]{:S(2)}) %collective-permute-start.10) | collective-permute-done | bytes 196640 | tf_op jit(solution)/shard_map/ppermute | solution.py:21
  59.8 9.1 %collective-permute-start.7 = (bf16[128,768]{1,0:T(8,128)(2,1)S(1)}, bf16[128,768]{1,0:T(8,128)(2,1)S(1)}, u32[]{:S(2)}, u32[]{:S(2)}) collective-permute-start(bf16[128,768]{1,0:T(8,128)(2,1)S(1)} %get-tuple-element.15), channel_id=1, source_target_pairs={{0,3},{1,2},{2,1},{3,0},{4,7},{5,6},{6,5},{7,4},{8,11},{9,10},{10,... | collective-permute-start | bytes 589832 | tf_op jit(solution)/shard_map/ppermute | solution.py:21
  68.9 7.0 %collective-permute-start.8 = (bf16[128,768]{1,0:T(8,128)(2,1)S(1)}, bf16[128,768]{1,0:T(8,128)(2,1)S(1)}, u32[]{:S(2)}, u32[]{:S(2)}) collective-permute-start(bf16[128,768]{1,0:T(8,128)(2,1)S(1)} %get-tuple-element.16), channel_id=1, source_target_pairs={{0,4},{1,5},{2,6},{3,7},{4,0},{5,1},{6,2},{7,3},{8,12},{9,13},{10,... | collective-permute-start | bytes 589832 | tf_op jit(solution)/shard_map/ppermute | solution.py:21
  75.9 3.8 %shard_map.95.total_ref = f32[1024,1024]{1,0:T(8,128)} custom-call(s32[1]{0:T(128)} %bitcast.core_ref.use_ref, bf16[1024,768]{1,0:T(8,128)(2,1)S(1)} %copy-done, bf16[768,1024]{1,0:T(8,128)(2,1)S(1)} %pad_maximum_fusion.mine_ref, bf16[768,1024]{1,0:T(8,128)(2,1)S(1)} %collective-permute-done.4.other_ref), custom_call_target="tpu_custom_call" | custom-call | flops 1610612736 | bytes 4194304 | tf_op jit(solution)/shard_map/pallas_call | solution.py:195
  79.8 8.9 %collective-permute-done.8.refs_4_ = bf16[128,768]{1,0:T(8,128)(2,1)S(1)} collective-permute-done((bf16[128,768]{1,0:T(8,128)(2,1)S(1)}, bf16[128,768]{1,0:T(8,128)(2,1)S(1)}, u32[]{:S(2)}, u32[]{:S(2)}) %collective-permute-start.8) | collective-permute-done | bytes 196640 | tf_op jit(solution)/shard_map/ppermute | solution.py:21
  88.7 1.9 %collective-permute-done.9.refs_5_ = bf16[128,768]{1,0:T(8,128)(2,1)S(1)} collective-permute-done((bf16[128,768]{1,0:T(8,128)(2,1)S(1)}, bf16[128,768]{1,0:T(8,128)(2,1)S(1)}, u32[]{:S(2)}, u32[]{:S(2)}) %collective-permute-start.9) | collective-permute-done | bytes 196640 | tf_op jit(solution)/shard_map/ppermute | solution.py:21
  90.6 9.7 %shard_map.97 = (bf16[1024,768]{1,0:T(8,128)(2,1)S(1)}, bf16[1024,1024]{1,0:T(8,128)(2,1)}) custom-call(s32[1]{0:T(128)} %bitcast.1.me_ref, s32[1]{0:T(128)} %bitcast.core_ref.use_ref, s32[8]{0:T(128)S(1)} %copy-done.2, bf16[1024,1024]{1,0:T(8,128)(2,1)} %cotangent_ref.1, f32[1024,1024]{1,0:T(8,128)} %shard_map.95.total_ref, ...), custom_call_target="tpu_custom_call" | custom-call | flops 1610612736 | bytes 4194304 | tf_op jit(solution)/shard_map/pallas_call | solution.py:202
  100.3 4.6 %shard_map.99 = bf16[768,1024]{1,0:T(8,128)(2,1)} custom-call(s32[1]{0:T(128)S(6)} %sub.21.use_ref, bf16[1024,768]{1,0:T(8,128)(2,1)S(1)} %copy-done, bf16[1024,768]{1,0:T(8,128)(2,1)S(1)} %get-tuple-element.20.aggregate_ref, bf16[1024,1024]{1,0:T(8,128)(2,1)} %get-tuple-element.21.grad_ref), custom_call_target="tpu_custom_call" | custom-call | flops 1610612736 | bytes 1572864 | tf_op jit(solution)/shard_map/pallas_call | solution.py:212
  104.9 3.4 %shard_map.98 = bf16[768,1024]{1,0:T(8,128)(2,1)S(1)} custom-call(s32[1]{0:T(128)} %bitcast.core_ref.use_ref, bf16[1024,768]{1,0:T(8,128)(2,1)S(1)} %copy-done, bf16[1024,768]{1,0:T(8,128)(2,1)S(1)} %get-tuple-element.20.aggregate_ref, bf16[1024,1024]{1,0:T(8,128)(2,1)} %get-tuple-element.21.grad_ref), custom_call_target="tpu_custom_call" | custom-call | flops 1610612736 | bytes 1572864 | tf_op jit(solution)/shard_map/pallas_call | solution.py:212
  108.6 2.1 %add_convert_fusion = bf16[768,1024]{1,0:T(8,128)(2,1)S(1)} fusion(bf16[768,1024]{1,0:T(8,128)(2,1)} %collective-permute-done.12, bf16[768,1024]{1,0:T(8,128)(2,1)S(1)} %shard_map.98), kind=kLoop, calls=%fused_computation | loop fusion | flops 3145728 | bytes 4718592 | tf_op jit(solution)/shard_map/convert_element_type | solution.py:147
  110.9 1.6 %collective-permute-start.15 = (bf16[8,96,256]{2,1,0:T(8,128)(2,1)S(1)}, bf16[8,96,256]{2,1,0:T(8,128)(2,1)S(1)}, u32[]{:S(2)}, u32[]{:S(2)}) collective-permute-start(bf16[8,96,256]{2,1,0:T(8,128)(2,1)S(1)} %constant_dynamic-slice_fusion), channel_id=1, source_target_pairs={{0,16},{8,24},{16,0},{24,8},{1,17},{9,25},{17,1},{25,9},{2,18},{10... | collective-permute-start | bytes 1179656 | tf_op jit(solution)/shard_map/ppermute | solution.py:21
  112.6 1.7 %collective-permute-start.13 = (bf16[4,96,512]{2,1,0:T(8,128)(2,1)S(1)}, bf16[4,96,512]{2,1,0:T(8,128)(2,1)S(1)}, u32[]{:S(2)}, u32[]{:S(2)}) collective-permute-start(bf16[4,96,512]{2,1,0:T(8,128)(2,1)S(1)} %dynamic-slice_bitcast_fusion), channel_id=1, source_target_pairs={{0,1},{1,0},{2,3},{3,2},{4,5},{5,4},{6,7},{7,6},{8,9},{9,8},{10,11... | collective-permute-start | bytes 1179656 | tf_op jit(solution)/shard_map/ppermute | solution.py:21
  114.3 7.9 %collective-permute-done.15 = bf16[8,96,256]{2,1,0:T(8,128)(2,1)S(1)} collective-permute-done((bf16[8,96,256]{2,1,0:T(8,128)(2,1)S(1)}, bf16[8,96,256]{2,1,0:T(8,128)(2,1)S(1)}, u32[]{:S(2)}, u32[]{:S(2)}) %collective-permute-start.15) | collective-permute-done | bytes 393248 | tf_op jit(solution)/shard_map/ppermute | solution.py:21
  122.3 1.7 %collective-permute-start.16 = (bf16[4,96,256]{2,1,0:T(8,128)(2,1)S(1)}, bf16[4,96,256]{2,1,0:T(8,128)(2,1)S(1)}, u32[]{:S(2)}, u32[]{:S(2)}) collective-permute-start(bf16[4,96,256]{2,1,0:T(8,128)(2,1)S(1)} %dynamic-slice_bitcast_fusion.1), channel_id=1, source_target_pairs={{0,1},{1,0},{2,3},{3,2},{4,5},{5,4},{6,7},{7,6},{8,9},{9,8},{10,11... | collective-permute-start | bytes 589832 | tf_op jit(solution)/shard_map/ppermute | solution.py:21
  124.2 1.6 %collective-permute-start.14 = (bf16[4,96,256]{2,1,0:T(8,128)(2,1)S(1)}, bf16[4,96,256]{2,1,0:T(8,128)(2,1)S(1)}, u32[]{:S(2)}, u32[]{:S(2)}) collective-permute-start(bf16[4,96,256]{2,1,0:T(8,128)(2,1)S(1)} %constant_dynamic-slice_fusion.1), channel_id=1, source_target_pairs={{0,16},{8,24},{16,0},{24,8},{1,17},{9,25},{17,1},{25,9},{2,18},{10... | collective-permute-start | bytes 589832 | tf_op jit(solution)/shard_map/ppermute | solution.py:21
  125.8 2.8 %collective-permute-done.16 = bf16[4,96,256]{2,1,0:T(8,128)(2,1)S(1)} collective-permute-done((bf16[4,96,256]{2,1,0:T(8,128)(2,1)S(1)}, bf16[4,96,256]{2,1,0:T(8,128)(2,1)S(1)}, u32[]{:S(2)}, u32[]{:S(2)}) %collective-permute-start.16) | collective-permute-done | bytes 196640 | tf_op jit(solution)/shard_map/ppermute | solution.py:21
  128.6 1.5 %collective-permute-done.14 = bf16[4,96,256]{2,1,0:T(8,128)(2,1)S(1)} collective-permute-done((bf16[4,96,256]{2,1,0:T(8,128)(2,1)S(1)}, bf16[4,96,256]{2,1,0:T(8,128)(2,1)S(1)}, u32[]{:S(2)}, u32[]{:S(2)}) %collective-permute-start.14) | collective-permute-done | bytes 196640 | tf_op jit(solution)/shard_map/ppermute | solution.py:21
  130.3 2.7 %collective-permute-start.18 = (bf16[96,512]{1,0:T(8,128)(2,1)S(1)}, bf16[96,512]{1,0:T(8,128)(2,1)S(1)}, u32[]{:S(2)}, u32[]{:S(2)}) collective-permute-start(bf16[96,512]{1,0:T(8,128)(2,1)S(1)} %get-tuple-element.31), channel_id=1, source_target_pairs={{0,4},{1,5},{2,6},{3,7},{4,0},{5,1},{6,2},{7,3},{8,12},{9,13},{10,... | collective-permute-start | bytes 294920 | tf_op jit(solution)/shard_map/ppermute | solution.py:21
  133.0 1.7 %collective-permute-start.19 = (bf16[96,512]{1,0:T(8,128)(2,1)S(1)}, bf16[96,512]{1,0:T(8,128)(2,1)S(1)}, u32[]{:S(2)}, u32[]{:S(2)}) collective-permute-start(bf16[96,512]{1,0:T(8,128)(2,1)S(1)} %get-tuple-element.32), channel_id=1, source_target_pairs={{0,6},{1,7},{2,4},{3,5},{4,2},{5,3},{6,0},{7,1},{8,14},{9,15},{10,... | collective-permute-start | bytes 294920 | tf_op jit(solution)/shard_map/ppermute | solution.py:21
  134.9 3.4 %collective-permute-done.18 = bf16[96,512]{1,0:T(8,128)(2,1)S(1)} collective-permute-done((bf16[96,512]{1,0:T(8,128)(2,1)S(1)}, bf16[96,512]{1,0:T(8,128)(2,1)S(1)}, u32[]{:S(2)}, u32[]{:S(2)}) %collective-permute-start.18) | collective-permute-done | bytes 98336 | tf_op jit(solution)/shard_map/ppermute | solution.py:21
  139.6 1.6 %collective-permute-start.20 = (bf16[96,512]{1,0:T(8,128)(2,1)S(1)}, bf16[96,512]{1,0:T(8,128)(2,1)S(1)}, u32[]{:S(2)}, u32[]{:S(2)}) collective-permute-start(bf16[96,512]{1,0:T(8,128)(2,1)S(1)} %fusion.4), channel_id=1, source_target_pairs={{0,16},{8,24},{16,0},{24,8},{1,17},{9,25},{17,1},{25,9},{2,18},{10... | collective-permute-start | bytes 294920 | tf_op jit(solution)/shard_map/ppermute | solution.py:21
  141.2 3.1 %collective-permute-done.20 = bf16[96,512]{1,0:T(8,128)(2,1)S(1)} collective-permute-done((bf16[96,512]{1,0:T(8,128)(2,1)S(1)}, bf16[96,512]{1,0:T(8,128)(2,1)S(1)}, u32[]{:S(2)}, u32[]{:S(2)}) %collective-permute-start.20) | collective-permute-done | bytes 98336 | tf_op jit(solution)/shard_map/ppermute | solution.py:21
  144.4 1.4 collective-permute-done.21
  (53 shorter events, 9.0 us)
Async XLA Ops:
  1.6 9.0 %collective-permute-start = (bf16[1,96,512]{2,1,0:T(8,128)(2,1)S(1)}, bf16[1,96,512]{2,1,0:T(8,128)(2,1)S(1)}, u32[]{:S(2)}, u32[]{:S(2)}) collective-permute-start(bf16[1,96,512]{2,1,0:T(8,128)(2,1)S(1)} %fusion.13), channel_id=1, source_target_pairs={{0,4},{1,5},{2,6},{3,7},{4,0},{5,1},{6,2},{7,3},{8,12},{9,13},{10,... | collective-permute-start | bytes 294920 | tf_op jit(solution)/shard_map/ppermute | solution.py:21
  10.7 6.2 %collective-permute-start.1 = (bf16[2,96,512]{2,1,0:T(8,128)(2,1)S(1)}, bf16[2,96,512]{2,1,0:T(8,128)(2,1)S(1)}, u32[]{:S(2)}, u32[]{:S(2)}) collective-permute-start(bf16[2,96,512]{2,1,0:T(8,128)(2,1)S(1)} %maximum_bitcast_fusion), channel_id=1, source_target_pairs={{0,2},{1,3},{2,0},{3,1},{4,6},{5,7},{6,4},{7,5},{8,10},{9,11},{10,... | collective-permute-start | bytes 589832 | tf_op jit(solution)/shard_map/ppermute | solution.py:21
  16.9 9.4 %collective-permute-start.2 = (bf16[4,96,512]{2,1,0:T(8,128)(2,1)S(1)}, bf16[4,96,512]{2,1,0:T(8,128)(2,1)S(1)}, u32[]{:S(2)}, u32[]{:S(2)}) collective-permute-start(bf16[4,96,512]{2,1,0:T(8,128)(2,1)S(1)} %bitcast.62), channel_id=1, source_target_pairs={{0,1},{1,0},{2,3},{3,2},{4,5},{5,4},{6,7},{7,6},{8,9},{9,8},{10,11... | collective-permute-start | bytes 1179656 | tf_op jit(solution)/shard_map/ppermute | solution.py:21
  26.5 16.9 %collective-permute-start.3 = (bf16[768,512]{1,0:T(8,128)(2,1)S(1)}, bf16[768,512]{1,0:T(8,128)(2,1)S(1)}, u32[]{:S(2)}, u32[]{:S(2)}) collective-permute-start(bf16[768,512]{1,0:T(8,128)(2,1)S(1)} %bitcast.61), channel_id=1, source_target_pairs={{0,16},{8,24},{16,0},{24,8},{1,17},{9,25},{17,1},{25,9},{2,18},{10... | collective-permute-start | bytes 2359304 | tf_op jit(solution)/shard_map/ppermute | solution.py:21
  43.6 1.4 copy-start
  43.7 1.7 %copy-start.3 = (bf16[32,128,128]{2,1,0:T(8,128)(2,1)S(1)}, bf16[32,128,128]{2,1,0:T(8,128)(2,1)}, u32[]{:S(2)}) copy-start(bf16[32,128,128]{2,1,0:T(8,128)(2,1)} %tiles_ref.1) | copy-start | bytes 3145732
  43.7 1.7 %copy-start.4 = (s32[32]{0:T(128)S(1)}, s32[32]{0:T(128)}, u32[]{:S(2)}) copy-start(s32[32]{0:T(128)} %src_ref.1) | copy-start | bytes 388
  43.7 1.7 %copy-start.5 = (s32[32]{0:T(128)S(1)}, s32[32]{0:T(128)}, u32[]{:S(2)}) copy-start(s32[32]{0:T(128)} %peer_ref.1) | copy-start | bytes 388
  43.9 32.0 %collective-permute-start.4 = (bf16[768,1024]{1,0:T(8,128)(2,1)S(1)}, bf16[768,1024]{1,0:T(8,128)(2,1)S(1)}, u32[]{:S(2)}, u32[]{:S(2)}) collective-permute-start(bf16[768,1024]{1,0:T(8,128)(2,1)S(1)} %pad_maximum_fusion.mine_ref), channel_id=1, source_target_pairs={{0,8},{8,0},{16,24},{24,16},{1,9},{9,1},{17,25},{25,17},{2,10},{10... | collective-permute-start | bytes 4718600 | tf_op jit(solution)/shard_map/ppermute | solution.py:21
  48.5 11.4 %collective-permute-start.10 = (bf16[128,768]{1,0:T(8,128)(2,1)S(1)}, bf16[128,768]{1,0:T(8,128)(2,1)S(1)}, u32[]{:S(2)}, u32[]{:S(2)}) collective-permute-start(bf16[128,768]{1,0:T(8,128)(2,1)S(1)} %get-tuple-element.18), channel_id=1, source_target_pairs={{0,6},{1,7},{2,4},{3,5},{4,2},{5,3},{6,0},{7,1},{8,14},{9,15},{10,... | collective-permute-start | bytes 589832 | tf_op jit(solution)/shard_map/ppermute | solution.py:21
  54.4 14.5 %collective-permute-start.11 = (bf16[128,768]{1,0:T(8,128)(2,1)S(1)}, bf16[128,768]{1,0:T(8,128)(2,1)S(1)}, u32[]{:S(2)}, u32[]{:S(2)}) collective-permute-start(bf16[128,768]{1,0:T(8,128)(2,1)S(1)} %get-tuple-element.19), channel_id=1, source_target_pairs={{0,7},{1,6},{2,5},{3,4},{4,3},{5,2},{6,1},{7,0},{8,15},{9,14},{10,... | collective-permute-start | bytes 589832 | tf_op jit(solution)/shard_map/ppermute | solution.py:21
  55.4 24.3 %collective-permute-start.5 = (bf16[128,768]{1,0:T(8,128)(2,1)S(1)}, bf16[128,768]{1,0:T(8,128)(2,1)S(1)}, u32[]{:S(2)}, u32[]{:S(2)}) collective-permute-start(bf16[128,768]{1,0:T(8,128)(2,1)S(1)} %get-tuple-element.13), channel_id=1, source_target_pairs={{0,1},{1,0},{2,3},{3,2},{4,5},{5,4},{6,7},{7,6},{8,9},{9,8},{10,11... | collective-permute-start | bytes 589832 | tf_op jit(solution)/shard_map/ppermute | solution.py:21
  56.0 23.8 %collective-permute-start.6 = (bf16[128,768]{1,0:T(8,128)(2,1)S(1)}, bf16[128,768]{1,0:T(8,128)(2,1)S(1)}, u32[]{:S(2)}, u32[]{:S(2)}) collective-permute-start(bf16[128,768]{1,0:T(8,128)(2,1)S(1)} %get-tuple-element.14), channel_id=1, source_target_pairs={{0,2},{1,3},{2,0},{3,1},{4,6},{5,7},{6,4},{7,5},{8,10},{9,11},{10,... | collective-permute-start | bytes 589832 | tf_op jit(solution)/shard_map/ppermute | solution.py:21
  59.8 19.9 %collective-permute-start.7 = (bf16[128,768]{1,0:T(8,128)(2,1)S(1)}, bf16[128,768]{1,0:T(8,128)(2,1)S(1)}, u32[]{:S(2)}, u32[]{:S(2)}) collective-permute-start(bf16[128,768]{1,0:T(8,128)(2,1)S(1)} %get-tuple-element.15), channel_id=1, source_target_pairs={{0,3},{1,2},{2,1},{3,0},{4,7},{5,6},{6,5},{7,4},{8,11},{9,10},{10,... | collective-permute-start | bytes 589832 | tf_op jit(solution)/shard_map/ppermute | solution.py:21
  68.9 19.8 %collective-permute-start.8 = (bf16[128,768]{1,0:T(8,128)(2,1)S(1)}, bf16[128,768]{1,0:T(8,128)(2,1)S(1)}, u32[]{:S(2)}, u32[]{:S(2)}) collective-permute-start(bf16[128,768]{1,0:T(8,128)(2,1)S(1)} %get-tuple-element.16), channel_id=1, source_target_pairs={{0,4},{1,5},{2,6},{3,7},{4,0},{5,1},{6,2},{7,3},{8,12},{9,13},{10,... | collective-permute-start | bytes 589832 | tf_op jit(solution)/shard_map/ppermute | solution.py:21
  75.9 3.8 %copy-start.1 = (bf16[768,1024]{1,0:T(8,128)(2,1)}, bf16[768,1024]{1,0:T(8,128)(2,1)S(1)}, u32[]{:S(2)}) copy-start(bf16[768,1024]{1,0:T(8,128)(2,1)S(1)} %collective-permute-done.4.other_ref) | copy-start | bytes 4718596
  75.9 14.7 %collective-permute-start.9 = (bf16[128,768]{1,0:T(8,128)(2,1)S(1)}, bf16[128,768]{1,0:T(8,128)(2,1)S(1)}, u32[]{:S(2)}, u32[]{:S(2)}) collective-permute-start(bf16[128,768]{1,0:T(8,128)(2,1)S(1)} %get-tuple-element.17), channel_id=1, source_target_pairs={{0,5},{1,4},{2,7},{3,6},{4,1},{5,0},{6,3},{7,2},{8,13},{9,12},{10,... | collective-permute-start | bytes 589832 | tf_op jit(solution)/shard_map/ppermute | solution.py:21
  75.9 14.7 %copy-start.2 = (s32[8]{0:T(128)S(1)}, s32[8]{0:T(128)}, u32[]{:S(2)}) copy-start(s32[8]{0:T(128)} %into_ref.1) | copy-start | bytes 100
  104.9 3.8 %collective-permute-start.12 = (bf16[768,1024]{1,0:T(8,128)(2,1)}, bf16[768,1024]{1,0:T(8,128)(2,1)}, u32[]{:S(2)}, u32[]{:S(2)}) collective-permute-start(bf16[768,1024]{1,0:T(8,128)(2,1)} %shard_map.99), channel_id=1, source_target_pairs={{0,8},{8,0},{16,24},{24,16},{1,9},{9,1},{17,25},{25,17},{2,10},{10... | collective-permute-start | bytes 4718600 | tf_op jit(solution)/shard_map/ppermute | solution.py:21
  110.9 11.3 %collective-permute-start.15 = (bf16[8,96,256]{2,1,0:T(8,128)(2,1)S(1)}, bf16[8,96,256]{2,1,0:T(8,128)(2,1)S(1)}, u32[]{:S(2)}, u32[]{:S(2)}) collective-permute-start(bf16[8,96,256]{2,1,0:T(8,128)(2,1)S(1)} %constant_dynamic-slice_fusion), channel_id=1, source_target_pairs={{0,16},{8,24},{16,0},{24,8},{1,17},{9,25},{17,1},{25,9},{2,18},{10... | collective-permute-start | bytes 1179656 | tf_op jit(solution)/shard_map/ppermute | solution.py:21
  112.6 11.5 %collective-permute-start.13 = (bf16[4,96,512]{2,1,0:T(8,128)(2,1)S(1)}, bf16[4,96,512]{2,1,0:T(8,128)(2,1)S(1)}, u32[]{:S(2)}, u32[]{:S(2)}) collective-permute-start(bf16[4,96,512]{2,1,0:T(8,128)(2,1)S(1)} %dynamic-slice_bitcast_fusion), channel_id=1, source_target_pairs={{0,1},{1,0},{2,3},{3,2},{4,5},{5,4},{6,7},{7,6},{8,9},{9,8},{10,11... | collective-permute-start | bytes 1179656 | tf_op jit(solution)/shard_map/ppermute | solution.py:21
  122.3 6.2 %collective-permute-start.16 = (bf16[4,96,256]{2,1,0:T(8,128)(2,1)S(1)}, bf16[4,96,256]{2,1,0:T(8,128)(2,1)S(1)}, u32[]{:S(2)}, u32[]{:S(2)}) collective-permute-start(bf16[4,96,256]{2,1,0:T(8,128)(2,1)S(1)} %dynamic-slice_bitcast_fusion.1), channel_id=1, source_target_pairs={{0,1},{1,0},{2,3},{3,2},{4,5},{5,4},{6,7},{7,6},{8,9},{9,8},{10,11... | collective-permute-start | bytes 589832 | tf_op jit(solution)/shard_map/ppermute | solution.py:21
  124.2 5.9 %collective-permute-start.14 = (bf16[4,96,256]{2,1,0:T(8,128)(2,1)S(1)}, bf16[4,96,256]{2,1,0:T(8,128)(2,1)S(1)}, u32[]{:S(2)}, u32[]{:S(2)}) collective-permute-start(bf16[4,96,256]{2,1,0:T(8,128)(2,1)S(1)} %constant_dynamic-slice_fusion.1), channel_id=1, source_target_pairs={{0,16},{8,24},{16,0},{24,8},{1,17},{9,25},{17,1},{25,9},{2,18},{10... | collective-permute-start | bytes 589832 | tf_op jit(solution)/shard_map/ppermute | solution.py:21
  130.3 4.7 %collective-permute-start.17 = (bf16[96,512]{1,0:T(8,128)(2,1)S(1)}, bf16[96,512]{1,0:T(8,128)(2,1)S(1)}, u32[]{:S(2)}, u32[]{:S(2)}) collective-permute-start(bf16[96,512]{1,0:T(8,128)(2,1)S(1)} %get-tuple-element.30), channel_id=1, source_target_pairs={{0,2},{1,3},{2,0},{3,1},{4,6},{5,7},{6,4},{7,5},{8,10},{9,11},{10,... | collective-permute-start | bytes 294920 | tf_op jit(solution)/shard_map/ppermute | solution.py:21
  130.3 8.0 %collective-permute-start.18 = (bf16[96,512]{1,0:T(8,128)(2,1)S(1)}, bf16[96,512]{1,0:T(8,128)(2,1)S(1)}, u32[]{:S(2)}, u32[]{:S(2)}) collective-permute-start(bf16[96,512]{1,0:T(8,128)(2,1)S(1)} %get-tuple-element.31), channel_id=1, source_target_pairs={{0,4},{1,5},{2,6},{3,7},{4,0},{5,1},{6,2},{7,3},{8,12},{9,13},{10,... | collective-permute-start | bytes 294920 | tf_op jit(solution)/shard_map/ppermute | solution.py:21
  133.0 6.5 %collective-permute-start.19 = (bf16[96,512]{1,0:T(8,128)(2,1)S(1)}, bf16[96,512]{1,0:T(8,128)(2,1)S(1)}, u32[]{:S(2)}, u32[]{:S(2)}) collective-permute-start(bf16[96,512]{1,0:T(8,128)(2,1)S(1)} %get-tuple-element.32), channel_id=1, source_target_pairs={{0,6},{1,7},{2,4},{3,5},{4,2},{5,3},{6,0},{7,1},{8,14},{9,15},{10,... | collective-permute-start | bytes 294920 | tf_op jit(solution)/shard_map/ppermute | solution.py:21
  139.6 4.7 %collective-permute-start.20 = (bf16[96,512]{1,0:T(8,128)(2,1)S(1)}, bf16[96,512]{1,0:T(8,128)(2,1)S(1)}, u32[]{:S(2)}, u32[]{:S(2)}) collective-permute-start(bf16[96,512]{1,0:T(8,128)(2,1)S(1)} %fusion.4), channel_id=1, source_target_pairs={{0,16},{8,24},{16,0},{24,8},{1,17},{9,25},{17,1},{25,9},{2,18},{10... | collective-permute-start | bytes 294920 | tf_op jit(solution)/shard_map/ppermute | solution.py:21
  144.4 1.5 %collective-permute-start.21 = (bf16[96,1024]{1,0:T(8,128)(2,1)S(1)}, bf16[96,1024]{1,0:T(8,128)(2,1)S(1)}, u32[]{:S(2)}, u32[]{:S(2)}) collective-permute-start(bf16[96,1024]{1,0:T(8,128)(2,1)S(1)} %pad_maximum_fusion.3), channel_id=1, source_target_pairs={{0,8},{8,0},{16,24},{24,16},{1,9},{9,1},{17,25},{25,17},{2,10},{10... | collective-permute-start | bytes 589832 | tf_op jit(solution)/shard_map/ppermute | solution.py:21

commit v2 on v1

v2 whole, which is shorter than its diff:
```python
import jax
import jax.numpy as jnp
from jax import lax
from jax.experimental import pallas as pl
from jax.experimental.pallas import tpu as pltpu
from jax.sharding import PartitionSpec as P

F32 = jnp.float32
BF16 = jnp.bfloat16
SCALE = 0.7978845608
CUBIC = 0.044715
MIB = 1 << 20
SMEM = pl.BlockSpec(memory_space=pltpu.SMEM)
VMEM = pl.BlockSpec(memory_space=pltpu.VMEM)


def swap(value, axis, step):
    size = lax.axis_size(axis)
    return lax.ppermute(value, axis, [(index, index ^ step) for index in range(size)])


def slots_kernel(src_ref, peer_ref, tiles_ref, features_ref, out_ref, dense):
    count, block, _ = tiles_ref.shape
    dense[...] = jnp.zeros_like(dense)

    def place(tile, carry):
        row = pl.multiple_of(peer_ref[tile] * block, block)
        column = pl.multiple_of(src_ref[tile] * block, block)
        at = (pl.ds(row, block), pl.ds(column, block))
        dense[at] = dense[at] + tiles_ref[tile].astype(F32)
        return carry

    lax.fori_loop(0, count, place, 0)
    chunk = 4 * block
    for first in range(0, out_ref.shape[0], chunk):
        rows = dense[first : first + chunk, :].astype(BF16)
        out_ref[first : first + chunk, :] = jnp.dot(
            rows, features_ref[...], preferred_element_type=F32
        ).astype(BF16)


def self_kernel(core_ref, features_ref, mine_ref, other_ref, out_ref):
    rows = features_ref.shape[0]
    chunk = 256

    def product(weight_ref):
        def body():
            for first in range(0, rows, chunk):
                at = slice(first, first + chunk)
                out_ref[at, :] = jnp.dot(features_ref[at, :], weight_ref[...], preferred_element_type=F32)

        return body

    pl.when(core_ref[0] == 0)(product(mine_ref))
    pl.when(core_ref[0] != 0)(product(other_ref))


def layer(core_ref, cotangent_ref, total_ref, mine_ref, other_ref, aggregate_ref, grad_ref):
    rows = aggregate_ref.shape[0]
    chunk = 256

    def product(weight_ref):
        def body():
            for first in range(0, rows, chunk):
                at = slice(first, first + chunk)
                value = total_ref[at, :] + jnp.dot(
                    aggregate_ref[at, :], weight_ref[...], preferred_element_type=F32
                )
                square = value * value
                bend = jnp.tanh(value * (SCALE + SCALE * CUBIC * square))
                inner = value * (SCALE + 3.0 * SCALE * CUBIC * square)
                slope = (1.0 + bend) * (0.5 + 0.5 * inner * (1.0 - bend))
                grad_ref[at, :] = (cotangent_ref[at, :].astype(F32) * slope).astype(BF16)

        return body

    pl.when(core_ref[0] == 0)(product(other_ref))
    pl.when(core_ref[0] != 0)(product(mine_ref))


def first_layer_kernel(
    core_ref, into_ref, cotangent_ref, total_ref, mine_ref, other_ref, slots_ref, aggregate_ref, grad_ref, summed
):
    senders, block, _ = slots_ref.shape
    summed[...] = jnp.zeros_like(summed)
    for sender in range(senders):
        at = pl.ds(pl.multiple_of(into_ref[sender] * block, block), block)
        summed[at, :] = summed[at, :] + slots_ref[sender].astype(F32)
    aggregate_ref[...] = summed[...].astype(BF16)
    layer(core_ref, cotangent_ref, total_ref, mine_ref, other_ref, aggregate_ref, grad_ref)


def term_kernel(use_ref, turned_ref, aggregate_ref, grad_ref, out_ref):
    @pl.when(use_ref[0] == 0)
    def _():
        out_ref[...] = jnp.dot(turned_ref[...], grad_ref[...], preferred_element_type=F32).astype(BF16)

    @pl.when(use_ref[0] != 0)
    def _():
        out_ref[...] = lax.dot_general(
            aggregate_ref[...], grad_ref[...], (((0,), (0,)), ((), ())), preferred_element_type=F32
        ).astype(BF16)


def call(kernel, outs, places, scratch=(), flops=0, moved=0, vmem=24):
    return pl.pallas_call(
        kernel,
        out_shape=outs,
        in_specs=places,
        out_specs=jax.tree.map(lambda _: VMEM, outs),
        scratch_shapes=list(scratch),
        compiler_params=pltpu.CompilerParams(vmem_limit_bytes=vmem * MIB),
        cost_estimate=pl.CostEstimate(flops=flops, bytes_accessed=moved, transcendentals=0),
    )


def after(value, *others):
    return lax.optimization_barrier((value, *others))[0]


def joined(held, other, upper, axis):
    return jnp.stack([jnp.where(upper, other, held), jnp.where(upper, held, other)], axis=axis)


def gather_low(held, me):
    held = joined(held, swap(held, "dom", 1), (me & 1) != 0, 1)
    return held.reshape(-1, held.shape[-1])


def gather_high(held, high):
    step = 1
    while step < lax.axis_size("rep") // 2:
        other = swap(held, "rep", 2 * step)
        upper = (high & step) != 0
        held = jnp.concatenate([jnp.where(upper, other, held), jnp.where(upper, held, other)], axis=-1)
        step *= 2
    return held


def added(left, right):
    return (left.astype(F32) + right.astype(F32)).astype(BF16)


def half(value, axis, which):
    size = value.shape[axis] // 2
    return lax.dynamic_slice_in_dim(value, which * size, size, axis)


def reduce_high(value, high):
    parts = lax.axis_size("rep") // 2
    step = parts // 2
    while step:
        upper = (high // step) % 2
        value = added(half(value, 2, upper), swap(half(value, 2, 1 - upper), "rep", 2 * step))
        step //= 2
    return value


def reduce_low(value, low):
    value = value.reshape(value.shape[0] // 2, 2, *value.shape[1:])
    sent = lax.dynamic_index_in_dim(value, 1 - low, 1, keepdims=False)
    kept = lax.dynamic_index_in_dim(value, low, 1, keepdims=False)
    return added(kept, swap(sent, "dom", 1))


def shards(features, cotangent, w_self, w_neigh, tile_vals, tile_src, tile_peer, in_block):
    dom_size = lax.axis_size("dom")
    rows, width = features.shape
    hidden = w_self.shape[1]
    block = tile_vals.shape[1]
    me = lax.axis_index("dom")
    rep = lax.axis_index("rep")
    parts = lax.axis_size("rep") // 2
    core, high = rep % 2, rep // 2
    low, place = me % 2, me // 2
    core_arg = core.astype(jnp.int32).reshape(1)

    half_width = hidden // 2
    share = half_width // parts

    own = jnp.where(core == 0, w_self, w_neigh)
    held = jnp.concatenate(
        [
            lax.dynamic_slice_in_dim(own, high * share, share, 1),
            lax.dynamic_slice_in_dim(own, half_width + high * share, share, 1),
        ],
        axis=1,
    )[None]
    step = dom_size // 2
    other = swap(held, "dom", step)

    slots = call(
        slots_kernel,
        jax.ShapeDtypeStruct((dom_size * block, width), BF16),
        [SMEM, SMEM, VMEM, VMEM],
        [pltpu.VMEM((dom_size * block, rows), F32)],
        flops=2 * dom_size * block * rows * width,
        moved=tile_vals.size * 2 + rows * width * 4,
    )(tile_src, tile_peer, tile_vals, features)
    other, slots = lax.optimization_barrier((other, slots))
    received = lax.all_to_all(slots.reshape(dom_size, block, width), "dom", split_axis=0, concat_axis=0, tiled=True)

    while step > 1:
        held = joined(held, other, (me & step) != 0, 1).reshape(-1, *held.shape[1:])
        step //= 2
        if step > 1:
            other = swap(held, "dom", step)
    weights = [
        gather_high(gather_low(held[..., :share], me), high),
        gather_low(gather_high(held[..., share:], high), me),
    ]

    others = [swap(weight, "rep", 1) for weight in weights]

    totals = [
        call(
            self_kernel,
            jax.ShapeDtypeStruct((rows, half_width), F32),
            [SMEM, VMEM, VMEM, VMEM],
            flops=2 * rows * width * half_width,
            moved=4 * rows * half_width,
        )(core_arg, features, weight, other)
        for weight, other in zip(weights, others)
    ]
    turned = features.T

    cotangents = [cotangent[:, :half_width], cotangent[:, half_width:]]

    def sums(grad):
        def term(use):
            return call(
                term_kernel,
                jax.ShapeDtypeStruct((width, half_width), BF16),
                [SMEM, VMEM, VMEM, VMEM],
                flops=2 * rows * width * half_width,
                moved=2 * width * half_width,
            )(use, turned, aggregate, grad)

        sent = swap(term(1 - core_arg), "rep", 1)
        chip = added(term(core_arg), sent).reshape(dom_size, width // dom_size, half_width)
        first, second = chip[:, :, : half_width // 2], chip[:, :, half_width // 2 :]
        first, second = reduce_low(first, low), reduce_high(second, high)
        first, second = reduce_high(first, high), reduce_low(second, low)
        both = jnp.concatenate([first, second], axis=2)
        total = lax.dynamic_index_in_dim(both, place, 0, keepdims=False).astype(F32)
        for step in range(1, dom_size // 2):
            piece = lax.dynamic_index_in_dim(both, place ^ step, 0, keepdims=False)
            total = total + swap(piece, "dom", 2 * step).astype(F32)
        return total.astype(BF16)

    aggregate, grad = call(
        first_layer_kernel,
        [jax.ShapeDtypeStruct((rows, width), BF16), jax.ShapeDtypeStruct((rows, half_width), BF16)],
        [SMEM, SMEM] + [VMEM] * 5,
        [pltpu.VMEM((rows, width), F32)],
        flops=2 * rows * width * half_width,
        moved=4 * rows * half_width,
    )(core_arg, in_block, cotangents[0], totals[0], weights[0], others[0], received)
    shares = [sums(grad)]
    grad = call(
        layer,
        jax.ShapeDtypeStruct((rows, half_width), BF16),
        [SMEM] + [VMEM] * 5,
        flops=2 * rows * width * half_width,
        moved=4 * rows * half_width,
    )(core_arg, cotangents[1], totals[1], weights[1], others[1], aggregate)
    shares.append(sums(grad))

    size = shares[0].shape[1] // 2
    held = jnp.stack([share[:, at : at + size] for share in shares for at in (0, size)])
    held = gather_high(held, high)
    whole = jnp.concatenate([held[index] for index in range(held.shape[0])], axis=1)
    opposite = swap(whole, "rep", 1)
    return (
        jnp.where(core == 0, whole, opposite).astype(F32),
        jnp.where(core == 0, opposite, whole).astype(F32),
    )


def solution(mesh):
    in_specs = (
        P(("rep", "dom"), None),
        P(("rep", "dom"), None),
        P("dom", None),
        P("dom", None),
        P(("rep", "dom"), None, None),
        P(("rep", "dom")),
        P(("rep", "dom")),
        P(("rep", "dom")),
    )
    out_specs = (P("dom", None), P("dom", None))
    return jax.shard_map(shards, mesh=mesh, in_specs=in_specs, out_specs=out_specs, check_vma=False)
```

time: 147 us -> 121 us (0.82)
  waiting for transfers between devices: 70.6 us -> 39.9 us
  local copies, waits for them, and re-layouts: 1.65 us -> 14 us
  starting transfers between devices: 44 us -> 37.9 us
  Pallas kernels: 24.6 us -> 21.5 us
    ppermute x22 -> x26, waiting for transfers between devices: 70.6 us -> 39.8 us  [swap(): lax.ppermute(value, axis, [(index, index ^ step) for index in range(size)])]
    ppermute x22 -> x26, starting transfers between devices: 44 us -> 33.5 us  [swap(): lax.ppermute(value, axis, [(index, index ^ step) for index in range(size)])]
    unnamed x12 -> x29, local copies, waits for them, and re-layouts: 1.37 us -> 11.1 us
    all_to_all x0 -> x1, starting transfers between devices: none -> 4.3 us  [shards(): lax.all_to_all(slots.reshape(dom_size, block, width), 'dom', split_axis=0...]
    pallas_call x5 -> x9, Pallas kernels: 24.6 us -> 21.5 us  [the longest x4 4.9 us: term(): call(term_kernel, jax.ShapeDtypeStruct((width, half_width), BF16), [SMEM,...]
    slice x1 -> x4, local copies, waits for them, and re-layouts: 0.17 us -> 1.69 us  [the longest x1 1.51 us: shards(): cotangents = [cotangent[:, :half_width], cotangent[:, half_width:]]]
  transfers between devices with their start and end apart: 22 -> 27, of which waited for: 16 -> 15; matrix products, arithmetic and copies ran while one was open for 0% -> 6% of each run, Pallas kernels for 7% -> 18%
where the time goes in v2:
time: 121 us; the launch traced here: 120 us
  waiting for transfers between devices  39.9 us (33%)
  starting transfers between devices  37.9 us (31%)
  Pallas kernels  21.5 us (18%)
  local copies, waits for them, and re-layouts  14 us (12%)
  other arithmetic  5.58 us (5%)
    ppermute x26, waiting for transfers between devices, swap(): lax.ppermute(value, axis, [(index, index ^ step) for index in range(size)])  39.8 us
    ppermute x26, starting transfers between devices, swap(): lax.ppermute(value, axis, [(index, index ^ step) for index in range(size)])  33.5 us
    unnamed x29, local copies, waits for them, and re-layouts  11.1 us
    pallas_call x4, Pallas kernels, term(): call(term_kernel, jax.ShapeDtypeStruct((width, half_width), BF16), [SMEM,...  4.9 us
    pallas_call x2, Pallas kernels, shards(): call(self_kernel, jax.ShapeDtypeStruct((rows, half_width), F32), [SMEM, V...  4.79 us
    pallas_call x1, Pallas kernels, shards(): call(first_layer_kernel, [jax.ShapeDtypeStruct((rows, width), BF16), jax....  4.33 us
    pallas_call x1, Pallas kernels, shards(): call(slots_kernel, jax.ShapeDtypeStruct((dom_size * block, width), BF16),...  4.33 us
    all_to_all x1, starting transfers between devices, shards(): lax.all_to_all(slots.reshape(dom_size, block, width), 'dom', split_axis=0...  4.3 us
  transfers between devices with their start and end apart: 27, of which 15 were waited for; matrix products, arithmetic and copies ran while one was open for 6% of the time, Pallas kernels for 18%

profile of v2, /device:TPU:0, one launch (start us, length us, event | category | flops | bytes accessed | tf_op | source)
XLA Modules:
  0.0 120.0 jit_solution(9740485579699050075)
XLA Ops:
  1.7 4.1 %collective-permute-start = (bf16[1,96,512]{2,1,0:T(8,128)(2,1)S(1)}, bf16[1,96,512]{2,1,0:T(8,128)(2,1)S(1)}, u32[]{:S(2)}, u32[]{:S(2)}) collective-permute-start(bf16[1,96,512]{2,1,0:T(8,128)(2,1)S(1)} %maximum_bitcast_fusion.1), channel_id=1, source_target_pairs={{0,4},{1,5},{2,6},{3,7},{4,0},{5,1},{6,2},{7,3},{8,12},{9,13},{10,... | collective-permute-start | bytes 294920 | tf_op jit(solution)/shard_map/ppermute | solution.py:19
  5.8 1.4 %copy-done = bf16[1024,768]{1,0:T(8,128)(2,1)S(1)} copy-done((bf16[1024,768]{1,0:T(8,128)(2,1)S(1)}, bf16[1024,768]{1,0:T(8,128)(2,1)}, u32[]{:S(2)}) %copy-start) | copy-done | bytes 1572888
  9.7 4.3 %shard_map.95 = bf16[1024,768]{1,0:T(8,128)(2,1)} custom-call(s32[32]{0:T(128)S(1)} %copy-done.11, s32[32]{0:T(128)S(1)} %copy-done.12, bf16[32,128,128]{2,1,0:T(8,128)(2,1)S(1)} %copy-done.10, bf16[1024,768]{1,0:T(8,128)(2,1)S(1)} %copy-done), custom_call_target="tpu_custom_call" | custom-call | flops 1610612736 | bytes 4194304 | tf_op jit(solution)/shard_map/pallas_call | solution.py:192
  14.1 1.6 %collective-permute-start.1 = (bf16[2,96,512]{2,1,0:T(8,128)(2,1)S(1)}, bf16[2,96,512]{2,1,0:T(8,128)(2,1)S(1)}, u32[]{:S(2)}, u32[]{:S(2)}) collective-permute-start(bf16[2,96,512]{2,1,0:T(8,128)(2,1)S(1)} %maximum_bitcast_fusion), channel_id=1, source_target_pairs={{0,2},{1,3},{2,0},{3,1},{4,6},{5,7},{6,4},{7,5},{8,10},{9,11},{10,... | collective-permute-start | bytes 589832 | tf_op jit(solution)/shard_map/ppermute | solution.py:19
  15.8 4.3 %all-to-all-start = ((bf16[8,128,768]{2,1,0:T(8,128)(2,1)}), bf16[8,128,768]{2,1,0:T(8,128)(2,1)}, u32[]{:S(2)}, u32[]{:S(2)}) async-start(bf16[8,128,768]{2,1,0:T(8,128)(2,1)} %bitcast.13), calls=%async_computation | async-start | bytes 3145728 | tf_op jit(solution)/shard_map/all_to_all | solution.py:201
  20.7 1.6 %collective-permute-start.13 = (bf16[4,96,256]{2,1,0:T(8,128)(2,1)S(1)}, bf16[4,96,256]{2,1,0:T(8,128)(2,1)S(1)}, u32[]{:S(2)}, u32[]{:S(2)}) collective-permute-start(bf16[4,96,256]{2,1,0:T(8,128)(2,1)S(1)} %get-tuple-element.28), channel_id=1, source_target_pairs={{0,16},{8,24},{16,0},{24,8},{1,17},{9,25},{17,1},{25,9},{2,18},{10... | collective-permute-start | bytes 589832 | tf_op jit(solution)/shard_map/ppermute | solution.py:19
  22.3 1.5 %collective-permute-start.2 = (bf16[4,96,256]{2,1,0:T(8,128)(2,1)S(1)}, bf16[4,96,256]{2,1,0:T(8,128)(2,1)S(1)}, u32[]{:S(2)}, u32[]{:S(2)}) collective-permute-start(bf16[4,96,256]{2,1,0:T(8,128)(2,1)S(1)} %get-tuple-element.29), channel_id=1, source_target_pairs={{0,1},{1,0},{2,3},{3,2},{4,5},{5,4},{6,7},{7,6},{8,9},{9,8},{10,11... | collective-permute-start | bytes 589832 | tf_op jit(solution)/shard_map/ppermute | solution.py:19
  23.7 2.7 %collective-permute-done.13 = bf16[4,96,256]{2,1,0:T(8,128)(2,1)S(1)} collective-permute-done((bf16[4,96,256]{2,1,0:T(8,128)(2,1)S(1)}, bf16[4,96,256]{2,1,0:T(8,128)(2,1)S(1)}, u32[]{:S(2)}, u32[]{:S(2)}) %collective-permute-start.13) | collective-permute-done | bytes 196640 | tf_op jit(solution)/shard_map/ppermute | solution.py:19
  26.4 11.7 %collective-permute-done.2 = bf16[4,96,256]{2,1,0:T(8,128)(2,1)S(1)} collective-permute-done((bf16[4,96,256]{2,1,0:T(8,128)(2,1)S(1)}, bf16[4,96,256]{2,1,0:T(8,128)(2,1)S(1)}, u32[]{:S(2)}, u32[]{:S(2)}) %collective-permute-start.2) | collective-permute-done | bytes 196640 | tf_op jit(solution)/shard_map/ppermute | solution.py:19
  38.3 1.6 %collective-permute-start.3 = (bf16[768,256]{1,0:T(8,128)(2,1)S(1)}, bf16[768,256]{1,0:T(8,128)(2,1)S(1)}, u32[]{:S(2)}, u32[]{:S(2)}) collective-permute-start(bf16[768,256]{1,0:T(8,128)(2,1)S(1)} %bitcast.118), channel_id=1, source_target_pairs={{0,16},{8,24},{16,0},{24,8},{1,17},{9,25},{17,1},{25,9},{2,18},{10... | collective-permute-start | bytes 1179656 | tf_op jit(solution)/shard_map/ppermute | solution.py:19
  39.9 2.5 %collective-permute-start.14 = (bf16[4,96,512]{2,1,0:T(8,128)(2,1)S(1)}, bf16[4,96,512]{2,1,0:T(8,128)(2,1)S(1)}, u32[]{:S(2)}, u32[]{:S(2)}) collective-permute-start(bf16[4,96,512]{2,1,0:T(8,128)(2,1)S(1)} %pad_maximum_fusion.4), channel_id=1, source_target_pairs={{0,1},{1,0},{2,3},{3,2},{4,5},{5,4},{6,7},{7,6},{8,9},{9,8},{10,11... | collective-permute-start | bytes 1179656 | tf_op jit(solution)/shard_map/ppermute | solution.py:19
  42.5 5.4 %collective-permute-done.3 = bf16[768,256]{1,0:T(8,128)(2,1)S(1)} collective-permute-done((bf16[768,256]{1,0:T(8,128)(2,1)S(1)}, bf16[768,256]{1,0:T(8,128)(2,1)S(1)}, u32[]{:S(2)}, u32[]{:S(2)}) %collective-permute-start.3) | collective-permute-done | bytes 393248 | tf_op jit(solution)/shard_map/ppermute | solution.py:19
  48.9 4.7 %collective-permute-done.14 = bf16[4,96,512]{2,1,0:T(8,128)(2,1)S(1)} collective-permute-done((bf16[4,96,512]{2,1,0:T(8,128)(2,1)S(1)}, bf16[4,96,512]{2,1,0:T(8,128)(2,1)S(1)}, u32[]{:S(2)}, u32[]{:S(2)}) %collective-permute-start.14) | collective-permute-done | bytes 393248 | tf_op jit(solution)/shard_map/ppermute | solution.py:19
  55.6 1.5 %fusion.33 = (bf16[1024,512]{1,0:T(8,128)(2,1)}, bf16[1024,512]{1,0:T(8,128)(2,1)}) fusion(bf16[1024,1024]{1,0:T(8,128)(2,1)S(1)} %copy-done.13), kind=kLoop, calls=%fused_computation.108 | loop fusion | bytes 4194304 | tf_op jit(solution)/shard_map/slice | solution.py:227
  57.9 2.4 %shard_map.96.total_ref = f32[1024,512]{1,0:T(8,128)S(1)} custom-call(s32[1]{0:T(128)} %bitcast.core_ref.use_ref, bf16[1024,768]{1,0:T(8,128)(2,1)S(1)} %copy-done.1, bf16[768,512]{1,0:T(8,128)(2,1)} %pad_maximum_fusion.mine_ref, bf16[768,512]{1,0:T(8,128)(2,1)} %collective-permute-done.4.other_ref), custom_call_target="tpu_custom_call" | custom-call | flops 805306368 | bytes 2097152 | tf_op jit(solution)/shard_map/pallas_call | solution.py:216
  61.6 1.6 %copy-done.4 = f32[1024,512]{1,0:T(8,128)S(1)} copy-done((f32[1024,512]{1,0:T(8,128)S(1)}, f32[1024,512]{1,0:T(8,128)}, u32[]{:S(2)}) %copy-start.4) | copy-done | bytes 2097176
  64.4 4.3 %shard_map.97 = (bf16[1024,768]{1,0:T(8,128)(2,1)S(1)}, bf16[1024,512]{1,0:T(8,128)(2,1)S(1)}) custom-call(s32[1]{0:T(128)} %bitcast.core_ref.use_ref, s32[8]{0:T(128)S(1)} %copy-done.9, bf16[1024,512]{1,0:T(8,128)(2,1)S(1)} %copy-done.7, f32[1024,512]{1,0:T(8,128)S(1)} %copy-done.4, bf16[768,512]{1,0:T(8,128)(2,1)} %pad_maximum_fusion.mine_ref, ...), custom_call_target="tpu_custom_call" | custom-call | flops 805306368 | bytes 2097152 | tf_op jit(solution)/shard_map/pallas_call | solution.py:251
  68.7 1.9 %shard_map.99 = bf16[768,512]{1,0:T(8,128)(2,1)} custom-call(s32[1]{0:T(128)S(6)} %sub.28.use_ref, bf16[768,1024]{1,0:T(8,128)(2,1)S(1)} %bitcast.110, bf16[1024,768]{1,0:T(8,128)(2,1)S(1)} %get-tuple-element.8.aggregate_ref, bf16[1024,512]{1,0:T(8,128)(2,1)S(1)} %get-tuple-element.9.grad_ref), custom_call_target="tpu_custom_call" | custom-call | flops 805306368 | bytes 786432 | tf_op jit(solution)/shard_map/pallas_call | solution.py:231
  72.1 2.4 %shard_map.100.total_ref = f32[1024,512]{1,0:T(8,128)S(1)} custom-call(s32[1]{0:T(128)} %bitcast.core_ref.use_ref, bf16[1024,768]{1,0:T(8,128)(2,1)S(1)} %copy-done.2, bf16[768,512]{1,0:T(8,128)(2,1)} %bitcast.29.mine_ref, bf16[768,512]{1,0:T(8,128)(2,1)} %collective-permute-done.15.other_ref), custom_call_target="tpu_custom_call" | custom-call | flops 805306368 | bytes 2097152 | tf_op jit(solution)/shard_map/pallas_call | solution.py:216
  74.5 3.2 %shard_map.101.grad_ref = bf16[1024,512]{1,0:T(8,128)(2,1)S(1)} custom-call(s32[1]{0:T(128)} %bitcast.core_ref.use_ref, bf16[1024,512]{1,0:T(8,128)(2,1)S(1)} %copy-done.8, f32[1024,512]{1,0:T(8,128)S(1)} %shard_map.100.total_ref, bf16[768,512]{1,0:T(8,128)(2,1)} %bitcast.29.mine_ref, bf16[768,512]{1,0:T(8,128)(2,1)} %collective-permute-done.15.other_ref, ...), custom_call_target="tpu_custom_call" | custom-call | flops 805306368 | bytes 2097152 | tf_op jit(solution)/shard_map/pallas_call | solution.py:260
  84.3 1.6 %collective-permute-start.19 = (bf16[8,96,128]{2,1,0:T(8,128)(2,1)S(1)}, bf16[8,96,128]{2,1,0:T(8,128)(2,1)S(1)}, u32[]{:S(2)}, u32[]{:S(2)}) collective-permute-start(bf16[8,96,128]{2,1,0:T(8,128)(2,1)S(1)} %constant_dynamic-slice_fusion), channel_id=1, source_target_pairs={{0,16},{8,24},{16,0},{24,8},{1,17},{9,25},{17,1},{25,9},{2,18},{10... | collective-permute-start | bytes 589832 | tf_op jit(solution)/shard_map/ppermute | solution.py:19
  86.0 1.5 %collective-permute-start.17 = (bf16[4,96,256]{2,1,0:T(8,128)(2,1)S(1)}, bf16[4,96,256]{2,1,0:T(8,128)(2,1)S(1)}, u32[]{:S(2)}, u32[]{:S(2)}) collective-permute-start(bf16[4,96,256]{2,1,0:T(8,128)(2,1)S(1)} %dynamic-slice_bitcast_fusion), channel_id=1, source_target_pairs={{0,1},{1,0},{2,3},{3,2},{4,5},{5,4},{6,7},{7,6},{8,9},{9,8},{10,11... | collective-permute-start | bytes 589832 | tf_op jit(solution)/shard_map/ppermute | solution.py:19
  87.5 3.1 %collective-permute-done.8 = bf16[8,96,128]{2,1,0:T(8,128)(2,1)S(1)} collective-permute-done((bf16[8,96,128]{2,1,0:T(8,128)(2,1)S(1)}, bf16[8,96,128]{2,1,0:T(8,128)(2,1)S(1)}, u32[]{:S(2)}, u32[]{:S(2)}) %collective-permute-start.8) | collective-permute-done | bytes 196640 | tf_op jit(solution)/shard_map/ppermute | solution.py:19
  92.9 1.9 %collective-permute-done.19 = bf16[8,96,128]{2,1,0:T(8,128)(2,1)S(1)} collective-permute-done((bf16[8,96,128]{2,1,0:T(8,128)(2,1)S(1)}, bf16[8,96,128]{2,1,0:T(8,128)(2,1)S(1)}, u32[]{:S(2)}, u32[]{:S(2)}) %collective-permute-start.19) | collective-permute-done | bytes 196640 | tf_op jit(solution)/shard_map/ppermute | solution.py:19
  97.8 3.9 %collective-permute-start.10 = (bf16[96,256]{1,0:T(8,128)(2,1)S(1)}, bf16[96,256]{1,0:T(8,128)(2,1)S(1)}, u32[]{:S(2)}, u32[]{:S(2)}) collective-permute-start(bf16[96,256]{1,0:T(8,128)(2,1)S(1)} %get-tuple-element.38), channel_id=1, source_target_pairs={{0,2},{1,3},{2,0},{3,1},{4,6},{5,7},{6,4},{7,5},{8,10},{9,11},{10,... | collective-permute-start | bytes 147464 | tf_op jit(solution)/shard_map/ppermute | solution.py:19
  102.2 2.0 %collective-permute-start.12 = (bf16[96,256]{1,0:T(8,128)(2,1)S(1)}, bf16[96,256]{1,0:T(8,128)(2,1)S(1)}, u32[]{:S(2)}, u32[]{:S(2)}) collective-permute-start(bf16[96,256]{1,0:T(8,128)(2,1)S(1)} %get-tuple-element.40), channel_id=1, source_target_pairs={{0,6},{1,7},{2,4},{3,5},{4,2},{5,3},{6,0},{7,1},{8,14},{9,15},{10,... | collective-permute-start | bytes 147464 | tf_op jit(solution)/shard_map/ppermute | solution.py:19
  106.8 2.0 %collective-permute-start.23 = (bf16[96,256]{1,0:T(8,128)(2,1)S(1)}, bf16[96,256]{1,0:T(8,128)(2,1)S(1)}, u32[]{:S(2)}, u32[]{:S(2)}) collective-permute-start(bf16[96,256]{1,0:T(8,128)(2,1)S(1)} %get-tuple-element.43), channel_id=1, source_target_pairs={{0,6},{1,7},{2,4},{3,5},{4,2},{5,3},{6,0},{7,1},{8,14},{9,15},{10,... | collective-permute-start | bytes 147464 | tf_op jit(solution)/shard_map/ppermute | solution.py:19
  109.4 1.6 %collective-permute-done.22 = bf16[96,256]{1,0:T(8,128)(2,1)S(1)} collective-permute-done((bf16[96,256]{1,0:T(8,128)(2,1)S(1)}, bf16[96,256]{1,0:T(8,128)(2,1)S(1)}, u32[]{:S(2)}, u32[]{:S(2)}) %collective-permute-start.22) | collective-permute-done | bytes 49184 | tf_op jit(solution)/shard_map/ppermute | solution.py:19
  110.9 1.7 %collective-permute-done.23 = bf16[96,256]{1,0:T(8,128)(2,1)S(1)} collective-permute-done((bf16[96,256]{1,0:T(8,128)(2,1)S(1)}, bf16[96,256]{1,0:T(8,128)(2,1)S(1)}, u32[]{:S(2)}, u32[]{:S(2)}) %collective-permute-start.23) | collective-permute-done | bytes 49184 | tf_op jit(solution)/shard_map/ppermute | solution.py:19
  112.7 1.6 %collective-permute-start.24 = (bf16[4,96,128]{2,1,0:T(8,128)(2,1)S(1)}, bf16[4,96,128]{2,1,0:T(8,128)(2,1)S(1)}, u32[]{:S(2)}, u32[]{:S(2)}) collective-permute-start(bf16[4,96,128]{2,1,0:T(8,128)(2,1)S(1)} %pad_maximum_fusion.6), channel_id=1, source_target_pairs={{0,16},{8,24},{16,0},{24,8},{1,17},{9,25},{17,1},{25,9},{2,18},{10... | collective-permute-start | bytes 294920 | tf_op jit(solution)/shard_map/ppermute | solution.py:19
  114.3 3.1 %collective-permute-done.24 = bf16[4,96,128]{2,1,0:T(8,128)(2,1)S(1)} collective-permute-done((bf16[4,96,128]{2,1,0:T(8,128)(2,1)S(1)}, bf16[4,96,128]{2,1,0:T(8,128)(2,1)S(1)}, u32[]{:S(2)}, u32[]{:S(2)}) %collective-permute-start.24) | collective-permute-done | bytes 98336 | tf_op jit(solution)/shard_map/ppermute | solution.py:19
  117.6 1.4 %collective-permute-done.25 = bf16[96,1024]{1,0:T(8,128)(2,1)S(1)} collective-permute-done((bf16[96,1024]{1,0:T(8,128)(2,1)S(1)}, bf16[96,1024]{1,0:T(8,128)(2,1)S(1)}, u32[]{:S(2)}, u32[]{:S(2)}) %collective-permute-start.25) | collective-permute-done | bytes 196640 | tf_op jit(solution)/shard_map/ppermute | solution.py:19
  (109 shorter events, 28.8 us)
Async XLA Ops:
  1.7 12.4 %collective-permute-start = (bf16[1,96,512]{2,1,0:T(8,128)(2,1)S(1)}, bf16[1,96,512]{2,1,0:T(8,128)(2,1)S(1)}, u32[]{:S(2)}, u32[]{:S(2)}) collective-permute-start(bf16[1,96,512]{2,1,0:T(8,128)(2,1)S(1)} %maximum_bitcast_fusion.1), channel_id=1, source_target_pairs={{0,4},{1,5},{2,6},{3,7},{4,0},{5,1},{6,2},{7,3},{8,12},{9,13},{10,... | collective-permute-start | bytes 294920 | tf_op jit(solution)/shard_map/ppermute | solution.py:19
  14.1 6.4 %collective-permute-start.1 = (bf16[2,96,512]{2,1,0:T(8,128)(2,1)S(1)}, bf16[2,96,512]{2,1,0:T(8,128)(2,1)S(1)}, u32[]{:S(2)}, u32[]{:S(2)}) collective-permute-start(bf16[2,96,512]{2,1,0:T(8,128)(2,1)S(1)} %maximum_bitcast_fusion), channel_id=1, source_target_pairs={{0,2},{1,3},{2,0},{3,1},{4,6},{5,7},{6,4},{7,5},{8,10},{9,11},{10,... | collective-permute-start | bytes 589832 | tf_op jit(solution)/shard_map/ppermute | solution.py:19
  15.8 45.8 %all-to-all-start = ((bf16[8,128,768]{2,1,0:T(8,128)(2,1)}), bf16[8,128,768]{2,1,0:T(8,128)(2,1)}, u32[]{:S(2)}, u32[]{:S(2)}) async-start(bf16[8,128,768]{2,1,0:T(8,128)(2,1)} %bitcast.13), calls=%async_computation | async-start | bytes 3145728 | tf_op jit(solution)/shard_map/all_to_all | solution.py:201
  20.7 5.7 %collective-permute-start.13 = (bf16[4,96,256]{2,1,0:T(8,128)(2,1)S(1)}, bf16[4,96,256]{2,1,0:T(8,128)(2,1)S(1)}, u32[]{:S(2)}, u32[]{:S(2)}) collective-permute-start(bf16[4,96,256]{2,1,0:T(8,128)(2,1)S(1)} %get-tuple-element.28), channel_id=1, source_target_pairs={{0,16},{8,24},{16,0},{24,8},{1,17},{9,25},{17,1},{25,9},{2,18},{10... | collective-permute-start | bytes 589832 | tf_op jit(solution)/shard_map/ppermute | solution.py:19
  22.3 15.9 %collective-permute-start.2 = (bf16[4,96,256]{2,1,0:T(8,128)(2,1)S(1)}, bf16[4,96,256]{2,1,0:T(8,128)(2,1)S(1)}, u32[]{:S(2)}, u32[]{:S(2)}) collective-permute-start(bf16[4,96,256]{2,1,0:T(8,128)(2,1)S(1)} %get-tuple-element.29), channel_id=1, source_target_pairs={{0,1},{1,0},{2,3},{3,2},{4,5},{5,4},{6,7},{7,6},{8,9},{9,8},{10,11... | collective-permute-start | bytes 589832 | tf_op jit(solution)/shard_map/ppermute | solution.py:19
  38.3 9.5 %collective-permute-start.3 = (bf16[768,256]{1,0:T(8,128)(2,1)S(1)}, bf16[768,256]{1,0:T(8,128)(2,1)S(1)}, u32[]{:S(2)}, u32[]{:S(2)}) collective-permute-start(bf16[768,256]{1,0:T(8,128)(2,1)S(1)} %bitcast.118), channel_id=1, source_target_pairs={{0,16},{8,24},{16,0},{24,8},{1,17},{9,25},{17,1},{25,9},{2,18},{10... | collective-permute-start | bytes 1179656 | tf_op jit(solution)/shard_map/ppermute | solution.py:19
  39.9 13.6 %collective-permute-start.14 = (bf16[4,96,512]{2,1,0:T(8,128)(2,1)S(1)}, bf16[4,96,512]{2,1,0:T(8,128)(2,1)S(1)}, u32[]{:S(2)}, u32[]{:S(2)}) collective-permute-start(bf16[4,96,512]{2,1,0:T(8,128)(2,1)S(1)} %pad_maximum_fusion.4), channel_id=1, source_target_pairs={{0,1},{1,0},{2,3},{3,2},{4,5},{5,4},{6,7},{7,6},{8,9},{9,8},{10,11... | collective-permute-start | bytes 1179656 | tf_op jit(solution)/shard_map/ppermute | solution.py:19
  48.9 9.0 %collective-permute-start.4 = (bf16[768,512]{1,0:T(8,128)(2,1)}, bf16[768,512]{1,0:T(8,128)(2,1)}, u32[]{:S(2)}, u32[]{:S(2)}) collective-permute-start(bf16[768,512]{1,0:T(8,128)(2,1)} %pad_maximum_fusion.mine_ref), channel_id=1, source_target_pairs={{0,8},{8,0},{16,24},{24,16},{1,9},{9,1},{17,25},{25,17},{2,10},{10... | collective-permute-start | bytes 2359304 | tf_op jit(solution)/shard_map/ppermute | solution.py:19
  53.7 1.9 %copy-start.13 = (bf16[1024,1024]{1,0:T(8,128)(2,1)S(1)}, bf16[1024,1024]{1,0:T(8,128)(2,1)}, u32[]{:S(2)}) copy-start(bf16[1024,1024]{1,0:T(8,128)(2,1)} %param.9) | copy-start | bytes 6291460
  54.8 2.3 %copy-start.1 = (bf16[1024,768]{1,0:T(8,128)(2,1)S(1)}, bf16[1024,768]{1,0:T(8,128)(2,1)}, u32[]{:S(2)}) copy-start(bf16[1024,768]{1,0:T(8,128)(2,1)} %features_ref.5) | copy-start | bytes 4718596
  54.8 15.9 %collective-permute-start.15 = (bf16[768,512]{1,0:T(8,128)(2,1)}, bf16[768,512]{1,0:T(8,128)(2,1)}, u32[]{:S(2)}, u32[]{:S(2)}) collective-permute-start(bf16[768,512]{1,0:T(8,128)(2,1)} %bitcast.29.mine_ref), channel_id=1, source_target_pairs={{0,8},{8,0},{16,24},{24,16},{1,9},{9,1},{17,25},{25,17},{2,10},{10... | collective-permute-start | bytes 2359304 | tf_op jit(solution)/shard_map/ppermute | solution.py:19
  57.8 3.7 %copy-start.9 = (s32[8]{0:T(128)S(1)}, s32[8]{0:T(128)}, u32[]{:S(2)}) copy-start(s32[8]{0:T(128)} %into_ref.1) | copy-start | bytes 100
  68.7 1.9 %copy-start.5 = (bf16[1024,512]{1,0:T(8,128)(2,1)}, bf16[1024,512]{1,0:T(8,128)(2,1)S(1)}, u32[]{:S(2)}) copy-start(bf16[1024,512]{1,0:T(8,128)(2,1)S(1)} %get-tuple-element.9.grad_ref) | copy-start | bytes 3145732
  70.7 10.6 %collective-permute-start.5 = (bf16[768,512]{1,0:T(8,128)(2,1)}, bf16[768,512]{1,0:T(8,128)(2,1)}, u32[]{:S(2)}, u32[]{:S(2)}) collective-permute-start(bf16[768,512]{1,0:T(8,128)(2,1)} %shard_map.99), channel_id=1, source_target_pairs={{0,8},{8,0},{16,24},{24,16},{1,9},{9,1},{17,25},{25,17},{2,10},{10... | collective-permute-start | bytes 2359304 | tf_op jit(solution)/shard_map/ppermute | solution.py:19
  72.1 2.4 %copy-start.8 = (bf16[1024,512]{1,0:T(8,128)(2,1)S(1)}, bf16[1024,512]{1,0:T(8,128)(2,1)}, u32[]{:S(2)}) copy-start(bf16[1024,512]{1,0:T(8,128)(2,1)} %get-tuple-element.10.cotangent_ref) | copy-start | bytes 3145732
  78.7 5.2 %collective-permute-start.16 = (bf16[768,512]{1,0:T(8,128)(2,1)S(1)}, bf16[768,512]{1,0:T(8,128)(2,1)S(1)}, u32[]{:S(2)}, u32[]{:S(2)}) collective-permute-start(bf16[768,512]{1,0:T(8,128)(2,1)S(1)} %shard_map.103), channel_id=1, source_target_pairs={{0,8},{8,0},{16,24},{24,16},{1,9},{9,1},{17,25},{25,17},{2,10},{10... | collective-permute-start | bytes 2359304 | tf_op jit(solution)/shard_map/ppermute | solution.py:19
  82.8 7.8 %collective-permute-start.8 = (bf16[8,96,128]{2,1,0:T(8,128)(2,1)S(1)}, bf16[8,96,128]{2,1,0:T(8,128)(2,1)S(1)}, u32[]{:S(2)}, u32[]{:S(2)}) collective-permute-start(bf16[8,96,128]{2,1,0:T(8,128)(2,1)S(1)} %constant_dynamic-slice_fusion.2), channel_id=1, source_target_pairs={{0,16},{8,24},{16,0},{24,8},{1,17},{9,25},{17,1},{25,9},{2,18},{10... | collective-permute-start | bytes 589832 | tf_op jit(solution)/shard_map/ppermute | solution.py:19
  83.9 7.8 %collective-permute-start.6 = (bf16[4,96,256]{2,1,0:T(8,128)(2,1)S(1)}, bf16[4,96,256]{2,1,0:T(8,128)(2,1)S(1)}, u32[]{:S(2)}, u32[]{:S(2)}) collective-permute-start(bf16[4,96,256]{2,1,0:T(8,128)(2,1)S(1)} %dynamic-slice_bitcast_fusion.1), channel_id=1, source_target_pairs={{0,1},{1,0},{2,3},{3,2},{4,5},{5,4},{6,7},{7,6},{8,9},{9,8},{10,11... | collective-permute-start | bytes 589832 | tf_op jit(solution)/shard_map/ppermute | solution.py:19
  84.3 10.5 %collective-permute-start.19 = (bf16[8,96,128]{2,1,0:T(8,128)(2,1)S(1)}, bf16[8,96,128]{2,1,0:T(8,128)(2,1)S(1)}, u32[]{:S(2)}, u32[]{:S(2)}) collective-permute-start(bf16[8,96,128]{2,1,0:T(8,128)(2,1)S(1)} %constant_dynamic-slice_fusion), channel_id=1, source_target_pairs={{0,16},{8,24},{16,0},{24,8},{1,17},{9,25},{17,1},{25,9},{2,18},{10... | collective-permute-start | bytes 589832 | tf_op jit(solution)/shard_map/ppermute | solution.py:19
  86.0 10.0 %collective-permute-start.17 = (bf16[4,96,256]{2,1,0:T(8,128)(2,1)S(1)}, bf16[4,96,256]{2,1,0:T(8,128)(2,1)S(1)}, u32[]{:S(2)}, u32[]{:S(2)}) collective-permute-start(bf16[4,96,256]{2,1,0:T(8,128)(2,1)S(1)} %dynamic-slice_bitcast_fusion), channel_id=1, source_target_pairs={{0,1},{1,0},{2,3},{3,2},{4,5},{5,4},{6,7},{7,6},{8,9},{9,8},{10,11... | collective-permute-start | bytes 589832 | tf_op jit(solution)/shard_map/ppermute | solution.py:19
  90.7 7.1 %collective-permute-start.9 = (bf16[4,96,128]{2,1,0:T(8,128)(2,1)S(1)}, bf16[4,96,128]{2,1,0:T(8,128)(2,1)S(1)}, u32[]{:S(2)}, u32[]{:S(2)}) collective-permute-start(bf16[4,96,128]{2,1,0:T(8,128)(2,1)S(1)} %dynamic-slice_bitcast_fusion.3), channel_id=1, source_target_pairs={{0,1},{1,0},{2,3},{3,2},{4,5},{5,4},{6,7},{7,6},{8,9},{9,8},{10,11... | collective-permute-start | bytes 294920 | tf_op jit(solution)/shard_map/ppermute | solution.py:19
  91.8 5.9 %collective-permute-start.7 = (bf16[4,96,128]{2,1,0:T(8,128)(2,1)S(1)}, bf16[4,96,128]{2,1,0:T(8,128)(2,1)S(1)}, u32[]{:S(2)}, u32[]{:S(2)}) collective-permute-start(bf16[4,96,128]{2,1,0:T(8,128)(2,1)S(1)} %constant_dynamic-slice_fusion.3), channel_id=1, source_target_pairs={{0,16},{8,24},{16,0},{24,8},{1,17},{9,25},{17,1},{25,9},{2,18},{10... | collective-permute-start | bytes 294920 | tf_op jit(solution)/shard_map/ppermute | solution.py:19
  94.9 9.3 %collective-permute-start.20 = (bf16[4,96,128]{2,1,0:T(8,128)(2,1)S(1)}, bf16[4,96,128]{2,1,0:T(8,128)(2,1)S(1)}, u32[]{:S(2)}, u32[]{:S(2)}) collective-permute-start(bf16[4,96,128]{2,1,0:T(8,128)(2,1)S(1)} %dynamic-slice_bitcast_fusion.2), channel_id=1, source_target_pairs={{0,1},{1,0},{2,3},{3,2},{4,5},{5,4},{6,7},{7,6},{8,9},{9,8},{10,11... | collective-permute-start | bytes 294920 | tf_op jit(solution)/shard_map/ppermute | solution.py:19
  96.0 8.2 %collective-permute-start.18 = (bf16[4,96,128]{2,1,0:T(8,128)(2,1)S(1)}, bf16[4,96,128]{2,1,0:T(8,128)(2,1)S(1)}, u32[]{:S(2)}, u32[]{:S(2)}) collective-permute-start(bf16[4,96,128]{2,1,0:T(8,128)(2,1)S(1)} %constant_dynamic-slice_fusion.1), channel_id=1, source_target_pairs={{0,16},{8,24},{16,0},{24,8},{1,17},{9,25},{17,1},{25,9},{2,18},{10... | collective-permute-start | bytes 294920 | tf_op jit(solution)/shard_map/ppermute | solution.py:19
  97.8 8.9 %collective-permute-start.10 = (bf16[96,256]{1,0:T(8,128)(2,1)S(1)}, bf16[96,256]{1,0:T(8,128)(2,1)S(1)}, u32[]{:S(2)}, u32[]{:S(2)}) collective-permute-start(bf16[96,256]{1,0:T(8,128)(2,1)S(1)} %get-tuple-element.38), channel_id=1, source_target_pairs={{0,2},{1,3},{2,0},{3,1},{4,6},{5,7},{6,4},{7,5},{8,10},{9,11},{10,... | collective-permute-start | bytes 147464 | tf_op jit(solution)/shard_map/ppermute | solution.py:19
  101.7 7.0 %collective-permute-start.11 = (bf16[96,256]{1,0:T(8,128)(2,1)S(1)}, bf16[96,256]{1,0:T(8,128)(2,1)S(1)}, u32[]{:S(2)}, u32[]{:S(2)}) collective-permute-start(bf16[96,256]{1,0:T(8,128)(2,1)S(1)} %get-tuple-element.39), channel_id=1, source_target_pairs={{0,4},{1,5},{2,6},{3,7},{4,0},{5,1},{6,2},{7,3},{8,12},{9,13},{10,... | collective-permute-start | bytes 147464 | tf_op jit(solution)/shard_map/ppermute | solution.py:19
  102.2 6.6 %collective-permute-start.12 = (bf16[96,256]{1,0:T(8,128)(2,1)S(1)}, bf16[96,256]{1,0:T(8,128)(2,1)S(1)}, u32[]{:S(2)}, u32[]{:S(2)}) collective-permute-start(bf16[96,256]{1,0:T(8,128)(2,1)S(1)} %get-tuple-element.40), channel_id=1, source_target_pairs={{0,6},{1,7},{2,4},{3,5},{4,2},{5,3},{6,0},{7,1},{8,14},{9,15},{10,... | collective-permute-start | bytes 147464 | tf_op jit(solution)/shard_map/ppermute | solution.py:19
  104.3 5.1 %collective-permute-start.21 = (bf16[96,256]{1,0:T(8,128)(2,1)S(1)}, bf16[96,256]{1,0:T(8,128)(2,1)S(1)}, u32[]{:S(2)}, u32[]{:S(2)}) collective-permute-start(bf16[96,256]{1,0:T(8,128)(2,1)S(1)} %get-tuple-element.41), channel_id=1, source_target_pairs={{0,2},{1,3},{2,0},{3,1},{4,6},{5,7},{6,4},{7,5},{8,10},{9,11},{10,... | collective-permute-start | bytes 147464 | tf_op jit(solution)/shard_map/ppermute | solution.py:19
  105.4 5.6 %collective-permute-start.22 = (bf16[96,256]{1,0:T(8,128)(2,1)S(1)}, bf16[96,256]{1,0:T(8,128)(2,1)S(1)}, u32[]{:S(2)}, u32[]{:S(2)}) collective-permute-start(bf16[96,256]{1,0:T(8,128)(2,1)S(1)} %get-tuple-element.42), channel_id=1, source_target_pairs={{0,4},{1,5},{2,6},{3,7},{4,0},{5,1},{6,2},{7,3},{8,12},{9,13},{10,... | collective-permute-start | bytes 147464 | tf_op jit(solution)/shard_map/ppermute | solution.py:19
  106.8 5.9 %collective-permute-start.23 = (bf16[96,256]{1,0:T(8,128)(2,1)S(1)}, bf16[96,256]{1,0:T(8,128)(2,1)S(1)}, u32[]{:S(2)}, u32[]{:S(2)}) collective-permute-start(bf16[96,256]{1,0:T(8,128)(2,1)S(1)} %get-tuple-element.43), channel_id=1, source_target_pairs={{0,6},{1,7},{2,4},{3,5},{4,2},{5,3},{6,0},{7,1},{8,14},{9,15},{10,... | collective-permute-start | bytes 147464 | tf_op jit(solution)/shard_map/ppermute | solution.py:19
  112.7 4.7 %collective-permute-start.24 = (bf16[4,96,128]{2,1,0:T(8,128)(2,1)S(1)}, bf16[4,96,128]{2,1,0:T(8,128)(2,1)S(1)}, u32[]{:S(2)}, u32[]{:S(2)}) collective-permute-start(bf16[4,96,128]{2,1,0:T(8,128)(2,1)S(1)} %pad_maximum_fusion.6), channel_id=1, source_target_pairs={{0,16},{8,24},{16,0},{24,8},{1,17},{9,25},{17,1},{25,9},{2,18},{10... | collective-permute-start | bytes 294920 | tf_op jit(solution)/shard_map/ppermute | solution.py:19
  117.5 1.5 %collective-permute-start.25 = (bf16[96,1024]{1,0:T(8,128)(2,1)S(1)}, bf16[96,1024]{1,0:T(8,128)(2,1)S(1)}, u32[]{:S(2)}, u32[]{:S(2)}) collective-permute-start(bf16[96,1024]{1,0:T(8,128)(2,1)S(1)} %pad_maximum_fusion.5), channel_id=1, source_target_pairs={{0,8},{8,0},{16,24},{24,16},{1,9},{9,1},{17,25},{25,17},{2,10},{10... | collective-permute-start | bytes 589832 | tf_op jit(solution)/shard_map/ppermute | solution.py:19
  (9 other events, 11.1 us)

commit v3 on v2

v3 whole, which is shorter than its diff:
```python
import functools

import jax
import jax.numpy as jnp
from jax import lax
from jax.experimental import pallas as pl
from jax.experimental.pallas import tpu as pltpu
from jax.sharding import PartitionSpec as P

F32 = jnp.float32
BF16 = jnp.bfloat16
SCALE = 0.7978845608
CUBIC = 0.044715
MIB = 1 << 20
HBM = pl.BlockSpec(memory_space=pltpu.HBM)
SMEM = pl.BlockSpec(memory_space=pltpu.SMEM)
VMEM = pl.BlockSpec(memory_space=pltpu.VMEM)
DMA = pltpu.SemaphoreType.DMA


def swap(value, axis, step):
    size = lax.axis_size(axis)
    return lax.ppermute(value, axis, [(index, index ^ step) for index in range(size)])


def slots_kernel(
    src_hbm, peer_hbm, tiles_hbm, features_hbm, out_hbm, src, peer, tiles, features, dense, out, in_sems, out_sems
):
    copies = [
        pltpu.make_async_copy(source, target, in_sems.at[index])
        for index, (source, target) in enumerate(
            [(src_hbm, src), (peer_hbm, peer), (tiles_hbm, tiles), (features_hbm, features)]
        )
    ]
    for copy in copies:
        copy.start()
    count, block, _ = tiles.shape
    dense[...] = jnp.zeros_like(dense)
    for copy in copies[:3]:
        copy.wait()

    def place(tile, carry):
        row = pl.multiple_of(peer[tile] * block, block)
        column = pl.multiple_of(src[tile] * block, block)
        at = (pl.ds(row, block), pl.ds(column, block))
        dense[at] = dense[at] + tiles[tile].astype(F32)
        return carry

    lax.fori_loop(0, count, place, 0)
    copies[3].wait()
    chunk = 4 * block
    results = []
    for index in range(out.shape[0] // chunk):
        at = slice(index * chunk, (index + 1) * chunk)
        out[at, :] = jnp.dot(dense[at, :].astype(BF16), features[...], preferred_element_type=F32).astype(BF16)
        results.append(pltpu.make_async_copy(out.at[at, :], out_hbm.at[at, :], out_sems.at[index]))
        results[-1].start()
    for result in results:
        result.wait()


def self_kernel(core_ref, features_ref, first_ref, second_ref, other_first_ref, other_second_ref, out_ref):
    rows = features_ref.shape[0]
    half_width = first_ref.shape[1]
    chunk = 256

    def product(*weight_refs):
        def body():
            for first in range(0, rows, chunk):
                at = slice(first, first + chunk)
                for index, weight_ref in enumerate(weight_refs):
                    out_ref[at, index * half_width : (index + 1) * half_width] = jnp.dot(
                        features_ref[at, :], weight_ref[...], preferred_element_type=F32
                    )

        return body

    pl.when(core_ref[0] == 0)(product(first_ref, second_ref))
    pl.when(core_ref[0] != 0)(product(other_first_ref, other_second_ref))


def layer_kernel(
    core_ref,
    into_ref,
    first_ref,
    second_ref,
    other_first_ref,
    other_second_ref,
    slots_hbm,
    total_hbm,
    cotangent_hbm,
    aggregate_ref,
    grad_ref,
    slots,
    total,
    cotangent,
    summed,
    slot_sems,
    row_sems,
):
    senders, block, _ = slots.shape
    rows = aggregate_ref.shape[0]
    half_width = first_ref.shape[1]
    chunk = 256
    arrivals = [
        pltpu.make_async_copy(slots_hbm.at[sender], slots.at[sender], slot_sems.at[sender]) for sender in range(senders)
    ]
    for arrival in arrivals:
        arrival.start()
    streams = []
    for index in range(rows // chunk):
        at = slice(index * chunk, (index + 1) * chunk)
        streams.append(
            [
                pltpu.make_async_copy(total_hbm.at[at, :], total.at[at, :], row_sems.at[0, index]),
                pltpu.make_async_copy(cotangent_hbm.at[at, :], cotangent.at[at, :], row_sems.at[1, index]),
            ]
        )
        for stream in streams[-1]:
            stream.start()
    summed[...] = jnp.zeros_like(summed)
    for sender in range(senders):
        arrivals[sender].wait()
        at = pl.ds(pl.multiple_of(into_ref[sender] * block, block), block)
        summed[at, :] = summed[at, :] + slots[sender].astype(F32)
    aggregate_ref[...] = summed[...].astype(BF16)

    def product(*weight_refs):
        def body():
            for index in range(rows // chunk):
                at = slice(index * chunk, (index + 1) * chunk)
                for stream in streams[index]:
                    stream.wait()
                for half, weight_ref in enumerate(weight_refs):
                    columns = slice(half * half_width, (half + 1) * half_width)
                    value = total[at, columns] + jnp.dot(
                        aggregate_ref[at, :], weight_ref[...], preferred_element_type=F32
                    )
                    square = value * value
                    bend = jnp.tanh(value * (SCALE + SCALE * CUBIC * square))
                    inner = value * (SCALE + 3.0 * SCALE * CUBIC * square)
                    slope = (1.0 + bend) * (0.5 + 0.5 * inner * (1.0 - bend))
                    grad_ref[at, columns] = (cotangent[at, columns].astype(F32) * slope).astype(BF16)

        return body

    pl.when(core_ref[0] == 0)(product(other_first_ref, other_second_ref))
    pl.when(core_ref[0] != 0)(product(first_ref, second_ref))


def term_kernel(half, use_ref, turned_ref, aggregate_ref, grad_ref, *refs):
    out_ref = refs[-1]
    half_width = out_ref.shape[1]
    columns = slice(half * half_width, (half + 1) * half_width)

    def store(value):
        if len(refs) > 1:
            value = value + refs[0][...].astype(F32)
        out_ref[...] = value.astype(BF16)

    @pl.when(use_ref[0] == 0)
    def _():
        store(jnp.dot(turned_ref[...], grad_ref[:, columns], preferred_element_type=F32))

    @pl.when(use_ref[0] != 0)
    def _():
        store(
            lax.dot_general(
                aggregate_ref[...], grad_ref[:, columns], (((0,), (0,)), ((), ())), preferred_element_type=F32
            )
        )


def call(kernel, outs, places, out_places, scratch=(), flops=0, moved=0, vmem=16):
    return pl.pallas_call(
        kernel,
        out_shape=outs,
        in_specs=places,
        out_specs=out_places,
        scratch_shapes=list(scratch),
        compiler_params=pltpu.CompilerParams(vmem_limit_bytes=vmem * MIB),
        cost_estimate=pl.CostEstimate(flops=flops, bytes_accessed=moved, transcendentals=0),
    )


def joined(held, other, upper, axis):
    return jnp.stack([jnp.where(upper, other, held), jnp.where(upper, held, other)], axis=axis)


def gather_low(held, me):
    held = joined(held, swap(held, "dom", 1), (me & 1) != 0, 1)
    return held.reshape(-1, held.shape[-1])


def gather_high(held, high):
    step = 1
    while step < lax.axis_size("rep") // 2:
        other = swap(held, "rep", 2 * step)
        upper = (high & step) != 0
        held = jnp.concatenate([jnp.where(upper, other, held), jnp.where(upper, held, other)], axis=-1)
        step *= 2
    return held


def added(left, right):
    return (left.astype(F32) + right.astype(F32)).astype(BF16)


def half_of(value, axis, which):
    size = value.shape[axis] // 2
    return lax.dynamic_slice_in_dim(value, which * size, size, axis)


def reduce_high(value, high):
    step = lax.axis_size("rep") // 4
    while step:
        upper = (high // step) % 2
        value = added(half_of(value, 2, upper), swap(half_of(value, 2, 1 - upper), "rep", 2 * step))
        step //= 2
    return value


def reduce_low(value, low):
    value = value.reshape(value.shape[0] // 2, 2, *value.shape[1:])
    sent = lax.dynamic_index_in_dim(value, 1 - low, 1, keepdims=False)
    kept = lax.dynamic_index_in_dim(value, low, 1, keepdims=False)
    return added(kept, swap(sent, "dom", 1))


def shards(features, cotangent, w_self, w_neigh, tile_vals, tile_src, tile_peer, in_block):
    dom_size = lax.axis_size("dom")
    rows, width = features.shape
    hidden = w_self.shape[1]
    block = tile_vals.shape[1]
    me = lax.axis_index("dom")
    rep = lax.axis_index("rep")
    parts = lax.axis_size("rep") // 2
    core, high = rep & 1, rep >> 1
    low, place = me & 1, me >> 1
    core_arg = core.astype(jnp.int32).reshape(1)
    half_width = hidden // 2
    share = half_width // parts

    own = jnp.where(core == 0, w_self, w_neigh)
    held = jnp.concatenate(
        [
            lax.dynamic_slice_in_dim(own, high * share, share, 1),
            lax.dynamic_slice_in_dim(own, half_width + high * share, share, 1),
        ],
        axis=1,
    )
    pieces = [held] + [swap(held, "dom", 2 * step) for step in range(1, dom_size // 2)]
    slots = call(
        slots_kernel,
        jax.ShapeDtypeStruct((dom_size * block, width), BF16),
        [HBM] * 4,
        HBM,
        [
            pltpu.SMEM(tile_src.shape, jnp.int32),
            pltpu.SMEM(tile_peer.shape, jnp.int32),
            pltpu.VMEM(tile_vals.shape, BF16),
            pltpu.VMEM(features.shape, BF16),
            pltpu.VMEM((dom_size * block, rows), F32),
            pltpu.VMEM((dom_size * block, width), BF16),
            DMA((4,)),
            DMA((dom_size // 4,)),
        ],
        flops=2 * dom_size * block * rows * width,
        moved=tile_vals.size * 2 + rows * width * 4,
        vmem=16 if dom_size <= 8 else 40,
    )(tile_src, tile_peer, tile_vals, features)
    received = lax.all_to_all(slots.reshape(dom_size, block, width), "dom", split_axis=0, concat_axis=0, tiled=True)

    *pieces, _ = lax.optimization_barrier((*pieces, slots))
    bit = 1
    while len(pieces) > 1:
        upper = (place & bit) != 0
        pieces = [joined(pieces[at], pieces[at + 1], upper, 0) for at in range(0, len(pieces), 2)]
        pieces = [piece.reshape(-1, *held.shape) for piece in pieces]
        bit *= 2
    weights = [
        gather_high(gather_low(pieces[0][..., :share], me), high),
        gather_low(gather_high(pieces[0][..., share:], high), me),
    ]
    weights += [swap(weight, "rep", 1) for weight in weights]
    total = call(
        self_kernel,
        jax.ShapeDtypeStruct((rows, hidden), F32),
        [SMEM] + [VMEM] * 5,
        VMEM,
        flops=2 * rows * width * hidden,
        moved=4 * rows * hidden,
    )(core_arg, features, *weights)
    turned = features.T

    aggregate, grad = call(
        layer_kernel,
        [jax.ShapeDtypeStruct((rows, width), BF16), jax.ShapeDtypeStruct((rows, hidden), BF16)],
        [SMEM, SMEM] + [VMEM] * 4 + [HBM] * 3,
        [VMEM, VMEM],
        [
            pltpu.VMEM((dom_size, block, width), BF16),
            pltpu.VMEM((rows, hidden), F32),
            pltpu.VMEM((rows, hidden), BF16),
            pltpu.VMEM((rows, width), F32),
            DMA((dom_size,)),
            DMA((2, rows // 256)),
        ],
        flops=2 * rows * width * hidden,
        moved=4 * rows * hidden,
        vmem=24 if dom_size <= 8 else 40,
    )(core_arg, in_block, *weights, received, total, cotangent)

    def term(half, use, *others):
        return call(
            functools.partial(term_kernel, half),
            jax.ShapeDtypeStruct((width, half_width), BF16),
            [SMEM] + [VMEM] * (3 + len(others)),
            VMEM,
            flops=2 * rows * width * half_width,
            moved=2 * width * half_width,
        )(use, turned, aggregate, grad, *others)

    others = [swap(term(half, 1 - core_arg), "rep", 1) for half in range(2)]
    first, second = [
        term(half, core_arg, others[half]).reshape(dom_size, width // dom_size, half_width) for half in range(2)
    ]
    first, second = reduce_low(first, low), reduce_high(second, high)
    first, second = reduce_high(first, high), reduce_low(second, low)
    both = jnp.concatenate([first, second], axis=2)
    summed = lax.dynamic_index_in_dim(both, place, 0, keepdims=False).astype(F32)
    for step in range(1, dom_size // 2):
        piece = lax.dynamic_index_in_dim(both, place ^ step, 0, keepdims=False)
        summed = summed + swap(piece, "dom", 2 * step).astype(F32)
    summed = summed.astype(BF16)
    held = gather_high(jnp.stack([summed[:, :share], summed[:, share:]]), high)
    whole = jnp.concatenate([held[0], held[1]], axis=1)
    opposite = swap(whole, "rep", 1)
    return (
        jnp.where(core == 0, whole, opposite).astype(F32),
        jnp.where(core == 0, opposite, whole).astype(F32),
    )


def solution(mesh):
    in_specs = (
        P(("rep", "dom"), None),
        P(("rep", "dom"), None),
        P("dom", None),
        P("dom", None),
        P(("rep", "dom"), None, None),
        P(("rep", "dom")),
        P(("rep", "dom")),
        P(("rep", "dom")),
    )
    out_specs = (P("dom", None), P("dom", None))
    return jax.shard_map(shards, mesh=mesh, in_specs=in_specs, out_specs=out_specs, check_vma=False)
```

time: 121 us -> 131 us (1.083)
  waiting for transfers between devices: 39.9 us -> 51.9 us
  starting transfers between devices: 37.9 us -> 29.7 us
  local copies, waits for them, and re-layouts: 14 us -> 21 us
  other arithmetic: 5.58 us -> 4.01 us
    ppermute x26 -> x20, waiting for transfers between devices: 39.8 us -> 51.9 us  [swap(): lax.ppermute(value, axis, [(index, index ^ step) for index in range(size)])]
    ppermute x26 -> x20, starting transfers between devices: 33.5 us -> 23.7 us  [swap(): lax.ppermute(value, axis, [(index, index ^ step) for index in range(size)])]
    unnamed x29 -> x39, local copies, waits for them, and re-layouts: 11.1 us -> 20 us
    all_to_all x1, starting transfers between devices: 4.3 us -> 6.04 us  [shards(): lax.all_to_all(slots.reshape(dom_size, block, width), 'dom', split_axis=0...]
    slice x4 -> x1, local copies, waits for them, and re-layouts: 1.69 us -> 0.03 us  [shards(): pieces[0][..., share:]]
    pallas_call x8 -> x6, Pallas kernels: 17.2 us -> 18.5 us  [the longest x4 8.03 us: term(): call(functools.partial(term_kernel, half), jax.ShapeDtypeStruct((width, h...]
  transfers between devices with their start and end apart: 27 -> 21, of which waited for: 15 -> 12; matrix products, arithmetic and copies ran while one was open for 6% -> 3% of each run, Pallas kernels for 18% -> 10%
where the time goes in v3:
time: 131 us; the launch traced here: 130 us
  waiting for transfers between devices  51.9 us (40%)
  starting transfers between devices  29.7 us (23%)
  Pallas kernels  22.3 us (17%)
  local copies, waits for them, and re-layouts  21 us (16%)
  other arithmetic  4.01 us (3%)
    ppermute x20, waiting for transfers between devices, swap(): lax.ppermute(value, axis, [(index, index ^ step) for index in range(size)])  51.9 us
    ppermute x20, starting transfers between devices, swap(): lax.ppermute(value, axis, [(index, index ^ step) for index in range(size)])  23.7 us
    unnamed x39, local copies, waits for them, and re-layouts  20 us
    pallas_call x4, Pallas kernels, term(): call(functools.partial(term_kernel, half), jax.ShapeDtypeStruct((width, h...  8.03 us
    pallas_call x1, Pallas kernels, shards(): call(layer_kernel, [jax.ShapeDtypeStruct((rows, width), BF16), jax.ShapeD...  7.3 us
    all_to_all x1, starting transfers between devices, shards(): lax.all_to_all(slots.reshape(dom_size, block, width), 'dom', split_axis=0...  6.04 us
    pallas_call x1, Pallas kernels, shards(): call(slots_kernel, jax.ShapeDtypeStruct((dom_size * block, width), BF16),...  3.84 us
    pallas_call x1, Pallas kernels, shards(): call(self_kernel, jax.ShapeDtypeStruct((rows, hidden), F32), [SMEM] + [VM...  3.16 us
  transfers between devices with their start and end apart: 21, of which 12 were waited for; matrix products, arithmetic and copies ran while one was open for 3% of the time, Pallas kernels for 10%

profile of v3, /device:TPU:0, one launch (start us, length us, event | category | flops | bytes accessed | tf_op | source)
XLA Modules:
  0.0 130.0 jit_solution(5874212004990683043)
XLA Ops:
  1.7 3.1 %collective-permute-start = (bf16[96,512]{1,0:T(8,128)(2,1)S(1)}, bf16[96,512]{1,0:T(8,128)(2,1)S(1)}, u32[]{:S(2)}, u32[]{:S(2)}) collective-permute-start(bf16[96,512]{1,0:T(8,128)(2,1)S(1)} %pad_maximum_fusion.9), channel_id=1, source_target_pairs={{0,2},{1,3},{2,0},{3,1},{4,6},{5,7},{6,4},{7,5},{8,10},{9,11},{10,... | collective-permute-start | bytes 294920 | tf_op jit(solution)/shard_map/ppermute | solution.py:23
  4.7 2.6 %collective-permute-start.1 = (bf16[96,512]{1,0:T(8,128)(2,1)S(1)}, bf16[96,512]{1,0:T(8,128)(2,1)S(1)}, u32[]{:S(2)}, u32[]{:S(2)}) collective-permute-start(bf16[96,512]{1,0:T(8,128)(2,1)S(1)} %pad_maximum_fusion.9), channel_id=1, source_target_pairs={{0,4},{1,5},{2,6},{3,7},{4,0},{5,1},{6,2},{7,3},{8,12},{9,13},{10,... | collective-permute-start | bytes 294920 | tf_op jit(solution)/shard_map/ppermute | solution.py:23
  11.3 3.8 %shard_map.95 = bf16[1024,768]{1,0:T(8,128)(2,1)} custom-call(s32[32]{0:T(128)S(1)} %copy-done.17, s32[32]{0:T(128)S(1)} %copy-done.18, bf16[32,128,128]{2,1,0:T(8,128)(2,1)S(1)} %copy-done.16, bf16[1024,768]{1,0:T(8,128)(2,1)S(1)} %copy-done.9), custom_call_target="tpu_custom_call" | custom-call | flops 1610612736 | bytes 4194304 | tf_op jit(solution)/shard_map/pallas_call | solution.py:253
  15.1 6.0 %all-to-all-start = ((bf16[8,128,768]{2,1,0:T(8,128)(2,1)}), bf16[8,128,768]{2,1,0:T(8,128)(2,1)}, u32[]{:S(2)}, u32[]{:S(2)}) async-start(bf16[8,128,768]{2,1,0:T(8,128)(2,1)} %bitcast.14), calls=%async_computation | async-start | bytes 3145728 | tf_op jit(solution)/shard_map/all_to_all | solution.py:272
  21.4 2.1 %collective-permute-start.3 = (bf16[4,96,256]{2,1,0:T(8,128)(2,1)S(1)}, bf16[4,96,256]{2,1,0:T(8,128)(2,1)S(1)}, u32[]{:S(2)}, u32[]{:S(2)}) collective-permute-start(bf16[4,96,256]{2,1,0:T(8,128)(2,1)S(1)} %get-tuple-element.30), channel_id=1, source_target_pairs={{0,1},{1,0},{2,3},{3,2},{4,5},{5,4},{6,7},{7,6},{8,9},{9,8},{10,11... | collective-permute-start | bytes 589832 | tf_op jit(solution)/shard_map/ppermute | solution.py:23
  23.4 1.5 %collective-permute-start.5 = (bf16[4,96,256]{2,1,0:T(8,128)(2,1)S(1)}, bf16[4,96,256]{2,1,0:T(8,128)(2,1)S(1)}, u32[]{:S(2)}, u32[]{:S(2)}) collective-permute-start(bf16[4,96,256]{2,1,0:T(8,128)(2,1)S(1)} %get-tuple-element.29), channel_id=1, source_target_pairs={{0,16},{8,24},{16,0},{24,8},{1,17},{9,25},{17,1},{25,9},{2,18},{10... | collective-permute-start | bytes 589832 | tf_op jit(solution)/shard_map/ppermute | solution.py:23
  25.0 13.9 %collective-permute-done.3 = bf16[4,96,256]{2,1,0:T(8,128)(2,1)S(1)} collective-permute-done((bf16[4,96,256]{2,1,0:T(8,128)(2,1)S(1)}, bf16[4,96,256]{2,1,0:T(8,128)(2,1)S(1)}, u32[]{:S(2)}, u32[]{:S(2)}) %collective-permute-start.3) | collective-permute-done | bytes 196640 | tf_op jit(solution)/shard_map/ppermute | solution.py:23
  39.0 2.5 %collective-permute-start.6 = (bf16[4,96,512]{2,1,0:T(8,128)(2,1)S(1)}, bf16[4,96,512]{2,1,0:T(8,128)(2,1)S(1)}, u32[]{:S(2)}, u32[]{:S(2)}) collective-permute-start(bf16[4,96,512]{2,1,0:T(8,128)(2,1)S(1)} %pad_maximum_fusion.4), channel_id=1, source_target_pairs={{0,1},{1,0},{2,3},{3,2},{4,5},{5,4},{6,7},{7,6},{8,9},{9,8},{10,11... | collective-permute-start | bytes 1179656 | tf_op jit(solution)/shard_map/ppermute | solution.py:23
  41.6 1.6 %collective-permute-start.4 = (bf16[768,256]{1,0:T(8,128)(2,1)S(1)}, bf16[768,256]{1,0:T(8,128)(2,1)S(1)}, u32[]{:S(2)}, u32[]{:S(2)}) collective-permute-start(bf16[768,256]{1,0:T(8,128)(2,1)S(1)} %bitcast.73), channel_id=1, source_target_pairs={{0,16},{8,24},{16,0},{24,8},{1,17},{9,25},{17,1},{25,9},{2,18},{10... | collective-permute-start | bytes 1179656 | tf_op jit(solution)/shard_map/ppermute | solution.py:23
  43.2 9.9 %collective-permute-done.6 = bf16[4,96,512]{2,1,0:T(8,128)(2,1)S(1)} collective-permute-done((bf16[4,96,512]{2,1,0:T(8,128)(2,1)S(1)}, bf16[4,96,512]{2,1,0:T(8,128)(2,1)S(1)}, u32[]{:S(2)}, u32[]{:S(2)}) %collective-permute-start.6) | collective-permute-done | bytes 393248 | tf_op jit(solution)/shard_map/ppermute | solution.py:23
  54.2 1.7 %copy.14 = bf16[1024,768]{0,1:T(8,128)(2,1)S(1)} copy(bf16[1024,768]{1,0:T(8,128)(2,1)} %features_ref.1) | data formatting | bytes 3145728 | tf_op args[0]
  58.4 3.2 %shard_map.96.total_hbm = f32[1024,1024]{1,0:T(8,128)S(1)} custom-call(s32[1]{0:T(128)} %bitcast.core_ref.use_ref, bf16[1024,768]{1,0:T(8,128)(2,1)S(1)} %copy-done.10, bf16[768,512]{1,0:T(8,128)(2,1)S(1)} %pad_maximum_fusion.first_ref, bf16[768,512]{1,0:T(8,128)(2,1)S(1)} %bitcast.65, bf16[768,512]{1,0:T(8,128)(2,1)} %collective-permute-done.7.other_first_ref, ...), custom_call_target="tpu_custom_call" | custom-call | flops 1610612736 | bytes 4194304 | tf_op jit(solution)/shard_map/pallas_call | solution.py:286
  61.6 2.0 %copy-done.3 = f32[1024,1024]{1,0:T(8,128)} copy-done((f32[1024,1024]{1,0:T(8,128)}, f32[1024,1024]{1,0:T(8,128)S(1)}, u32[]{:S(2)}) %copy-start.3) | copy-done | bytes 4194328
  63.5 2.2 %copy-done.4 = f32[1024,1024]{1,0:T(8,128)S(1)} copy-done((f32[1024,1024]{1,0:T(8,128)S(1)}, f32[1024,1024]{1,0:T(8,128)}, u32[]{:S(2)}) %copy-start.4) | copy-done | bytes 4194328
  68.0 1.6 %copy-done.14 = bf16[1024,1024]{1,0:T(8,128)(2,1)S(1)} copy-done((bf16[1024,1024]{1,0:T(8,128)(2,1)S(1)}, bf16[1024,1024]{1,0:T(8,128)(2,1)}, u32[]{:S(2)}) %copy-start.14) | copy-done | bytes 2097176
  69.6 7.3 %shard_map.97 = (bf16[1024,768]{1,0:T(8,128)(2,1)S(1)}, bf16[1024,1024]{1,0:T(8,128)(2,1)S(1)}) custom-call(s32[1]{0:T(128)} %bitcast.core_ref.use_ref, s32[8]{0:T(128)S(1)} %copy-done.15, bf16[768,512]{1,0:T(8,128)(2,1)S(1)} %copy-done.8, bf16[768,512]{1,0:T(8,128)(2,1)S(1)} %bitcast.66, bf16[768,512]{1,0:T(8,128)(2,1)} %collective-permute-done.7.other_first_ref, ...), custom_call_target="tpu_custom_call" | custom-call | flops 1610612736 | bytes 4194304 | tf_op jit(solution)/shard_map/pallas_call | solution.py:296
  76.9 1.9 %shard_map.100 = bf16[768,512]{1,0:T(8,128)(2,1)} custom-call(s32[1]{0:T(128)S(6)} %sub.15.use_ref, bf16[768,1024]{1,0:T(8,128)(2,1)S(1)} %bitcast.60, bf16[1024,768]{1,0:T(8,128)(2,1)S(1)} %get-tuple-element.12.aggregate_ref, bf16[1024,1024]{1,0:T(8,128)(2,1)S(1)} %get-tuple-element.13.grad_ref), custom_call_target="tpu_custom_call" | custom-call | flops 805306368 | bytes 786432 | tf_op jit(solution)/shard_map/pallas_call | solution.py:315
  78.9 1.9 %shard_map.98 = bf16[768,512]{1,0:T(8,128)(2,1)} custom-call(s32[1]{0:T(128)S(6)} %sub.15.use_ref, bf16[768,1024]{1,0:T(8,128)(2,1)S(1)} %bitcast.61, bf16[1024,768]{1,0:T(8,128)(2,1)S(1)} %get-tuple-element.12.aggregate_ref, bf16[1024,1024]{1,0:T(8,128)(2,1)S(1)} %get-tuple-element.13.grad_ref), custom_call_target="tpu_custom_call" | custom-call | flops 805306368 | bytes 786432 | tf_op jit(solution)/shard_map/pallas_call | solution.py:315
  81.4 1.6 %copy-done.1 = bf16[1024,1024]{1,0:T(8,128)(2,1)S(1)} copy-done((bf16[1024,1024]{1,0:T(8,128)(2,1)S(1)}, bf16[1024,1024]{1,0:T(8,128)(2,1)}, u32[]{:S(2)}) %copy-start.1) | copy-done | bytes 2097176
  83.0 2.1 %shard_map.101 = bf16[768,512]{1,0:T(8,128)(2,1)S(1)} custom-call(s32[1]{0:T(128)} %bitcast.core_ref.use_ref, bf16[768,1024]{1,0:T(8,128)(2,1)S(1)} %bitcast.62, bf16[1024,768]{1,0:T(8,128)(2,1)S(1)} %get-tuple-element.12.aggregate_ref, bf16[1024,1024]{1,0:T(8,128)(2,1)S(1)} %copy-done.1, bf16[768,512]{1,0:T(8,128)(2,1)} %collective-permute-done.12.refs_0_), custom_call_target="tpu_custom_call" | custom-call | flops 805306368 | bytes 786432 | tf_op jit(solution)/shard_map/pallas_call | solution.py:315
  86.8 1.5 %collective-permute-start.13 = (bf16[8,96,256]{2,1,0:T(8,128)(2,1)}, bf16[8,96,256]{2,1,0:T(8,128)(2,1)S(1)}, u32[]{:S(2)}, u32[]{:S(2)}) collective-permute-start(bf16[8,96,256]{2,1,0:T(8,128)(2,1)} %constant_dynamic-slice_fusion), channel_id=1, source_target_pairs={{0,16},{8,24},{16,0},{24,8},{1,17},{9,25},{17,1},{25,9},{2,18},{10... | collective-permute-start | bytes 1179656 | tf_op jit(solution)/shard_map/ppermute | solution.py:23
  88.3 1.6 %copy-done.2 = bf16[1024,1024]{1,0:T(8,128)(2,1)S(1)} copy-done((bf16[1024,1024]{1,0:T(8,128)(2,1)S(1)}, bf16[1024,1024]{1,0:T(8,128)(2,1)}, u32[]{:S(2)}) %copy-start.2) | copy-done | bytes 2097176
  89.9 2.1 %shard_map.99 = bf16[768,512]{1,0:T(8,128)(2,1)S(1)} custom-call(s32[1]{0:T(128)} %bitcast.core_ref.use_ref, bf16[768,1024]{1,0:T(8,128)(2,1)S(1)} %bitcast.63, bf16[1024,768]{1,0:T(8,128)(2,1)S(1)} %get-tuple-element.12.aggregate_ref, bf16[1024,1024]{1,0:T(8,128)(2,1)S(1)} %copy-done.2, bf16[768,512]{1,0:T(8,128)(2,1)} %collective-permute-done.9.refs_0_), custom_call_target="tpu_custom_call" | custom-call | flops 805306368 | bytes 786432 | tf_op jit(solution)/shard_map/pallas_call | solution.py:315
  93.1 5.1 %collective-permute-done.13 = bf16[8,96,256]{2,1,0:T(8,128)(2,1)S(1)} collective-permute-done((bf16[8,96,256]{2,1,0:T(8,128)(2,1)}, bf16[8,96,256]{2,1,0:T(8,128)(2,1)S(1)}, u32[]{:S(2)}, u32[]{:S(2)}) %collective-permute-start.13) | collective-permute-done | bytes 393248 | tf_op jit(solution)/shard_map/ppermute | solution.py:23
  99.4 5.6 %collective-permute-done.10 = bf16[4,96,512]{2,1,0:T(8,128)(2,1)S(1)} collective-permute-done((bf16[4,96,512]{2,1,0:T(8,128)(2,1)S(1)}, bf16[4,96,512]{2,1,0:T(8,128)(2,1)S(1)}, u32[]{:S(2)}, u32[]{:S(2)}) %collective-permute-start.10) | collective-permute-done | bytes 393248 | tf_op jit(solution)/shard_map/ppermute | solution.py:23
  105.8 2.4 %collective-permute-done.14 = bf16[4,96,256]{2,1,0:T(8,128)(2,1)S(1)} collective-permute-done((bf16[4,96,256]{2,1,0:T(8,128)(2,1)S(1)}, bf16[4,96,256]{2,1,0:T(8,128)(2,1)S(1)}, u32[]{:S(2)}, u32[]{:S(2)}) %collective-permute-start.14) | collective-permute-done | bytes 196640 | tf_op jit(solution)/shard_map/ppermute | solution.py:23
  108.3 2.7 %collective-permute-done.11 = bf16[4,96,256]{2,1,0:T(8,128)(2,1)S(1)} collective-permute-done((bf16[4,96,256]{2,1,0:T(8,128)(2,1)S(1)}, bf16[4,96,256]{2,1,0:T(8,128)(2,1)S(1)}, u32[]{:S(2)}, u32[]{:S(2)}) %collective-permute-start.11) | collective-permute-done | bytes 196640 | tf_op jit(solution)/shard_map/ppermute | solution.py:23
  111.0 3.9 %collective-permute-start.15 = (bf16[96,512]{1,0:T(8,128)(2,1)S(1)}, bf16[96,512]{1,0:T(8,128)(2,1)S(1)}, u32[]{:S(2)}, u32[]{:S(2)}) collective-permute-start(bf16[96,512]{1,0:T(8,128)(2,1)S(1)} %get-tuple-element.24), channel_id=1, source_target_pairs={{0,2},{1,3},{2,0},{3,1},{4,6},{5,7},{6,4},{7,5},{8,10},{9,11},{10,... | collective-permute-start | bytes 294920 | tf_op jit(solution)/shard_map/ppermute | solution.py:23
  115.7 1.7 %collective-permute-start.17 = (bf16[96,512]{1,0:T(8,128)(2,1)S(1)}, bf16[96,512]{1,0:T(8,128)(2,1)S(1)}, u32[]{:S(2)}, u32[]{:S(2)}) collective-permute-start(bf16[96,512]{1,0:T(8,128)(2,1)S(1)} %get-tuple-element.26), channel_id=1, source_target_pairs={{0,6},{1,7},{2,4},{3,5},{4,2},{5,3},{6,0},{7,1},{8,14},{9,15},{10,... | collective-permute-start | bytes 294920 | tf_op jit(solution)/shard_map/ppermute | solution.py:23
  117.4 2.0 %collective-permute-done.15 = bf16[96,512]{1,0:T(8,128)(2,1)S(1)} collective-permute-done((bf16[96,512]{1,0:T(8,128)(2,1)S(1)}, bf16[96,512]{1,0:T(8,128)(2,1)S(1)}, u32[]{:S(2)}, u32[]{:S(2)}) %collective-permute-start.15) | collective-permute-done | bytes 98336 | tf_op jit(solution)/shard_map/ppermute | solution.py:23
  119.4 3.2 %collective-permute-done.16 = bf16[96,512]{1,0:T(8,128)(2,1)S(1)} collective-permute-done((bf16[96,512]{1,0:T(8,128)(2,1)S(1)}, bf16[96,512]{1,0:T(8,128)(2,1)S(1)}, u32[]{:S(2)}, u32[]{:S(2)}) %collective-permute-start.16) | collective-permute-done | bytes 98336 | tf_op jit(solution)/shard_map/ppermute | solution.py:23
  123.3 4.1 %collective-permute-done.18 = bf16[2,96,256]{2,1,0:T(8,128)(2,1)S(1)} collective-permute-done((bf16[2,96,256]{2,1,0:T(8,128)(2,1)S(1)}, bf16[2,96,256]{2,1,0:T(8,128)(2,1)S(1)}, u32[]{:S(2)}, u32[]{:S(2)}) %collective-permute-start.18) | collective-permute-done | bytes 98336 | tf_op jit(solution)/shard_map/ppermute | solution.py:23
  (87 shorter events, 20.3 us)
Async XLA Ops:
  1.7 19.5 %collective-permute-start = (bf16[96,512]{1,0:T(8,128)(2,1)S(1)}, bf16[96,512]{1,0:T(8,128)(2,1)S(1)}, u32[]{:S(2)}, u32[]{:S(2)}) collective-permute-start(bf16[96,512]{1,0:T(8,128)(2,1)S(1)} %pad_maximum_fusion.9), channel_id=1, source_target_pairs={{0,2},{1,3},{2,0},{3,1},{4,6},{5,7},{6,4},{7,5},{8,10},{9,11},{10,... | collective-permute-start | bytes 294920 | tf_op jit(solution)/shard_map/ppermute | solution.py:23
  4.7 16.4 %collective-permute-start.1 = (bf16[96,512]{1,0:T(8,128)(2,1)S(1)}, bf16[96,512]{1,0:T(8,128)(2,1)S(1)}, u32[]{:S(2)}, u32[]{:S(2)}) collective-permute-start(bf16[96,512]{1,0:T(8,128)(2,1)S(1)} %pad_maximum_fusion.9), channel_id=1, source_target_pairs={{0,4},{1,5},{2,6},{3,7},{4,0},{5,1},{6,2},{7,3},{8,12},{9,13},{10,... | collective-permute-start | bytes 294920 | tf_op jit(solution)/shard_map/ppermute | solution.py:23
  7.3 13.9 %collective-permute-start.2 = (bf16[96,512]{1,0:T(8,128)(2,1)S(1)}, bf16[96,512]{1,0:T(8,128)(2,1)S(1)}, u32[]{:S(2)}, u32[]{:S(2)}) collective-permute-start(bf16[96,512]{1,0:T(8,128)(2,1)S(1)} %pad_maximum_fusion.9), channel_id=1, source_target_pairs={{0,6},{1,7},{2,4},{3,5},{4,2},{5,3},{6,0},{7,1},{8,14},{9,15},{10,... | collective-permute-start | bytes 294920 | tf_op jit(solution)/shard_map/ppermute | solution.py:23
  15.1 48.4 %all-to-all-start = ((bf16[8,128,768]{2,1,0:T(8,128)(2,1)}), bf16[8,128,768]{2,1,0:T(8,128)(2,1)}, u32[]{:S(2)}, u32[]{:S(2)}) async-start(bf16[8,128,768]{2,1,0:T(8,128)(2,1)} %bitcast.14), calls=%async_computation | async-start | bytes 3145728 | tf_op jit(solution)/shard_map/all_to_all | solution.py:272
  21.4 17.5 %collective-permute-start.3 = (bf16[4,96,256]{2,1,0:T(8,128)(2,1)S(1)}, bf16[4,96,256]{2,1,0:T(8,128)(2,1)S(1)}, u32[]{:S(2)}, u32[]{:S(2)}) collective-permute-start(bf16[4,96,256]{2,1,0:T(8,128)(2,1)S(1)} %get-tuple-element.30), channel_id=1, source_target_pairs={{0,1},{1,0},{2,3},{3,2},{4,5},{5,4},{6,7},{7,6},{8,9},{9,8},{10,11... | collective-permute-start | bytes 589832 | tf_op jit(solution)/shard_map/ppermute | solution.py:23
  23.4 15.5 %collective-permute-start.5 = (bf16[4,96,256]{2,1,0:T(8,128)(2,1)S(1)}, bf16[4,96,256]{2,1,0:T(8,128)(2,1)S(1)}, u32[]{:S(2)}, u32[]{:S(2)}) collective-permute-start(bf16[4,96,256]{2,1,0:T(8,128)(2,1)S(1)} %get-tuple-element.29), channel_id=1, source_target_pairs={{0,16},{8,24},{16,0},{24,8},{1,17},{9,25},{17,1},{25,9},{2,18},{10... | collective-permute-start | bytes 589832 | tf_op jit(solution)/shard_map/ppermute | solution.py:23
  39.0 14.1 %collective-permute-start.6 = (bf16[4,96,512]{2,1,0:T(8,128)(2,1)S(1)}, bf16[4,96,512]{2,1,0:T(8,128)(2,1)S(1)}, u32[]{:S(2)}, u32[]{:S(2)}) collective-permute-start(bf16[4,96,512]{2,1,0:T(8,128)(2,1)S(1)} %pad_maximum_fusion.4), channel_id=1, source_target_pairs={{0,1},{1,0},{2,3},{3,2},{4,5},{5,4},{6,7},{7,6},{8,9},{9,8},{10,11... | collective-permute-start | bytes 1179656 | tf_op jit(solution)/shard_map/ppermute | solution.py:23
  41.6 11.8 %collective-permute-start.4 = (bf16[768,256]{1,0:T(8,128)(2,1)S(1)}, bf16[768,256]{1,0:T(8,128)(2,1)S(1)}, u32[]{:S(2)}, u32[]{:S(2)}) collective-permute-start(bf16[768,256]{1,0:T(8,128)(2,1)S(1)} %bitcast.73), channel_id=1, source_target_pairs={{0,16},{8,24},{16,0},{24,8},{1,17},{9,25},{17,1},{25,9},{2,18},{10... | collective-permute-start | bytes 1179656 | tf_op jit(solution)/shard_map/ppermute | solution.py:23
  53.3 3.6 %copy-start.5 = (bf16[4,2,96,512]{3,2,1,0:T(8,128)(2,1)}, bf16[4,2,96,512]{3,2,1,0:T(8,128)(2,1)S(1)}, u32[]{:S(2)}) copy-start(bf16[4,2,96,512]{3,2,1,0:T(8,128)(2,1)S(1)} %pad_maximum_fusion.1) | copy-start | bytes 2359300
  53.4 2.5 %collective-permute-start.8 = (bf16[768,512]{1,0:T(8,128)(2,1)S(1)}, bf16[768,512]{1,0:T(8,128)(2,1)}, u32[]{:S(2)}, u32[]{:S(2)}) collective-permute-start(bf16[768,512]{1,0:T(8,128)(2,1)S(1)} %bitcast.64), channel_id=1, source_target_pairs={{0,8},{8,0},{16,24},{24,16},{1,9},{9,1},{17,25},{25,17},{2,10},{10... | collective-permute-start | bytes 2359304 | tf_op jit(solution)/shard_map/ppermute | solution.py:23
  53.6 3.4 %copy-start.7 = (bf16[768,512]{1,0:T(8,128)(2,1)}, bf16[768,512]{1,0:T(8,128)(2,1)S(1)}, u32[]{:S(2)}) copy-start(bf16[768,512]{1,0:T(8,128)(2,1)S(1)} %pad_maximum_fusion.first_ref) | copy-start | bytes 2359300
  53.6 3.4 %collective-permute-start.7 = (bf16[768,512]{1,0:T(8,128)(2,1)S(1)}, bf16[768,512]{1,0:T(8,128)(2,1)}, u32[]{:S(2)}, u32[]{:S(2)}) collective-permute-start(bf16[768,512]{1,0:T(8,128)(2,1)S(1)} %pad_maximum_fusion.first_ref), channel_id=1, source_target_pairs={{0,8},{8,0},{16,24},{24,16},{1,9},{9,1},{17,25},{25,17},{2,10},{10... | collective-permute-start | bytes 2359304 | tf_op jit(solution)/shard_map/ppermute | solution.py:23
  55.9 7.7 %copy-start.15 = (s32[8]{0:T(128)S(1)}, s32[8]{0:T(128)}, u32[]{:S(2)}) copy-start(s32[8]{0:T(128)} %into_ref.1) | copy-start | bytes 100
  57.0 1.4 %copy-start.10 = (bf16[1024,768]{1,0:T(8,128)(2,1)S(1)}, bf16[1024,768]{1,0:T(8,128)(2,1)}, u32[]{:S(2)}) copy-start(bf16[1024,768]{1,0:T(8,128)(2,1)} %features_ref.1) | copy-start | bytes 4718596
  61.5 2.0 %copy-start.3 = (f32[1024,1024]{1,0:T(8,128)}, f32[1024,1024]{1,0:T(8,128)S(1)}, u32[]{:S(2)}) copy-start(f32[1024,1024]{1,0:T(8,128)S(1)} %shard_map.96.total_hbm) | copy-start | bytes 12582916
  63.5 2.2 %copy-start.4 = (f32[1024,1024]{1,0:T(8,128)S(1)}, f32[1024,1024]{1,0:T(8,128)}, u32[]{:S(2)}) copy-start(f32[1024,1024]{1,0:T(8,128)} %copy-done.3) | copy-start | bytes 12582916
  68.0 1.6 %copy-start.14 = (bf16[1024,1024]{1,0:T(8,128)(2,1)S(1)}, bf16[1024,1024]{1,0:T(8,128)(2,1)}, u32[]{:S(2)}) copy-start(bf16[1024,1024]{1,0:T(8,128)(2,1)} %cotangent_hbm.1) | copy-start | bytes 6291460
  76.9 2.0 %copy-start = (bf16[1024,1024]{1,0:T(8,128)(2,1)}, bf16[1024,1024]{1,0:T(8,128)(2,1)S(1)}, u32[]{:S(2)}) copy-start(bf16[1024,1024]{1,0:T(8,128)(2,1)S(1)} %get-tuple-element.13.grad_ref) | copy-start | bytes 6291460
  78.8 2.6 %collective-permute-start.12 = (bf16[768,512]{1,0:T(8,128)(2,1)}, bf16[768,512]{1,0:T(8,128)(2,1)}, u32[]{:S(2)}, u32[]{:S(2)}) collective-permute-start(bf16[768,512]{1,0:T(8,128)(2,1)} %shard_map.100), channel_id=1, source_target_pairs={{0,8},{8,0},{16,24},{24,16},{1,9},{9,1},{17,25},{25,17},{2,10},{10... | collective-permute-start | bytes 2359304 | tf_op jit(solution)/shard_map/ppermute | solution.py:23
  80.8 7.5 %collective-permute-start.9 = (bf16[768,512]{1,0:T(8,128)(2,1)}, bf16[768,512]{1,0:T(8,128)(2,1)}, u32[]{:S(2)}, u32[]{:S(2)}) collective-permute-start(bf16[768,512]{1,0:T(8,128)(2,1)} %shard_map.98), channel_id=1, source_target_pairs={{0,8},{8,0},{16,24},{24,16},{1,9},{9,1},{17,25},{25,17},{2,10},{10... | collective-permute-start | bytes 2359304 | tf_op jit(solution)/shard_map/ppermute | solution.py:23
  81.4 1.6 %copy-start.1 = (bf16[1024,1024]{1,0:T(8,128)(2,1)S(1)}, bf16[1024,1024]{1,0:T(8,128)(2,1)}, u32[]{:S(2)}) copy-start(bf16[1024,1024]{1,0:T(8,128)(2,1)} %copy-done) | copy-start | bytes 6291460
  86.8 11.4 %collective-permute-start.13 = (bf16[8,96,256]{2,1,0:T(8,128)(2,1)}, bf16[8,96,256]{2,1,0:T(8,128)(2,1)S(1)}, u32[]{:S(2)}, u32[]{:S(2)}) collective-permute-start(bf16[8,96,256]{2,1,0:T(8,128)(2,1)} %constant_dynamic-slice_fusion), channel_id=1, source_target_pairs={{0,16},{8,24},{16,0},{24,8},{1,17},{9,25},{17,1},{25,9},{2,18},{10... | collective-permute-start | bytes 1179656 | tf_op jit(solution)/shard_map/ppermute | solution.py:23
  88.3 1.6 %copy-start.2 = (bf16[1024,1024]{1,0:T(8,128)(2,1)S(1)}, bf16[1024,1024]{1,0:T(8,128)(2,1)}, u32[]{:S(2)}) copy-start(bf16[1024,1024]{1,0:T(8,128)(2,1)} %copy-done) | copy-start | bytes 6291460
  93.0 12.1 %copy-start.13 = (bf16[768,512]{1,0:T(8,128)(2,1)S(1)}, bf16[768,512]{1,0:T(8,128)(2,1)}, u32[]{:S(2)}) copy-start(bf16[768,512]{1,0:T(8,128)(2,1)} %copy-done.12) | copy-start | bytes 2359300
  93.0 12.1 %collective-permute-start.10 = (bf16[4,96,512]{2,1,0:T(8,128)(2,1)S(1)}, bf16[4,96,512]{2,1,0:T(8,128)(2,1)S(1)}, u32[]{:S(2)}, u32[]{:S(2)}) collective-permute-start(bf16[4,96,512]{2,1,0:T(8,128)(2,1)S(1)} %dynamic-slice_bitcast_fusion), channel_id=1, source_target_pairs={{0,1},{1,0},{2,3},{3,2},{4,5},{5,4},{6,7},{7,6},{8,9},{9,8},{10,11... | collective-permute-start | bytes 1179656 | tf_op jit(solution)/shard_map/ppermute | solution.py:23
  99.3 8.9 %collective-permute-start.14 = (bf16[4,96,256]{2,1,0:T(8,128)(2,1)S(1)}, bf16[4,96,256]{2,1,0:T(8,128)(2,1)S(1)}, u32[]{:S(2)}, u32[]{:S(2)}) collective-permute-start(bf16[4,96,256]{2,1,0:T(8,128)(2,1)S(1)} %dynamic-slice_bitcast_fusion.1), channel_id=1, source_target_pairs={{0,1},{1,0},{2,3},{3,2},{4,5},{5,4},{6,7},{7,6},{8,9},{9,8},{10,11... | collective-permute-start | bytes 589832 | tf_op jit(solution)/shard_map/ppermute | solution.py:23
  105.2 5.7 %collective-permute-start.11 = (bf16[4,96,256]{2,1,0:T(8,128)(2,1)S(1)}, bf16[4,96,256]{2,1,0:T(8,128)(2,1)S(1)}, u32[]{:S(2)}, u32[]{:S(2)}) collective-permute-start(bf16[4,96,256]{2,1,0:T(8,128)(2,1)S(1)} %constant_dynamic-slice_fusion.1), channel_id=1, source_target_pairs={{0,16},{8,24},{16,0},{24,8},{1,17},{9,25},{17,1},{25,9},{2,18},{10... | collective-permute-start | bytes 589832 | tf_op jit(solution)/shard_map/ppermute | solution.py:23
  111.0 8.3 %collective-permute-start.15 = (bf16[96,512]{1,0:T(8,128)(2,1)S(1)}, bf16[96,512]{1,0:T(8,128)(2,1)S(1)}, u32[]{:S(2)}, u32[]{:S(2)}) collective-permute-start(bf16[96,512]{1,0:T(8,128)(2,1)S(1)} %get-tuple-element.24), channel_id=1, source_target_pairs={{0,2},{1,3},{2,0},{3,1},{4,6},{5,7},{6,4},{7,5},{8,10},{9,11},{10,... | collective-permute-start | bytes 294920 | tf_op jit(solution)/shard_map/ppermute | solution.py:23
  114.9 7.7 %collective-permute-start.16 = (bf16[96,512]{1,0:T(8,128)(2,1)S(1)}, bf16[96,512]{1,0:T(8,128)(2,1)S(1)}, u32[]{:S(2)}, u32[]{:S(2)}) collective-permute-start(bf16[96,512]{1,0:T(8,128)(2,1)S(1)} %get-tuple-element.25), channel_id=1, source_target_pairs={{0,4},{1,5},{2,6},{3,7},{4,0},{5,1},{6,2},{7,3},{8,12},{9,13},{10,... | collective-permute-start | bytes 294920 | tf_op jit(solution)/shard_map/ppermute | solution.py:23
  115.7 7.0 %collective-permute-start.17 = (bf16[96,512]{1,0:T(8,128)(2,1)S(1)}, bf16[96,512]{1,0:T(8,128)(2,1)S(1)}, u32[]{:S(2)}, u32[]{:S(2)}) collective-permute-start(bf16[96,512]{1,0:T(8,128)(2,1)S(1)} %get-tuple-element.26), channel_id=1, source_target_pairs={{0,6},{1,7},{2,4},{3,5},{4,2},{5,3},{6,0},{7,1},{8,14},{9,15},{10,... | collective-permute-start | bytes 294920 | tf_op jit(solution)/shard_map/ppermute | solution.py:23
  122.7 4.7 %collective-permute-start.18 = (bf16[2,96,256]{2,1,0:T(8,128)(2,1)S(1)}, bf16[2,96,256]{2,1,0:T(8,128)(2,1)S(1)}, u32[]{:S(2)}, u32[]{:S(2)}) collective-permute-start(bf16[2,96,256]{2,1,0:T(8,128)(2,1)S(1)} %pad_maximum_fusion.10), channel_id=1, source_target_pairs={{0,16},{8,24},{16,0},{24,8},{1,17},{9,25},{17,1},{25,9},{2,18},{10... | collective-permute-start | bytes 294920 | tf_op jit(solution)/shard_map/ppermute | solution.py:23
  127.5 1.5 %collective-permute-start.19 = (bf16[96,1024]{1,0:T(8,128)(2,1)S(1)}, bf16[96,1024]{1,0:T(8,128)(2,1)S(1)}, u32[]{:S(2)}, u32[]{:S(2)}) collective-permute-start(bf16[96,1024]{1,0:T(8,128)(2,1)S(1)} %pad_maximum_fusion.7), channel_id=1, source_target_pairs={{0,8},{8,0},{16,24},{24,16},{1,9},{9,1},{17,25},{25,17},{2,10},{10... | collective-permute-start | bytes 589832 | tf_op jit(solution)/shard_map/ppermute | solution.py:23
  (8 other events, 8.0 us)

commit v4 on v3

v4 whole, which is shorter than its diff:
```python
import jax
import jax.numpy as jnp
from jax import lax
from jax.experimental import pallas as pl
from jax.experimental.pallas import tpu as pltpu
from jax.sharding import PartitionSpec as P

F32 = jnp.float32
BF16 = jnp.bfloat16
SCALE = 0.7978845608
CUBIC = 0.044715
MIB = 1 << 20
HBM = pl.BlockSpec(memory_space=pltpu.HBM)
SMEM = pl.BlockSpec(memory_space=pltpu.SMEM)
VMEM = pl.BlockSpec(memory_space=pltpu.VMEM)
DMA = pltpu.SemaphoreType.DMA


def swap(value, axis, step):
    size = lax.axis_size(axis)
    return lax.ppermute(value, axis, [(index, index ^ step) for index in range(size)])


def slots_kernel(
    src_hbm, peer_hbm, tiles_hbm, features_hbm, out_hbm, src, peer, tiles, features, dense, out, in_sems, out_sems
):
    copies = [
        pltpu.make_async_copy(source, target, in_sems.at[index])
        for index, (source, target) in enumerate(
            [(src_hbm, src), (peer_hbm, peer), (tiles_hbm, tiles), (features_hbm, features)]
        )
    ]
    for copy in copies:
        copy.start()
    count, block, _ = tiles.shape
    dense[...] = jnp.zeros_like(dense)
    for copy in copies[:3]:
        copy.wait()

    def place(tile, carry):
        row = pl.multiple_of(peer[tile] * block, block)
        column = pl.multiple_of(src[tile] * block, block)
        at = (pl.ds(row, block), pl.ds(column, block))
        dense[at] = dense[at] + tiles[tile].astype(F32)
        return carry

    lax.fori_loop(0, count, place, 0)
    copies[3].wait()
    chunk = 4 * block
    results = []
    for index in range(out.shape[0] // chunk):
        at = slice(index * chunk, (index + 1) * chunk)
        out[at, :] = jnp.dot(dense[at, :].astype(BF16), features[...], preferred_element_type=F32).astype(BF16)
        results.append(pltpu.make_async_copy(out.at[at, :], out_hbm.at[at, :], out_sems.at[index]))
        results[-1].start()
    for result in results:
        result.wait()


def layer_kernel(
    core_ref,
    into_ref,
    slots_hbm,
    features_hbm,
    turned_hbm,
    cotangent_hbm,
    mine_first_hbm,
    mine_second_hbm,
    other_first_hbm,
    other_second_hbm,
    aggregate_hbm,
    grad_hbm,
    sent_hbm,
    slots,
    features,
    turned,
    cotangent,
    w_self,
    w_neigh,
    summed,
    aggregate,
    grad,
    sent,
    slot_sems,
    weight_sems,
    row_sems,
    out_sems,
):
    senders, block, _ = slots.shape
    rows, width = features.shape
    split = mine_first_hbm.shape[1]
    chunk = 256
    core = core_ref[0]
    arrivals = [
        pltpu.make_async_copy(slots_hbm.at[sender], slots.at[sender], slot_sems.at[sender]) for sender in range(senders)
    ]
    for arrival in arrivals:
        arrival.start()

    def weight_copies(first_hbm, second_hbm, target, index):
        return [
            pltpu.make_async_copy(first_hbm, target.at[:, :split], weight_sems.at[index]),
            pltpu.make_async_copy(second_hbm, target.at[:, split:], weight_sems.at[index + 1]),
        ]

    mine = (mine_first_hbm, mine_second_hbm)
    other = (other_first_hbm, other_second_hbm)

    @pl.when(core == 0)
    def _():
        for copy in weight_copies(*mine, w_self, 0) + weight_copies(*other, w_neigh, 2):
            copy.start()

    @pl.when(core != 0)
    def _():
        for copy in weight_copies(*other, w_self, 0) + weight_copies(*mine, w_neigh, 2):
            copy.start()

    weights = weight_copies(*mine, w_self, 0) + weight_copies(*other, w_neigh, 2)
    spans = [slice(first, first + chunk) for first in range(0, rows, chunk)]
    streams = [
        [
            pltpu.make_async_copy(features_hbm.at[at, :], features.at[at, :], row_sems.at[0, index]),
            pltpu.make_async_copy(cotangent_hbm.at[at, :], cotangent.at[at, :], row_sems.at[1, index]),
        ]
        for index, at in enumerate(spans)
    ]
    for stream in streams:
        for copy in stream:
            copy.start()
    turning = pltpu.make_async_copy(turned_hbm, turned, out_sems.at[0])
    turning.start()

    summed[...] = jnp.zeros_like(summed)
    for sender in range(senders):
        arrivals[sender].wait()
        at = pl.ds(pl.multiple_of(into_ref[sender] * block, block), block)
        summed[at, :] = summed[at, :] + slots[sender].astype(F32)
    aggregate[...] = summed[...].astype(BF16)
    results = [pltpu.make_async_copy(aggregate, aggregate_hbm, out_sems.at[1])]
    results[0].start()
    for copy in weights:
        copy.wait()
    span = 512
    for index, at in enumerate(spans):
        for copy in streams[index]:
            copy.wait()
        for first in range(0, grad.shape[1], span):
            columns = slice(first, first + span)
            value = jnp.dot(features[at, :], w_self[:, columns], preferred_element_type=F32) + jnp.dot(
                aggregate[at, :], w_neigh[:, columns], preferred_element_type=F32
            )
            square = value * value
            bend = jnp.tanh(value * (SCALE + SCALE * CUBIC * square))
            inner = value * (SCALE + 3.0 * SCALE * CUBIC * square)
            slope = (1.0 + bend) * (0.5 + 0.5 * inner * (1.0 - bend))
            grad[at, columns] = (cotangent[at, columns].astype(F32) * slope).astype(BF16)
        results.append(pltpu.make_async_copy(grad.at[at, :], grad_hbm.at[at, :], out_sems.at[2 + index]))
        results[-1].start()
    turning.wait()
    term(1 - core, turned, aggregate, grad, sent, sent_hbm, out_sems, 2 + len(spans))
    for result in results:
        result.wait()


def term(use, turned, aggregate, grad, out, out_hbm, sems, first_sem):
    chunk = 256
    spans = [slice(first, first + chunk) for first in range(0, out.shape[0], chunk)]
    copies = [
        pltpu.make_async_copy(out.at[at, :], out_hbm.at[at, :], sems.at[first_sem + index])
        for index, at in enumerate(spans)
    ]

    @pl.when(use == 0)
    def _():
        for at, copy in zip(spans, copies):
            out[at, :] = jnp.dot(turned[at, :], grad[...], preferred_element_type=F32).astype(BF16)
            copy.start()

    @pl.when(use != 0)
    def _():
        contract = (((0,), (0,)), ((), ()))
        for at, copy in zip(spans, copies):
            out[at, :] = lax.dot_general(
                aggregate[:, at], grad[...], contract, preferred_element_type=F32
            ).astype(BF16)
            copy.start()

    for copy in copies:
        copy.wait()


def kept_kernel(core_ref, turned_hbm, aggregate_hbm, grad_hbm, out_hbm, turned, aggregate, grad, out, in_sems, out_sems):
    grads = pltpu.make_async_copy(grad_hbm, grad, in_sems.at[0])
    grads.start()
    core = core_ref[0]

    @pl.when(core == 0)
    def _():
        copy = pltpu.make_async_copy(turned_hbm, turned, in_sems.at[1])
        copy.start()
        copy.wait()

    @pl.when(core != 0)
    def _():
        copy = pltpu.make_async_copy(aggregate_hbm, aggregate, in_sems.at[1])
        copy.start()
        copy.wait()

    grads.wait()
    term(core, turned, aggregate, grad, out, out_hbm, out_sems, 0)


def call(kernel, outs, places, out_places, scratch=(), flops=0, moved=0, vmem=56):
    return pl.pallas_call(
        kernel,
        out_shape=outs,
        in_specs=places,
        out_specs=out_places,
        scratch_shapes=list(scratch),
        compiler_params=pltpu.CompilerParams(vmem_limit_bytes=vmem * MIB),
        cost_estimate=pl.CostEstimate(flops=flops, bytes_accessed=moved, transcendentals=0),
    )


def joined(held, other, upper, axis):
    return jnp.stack([jnp.where(upper, other, held), jnp.where(upper, held, other)], axis=axis)


def gather_low(held, me):
    held = joined(held, swap(held, "dom", 1), (me & 1) != 0, 1)
    return held.reshape(-1, held.shape[-1])


def gather_high(held, high):
    step = 1
    while step < lax.axis_size("rep") // 2:
        other = swap(held, "rep", 2 * step)
        upper = (high & step) != 0
        held = jnp.concatenate([jnp.where(upper, other, held), jnp.where(upper, held, other)], axis=-1)
        step *= 2
    return held


def added(left, right):
    return (left.astype(F32) + right.astype(F32)).astype(BF16)


def half_of(value, axis, which):
    size = value.shape[axis] // 2
    return lax.dynamic_slice_in_dim(value, which * size, size, axis)


def reduce_high(value, high):
    step = lax.axis_size("rep") // 4
    while step:
        upper = (high // step) % 2
        value = added(half_of(value, 2, upper), swap(half_of(value, 2, 1 - upper), "rep", 2 * step))
        step //= 2
    return value


def reduce_low(value, low):
    value = value.reshape(value.shape[0] // 2, 2, *value.shape[1:])
    sent = lax.dynamic_index_in_dim(value, 1 - low, 1, keepdims=False)
    kept = lax.dynamic_index_in_dim(value, low, 1, keepdims=False)
    return added(kept, swap(sent, "dom", 1))


def shards(features, cotangent, w_self, w_neigh, tile_vals, tile_src, tile_peer, in_block):
    dom_size = lax.axis_size("dom")
    rows, width = features.shape
    hidden = w_self.shape[1]
    block = tile_vals.shape[1]
    me = lax.axis_index("dom")
    rep = lax.axis_index("rep")
    parts = lax.axis_size("rep") // 2
    core, high = rep & 1, rep >> 1
    low, place = me & 1, me >> 1
    core_arg = core.astype(jnp.int32).reshape(1)

    own = jnp.where(core == 0, w_self, w_neigh)
    split = hidden // 4
    share = split // parts
    rest = (hidden - split) // parts
    held = jnp.concatenate(
        [
            lax.dynamic_slice_in_dim(own, high * share, share, 1),
            lax.dynamic_slice_in_dim(own, split + high * rest, rest, 1),
        ],
        axis=1,
    )[None]
    step = dom_size // 2
    other = swap(held, "dom", step)
    slots = call(
        slots_kernel,
        jax.ShapeDtypeStruct((dom_size * block, width), BF16),
        [HBM] * 4,
        HBM,
        [
            pltpu.SMEM(tile_src.shape, jnp.int32),
            pltpu.SMEM(tile_peer.shape, jnp.int32),
            pltpu.VMEM(tile_vals.shape, BF16),
            pltpu.VMEM(features.shape, BF16),
            pltpu.VMEM((dom_size * block, rows), F32),
            pltpu.VMEM((dom_size * block, width), BF16),
            DMA((4,)),
            DMA((dom_size // 4,)),
        ],
        flops=2 * dom_size * block * rows * width,
        moved=tile_vals.size * 2 + rows * width * 4,
    )(tile_src, tile_peer, tile_vals, features)
    received = lax.all_to_all(slots.reshape(dom_size, block, width), "dom", split_axis=0, concat_axis=0, tiled=True)

    other, _ = lax.optimization_barrier((other, slots))
    while step > 1:
        held = joined(held, other, (me & step) != 0, 1).reshape(-1, *held.shape[1:])
        step //= 2
        if step > 1:
            other = swap(held, "dom", step)
    weights = [
        gather_high(gather_low(held[..., :share], me), high),
        gather_low(gather_high(held[..., share:], high), me),
    ]
    weights += [swap(weight, "rep", 1) for weight in weights]
    turned = features.T

    aggregate, grad, sent = call(
        layer_kernel,
        [
            jax.ShapeDtypeStruct((rows, width), BF16),
            jax.ShapeDtypeStruct((rows, hidden), BF16),
            jax.ShapeDtypeStruct((width, hidden), BF16),
        ],
        [SMEM, SMEM] + [HBM] * 8,
        [HBM] * 3,
        [
            pltpu.VMEM((dom_size, block, width), BF16),
            pltpu.VMEM((rows, width), BF16),
            pltpu.VMEM((width, rows), BF16),
            pltpu.VMEM((rows, hidden), BF16),
            pltpu.VMEM((width, hidden), BF16),
            pltpu.VMEM((width, hidden), BF16),
            pltpu.VMEM((rows, width), F32),
            pltpu.VMEM((rows, width), BF16),
            pltpu.VMEM((rows, hidden), BF16),
            pltpu.VMEM((width, hidden), BF16),
            DMA((dom_size,)),
            DMA((4,)),
            DMA((2, rows // 256)),
            DMA((2 + rows // 256 + width // 256,)),
        ],
        flops=6 * rows * width * hidden,
        moved=16 * rows * hidden,
    )(core_arg, in_block, received, features, turned, cotangent, *weights)
    other = swap(sent, "rep", 1)
    kept = call(
        kept_kernel,
        jax.ShapeDtypeStruct((width, hidden), BF16),
        [SMEM] + [HBM] * 3,
        HBM,
        [
            pltpu.VMEM((width, rows), BF16),
            pltpu.VMEM((rows, width), BF16),
            pltpu.VMEM((rows, hidden), BF16),
            pltpu.VMEM((width, hidden), BF16),
            DMA((2,)),
            DMA((width // 256,)),
        ],
        flops=2 * rows * width * hidden,
        moved=6 * rows * hidden,
        vmem=16,
    )(core_arg, turned, aggregate, grad)
    chip = added(kept, other).reshape(dom_size, width // dom_size, hidden)
    first, second = chip[:, :, : hidden // 2], chip[:, :, hidden // 2 :]
    first, second = reduce_low(first, low), reduce_high(second, high)
    first, second = reduce_high(first, high), reduce_low(second, low)
    both = jnp.concatenate([first, second], axis=2)
    summed = lax.dynamic_index_in_dim(both, place, 0, keepdims=False).astype(F32)
    for step in range(1, dom_size // 2):
        piece = lax.dynamic_index_in_dim(both, place ^ step, 0, keepdims=False)
        summed = summed + swap(piece, "dom", 2 * step).astype(F32)
    summed = summed.astype(BF16)
    size = summed.shape[1] // 2
    held = gather_high(jnp.stack([summed[:, :size], summed[:, size:]]), high)
    whole = jnp.concatenate([held[0], held[1]], axis=1)
    opposite = swap(whole, "rep", 1)
    return (
        jnp.where(core == 0, whole, opposite).astype(F32),
        jnp.where(core == 0, opposite, whole).astype(F32),
    )


def solution(mesh):
    in_specs = (
        P(("rep", "dom"), None),
        P(("rep", "dom"), None),
        P("dom", None),
        P("dom", None),
        P(("rep", "dom"), None, None),
        P(("rep", "dom")),
        P(("rep", "dom")),
        P(("rep", "dom")),
    )
    out_specs = (P("dom", None), P("dom", None))
    return jax.shard_map(shards, mesh=mesh, in_specs=in_specs, out_specs=out_specs, check_vma=False)
```

time: 131 us -> 124 us (0.947)
  waiting for transfers between devices: 51.9 us -> 68.4 us
  local copies, waits for them, and re-layouts: 21 us -> 5.85 us
  starting transfers between devices: 29.7 us -> 24.6 us
  Pallas kernels: 22.3 us -> 20 us
    ppermute x20 -> x18, waiting for transfers between devices: 51.9 us -> 68.4 us  [swap(): lax.ppermute(value, axis, [(index, index ^ step) for index in range(size)])]
    unnamed x39 -> x15, local copies, waits for them, and re-layouts: 20 us -> 5.38 us
    pallas_call x5 -> x1, Pallas kernels: 11.2 us -> 2.54 us  [shards(): call(kept_kernel, jax.ShapeDtypeStruct((width, hidden), BF16), [SMEM] + [...]
    ppermute x20 -> x18, starting transfers between devices: 23.7 us -> 18 us  [swap(): lax.ppermute(value, axis, [(index, index ^ step) for index in range(size)])]
    pallas_call x1, Pallas kernels: 7.3 us -> 12.9 us  [shards(): call(layer_kernel, [jax.ShapeDtypeStruct((rows, width), BF16), jax.ShapeD...]
  transfers between devices with their start and end apart: 21 -> 19, of which waited for: 12 -> 14; matrix products, arithmetic and copies ran while one was open for 3% -> 2% of each run, Pallas kernels for 10% -> 6%
where the time goes in v4:
time: 124 us
  waiting for transfers between devices  68.4 us (55%)
  starting transfers between devices  24.6 us (20%)
  Pallas kernels  20 us (16%)
  local copies, waits for them, and re-layouts  5.85 us (5%)
  other arithmetic  3.79 us (3%)
    ppermute x18, waiting for transfers between devices, swap(): lax.ppermute(value, axis, [(index, index ^ step) for index in range(size)])  68.4 us
    ppermute x18, starting transfers between devices, swap(): lax.ppermute(value, axis, [(index, index ^ step) for index in range(size)])  18 us
    pallas_call x1, Pallas kernels, shards(): call(layer_kernel, [jax.ShapeDtypeStruct((rows, width), BF16), jax.ShapeD...  12.9 us
    all_to_all x1, starting transfers between devices, shards(): lax.all_to_all(slots.reshape(dom_size, block, width), 'dom', split_axis=0...  6.55 us
    unnamed x15, local copies, waits for them, and re-layouts  5.38 us
    pallas_call x1, Pallas kernels, shards(): call(slots_kernel, jax.ShapeDtypeStruct((dom_size * block, width), BF16),...  4.53 us
    pallas_call x1, Pallas kernels, shards(): call(kept_kernel, jax.ShapeDtypeStruct((width, hidden), BF16), [SMEM] + [...  2.54 us
  transfers between devices with their start and end apart: 19, of which 14 were waited for; matrix products, arithmetic and copies ran while one was open for 2% of the time, Pallas kernels for 6%

profile of v4, /device:TPU:0, one launch (start us, length us, event | category | flops | bytes accessed | tf_op | source)
XLA Modules:
  0.0 123.7 jit_solution(6312170780469215731)
XLA Ops:
  0.6 1.0 broadcast_select_fusion.4
  1.7 4.1 %collective-permute-start = (bf16[1,96,512]{2,1,0:T(8,128)(2,1)S(1)}, bf16[1,96,512]{2,1,0:T(8,128)(2,1)S(1)}, u32[]{:S(2)}, u32[]{:S(2)}) collective-permute-start(bf16[1,96,512]{2,1,0:T(8,128)(2,1)S(1)} %maximum_bitcast_fusion.1), channel_id=1, source_target_pairs={{0,4},{1,5},{2,6},{3,7},{4,0},{5,1},{6,2},{7,3},{8,12},{9,13},{10,... | collective-permute-start | bytes 294920 | tf_op jit(solution)/shard_map/ppermute | solution.py:21
  5.8 4.5 %shard_map.95 = bf16[1024,768]{1,0:T(8,128)(2,1)} custom-call(s32[32]{0:T(128)} %src_hbm.1, s32[32]{0:T(128)} %peer_hbm.1, bf16[32,128,128]{2,1,0:T(8,128)(2,1)} %tiles_hbm.1, bf16[1024,768]{1,0:T(8,128)(2,1)} %features_hbm.3), custom_call_target="tpu_custom_call" | custom-call | flops 1610612736 | bytes 4194304 | tf_op jit(solution)/shard_map/pallas_call | solution.py:295
  10.8 1.3 %collective-permute-start.1 = (bf16[2,96,512]{2,1,0:T(8,128)(2,1)S(1)}, bf16[2,96,512]{2,1,0:T(8,128)(2,1)S(1)}, u32[]{:S(2)}, u32[]{:S(2)}) collective-permute-start(bf16[2,96,512]{2,1,0:T(8,128)(2,1)S(1)} %maximum_bitcast_fusion), channel_id=1, source_target_pairs={{0,2},{1,3},{2,0},{3,1},{4,6},{5,7},{6,4},{7,5},{8,10},{9,11},{10,... | collective-permute-start | bytes 589832 | tf_op jit(solution)/shard_map/ppermute | solution.py:21
  12.0 4.9 %collective-permute-done.1 = bf16[2,96,512]{2,1,0:T(8,128)(2,1)S(1)} collective-permute-done((bf16[2,96,512]{2,1,0:T(8,128)(2,1)S(1)}, bf16[2,96,512]{2,1,0:T(8,128)(2,1)S(1)}, u32[]{:S(2)}, u32[]{:S(2)}) %collective-permute-start.1) | collective-permute-done | bytes 196640 | tf_op jit(solution)/shard_map/ppermute | solution.py:21
  17.0 1.5 %collective-permute-start.4 = (bf16[4,96,384]{2,1,0:T(8,128)(2,1)S(1)}, bf16[4,96,384]{2,1,0:T(8,128)(2,1)S(1)}, u32[]{:S(2)}, u32[]{:S(2)}) collective-permute-start(bf16[4,96,384]{2,1,0:T(8,128)(2,1)S(1)} %slice.33), channel_id=1, source_target_pairs={{0,16},{8,24},{16,0},{24,8},{1,17},{9,25},{17,1},{25,9},{2,18},{10... | collective-permute-start | bytes 884744 | tf_op jit(solution)/shard_map/ppermute | solution.py:21
  18.5 6.6 %all-to-all-start = ((bf16[8,128,768]{2,1,0:T(8,128)(2,1)}), bf16[8,128,768]{2,1,0:T(8,128)(2,1)}, u32[]{:S(2)}, u32[]{:S(2)}) async-start(bf16[8,128,768]{2,1,0:T(8,128)(2,1)} %bitcast.2), calls=%async_computation | async-start | bytes 3145728 | tf_op jit(solution)/shard_map/all_to_all | solution.py:313
  25.2 2.1 %collective-permute-start.5 = (bf16[4,96,768]{2,1,0:T(8,128)(2,1)S(1)}, bf16[4,96,768]{2,1,0:T(8,128)(2,1)S(1)}, u32[]{:S(2)}, u32[]{:S(2)}) collective-permute-start(bf16[4,96,768]{2,1,0:T(8,128)(2,1)S(1)} %pad_maximum_fusion.1), channel_id=1, source_target_pairs={{0,1},{1,0},{2,3},{3,2},{4,5},{5,4},{6,7},{7,6},{8,9},{9,8},{10,11... | collective-permute-start | bytes 1769480 | tf_op jit(solution)/shard_map/ppermute | solution.py:21
  27.4 29.6 %collective-permute-done.5 = bf16[4,96,768]{2,1,0:T(8,128)(2,1)S(1)} collective-permute-done((bf16[4,96,768]{2,1,0:T(8,128)(2,1)S(1)}, bf16[4,96,768]{2,1,0:T(8,128)(2,1)S(1)}, u32[]{:S(2)}, u32[]{:S(2)}) %collective-permute-start.5) | collective-permute-done | bytes 589856 | tf_op jit(solution)/shard_map/ppermute | solution.py:21
  57.6 0.5 collective-permute-done.2
  58.2 0.6 collective-permute-start.3
  58.7 6.3 %collective-permute-done.3 = bf16[768,128]{1,0:T(8,128)(2,1)S(1)} collective-permute-done((bf16[768,128]{1,0:T(8,128)(2,1)S(1)}, bf16[768,128]{1,0:T(8,128)(2,1)S(1)}, u32[]{:S(2)}, u32[]{:S(2)}) %collective-permute-start.3) | collective-permute-done | bytes 196640 | tf_op jit(solution)/shard_map/ppermute | solution.py:21
  65.2 1.6 %copy.13 = bf16[1024,768]{0,1:T(8,128)(2,1)} copy(bf16[1024,768]{1,0:T(8,128)(2,1)S(1)} %copy-done.3) | data formatting | bytes 3145728 | tf_op args[0]
  66.9 0.7 copy-done.6
  67.7 12.9 %shard_map.96 = (bf16[1024,768]{1,0:T(8,128)(2,1)}, bf16[1024,1024]{1,0:T(8,128)(2,1)}, bf16[768,1024]{1,0:T(8,128)(2,1)}) custom-call(s32[1]{0:T(128)} %bitcast.core_ref, s32[8]{0:T(128)} %into_ref.1, bf16[8,128,768]{2,1,0:T(8,128)(2,1)} %all-to-all-done.slots_hbm, bf16[1024,768]{1,0:T(8,128)(2,1)} %features_hbm.3, bf16[768,1024]{1,0:T(8,128)(2,1)} %bitcast.74, ...), custom_call_target="tpu_custom_call" | custom-call | flops 4831838208 | bytes 16777216 | tf_op jit(solution)/shard_map/pallas_call | solution.py:328
  80.9 1.6 %copy-done.1 = bf16[1024,1024]{1,0:T(8,128)(2,1)S(1)} copy-done((bf16[1024,1024]{1,0:T(8,128)(2,1)S(1)}, bf16[1024,1024]{1,0:T(8,128)(2,1)}, u32[]{:S(2)}) %copy-start.1) | copy-done | bytes 2097176
  82.5 1.4 %copy-done.2 = bf16[1024,768]{1,0:T(8,128)(2,1)S(1)} copy-done((bf16[1024,768]{1,0:T(8,128)(2,1)S(1)}, bf16[1024,768]{1,0:T(8,128)(2,1)}, u32[]{:S(2)}) %copy-start.2) | copy-done | bytes 1572888
  83.9 2.5 %shard_map.97 = bf16[768,1024]{1,0:T(8,128)(2,1)S(1)} custom-call(s32[1]{0:T(128)} %bitcast.core_ref, bf16[768,1024]{1,0:T(8,128)(2,1)S(1)} %bitcast.75, bf16[1024,768]{1,0:T(8,128)(2,1)S(1)} %copy-done.2, bf16[1024,1024]{1,0:T(8,128)(2,1)S(1)} %copy-done.1), custom_call_target="tpu_custom_call" | custom-call | flops 1610612736 | bytes 6291456 | tf_op jit(solution)/shard_map/pallas_call | solution.py:357
  86.5 0.7 add_convert_fusion
  87.4 0.6 collective-permute-start.11
  88.1 10.7 %collective-permute-done.11 = bf16[8,96,256]{2,1,0:T(8,128)(2,1)S(1)} collective-permute-done((bf16[8,96,256]{2,1,0:T(8,128)(2,1)S(1)}, bf16[8,96,256]{2,1,0:T(8,128)(2,1)S(1)}, u32[]{:S(2)}, u32[]{:S(2)}) %collective-permute-start.11) | collective-permute-done | bytes 393248 | tf_op jit(solution)/shard_map/ppermute | solution.py:21
  99.3 1.6 %collective-permute-start.10 = (bf16[4,96,256]{2,1,0:T(8,128)(2,1)S(1)}, bf16[4,96,256]{2,1,0:T(8,128)(2,1)S(1)}, u32[]{:S(2)}, u32[]{:S(2)}) collective-permute-start(bf16[4,96,256]{2,1,0:T(8,128)(2,1)S(1)} %constant_dynamic-slice_fusion.1), channel_id=1, source_target_pairs={{0,16},{8,24},{16,0},{24,8},{1,17},{9,25},{17,1},{25,9},{2,18},{10... | collective-permute-start | bytes 589832 | tf_op jit(solution)/shard_map/ppermute | solution.py:21
  100.8 4.5 %collective-permute-done.12 = bf16[4,96,256]{2,1,0:T(8,128)(2,1)S(1)} collective-permute-done((bf16[4,96,256]{2,1,0:T(8,128)(2,1)S(1)}, bf16[4,96,256]{2,1,0:T(8,128)(2,1)S(1)}, u32[]{:S(2)}, u32[]{:S(2)}) %collective-permute-start.12) | collective-permute-done | bytes 196640 | tf_op jit(solution)/shard_map/ppermute | solution.py:21
  105.7 1.8 %collective-permute-start.13 = (bf16[96,512]{1,0:T(8,128)(2,1)S(1)}, bf16[96,512]{1,0:T(8,128)(2,1)S(1)}, u32[]{:S(2)}, u32[]{:S(2)}) collective-permute-start(bf16[96,512]{1,0:T(8,128)(2,1)S(1)} %get-tuple-element.20), channel_id=1, source_target_pairs={{0,2},{1,3},{2,0},{3,1},{4,6},{5,7},{6,4},{7,5},{8,10},{9,11},{10,... | collective-permute-start | bytes 294920 | tf_op jit(solution)/shard_map/ppermute | solution.py:21
  107.5 2.3 %collective-permute-start.14 = (bf16[96,512]{1,0:T(8,128)(2,1)S(1)}, bf16[96,512]{1,0:T(8,128)(2,1)S(1)}, u32[]{:S(2)}, u32[]{:S(2)}) collective-permute-start(bf16[96,512]{1,0:T(8,128)(2,1)S(1)} %get-tuple-element.21), channel_id=1, source_target_pairs={{0,4},{1,5},{2,6},{3,7},{4,0},{5,1},{6,2},{7,3},{8,12},{9,13},{10,... | collective-permute-start | bytes 294920 | tf_op jit(solution)/shard_map/ppermute | solution.py:21
  109.7 0.4 collective-permute-start.15
  110.1 0.7 collective-permute-done.13
  110.9 5.5 %collective-permute-done.14 = bf16[96,512]{1,0:T(8,128)(2,1)S(1)} collective-permute-done((bf16[96,512]{1,0:T(8,128)(2,1)S(1)}, bf16[96,512]{1,0:T(8,128)(2,1)S(1)}, u32[]{:S(2)}, u32[]{:S(2)}) %collective-permute-start.14) | collective-permute-done | bytes 98336 | tf_op jit(solution)/shard_map/ppermute | solution.py:21
  116.5 1.1 collective-permute-start.16
  117.6 3.6 %collective-permute-done.16 = bf16[2,96,256]{2,1,0:T(8,128)(2,1)S(1)} collective-permute-done((bf16[2,96,256]{2,1,0:T(8,128)(2,1)S(1)}, bf16[2,96,256]{2,1,0:T(8,128)(2,1)S(1)}, u32[]{:S(2)}, u32[]{:S(2)}) %collective-permute-start.16) | collective-permute-done | bytes 98336 | tf_op jit(solution)/shard_map/ppermute | solution.py:21
  121.3 1.4 %collective-permute-done.17 = bf16[96,1024]{1,0:T(8,128)(2,1)S(1)} collective-permute-done((bf16[96,1024]{1,0:T(8,128)(2,1)S(1)}, bf16[96,1024]{1,0:T(8,128)(2,1)S(1)}, u32[]{:S(2)}, u32[]{:S(2)}) %collective-permute-start.17) | collective-permute-done | bytes 196640 | tf_op jit(solution)/shard_map/ppermute | solution.py:21
  122.7 1.0 select_convert_fusion
  (62 shorter events, 3.2 us)
Async XLA Ops:
  1.7 9.0 %collective-permute-start = (bf16[1,96,512]{2,1,0:T(8,128)(2,1)S(1)}, bf16[1,96,512]{2,1,0:T(8,128)(2,1)S(1)}, u32[]{:S(2)}, u32[]{:S(2)}) collective-permute-start(bf16[1,96,512]{2,1,0:T(8,128)(2,1)S(1)} %maximum_bitcast_fusion.1), channel_id=1, source_target_pairs={{0,4},{1,5},{2,6},{3,7},{4,0},{5,1},{6,2},{7,3},{8,12},{9,13},{10,... | collective-permute-start | bytes 294920 | tf_op jit(solution)/shard_map/ppermute | solution.py:21
  10.8 6.2 %collective-permute-start.1 = (bf16[2,96,512]{2,1,0:T(8,128)(2,1)S(1)}, bf16[2,96,512]{2,1,0:T(8,128)(2,1)S(1)}, u32[]{:S(2)}, u32[]{:S(2)}) collective-permute-start(bf16[2,96,512]{2,1,0:T(8,128)(2,1)S(1)} %maximum_bitcast_fusion), channel_id=1, source_target_pairs={{0,2},{1,3},{2,0},{3,1},{4,6},{5,7},{6,4},{7,5},{8,10},{9,11},{10,... | collective-permute-start | bytes 589832 | tf_op jit(solution)/shard_map/ppermute | solution.py:21
  17.0 8.1 %collective-permute-start.4 = (bf16[4,96,384]{2,1,0:T(8,128)(2,1)S(1)}, bf16[4,96,384]{2,1,0:T(8,128)(2,1)S(1)}, u32[]{:S(2)}, u32[]{:S(2)}) collective-permute-start(bf16[4,96,384]{2,1,0:T(8,128)(2,1)S(1)} %slice.33), channel_id=1, source_target_pairs={{0,16},{8,24},{16,0},{24,8},{1,17},{9,25},{17,1},{25,9},{2,18},{10... | collective-permute-start | bytes 884744 | tf_op jit(solution)/shard_map/ppermute | solution.py:21
  18.5 48.4 %all-to-all-start = ((bf16[8,128,768]{2,1,0:T(8,128)(2,1)}), bf16[8,128,768]{2,1,0:T(8,128)(2,1)}, u32[]{:S(2)}, u32[]{:S(2)}) async-start(bf16[8,128,768]{2,1,0:T(8,128)(2,1)} %bitcast.2), calls=%async_computation | async-start | bytes 3145728 | tf_op jit(solution)/shard_map/all_to_all | solution.py:313
  25.2 31.8 %collective-permute-start.5 = (bf16[4,96,768]{2,1,0:T(8,128)(2,1)S(1)}, bf16[4,96,768]{2,1,0:T(8,128)(2,1)S(1)}, u32[]{:S(2)}, u32[]{:S(2)}) collective-permute-start(bf16[4,96,768]{2,1,0:T(8,128)(2,1)S(1)} %pad_maximum_fusion.1), channel_id=1, source_target_pairs={{0,1},{1,0},{2,3},{3,2},{4,5},{5,4},{6,7},{7,6},{8,9},{9,8},{10,11... | collective-permute-start | bytes 1769480 | tf_op jit(solution)/shard_map/ppermute | solution.py:21
  27.3 30.8 %collective-permute-start.2 = (bf16[4,96,128]{2,1,0:T(8,128)(2,1)S(1)}, bf16[4,96,128]{2,1,0:T(8,128)(2,1)S(1)}, u32[]{:S(2)}, u32[]{:S(2)}) collective-permute-start(bf16[4,96,128]{2,1,0:T(8,128)(2,1)S(1)} %slice.32), channel_id=1, source_target_pairs={{0,1},{1,0},{2,3},{3,2},{4,5},{5,4},{6,7},{7,6},{8,9},{9,8},{10,11... | collective-permute-start | bytes 294920 | tf_op jit(solution)/shard_map/ppermute | solution.py:21
  57.5 9.4 %copy-start.4 = (bf16[4,2,96,768]{3,2,1,0:T(8,128)(2,1)}, bf16[4,2,96,768]{3,2,1,0:T(8,128)(2,1)S(1)}, u32[]{:S(2)}) copy-start(bf16[4,2,96,768]{3,2,1,0:T(8,128)(2,1)S(1)} %copy.16) | copy-start | bytes 3538948
  57.5 7.7 %copy-start.3 = (bf16[1024,768]{1,0:T(8,128)(2,1)S(1)}, bf16[1024,768]{1,0:T(8,128)(2,1)}, u32[]{:S(2)}) copy-start(bf16[1024,768]{1,0:T(8,128)(2,1)} %features_hbm.3) | copy-start | bytes 4718596
  57.5 9.4 %collective-permute-start.7 = (bf16[768,768]{1,0:T(8,128)(2,1)S(1)}, bf16[768,768]{1,0:T(8,128)(2,1)}, u32[]{:S(2)}, u32[]{:S(2)}) collective-permute-start(bf16[768,768]{1,0:T(8,128)(2,1)S(1)} %bitcast.85), channel_id=1, source_target_pairs={{0,8},{8,0},{16,24},{24,16},{1,9},{9,1},{17,25},{25,17},{2,10},{10... | collective-permute-start | bytes 3538952 | tf_op jit(solution)/shard_map/ppermute | solution.py:21
  58.2 6.8 %collective-permute-start.3 = (bf16[768,128]{1,0:T(8,128)(2,1)S(1)}, bf16[768,128]{1,0:T(8,128)(2,1)S(1)}, u32[]{:S(2)}, u32[]{:S(2)}) collective-permute-start(bf16[768,128]{1,0:T(8,128)(2,1)S(1)} %bitcast.87), channel_id=1, source_target_pairs={{0,16},{8,24},{16,0},{24,8},{1,17},{9,25},{17,1},{25,9},{2,18},{10... | collective-permute-start | bytes 589832 | tf_op jit(solution)/shard_map/ppermute | solution.py:21
  65.1 1.8 %copy-start.5 = (bf16[768,256]{1,0:T(8,128)(2,1)}, bf16[768,256]{1,0:T(8,128)(2,1)S(1)}, u32[]{:S(2)}) copy-start(bf16[768,256]{1,0:T(8,128)(2,1)S(1)} %pad_maximum_fusion.3.mine_first_hbm) | copy-start | bytes 1179652
  65.1 1.8 %collective-permute-start.6 = (bf16[768,256]{1,0:T(8,128)(2,1)S(1)}, bf16[768,256]{1,0:T(8,128)(2,1)S(1)}, u32[]{:S(2)}, u32[]{:S(2)}) collective-permute-start(bf16[768,256]{1,0:T(8,128)(2,1)S(1)} %pad_maximum_fusion.3.mine_first_hbm), channel_id=1, source_target_pairs={{0,8},{8,0},{16,24},{24,16},{1,9},{9,1},{17,25},{25,17},{2,10},{10... | collective-permute-start | bytes 1179656 | tf_op jit(solution)/shard_map/ppermute | solution.py:21
  66.9 0.7 copy-start.6
  67.6 13.3 %copy-start = (bf16[1024,768]{0,1:T(8,128)(2,1)S(1)}, bf16[1024,768]{0,1:T(8,128)(2,1)}, u32[]{:S(2)}) copy-start(bf16[1024,768]{0,1:T(8,128)(2,1)} %copy.13) | copy-start | bytes 4718596
  80.6 5.9 %collective-permute-start.8 = (bf16[768,1024]{1,0:T(8,128)(2,1)}, bf16[768,1024]{1,0:T(8,128)(2,1)S(1)}, u32[]{:S(2)}, u32[]{:S(2)}) collective-permute-start(bf16[768,1024]{1,0:T(8,128)(2,1)} %get-tuple-element.9), channel_id=1, source_target_pairs={{0,8},{8,0},{16,24},{24,16},{1,9},{9,1},{17,25},{25,17},{2,10},{10... | collective-permute-start | bytes 4718600 | tf_op jit(solution)/shard_map/ppermute | solution.py:21
  80.9 1.6 %copy-start.1 = (bf16[1024,1024]{1,0:T(8,128)(2,1)S(1)}, bf16[1024,1024]{1,0:T(8,128)(2,1)}, u32[]{:S(2)}) copy-start(bf16[1024,1024]{1,0:T(8,128)(2,1)} %get-tuple-element.8.grad_hbm) | copy-start | bytes 6291460
  82.5 1.4 %copy-start.2 = (bf16[1024,768]{1,0:T(8,128)(2,1)S(1)}, bf16[1024,768]{1,0:T(8,128)(2,1)}, u32[]{:S(2)}) copy-start(bf16[1024,768]{1,0:T(8,128)(2,1)} %get-tuple-element.7.aggregate_hbm) | copy-start | bytes 4718596
  87.4 11.4 %collective-permute-start.11 = (bf16[8,96,256]{2,1,0:T(8,128)(2,1)S(1)}, bf16[8,96,256]{2,1,0:T(8,128)(2,1)S(1)}, u32[]{:S(2)}, u32[]{:S(2)}) collective-permute-start(bf16[8,96,256]{2,1,0:T(8,128)(2,1)S(1)} %constant_dynamic-slice_fusion), channel_id=1, source_target_pairs={{0,16},{8,24},{16,0},{24,8},{1,17},{9,25},{17,1},{25,9},{2,18},{10... | collective-permute-start | bytes 1179656 | tf_op jit(solution)/shard_map/ppermute | solution.py:21
  88.0 11.1 %collective-permute-start.9 = (bf16[4,96,512]{2,1,0:T(8,128)(2,1)S(1)}, bf16[4,96,512]{2,1,0:T(8,128)(2,1)S(1)}, u32[]{:S(2)}, u32[]{:S(2)}) collective-permute-start(bf16[4,96,512]{2,1,0:T(8,128)(2,1)S(1)} %dynamic-slice_bitcast_fusion), channel_id=1, source_target_pairs={{0,1},{1,0},{2,3},{3,2},{4,5},{5,4},{6,7},{7,6},{8,9},{9,8},{10,11... | collective-permute-start | bytes 1179656 | tf_op jit(solution)/shard_map/ppermute | solution.py:21
  98.9 6.4 %collective-permute-start.12 = (bf16[4,96,256]{2,1,0:T(8,128)(2,1)S(1)}, bf16[4,96,256]{2,1,0:T(8,128)(2,1)S(1)}, u32[]{:S(2)}, u32[]{:S(2)}) collective-permute-start(bf16[4,96,256]{2,1,0:T(8,128)(2,1)S(1)} %dynamic-slice_bitcast_fusion.1), channel_id=1, source_target_pairs={{0,1},{1,0},{2,3},{3,2},{4,5},{5,4},{6,7},{7,6},{8,9},{9,8},{10,11... | collective-permute-start | bytes 589832 | tf_op jit(solution)/shard_map/ppermute | solution.py:21
  99.3 6.3 %collective-permute-start.10 = (bf16[4,96,256]{2,1,0:T(8,128)(2,1)S(1)}, bf16[4,96,256]{2,1,0:T(8,128)(2,1)S(1)}, u32[]{:S(2)}, u32[]{:S(2)}) collective-permute-start(bf16[4,96,256]{2,1,0:T(8,128)(2,1)S(1)} %constant_dynamic-slice_fusion.1), channel_id=1, source_target_pairs={{0,16},{8,24},{16,0},{24,8},{1,17},{9,25},{17,1},{25,9},{2,18},{10... | collective-permute-start | bytes 589832 | tf_op jit(solution)/shard_map/ppermute | solution.py:21
  105.7 5.2 %collective-permute-start.13 = (bf16[96,512]{1,0:T(8,128)(2,1)S(1)}, bf16[96,512]{1,0:T(8,128)(2,1)S(1)}, u32[]{:S(2)}, u32[]{:S(2)}) collective-permute-start(bf16[96,512]{1,0:T(8,128)(2,1)S(1)} %get-tuple-element.20), channel_id=1, source_target_pairs={{0,2},{1,3},{2,0},{3,1},{4,6},{5,7},{6,4},{7,5},{8,10},{9,11},{10,... | collective-permute-start | bytes 294920 | tf_op jit(solution)/shard_map/ppermute | solution.py:21
  107.5 8.9 %collective-permute-start.14 = (bf16[96,512]{1,0:T(8,128)(2,1)S(1)}, bf16[96,512]{1,0:T(8,128)(2,1)S(1)}, u32[]{:S(2)}, u32[]{:S(2)}) collective-permute-start(bf16[96,512]{1,0:T(8,128)(2,1)S(1)} %get-tuple-element.21), channel_id=1, source_target_pairs={{0,4},{1,5},{2,6},{3,7},{4,0},{5,1},{6,2},{7,3},{8,12},{9,13},{10,... | collective-permute-start | bytes 294920 | tf_op jit(solution)/shard_map/ppermute | solution.py:21
  109.7 6.6 %collective-permute-start.15 = (bf16[96,512]{1,0:T(8,128)(2,1)S(1)}, bf16[96,512]{1,0:T(8,128)(2,1)S(1)}, u32[]{:S(2)}, u32[]{:S(2)}) collective-permute-start(bf16[96,512]{1,0:T(8,128)(2,1)S(1)} %get-tuple-element.22), channel_id=1, source_target_pairs={{0,6},{1,7},{2,4},{3,5},{4,2},{5,3},{6,0},{7,1},{8,14},{9,15},{10,... | collective-permute-start | bytes 294920 | tf_op jit(solution)/shard_map/ppermute | solution.py:21
  116.5 4.7 %collective-permute-start.16 = (bf16[2,96,256]{2,1,0:T(8,128)(2,1)S(1)}, bf16[2,96,256]{2,1,0:T(8,128)(2,1)S(1)}, u32[]{:S(2)}, u32[]{:S(2)}) collective-permute-start(bf16[2,96,256]{2,1,0:T(8,128)(2,1)S(1)} %pad_maximum_fusion.7), channel_id=1, source_target_pairs={{0,16},{8,24},{16,0},{24,8},{1,17},{9,25},{17,1},{25,9},{2,18},{10... | collective-permute-start | bytes 294920 | tf_op jit(solution)/shard_map/ppermute | solution.py:21
  121.2 1.5 %collective-permute-start.17 = (bf16[96,1024]{1,0:T(8,128)(2,1)S(1)}, bf16[96,1024]{1,0:T(8,128)(2,1)S(1)}, u32[]{:S(2)}, u32[]{:S(2)}) collective-permute-start(bf16[96,1024]{1,0:T(8,128)(2,1)S(1)} %pad_maximum_fusion.5), channel_id=1, source_target_pairs={{0,8},{8,0},{16,24},{24,16},{1,9},{9,1},{17,25},{25,17},{2,10},{10... | collective-permute-start | bytes 589832 | tf_op jit(solution)/shard_map/ppermute | solution.py:21

commit v5 on v4

--- a/solution.py
+++ b/solution.py
@@ -57,38 +57,57 @@
         result.wait()
 
 
+def self_kernel(core_ref, features_hbm, mine_hbm, other_hbm, out_hbm, features, weights, out, in_sems, out_sems):
+    rows = features.shape[0]
+    chunk = 256
+    core = core_ref[0]
+    copies = [
+        pltpu.make_async_copy(mine_hbm, weights, in_sems.at[0]),
+        pltpu.make_async_copy(features_hbm, features, in_sems.at[1]),
+    ]
+    pl.when(core == 0)(copies[0].start)
+    pl.when(core != 0)(pltpu.make_async_copy(other_hbm, weights, in_sems.at[0]).start)
+    copies[1].start()
+    for copy in copies:
+        copy.wait()
+    results = []
+    for index in range(rows // chunk):
+        at = slice(index * chunk, (index + 1) * chunk)
+        out[at, :] = jnp.dot(features[at, :], weights[...], preferred_element_type=F32)
+        results.append(pltpu.make_async_copy(out.at[at, :], out_hbm.at[at, :], out_sems.at[index]))
+        results[-1].start()
+    for result in results:
+        result.wait()
+
+
 def layer_kernel(
     core_ref,
     into_ref,
     slots_hbm,
-    features_hbm,
+    total_hbm,
     turned_hbm,
     cotangent_hbm,
-    mine_first_hbm,
-    mine_second_hbm,
-    other_first_hbm,
-    other_second_hbm,
+    mine_hbm,
+    other_hbm,
     aggregate_hbm,
     grad_hbm,
     sent_hbm,
     slots,
-    features,
+    total,
     turned,
     cotangent,
-    w_self,
     w_neigh,
     summed,
     aggregate,
     grad,
     sent,
     slot_sems,
-    weight_sems,
+    weight_sem,
     row_sems,
     out_sems,
 ):
     senders, block, _ = slots.shape
-    rows, width = features.shape
-    split = mine_first_hbm.shape[1]
+    rows = total.shape[0]
     chunk = 256
     core = core_ref[0]
     arrivals = [
@@ -96,31 +115,13 @@
     ]
     for arrival in arrivals:
         arrival.start()
-
-    def weight_copies(first_hbm, second_hbm, target, index):
-        return [
-            pltpu.make_async_copy(first_hbm, target.at[:, :split], weight_sems.at[index]),
-            pltpu.make_async_copy(second_hbm, target.at[:, split:], weight_sems.at[index + 1]),
-        ]
-
-    mine = (mine_first_hbm, mine_second_hbm)
-    other = (other_first_hbm, other_second_hbm)
-
-    @pl.when(core == 0)
-    def _():
-        for copy in weight_copies(*mine, w_self, 0) + weight_copies(*other, w_neigh, 2):
-            copy.start()
-
-    @pl.when(core != 0)
-    def _():
-        for copy in weight_copies(*other, w_self, 0) + weight_copies(*mine, w_neigh, 2):
-            copy.start()
-
-    weights = weight_copies(*mine, w_self, 0) + weight_copies(*other, w_neigh, 2)
+    weights = pltpu.make_async_copy(other_hbm, w_neigh, weight_sem.at[0])
+    pl.when(core == 0)(weights.start)
+    pl.when(core != 0)(pltpu.make_async_copy(mine_hbm, w_neigh, weight_sem.at[0]).start)
     spans = [slice(first, first + chunk) for first in range(0, rows, chunk)]
     streams = [
         [
-            pltpu.make_async_copy(features_hbm.at[at, :], features.at[at, :], row_sems.at[0, index]),
+            pltpu.make_async_copy(total_hbm.at[at, :], total.at[at, :], row_sems.at[0, index]),
             pltpu.make_async_copy(cotangent_hbm.at[at, :], cotangent.at[at, :], row_sems.at[1, index]),
         ]
         for index, at in enumerate(spans)
@@ -139,15 +140,14 @@
     aggregate[...] = summed[...].astype(BF16)
     results = [pltpu.make_async_copy(aggregate, aggregate_hbm, out_sems.at[1])]
     results[0].start()
-    for copy in weights:
-        copy.wait()
+    weights.wait()
     span = 512
     for index, at in enumerate(spans):
         for copy in streams[index]:
             copy.wait()
         for first in range(0, grad.shape[1], span):
             columns = slice(first, first + span)
-            value = jnp.dot(features[at, :], w_self[:, columns], preferred_element_type=F32) + jnp.dot(
+            value = total[at, columns] + jnp.dot(
                 aggregate[at, :], w_neigh[:, columns], preferred_element_type=F32
             )
             square = value * value
@@ -280,18 +280,8 @@
     core_arg = core.astype(jnp.int32).reshape(1)
 
     own = jnp.where(core == 0, w_self, w_neigh)
-    split = hidden // 4
-    share = split // parts
-    rest = (hidden - split) // parts
-    held = jnp.concatenate(
-        [
-            lax.dynamic_slice_in_dim(own, high * share, share, 1),
-            lax.dynamic_slice_in_dim(own, split + high * rest, rest, 1),
-        ],
-        axis=1,
-    )[None]
-    step = dom_size // 2
-    other = swap(held, "dom", step)
+    held = lax.dynamic_slice_in_dim(own, high * (hidden // parts), hidden // parts, 1)
+    pieces = [held] + [swap(held, "dom", 2 * step) for step in range(1, dom_size // 2)]
     slots = call(
         slots_kernel,
         jax.ShapeDtypeStruct((dom_size * block, width), BF16),
@@ -310,19 +300,31 @@
         flops=2 * dom_size * block * rows * width,
         moved=tile_vals.size * 2 + rows * width * 4,
     )(tile_src, tile_peer, tile_vals, features)
+    *pieces, slots = lax.optimization_barrier((*pieces, slots))
     received = lax.all_to_all(slots.reshape(dom_size, block, width), "dom", split_axis=0, concat_axis=0, tiled=True)
-
-    other, _ = lax.optimization_barrier((other, slots))
-    while step > 1:
-        held = joined(held, other, (me & step) != 0, 1).reshape(-1, *held.shape[1:])
-        step //= 2
-        if step > 1:
-            other = swap(held, "dom", step)
-    weights = [
-        gather_high(gather_low(held[..., :share], me), high),
-        gather_low(gather_high(held[..., share:], high), me),
-    ]
-    weights += [swap(weight, "rep", 1) for weight in weights]
+    bit = 1
+    while len(pieces) > 1:
+        upper = (place & bit) != 0
+        pieces = [joined(pieces[at], pieces[at + 1], upper, 0) for at in range(0, len(pieces), 2)]
+        pieces = [piece.reshape(-1, *held.shape) for piece in pieces]
+        bit *= 2
+    mine = gather_high(gather_low(pieces[0], me), high)
+    other = swap(mine, "rep", 1)
+    total = call(
+        self_kernel,
+        jax.ShapeDtypeStruct((rows, hidden), F32),
+        [SMEM] + [HBM] * 3,
+        HBM,
+        [
+            pltpu.VMEM((rows, width), BF16),
+            pltpu.VMEM((width, hidden), BF16),
+            pltpu.VMEM((rows, hidden), F32),
+            DMA((2,)),
+            DMA((rows // 256,)),
+        ],
+        flops=2 * rows * width * hidden,
+        moved=8 * rows * hidden,
+    )(core_arg, features, mine, other)
     turned = features.T
 
     aggregate, grad, sent = call(
@@ -332,28 +334,27 @@
             jax.ShapeDtypeStruct((rows, hidden), BF16),
             jax.ShapeDtypeStruct((width, hidden), BF16),
         ],
-        [SMEM, SMEM] + [HBM] * 8,
+        [SMEM, SMEM] + [HBM] * 6,
         [HBM] * 3,
         [
             pltpu.VMEM((dom_size, block, width), BF16),
-            pltpu.VMEM((rows, width), BF16),
+            pltpu.VMEM((rows, hidden), F32),
             pltpu.VMEM((width, rows), BF16),
             pltpu.VMEM((rows, hidden), BF16),
-            pltpu.VMEM((width, hidden), BF16),
             pltpu.VMEM((width, hidden), BF16),
             pltpu.VMEM((rows, width), F32),
             pltpu.VMEM((rows, width), BF16),
             pltpu.VMEM((rows, hidden), BF16),
             pltpu.VMEM((width, hidden), BF16),
             DMA((dom_size,)),
-            DMA((4,)),
+            DMA((1,)),
             DMA((2, rows // 256)),
             DMA((2 + rows // 256 + width // 256,)),
         ],
         flops=6 * rows * width * hidden,
         moved=16 * rows * hidden,
-    )(core_arg, in_block, received, features, turned, cotangent, *weights)
-    other = swap(sent, "rep", 1)
+    )(core_arg, in_block, received, total, turned, cotangent, mine, other)
+    arrived = swap(sent, "rep", 1)
     kept = call(
         kept_kernel,
         jax.ShapeDtypeStruct((width, hidden), BF16),
@@ -369,9 +370,8 @@
         ],
         flops=2 * rows * width * hidden,
         moved=6 * rows * hidden,
-        vmem=16,
     )(core_arg, turned, aggregate, grad)
-    chip = added(kept, other).reshape(dom_size, width // dom_size, hidden)
+    chip = added(kept, arrived).reshape(dom_size, width // dom_size, hidden)
     first, second = chip[:, :, : hidden // 2], chip[:, :, hidden // 2 :]
     first, second = reduce_low(first, low), reduce_high(second, high)
     first, second = reduce_high(first, high), reduce_low(second, low)

time: 124 us -> 122 us (0.984)
  Pallas kernels: 20 us -> 25.4 us
  waiting for transfers between devices: 68.4 us -> 63.3 us
  local copies, waits for them, and re-layouts: 5.85 us -> 3.53 us
  other arithmetic: 3.79 us -> 5.15 us
  starting transfers between devices: 24.6 us -> 23.3 us
    ppermute x18 -> x16, waiting for transfers between devices: 68.4 us -> 46.5 us  [swap(): lax.ppermute(value, axis, [(index, index ^ step) for index in range(size)])]
    all_to_all x1, waiting for transfers between devices: 0.01 us -> 16.8 us  [shards(): lax.all_to_all(slots.reshape(dom_size, block, width), 'dom', split_axis=0...]
    pallas_call x0 -> x1, Pallas kernels: none -> 4.69 us  [shards(): call(self_kernel, jax.ShapeDtypeStruct((rows, hidden), F32), [SMEM] + [HB...]
    pallas_call x1, Pallas kernels: 2.54 us -> 4.7 us  [shards(): call(kept_kernel, jax.ShapeDtypeStruct((width, hidden), BF16), [SMEM] + [...]
    unnamed x15 -> x5, local copies, waits for them, and re-layouts: 5.38 us -> 3.24 us
    pallas_call x1, Pallas kernels: 12.9 us -> 11.5 us  [shards(): call(layer_kernel, [jax.ShapeDtypeStruct((rows, width), BF16), jax.ShapeD...]
    convert_element_type x5, other arithmetic: 1.03 us -> 2.42 us  [added(): return (left.astype(F32) + right.astype(F32)).astype(BF16)]
    ppermute x18 -> x16, starting transfers between devices: 18 us -> 17.8 us  [swap(): lax.ppermute(value, axis, [(index, index ^ step) for index in range(size)])]
  transfers between devices with their start and end apart: 19 -> 17, of which waited for: 14 -> 12; matrix products, arithmetic and copies ran while one was open for 2% -> 2% of each run, Pallas kernels for 6% -> 11%
where the time goes in v5:
time: 122 us
  waiting for transfers between devices  63.3 us (52%)
  Pallas kernels  25.4 us (21%)
  starting transfers between devices  23.3 us (19%)
  other arithmetic  5.15 us (4%)
  local copies, waits for them, and re-layouts  3.53 us (3%)
    ppermute x16, waiting for transfers between devices, swap(): lax.ppermute(value, axis, [(index, index ^ step) for index in range(size)])  46.5 us
    ppermute x16, starting transfers between devices, swap(): lax.ppermute(value, axis, [(index, index ^ step) for index in range(size)])  17.8 us
    all_to_all x1, waiting for transfers between devices, shards(): lax.all_to_all(slots.reshape(dom_size, block, width), 'dom', split_axis=0...  16.8 us
    pallas_call x1, Pallas kernels, shards(): call(layer_kernel, [jax.ShapeDtypeStruct((rows, width), BF16), jax.ShapeD...  11.5 us
    all_to_all x1, starting transfers between devices, shards(): lax.all_to_all(slots.reshape(dom_size, block, width), 'dom', split_axis=0...  5.52 us
    pallas_call x1, Pallas kernels, shards(): call(kept_kernel, jax.ShapeDtypeStruct((width, hidden), BF16), [SMEM] + [...  4.7 us
    pallas_call x1, Pallas kernels, shards(): call(self_kernel, jax.ShapeDtypeStruct((rows, hidden), F32), [SMEM] + [HB...  4.69 us
    pallas_call x1, Pallas kernels, shards(): call(slots_kernel, jax.ShapeDtypeStruct((dom_size * block, width), BF16),...  4.54 us
  transfers between devices with their start and end apart: 17, of which 12 were waited for; matrix products, arithmetic and copies ran while one was open for 2% of the time, Pallas kernels for 11%

profile of v5, /device:TPU:0, one launch (start us, length us, event | category | flops | bytes accessed | tf_op | source)
XLA Modules:
  0.0 121.6 jit_solution(12906794596910198805)
XLA Ops:
  0.6 1.0 dynamic-slice_select_fusion
  1.6 3.1 %collective-permute-start = (bf16[96,512]{1,0:T(8,128)(2,1)S(1)}, bf16[96,512]{1,0:T(8,128)(2,1)S(1)}, u32[]{:S(2)}, u32[]{:S(2)}) collective-permute-start(bf16[96,512]{1,0:T(8,128)(2,1)S(1)} %dynamic-slice_select_fusion), channel_id=1, source_target_pairs={{0,2},{1,3},{2,0},{3,1},{4,6},{5,7},{6,4},{7,5},{8,10},{9,11},{10,... | collective-permute-start | bytes 294920 | tf_op jit(solution)/shard_map/ppermute | solution.py:21
  4.7 2.6 %collective-permute-start.1 = (bf16[96,512]{1,0:T(8,128)(2,1)S(1)}, bf16[96,512]{1,0:T(8,128)(2,1)S(1)}, u32[]{:S(2)}, u32[]{:S(2)}) collective-permute-start(bf16[96,512]{1,0:T(8,128)(2,1)S(1)} %dynamic-slice_select_fusion), channel_id=1, source_target_pairs={{0,4},{1,5},{2,6},{3,7},{4,0},{5,1},{6,2},{7,3},{8,12},{9,13},{10,... | collective-permute-start | bytes 294920 | tf_op jit(solution)/shard_map/ppermute | solution.py:21
  7.3 4.5 %shard_map.95 = bf16[1024,768]{1,0:T(8,128)(2,1)} custom-call(s32[32]{0:T(128)} %src_hbm.1, s32[32]{0:T(128)} %peer_hbm.1, bf16[32,128,128]{2,1,0:T(8,128)(2,1)} %tiles_hbm.1, bf16[1024,768]{1,0:T(8,128)(2,1)} %features_hbm.3), custom_call_target="tpu_custom_call" | custom-call | flops 1610612736 | bytes 4194304 | tf_op jit(solution)/shard_map/pallas_call | solution.py:285
  11.8 3.3 %collective-permute-done.1 = bf16[96,512]{1,0:T(8,128)(2,1)S(1)} collective-permute-done((bf16[96,512]{1,0:T(8,128)(2,1)S(1)}, bf16[96,512]{1,0:T(8,128)(2,1)S(1)}, u32[]{:S(2)}, u32[]{:S(2)}) %collective-permute-start.1) | collective-permute-done | bytes 98336 | tf_op jit(solution)/shard_map/ppermute | solution.py:21
  15.3 1.6 %collective-permute-start.3 = (bf16[4,96,512]{2,1,0:T(8,128)(2,1)S(1)}, bf16[4,96,512]{2,1,0:T(8,128)(2,1)S(1)}, u32[]{:S(2)}, u32[]{:S(2)}) collective-permute-start(bf16[4,96,512]{2,1,0:T(8,128)(2,1)S(1)} %bitcast.63), channel_id=1, source_target_pairs={{0,1},{1,0},{2,3},{3,2},{4,5},{5,4},{6,7},{7,6},{8,9},{9,8},{10,11... | collective-permute-start | bytes 1179656 | tf_op jit(solution)/shard_map/ppermute | solution.py:21
  16.8 7.5 %collective-permute-done.3 = bf16[4,96,512]{2,1,0:T(8,128)(2,1)S(1)} collective-permute-done((bf16[4,96,512]{2,1,0:T(8,128)(2,1)S(1)}, bf16[4,96,512]{2,1,0:T(8,128)(2,1)S(1)}, u32[]{:S(2)}, u32[]{:S(2)}) %collective-permute-start.3) | collective-permute-done | bytes 393248 | tf_op jit(solution)/shard_map/ppermute | solution.py:21
  24.5 1.6 %collective-permute-start.4 = (bf16[768,512]{1,0:T(8,128)(2,1)S(1)}, bf16[768,512]{1,0:T(8,128)(2,1)S(1)}, u32[]{:S(2)}, u32[]{:S(2)}) collective-permute-start(bf16[768,512]{1,0:T(8,128)(2,1)S(1)} %bitcast.62), channel_id=1, source_target_pairs={{0,16},{8,24},{16,0},{24,8},{1,17},{9,25},{17,1},{25,9},{2,18},{10... | collective-permute-start | bytes 2359304 | tf_op jit(solution)/shard_map/ppermute | solution.py:21
  26.1 5.5 %all-to-all-start = ((bf16[8,128,768]{2,1,0:T(8,128)(2,1)}), bf16[8,128,768]{2,1,0:T(8,128)(2,1)}, u32[]{:S(2)}, u32[]{:S(2)}) async-start(bf16[8,128,768]{2,1,0:T(8,128)(2,1)} %bitcast.2), calls=%async_computation | async-start | bytes 3145728 | tf_op jit(solution)/shard_map/all_to_all | solution.py:304
  31.6 9.4 %collective-permute-done.4 = bf16[768,512]{1,0:T(8,128)(2,1)S(1)} collective-permute-done((bf16[768,512]{1,0:T(8,128)(2,1)S(1)}, bf16[768,512]{1,0:T(8,128)(2,1)S(1)}, u32[]{:S(2)}, u32[]{:S(2)}) %collective-permute-start.4) | collective-permute-done | bytes 786464 | tf_op jit(solution)/shard_map/ppermute | solution.py:21
  41.5 1.6 %copy-done = bf16[1024,768]{1,0:T(8,128)(2,1)S(1)} copy-done((bf16[1024,768]{1,0:T(8,128)(2,1)S(1)}, bf16[1024,768]{1,0:T(8,128)(2,1)}, u32[]{:S(2)}) %copy-start) | copy-done | bytes 1572888
  43.1 1.6 %copy.12 = bf16[1024,768]{0,1:T(8,128)(2,1)} copy(bf16[1024,768]{1,0:T(8,128)(2,1)S(1)} %copy-done) | data formatting | bytes 3145728 | tf_op args[0]
  44.7 0.3 collective-permute-done.5.other_hbm
  45.0 4.7 %shard_map.96.total_hbm = f32[1024,1024]{1,0:T(8,128)} custom-call(s32[1]{0:T(128)} %bitcast.core_ref, bf16[1024,768]{1,0:T(8,128)(2,1)} %features_hbm.3, bf16[768,1024]{1,0:T(8,128)(2,1)} %copy-done.1, bf16[768,1024]{1,0:T(8,128)(2,1)} %collective-permute-done.5.other_hbm), custom_call_target="tpu_custom_call" | custom-call | flops 1610612736 | bytes 8388608 | tf_op jit(solution)/shard_map/pallas_call | solution.py:313
  49.7 16.8 %all-to-all-done.slots_hbm = bf16[8,128,768]{2,1,0:T(8,128)(2,1)} async-done(((bf16[8,128,768]{2,1,0:T(8,128)(2,1)}), bf16[8,128,768]{2,1,0:T(8,128)(2,1)}, u32[]{:S(2)}, u32[]{:S(2)}) %all-to-all-start) | async-done | bytes 1572896 | tf_op jit(solution)/shard_map/all_to_all | solution.py:304
  66.5 11.5 %shard_map.97 = (bf16[1024,768]{1,0:T(8,128)(2,1)}, bf16[1024,1024]{1,0:T(8,128)(2,1)}, bf16[768,1024]{1,0:T(8,128)(2,1)}) custom-call(s32[1]{0:T(128)} %bitcast.core_ref, s32[8]{0:T(128)} %into_ref.1, bf16[8,128,768]{2,1,0:T(8,128)(2,1)} %all-to-all-done.slots_hbm, f32[1024,1024]{1,0:T(8,128)} %shard_map.96.total_hbm, bf16[768,1024]{1,0:T(8,128)(2,1)} %bitcast.57, ...), custom_call_target="tpu_custom_call" | custom-call | flops 4831838208 | bytes 16777216 | tf_op jit(solution)/shard_map/pallas_call | solution.py:330
  78.1 4.7 %shard_map.98 = bf16[768,1024]{1,0:T(8,128)(2,1)} custom-call(s32[1]{0:T(128)} %bitcast.core_ref, bf16[768,1024]{1,0:T(8,128)(2,1)} %bitcast.58, bf16[1024,768]{1,0:T(8,128)(2,1)} %get-tuple-element.15.aggregate_hbm, bf16[1024,1024]{1,0:T(8,128)(2,1)} %get-tuple-element.16.grad_hbm), custom_call_target="tpu_custom_call" | custom-call | flops 1610612736 | bytes 6291456 | tf_op jit(solution)/shard_map/pallas_call | solution.py:358
  82.9 2.1 %add_convert_fusion = bf16[768,1024]{1,0:T(8,128)(2,1)S(1)} fusion(bf16[768,1024]{1,0:T(8,128)(2,1)S(1)} %collective-permute-done.6, bf16[768,1024]{1,0:T(8,128)(2,1)} %shard_map.98), kind=kLoop, calls=%fused_computation | loop fusion | flops 3145728 | bytes 4718592 | tf_op jit(solution)/shard_map/convert_element_type | solution.py:246
  85.2 0.6 collective-permute-start.9
  85.8 1.3 %collective-permute-start.7 = (bf16[4,96,512]{2,1,0:T(8,128)(2,1)S(1)}, bf16[4,96,512]{2,1,0:T(8,128)(2,1)S(1)}, u32[]{:S(2)}, u32[]{:S(2)}) collective-permute-start(bf16[4,96,512]{2,1,0:T(8,128)(2,1)S(1)} %dynamic-slice_bitcast_fusion), channel_id=1, source_target_pairs={{0,1},{1,0},{2,3},{3,2},{4,5},{5,4},{6,7},{7,6},{8,9},{9,8},{10,11... | collective-permute-start | bytes 1179656 | tf_op jit(solution)/shard_map/ppermute | solution.py:21
  87.1 9.7 %collective-permute-done.9 = bf16[8,96,256]{2,1,0:T(8,128)(2,1)S(1)} collective-permute-done((bf16[8,96,256]{2,1,0:T(8,128)(2,1)S(1)}, bf16[8,96,256]{2,1,0:T(8,128)(2,1)S(1)}, u32[]{:S(2)}, u32[]{:S(2)}) %collective-permute-start.9) | collective-permute-done | bytes 393248 | tf_op jit(solution)/shard_map/ppermute | solution.py:21
  96.9 1.3 %collective-permute-start.10 = (bf16[4,96,256]{2,1,0:T(8,128)(2,1)S(1)}, bf16[4,96,256]{2,1,0:T(8,128)(2,1)S(1)}, u32[]{:S(2)}, u32[]{:S(2)}) collective-permute-start(bf16[4,96,256]{2,1,0:T(8,128)(2,1)S(1)} %dynamic-slice_bitcast_fusion.1), channel_id=1, source_target_pairs={{0,1},{1,0},{2,3},{3,2},{4,5},{5,4},{6,7},{7,6},{8,9},{9,8},{10,11... | collective-permute-start | bytes 589832 | tf_op jit(solution)/shard_map/ppermute | solution.py:21
  98.3 0.6 collective-permute-start.8
  98.9 4.6 %collective-permute-done.10 = bf16[4,96,256]{2,1,0:T(8,128)(2,1)S(1)} collective-permute-done((bf16[4,96,256]{2,1,0:T(8,128)(2,1)S(1)}, bf16[4,96,256]{2,1,0:T(8,128)(2,1)S(1)}, u32[]{:S(2)}, u32[]{:S(2)}) %collective-permute-start.10) | collective-permute-done | bytes 196640 | tf_op jit(solution)/shard_map/ppermute | solution.py:21
  103.6 1.1 collective-permute-done.8
  104.8 2.0 %collective-permute-start.12 = (bf16[96,512]{1,0:T(8,128)(2,1)S(1)}, bf16[96,512]{1,0:T(8,128)(2,1)S(1)}, u32[]{:S(2)}, u32[]{:S(2)}) collective-permute-start(bf16[96,512]{1,0:T(8,128)(2,1)S(1)} %get-tuple-element.27), channel_id=1, source_target_pairs={{0,4},{1,5},{2,6},{3,7},{4,0},{5,1},{6,2},{7,3},{8,12},{9,13},{10,... | collective-permute-start | bytes 294920 | tf_op jit(solution)/shard_map/ppermute | solution.py:21
  106.9 2.4 %collective-permute-start.13 = (bf16[96,512]{1,0:T(8,128)(2,1)S(1)}, bf16[96,512]{1,0:T(8,128)(2,1)S(1)}, u32[]{:S(2)}, u32[]{:S(2)}) collective-permute-start(bf16[96,512]{1,0:T(8,128)(2,1)S(1)} %get-tuple-element.28), channel_id=1, source_target_pairs={{0,6},{1,7},{2,4},{3,5},{4,2},{5,3},{6,0},{7,1},{8,14},{9,15},{10,... | collective-permute-start | bytes 294920 | tf_op jit(solution)/shard_map/ppermute | solution.py:21
  109.4 4.9 %collective-permute-done.12 = bf16[96,512]{1,0:T(8,128)(2,1)S(1)} collective-permute-done((bf16[96,512]{1,0:T(8,128)(2,1)S(1)}, bf16[96,512]{1,0:T(8,128)(2,1)S(1)}, u32[]{:S(2)}, u32[]{:S(2)}) %collective-permute-start.12) | collective-permute-done | bytes 98336 | tf_op jit(solution)/shard_map/ppermute | solution.py:21
  114.4 0.6 collective-permute-start.14
  115.0 4.1 %collective-permute-done.14 = bf16[2,96,256]{2,1,0:T(8,128)(2,1)S(1)} collective-permute-done((bf16[2,96,256]{2,1,0:T(8,128)(2,1)S(1)}, bf16[2,96,256]{2,1,0:T(8,128)(2,1)S(1)}, u32[]{:S(2)}, u32[]{:S(2)}) %collective-permute-start.14) | collective-permute-done | bytes 98336 | tf_op jit(solution)/shard_map/ppermute | solution.py:21
  119.2 1.4 %collective-permute-done.15 = bf16[96,1024]{1,0:T(8,128)(2,1)S(1)} collective-permute-done((bf16[96,1024]{1,0:T(8,128)(2,1)S(1)}, bf16[96,1024]{1,0:T(8,128)(2,1)S(1)}, u32[]{:S(2)}, u32[]{:S(2)}) %collective-permute-start.15) | collective-permute-done | bytes 196640 | tf_op jit(solution)/shard_map/ppermute | solution.py:21
  120.7 1.0 select_convert_fusion
  (37 shorter events, 2.0 us)
Async XLA Ops:
  1.6 10.2 %collective-permute-start = (bf16[96,512]{1,0:T(8,128)(2,1)S(1)}, bf16[96,512]{1,0:T(8,128)(2,1)S(1)}, u32[]{:S(2)}, u32[]{:S(2)}) collective-permute-start(bf16[96,512]{1,0:T(8,128)(2,1)S(1)} %dynamic-slice_select_fusion), channel_id=1, source_target_pairs={{0,2},{1,3},{2,0},{3,1},{4,6},{5,7},{6,4},{7,5},{8,10},{9,11},{10,... | collective-permute-start | bytes 294920 | tf_op jit(solution)/shard_map/ppermute | solution.py:21
  4.7 10.4 %collective-permute-start.1 = (bf16[96,512]{1,0:T(8,128)(2,1)S(1)}, bf16[96,512]{1,0:T(8,128)(2,1)S(1)}, u32[]{:S(2)}, u32[]{:S(2)}) collective-permute-start(bf16[96,512]{1,0:T(8,128)(2,1)S(1)} %dynamic-slice_select_fusion), channel_id=1, source_target_pairs={{0,4},{1,5},{2,6},{3,7},{4,0},{5,1},{6,2},{7,3},{8,12},{9,13},{10,... | collective-permute-start | bytes 294920 | tf_op jit(solution)/shard_map/ppermute | solution.py:21
  7.3 7.8 %collective-permute-start.2 = (bf16[96,512]{1,0:T(8,128)(2,1)S(1)}, bf16[96,512]{1,0:T(8,128)(2,1)S(1)}, u32[]{:S(2)}, u32[]{:S(2)}) collective-permute-start(bf16[96,512]{1,0:T(8,128)(2,1)S(1)} %dynamic-slice_select_fusion), channel_id=1, source_target_pairs={{0,6},{1,7},{2,4},{3,5},{4,2},{5,3},{6,0},{7,1},{8,14},{9,15},{10,... | collective-permute-start | bytes 294920 | tf_op jit(solution)/shard_map/ppermute | solution.py:21
  15.3 9.0 %collective-permute-start.3 = (bf16[4,96,512]{2,1,0:T(8,128)(2,1)S(1)}, bf16[4,96,512]{2,1,0:T(8,128)(2,1)S(1)}, u32[]{:S(2)}, u32[]{:S(2)}) collective-permute-start(bf16[4,96,512]{2,1,0:T(8,128)(2,1)S(1)} %bitcast.63), channel_id=1, source_target_pairs={{0,1},{1,0},{2,3},{3,2},{4,5},{5,4},{6,7},{7,6},{8,9},{9,8},{10,11... | collective-permute-start | bytes 1179656 | tf_op jit(solution)/shard_map/ppermute | solution.py:21
  24.5 16.5 %collective-permute-start.4 = (bf16[768,512]{1,0:T(8,128)(2,1)S(1)}, bf16[768,512]{1,0:T(8,128)(2,1)S(1)}, u32[]{:S(2)}, u32[]{:S(2)}) collective-permute-start(bf16[768,512]{1,0:T(8,128)(2,1)S(1)} %bitcast.62), channel_id=1, source_target_pairs={{0,16},{8,24},{16,0},{24,8},{1,17},{9,25},{17,1},{25,9},{2,18},{10... | collective-permute-start | bytes 2359304 | tf_op jit(solution)/shard_map/ppermute | solution.py:21
  26.1 40.5 %all-to-all-start = ((bf16[8,128,768]{2,1,0:T(8,128)(2,1)}), bf16[8,128,768]{2,1,0:T(8,128)(2,1)}, u32[]{:S(2)}, u32[]{:S(2)}) async-start(bf16[8,128,768]{2,1,0:T(8,128)(2,1)} %bitcast.2), calls=%async_computation | async-start | bytes 3145728 | tf_op jit(solution)/shard_map/all_to_all | solution.py:304
  41.2 1.9 %copy-start = (bf16[1024,768]{1,0:T(8,128)(2,1)S(1)}, bf16[1024,768]{1,0:T(8,128)(2,1)}, u32[]{:S(2)}) copy-start(bf16[1024,768]{1,0:T(8,128)(2,1)} %features_hbm.3) | copy-start | bytes 4718596
  41.4 3.3 %copy-start.1 = (bf16[768,1024]{1,0:T(8,128)(2,1)}, bf16[768,1024]{1,0:T(8,128)(2,1)S(1)}, u32[]{:S(2)}) copy-start(bf16[768,1024]{1,0:T(8,128)(2,1)S(1)} %pad_maximum_fusion.mine_hbm) | copy-start | bytes 4718596
  41.4 3.6 %collective-permute-start.5 = (bf16[768,1024]{1,0:T(8,128)(2,1)S(1)}, bf16[768,1024]{1,0:T(8,128)(2,1)}, u32[]{:S(2)}, u32[]{:S(2)}) collective-permute-start(bf16[768,1024]{1,0:T(8,128)(2,1)S(1)} %pad_maximum_fusion.mine_hbm), channel_id=1, source_target_pairs={{0,8},{8,0},{16,24},{24,16},{1,9},{9,1},{17,25},{25,17},{2,10},{10... | collective-permute-start | bytes 4718600 | tf_op jit(solution)/shard_map/ppermute | solution.py:21
  78.1 4.8 %collective-permute-start.6 = (bf16[768,1024]{1,0:T(8,128)(2,1)}, bf16[768,1024]{1,0:T(8,128)(2,1)S(1)}, u32[]{:S(2)}, u32[]{:S(2)}) collective-permute-start(bf16[768,1024]{1,0:T(8,128)(2,1)} %get-tuple-element.17), channel_id=1, source_target_pairs={{0,8},{8,0},{16,24},{24,16},{1,9},{9,1},{17,25},{25,17},{2,10},{10... | collective-permute-start | bytes 4718600 | tf_op jit(solution)/shard_map/ppermute | solution.py:21
  85.2 11.6 %collective-permute-start.9 = (bf16[8,96,256]{2,1,0:T(8,128)(2,1)S(1)}, bf16[8,96,256]{2,1,0:T(8,128)(2,1)S(1)}, u32[]{:S(2)}, u32[]{:S(2)}) collective-permute-start(bf16[8,96,256]{2,1,0:T(8,128)(2,1)S(1)} %constant_dynamic-slice_fusion), channel_id=1, source_target_pairs={{0,16},{8,24},{16,0},{24,8},{1,17},{9,25},{17,1},{25,9},{2,18},{10... | collective-permute-start | bytes 1179656 | tf_op jit(solution)/shard_map/ppermute | solution.py:21
  85.8 12.4 %collective-permute-start.7 = (bf16[4,96,512]{2,1,0:T(8,128)(2,1)S(1)}, bf16[4,96,512]{2,1,0:T(8,128)(2,1)S(1)}, u32[]{:S(2)}, u32[]{:S(2)}) collective-permute-start(bf16[4,96,512]{2,1,0:T(8,128)(2,1)S(1)} %dynamic-slice_bitcast_fusion), channel_id=1, source_target_pairs={{0,1},{1,0},{2,3},{3,2},{4,5},{5,4},{6,7},{7,6},{8,9},{9,8},{10,11... | collective-permute-start | bytes 1179656 | tf_op jit(solution)/shard_map/ppermute | solution.py:21
  96.9 6.6 %collective-permute-start.10 = (bf16[4,96,256]{2,1,0:T(8,128)(2,1)S(1)}, bf16[4,96,256]{2,1,0:T(8,128)(2,1)S(1)}, u32[]{:S(2)}, u32[]{:S(2)}) collective-permute-start(bf16[4,96,256]{2,1,0:T(8,128)(2,1)S(1)} %dynamic-slice_bitcast_fusion.1), channel_id=1, source_target_pairs={{0,1},{1,0},{2,3},{3,2},{4,5},{5,4},{6,7},{7,6},{8,9},{9,8},{10,11... | collective-permute-start | bytes 589832 | tf_op jit(solution)/shard_map/ppermute | solution.py:21
  98.3 6.3 %collective-permute-start.8 = (bf16[4,96,256]{2,1,0:T(8,128)(2,1)S(1)}, bf16[4,96,256]{2,1,0:T(8,128)(2,1)S(1)}, u32[]{:S(2)}, u32[]{:S(2)}) collective-permute-start(bf16[4,96,256]{2,1,0:T(8,128)(2,1)S(1)} %constant_dynamic-slice_fusion.1), channel_id=1, source_target_pairs={{0,16},{8,24},{16,0},{24,8},{1,17},{9,25},{17,1},{25,9},{2,18},{10... | collective-permute-start | bytes 589832 | tf_op jit(solution)/shard_map/ppermute | solution.py:21
  104.8 4.7 %collective-permute-start.11 = (bf16[96,512]{1,0:T(8,128)(2,1)S(1)}, bf16[96,512]{1,0:T(8,128)(2,1)S(1)}, u32[]{:S(2)}, u32[]{:S(2)}) collective-permute-start(bf16[96,512]{1,0:T(8,128)(2,1)S(1)} %get-tuple-element.26), channel_id=1, source_target_pairs={{0,2},{1,3},{2,0},{3,1},{4,6},{5,7},{6,4},{7,5},{8,10},{9,11},{10,... | collective-permute-start | bytes 294920 | tf_op jit(solution)/shard_map/ppermute | solution.py:21
  104.8 9.5 %collective-permute-start.12 = (bf16[96,512]{1,0:T(8,128)(2,1)S(1)}, bf16[96,512]{1,0:T(8,128)(2,1)S(1)}, u32[]{:S(2)}, u32[]{:S(2)}) collective-permute-start(bf16[96,512]{1,0:T(8,128)(2,1)S(1)} %get-tuple-element.27), channel_id=1, source_target_pairs={{0,4},{1,5},{2,6},{3,7},{4,0},{5,1},{6,2},{7,3},{8,12},{9,13},{10,... | collective-permute-start | bytes 294920 | tf_op jit(solution)/shard_map/ppermute | solution.py:21
  106.9 7.5 %collective-permute-start.13 = (bf16[96,512]{1,0:T(8,128)(2,1)S(1)}, bf16[96,512]{1,0:T(8,128)(2,1)S(1)}, u32[]{:S(2)}, u32[]{:S(2)}) collective-permute-start(bf16[96,512]{1,0:T(8,128)(2,1)S(1)} %get-tuple-element.28), channel_id=1, source_target_pairs={{0,6},{1,7},{2,4},{3,5},{4,2},{5,3},{6,0},{7,1},{8,14},{9,15},{10,... | collective-permute-start | bytes 294920 | tf_op jit(solution)/shard_map/ppermute | solution.py:21
  114.4 4.7 %collective-permute-start.14 = (bf16[2,96,256]{2,1,0:T(8,128)(2,1)S(1)}, bf16[2,96,256]{2,1,0:T(8,128)(2,1)S(1)}, u32[]{:S(2)}, u32[]{:S(2)}) collective-permute-start(bf16[2,96,256]{2,1,0:T(8,128)(2,1)S(1)} %pad_maximum_fusion.7), channel_id=1, source_target_pairs={{0,16},{8,24},{16,0},{24,8},{1,17},{9,25},{17,1},{25,9},{2,18},{10... | collective-permute-start | bytes 294920 | tf_op jit(solution)/shard_map/ppermute | solution.py:21
  119.2 1.5 %collective-permute-start.15 = (bf16[96,1024]{1,0:T(8,128)(2,1)S(1)}, bf16[96,1024]{1,0:T(8,128)(2,1)S(1)}, u32[]{:S(2)}, u32[]{:S(2)}) collective-permute-start(bf16[96,1024]{1,0:T(8,128)(2,1)S(1)} %pad_maximum_fusion.5), channel_id=1, source_target_pairs={{0,8},{8,0},{16,24},{24,16},{1,9},{9,1},{17,25},{25,17},{2,10},{10... | collective-permute-start | bytes 589832 | tf_op jit(solution)/shard_map/ppermute | solution.py:21

commit v6 on v4

--- a/solution.py
+++ b/solution.py
@@ -227,11 +227,6 @@
     return jnp.stack([jnp.where(upper, other, held), jnp.where(upper, held, other)], axis=axis)
 
 
-def gather_low(held, me):
-    held = joined(held, swap(held, "dom", 1), (me & 1) != 0, 1)
-    return held.reshape(-1, held.shape[-1])
-
-
 def gather_high(held, high):
     step = 1
     while step < lax.axis_size("rep") // 2:
@@ -279,19 +274,11 @@
     low, place = me & 1, me >> 1
     core_arg = core.astype(jnp.int32).reshape(1)
 
+    share = hidden // parts
     own = jnp.where(core == 0, w_self, w_neigh)
-    split = hidden // 4
-    share = split // parts
-    rest = (hidden - split) // parts
-    held = jnp.concatenate(
-        [
-            lax.dynamic_slice_in_dim(own, high * share, share, 1),
-            lax.dynamic_slice_in_dim(own, split + high * rest, rest, 1),
-        ],
-        axis=1,
-    )[None]
-    step = dom_size // 2
-    other = swap(held, "dom", step)
+    held = lax.dynamic_slice_in_dim(own, high * share, share, 1)
+    top = dom_size // 2
+    pieces = [held] + [swap(held, "dom", step) for step in (1, top, top + 1)]
     slots = call(
         slots_kernel,
         jax.ShapeDtypeStruct((dom_size * block, width), BF16),
@@ -310,18 +297,18 @@
         flops=2 * dom_size * block * rows * width,
         moved=tile_vals.size * 2 + rows * width * 4,
     )(tile_src, tile_peer, tile_vals, features)
+    *pieces, _ = lax.optimization_barrier((*pieces, slots))
     received = lax.all_to_all(slots.reshape(dom_size, block, width), "dom", split_axis=0, concat_axis=0, tiled=True)
-
-    other, _ = lax.optimization_barrier((other, slots))
+    pairs = [joined(pieces[at], pieces[at + 1], low != 0, 0) for at in (0, 2)]
+    held = joined(*pairs, (me & top) != 0, 0)
+    step = top // 2
     while step > 1:
-        held = joined(held, other, (me & step) != 0, 1).reshape(-1, *held.shape[1:])
+        held = joined(held, swap(held, "dom", step), (me & step) != 0, 1)
+        held = held.reshape(-1, *held.shape[2:])
         step //= 2
-        if step > 1:
-            other = swap(held, "dom", step)
-    weights = [
-        gather_high(gather_low(held[..., :share], me), high),
-        gather_low(gather_high(held[..., share:], high), me),
-    ]
+    held = held.reshape(-1, share)
+    mine = gather_high(held, high)
+    weights = [mine[:, : hidden // 2], mine[:, hidden // 2 :]]
     weights += [swap(weight, "rep", 1) for weight in weights]
     turned = features.T
 
@@ -353,7 +340,7 @@
         flops=6 * rows * width * hidden,
         moved=16 * rows * hidden,
     )(core_arg, in_block, received, features, turned, cotangent, *weights)
-    other = swap(sent, "rep", 1)
+    arrived = swap(sent, "rep", 1)
     kept = call(
         kept_kernel,
         jax.ShapeDtypeStruct((width, hidden), BF16),
@@ -369,9 +356,8 @@
         ],
         flops=2 * rows * width * hidden,
         moved=6 * rows * hidden,
-        vmem=16,
     )(core_arg, turned, aggregate, grad)
-    chip = added(kept, other).reshape(dom_size, width // dom_size, hidden)
+    chip = added(kept, arrived).reshape(dom_size, width // dom_size, hidden)
     first, second = chip[:, :, : hidden // 2], chip[:, :, hidden // 2 :]
     first, second = reduce_low(first, low), reduce_high(second, high)
     first, second = reduce_high(first, high), reduce_low(second, low)

time: 124 us -> 135 us (1.089)
  starting transfers between devices: 24.6 us -> 29.7 us
  waiting for transfers between devices: 68.4 us -> 72.4 us
  other arithmetic: 3.79 us -> 6.95 us
  local copies, waits for them, and re-layouts: 5.85 us -> 2.87 us
  Pallas kernels: 20 us -> 22.1 us
    ppermute x18 -> x17, starting transfers between devices: 18 us -> 23.6 us  [swap(): lax.ppermute(value, axis, [(index, index ^ step) for index in range(size)])]
    ppermute x18 -> x17, waiting for transfers between devices: 68.4 us -> 72.4 us  [swap(): lax.ppermute(value, axis, [(index, index ^ step) for index in range(size)])]
    unnamed x15 -> x7, local copies, waits for them, and re-layouts: 5.38 us -> 2.51 us
    select_n x0 -> x2, other arithmetic: none -> 2.24 us  [the longest x1 2.2 us: gather_high(): jnp.where(upper, held, other)]
    pallas_call x1, Pallas kernels: 2.54 us -> 4.69 us  [shards(): call(kept_kernel, jax.ShapeDtypeStruct((width, hidden), BF16), [SMEM] + [...]
    convert_element_type x5, other arithmetic: 1.03 us -> 2.42 us  [added(): return (left.astype(F32) + right.astype(F32)).astype(BF16)]
  transfers between devices with their start and end apart: 19 -> 18, of which waited for: 14 -> 10; matrix products, arithmetic and copies ran while one was open for 2% -> 3% of each run, Pallas kernels for 6% -> 7%
where the time goes in v6:
time: 135 us
  waiting for transfers between devices  72.4 us (54%)
  starting transfers between devices  29.7 us (22%)
  Pallas kernels  22.1 us (16%)
  other arithmetic  6.95 us (5%)
  local copies, waits for them, and re-layouts  2.87 us (2%)
    ppermute x17, waiting for transfers between devices, swap(): lax.ppermute(value, axis, [(index, index ^ step) for index in range(size)])  72.4 us
    ppermute x17, starting transfers between devices, swap(): lax.ppermute(value, axis, [(index, index ^ step) for index in range(size)])  23.6 us
    pallas_call x1, Pallas kernels, shards(): call(layer_kernel, [jax.ShapeDtypeStruct((rows, width), BF16), jax.ShapeD...  12.8 us
    all_to_all x1, starting transfers between devices, shards(): lax.all_to_all(slots.reshape(dom_size, block, width), 'dom', split_axis=0...  6.12 us
    pallas_call x1, Pallas kernels, shards(): call(kept_kernel, jax.ShapeDtypeStruct((width, hidden), BF16), [SMEM] + [...  4.69 us
    pallas_call x1, Pallas kernels, shards(): call(slots_kernel, jax.ShapeDtypeStruct((dom_size * block, width), BF16),...  4.55 us
  transfers between devices with their start and end apart: 18, of which 10 were waited for; matrix products, arithmetic and copies ran while one was open for 3% of the time, Pallas kernels for 7%

profile of v6, /device:TPU:0, one launch (start us, length us, event | category | flops | bytes accessed | tf_op | source)
XLA Modules:
  0.0 134.9 jit_solution(5124760428933271175)
XLA Ops:
  0.6 1.0 dynamic-slice_select_fusion
  1.6 3.0 %collective-permute-start = (bf16[96,512]{1,0:T(8,128)(2,1)S(1)}, bf16[96,512]{1,0:T(8,128)(2,1)S(1)}, u32[]{:S(2)}, u32[]{:S(2)}) collective-permute-start(bf16[96,512]{1,0:T(8,128)(2,1)S(1)} %dynamic-slice_select_fusion), channel_id=1, source_target_pairs={{0,1},{1,0},{2,3},{3,2},{4,5},{5,4},{6,7},{7,6},{8,9},{9,8},{10,11... | collective-permute-start | bytes 294920 | tf_op jit(solution)/shard_map/ppermute | solution.py:21
  4.6 2.6 %collective-permute-start.1 = (bf16[96,512]{1,0:T(8,128)(2,1)S(1)}, bf16[96,512]{1,0:T(8,128)(2,1)S(1)}, u32[]{:S(2)}, u32[]{:S(2)}) collective-permute-start(bf16[96,512]{1,0:T(8,128)(2,1)S(1)} %dynamic-slice_select_fusion), channel_id=1, source_target_pairs={{0,4},{1,5},{2,6},{3,7},{4,0},{5,1},{6,2},{7,3},{8,12},{9,13},{10,... | collective-permute-start | bytes 294920 | tf_op jit(solution)/shard_map/ppermute | solution.py:21
  7.2 4.5 %shard_map.95 = bf16[1024,768]{1,0:T(8,128)(2,1)} custom-call(s32[32]{0:T(128)} %src_hbm.1, s32[32]{0:T(128)} %peer_hbm.1, bf16[32,128,128]{2,1,0:T(8,128)(2,1)} %tiles_hbm.1, bf16[1024,768]{1,0:T(8,128)(2,1)} %features_hbm.3), custom_call_target="tpu_custom_call" | custom-call | flops 1610612736 | bytes 4194304 | tf_op jit(solution)/shard_map/pallas_call | solution.py:282
  11.8 6.1 %all-to-all-start = ((bf16[8,128,768]{2,1,0:T(8,128)(2,1)}), bf16[8,128,768]{2,1,0:T(8,128)(2,1)}, u32[]{:S(2)}, u32[]{:S(2)}) async-start(bf16[8,128,768]{2,1,0:T(8,128)(2,1)} %bitcast.58), calls=%async_computation | async-start | bytes 3145728 | tf_op jit(solution)/shard_map/all_to_all | solution.py:301
  18.1 2.1 %collective-permute-start.3 = (bf16[2,2,96,512]{3,2,1,0:T(8,128)(2,1)S(1)}, bf16[2,2,96,512]{3,2,1,0:T(8,128)(2,1)S(1)}, u32[]{:S(2)}, u32[]{:S(2)}) collective-permute-start(bf16[2,2,96,512]{3,2,1,0:T(8,128)(2,1)S(1)} %pad_maximum_fusion.1), channel_id=1, source_target_pairs={{0,2},{1,3},{2,0},{3,1},{4,6},{5,7},{6,4},{7,5},{8,10},{9,11},{10,... | collective-permute-start | bytes 1179656 | tf_op jit(solution)/shard_map/ppermute | solution.py:21
  20.1 30.8 %collective-permute-done.3 = bf16[2,2,96,512]{3,2,1,0:T(8,128)(2,1)S(1)} collective-permute-done((bf16[2,2,96,512]{3,2,1,0:T(8,128)(2,1)S(1)}, bf16[2,2,96,512]{3,2,1,0:T(8,128)(2,1)S(1)}, u32[]{:S(2)}, u32[]{:S(2)}) %collective-permute-start.3) | collective-permute-done | bytes 393248 | tf_op jit(solution)/shard_map/ppermute | solution.py:21
  51.2 1.6 %collective-permute-start.4 = (bf16[768,512]{1,0:T(8,128)(2,1)S(1)}, bf16[768,512]{1,0:T(8,128)(2,1)}, u32[]{:S(2)}, u32[]{:S(2)}) collective-permute-start(bf16[768,512]{1,0:T(8,128)(2,1)S(1)} %bitcast.57), channel_id=1, source_target_pairs={{0,16},{8,24},{16,0},{24,8},{1,17},{9,25},{17,1},{25,9},{2,18},{10... | collective-permute-start | bytes 2359304 | tf_op jit(solution)/shard_map/ppermute | solution.py:21
  52.8 16.1 %collective-permute-done.4 = bf16[768,512]{1,0:T(8,128)(2,1)} collective-permute-done((bf16[768,512]{1,0:T(8,128)(2,1)S(1)}, bf16[768,512]{1,0:T(8,128)(2,1)}, u32[]{:S(2)}, u32[]{:S(2)}) %collective-permute-start.4) | collective-permute-done | bytes 786464 | tf_op jit(solution)/shard_map/ppermute | solution.py:21
  68.9 2.2 %broadcast_select_fusion = (bf16[768,512]{1,0:T(8,128)(2,1)S(1)}, bf16[768,512]{1,0:T(8,128)(2,1)}) fusion(bf16[768,512]{1,0:T(8,128)(2,1)} %collective-permute-done.4, pred[]{:T(512)S(6)} %ne.28, bf16[2,2,2,96,512]{4,3,2,1,0:T(8,128)(2,1)S(1)} %copy.13), kind=kLoop, calls=%fused_computation.5 | loop fusion | flops 786432 | bytes 3145729 | tf_op jit(solution)/shard_map/jit(_where)/select_n | solution.py:235
  71.1 0.5 collective-permute-start.6
  71.6 1.6 %copy.12 = bf16[1024,768]{0,1:T(8,128)(2,1)} copy(bf16[1024,768]{1,0:T(8,128)(2,1)S(1)} %copy-done) | data formatting | bytes 3145728 | tf_op args[0]
  73.2 1.4 %collective-permute-done.5.other_first_hbm = bf16[768,512]{1,0:T(8,128)(2,1)S(1)} collective-permute-done((bf16[768,512]{1,0:T(8,128)(2,1)}, bf16[768,512]{1,0:T(8,128)(2,1)S(1)}, u32[]{:S(2)}, u32[]{:S(2)}) %collective-permute-start.5) | collective-permute-done | bytes 786464 | tf_op jit(solution)/shard_map/ppermute | solution.py:21
  74.7 0.9 copy-done.2
  75.5 12.8 %shard_map.96 = (bf16[1024,768]{1,0:T(8,128)(2,1)}, bf16[1024,1024]{1,0:T(8,128)(2,1)}, bf16[768,1024]{1,0:T(8,128)(2,1)}) custom-call(s32[1]{0:T(128)} %bitcast.core_ref, s32[8]{0:T(128)} %into_ref.1, bf16[8,128,768]{2,1,0:T(8,128)(2,1)} %all-to-all-done.slots_hbm, bf16[1024,768]{1,0:T(8,128)(2,1)} %features_hbm.3, bf16[768,1024]{1,0:T(8,128)(2,1)} %bitcast.52, ...), custom_call_target="tpu_custom_call" | custom-call | flops 4831838208 | bytes 16777216 | tf_op jit(solution)/shard_map/pallas_call | solution.py:315
  88.5 4.7 %shard_map.97 = bf16[768,1024]{1,0:T(8,128)(2,1)} custom-call(s32[1]{0:T(128)} %bitcast.core_ref, bf16[768,1024]{1,0:T(8,128)(2,1)} %bitcast.53, bf16[1024,768]{1,0:T(8,128)(2,1)} %get-tuple-element.13.aggregate_hbm, bf16[1024,1024]{1,0:T(8,128)(2,1)} %get-tuple-element.14.grad_hbm), custom_call_target="tpu_custom_call" | custom-call | flops 1610612736 | bytes 6291456 | tf_op jit(solution)/shard_map/pallas_call | solution.py:344
  93.2 2.1 %add_convert_fusion = bf16[768,1024]{1,0:T(8,128)(2,1)S(1)} fusion(bf16[768,1024]{1,0:T(8,128)(2,1)S(1)} %collective-permute-done.7, bf16[768,1024]{1,0:T(8,128)(2,1)} %shard_map.97), kind=kLoop, calls=%fused_computation | loop fusion | flops 3145728 | bytes 4718592 | tf_op jit(solution)/shard_map/convert_element_type | solution.py:241
  95.5 1.6 %collective-permute-start.10 = (bf16[8,96,256]{2,1,0:T(8,128)(2,1)S(1)}, bf16[8,96,256]{2,1,0:T(8,128)(2,1)S(1)}, u32[]{:S(2)}, u32[]{:S(2)}) collective-permute-start(bf16[8,96,256]{2,1,0:T(8,128)(2,1)S(1)} %constant_dynamic-slice_fusion), channel_id=1, source_target_pairs={{0,16},{8,24},{16,0},{24,8},{1,17},{9,25},{17,1},{25,9},{2,18},{10... | collective-permute-start | bytes 1179656 | tf_op jit(solution)/shard_map/ppermute | solution.py:21
  97.1 1.6 %collective-permute-start.8 = (bf16[4,96,512]{2,1,0:T(8,128)(2,1)S(1)}, bf16[4,96,512]{2,1,0:T(8,128)(2,1)S(1)}, u32[]{:S(2)}, u32[]{:S(2)}) collective-permute-start(bf16[4,96,512]{2,1,0:T(8,128)(2,1)S(1)} %dynamic-slice_bitcast_fusion), channel_id=1, source_target_pairs={{0,1},{1,0},{2,3},{3,2},{4,5},{5,4},{6,7},{7,6},{8,9},{9,8},{10,11... | collective-permute-start | bytes 1179656 | tf_op jit(solution)/shard_map/ppermute | solution.py:21
  98.7 8.4 %collective-permute-done.10 = bf16[8,96,256]{2,1,0:T(8,128)(2,1)S(1)} collective-permute-done((bf16[8,96,256]{2,1,0:T(8,128)(2,1)S(1)}, bf16[8,96,256]{2,1,0:T(8,128)(2,1)S(1)}, u32[]{:S(2)}, u32[]{:S(2)}) %collective-permute-start.10) | collective-permute-done | bytes 393248 | tf_op jit(solution)/shard_map/ppermute | solution.py:21
  107.2 1.6 %collective-permute-start.11 = (bf16[4,96,256]{2,1,0:T(8,128)(2,1)S(1)}, bf16[4,96,256]{2,1,0:T(8,128)(2,1)S(1)}, u32[]{:S(2)}, u32[]{:S(2)}) collective-permute-start(bf16[4,96,256]{2,1,0:T(8,128)(2,1)S(1)} %dynamic-slice_bitcast_fusion.1), channel_id=1, source_target_pairs={{0,1},{1,0},{2,3},{3,2},{4,5},{5,4},{6,7},{7,6},{8,9},{9,8},{10,11... | collective-permute-start | bytes 589832 | tf_op jit(solution)/shard_map/ppermute | solution.py:21
  108.9 1.6 %collective-permute-start.9 = (bf16[4,96,256]{2,1,0:T(8,128)(2,1)S(1)}, bf16[4,96,256]{2,1,0:T(8,128)(2,1)S(1)}, u32[]{:S(2)}, u32[]{:S(2)}) collective-permute-start(bf16[4,96,256]{2,1,0:T(8,128)(2,1)S(1)} %constant_dynamic-slice_fusion.1), channel_id=1, source_target_pairs={{0,16},{8,24},{16,0},{24,8},{1,17},{9,25},{17,1},{25,9},{2,18},{10... | collective-permute-start | bytes 589832 | tf_op jit(solution)/shard_map/ppermute | solution.py:21
  110.5 3.3 %collective-permute-done.11 = bf16[4,96,256]{2,1,0:T(8,128)(2,1)S(1)} collective-permute-done((bf16[4,96,256]{2,1,0:T(8,128)(2,1)S(1)}, bf16[4,96,256]{2,1,0:T(8,128)(2,1)S(1)}, u32[]{:S(2)}, u32[]{:S(2)}) %collective-permute-start.11) | collective-permute-done | bytes 196640 | tf_op jit(solution)/shard_map/ppermute | solution.py:21
  113.9 1.4 %collective-permute-done.9 = bf16[4,96,256]{2,1,0:T(8,128)(2,1)S(1)} collective-permute-done((bf16[4,96,256]{2,1,0:T(8,128)(2,1)S(1)}, bf16[4,96,256]{2,1,0:T(8,128)(2,1)S(1)}, u32[]{:S(2)}, u32[]{:S(2)}) %collective-permute-start.9) | collective-permute-done | bytes 196640 | tf_op jit(solution)/shard_map/ppermute | solution.py:21
  115.3 2.5 %collective-permute-start.12 = (bf16[96,512]{1,0:T(8,128)(2,1)S(1)}, bf16[96,512]{1,0:T(8,128)(2,1)S(1)}, u32[]{:S(2)}, u32[]{:S(2)}) collective-permute-start(bf16[96,512]{1,0:T(8,128)(2,1)S(1)} %get-tuple-element.24), channel_id=1, source_target_pairs={{0,2},{1,3},{2,0},{3,1},{4,6},{5,7},{6,4},{7,5},{8,10},{9,11},{10,... | collective-permute-start | bytes 294920 | tf_op jit(solution)/shard_map/ppermute | solution.py:21
  117.9 1.9 %collective-permute-start.13 = (bf16[96,512]{1,0:T(8,128)(2,1)S(1)}, bf16[96,512]{1,0:T(8,128)(2,1)S(1)}, u32[]{:S(2)}, u32[]{:S(2)}) collective-permute-start(bf16[96,512]{1,0:T(8,128)(2,1)S(1)} %get-tuple-element.25), channel_id=1, source_target_pairs={{0,4},{1,5},{2,6},{3,7},{4,0},{5,1},{6,2},{7,3},{8,12},{9,13},{10,... | collective-permute-start | bytes 294920 | tf_op jit(solution)/shard_map/ppermute | solution.py:21
  119.8 1.4 %collective-permute-start.14 = (bf16[96,512]{1,0:T(8,128)(2,1)S(1)}, bf16[96,512]{1,0:T(8,128)(2,1)S(1)}, u32[]{:S(2)}, u32[]{:S(2)}) collective-permute-start(bf16[96,512]{1,0:T(8,128)(2,1)S(1)} %get-tuple-element.26), channel_id=1, source_target_pairs={{0,6},{1,7},{2,4},{3,5},{4,2},{5,3},{6,0},{7,1},{8,14},{9,15},{10,... | collective-permute-start | bytes 294920 | tf_op jit(solution)/shard_map/ppermute | solution.py:21
  121.5 6.1 %collective-permute-done.13 = bf16[96,512]{1,0:T(8,128)(2,1)S(1)} collective-permute-done((bf16[96,512]{1,0:T(8,128)(2,1)S(1)}, bf16[96,512]{1,0:T(8,128)(2,1)S(1)}, u32[]{:S(2)}, u32[]{:S(2)}) %collective-permute-start.13) | collective-permute-done | bytes 98336 | tf_op jit(solution)/shard_map/ppermute | solution.py:21
  127.7 1.6 %collective-permute-start.15 = (bf16[2,96,256]{2,1,0:T(8,128)(2,1)S(1)}, bf16[2,96,256]{2,1,0:T(8,128)(2,1)S(1)}, u32[]{:S(2)}, u32[]{:S(2)}) collective-permute-start(bf16[2,96,256]{2,1,0:T(8,128)(2,1)S(1)} %pad_maximum_fusion.6), channel_id=1, source_target_pairs={{0,16},{8,24},{16,0},{24,8},{1,17},{9,25},{17,1},{25,9},{2,18},{10... | collective-permute-start | bytes 294920 | tf_op jit(solution)/shard_map/ppermute | solution.py:21
  129.3 3.1 %collective-permute-done.15 = bf16[2,96,256]{2,1,0:T(8,128)(2,1)S(1)} collective-permute-done((bf16[2,96,256]{2,1,0:T(8,128)(2,1)S(1)}, bf16[2,96,256]{2,1,0:T(8,128)(2,1)S(1)}, u32[]{:S(2)}, u32[]{:S(2)}) %collective-permute-start.15) | collective-permute-done | bytes 98336 | tf_op jit(solution)/shard_map/ppermute | solution.py:21
  132.5 1.4 %collective-permute-done.16 = bf16[96,1024]{1,0:T(8,128)(2,1)S(1)} collective-permute-done((bf16[96,1024]{1,0:T(8,128)(2,1)S(1)}, bf16[96,1024]{1,0:T(8,128)(2,1)S(1)}, u32[]{:S(2)}, u32[]{:S(2)}) %collective-permute-start.16) | collective-permute-done | bytes 196640 | tf_op jit(solution)/shard_map/ppermute | solution.py:21
  134.0 1.0 select_convert_fusion
  (40 shorter events, 1.7 us)
Async XLA Ops:
  1.6 16.3 %collective-permute-start = (bf16[96,512]{1,0:T(8,128)(2,1)S(1)}, bf16[96,512]{1,0:T(8,128)(2,1)S(1)}, u32[]{:S(2)}, u32[]{:S(2)}) collective-permute-start(bf16[96,512]{1,0:T(8,128)(2,1)S(1)} %dynamic-slice_select_fusion), channel_id=1, source_target_pairs={{0,1},{1,0},{2,3},{3,2},{4,5},{5,4},{6,7},{7,6},{8,9},{9,8},{10,11... | collective-permute-start | bytes 294920 | tf_op jit(solution)/shard_map/ppermute | solution.py:21
  4.6 13.3 %collective-permute-start.1 = (bf16[96,512]{1,0:T(8,128)(2,1)S(1)}, bf16[96,512]{1,0:T(8,128)(2,1)S(1)}, u32[]{:S(2)}, u32[]{:S(2)}) collective-permute-start(bf16[96,512]{1,0:T(8,128)(2,1)S(1)} %dynamic-slice_select_fusion), channel_id=1, source_target_pairs={{0,4},{1,5},{2,6},{3,7},{4,0},{5,1},{6,2},{7,3},{8,12},{9,13},{10,... | collective-permute-start | bytes 294920 | tf_op jit(solution)/shard_map/ppermute | solution.py:21
  7.2 10.7 %collective-permute-start.2 = (bf16[96,512]{1,0:T(8,128)(2,1)S(1)}, bf16[96,512]{1,0:T(8,128)(2,1)S(1)}, u32[]{:S(2)}, u32[]{:S(2)}) collective-permute-start(bf16[96,512]{1,0:T(8,128)(2,1)S(1)} %dynamic-slice_select_fusion), channel_id=1, source_target_pairs={{0,5},{1,4},{2,7},{3,6},{4,1},{5,0},{6,3},{7,2},{8,13},{9,12},{10,... | collective-permute-start | bytes 294920 | tf_op jit(solution)/shard_map/ppermute | solution.py:21
  11.8 62.9 %all-to-all-start = ((bf16[8,128,768]{2,1,0:T(8,128)(2,1)}), bf16[8,128,768]{2,1,0:T(8,128)(2,1)}, u32[]{:S(2)}, u32[]{:S(2)}) async-start(bf16[8,128,768]{2,1,0:T(8,128)(2,1)} %bitcast.58), calls=%async_computation | async-start | bytes 3145728 | tf_op jit(solution)/shard_map/all_to_all | solution.py:301
  18.1 32.9 %collective-permute-start.3 = (bf16[2,2,96,512]{3,2,1,0:T(8,128)(2,1)S(1)}, bf16[2,2,96,512]{3,2,1,0:T(8,128)(2,1)S(1)}, u32[]{:S(2)}, u32[]{:S(2)}) collective-permute-start(bf16[2,2,96,512]{3,2,1,0:T(8,128)(2,1)S(1)} %pad_maximum_fusion.1), channel_id=1, source_target_pairs={{0,2},{1,3},{2,0},{3,1},{4,6},{5,7},{6,4},{7,5},{8,10},{9,11},{10,... | collective-permute-start | bytes 1179656 | tf_op jit(solution)/shard_map/ppermute | solution.py:21
  51.2 17.7 %collective-permute-start.4 = (bf16[768,512]{1,0:T(8,128)(2,1)S(1)}, bf16[768,512]{1,0:T(8,128)(2,1)}, u32[]{:S(2)}, u32[]{:S(2)}) collective-permute-start(bf16[768,512]{1,0:T(8,128)(2,1)S(1)} %bitcast.57), channel_id=1, source_target_pairs={{0,16},{8,24},{16,0},{24,8},{1,17},{9,25},{17,1},{25,9},{2,18},{10... | collective-permute-start | bytes 2359304 | tf_op jit(solution)/shard_map/ppermute | solution.py:21
  52.8 18.8 %copy-start = (bf16[1024,768]{1,0:T(8,128)(2,1)S(1)}, bf16[1024,768]{1,0:T(8,128)(2,1)}, u32[]{:S(2)}) copy-start(bf16[1024,768]{1,0:T(8,128)(2,1)} %features_hbm.3) | copy-start | bytes 4718596
  71.1 2.2 %copy-start.1 = (bf16[768,512]{1,0:T(8,128)(2,1)}, bf16[768,512]{1,0:T(8,128)(2,1)S(1)}, u32[]{:S(2)}) copy-start(bf16[768,512]{1,0:T(8,128)(2,1)S(1)} %get-tuple-element.18.mine_second_hbm) | copy-start | bytes 2359300
  71.1 3.6 %collective-permute-start.5 = (bf16[768,512]{1,0:T(8,128)(2,1)}, bf16[768,512]{1,0:T(8,128)(2,1)S(1)}, u32[]{:S(2)}, u32[]{:S(2)}) collective-permute-start(bf16[768,512]{1,0:T(8,128)(2,1)} %get-tuple-element.19.mine_first_hbm), channel_id=1, source_target_pairs={{0,8},{8,0},{16,24},{24,16},{1,9},{9,1},{17,25},{25,17},{2,10},{10... | collective-permute-start | bytes 2359304 | tf_op jit(solution)/shard_map/ppermute | solution.py:21
  71.1 3.6 %collective-permute-start.6 = (bf16[768,512]{1,0:T(8,128)(2,1)S(1)}, bf16[768,512]{1,0:T(8,128)(2,1)}, u32[]{:S(2)}, u32[]{:S(2)}) collective-permute-start(bf16[768,512]{1,0:T(8,128)(2,1)S(1)} %get-tuple-element.18.mine_second_hbm), channel_id=1, source_target_pairs={{0,8},{8,0},{16,24},{24,16},{1,9},{9,1},{17,25},{25,17},{2,10},{10... | collective-permute-start | bytes 2359304 | tf_op jit(solution)/shard_map/ppermute | solution.py:21
  74.7 0.9 copy-start.2
  88.4 4.8 %collective-permute-start.7 = (bf16[768,1024]{1,0:T(8,128)(2,1)}, bf16[768,1024]{1,0:T(8,128)(2,1)S(1)}, u32[]{:S(2)}, u32[]{:S(2)}) collective-permute-start(bf16[768,1024]{1,0:T(8,128)(2,1)} %get-tuple-element.15), channel_id=1, source_target_pairs={{0,8},{8,0},{16,24},{24,16},{1,9},{9,1},{17,25},{25,17},{2,10},{10... | collective-permute-start | bytes 4718600 | tf_op jit(solution)/shard_map/ppermute | solution.py:21
  95.5 11.6 %collective-permute-start.10 = (bf16[8,96,256]{2,1,0:T(8,128)(2,1)S(1)}, bf16[8,96,256]{2,1,0:T(8,128)(2,1)S(1)}, u32[]{:S(2)}, u32[]{:S(2)}) collective-permute-start(bf16[8,96,256]{2,1,0:T(8,128)(2,1)S(1)} %constant_dynamic-slice_fusion), channel_id=1, source_target_pairs={{0,16},{8,24},{16,0},{24,8},{1,17},{9,25},{17,1},{25,9},{2,18},{10... | collective-permute-start | bytes 1179656 | tf_op jit(solution)/shard_map/ppermute | solution.py:21
  97.1 11.7 %collective-permute-start.8 = (bf16[4,96,512]{2,1,0:T(8,128)(2,1)S(1)}, bf16[4,96,512]{2,1,0:T(8,128)(2,1)S(1)}, u32[]{:S(2)}, u32[]{:S(2)}) collective-permute-start(bf16[4,96,512]{2,1,0:T(8,128)(2,1)S(1)} %dynamic-slice_bitcast_fusion), channel_id=1, source_target_pairs={{0,1},{1,0},{2,3},{3,2},{4,5},{5,4},{6,7},{7,6},{8,9},{9,8},{10,11... | collective-permute-start | bytes 1179656 | tf_op jit(solution)/shard_map/ppermute | solution.py:21
  107.2 6.6 %collective-permute-start.11 = (bf16[4,96,256]{2,1,0:T(8,128)(2,1)S(1)}, bf16[4,96,256]{2,1,0:T(8,128)(2,1)S(1)}, u32[]{:S(2)}, u32[]{:S(2)}) collective-permute-start(bf16[4,96,256]{2,1,0:T(8,128)(2,1)S(1)} %dynamic-slice_bitcast_fusion.1), channel_id=1, source_target_pairs={{0,1},{1,0},{2,3},{3,2},{4,5},{5,4},{6,7},{7,6},{8,9},{9,8},{10,11... | collective-permute-start | bytes 589832 | tf_op jit(solution)/shard_map/ppermute | solution.py:21
  108.9 6.3 %collective-permute-start.9 = (bf16[4,96,256]{2,1,0:T(8,128)(2,1)S(1)}, bf16[4,96,256]{2,1,0:T(8,128)(2,1)S(1)}, u32[]{:S(2)}, u32[]{:S(2)}) collective-permute-start(bf16[4,96,256]{2,1,0:T(8,128)(2,1)S(1)} %constant_dynamic-slice_fusion.1), channel_id=1, source_target_pairs={{0,16},{8,24},{16,0},{24,8},{1,17},{9,25},{17,1},{25,9},{2,18},{10... | collective-permute-start | bytes 589832 | tf_op jit(solution)/shard_map/ppermute | solution.py:21
  115.3 6.2 %collective-permute-start.12 = (bf16[96,512]{1,0:T(8,128)(2,1)S(1)}, bf16[96,512]{1,0:T(8,128)(2,1)S(1)}, u32[]{:S(2)}, u32[]{:S(2)}) collective-permute-start(bf16[96,512]{1,0:T(8,128)(2,1)S(1)} %get-tuple-element.24), channel_id=1, source_target_pairs={{0,2},{1,3},{2,0},{3,1},{4,6},{5,7},{6,4},{7,5},{8,10},{9,11},{10,... | collective-permute-start | bytes 294920 | tf_op jit(solution)/shard_map/ppermute | solution.py:21
  117.9 9.7 %collective-permute-start.13 = (bf16[96,512]{1,0:T(8,128)(2,1)S(1)}, bf16[96,512]{1,0:T(8,128)(2,1)S(1)}, u32[]{:S(2)}, u32[]{:S(2)}) collective-permute-start(bf16[96,512]{1,0:T(8,128)(2,1)S(1)} %get-tuple-element.25), channel_id=1, source_target_pairs={{0,4},{1,5},{2,6},{3,7},{4,0},{5,1},{6,2},{7,3},{8,12},{9,13},{10,... | collective-permute-start | bytes 294920 | tf_op jit(solution)/shard_map/ppermute | solution.py:21
  119.8 7.8 %collective-permute-start.14 = (bf16[96,512]{1,0:T(8,128)(2,1)S(1)}, bf16[96,512]{1,0:T(8,128)(2,1)S(1)}, u32[]{:S(2)}, u32[]{:S(2)}) collective-permute-start(bf16[96,512]{1,0:T(8,128)(2,1)S(1)} %get-tuple-element.26), channel_id=1, source_target_pairs={{0,6},{1,7},{2,4},{3,5},{4,2},{5,3},{6,0},{7,1},{8,14},{9,15},{10,... | collective-permute-start | bytes 294920 | tf_op jit(solution)/shard_map/ppermute | solution.py:21
  127.7 4.7 %collective-permute-start.15 = (bf16[2,96,256]{2,1,0:T(8,128)(2,1)S(1)}, bf16[2,96,256]{2,1,0:T(8,128)(2,1)S(1)}, u32[]{:S(2)}, u32[]{:S(2)}) collective-permute-start(bf16[2,96,256]{2,1,0:T(8,128)(2,1)S(1)} %pad_maximum_fusion.6), channel_id=1, source_target_pairs={{0,16},{8,24},{16,0},{24,8},{1,17},{9,25},{17,1},{25,9},{2,18},{10... | collective-permute-start | bytes 294920 | tf_op jit(solution)/shard_map/ppermute | solution.py:21
  132.5 1.5 %collective-permute-start.16 = (bf16[96,1024]{1,0:T(8,128)(2,1)S(1)}, bf16[96,1024]{1,0:T(8,128)(2,1)S(1)}, u32[]{:S(2)}, u32[]{:S(2)}) collective-permute-start(bf16[96,1024]{1,0:T(8,128)(2,1)S(1)} %pad_maximum_fusion.4), channel_id=1, source_target_pairs={{0,8},{8,0},{16,24},{24,16},{1,9},{9,1},{17,25},{25,17},{2,10},{10... | collective-permute-start | bytes 589832 | tf_op jit(solution)/shard_map/ppermute | solution.py:21

commit v7 on v6

--- a/solution.py
+++ b/solution.py
@@ -19,6 +19,14 @@
 def swap(value, axis, step):
     size = lax.axis_size(axis)
     return lax.ppermute(value, axis, [(index, index ^ step) for index in range(size)])
+
+
+def cross(value, step):
+    reps, doms = lax.axis_size("rep"), lax.axis_size("dom")
+    pairs = [
+        (rep * doms + dom, rep * doms + (dom ^ step ^ (rep & 1))) for rep in range(reps) for dom in range(doms)
+    ]
+    return lax.ppermute(value, ("rep", "dom"), [(source, target) for source, target in pairs if source != target])
 
 
 def slots_kernel(
@@ -64,72 +72,46 @@
     features_hbm,
     turned_hbm,
     cotangent_hbm,
-    mine_first_hbm,
-    mine_second_hbm,
-    other_first_hbm,
-    other_second_hbm,
+    weights_hbm,
     aggregate_hbm,
     grad_hbm,
     sent_hbm,
     slots,
     features,
-    turned,
+    left,
     cotangent,
-    w_self,
-    w_neigh,
+    weights,
     summed,
     aggregate,
     grad,
     sent,
     slot_sems,
-    weight_sems,
     row_sems,
+    column_sems,
     out_sems,
 ):
     senders, block, _ = slots.shape
-    rows, width = features.shape
-    split = mine_first_hbm.shape[1]
-    chunk = 256
+    hidden = grad.shape[1]
     core = core_ref[0]
     arrivals = [
         pltpu.make_async_copy(slots_hbm.at[sender], slots.at[sender], slot_sems.at[sender]) for sender in range(senders)
     ]
     for arrival in arrivals:
         arrival.start()
-
-    def weight_copies(first_hbm, second_hbm, target, index):
-        return [
-            pltpu.make_async_copy(first_hbm, target.at[:, :split], weight_sems.at[index]),
-            pltpu.make_async_copy(second_hbm, target.at[:, split:], weight_sems.at[index + 1]),
-        ]
-
-    mine = (mine_first_hbm, mine_second_hbm)
-    other = (other_first_hbm, other_second_hbm)
-
-    @pl.when(core == 0)
-    def _():
-        for copy in weight_copies(*mine, w_self, 0) + weight_copies(*other, w_neigh, 2):
-            copy.start()
-
-    @pl.when(core != 0)
-    def _():
-        for copy in weight_copies(*other, w_self, 0) + weight_copies(*mine, w_neigh, 2):
-            copy.start()
-
-    weights = weight_copies(*mine, w_self, 0) + weight_copies(*other, w_neigh, 2)
-    spans = [slice(first, first + chunk) for first in range(0, rows, chunk)]
+    inputs = pltpu.make_async_copy(features_hbm, features, row_sems.at[0])
+    inputs.start()
+    spans = [slice(first, first + 256) for first in range(0, hidden, 256)]
     streams = [
         [
-            pltpu.make_async_copy(features_hbm.at[at, :], features.at[at, :], row_sems.at[0, index]),
-            pltpu.make_async_copy(cotangent_hbm.at[at, :], cotangent.at[at, :], row_sems.at[1, index]),
+            pltpu.make_async_copy(weights_hbm.at[0, :, at], weights.at[0, :, at], column_sems.at[0, index]),
+            pltpu.make_async_copy(weights_hbm.at[1, :, at], weights.at[1, :, at], column_sems.at[1, index]),
+            pltpu.make_async_copy(cotangent_hbm.at[:, at], cotangent.at[:, at], column_sems.at[2, index]),
         ]
         for index, at in enumerate(spans)
     ]
     for stream in streams:
         for copy in stream:
             copy.start()
-    turning = pltpu.make_async_copy(turned_hbm, turned, out_sems.at[0])
-    turning.start()
 
     summed[...] = jnp.zeros_like(summed)
     for sender in range(senders):
@@ -137,78 +119,69 @@
         at = pl.ds(pl.multiple_of(into_ref[sender] * block, block), block)
         summed[at, :] = summed[at, :] + slots[sender].astype(F32)
     aggregate[...] = summed[...].astype(BF16)
-    results = [pltpu.make_async_copy(aggregate, aggregate_hbm, out_sems.at[1])]
+    results = [pltpu.make_async_copy(aggregate, aggregate_hbm, row_sems.at[1])]
     results[0].start()
-    for copy in weights:
-        copy.wait()
-    span = 512
+
+    @pl.when(core == 0)
+    def _():
+        left[...] = aggregate[...].T
+
+    @pl.when(core != 0)
+    def _():
+        turning = pltpu.make_async_copy(turned_hbm, left, row_sems.at[2])
+        turning.start()
+        turning.wait()
+
+    inputs.wait()
     for index, at in enumerate(spans):
         for copy in streams[index]:
             copy.wait()
-        for first in range(0, grad.shape[1], span):
-            columns = slice(first, first + span)
-            value = jnp.dot(features[at, :], w_self[:, columns], preferred_element_type=F32) + jnp.dot(
-                aggregate[at, :], w_neigh[:, columns], preferred_element_type=F32
-            )
-            square = value * value
-            bend = jnp.tanh(value * (SCALE + SCALE * CUBIC * square))
-            inner = value * (SCALE + 3.0 * SCALE * CUBIC * square)
-            slope = (1.0 + bend) * (0.5 + 0.5 * inner * (1.0 - bend))
-            grad[at, columns] = (cotangent[at, columns].astype(F32) * slope).astype(BF16)
-        results.append(pltpu.make_async_copy(grad.at[at, :], grad_hbm.at[at, :], out_sems.at[2 + index]))
+        value = jnp.dot(features[...], weights[0, :, at], preferred_element_type=F32) + jnp.dot(
+            aggregate[...], weights[1, :, at], preferred_element_type=F32
+        )
+        square = value * value
+        bend = jnp.tanh(value * (SCALE + SCALE * CUBIC * square))
+        inner = value * (SCALE + 3.0 * SCALE * CUBIC * square)
+        slope = (1.0 + bend) * (0.5 + 0.5 * inner * (1.0 - bend))
+        grad[:, at] = (cotangent[:, at].astype(F32) * slope).astype(BF16)
+        results.append(pltpu.make_async_copy(grad.at[:, at], grad_hbm.at[:, at], out_sems.at[0, index]))
         results[-1].start()
-    turning.wait()
-    term(1 - core, turned, aggregate, grad, sent, sent_hbm, out_sems, 2 + len(spans))
+        sent[:, at] = jnp.dot(left[...], grad[:, at], preferred_element_type=F32).astype(BF16)
+        results.append(pltpu.make_async_copy(sent.at[:, at], sent_hbm.at[:, at], out_sems.at[1, index]))
+        results[-1].start()
     for result in results:
         result.wait()
 
 
-def term(use, turned, aggregate, grad, out, out_hbm, sems, first_sem):
-    chunk = 256
-    spans = [slice(first, first + chunk) for first in range(0, out.shape[0], chunk)]
-    copies = [
-        pltpu.make_async_copy(out.at[at, :], out_hbm.at[at, :], sems.at[first_sem + index])
-        for index, at in enumerate(spans)
-    ]
-
-    @pl.when(use == 0)
-    def _():
-        for at, copy in zip(spans, copies):
-            out[at, :] = jnp.dot(turned[at, :], grad[...], preferred_element_type=F32).astype(BF16)
+def kept_kernel(core_ref, turned_hbm, aggregate_hbm, grad_hbm, out_hbm, turned, aggregate, grad, out, in_sems, out_sems):
+    core = core_ref[0]
+    spans = [slice(first, first + 512) for first in range(0, out.shape[1], 512)]
+    grads = [
+        pltpu.make_async_copy(grad_hbm.at[:, at], grad.at[:, at], in_sems.at[1 + index]) for index, at in enumerate(spans)
+    ]
+    results = [
+        pltpu.make_async_copy(out.at[:, at], out_hbm.at[:, at], out_sems.at[index]) for index, at in enumerate(spans)
+    ]
+
+    def product(left_hbm, left, contract):
+        def body():
+            copy = pltpu.make_async_copy(left_hbm, left, in_sems.at[0])
             copy.start()
-
-    @pl.when(use != 0)
-    def _():
-        contract = (((0,), (0,)), ((), ()))
-        for at, copy in zip(spans, copies):
-            out[at, :] = lax.dot_general(
-                aggregate[:, at], grad[...], contract, preferred_element_type=F32
-            ).astype(BF16)
-            copy.start()
-
-    for copy in copies:
-        copy.wait()
-
-
-def kept_kernel(core_ref, turned_hbm, aggregate_hbm, grad_hbm, out_hbm, turned, aggregate, grad, out, in_sems, out_sems):
-    grads = pltpu.make_async_copy(grad_hbm, grad, in_sems.at[0])
-    grads.start()
-    core = core_ref[0]
-
-    @pl.when(core == 0)
-    def _():
-        copy = pltpu.make_async_copy(turned_hbm, turned, in_sems.at[1])
-        copy.start()
-        copy.wait()
-
-    @pl.when(core != 0)
-    def _():
-        copy = pltpu.make_async_copy(aggregate_hbm, aggregate, in_sems.at[1])
-        copy.start()
-        copy.wait()
-
-    grads.wait()
-    term(core, turned, aggregate, grad, out, out_hbm, out_sems, 0)
+            for stream in grads:
+                stream.start()
+            copy.wait()
+            for at, stream, result in zip(spans, grads, results):
+                stream.wait()
+                value = lax.dot_general(left[...], grad[:, at], (contract, ((), ())), preferred_element_type=F32)
+                out[:, at] = value.astype(BF16)
+                result.start()
+
+        return body
+
+    pl.when(core == 0)(product(turned_hbm, turned, ((1,), (0,))))
+    pl.when(core != 0)(product(aggregate_hbm, aggregate, ((0,), (0,))))
+    for result in results:
+        result.wait()
 
 
 def call(kernel, outs, places, out_places, scratch=(), flops=0, moved=0, vmem=56):
@@ -275,10 +248,8 @@
     core_arg = core.astype(jnp.int32).reshape(1)
 
     share = hidden // parts
-    own = jnp.where(core == 0, w_self, w_neigh)
-    held = lax.dynamic_slice_in_dim(own, high * share, share, 1)
-    top = dom_size // 2
-    pieces = [held] + [swap(held, "dom", step) for step in (1, top, top + 1)]
+    held = jnp.stack([lax.dynamic_slice_in_dim(weight, high * share, share, 1) for weight in (w_self, w_neigh)])
+    pieces = [cross(held, 2 * step) for step in range(dom_size // 2)]
     slots = call(
         slots_kernel,
         jax.ShapeDtypeStruct((dom_size * block, width), BF16),
@@ -299,17 +270,19 @@
     )(tile_src, tile_peer, tile_vals, features)
     *pieces, _ = lax.optimization_barrier((*pieces, slots))
     received = lax.all_to_all(slots.reshape(dom_size, block, width), "dom", split_axis=0, concat_axis=0, tiled=True)
-    pairs = [joined(pieces[at], pieces[at + 1], low != 0, 0) for at in (0, 2)]
-    held = joined(*pairs, (me & top) != 0, 0)
-    step = top // 2
-    while step > 1:
-        held = joined(held, swap(held, "dom", step), (me & step) != 0, 1)
-        held = held.reshape(-1, *held.shape[2:])
-        step //= 2
-    held = held.reshape(-1, share)
-    mine = gather_high(held, high)
-    weights = [mine[:, : hidden // 2], mine[:, hidden // 2 :]]
-    weights += [swap(weight, "rep", 1) for weight in weights]
+    pieces[0] = jnp.where(core == 0, held, pieces[0])
+    pieces = [piece[:, None] for piece in pieces]
+    bit = 1
+    while len(pieces) > 1:
+        upper = (place & bit) != 0
+        pieces = [
+            jnp.concatenate([jnp.where(upper, b, a), jnp.where(upper, a, b)], axis=1)
+            for a, b in zip(pieces[::2], pieces[1::2])
+        ]
+        bit *= 2
+    mine = gather_high(pieces[0], high)
+    other = swap(mine, "rep", 1)
+    weights = joined(mine, other, (low ^ core) != 0, 2).reshape(2, width, hidden)
     turned = features.T
 
     aggregate, grad, sent = call(
@@ -319,27 +292,26 @@
             jax.ShapeDtypeStruct((rows, hidden), BF16),
             jax.ShapeDtypeStruct((width, hidden), BF16),
         ],
-        [SMEM, SMEM] + [HBM] * 8,
+        [SMEM, SMEM] + [HBM] * 5,
         [HBM] * 3,
         [
             pltpu.VMEM((dom_size, block, width), BF16),
             pltpu.VMEM((rows, width), BF16),
             pltpu.VMEM((width, rows), BF16),
             pltpu.VMEM((rows, hidden), BF16),
-            pltpu.VMEM((width, hidden), BF16),
-            pltpu.VMEM((width, hidden), BF16),
+            pltpu.VMEM((2, width, hidden), BF16),
             pltpu.VMEM((rows, width), F32),
             pltpu.VMEM((rows, width), BF16),
             pltpu.VMEM((rows, hidden), BF16),
             pltpu.VMEM((width, hidden), BF16),
             DMA((dom_size,)),
-            DMA((4,)),
-            DMA((2, rows // 256)),
-            DMA((2 + rows // 256 + width // 256,)),
+            DMA((3,)),
+            DMA((3, hidden // 256)),
+            DMA((2, hidden // 256)),
         ],
         flops=6 * rows * width * hidden,
         moved=16 * rows * hidden,
-    )(core_arg, in_block, received, features, turned, cotangent, *weights)
+    )(core_arg, in_block, received, features, turned, cotangent, weights)
     arrived = swap(sent, "rep", 1)
     kept = call(
         kept_kernel,
@@ -351,8 +323,8 @@
             pltpu.VMEM((rows, width), BF16),
             pltpu.VMEM((rows, hidden), BF16),
             pltpu.VMEM((width, hidden), BF16),
-            DMA((2,)),
-            DMA((width // 256,)),
+            DMA((1 + hidden // 512,)),
+            DMA((hidden // 512,)),
         ],
         flops=2 * rows * width * hidden,
         moved=6 * rows * hidden,

time: 135 us -> 130 us (0.963)
  waiting for transfers between devices: 72.4 us -> 61.9 us
  Pallas kernels: 22.1 us -> 25.7 us
  other arithmetic: 6.95 us -> 9.42 us
    ppermute x17 -> x12, waiting for transfers between devices: 72.4 us -> 34.4 us  [swap(): lax.ppermute(value, axis, [(index, index ^ step) for index in range(size)])]
    all_to_all x1, waiting for transfers between devices: 0.01 us -> 19.2 us  [shards(): lax.all_to_all(slots.reshape(dom_size, block, width), 'dom', split_axis=0...]
    ppermute x17 -> x12, starting transfers between devices: 23.6 us -> 14.1 us  [swap(): lax.ppermute(value, axis, [(index, index ^ step) for index in range(size)])]
    ppermute x0 -> x4, waiting for transfers between devices: none -> 8.31 us  [cross(): lax.ppermute(value, ('rep', 'dom'), [(source, target) for source, target...]
    ppermute x0 -> x4, starting transfers between devices: none -> 6.35 us  [cross(): lax.ppermute(value, ('rep', 'dom'), [(source, target) for source, target...]
    another operation x4 -> x2, other arithmetic: 0.2 us -> 4.12 us  [joined(): jnp.stack([jnp.where(upper, other, held), jnp.where(upper, held, other)],...]
    pallas_call x1, Pallas kernels: 12.8 us -> 16.5 us  [shards(): call(layer_kernel, [jax.ShapeDtypeStruct((rows, width), BF16), jax.ShapeD...]
    select_n x3, other arithmetic: 3.21 us -> 0.15 us  [shards(): jnp.where(upper, b, a)]
  transfers between devices with their start and end apart: 18 -> 17, of which waited for: 10 -> 12; matrix products, arithmetic and copies ran while one was open for 3% -> 6% of each run, Pallas kernels for 7% -> 7%
where the time goes in v7:
time: 130 us
  waiting for transfers between devices  61.9 us (48%)
  starting transfers between devices  29.2 us (22%)
  Pallas kernels  25.7 us (20%)
  other arithmetic  9.42 us (7%)
  local copies, waits for them, and re-layouts  2.95 us (2%)
    ppermute x12, waiting for transfers between devices, swap(): lax.ppermute(value, axis, [(index, index ^ step) for index in range(size)])  34.4 us
    all_to_all x1, waiting for transfers between devices, shards(): lax.all_to_all(slots.reshape(dom_size, block, width), 'dom', split_axis=0...  19.2 us
    pallas_call x1, Pallas kernels, shards(): call(layer_kernel, [jax.ShapeDtypeStruct((rows, width), BF16), jax.ShapeD...  16.5 us
    ppermute x12, starting transfers between devices, swap(): lax.ppermute(value, axis, [(index, index ^ step) for index in range(size)])  14.1 us
    all_to_all x1, starting transfers between devices, shards(): lax.all_to_all(slots.reshape(dom_size, block, width), 'dom', split_axis=0...  8.75 us
    ppermute x4, waiting for transfers between devices, cross(): lax.ppermute(value, ('rep', 'dom'), [(source, target) for source, target...  8.31 us
    ppermute x4, starting transfers between devices, cross(): lax.ppermute(value, ('rep', 'dom'), [(source, target) for source, target...  6.35 us
    pallas_call x1, Pallas kernels, shards(): call(kept_kernel, jax.ShapeDtypeStruct((width, hidden), BF16), [SMEM] + [...  4.65 us
  transfers between devices with their start and end apart: 17, of which 12 were waited for; matrix products, arithmetic and copies ran while one was open for 6% of the time, Pallas kernels for 7%

profile of v7, /device:TPU:0, one launch (start us, length us, event | category | flops | bytes accessed | tf_op | source)
XLA Modules:
  0.0 130.0 jit_solution(10945719812190127796)
XLA Ops:
  0.6 1.0 dynamic-slice_bitcast_fusion.2
  1.6 0.7 collective-permute-start
  2.3 3.1 %collective-permute-start.1 = (bf16[2,96,512]{2,1,0:T(8,128)(2,1)S(1)}, bf16[2,96,512]{2,1,0:T(8,128)(2,1)S(1)}, u32[]{:S(2)}, u32[]{:S(2)}) collective-permute-start(bf16[2,96,512]{2,1,0:T(8,128)(2,1)S(1)} %pad_maximum_fusion.5), channel_id=1, source_target_pairs={{0,2},{1,3},{2,0},{3,1},{4,6},{5,7},{6,4},{7,5},{8,11},{9,10},{10,... | collective-permute-start | bytes 589832 | tf_op jit(solution)/shard_map/ppermute | solution.py:29
  5.4 2.6 %collective-permute-start.2 = (bf16[2,96,512]{2,1,0:T(8,128)(2,1)S(1)}, bf16[2,96,512]{2,1,0:T(8,128)(2,1)S(1)}, u32[]{:S(2)}, u32[]{:S(2)}) collective-permute-start(bf16[2,96,512]{2,1,0:T(8,128)(2,1)S(1)} %pad_maximum_fusion.5), channel_id=1, source_target_pairs={{0,4},{1,5},{2,6},{3,7},{4,0},{5,1},{6,2},{7,3},{8,13},{9,12},{10,... | collective-permute-start | bytes 589832 | tf_op jit(solution)/shard_map/ppermute | solution.py:29
  8.0 4.5 %shard_map.95 = bf16[1024,768]{1,0:T(8,128)(2,1)} custom-call(s32[32]{0:T(128)} %src_hbm.1, s32[32]{0:T(128)} %peer_hbm.1, bf16[32,128,128]{2,1,0:T(8,128)(2,1)} %tiles_hbm.1, bf16[1024,768]{1,0:T(8,128)(2,1)} %features_hbm.3), custom_call_target="tpu_custom_call" | custom-call | flops 1610612736 | bytes 4194304 | tf_op jit(solution)/shard_map/pallas_call | solution.py:253
  12.5 1.1 collective-permute-done.2
  13.6 7.2 %collective-permute-done.3 = bf16[2,96,512]{2,1,0:T(8,128)(2,1)S(1)} collective-permute-done((bf16[2,96,512]{2,1,0:T(8,128)(2,1)S(1)}, bf16[2,96,512]{2,1,0:T(8,128)(2,1)S(1)}, u32[]{:S(2)}, u32[]{:S(2)}) %collective-permute-start.3) | collective-permute-done | bytes 196640 | tf_op jit(solution)/shard_map/ppermute | solution.py:29
  21.1 1.6 %collective-permute-start.4 = (bf16[2,4,96,512]{3,2,1,0:T(8,128)(2,1)S(1)}, bf16[2,4,96,512]{3,2,1,0:T(8,128)(2,1)S(1)}, u32[]{:S(2)}, u32[]{:S(2)}) collective-permute-start(bf16[2,4,96,512]{3,2,1,0:T(8,128)(2,1)S(1)} %pad_maximum_fusion.2), channel_id=1, source_target_pairs={{0,16},{8,24},{16,0},{24,8},{1,17},{9,25},{17,1},{25,9},{2,18},{10... | collective-permute-start | bytes 2359304 | tf_op jit(solution)/shard_map/ppermute | solution.py:21
  22.7 8.7 %all-to-all-start = ((bf16[8,128,768]{2,1,0:T(8,128)(2,1)}), bf16[8,128,768]{2,1,0:T(8,128)(2,1)}, u32[]{:S(2)}, u32[]{:S(2)}) async-start(bf16[8,128,768]{2,1,0:T(8,128)(2,1)} %bitcast.2), calls=%async_computation | async-start | bytes 3145728 | tf_op jit(solution)/shard_map/all_to_all | solution.py:272
  31.4 7.6 %collective-permute-done.4 = bf16[2,4,96,512]{3,2,1,0:T(8,128)(2,1)S(1)} collective-permute-done((bf16[2,4,96,512]{3,2,1,0:T(8,128)(2,1)S(1)}, bf16[2,4,96,512]{3,2,1,0:T(8,128)(2,1)S(1)}, u32[]{:S(2)}, u32[]{:S(2)}) %collective-permute-start.4) | collective-permute-done | bytes 786464 | tf_op jit(solution)/shard_map/ppermute | solution.py:21
  39.2 1.4 %pad_maximum_fusion.1 = bf16[2,4,96,1024]{3,2,1,0:T(8,128)(2,1)} fusion(bf16[2,4,96,512]{3,2,1,0:T(8,128)(2,1)S(1)} %get-tuple-element.21, bf16[2,4,96,512]{3,2,1,0:T(8,128)(2,1)S(1)} %get-tuple-element.20), kind=kLoop, calls=%fused_computation.2 | loop fusion | flops 3145728 | bytes 3145728 | tf_op jit(solution)/shard_map/concatenate | solution.py:208
  40.6 2.7 %collective-permute-start.5 = (bf16[2,4,96,1024]{3,2,1,0:T(8,128)(2,1)}, bf16[2,4,96,1024]{3,2,1,0:T(8,128)(2,1)}, u32[]{:S(2)}, u32[]{:S(2)}) collective-permute-start(bf16[2,4,96,1024]{3,2,1,0:T(8,128)(2,1)} %pad_maximum_fusion.1), channel_id=1, source_target_pairs={{0,8},{8,0},{16,24},{24,16},{1,9},{9,1},{17,25},{25,17},{2,10},{10... | collective-permute-start | bytes 4718600 | tf_op jit(solution)/shard_map/ppermute | solution.py:21
  43.3 1.7 %copy.15 = bf16[1024,768]{0,1:T(8,128)(2,1)} copy(bf16[1024,768]{1,0:T(8,128)(2,1)S(1)} %copy-done) | data formatting | bytes 3145728 | tf_op args[0]
  45.0 1.7 %collective-permute-done.5 = bf16[2,4,96,1024]{3,2,1,0:T(8,128)(2,1)} collective-permute-done((bf16[2,4,96,1024]{3,2,1,0:T(8,128)(2,1)}, bf16[2,4,96,1024]{3,2,1,0:T(8,128)(2,1)}, u32[]{:S(2)}, u32[]{:S(2)}) %collective-permute-start.5) | collective-permute-done | bytes 1572896 | tf_op jit(solution)/shard_map/ppermute | solution.py:21
  46.7 2.2 %select_bitcast_fusion.1 = (bf16[2,4,1,96,1024]{4,3,2,1,0:T(8,128)(2,1)S(1)}, bf16[2,4,1,96,1024]{4,3,2,1,0:T(8,128)(2,1)S(1)}) fusion(bf16[2,4,96,1024]{3,2,1,0:T(8,128)(2,1)} %collective-permute-done.5, pred[]{:T(512)S(6)} %ne.28, bf16[2,4,96,512]{3,2,1,0:T(8,128)(2,1)S(1)} %get-tuple-element.21, bf16[2,4,96,512]{3,2,1,0:T(8,128)(2,1)S(1)} %get-tuple-element.20), kind=kLoop, calls=%fused_computation.4 | loop fusion | flops 4718592 | bytes 6291457 | tf_op jit(solution)/shard_map/stack | solution.py:200
  48.9 1.9 %pad_maximum_fusion = bf16[2,4,2,96,1024]{4,3,2,1,0:T(8,128)(2,1)} fusion(bf16[2,4,1,96,1024]{4,3,2,1,0:T(8,128)(2,1)S(1)} %get-tuple-element.17, bf16[2,4,1,96,1024]{4,3,2,1,0:T(8,128)(2,1)S(1)} %get-tuple-element.16), kind=kLoop, calls=%fused_computation | loop fusion | flops 1572864 | bytes 6291456 | tf_op jit(solution)/shard_map/stack | solution.py:200
  50.8 19.2 %all-to-all-done.slots_hbm = bf16[8,128,768]{2,1,0:T(8,128)(2,1)} async-done(((bf16[8,128,768]{2,1,0:T(8,128)(2,1)}), bf16[8,128,768]{2,1,0:T(8,128)(2,1)}, u32[]{:S(2)}, u32[]{:S(2)}) %all-to-all-start) | async-done | bytes 1572896 | tf_op jit(solution)/shard_map/all_to_all | solution.py:272
  70.0 16.5 %shard_map.96 = (bf16[1024,768]{1,0:T(8,128)(2,1)}, bf16[1024,1024]{1,0:T(8,128)(2,1)}, bf16[768,1024]{1,0:T(8,128)(2,1)}) custom-call(s32[1]{0:T(128)} %bitcast.core_ref, s32[8]{0:T(128)} %into_ref.1, bf16[8,128,768]{2,1,0:T(8,128)(2,1)} %all-to-all-done.slots_hbm, bf16[1024,768]{1,0:T(8,128)(2,1)} %features_hbm.3, bf16[768,1024]{1,0:T(8,128)(2,1)} %bitcast.62, ...), custom_call_target="tpu_custom_call" | custom-call | flops 4831838208 | bytes 16777216 | tf_op jit(solution)/shard_map/pallas_call | solution.py:288
  86.5 1.6 %collective-permute-start.6 = (bf16[768,1024]{1,0:T(8,128)(2,1)}, bf16[768,1024]{1,0:T(8,128)(2,1)S(1)}, u32[]{:S(2)}, u32[]{:S(2)}) collective-permute-start(bf16[768,1024]{1,0:T(8,128)(2,1)} %get-tuple-element.15), channel_id=1, source_target_pairs={{0,8},{8,0},{16,24},{24,16},{1,9},{9,1},{17,25},{25,17},{2,10},{10... | collective-permute-start | bytes 4718600 | tf_op jit(solution)/shard_map/ppermute | solution.py:21
  88.1 4.7 %shard_map.97 = bf16[768,1024]{1,0:T(8,128)(2,1)} custom-call(s32[1]{0:T(128)} %bitcast.core_ref, bf16[768,1024]{1,0:T(8,128)(2,1)} %bitcast.63, bf16[1024,768]{1,0:T(8,128)(2,1)} %get-tuple-element.13.aggregate_hbm, bf16[1024,1024]{1,0:T(8,128)(2,1)} %get-tuple-element.14.grad_hbm), custom_call_target="tpu_custom_call" | custom-call | flops 1610612736 | bytes 6291456 | tf_op jit(solution)/shard_map/pallas_call | solution.py:316
  92.8 2.1 %add_convert_fusion = bf16[768,1024]{1,0:T(8,128)(2,1)S(1)} fusion(bf16[768,1024]{1,0:T(8,128)(2,1)S(1)} %collective-permute-done.6, bf16[768,1024]{1,0:T(8,128)(2,1)} %shard_map.97), kind=kLoop, calls=%fused_computation.1 | loop fusion | flops 3145728 | bytes 4718592 | tf_op jit(solution)/shard_map/convert_element_type | solution.py:214
  95.1 0.6 collective-permute-start.9
  95.9 10.5 %collective-permute-done.9 = bf16[8,96,256]{2,1,0:T(8,128)(2,1)S(1)} collective-permute-done((bf16[8,96,256]{2,1,0:T(8,128)(2,1)S(1)}, bf16[8,96,256]{2,1,0:T(8,128)(2,1)S(1)}, u32[]{:S(2)}, u32[]{:S(2)}) %collective-permute-start.9) | collective-permute-done | bytes 393248 | tf_op jit(solution)/shard_map/ppermute | solution.py:21
  106.9 1.6 %collective-permute-start.8 = (bf16[4,96,256]{2,1,0:T(8,128)(2,1)S(1)}, bf16[4,96,256]{2,1,0:T(8,128)(2,1)S(1)}, u32[]{:S(2)}, u32[]{:S(2)}) collective-permute-start(bf16[4,96,256]{2,1,0:T(8,128)(2,1)S(1)} %constant_dynamic-slice_fusion.1), channel_id=1, source_target_pairs={{0,16},{8,24},{16,0},{24,8},{1,17},{9,25},{17,1},{25,9},{2,18},{10... | collective-permute-start | bytes 589832 | tf_op jit(solution)/shard_map/ppermute | solution.py:21
  108.5 4.4 %collective-permute-done.10 = bf16[4,96,256]{2,1,0:T(8,128)(2,1)S(1)} collective-permute-done((bf16[4,96,256]{2,1,0:T(8,128)(2,1)S(1)}, bf16[4,96,256]{2,1,0:T(8,128)(2,1)S(1)}, u32[]{:S(2)}, u32[]{:S(2)}) %collective-permute-start.10) | collective-permute-done | bytes 196640 | tf_op jit(solution)/shard_map/ppermute | solution.py:21
  113.3 2.5 %collective-permute-start.12 = (bf16[96,512]{1,0:T(8,128)(2,1)S(1)}, bf16[96,512]{1,0:T(8,128)(2,1)S(1)}, u32[]{:S(2)}, u32[]{:S(2)}) collective-permute-start(bf16[96,512]{1,0:T(8,128)(2,1)S(1)} %get-tuple-element.29), channel_id=1, source_target_pairs={{0,4},{1,5},{2,6},{3,7},{4,0},{5,1},{6,2},{7,3},{8,12},{9,13},{10,... | collective-permute-start | bytes 294920 | tf_op jit(solution)/shard_map/ppermute | solution.py:21
  115.8 1.9 %collective-permute-start.13 = (bf16[96,512]{1,0:T(8,128)(2,1)S(1)}, bf16[96,512]{1,0:T(8,128)(2,1)S(1)}, u32[]{:S(2)}, u32[]{:S(2)}) collective-permute-start(bf16[96,512]{1,0:T(8,128)(2,1)S(1)} %get-tuple-element.30), channel_id=1, source_target_pairs={{0,6},{1,7},{2,4},{3,5},{4,2},{5,3},{6,0},{7,1},{8,14},{9,15},{10,... | collective-permute-start | bytes 294920 | tf_op jit(solution)/shard_map/ppermute | solution.py:21
  117.9 4.8 %collective-permute-done.12 = bf16[96,512]{1,0:T(8,128)(2,1)S(1)} collective-permute-done((bf16[96,512]{1,0:T(8,128)(2,1)S(1)}, bf16[96,512]{1,0:T(8,128)(2,1)S(1)}, u32[]{:S(2)}, u32[]{:S(2)}) %collective-permute-start.12) | collective-permute-done | bytes 98336 | tf_op jit(solution)/shard_map/ppermute | solution.py:21
  122.8 1.2 collective-permute-start.14
  124.0 3.5 %collective-permute-done.14 = bf16[2,96,256]{2,1,0:T(8,128)(2,1)S(1)} collective-permute-done((bf16[2,96,256]{2,1,0:T(8,128)(2,1)S(1)}, bf16[2,96,256]{2,1,0:T(8,128)(2,1)S(1)}, u32[]{:S(2)}, u32[]{:S(2)}) %collective-permute-start.14) | collective-permute-done | bytes 98336 | tf_op jit(solution)/shard_map/ppermute | solution.py:21
  127.6 1.4 %collective-permute-done.15 = bf16[96,1024]{1,0:T(8,128)(2,1)S(1)} collective-permute-done((bf16[96,1024]{1,0:T(8,128)(2,1)S(1)}, bf16[96,1024]{1,0:T(8,128)(2,1)S(1)}, u32[]{:S(2)}, u32[]{:S(2)}) %collective-permute-start.15) | collective-permute-done | bytes 196640 | tf_op jit(solution)/shard_map/ppermute | solution.py:21
  129.1 1.0 select_convert_fusion
  (36 shorter events, 2.1 us)
Async XLA Ops:
  1.6 10.9 %collective-permute-start = (bf16[2,96,512]{2,1,0:T(8,128)(2,1)S(1)}, bf16[2,96,512]{2,1,0:T(8,128)(2,1)S(1)}, u32[]{:S(2)}, u32[]{:S(2)}) collective-permute-start(bf16[2,96,512]{2,1,0:T(8,128)(2,1)S(1)} %pad_maximum_fusion.5), channel_id=1, source_target_pairs={{8,9},{9,8},{10,11},{11,10},{12,13},{13,12},{14,15},{15,14},{24,25... | collective-permute-start | bytes 589832 | tf_op jit(solution)/shard_map/ppermute | solution.py:29
  2.3 10.2 %collective-permute-start.1 = (bf16[2,96,512]{2,1,0:T(8,128)(2,1)S(1)}, bf16[2,96,512]{2,1,0:T(8,128)(2,1)S(1)}, u32[]{:S(2)}, u32[]{:S(2)}) collective-permute-start(bf16[2,96,512]{2,1,0:T(8,128)(2,1)S(1)} %pad_maximum_fusion.5), channel_id=1, source_target_pairs={{0,2},{1,3},{2,0},{3,1},{4,6},{5,7},{6,4},{7,5},{8,11},{9,10},{10,... | collective-permute-start | bytes 589832 | tf_op jit(solution)/shard_map/ppermute | solution.py:29
  5.4 8.2 %collective-permute-start.2 = (bf16[2,96,512]{2,1,0:T(8,128)(2,1)S(1)}, bf16[2,96,512]{2,1,0:T(8,128)(2,1)S(1)}, u32[]{:S(2)}, u32[]{:S(2)}) collective-permute-start(bf16[2,96,512]{2,1,0:T(8,128)(2,1)S(1)} %pad_maximum_fusion.5), channel_id=1, source_target_pairs={{0,4},{1,5},{2,6},{3,7},{4,0},{5,1},{6,2},{7,3},{8,13},{9,12},{10,... | collective-permute-start | bytes 589832 | tf_op jit(solution)/shard_map/ppermute | solution.py:29
  8.0 12.8 %collective-permute-start.3 = (bf16[2,96,512]{2,1,0:T(8,128)(2,1)S(1)}, bf16[2,96,512]{2,1,0:T(8,128)(2,1)S(1)}, u32[]{:S(2)}, u32[]{:S(2)}) collective-permute-start(bf16[2,96,512]{2,1,0:T(8,128)(2,1)S(1)} %pad_maximum_fusion.5), channel_id=1, source_target_pairs={{0,6},{1,7},{2,4},{3,5},{4,2},{5,3},{6,0},{7,1},{8,15},{9,14},{10,... | collective-permute-start | bytes 589832 | tf_op jit(solution)/shard_map/ppermute | solution.py:29
  21.1 18.0 %collective-permute-start.4 = (bf16[2,4,96,512]{3,2,1,0:T(8,128)(2,1)S(1)}, bf16[2,4,96,512]{3,2,1,0:T(8,128)(2,1)S(1)}, u32[]{:S(2)}, u32[]{:S(2)}) collective-permute-start(bf16[2,4,96,512]{3,2,1,0:T(8,128)(2,1)S(1)} %pad_maximum_fusion.2), channel_id=1, source_target_pairs={{0,16},{8,24},{16,0},{24,8},{1,17},{9,25},{17,1},{25,9},{2,18},{10... | collective-permute-start | bytes 2359304 | tf_op jit(solution)/shard_map/ppermute | solution.py:21
  22.7 47.3 %all-to-all-start = ((bf16[8,128,768]{2,1,0:T(8,128)(2,1)}), bf16[8,128,768]{2,1,0:T(8,128)(2,1)}, u32[]{:S(2)}, u32[]{:S(2)}) async-start(bf16[8,128,768]{2,1,0:T(8,128)(2,1)} %bitcast.2), calls=%async_computation | async-start | bytes 3145728 | tf_op jit(solution)/shard_map/all_to_all | solution.py:272
  39.2 4.2 %copy-start = (bf16[1024,768]{1,0:T(8,128)(2,1)S(1)}, bf16[1024,768]{1,0:T(8,128)(2,1)}, u32[]{:S(2)}) copy-start(bf16[1024,768]{1,0:T(8,128)(2,1)} %features_hbm.3) | copy-start | bytes 4718596
  40.6 6.1 %collective-permute-start.5 = (bf16[2,4,96,1024]{3,2,1,0:T(8,128)(2,1)}, bf16[2,4,96,1024]{3,2,1,0:T(8,128)(2,1)}, u32[]{:S(2)}, u32[]{:S(2)}) collective-permute-start(bf16[2,4,96,1024]{3,2,1,0:T(8,128)(2,1)} %pad_maximum_fusion.1), channel_id=1, source_target_pairs={{0,8},{8,0},{16,24},{24,16},{1,9},{9,1},{17,25},{25,17},{2,10},{10... | collective-permute-start | bytes 4718600 | tf_op jit(solution)/shard_map/ppermute | solution.py:21
  86.5 6.2 %collective-permute-start.6 = (bf16[768,1024]{1,0:T(8,128)(2,1)}, bf16[768,1024]{1,0:T(8,128)(2,1)S(1)}, u32[]{:S(2)}, u32[]{:S(2)}) collective-permute-start(bf16[768,1024]{1,0:T(8,128)(2,1)} %get-tuple-element.15), channel_id=1, source_target_pairs={{0,8},{8,0},{16,24},{24,16},{1,9},{9,1},{17,25},{25,17},{2,10},{10... | collective-permute-start | bytes 4718600 | tf_op jit(solution)/shard_map/ppermute | solution.py:21
  95.1 11.4 %collective-permute-start.9 = (bf16[8,96,256]{2,1,0:T(8,128)(2,1)S(1)}, bf16[8,96,256]{2,1,0:T(8,128)(2,1)S(1)}, u32[]{:S(2)}, u32[]{:S(2)}) collective-permute-start(bf16[8,96,256]{2,1,0:T(8,128)(2,1)S(1)} %constant_dynamic-slice_fusion), channel_id=1, source_target_pairs={{0,16},{8,24},{16,0},{24,8},{1,17},{9,25},{17,1},{25,9},{2,18},{10... | collective-permute-start | bytes 1179656 | tf_op jit(solution)/shard_map/ppermute | solution.py:21
  95.7 11.1 %collective-permute-start.7 = (bf16[4,96,512]{2,1,0:T(8,128)(2,1)S(1)}, bf16[4,96,512]{2,1,0:T(8,128)(2,1)S(1)}, u32[]{:S(2)}, u32[]{:S(2)}) collective-permute-start(bf16[4,96,512]{2,1,0:T(8,128)(2,1)S(1)} %dynamic-slice_bitcast_fusion), channel_id=1, source_target_pairs={{0,1},{1,0},{2,3},{3,2},{4,5},{5,4},{6,7},{7,6},{8,9},{9,8},{10,11... | collective-permute-start | bytes 1179656 | tf_op jit(solution)/shard_map/ppermute | solution.py:21
  106.6 6.3 %collective-permute-start.10 = (bf16[4,96,256]{2,1,0:T(8,128)(2,1)S(1)}, bf16[4,96,256]{2,1,0:T(8,128)(2,1)S(1)}, u32[]{:S(2)}, u32[]{:S(2)}) collective-permute-start(bf16[4,96,256]{2,1,0:T(8,128)(2,1)S(1)} %dynamic-slice_bitcast_fusion.1), channel_id=1, source_target_pairs={{0,1},{1,0},{2,3},{3,2},{4,5},{5,4},{6,7},{7,6},{8,9},{9,8},{10,11... | collective-permute-start | bytes 589832 | tf_op jit(solution)/shard_map/ppermute | solution.py:21
  106.9 6.2 %collective-permute-start.8 = (bf16[4,96,256]{2,1,0:T(8,128)(2,1)S(1)}, bf16[4,96,256]{2,1,0:T(8,128)(2,1)S(1)}, u32[]{:S(2)}, u32[]{:S(2)}) collective-permute-start(bf16[4,96,256]{2,1,0:T(8,128)(2,1)S(1)} %constant_dynamic-slice_fusion.1), channel_id=1, source_target_pairs={{0,16},{8,24},{16,0},{24,8},{1,17},{9,25},{17,1},{25,9},{2,18},{10... | collective-permute-start | bytes 589832 | tf_op jit(solution)/shard_map/ppermute | solution.py:21
  113.2 4.7 %collective-permute-start.11 = (bf16[96,512]{1,0:T(8,128)(2,1)S(1)}, bf16[96,512]{1,0:T(8,128)(2,1)S(1)}, u32[]{:S(2)}, u32[]{:S(2)}) collective-permute-start(bf16[96,512]{1,0:T(8,128)(2,1)S(1)} %get-tuple-element.28), channel_id=1, source_target_pairs={{0,2},{1,3},{2,0},{3,1},{4,6},{5,7},{6,4},{7,5},{8,10},{9,11},{10,... | collective-permute-start | bytes 294920 | tf_op jit(solution)/shard_map/ppermute | solution.py:21
  113.3 9.4 %collective-permute-start.12 = (bf16[96,512]{1,0:T(8,128)(2,1)S(1)}, bf16[96,512]{1,0:T(8,128)(2,1)S(1)}, u32[]{:S(2)}, u32[]{:S(2)}) collective-permute-start(bf16[96,512]{1,0:T(8,128)(2,1)S(1)} %get-tuple-element.29), channel_id=1, source_target_pairs={{0,4},{1,5},{2,6},{3,7},{4,0},{5,1},{6,2},{7,3},{8,12},{9,13},{10,... | collective-permute-start | bytes 294920 | tf_op jit(solution)/shard_map/ppermute | solution.py:21
  115.8 6.9 %collective-permute-start.13 = (bf16[96,512]{1,0:T(8,128)(2,1)S(1)}, bf16[96,512]{1,0:T(8,128)(2,1)S(1)}, u32[]{:S(2)}, u32[]{:S(2)}) collective-permute-start(bf16[96,512]{1,0:T(8,128)(2,1)S(1)} %get-tuple-element.30), channel_id=1, source_target_pairs={{0,6},{1,7},{2,4},{3,5},{4,2},{5,3},{6,0},{7,1},{8,14},{9,15},{10,... | collective-permute-start | bytes 294920 | tf_op jit(solution)/shard_map/ppermute | solution.py:21
  122.8 4.7 %collective-permute-start.14 = (bf16[2,96,256]{2,1,0:T(8,128)(2,1)S(1)}, bf16[2,96,256]{2,1,0:T(8,128)(2,1)S(1)}, u32[]{:S(2)}, u32[]{:S(2)}) collective-permute-start(bf16[2,96,256]{2,1,0:T(8,128)(2,1)S(1)} %pad_maximum_fusion.8), channel_id=1, source_target_pairs={{0,16},{8,24},{16,0},{24,8},{1,17},{9,25},{17,1},{25,9},{2,18},{10... | collective-permute-start | bytes 294920 | tf_op jit(solution)/shard_map/ppermute | solution.py:21
  127.5 1.5 %collective-permute-start.15 = (bf16[96,1024]{1,0:T(8,128)(2,1)S(1)}, bf16[96,1024]{1,0:T(8,128)(2,1)S(1)}, u32[]{:S(2)}, u32[]{:S(2)}) collective-permute-start(bf16[96,1024]{1,0:T(8,128)(2,1)S(1)} %pad_maximum_fusion.6), channel_id=1, source_target_pairs={{0,8},{8,0},{16,24},{24,16},{1,9},{9,1},{17,25},{25,17},{2,10},{10... | collective-permute-start | bytes 589832 | tf_op jit(solution)/shard_map/ppermute | solution.py:21

commit v8 on v7

--- a/solution.py
+++ b/solution.py
@@ -29,20 +29,30 @@
     return lax.ppermute(value, ("rep", "dom"), [(source, target) for source, target in pairs if source != target])
 
 
+def split_copies(source, target, sems, count=4):
+    size = source.shape[0] // count
+    return [
+        pltpu.make_async_copy(
+            source.at[index * size : (index + 1) * size], target.at[index * size : (index + 1) * size], sems.at[index]
+        )
+        for index in range(count)
+    ]
+
+
 def slots_kernel(
     src_hbm, peer_hbm, tiles_hbm, features_hbm, out_hbm, src, peer, tiles, features, dense, out, in_sems, out_sems
 ):
-    copies = [
-        pltpu.make_async_copy(source, target, in_sems.at[index])
-        for index, (source, target) in enumerate(
-            [(src_hbm, src), (peer_hbm, peer), (tiles_hbm, tiles), (features_hbm, features)]
-        )
-    ]
-    for copy in copies:
+    scalars = [
+        pltpu.make_async_copy(src_hbm, src, in_sems.at[2, 0]),
+        pltpu.make_async_copy(peer_hbm, peer, in_sems.at[2, 1]),
+    ]
+    tile_copies = split_copies(tiles_hbm, tiles, in_sems.at[0])
+    feature_copies = split_copies(features_hbm, features, in_sems.at[1])
+    for copy in scalars + tile_copies + feature_copies:
         copy.start()
     count, block, _ = tiles.shape
     dense[...] = jnp.zeros_like(dense)
-    for copy in copies[:3]:
+    for copy in scalars + tile_copies:
         copy.wait()
 
     def place(tile, carry):
@@ -53,7 +63,8 @@
         return carry
 
     lax.fori_loop(0, count, place, 0)
-    copies[3].wait()
+    for copy in feature_copies:
+        copy.wait()
     chunk = 4 * block
     results = []
     for index in range(out.shape[0] // chunk):
@@ -72,7 +83,8 @@
     features_hbm,
     turned_hbm,
     cotangent_hbm,
-    weights_hbm,
+    w_self_hbm,
+    w_neigh_hbm,
     aggregate_hbm,
     grad_hbm,
     sent_hbm,
@@ -80,38 +92,34 @@
     features,
     left,
     cotangent,
-    weights,
+    w_self,
+    w_neigh,
     summed,
+    values,
     aggregate,
     grad,
     sent,
     slot_sems,
     row_sems,
-    column_sems,
+    weight_sems,
     out_sems,
 ):
     senders, block, _ = slots.shape
-    hidden = grad.shape[1]
+    rows, hidden = grad.shape
     core = core_ref[0]
     arrivals = [
         pltpu.make_async_copy(slots_hbm.at[sender], slots.at[sender], slot_sems.at[sender]) for sender in range(senders)
     ]
-    for arrival in arrivals:
-        arrival.start()
-    inputs = pltpu.make_async_copy(features_hbm, features, row_sems.at[0])
-    inputs.start()
-    spans = [slice(first, first + 256) for first in range(0, hidden, 256)]
-    streams = [
-        [
-            pltpu.make_async_copy(weights_hbm.at[0, :, at], weights.at[0, :, at], column_sems.at[0, index]),
-            pltpu.make_async_copy(weights_hbm.at[1, :, at], weights.at[1, :, at], column_sems.at[1, index]),
-            pltpu.make_async_copy(cotangent_hbm.at[:, at], cotangent.at[:, at], column_sems.at[2, index]),
-        ]
-        for index, at in enumerate(spans)
-    ]
-    for stream in streams:
-        for copy in stream:
-            copy.start()
+    chunk = 256
+    parts = rows // chunk
+    weight_copies = split_copies(w_self_hbm, w_self, weight_sems.at[0])
+    weight_copies += split_copies(w_neigh_hbm, w_neigh, weight_sems.at[1])
+    feature_copies = split_copies(features_hbm, features, row_sems.at[0], parts)
+    cotangent_copies = split_copies(cotangent_hbm, cotangent, row_sems.at[1], parts)
+    for copy in arrivals + weight_copies + feature_copies + cotangent_copies:
+        copy.start()
+    turning = pltpu.make_async_copy(turned_hbm, left, weight_sems.at[2, 0])
+    pl.when(core != 0)(turning.start)
 
     summed[...] = jnp.zeros_like(summed)
     for sender in range(senders):
@@ -119,33 +127,46 @@
         at = pl.ds(pl.multiple_of(into_ref[sender] * block, block), block)
         summed[at, :] = summed[at, :] + slots[sender].astype(F32)
     aggregate[...] = summed[...].astype(BF16)
-    results = [pltpu.make_async_copy(aggregate, aggregate_hbm, row_sems.at[1])]
+    results = [pltpu.make_async_copy(aggregate, aggregate_hbm, weight_sems.at[2, 1])]
     results[0].start()
 
     @pl.when(core == 0)
     def _():
         left[...] = aggregate[...].T
 
-    @pl.when(core != 0)
-    def _():
-        turning = pltpu.make_async_copy(turned_hbm, left, row_sems.at[2])
-        turning.start()
-        turning.wait()
-
-    inputs.wait()
-    for index, at in enumerate(spans):
-        for copy in streams[index]:
-            copy.wait()
-        value = jnp.dot(features[...], weights[0, :, at], preferred_element_type=F32) + jnp.dot(
-            aggregate[...], weights[1, :, at], preferred_element_type=F32
-        )
-        square = value * value
-        bend = jnp.tanh(value * (SCALE + SCALE * CUBIC * square))
-        inner = value * (SCALE + 3.0 * SCALE * CUBIC * square)
-        slope = (1.0 + bend) * (0.5 + 0.5 * inner * (1.0 - bend))
-        grad[:, at] = (cotangent[:, at].astype(F32) * slope).astype(BF16)
-        results.append(pltpu.make_async_copy(grad.at[:, at], grad_hbm.at[:, at], out_sems.at[0, index]))
+    pl.when(core != 0)(turning.wait)
+    for copy in weight_copies + feature_copies:
+        copy.wait()
+    span = 512
+
+    def multiply(index):
+        at = slice(index * chunk, (index + 1) * chunk)
+        for first in range(0, hidden, span):
+            columns = slice(first, first + span)
+            values[index % 2, :, columns] = jnp.dot(
+                features[at, :], w_self[:, columns], preferred_element_type=F32
+            ) + jnp.dot(aggregate[at, :], w_neigh[:, columns], preferred_element_type=F32)
+
+    multiply(0)
+    for index in range(parts):
+        if index + 1 < parts:
+            multiply(index + 1)
+        cotangent_copies[index].wait()
+        for row in range(0, chunk, 16):
+            at = slice(index * chunk + row, index * chunk + row + 16)
+            for first in range(0, hidden, span):
+                columns = slice(first, first + span)
+                value = values[index % 2, row : row + 16, columns]
+                square = value * value
+                bend = jnp.tanh(value * (SCALE + SCALE * CUBIC * square))
+                inner = value * (SCALE + 3.0 * SCALE * CUBIC * square)
+                slope = (1.0 + bend) * (0.5 + 0.5 * inner * (1.0 - bend))
+                grad[at, columns] = (cotangent[at, columns].astype(F32) * slope).astype(BF16)
+        at = slice(index * chunk, (index + 1) * chunk)
+        results.append(pltpu.make_async_copy(grad.at[at, :], grad_hbm.at[at, :], out_sems.at[0, index]))
         results[-1].start()
+    for index, first in enumerate(range(0, hidden, span)):
+        at = slice(first, first + span)
         sent[:, at] = jnp.dot(left[...], grad[:, at], preferred_element_type=F32).astype(BF16)
         results.append(pltpu.make_async_copy(sent.at[:, at], sent_hbm.at[:, at], out_sems.at[1, index]))
         results[-1].start()
@@ -156,22 +177,19 @@
 def kept_kernel(core_ref, turned_hbm, aggregate_hbm, grad_hbm, out_hbm, turned, aggregate, grad, out, in_sems, out_sems):
     core = core_ref[0]
     spans = [slice(first, first + 512) for first in range(0, out.shape[1], 512)]
-    grads = [
-        pltpu.make_async_copy(grad_hbm.at[:, at], grad.at[:, at], in_sems.at[1 + index]) for index, at in enumerate(spans)
-    ]
+    grads = split_copies(grad_hbm, grad, in_sems.at[1])
     results = [
         pltpu.make_async_copy(out.at[:, at], out_hbm.at[:, at], out_sems.at[index]) for index, at in enumerate(spans)
     ]
 
     def product(left_hbm, left, contract):
         def body():
-            copy = pltpu.make_async_copy(left_hbm, left, in_sems.at[0])
-            copy.start()
-            for stream in grads:
-                stream.start()
-            copy.wait()
-            for at, stream, result in zip(spans, grads, results):
-                stream.wait()
+            copies = split_copies(left_hbm, left, in_sems.at[0]) + grads
+            for copy in copies:
+                copy.start()
+            for copy in copies:
+                copy.wait()
+            for at, result in zip(spans, results):
                 value = lax.dot_general(left[...], grad[:, at], (contract, ((), ())), preferred_element_type=F32)
                 out[:, at] = value.astype(BF16)
                 result.start()
@@ -262,7 +280,7 @@
             pltpu.VMEM(features.shape, BF16),
             pltpu.VMEM((dom_size * block, rows), F32),
             pltpu.VMEM((dom_size * block, width), BF16),
-            DMA((4,)),
+            DMA((3, 4)),
             DMA((dom_size // 4,)),
         ],
         flops=2 * dom_size * block * rows * width,
@@ -281,8 +299,10 @@
         ]
         bit *= 2
     mine = gather_high(pieces[0], high)
-    other = swap(mine, "rep", 1)
-    weights = joined(mine, other, (low ^ core) != 0, 2).reshape(2, width, hidden)
+    weights = [
+        joined(mine[index], swap(mine[index], "rep", 1), (low ^ core) != 0, 1).reshape(width, hidden)
+        for index in range(2)
+    ]
     turned = features.T
 
     aggregate, grad, sent = call(
@@ -292,26 +312,28 @@
             jax.ShapeDtypeStruct((rows, hidden), BF16),
             jax.ShapeDtypeStruct((width, hidden), BF16),
         ],
-        [SMEM, SMEM] + [HBM] * 5,
+        [SMEM, SMEM] + [HBM] * 6,
         [HBM] * 3,
         [
             pltpu.VMEM((dom_size, block, width), BF16),
             pltpu.VMEM((rows, width), BF16),
             pltpu.VMEM((width, rows), BF16),
             pltpu.VMEM((rows, hidden), BF16),
-            pltpu.VMEM((2, width, hidden), BF16),
+            pltpu.VMEM((width, hidden), BF16),
+            pltpu.VMEM((width, hidden), BF16),
             pltpu.VMEM((rows, width), F32),
+            pltpu.VMEM((2, 256, hidden), F32),
             pltpu.VMEM((rows, width), BF16),
             pltpu.VMEM((rows, hidden), BF16),
             pltpu.VMEM((width, hidden), BF16),
             DMA((dom_size,)),
-            DMA((3,)),
-            DMA((3, hidden // 256)),
-            DMA((2, hidden // 256)),
+            DMA((2, rows // 256)),
+            DMA((3, 4)),
+            DMA((2, rows // 256)),
         ],
         flops=6 * rows * width * hidden,
         moved=16 * rows * hidden,
-    )(core_arg, in_block, received, features, turned, cotangent, weights)
+    )(core_arg, in_block, received, features, turned, cotangent, *weights)
     arrived = swap(sent, "rep", 1)
     kept = call(
         kept_kernel,
@@ -323,7 +345,7 @@
             pltpu.VMEM((rows, width), BF16),
             pltpu.VMEM((rows, hidden), BF16),
             pltpu.VMEM((width, hidden), BF16),
-            DMA((1 + hidden // 512,)),
+            DMA((2, 4)),
             DMA((hidden // 512,)),
         ],
         flops=2 * rows * width * hidden,

time: 130 us -> 126 us (0.969)
  Pallas kernels: 25.7 us -> 22.7 us
  other arithmetic: 9.42 us -> 7.99 us
    pallas_call x1, Pallas kernels: 16.5 us -> 13.2 us  [shards(): call(layer_kernel, [jax.ShapeDtypeStruct((rows, width), BF16), jax.ShapeD...]
    concatenate x1 -> x0, other arithmetic: 1.41 us -> none  [gather_high(): jnp.concatenate([jnp.where(upper, other, held), jnp.where(upper, held, ot...]
    ppermute x12 -> x13, waiting for transfers between devices: 34.4 us -> 33 us  [swap(): lax.ppermute(value, axis, [(index, index ^ step) for index in range(size)])]
    another operation x0 -> x1, local copies, waits for them, and re-layouts: none -> 1.36 us  [joined(): jnp.stack([jnp.where(upper, other, held), jnp.where(upper, held, other)],...]
    all_to_all x1, waiting for transfers between devices: 19.2 us -> 20.5 us  [shards(): lax.all_to_all(slots.reshape(dom_size, block, width), 'dom', split_axis=0...]
    ppermute x12 -> x13, starting transfers between devices: 14.1 us -> 13.1 us  [swap(): lax.ppermute(value, axis, [(index, index ^ step) for index in range(size)])]
    another operation x2 -> x4, other arithmetic: 4.12 us -> 3.92 us  [joined(): jnp.stack([jnp.where(upper, other, held), jnp.where(upper, held, other)],...]
  transfers between devices with their start and end apart: 17 -> 18, of which waited for: 12 -> 12; matrix products, arithmetic and copies ran while one was open for 6% -> 6% of each run, Pallas kernels for 7% -> 8%
where the time goes in v8:
time: 126 us
  waiting for transfers between devices  61.8 us (49%)
  starting transfers between devices  28.2 us (22%)
  Pallas kernels  22.7 us (18%)
  other arithmetic  7.99 us (6%)
  local copies, waits for them, and re-layouts  4.24 us (3%)
    ppermute x13, waiting for transfers between devices, swap(): lax.ppermute(value, axis, [(index, index ^ step) for index in range(size)])  33 us
    all_to_all x1, waiting for transfers between devices, shards(): lax.all_to_all(slots.reshape(dom_size, block, width), 'dom', split_axis=0...  20.5 us
    pallas_call x1, Pallas kernels, shards(): call(layer_kernel, [jax.ShapeDtypeStruct((rows, width), BF16), jax.ShapeD...  13.2 us
    ppermute x13, starting transfers between devices, swap(): lax.ppermute(value, axis, [(index, index ^ step) for index in range(size)])  13.1 us
    all_to_all x1, starting transfers between devices, shards(): lax.all_to_all(slots.reshape(dom_size, block, width), 'dom', split_axis=0...  8.75 us
    ppermute x4, waiting for transfers between devices, cross(): lax.ppermute(value, ('rep', 'dom'), [(source, target) for source, target...  8.24 us
    ppermute x4, starting transfers between devices, cross(): lax.ppermute(value, ('rep', 'dom'), [(source, target) for source, target...  6.35 us
    pallas_call x1, Pallas kernels, shards(): call(kept_kernel, jax.ShapeDtypeStruct((width, hidden), BF16), [SMEM] + [...  5.01 us
  transfers between devices with their start and end apart: 18, of which 12 were waited for; matrix products, arithmetic and copies ran while one was open for 6% of the time, Pallas kernels for 8%

profile of v8, /device:TPU:0, one launch (start us, length us, event | category | flops | bytes accessed | tf_op | source)
XLA Modules:
  0.0 125.9 jit_solution(16232735435270453627)
XLA Ops:
  0.6 1.0 dynamic-slice_bitcast_fusion.2
  1.6 0.7 collective-permute-start
  2.3 3.1 %collective-permute-start.1 = (bf16[2,96,512]{2,1,0:T(8,128)(2,1)S(1)}, bf16[2,96,512]{2,1,0:T(8,128)(2,1)S(1)}, u32[]{:S(2)}, u32[]{:S(2)}) collective-permute-start(bf16[2,96,512]{2,1,0:T(8,128)(2,1)S(1)} %pad_maximum_fusion.6), channel_id=1, source_target_pairs={{0,2},{1,3},{2,0},{3,1},{4,6},{5,7},{6,4},{7,5},{8,11},{9,10},{10,... | collective-permute-start | bytes 589832 | tf_op jit(solution)/shard_map/ppermute | solution.py:29
  5.4 2.6 %collective-permute-start.2 = (bf16[2,96,512]{2,1,0:T(8,128)(2,1)S(1)}, bf16[2,96,512]{2,1,0:T(8,128)(2,1)S(1)}, u32[]{:S(2)}, u32[]{:S(2)}) collective-permute-start(bf16[2,96,512]{2,1,0:T(8,128)(2,1)S(1)} %pad_maximum_fusion.6), channel_id=1, source_target_pairs={{0,4},{1,5},{2,6},{3,7},{4,0},{5,1},{6,2},{7,3},{8,13},{9,12},{10,... | collective-permute-start | bytes 589832 | tf_op jit(solution)/shard_map/ppermute | solution.py:29
  8.0 4.6 %shard_map.95 = bf16[1024,768]{1,0:T(8,128)(2,1)} custom-call(s32[32]{0:T(128)} %src_hbm.1, s32[32]{0:T(128)} %peer_hbm.1, bf16[32,128,128]{2,1,0:T(8,128)(2,1)} %tiles_hbm.1, bf16[1024,768]{1,0:T(8,128)(2,1)} %features_hbm.3), custom_call_target="tpu_custom_call" | custom-call | flops 1610612736 | bytes 4194304 | tf_op jit(solution)/shard_map/pallas_call | solution.py:271
  12.6 1.0 collective-permute-done.2
  13.6 7.2 %collective-permute-done.3 = bf16[2,96,512]{2,1,0:T(8,128)(2,1)S(1)} collective-permute-done((bf16[2,96,512]{2,1,0:T(8,128)(2,1)S(1)}, bf16[2,96,512]{2,1,0:T(8,128)(2,1)S(1)}, u32[]{:S(2)}, u32[]{:S(2)}) %collective-permute-start.3) | collective-permute-done | bytes 196640 | tf_op jit(solution)/shard_map/ppermute | solution.py:29
  21.1 1.6 %collective-permute-start.4 = (bf16[2,4,96,512]{3,2,1,0:T(8,128)(2,1)S(1)}, bf16[2,4,96,512]{3,2,1,0:T(8,128)(2,1)S(1)}, u32[]{:S(2)}, u32[]{:S(2)}) collective-permute-start(bf16[2,4,96,512]{3,2,1,0:T(8,128)(2,1)S(1)} %pad_maximum_fusion.3), channel_id=1, source_target_pairs={{0,16},{8,24},{16,0},{24,8},{1,17},{9,25},{17,1},{25,9},{2,18},{10... | collective-permute-start | bytes 2359304 | tf_op jit(solution)/shard_map/ppermute | solution.py:21
  22.7 8.7 %all-to-all-start = ((bf16[8,128,768]{2,1,0:T(8,128)(2,1)}), bf16[8,128,768]{2,1,0:T(8,128)(2,1)}, u32[]{:S(2)}, u32[]{:S(2)}) async-start(bf16[8,128,768]{2,1,0:T(8,128)(2,1)} %bitcast.2), calls=%async_computation | async-start | bytes 3145728 | tf_op jit(solution)/shard_map/all_to_all | solution.py:290
  31.4 7.6 %collective-permute-done.4 = bf16[2,4,96,512]{3,2,1,0:T(8,128)(2,1)S(1)} collective-permute-done((bf16[2,4,96,512]{3,2,1,0:T(8,128)(2,1)S(1)}, bf16[2,4,96,512]{3,2,1,0:T(8,128)(2,1)S(1)}, u32[]{:S(2)}, u32[]{:S(2)}) %collective-permute-start.4) | collective-permute-done | bytes 786464 | tf_op jit(solution)/shard_map/ppermute | solution.py:21
  39.4 2.8 %collective-permute-start.5 = (bf16[4,96,1024]{2,1,0:T(8,128)(2,1)S(1)}, bf16[4,96,1024]{2,1,0:T(8,128)(2,1)}, u32[]{:S(2)}, u32[]{:S(2)}) collective-permute-start(bf16[4,96,1024]{2,1,0:T(8,128)(2,1)S(1)} %get-tuple-element.21), channel_id=1, source_target_pairs={{0,8},{8,0},{16,24},{24,16},{1,9},{9,1},{17,25},{25,17},{2,10},{10... | collective-permute-start | bytes 2359304 | tf_op jit(solution)/shard_map/ppermute | solution.py:21
  42.2 1.6 %copy.16 = bf16[1024,768]{0,1:T(8,128)(2,1)} copy(bf16[1024,768]{1,0:T(8,128)(2,1)S(1)} %copy-done) | data formatting | bytes 3145728 | tf_op args[0]
  44.2 1.2 select_bitcast_fusion.3
  45.6 1.4 %copy.20 = bf16[4,2,96,1024]{3,2,1,0:T(8,128)(2,1)} copy(bf16[4,2,96,1024]{3,2,0,1:T(8,128)(2,1)S(1)} %pad_maximum_fusion) | data formatting | bytes 3145728 | tf_op jit(solution)/shard_map/stack | solution.py:218
  47.0 1.2 select_bitcast_fusion.1
  48.2 1.3 %pad_maximum_fusion.1 = bf16[4,2,96,1024]{3,2,1,0:T(8,128)(2,1)} fusion(bf16[4,1,96,1024]{3,2,1,0:T(8,128)(2,1)S(1)} %get-tuple-element.19, bf16[4,1,96,1024]{3,2,1,0:T(8,128)(2,1)S(1)} %get-tuple-element.18), kind=kLoop, calls=%fused_computation.4 | loop fusion | flops 786432 | bytes 3145728 | tf_op jit(solution)/shard_map/stack | solution.py:218
  49.5 20.5 %all-to-all-done.slots_hbm = bf16[8,128,768]{2,1,0:T(8,128)(2,1)} async-done(((bf16[8,128,768]{2,1,0:T(8,128)(2,1)}), bf16[8,128,768]{2,1,0:T(8,128)(2,1)}, u32[]{:S(2)}, u32[]{:S(2)}) %all-to-all-start) | async-done | bytes 1572896 | tf_op jit(solution)/shard_map/all_to_all | solution.py:290
  70.0 13.2 %shard_map.96 = (bf16[1024,768]{1,0:T(8,128)(2,1)}, bf16[1024,1024]{1,0:T(8,128)(2,1)}, bf16[768,1024]{1,0:T(8,128)(2,1)}) custom-call(s32[1]{0:T(128)} %bitcast.core_ref, s32[8]{0:T(128)} %into_ref.1, bf16[8,128,768]{2,1,0:T(8,128)(2,1)} %all-to-all-done.slots_hbm, bf16[1024,768]{1,0:T(8,128)(2,1)} %features_hbm.3, bf16[768,1024]{1,0:T(8,128)(2,1)} %bitcast.71, ...), custom_call_target="tpu_custom_call" | custom-call | flops 4831838208 | bytes 16777216 | tf_op jit(solution)/shard_map/pallas_call | solution.py:308
  83.3 5.0 %shard_map.97 = bf16[768,1024]{1,0:T(8,128)(2,1)} custom-call(s32[1]{0:T(128)} %bitcast.core_ref, bf16[768,1024]{1,0:T(8,128)(2,1)} %bitcast.72, bf16[1024,768]{1,0:T(8,128)(2,1)} %get-tuple-element.13.aggregate_hbm, bf16[1024,1024]{1,0:T(8,128)(2,1)} %get-tuple-element.14.grad_hbm), custom_call_target="tpu_custom_call" | custom-call | flops 1610612736 | bytes 6291456 | tf_op jit(solution)/shard_map/pallas_call | solution.py:338
  88.3 2.1 %add_convert_fusion = bf16[768,1024]{1,0:T(8,128)(2,1)S(1)} fusion(bf16[768,1024]{1,0:T(8,128)(2,1)S(1)} %collective-permute-done.7, bf16[768,1024]{1,0:T(8,128)(2,1)} %shard_map.97), kind=kLoop, calls=%fused_computation | loop fusion | flops 3145728 | bytes 4718592 | tf_op jit(solution)/shard_map/convert_element_type | solution.py:232
  91.2 0.7 collective-permute-start.8
  91.9 10.1 %collective-permute-done.10 = bf16[8,96,256]{2,1,0:T(8,128)(2,1)S(1)} collective-permute-done((bf16[8,96,256]{2,1,0:T(8,128)(2,1)S(1)}, bf16[8,96,256]{2,1,0:T(8,128)(2,1)S(1)}, u32[]{:S(2)}, u32[]{:S(2)}) %collective-permute-start.10) | collective-permute-done | bytes 393248 | tf_op jit(solution)/shard_map/ppermute | solution.py:21
  102.2 0.7 collective-permute-start.11
  103.0 1.1 collective-permute-start.9
  104.1 4.5 %collective-permute-done.11 = bf16[4,96,256]{2,1,0:T(8,128)(2,1)S(1)} collective-permute-done((bf16[4,96,256]{2,1,0:T(8,128)(2,1)S(1)}, bf16[4,96,256]{2,1,0:T(8,128)(2,1)S(1)}, u32[]{:S(2)}, u32[]{:S(2)}) %collective-permute-start.11) | collective-permute-done | bytes 196640 | tf_op jit(solution)/shard_map/ppermute | solution.py:21
  109.3 2.0 %collective-permute-start.13 = (bf16[96,512]{1,0:T(8,128)(2,1)S(1)}, bf16[96,512]{1,0:T(8,128)(2,1)S(1)}, u32[]{:S(2)}, u32[]{:S(2)}) collective-permute-start(bf16[96,512]{1,0:T(8,128)(2,1)S(1)} %get-tuple-element.33), channel_id=1, source_target_pairs={{0,4},{1,5},{2,6},{3,7},{4,0},{5,1},{6,2},{7,3},{8,12},{9,13},{10,... | collective-permute-start | bytes 294920 | tf_op jit(solution)/shard_map/ppermute | solution.py:21
  111.3 2.4 %collective-permute-start.14 = (bf16[96,512]{1,0:T(8,128)(2,1)S(1)}, bf16[96,512]{1,0:T(8,128)(2,1)S(1)}, u32[]{:S(2)}, u32[]{:S(2)}) collective-permute-start(bf16[96,512]{1,0:T(8,128)(2,1)S(1)} %get-tuple-element.34), channel_id=1, source_target_pairs={{0,6},{1,7},{2,4},{3,5},{4,2},{5,3},{6,0},{7,1},{8,14},{9,15},{10,... | collective-permute-start | bytes 294920 | tf_op jit(solution)/shard_map/ppermute | solution.py:21
  113.9 4.7 %collective-permute-done.13 = bf16[96,512]{1,0:T(8,128)(2,1)S(1)} collective-permute-done((bf16[96,512]{1,0:T(8,128)(2,1)S(1)}, bf16[96,512]{1,0:T(8,128)(2,1)S(1)}, u32[]{:S(2)}, u32[]{:S(2)}) %collective-permute-start.13) | collective-permute-done | bytes 98336 | tf_op jit(solution)/shard_map/ppermute | solution.py:21
  118.6 1.0 collective-permute-start.15
  119.6 3.7 %collective-permute-done.15 = bf16[2,96,256]{2,1,0:T(8,128)(2,1)S(1)} collective-permute-done((bf16[2,96,256]{2,1,0:T(8,128)(2,1)S(1)}, bf16[2,96,256]{2,1,0:T(8,128)(2,1)S(1)}, u32[]{:S(2)}, u32[]{:S(2)}) %collective-permute-start.15) | collective-permute-done | bytes 98336 | tf_op jit(solution)/shard_map/ppermute | solution.py:21
  123.5 1.4 %collective-permute-done.16 = bf16[96,1024]{1,0:T(8,128)(2,1)S(1)} collective-permute-done((bf16[96,1024]{1,0:T(8,128)(2,1)S(1)}, bf16[96,1024]{1,0:T(8,128)(2,1)S(1)}, u32[]{:S(2)}, u32[]{:S(2)}) %collective-permute-start.16) | collective-permute-done | bytes 196640 | tf_op jit(solution)/shard_map/ppermute | solution.py:21
  124.9 1.0 select_convert_fusion
  (41 shorter events, 3.4 us)
Async XLA Ops:
  1.6 10.9 %collective-permute-start = (bf16[2,96,512]{2,1,0:T(8,128)(2,1)S(1)}, bf16[2,96,512]{2,1,0:T(8,128)(2,1)S(1)}, u32[]{:S(2)}, u32[]{:S(2)}) collective-permute-start(bf16[2,96,512]{2,1,0:T(8,128)(2,1)S(1)} %pad_maximum_fusion.6), channel_id=1, source_target_pairs={{8,9},{9,8},{10,11},{11,10},{12,13},{13,12},{14,15},{15,14},{24,25... | collective-permute-start | bytes 589832 | tf_op jit(solution)/shard_map/ppermute | solution.py:29
  2.3 10.3 %collective-permute-start.1 = (bf16[2,96,512]{2,1,0:T(8,128)(2,1)S(1)}, bf16[2,96,512]{2,1,0:T(8,128)(2,1)S(1)}, u32[]{:S(2)}, u32[]{:S(2)}) collective-permute-start(bf16[2,96,512]{2,1,0:T(8,128)(2,1)S(1)} %pad_maximum_fusion.6), channel_id=1, source_target_pairs={{0,2},{1,3},{2,0},{3,1},{4,6},{5,7},{6,4},{7,5},{8,11},{9,10},{10,... | collective-permute-start | bytes 589832 | tf_op jit(solution)/shard_map/ppermute | solution.py:29
  5.4 8.2 %collective-permute-start.2 = (bf16[2,96,512]{2,1,0:T(8,128)(2,1)S(1)}, bf16[2,96,512]{2,1,0:T(8,128)(2,1)S(1)}, u32[]{:S(2)}, u32[]{:S(2)}) collective-permute-start(bf16[2,96,512]{2,1,0:T(8,128)(2,1)S(1)} %pad_maximum_fusion.6), channel_id=1, source_target_pairs={{0,4},{1,5},{2,6},{3,7},{4,0},{5,1},{6,2},{7,3},{8,13},{9,12},{10,... | collective-permute-start | bytes 589832 | tf_op jit(solution)/shard_map/ppermute | solution.py:29
  8.0 12.8 %collective-permute-start.3 = (bf16[2,96,512]{2,1,0:T(8,128)(2,1)S(1)}, bf16[2,96,512]{2,1,0:T(8,128)(2,1)S(1)}, u32[]{:S(2)}, u32[]{:S(2)}) collective-permute-start(bf16[2,96,512]{2,1,0:T(8,128)(2,1)S(1)} %pad_maximum_fusion.6), channel_id=1, source_target_pairs={{0,6},{1,7},{2,4},{3,5},{4,2},{5,3},{6,0},{7,1},{8,15},{9,14},{10,... | collective-permute-start | bytes 589832 | tf_op jit(solution)/shard_map/ppermute | solution.py:29
  21.1 18.0 %collective-permute-start.4 = (bf16[2,4,96,512]{3,2,1,0:T(8,128)(2,1)S(1)}, bf16[2,4,96,512]{3,2,1,0:T(8,128)(2,1)S(1)}, u32[]{:S(2)}, u32[]{:S(2)}) collective-permute-start(bf16[2,4,96,512]{3,2,1,0:T(8,128)(2,1)S(1)} %pad_maximum_fusion.3), channel_id=1, source_target_pairs={{0,16},{8,24},{16,0},{24,8},{1,17},{9,25},{17,1},{25,9},{2,18},{10... | collective-permute-start | bytes 2359304 | tf_op jit(solution)/shard_map/ppermute | solution.py:21
  22.7 47.4 %all-to-all-start = ((bf16[8,128,768]{2,1,0:T(8,128)(2,1)}), bf16[8,128,768]{2,1,0:T(8,128)(2,1)}, u32[]{:S(2)}, u32[]{:S(2)}) async-start(bf16[8,128,768]{2,1,0:T(8,128)(2,1)} %bitcast.2), calls=%async_computation | async-start | bytes 3145728 | tf_op jit(solution)/shard_map/all_to_all | solution.py:290
  39.2 3.1 %copy-start = (bf16[1024,768]{1,0:T(8,128)(2,1)S(1)}, bf16[1024,768]{1,0:T(8,128)(2,1)}, u32[]{:S(2)}) copy-start(bf16[1024,768]{1,0:T(8,128)(2,1)} %features_hbm.3) | copy-start | bytes 4718596
  39.4 4.9 %collective-permute-start.5 = (bf16[4,96,1024]{2,1,0:T(8,128)(2,1)S(1)}, bf16[4,96,1024]{2,1,0:T(8,128)(2,1)}, u32[]{:S(2)}, u32[]{:S(2)}) collective-permute-start(bf16[4,96,1024]{2,1,0:T(8,128)(2,1)S(1)} %get-tuple-element.21), channel_id=1, source_target_pairs={{0,8},{8,0},{16,24},{24,16},{1,9},{9,1},{17,25},{25,17},{2,10},{10... | collective-permute-start | bytes 2359304 | tf_op jit(solution)/shard_map/ppermute | solution.py:21
  42.2 4.8 %collective-permute-start.6 = (bf16[4,96,1024]{2,1,0:T(8,128)(2,1)S(1)}, bf16[4,96,1024]{2,1,0:T(8,128)(2,1)}, u32[]{:S(2)}, u32[]{:S(2)}) collective-permute-start(bf16[4,96,1024]{2,1,0:T(8,128)(2,1)S(1)} %get-tuple-element.20), channel_id=1, source_target_pairs={{0,8},{8,0},{16,24},{24,16},{1,9},{9,1},{17,25},{25,17},{2,10},{10... | collective-permute-start | bytes 2359304 | tf_op jit(solution)/shard_map/ppermute | solution.py:21
  83.2 5.1 %collective-permute-start.7 = (bf16[768,1024]{1,0:T(8,128)(2,1)}, bf16[768,1024]{1,0:T(8,128)(2,1)S(1)}, u32[]{:S(2)}, u32[]{:S(2)}) collective-permute-start(bf16[768,1024]{1,0:T(8,128)(2,1)} %get-tuple-element.15), channel_id=1, source_target_pairs={{0,8},{8,0},{16,24},{24,16},{1,9},{9,1},{17,25},{25,17},{2,10},{10... | collective-permute-start | bytes 4718600 | tf_op jit(solution)/shard_map/ppermute | solution.py:21
  90.6 11.4 %collective-permute-start.10 = (bf16[8,96,256]{2,1,0:T(8,128)(2,1)S(1)}, bf16[8,96,256]{2,1,0:T(8,128)(2,1)S(1)}, u32[]{:S(2)}, u32[]{:S(2)}) collective-permute-start(bf16[8,96,256]{2,1,0:T(8,128)(2,1)S(1)} %constant_dynamic-slice_fusion), channel_id=1, source_target_pairs={{0,16},{8,24},{16,0},{24,8},{1,17},{9,25},{17,1},{25,9},{2,18},{10... | collective-permute-start | bytes 1179656 | tf_op jit(solution)/shard_map/ppermute | solution.py:21
  91.2 11.6 %collective-permute-start.8 = (bf16[4,96,512]{2,1,0:T(8,128)(2,1)S(1)}, bf16[4,96,512]{2,1,0:T(8,128)(2,1)S(1)}, u32[]{:S(2)}, u32[]{:S(2)}) collective-permute-start(bf16[4,96,512]{2,1,0:T(8,128)(2,1)S(1)} %dynamic-slice_bitcast_fusion), channel_id=1, source_target_pairs={{0,1},{1,0},{2,3},{3,2},{4,5},{5,4},{6,7},{7,6},{8,9},{9,8},{10,11... | collective-permute-start | bytes 1179656 | tf_op jit(solution)/shard_map/ppermute | solution.py:21
  102.2 6.4 %collective-permute-start.11 = (bf16[4,96,256]{2,1,0:T(8,128)(2,1)S(1)}, bf16[4,96,256]{2,1,0:T(8,128)(2,1)S(1)}, u32[]{:S(2)}, u32[]{:S(2)}) collective-permute-start(bf16[4,96,256]{2,1,0:T(8,128)(2,1)S(1)} %dynamic-slice_bitcast_fusion.1), channel_id=1, source_target_pairs={{0,1},{1,0},{2,3},{3,2},{4,5},{5,4},{6,7},{7,6},{8,9},{9,8},{10,11... | collective-permute-start | bytes 589832 | tf_op jit(solution)/shard_map/ppermute | solution.py:21
  103.0 6.1 %collective-permute-start.9 = (bf16[4,96,256]{2,1,0:T(8,128)(2,1)S(1)}, bf16[4,96,256]{2,1,0:T(8,128)(2,1)S(1)}, u32[]{:S(2)}, u32[]{:S(2)}) collective-permute-start(bf16[4,96,256]{2,1,0:T(8,128)(2,1)S(1)} %constant_dynamic-slice_fusion.1), channel_id=1, source_target_pairs={{0,16},{8,24},{16,0},{24,8},{1,17},{9,25},{17,1},{25,9},{2,18},{10... | collective-permute-start | bytes 589832 | tf_op jit(solution)/shard_map/ppermute | solution.py:21
  109.2 4.7 %collective-permute-start.12 = (bf16[96,512]{1,0:T(8,128)(2,1)S(1)}, bf16[96,512]{1,0:T(8,128)(2,1)S(1)}, u32[]{:S(2)}, u32[]{:S(2)}) collective-permute-start(bf16[96,512]{1,0:T(8,128)(2,1)S(1)} %get-tuple-element.32), channel_id=1, source_target_pairs={{0,2},{1,3},{2,0},{3,1},{4,6},{5,7},{6,4},{7,5},{8,10},{9,11},{10,... | collective-permute-start | bytes 294920 | tf_op jit(solution)/shard_map/ppermute | solution.py:21
  109.3 9.3 %collective-permute-start.13 = (bf16[96,512]{1,0:T(8,128)(2,1)S(1)}, bf16[96,512]{1,0:T(8,128)(2,1)S(1)}, u32[]{:S(2)}, u32[]{:S(2)}) collective-permute-start(bf16[96,512]{1,0:T(8,128)(2,1)S(1)} %get-tuple-element.33), channel_id=1, source_target_pairs={{0,4},{1,5},{2,6},{3,7},{4,0},{5,1},{6,2},{7,3},{8,12},{9,13},{10,... | collective-permute-start | bytes 294920 | tf_op jit(solution)/shard_map/ppermute | solution.py:21
  111.3 7.2 %collective-permute-start.14 = (bf16[96,512]{1,0:T(8,128)(2,1)S(1)}, bf16[96,512]{1,0:T(8,128)(2,1)S(1)}, u32[]{:S(2)}, u32[]{:S(2)}) collective-permute-start(bf16[96,512]{1,0:T(8,128)(2,1)S(1)} %get-tuple-element.34), channel_id=1, source_target_pairs={{0,6},{1,7},{2,4},{3,5},{4,2},{5,3},{6,0},{7,1},{8,14},{9,15},{10,... | collective-permute-start | bytes 294920 | tf_op jit(solution)/shard_map/ppermute | solution.py:21
  118.6 4.7 %collective-permute-start.15 = (bf16[2,96,256]{2,1,0:T(8,128)(2,1)S(1)}, bf16[2,96,256]{2,1,0:T(8,128)(2,1)S(1)}, u32[]{:S(2)}, u32[]{:S(2)}) collective-permute-start(bf16[2,96,256]{2,1,0:T(8,128)(2,1)S(1)} %pad_maximum_fusion.9), channel_id=1, source_target_pairs={{0,16},{8,24},{16,0},{24,8},{1,17},{9,25},{17,1},{25,9},{2,18},{10... | collective-permute-start | bytes 294920 | tf_op jit(solution)/shard_map/ppermute | solution.py:21
  123.4 1.5 %collective-permute-start.16 = (bf16[96,1024]{1,0:T(8,128)(2,1)S(1)}, bf16[96,1024]{1,0:T(8,128)(2,1)S(1)}, u32[]{:S(2)}, u32[]{:S(2)}) collective-permute-start(bf16[96,1024]{1,0:T(8,128)(2,1)S(1)} %pad_maximum_fusion.7), channel_id=1, source_target_pairs={{0,8},{8,0},{16,24},{24,16},{1,9},{9,1},{17,25},{25,17},{2,10},{10... | collective-permute-start | bytes 589832 | tf_op jit(solution)/shard_map/ppermute | solution.py:21

commit v9 on v8

--- a/solution.py
+++ b/solution.py
@@ -1,3 +1,5 @@
+import functools
+
 import jax
 import jax.numpy as jnp
 from jax import lax
@@ -77,48 +79,44 @@
 
 
 def layer_kernel(
+    sources,
     core_ref,
+    flip_ref,
     into_ref,
     slots_hbm,
     features_hbm,
     turned_hbm,
     cotangent_hbm,
-    w_self_hbm,
-    w_neigh_hbm,
-    aggregate_hbm,
-    grad_hbm,
-    sent_hbm,
-    slots,
-    features,
-    left,
-    cotangent,
-    w_self,
-    w_neigh,
-    summed,
-    values,
-    aggregate,
-    grad,
-    sent,
-    slot_sems,
-    row_sems,
-    weight_sems,
-    out_sems,
+    *refs,
 ):
+    self_hbms, neigh_hbms, refs = refs[:sources], refs[sources : 2 * sources], refs[2 * sources :]
+    aggregate_hbm, grad_hbm, sent_hbm, slots, features, left, cotangent, w_self, w_neigh, summed = refs[:10]
+    values, aggregate, grad, sent, slot_sems, row_sems, weight_sems, out_sems = refs[10:]
     senders, block, _ = slots.shape
     rows, hidden = grad.shape
+    width = features.shape[1]
     core = core_ref[0]
     arrivals = [
         pltpu.make_async_copy(slots_hbm.at[sender], slots.at[sender], slot_sems.at[sender]) for sender in range(senders)
     ]
     chunk = 256
     parts = rows // chunk
-    weight_copies = split_copies(w_self_hbm, w_self, weight_sems.at[0])
-    weight_copies += split_copies(w_neigh_hbm, w_neigh, weight_sems.at[1])
+    flip = flip_ref[0]
+    weight_copies = []
+    for index, (weight_hbms, weight) in enumerate([(self_hbms, w_self), (neigh_hbms, w_neigh)]):
+        for source, weight_hbm in enumerate(weight_hbms):
+            for piece in range(weight_hbm.shape[0]):
+                target = piece if sources == 1 else 2 * piece + (flip ^ source)
+                weight_copies.append(
+                    pltpu.make_async_copy(
+                        weight_hbm.at[piece], weight.at[target], weight_sems.at[index, sources * piece + source]
+                    )
+                )
     feature_copies = split_copies(features_hbm, features, row_sems.at[0], parts)
     cotangent_copies = split_copies(cotangent_hbm, cotangent, row_sems.at[1], parts)
     for copy in arrivals + weight_copies + feature_copies + cotangent_copies:
         copy.start()
-    turning = pltpu.make_async_copy(turned_hbm, left, weight_sems.at[2, 0])
+    turning = pltpu.make_async_copy(turned_hbm, left, row_sems.at[2, 0])
     pl.when(core != 0)(turning.start)
 
     summed[...] = jnp.zeros_like(summed)
@@ -127,7 +125,7 @@
         at = pl.ds(pl.multiple_of(into_ref[sender] * block, block), block)
         summed[at, :] = summed[at, :] + slots[sender].astype(F32)
     aggregate[...] = summed[...].astype(BF16)
-    results = [pltpu.make_async_copy(aggregate, aggregate_hbm, weight_sems.at[2, 1])]
+    results = [pltpu.make_async_copy(aggregate, aggregate_hbm, row_sems.at[2, 1])]
     results[0].start()
 
     @pl.when(core == 0)
@@ -144,8 +142,10 @@
         for first in range(0, hidden, span):
             columns = slice(first, first + span)
             values[index % 2, :, columns] = jnp.dot(
-                features[at, :], w_self[:, columns], preferred_element_type=F32
-            ) + jnp.dot(aggregate[at, :], w_neigh[:, columns], preferred_element_type=F32)
+                features[at, :], w_self[:, :, columns].reshape(width, span), preferred_element_type=F32
+            ) + jnp.dot(
+                aggregate[at, :], w_neigh[:, :, columns].reshape(width, span), preferred_element_type=F32
+            )
 
     multiply(0)
     for index in range(parts):
@@ -299,41 +299,42 @@
         ]
         bit *= 2
     mine = gather_high(pieces[0], high)
-    weights = [
-        joined(mine[index], swap(mine[index], "rep", 1), (low ^ core) != 0, 1).reshape(width, hidden)
-        for index in range(2)
-    ]
+    flip = low ^ core
+    weights = [[mine[index], swap(mine[index], "rep", 1)] for index in range(2)]
+    if (width // dom_size) % 16:
+        weights = [[joined(*weight, flip != 0, 1).reshape(-1, 128, hidden)] for weight in weights]
+    sources, pieces = len(weights[0]), sum(weight.shape[0] for weight in weights[0])
     turned = features.T
 
     aggregate, grad, sent = call(
-        layer_kernel,
+        functools.partial(layer_kernel, sources),
         [
             jax.ShapeDtypeStruct((rows, width), BF16),
             jax.ShapeDtypeStruct((rows, hidden), BF16),
             jax.ShapeDtypeStruct((width, hidden), BF16),
         ],
-        [SMEM, SMEM] + [HBM] * 6,
+        [SMEM] * 3 + [HBM] * (4 + 2 * sources),
         [HBM] * 3,
         [
             pltpu.VMEM((dom_size, block, width), BF16),
             pltpu.VMEM((rows, width), BF16),
             pltpu.VMEM((width, rows), BF16),
             pltpu.VMEM((rows, hidden), BF16),
-            pltpu.VMEM((width, hidden), BF16),
-            pltpu.VMEM((width, hidden), BF16),
+            pltpu.VMEM((pieces, width // pieces, hidden), BF16),
+            pltpu.VMEM((pieces, width // pieces, hidden), BF16),
             pltpu.VMEM((rows, width), F32),
             pltpu.VMEM((2, 256, hidden), F32),
             pltpu.VMEM((rows, width), BF16),
             pltpu.VMEM((rows, hidden), BF16),
             pltpu.VMEM((width, hidden), BF16),
             DMA((dom_size,)),
-            DMA((2, rows // 256)),
-            DMA((3, 4)),
+            DMA((3, rows // 256)),
+            DMA((2, pieces)),
             DMA((2, rows // 256)),
         ],
         flops=6 * rows * width * hidden,
         moved=16 * rows * hidden,
-    )(core_arg, in_block, received, features, turned, cotangent, *weights)
+    )(core_arg, flip.astype(jnp.int32).reshape(1), in_block, received, features, turned, cotangent, *weights[0], *weights[1])
     arrived = swap(sent, "rep", 1)
     kept = call(
         kept_kernel,

time: 126 us -> 120 us (0.952)
  waiting for transfers between devices: 61.8 us -> 56 us
  other arithmetic: 7.99 us -> 6.39 us
    ppermute x13, waiting for transfers between devices: 33 us -> 42.3 us  [swap(): lax.ppermute(value, axis, [(index, index ^ step) for index in range(size)])]
    all_to_all x1, waiting for transfers between devices: 20.5 us -> 11.4 us  [shards(): lax.all_to_all(slots.reshape(dom_size, block, width), 'dom', split_axis=0...]
    ppermute x4, waiting for transfers between devices: 8.24 us -> 2.2 us  [cross(): lax.ppermute(value, ('rep', 'dom'), [(source, target) for source, target...]
    another operation x4 -> x0, other arithmetic: 3.92 us -> none  [joined(): jnp.stack([jnp.where(upper, other, held), jnp.where(upper, held, other)],...]
    ppermute x13, starting transfers between devices: 13.1 us -> 16.8 us  [swap(): lax.ppermute(value, axis, [(index, index ^ step) for index in range(size)])]
    all_to_all x1, starting transfers between devices: 8.75 us -> 6.04 us  [shards(): lax.all_to_all(slots.reshape(dom_size, block, width), 'dom', split_axis=0...]
    another operation x1 -> x0, local copies, waits for them, and re-layouts: 1.36 us -> none  [joined(): jnp.stack([jnp.where(upper, other, held), jnp.where(upper, held, other)],...]
    unnamed x3 -> x5, local copies, waits for them, and re-layouts: 1.63 us -> 2.89 us
  transfers between devices with their start and end apart: 18 -> 18, of which waited for: 12 -> 13; matrix products, arithmetic and copies ran while one was open for 6% -> 4% of each run, Pallas kernels for 8% -> 8%
where the time goes in v9:
time: 120 us; the launch traced here: 119 us
  waiting for transfers between devices  56 us (47%)
  starting transfers between devices  29.2 us (24%)
  Pallas kernels  22.8 us (19%)
  other arithmetic  6.39 us (5%)
  local copies, waits for them, and re-layouts  4.14 us (3%)
    ppermute x13, waiting for transfers between devices, swap(): lax.ppermute(value, axis, [(index, index ^ step) for index in range(size)])  42.3 us
    ppermute x13, starting transfers between devices, swap(): lax.ppermute(value, axis, [(index, index ^ step) for index in range(size)])  16.8 us
    pallas_call x1, Pallas kernels, shards(): call(functools.partial(layer_kernel, sources), [jax.ShapeDtypeStruct((row...  13.4 us
    all_to_all x1, waiting for transfers between devices, shards(): lax.all_to_all(slots.reshape(dom_size, block, width), 'dom', split_axis=0...  11.4 us
    ppermute x4, starting transfers between devices, cross(): lax.ppermute(value, ('rep', 'dom'), [(source, target) for source, target...  6.35 us
    all_to_all x1, starting transfers between devices, shards(): lax.all_to_all(slots.reshape(dom_size, block, width), 'dom', split_axis=0...  6.04 us
    pallas_call x1, Pallas kernels, shards(): call(kept_kernel, jax.ShapeDtypeStruct((width, hidden), BF16), [SMEM] + [...  4.87 us
    pallas_call x1, Pallas kernels, shards(): call(slots_kernel, jax.ShapeDtypeStruct((dom_size * block, width), BF16),...  4.58 us
  transfers between devices with their start and end apart: 18, of which 13 were waited for; matrix products, arithmetic and copies ran while one was open for 4% of the time, Pallas kernels for 8%

profile of v9, /device:TPU:0, one launch (start us, length us, event | category | flops | bytes accessed | tf_op | source)
XLA Modules:
  0.0 119.4 jit_solution(2413680974845594535)
XLA Ops:
  0.6 1.0 dynamic-slice_bitcast_fusion.2
  2.3 3.1 %collective-permute-start.1 = (bf16[2,96,512]{2,1,0:T(8,128)(2,1)S(1)}, bf16[2,96,512]{2,1,0:T(8,128)(2,1)S(1)}, u32[]{:S(2)}, u32[]{:S(2)}) collective-permute-start(bf16[2,96,512]{2,1,0:T(8,128)(2,1)S(1)} %pad_maximum_fusion.4), channel_id=1, source_target_pairs={{0,2},{1,3},{2,0},{3,1},{4,6},{5,7},{6,4},{7,5},{8,11},{9,10},{10,... | collective-permute-start | bytes 589832 | tf_op jit(solution)/shard_map/ppermute | solution.py:31
  5.4 2.6 %collective-permute-start.2 = (bf16[2,96,512]{2,1,0:T(8,128)(2,1)S(1)}, bf16[2,96,512]{2,1,0:T(8,128)(2,1)S(1)}, u32[]{:S(2)}, u32[]{:S(2)}) collective-permute-start(bf16[2,96,512]{2,1,0:T(8,128)(2,1)S(1)} %pad_maximum_fusion.4), channel_id=1, source_target_pairs={{0,4},{1,5},{2,6},{3,7},{4,0},{5,1},{6,2},{7,3},{8,13},{9,12},{10,... | collective-permute-start | bytes 589832 | tf_op jit(solution)/shard_map/ppermute | solution.py:31
  8.0 4.6 %shard_map.95 = bf16[1024,768]{1,0:T(8,128)(2,1)} custom-call(s32[32]{0:T(128)} %src_hbm.1, s32[32]{0:T(128)} %peer_hbm.1, bf16[32,128,128]{2,1,0:T(8,128)(2,1)} %tiles_hbm.1, bf16[1024,768]{1,0:T(8,128)(2,1)} %features_hbm.3), custom_call_target="tpu_custom_call" | custom-call | flops 1610612736 | bytes 4194304 | tf_op jit(solution)/shard_map/pallas_call | solution.py:271
  12.6 6.0 %all-to-all-start = ((bf16[8,128,768]{2,1,0:T(8,128)(2,1)}), bf16[8,128,768]{2,1,0:T(8,128)(2,1)S(1)}, u32[]{:S(2)}, u32[]{:S(2)}) async-start(bf16[8,128,768]{2,1,0:T(8,128)(2,1)} %bitcast.65), calls=%async_computation | async-start | bytes 3145728 | tf_op jit(solution)/shard_map/all_to_all | solution.py:290
  18.6 2.2 %collective-permute-done.3 = bf16[2,96,512]{2,1,0:T(8,128)(2,1)S(1)} collective-permute-done((bf16[2,96,512]{2,1,0:T(8,128)(2,1)S(1)}, bf16[2,96,512]{2,1,0:T(8,128)(2,1)S(1)}, u32[]{:S(2)}, u32[]{:S(2)}) %collective-permute-start.3) | collective-permute-done | bytes 196640 | tf_op jit(solution)/shard_map/ppermute | solution.py:31
  21.1 1.6 %collective-permute-start.4 = (bf16[2,4,96,512]{3,2,1,0:T(8,128)(2,1)S(1)}, bf16[2,4,96,512]{3,2,1,0:T(8,128)(2,1)}, u32[]{:S(2)}, u32[]{:S(2)}) collective-permute-start(bf16[2,4,96,512]{3,2,1,0:T(8,128)(2,1)S(1)} %pad_maximum_fusion.1), channel_id=1, source_target_pairs={{0,16},{8,24},{16,0},{24,8},{1,17},{9,25},{17,1},{25,9},{2,18},{10... | collective-permute-start | bytes 2359304 | tf_op jit(solution)/shard_map/ppermute | solution.py:23
  22.7 16.5 %collective-permute-done.4 = bf16[2,4,96,512]{3,2,1,0:T(8,128)(2,1)} collective-permute-done((bf16[2,4,96,512]{3,2,1,0:T(8,128)(2,1)S(1)}, bf16[2,4,96,512]{3,2,1,0:T(8,128)(2,1)}, u32[]{:S(2)}, u32[]{:S(2)}) %collective-permute-start.4) | collective-permute-done | bytes 786464 | tf_op jit(solution)/shard_map/ppermute | solution.py:23
  39.1 1.2 %broadcast_select_fusion = (bf16[2,4,96,512]{3,2,1,0:T(8,128)(2,1)S(1)}, bf16[2,4,96,512]{3,2,1,0:T(8,128)(2,1)S(1)}) fusion(bf16[2,4,96,512]{3,2,1,0:T(8,128)(2,1)} %collective-permute-done.4, pred[]{:T(512)S(6)} %ne.24, bf16[2,2,96,512]{3,2,1,0:T(8,128)(2,1)S(1)} %get-tuple-element.23, bf16[2,2,96,512]{3,2,1,0:T(8,128)(2,1)S(1)} %get-tuple-element.22), kind=kLoop, calls=%fused_computation.11 | loop fusion | flops 1179648 | bytes 3145729 | tf_op jit(solution)/shard_map/jit(_where)/select_n | solution.py:226
  40.4 1.4 %fusion.2 = (bf16[4,96,1024]{2,1,0:T(8,128)(2,1)}, bf16[4,96,1024]{2,1,0:T(8,128)(2,1)}) fusion(bf16[2,4,96,512]{3,2,1,0:T(8,128)(2,1)S(1)} %get-tuple-element.20, bf16[2,4,96,512]{3,2,1,0:T(8,128)(2,1)S(1)} %get-tuple-element.21), kind=kLoop, calls=%fused_computation.6 | loop fusion | flops 3145728 | bytes 3145728 | tf_op jit(solution)/shard_map/squeeze | solution.py:303
  41.8 2.5 %collective-permute-start.5 = (bf16[4,96,1024]{2,1,0:T(8,128)(2,1)}, bf16[4,96,1024]{2,1,0:T(8,128)(2,1)}, u32[]{:S(2)}, u32[]{:S(2)}) collective-permute-start(bf16[4,96,1024]{2,1,0:T(8,128)(2,1)} %get-tuple-element.19.refs_0_), channel_id=1, source_target_pairs={{0,8},{8,0},{16,24},{24,16},{1,9},{9,1},{17,25},{25,17},{2,10},{10... | collective-permute-start | bytes 2359304 | tf_op jit(solution)/shard_map/ppermute | solution.py:23
  44.3 1.6 %copy.14 = bf16[1024,768]{0,1:T(8,128)(2,1)} copy(bf16[1024,768]{1,0:T(8,128)(2,1)S(1)} %copy-done) | data formatting | bytes 3145728 | tf_op args[0]
  46.6 1.1 collective-permute-done.6.refs_3_
  47.7 11.4 %all-to-all-done.slots_hbm = bf16[8,128,768]{2,1,0:T(8,128)(2,1)S(1)} async-done(((bf16[8,128,768]{2,1,0:T(8,128)(2,1)}), bf16[8,128,768]{2,1,0:T(8,128)(2,1)S(1)}, u32[]{:S(2)}, u32[]{:S(2)}) %all-to-all-start) | async-done | bytes 1572896 | tf_op jit(solution)/shard_map/all_to_all | solution.py:290
  59.1 1.2 %copy-done.1 = bf16[8,128,768]{2,1,0:T(8,128)(2,1)} copy-done((bf16[8,128,768]{2,1,0:T(8,128)(2,1)}, bf16[8,128,768]{2,1,0:T(8,128)(2,1)S(1)}, u32[]{:S(2)}) %copy-start.1) | copy-done | bytes 1572888
  60.4 13.4 %shard_map.96 = (bf16[1024,768]{1,0:T(8,128)(2,1)}, bf16[1024,1024]{1,0:T(8,128)(2,1)}, bf16[768,1024]{1,0:T(8,128)(2,1)}) custom-call(s32[1]{0:T(128)} %bitcast.core_ref, s32[1]{0:T(128)} %bitcast.2.flip_ref, s32[8]{0:T(128)} %into_ref.1, bf16[8,128,768]{2,1,0:T(8,128)(2,1)} %copy-done.1, bf16[1024,768]{1,0:T(8,128)(2,1)} %features_hbm.3, ...), custom_call_target="tpu_custom_call" | custom-call | flops 4831838208 | bytes 16777216 | tf_op jit(solution)/shard_map/pallas_call | solution.py:309
  73.8 1.8 %collective-permute-start.7 = (bf16[768,1024]{1,0:T(8,128)(2,1)}, bf16[768,1024]{1,0:T(8,128)(2,1)S(1)}, u32[]{:S(2)}, u32[]{:S(2)}) collective-permute-start(bf16[768,1024]{1,0:T(8,128)(2,1)} %get-tuple-element.15), channel_id=1, source_target_pairs={{0,8},{8,0},{16,24},{24,16},{1,9},{9,1},{17,25},{25,17},{2,10},{10... | collective-permute-start | bytes 4718600 | tf_op jit(solution)/shard_map/ppermute | solution.py:23
  75.5 4.9 %shard_map.97 = bf16[768,1024]{1,0:T(8,128)(2,1)} custom-call(s32[1]{0:T(128)} %bitcast.core_ref, bf16[768,1024]{1,0:T(8,128)(2,1)} %bitcast.61, bf16[1024,768]{1,0:T(8,128)(2,1)} %get-tuple-element.13.aggregate_hbm, bf16[1024,1024]{1,0:T(8,128)(2,1)} %get-tuple-element.14.grad_hbm), custom_call_target="tpu_custom_call" | custom-call | flops 1610612736 | bytes 6291456 | tf_op jit(solution)/shard_map/pallas_call | solution.py:339
  80.4 2.1 %add_convert_fusion = bf16[768,1024]{1,0:T(8,128)(2,1)S(1)} fusion(bf16[768,1024]{1,0:T(8,128)(2,1)S(1)} %collective-permute-done.7, bf16[768,1024]{1,0:T(8,128)(2,1)} %shard_map.97), kind=kLoop, calls=%fused_computation | loop fusion | flops 3145728 | bytes 4718592 | tf_op jit(solution)/shard_map/convert_element_type | solution.py:232
  82.7 1.6 %collective-permute-start.10 = (bf16[8,96,256]{2,1,0:T(8,128)(2,1)S(1)}, bf16[8,96,256]{2,1,0:T(8,128)(2,1)S(1)}, u32[]{:S(2)}, u32[]{:S(2)}) collective-permute-start(bf16[8,96,256]{2,1,0:T(8,128)(2,1)S(1)} %constant_dynamic-slice_fusion), channel_id=1, source_target_pairs={{0,16},{8,24},{16,0},{24,8},{1,17},{9,25},{17,1},{25,9},{2,18},{10... | collective-permute-start | bytes 1179656 | tf_op jit(solution)/shard_map/ppermute | solution.py:23
  85.3 8.8 %collective-permute-done.10 = bf16[8,96,256]{2,1,0:T(8,128)(2,1)S(1)} collective-permute-done((bf16[8,96,256]{2,1,0:T(8,128)(2,1)S(1)}, bf16[8,96,256]{2,1,0:T(8,128)(2,1)S(1)}, u32[]{:S(2)}, u32[]{:S(2)}) %collective-permute-start.10) | collective-permute-done | bytes 393248 | tf_op jit(solution)/shard_map/ppermute | solution.py:23
  94.2 0.9 collective-permute-start.11
  95.6 1.3 %collective-permute-start.9 = (bf16[4,96,256]{2,1,0:T(8,128)(2,1)S(1)}, bf16[4,96,256]{2,1,0:T(8,128)(2,1)S(1)}, u32[]{:S(2)}, u32[]{:S(2)}) collective-permute-start(bf16[4,96,256]{2,1,0:T(8,128)(2,1)S(1)} %constant_dynamic-slice_fusion.1), channel_id=1, source_target_pairs={{0,16},{8,24},{16,0},{24,8},{1,17},{9,25},{17,1},{25,9},{2,18},{10... | collective-permute-start | bytes 589832 | tf_op jit(solution)/shard_map/ppermute | solution.py:23
  96.9 3.6 %collective-permute-done.11 = bf16[4,96,256]{2,1,0:T(8,128)(2,1)S(1)} collective-permute-done((bf16[4,96,256]{2,1,0:T(8,128)(2,1)S(1)}, bf16[4,96,256]{2,1,0:T(8,128)(2,1)S(1)}, u32[]{:S(2)}, u32[]{:S(2)}) %collective-permute-start.11) | collective-permute-done | bytes 196640 | tf_op jit(solution)/shard_map/ppermute | solution.py:23
  100.6 1.0 collective-permute-done.9
  102.0 2.5 %collective-permute-start.13 = (bf16[96,512]{1,0:T(8,128)(2,1)S(1)}, bf16[96,512]{1,0:T(8,128)(2,1)S(1)}, u32[]{:S(2)}, u32[]{:S(2)}) collective-permute-start(bf16[96,512]{1,0:T(8,128)(2,1)S(1)} %get-tuple-element.29), channel_id=1, source_target_pairs={{0,4},{1,5},{2,6},{3,7},{4,0},{5,1},{6,2},{7,3},{8,12},{9,13},{10,... | collective-permute-start | bytes 294920 | tf_op jit(solution)/shard_map/ppermute | solution.py:23
  104.6 1.5 %collective-permute-start.14 = (bf16[96,512]{1,0:T(8,128)(2,1)S(1)}, bf16[96,512]{1,0:T(8,128)(2,1)S(1)}, u32[]{:S(2)}, u32[]{:S(2)}) collective-permute-start(bf16[96,512]{1,0:T(8,128)(2,1)S(1)} %get-tuple-element.30), channel_id=1, source_target_pairs={{0,6},{1,7},{2,4},{3,5},{4,2},{5,3},{6,0},{7,1},{8,14},{9,15},{10,... | collective-permute-start | bytes 294920 | tf_op jit(solution)/shard_map/ppermute | solution.py:23
  106.3 5.7 %collective-permute-done.13 = bf16[96,512]{1,0:T(8,128)(2,1)S(1)} collective-permute-done((bf16[96,512]{1,0:T(8,128)(2,1)S(1)}, bf16[96,512]{1,0:T(8,128)(2,1)S(1)}, u32[]{:S(2)}, u32[]{:S(2)}) %collective-permute-start.13) | collective-permute-done | bytes 98336 | tf_op jit(solution)/shard_map/ppermute | solution.py:23
  112.2 1.5 %collective-permute-start.15 = (bf16[2,96,256]{2,1,0:T(8,128)(2,1)S(1)}, bf16[2,96,256]{2,1,0:T(8,128)(2,1)S(1)}, u32[]{:S(2)}, u32[]{:S(2)}) collective-permute-start(bf16[2,96,256]{2,1,0:T(8,128)(2,1)S(1)} %pad_maximum_fusion.7), channel_id=1, source_target_pairs={{0,16},{8,24},{16,0},{24,8},{1,17},{9,25},{17,1},{25,9},{2,18},{10... | collective-permute-start | bytes 294920 | tf_op jit(solution)/shard_map/ppermute | solution.py:23
  113.7 3.1 %collective-permute-done.15 = bf16[2,96,256]{2,1,0:T(8,128)(2,1)S(1)} collective-permute-done((bf16[2,96,256]{2,1,0:T(8,128)(2,1)S(1)}, bf16[2,96,256]{2,1,0:T(8,128)(2,1)S(1)}, u32[]{:S(2)}, u32[]{:S(2)}) %collective-permute-start.15) | collective-permute-done | bytes 98336 | tf_op jit(solution)/shard_map/ppermute | solution.py:23
  117.0 1.4 %collective-permute-done.16 = bf16[96,1024]{1,0:T(8,128)(2,1)S(1)} collective-permute-done((bf16[96,1024]{1,0:T(8,128)(2,1)S(1)}, bf16[96,1024]{1,0:T(8,128)(2,1)S(1)}, u32[]{:S(2)}, u32[]{:S(2)}) %collective-permute-start.16) | collective-permute-done | bytes 196640 | tf_op jit(solution)/shard_map/ppermute | solution.py:23
  118.4 1.0 select_convert_fusion
  (38 shorter events, 4.2 us)
Async XLA Ops:
  1.6 17.0 %collective-permute-start = (bf16[2,96,512]{2,1,0:T(8,128)(2,1)S(1)}, bf16[2,96,512]{2,1,0:T(8,128)(2,1)S(1)}, u32[]{:S(2)}, u32[]{:S(2)}) collective-permute-start(bf16[2,96,512]{2,1,0:T(8,128)(2,1)S(1)} %pad_maximum_fusion.4), channel_id=1, source_target_pairs={{8,9},{9,8},{10,11},{11,10},{12,13},{13,12},{14,15},{15,14},{24,25... | collective-permute-start | bytes 589832 | tf_op jit(solution)/shard_map/ppermute | solution.py:31
  2.3 16.3 %collective-permute-start.1 = (bf16[2,96,512]{2,1,0:T(8,128)(2,1)S(1)}, bf16[2,96,512]{2,1,0:T(8,128)(2,1)S(1)}, u32[]{:S(2)}, u32[]{:S(2)}) collective-permute-start(bf16[2,96,512]{2,1,0:T(8,128)(2,1)S(1)} %pad_maximum_fusion.4), channel_id=1, source_target_pairs={{0,2},{1,3},{2,0},{3,1},{4,6},{5,7},{6,4},{7,5},{8,11},{9,10},{10,... | collective-permute-start | bytes 589832 | tf_op jit(solution)/shard_map/ppermute | solution.py:31
  5.4 13.2 %collective-permute-start.2 = (bf16[2,96,512]{2,1,0:T(8,128)(2,1)S(1)}, bf16[2,96,512]{2,1,0:T(8,128)(2,1)S(1)}, u32[]{:S(2)}, u32[]{:S(2)}) collective-permute-start(bf16[2,96,512]{2,1,0:T(8,128)(2,1)S(1)} %pad_maximum_fusion.4), channel_id=1, source_target_pairs={{0,4},{1,5},{2,6},{3,7},{4,0},{5,1},{6,2},{7,3},{8,13},{9,12},{10,... | collective-permute-start | bytes 589832 | tf_op jit(solution)/shard_map/ppermute | solution.py:31
  8.0 12.8 %collective-permute-start.3 = (bf16[2,96,512]{2,1,0:T(8,128)(2,1)S(1)}, bf16[2,96,512]{2,1,0:T(8,128)(2,1)S(1)}, u32[]{:S(2)}, u32[]{:S(2)}) collective-permute-start(bf16[2,96,512]{2,1,0:T(8,128)(2,1)S(1)} %pad_maximum_fusion.4), channel_id=1, source_target_pairs={{0,6},{1,7},{2,4},{3,5},{4,2},{5,3},{6,0},{7,1},{8,15},{9,14},{10,... | collective-permute-start | bytes 589832 | tf_op jit(solution)/shard_map/ppermute | solution.py:31
  12.6 46.5 %all-to-all-start = ((bf16[8,128,768]{2,1,0:T(8,128)(2,1)}), bf16[8,128,768]{2,1,0:T(8,128)(2,1)S(1)}, u32[]{:S(2)}, u32[]{:S(2)}) async-start(bf16[8,128,768]{2,1,0:T(8,128)(2,1)} %bitcast.65), calls=%async_computation | async-start | bytes 3145728 | tf_op jit(solution)/shard_map/all_to_all | solution.py:290
  21.1 18.1 %collective-permute-start.4 = (bf16[2,4,96,512]{3,2,1,0:T(8,128)(2,1)S(1)}, bf16[2,4,96,512]{3,2,1,0:T(8,128)(2,1)}, u32[]{:S(2)}, u32[]{:S(2)}) collective-permute-start(bf16[2,4,96,512]{3,2,1,0:T(8,128)(2,1)S(1)} %pad_maximum_fusion.1), channel_id=1, source_target_pairs={{0,16},{8,24},{16,0},{24,8},{1,17},{9,25},{17,1},{25,9},{2,18},{10... | collective-permute-start | bytes 2359304 | tf_op jit(solution)/shard_map/ppermute | solution.py:23
  40.4 3.9 %copy-start = (bf16[1024,768]{1,0:T(8,128)(2,1)S(1)}, bf16[1024,768]{1,0:T(8,128)(2,1)}, u32[]{:S(2)}) copy-start(bf16[1024,768]{1,0:T(8,128)(2,1)} %features_hbm.3) | copy-start | bytes 4718596
  41.8 4.8 %collective-permute-start.5 = (bf16[4,96,1024]{2,1,0:T(8,128)(2,1)}, bf16[4,96,1024]{2,1,0:T(8,128)(2,1)}, u32[]{:S(2)}, u32[]{:S(2)}) collective-permute-start(bf16[4,96,1024]{2,1,0:T(8,128)(2,1)} %get-tuple-element.19.refs_0_), channel_id=1, source_target_pairs={{0,8},{8,0},{16,24},{24,16},{1,9},{9,1},{17,25},{25,17},{2,10},{10... | collective-permute-start | bytes 2359304 | tf_op jit(solution)/shard_map/ppermute | solution.py:23
  44.3 3.4 %collective-permute-start.6 = (bf16[4,96,1024]{2,1,0:T(8,128)(2,1)}, bf16[4,96,1024]{2,1,0:T(8,128)(2,1)}, u32[]{:S(2)}, u32[]{:S(2)}) collective-permute-start(bf16[4,96,1024]{2,1,0:T(8,128)(2,1)} %get-tuple-element.18.refs_2_), channel_id=1, source_target_pairs={{0,8},{8,0},{16,24},{24,16},{1,9},{9,1},{17,25},{25,17},{2,10},{10... | collective-permute-start | bytes 2359304 | tf_op jit(solution)/shard_map/ppermute | solution.py:23
  59.1 1.2 %copy-start.1 = (bf16[8,128,768]{2,1,0:T(8,128)(2,1)}, bf16[8,128,768]{2,1,0:T(8,128)(2,1)S(1)}, u32[]{:S(2)}) copy-start(bf16[8,128,768]{2,1,0:T(8,128)(2,1)S(1)} %all-to-all-done.slots_hbm) | copy-start | bytes 4718596
  73.8 6.6 %collective-permute-start.7 = (bf16[768,1024]{1,0:T(8,128)(2,1)}, bf16[768,1024]{1,0:T(8,128)(2,1)S(1)}, u32[]{:S(2)}, u32[]{:S(2)}) collective-permute-start(bf16[768,1024]{1,0:T(8,128)(2,1)} %get-tuple-element.15), channel_id=1, source_target_pairs={{0,8},{8,0},{16,24},{24,16},{1,9},{9,1},{17,25},{25,17},{2,10},{10... | collective-permute-start | bytes 4718600 | tf_op jit(solution)/shard_map/ppermute | solution.py:23
  82.7 11.3 %collective-permute-start.10 = (bf16[8,96,256]{2,1,0:T(8,128)(2,1)S(1)}, bf16[8,96,256]{2,1,0:T(8,128)(2,1)S(1)}, u32[]{:S(2)}, u32[]{:S(2)}) collective-permute-start(bf16[8,96,256]{2,1,0:T(8,128)(2,1)S(1)} %constant_dynamic-slice_fusion), channel_id=1, source_target_pairs={{0,16},{8,24},{16,0},{24,8},{1,17},{9,25},{17,1},{25,9},{2,18},{10... | collective-permute-start | bytes 1179656 | tf_op jit(solution)/shard_map/ppermute | solution.py:23
  84.4 11.1 %collective-permute-start.8 = (bf16[4,96,512]{2,1,0:T(8,128)(2,1)S(1)}, bf16[4,96,512]{2,1,0:T(8,128)(2,1)S(1)}, u32[]{:S(2)}, u32[]{:S(2)}) collective-permute-start(bf16[4,96,512]{2,1,0:T(8,128)(2,1)S(1)} %dynamic-slice_bitcast_fusion), channel_id=1, source_target_pairs={{0,1},{1,0},{2,3},{3,2},{4,5},{5,4},{6,7},{7,6},{8,9},{9,8},{10,11... | collective-permute-start | bytes 1179656 | tf_op jit(solution)/shard_map/ppermute | solution.py:23
  94.2 6.3 %collective-permute-start.11 = (bf16[4,96,256]{2,1,0:T(8,128)(2,1)S(1)}, bf16[4,96,256]{2,1,0:T(8,128)(2,1)S(1)}, u32[]{:S(2)}, u32[]{:S(2)}) collective-permute-start(bf16[4,96,256]{2,1,0:T(8,128)(2,1)S(1)} %dynamic-slice_bitcast_fusion.1), channel_id=1, source_target_pairs={{0,1},{1,0},{2,3},{3,2},{4,5},{5,4},{6,7},{7,6},{8,9},{9,8},{10,11... | collective-permute-start | bytes 589832 | tf_op jit(solution)/shard_map/ppermute | solution.py:23
  95.6 6.0 %collective-permute-start.9 = (bf16[4,96,256]{2,1,0:T(8,128)(2,1)S(1)}, bf16[4,96,256]{2,1,0:T(8,128)(2,1)S(1)}, u32[]{:S(2)}, u32[]{:S(2)}) collective-permute-start(bf16[4,96,256]{2,1,0:T(8,128)(2,1)S(1)} %constant_dynamic-slice_fusion.1), channel_id=1, source_target_pairs={{0,16},{8,24},{16,0},{24,8},{1,17},{9,25},{17,1},{25,9},{2,18},{10... | collective-permute-start | bytes 589832 | tf_op jit(solution)/shard_map/ppermute | solution.py:23
  101.7 4.7 %collective-permute-start.12 = (bf16[96,512]{1,0:T(8,128)(2,1)S(1)}, bf16[96,512]{1,0:T(8,128)(2,1)S(1)}, u32[]{:S(2)}, u32[]{:S(2)}) collective-permute-start(bf16[96,512]{1,0:T(8,128)(2,1)S(1)} %get-tuple-element.28), channel_id=1, source_target_pairs={{0,2},{1,3},{2,0},{3,1},{4,6},{5,7},{6,4},{7,5},{8,10},{9,11},{10,... | collective-permute-start | bytes 294920 | tf_op jit(solution)/shard_map/ppermute | solution.py:23
  102.0 10.0 %collective-permute-start.13 = (bf16[96,512]{1,0:T(8,128)(2,1)S(1)}, bf16[96,512]{1,0:T(8,128)(2,1)S(1)}, u32[]{:S(2)}, u32[]{:S(2)}) collective-permute-start(bf16[96,512]{1,0:T(8,128)(2,1)S(1)} %get-tuple-element.29), channel_id=1, source_target_pairs={{0,4},{1,5},{2,6},{3,7},{4,0},{5,1},{6,2},{7,3},{8,12},{9,13},{10,... | collective-permute-start | bytes 294920 | tf_op jit(solution)/shard_map/ppermute | solution.py:23
  104.6 7.5 %collective-permute-start.14 = (bf16[96,512]{1,0:T(8,128)(2,1)S(1)}, bf16[96,512]{1,0:T(8,128)(2,1)S(1)}, u32[]{:S(2)}, u32[]{:S(2)}) collective-permute-start(bf16[96,512]{1,0:T(8,128)(2,1)S(1)} %get-tuple-element.30), channel_id=1, source_target_pairs={{0,6},{1,7},{2,4},{3,5},{4,2},{5,3},{6,0},{7,1},{8,14},{9,15},{10,... | collective-permute-start | bytes 294920 | tf_op jit(solution)/shard_map/ppermute | solution.py:23
  112.2 4.7 %collective-permute-start.15 = (bf16[2,96,256]{2,1,0:T(8,128)(2,1)S(1)}, bf16[2,96,256]{2,1,0:T(8,128)(2,1)S(1)}, u32[]{:S(2)}, u32[]{:S(2)}) collective-permute-start(bf16[2,96,256]{2,1,0:T(8,128)(2,1)S(1)} %pad_maximum_fusion.7), channel_id=1, source_target_pairs={{0,16},{8,24},{16,0},{24,8},{1,17},{9,25},{17,1},{25,9},{2,18},{10... | collective-permute-start | bytes 294920 | tf_op jit(solution)/shard_map/ppermute | solution.py:23
  116.9 1.5 %collective-permute-start.16 = (bf16[96,1024]{1,0:T(8,128)(2,1)S(1)}, bf16[96,1024]{1,0:T(8,128)(2,1)S(1)}, u32[]{:S(2)}, u32[]{:S(2)}) collective-permute-start(bf16[96,1024]{1,0:T(8,128)(2,1)S(1)} %pad_maximum_fusion.5), channel_id=1, source_target_pairs={{0,8},{8,0},{16,24},{24,16},{1,9},{9,1},{17,25},{25,17},{2,10},{10... | collective-permute-start | bytes 589832 | tf_op jit(solution)/shard_map/ppermute | solution.py:23

commit v10 on v9

--- a/solution.py
+++ b/solution.py
@@ -90,8 +90,8 @@
     *refs,
 ):
     self_hbms, neigh_hbms, refs = refs[:sources], refs[sources : 2 * sources], refs[2 * sources :]
-    aggregate_hbm, grad_hbm, sent_hbm, slots, features, left, cotangent, w_self, w_neigh, summed = refs[:10]
-    values, aggregate, grad, sent, slot_sems, row_sems, weight_sems, out_sems = refs[10:]
+    aggregate_hbm, grad_hbm, *sent_hbms, slots, features, left, cotangent, w_self, w_neigh, summed = refs[:11]
+    values, aggregate, grad, sent, slot_sems, row_sems, weight_sems, out_sems = refs[11:]
     senders, block, _ = slots.shape
     rows, hidden = grad.shape
     width = features.shape[1]
@@ -135,7 +135,7 @@
     pl.when(core != 0)(turning.wait)
     for copy in weight_copies + feature_copies:
         copy.wait()
-    span = 512
+    span = hidden // 2
 
     def multiply(index):
         at = slice(index * chunk, (index + 1) * chunk)
@@ -152,34 +152,34 @@
         if index + 1 < parts:
             multiply(index + 1)
         cotangent_copies[index].wait()
-        for row in range(0, chunk, 16):
-            at = slice(index * chunk + row, index * chunk + row + 16)
+        for row in range(0, chunk, 32):
+            at = slice(index * chunk + row, index * chunk + row + 32)
             for first in range(0, hidden, span):
                 columns = slice(first, first + span)
-                value = values[index % 2, row : row + 16, columns]
+                value = values[index % 2, row : row + 32, columns].astype(BF16)
                 square = value * value
-                bend = jnp.tanh(value * (SCALE + SCALE * CUBIC * square))
-                inner = value * (SCALE + 3.0 * SCALE * CUBIC * square)
-                slope = (1.0 + bend) * (0.5 + 0.5 * inner * (1.0 - bend))
-                grad[at, columns] = (cotangent[at, columns].astype(F32) * slope).astype(BF16)
+                bend = jnp.tanh(value * (square * (SCALE * CUBIC) + SCALE))
+                inner = value * (square * (1.5 * SCALE * CUBIC) + 0.5 * SCALE)
+                grad[at, columns] = cotangent[at, columns] * ((1.0 + bend) * (inner * (1.0 - bend) + 0.5))
         at = slice(index * chunk, (index + 1) * chunk)
         results.append(pltpu.make_async_copy(grad.at[at, :], grad_hbm.at[at, :], out_sems.at[0, index]))
         results[-1].start()
-    for index, first in enumerate(range(0, hidden, span)):
-        at = slice(first, first + span)
-        sent[:, at] = jnp.dot(left[...], grad[:, at], preferred_element_type=F32).astype(BF16)
-        results.append(pltpu.make_async_copy(sent.at[:, at], sent_hbm.at[:, at], out_sems.at[1, index]))
+    for index, sent_hbm in enumerate(sent_hbms):
+        at = slice(index * span, (index + 1) * span)
+        sent[index] = jnp.dot(left[...], grad[:, at], preferred_element_type=F32).astype(BF16)
+        results.append(pltpu.make_async_copy(sent.at[index], sent_hbm, out_sems.at[1, index]))
         results[-1].start()
     for result in results:
         result.wait()
 
 
-def kept_kernel(core_ref, turned_hbm, aggregate_hbm, grad_hbm, out_hbm, turned, aggregate, grad, out, in_sems, out_sems):
+def kept_kernel(core_ref, turned_hbm, aggregate_hbm, grad_hbm, *refs):
+    *out_hbms, turned, aggregate, grad, out, in_sems, out_sems = refs
     core = core_ref[0]
-    spans = [slice(first, first + 512) for first in range(0, out.shape[1], 512)]
     grads = split_copies(grad_hbm, grad, in_sems.at[1])
+    span = out.shape[2]
     results = [
-        pltpu.make_async_copy(out.at[:, at], out_hbm.at[:, at], out_sems.at[index]) for index, at in enumerate(spans)
+        pltpu.make_async_copy(out.at[index], out_hbm, out_sems.at[index]) for index, out_hbm in enumerate(out_hbms)
     ]
 
     def product(left_hbm, left, contract):
@@ -189,9 +189,10 @@
                 copy.start()
             for copy in copies:
                 copy.wait()
-            for at, result in zip(spans, results):
-                value = lax.dot_general(left[...], grad[:, at], (contract, ((), ())), preferred_element_type=F32)
-                out[:, at] = value.astype(BF16)
+            for index, result in enumerate(results):
+                columns = slice(index * span, (index + 1) * span)
+                value = lax.dot_general(left[...], grad[:, columns], (contract, ((), ())), preferred_element_type=F32)
+                out[index] = value.astype(BF16)
                 result.start()
 
         return body
@@ -228,8 +229,8 @@
     return held
 
 
-def added(left, right):
-    return (left.astype(F32) + right.astype(F32)).astype(BF16)
+def added(terms):
+    return sum(term.astype(F32) for term in terms).astype(BF16)
 
 
 def half_of(value, axis, which):
@@ -237,20 +238,24 @@
     return lax.dynamic_slice_in_dim(value, which * size, size, axis)
 
 
-def reduce_high(value, high):
+def exchanged(terms, take, which, axis, step):
+    arrived = swap(added([take(term, 1 - which) for term in terms]), axis, step)
+    return added([take(term, which) for term in terms] + [arrived])
+
+
+def reduce_high(terms, high):
     step = lax.axis_size("rep") // 4
     while step:
-        upper = (high // step) % 2
-        value = added(half_of(value, 2, upper), swap(half_of(value, 2, 1 - upper), "rep", 2 * step))
+        terms = [exchanged(terms, lambda term, which: half_of(term, 2, which), (high // step) % 2, "rep", 2 * step)]
         step //= 2
-    return value
-
-
-def reduce_low(value, low):
-    value = value.reshape(value.shape[0] // 2, 2, *value.shape[1:])
-    sent = lax.dynamic_index_in_dim(value, 1 - low, 1, keepdims=False)
-    kept = lax.dynamic_index_in_dim(value, low, 1, keepdims=False)
-    return added(kept, swap(sent, "dom", 1))
+    return terms
+
+
+def reduce_low(terms, low):
+    def take(term, which):
+        return lax.dynamic_index_in_dim(term.reshape(-1, 2, *term.shape[1:]), which, 1, keepdims=False)
+
+    return [exchanged(terms, take, low, "dom", 1)]
 
 
 def shards(features, cotangent, w_self, w_neigh, tile_vals, tile_src, tile_peer, in_block):
@@ -306,15 +311,16 @@
     sources, pieces = len(weights[0]), sum(weight.shape[0] for weight in weights[0])
     turned = features.T
 
-    aggregate, grad, sent = call(
+    term_halves = [jax.ShapeDtypeStruct((width, hidden // 2), BF16)] * 2
+    aggregate, grad, *sent = call(
         functools.partial(layer_kernel, sources),
         [
             jax.ShapeDtypeStruct((rows, width), BF16),
             jax.ShapeDtypeStruct((rows, hidden), BF16),
-            jax.ShapeDtypeStruct((width, hidden), BF16),
+            *term_halves,
         ],
         [SMEM] * 3 + [HBM] * (4 + 2 * sources),
-        [HBM] * 3,
+        [HBM] * 4,
         [
             pltpu.VMEM((dom_size, block, width), BF16),
             pltpu.VMEM((rows, width), BF16),
@@ -326,7 +332,7 @@
             pltpu.VMEM((2, 256, hidden), F32),
             pltpu.VMEM((rows, width), BF16),
             pltpu.VMEM((rows, hidden), BF16),
-            pltpu.VMEM((width, hidden), BF16),
+            pltpu.VMEM((2, width, hidden // 2), BF16),
             DMA((dom_size,)),
             DMA((3, rows // 256)),
             DMA((2, pieces)),
@@ -335,27 +341,28 @@
         flops=6 * rows * width * hidden,
         moved=16 * rows * hidden,
     )(core_arg, flip.astype(jnp.int32).reshape(1), in_block, received, features, turned, cotangent, *weights[0], *weights[1])
-    arrived = swap(sent, "rep", 1)
+    arrived = [swap(half, "rep", 1) for half in sent]
     kept = call(
         kept_kernel,
-        jax.ShapeDtypeStruct((width, hidden), BF16),
+        term_halves,
         [SMEM] + [HBM] * 3,
-        HBM,
+        [HBM] * 2,
         [
             pltpu.VMEM((width, rows), BF16),
             pltpu.VMEM((rows, width), BF16),
             pltpu.VMEM((rows, hidden), BF16),
-            pltpu.VMEM((width, hidden), BF16),
+            pltpu.VMEM((2, width, hidden // 2), BF16),
             DMA((2, 4)),
-            DMA((hidden // 512,)),
+            DMA((2,)),
         ],
         flops=2 * rows * width * hidden,
         moved=6 * rows * hidden,
     )(core_arg, turned, aggregate, grad)
-    chip = added(kept, arrived).reshape(dom_size, width // dom_size, hidden)
-    first, second = chip[:, :, : hidden // 2], chip[:, :, hidden // 2 :]
+    first, second = [
+        [term.reshape(dom_size, width // dom_size, hidden // 2) for term in terms] for terms in zip(kept, arrived)
+    ]
     first, second = reduce_low(first, low), reduce_high(second, high)
-    first, second = reduce_high(first, high), reduce_low(second, low)
+    (first,), (second,) = reduce_high(first, high), reduce_low(second, low)
     both = jnp.concatenate([first, second], axis=2)
     summed = lax.dynamic_index_in_dim(both, place, 0, keepdims=False).astype(F32)
     for step in range(1, dom_size // 2):

time: 120 us -> 121 us (level)
  other arithmetic: 6.39 us -> 9.22 us
  starting transfers between devices: 29.2 us -> 27.8 us
    convert_element_type x5 -> x6, other arithmetic: 2.42 us -> 5.27 us  [added(): return sum((term.astype(F32) for term in terms)).astype(BF16)]
    ppermute x13 -> x14, starting transfers between devices: 16.8 us -> 15.4 us  [swap(): lax.ppermute(value, axis, [(index, index ^ step) for index in range(size)])]
    ppermute x13 -> x14, waiting for transfers between devices: 42.3 us -> 43.4 us  [swap(): lax.ppermute(value, axis, [(index, index ^ step) for index in range(size)])]
    unnamed x5 -> x9, local copies, waits for them, and re-layouts: 2.89 us -> 2.84 us
  transfers between devices with their start and end apart: 18 -> 19, of which waited for: 13 -> 13; matrix products, arithmetic and copies ran while one was open for 4% -> 8% of each run, Pallas kernels for 8% -> 8%
where the time goes in v10:
time: 121 us
  waiting for transfers between devices  57 us (47%)
  starting transfers between devices  27.8 us (23%)
  Pallas kernels  21.8 us (18%)
  other arithmetic  9.22 us (8%)
  local copies, waits for them, and re-layouts  3.85 us (3%)
    ppermute x14, waiting for transfers between devices, swap(): lax.ppermute(value, axis, [(index, index ^ step) for index in range(size)])  43.4 us
    ppermute x14, starting transfers between devices, swap(): lax.ppermute(value, axis, [(index, index ^ step) for index in range(size)])  15.4 us
    pallas_call x1, Pallas kernels, shards(): call(functools.partial(layer_kernel, sources), [jax.ShapeDtypeStruct((row...  12.5 us
    all_to_all x1, waiting for transfers between devices, shards(): lax.all_to_all(slots.reshape(dom_size, block, width), 'dom', split_axis=0...  11.4 us
    ppermute x4, starting transfers between devices, cross(): lax.ppermute(value, ('rep', 'dom'), [(source, target) for source, target...  6.35 us
    all_to_all x1, starting transfers between devices, shards(): lax.all_to_all(slots.reshape(dom_size, block, width), 'dom', split_axis=0...  6.03 us
    convert_element_type x6, other arithmetic, added(): return sum((term.astype(F32) for term in terms)).astype(BF16)  5.27 us
    pallas_call x1, Pallas kernels, shards(): call(kept_kernel, term_halves, [SMEM] + [HBM] * 3, [HBM] * 2, [pltpu.VMEM...  4.79 us
  transfers between devices with their start and end apart: 19, of which 13 were waited for; matrix products, arithmetic and copies ran while one was open for 8% of the time, Pallas kernels for 8%

profile of v10, /device:TPU:0, one launch (start us, length us, event | category | flops | bytes accessed | tf_op | source)
XLA Modules:
  0.0 120.6 jit_solution(6317753219875803981)
XLA Ops:
  2.3 3.1 %collective-permute-start.1 = (bf16[2,96,512]{2,1,0:T(8,128)(2,1)S(1)}, bf16[2,96,512]{2,1,0:T(8,128)(2,1)S(1)}, u32[]{:S(2)}, u32[]{:S(2)}) collective-permute-start(bf16[2,96,512]{2,1,0:T(8,128)(2,1)S(1)} %pad_maximum_fusion.4), channel_id=1, source_target_pairs={{0,2},{1,3},{2,0},{3,1},{4,6},{5,7},{6,4},{7,5},{8,11},{9,10},{10,... | collective-permute-start | bytes 589832 | tf_op jit(solution)/shard_map/ppermute | solution.py:31
  5.4 2.6 %collective-permute-start.2 = (bf16[2,96,512]{2,1,0:T(8,128)(2,1)S(1)}, bf16[2,96,512]{2,1,0:T(8,128)(2,1)S(1)}, u32[]{:S(2)}, u32[]{:S(2)}) collective-permute-start(bf16[2,96,512]{2,1,0:T(8,128)(2,1)S(1)} %pad_maximum_fusion.4), channel_id=1, source_target_pairs={{0,4},{1,5},{2,6},{3,7},{4,0},{5,1},{6,2},{7,3},{8,13},{9,12},{10,... | collective-permute-start | bytes 589832 | tf_op jit(solution)/shard_map/ppermute | solution.py:31
  8.0 4.6 %shard_map.95 = bf16[1024,768]{1,0:T(8,128)(2,1)} custom-call(s32[32]{0:T(128)} %src_hbm.1, s32[32]{0:T(128)} %peer_hbm.1, bf16[32,128,128]{2,1,0:T(8,128)(2,1)} %tiles_hbm.1, bf16[1024,768]{1,0:T(8,128)(2,1)} %features_hbm.3), custom_call_target="tpu_custom_call" | custom-call | flops 1610612736 | bytes 4194304 | tf_op jit(solution)/shard_map/pallas_call | solution.py:276
  12.6 6.0 %all-to-all-start = ((bf16[8,128,768]{2,1,0:T(8,128)(2,1)}), bf16[8,128,768]{2,1,0:T(8,128)(2,1)S(1)}, u32[]{:S(2)}, u32[]{:S(2)}) async-start(bf16[8,128,768]{2,1,0:T(8,128)(2,1)} %bitcast.69), calls=%async_computation | async-start | bytes 3145728 | tf_op jit(solution)/shard_map/all_to_all | solution.py:295
  18.6 2.2 %collective-permute-done.3 = bf16[2,96,512]{2,1,0:T(8,128)(2,1)S(1)} collective-permute-done((bf16[2,96,512]{2,1,0:T(8,128)(2,1)S(1)}, bf16[2,96,512]{2,1,0:T(8,128)(2,1)S(1)}, u32[]{:S(2)}, u32[]{:S(2)}) %collective-permute-start.3) | collective-permute-done | bytes 196640 | tf_op jit(solution)/shard_map/ppermute | solution.py:31
  21.1 1.6 %collective-permute-start.4 = (bf16[2,4,96,512]{3,2,1,0:T(8,128)(2,1)S(1)}, bf16[2,4,96,512]{3,2,1,0:T(8,128)(2,1)}, u32[]{:S(2)}, u32[]{:S(2)}) collective-permute-start(bf16[2,4,96,512]{3,2,1,0:T(8,128)(2,1)S(1)} %pad_maximum_fusion.1), channel_id=1, source_target_pairs={{0,16},{8,24},{16,0},{24,8},{1,17},{9,25},{17,1},{25,9},{2,18},{10... | collective-permute-start | bytes 2359304 | tf_op jit(solution)/shard_map/ppermute | solution.py:23
  22.7 16.5 %collective-permute-done.4 = bf16[2,4,96,512]{3,2,1,0:T(8,128)(2,1)} collective-permute-done((bf16[2,4,96,512]{3,2,1,0:T(8,128)(2,1)S(1)}, bf16[2,4,96,512]{3,2,1,0:T(8,128)(2,1)}, u32[]{:S(2)}, u32[]{:S(2)}) %collective-permute-start.4) | collective-permute-done | bytes 786464 | tf_op jit(solution)/shard_map/ppermute | solution.py:23
  39.1 1.2 %broadcast_select_fusion = (bf16[2,4,96,512]{3,2,1,0:T(8,128)(2,1)S(1)}, bf16[2,4,96,512]{3,2,1,0:T(8,128)(2,1)S(1)}) fusion(bf16[2,4,96,512]{3,2,1,0:T(8,128)(2,1)} %collective-permute-done.4, pred[]{:T(512)S(6)} %ne.24, bf16[2,2,96,512]{3,2,1,0:T(8,128)(2,1)S(1)} %get-tuple-element.27, bf16[2,2,96,512]{3,2,1,0:T(8,128)(2,1)S(1)} %get-tuple-element.26), kind=kLoop, calls=%fused_computation.12 | loop fusion | flops 1179648 | bytes 3145729 | tf_op jit(solution)/shard_map/jit(_where)/select_n | solution.py:227
  40.4 1.4 %fusion.2 = (bf16[4,96,1024]{2,1,0:T(8,128)(2,1)}, bf16[4,96,1024]{2,1,0:T(8,128)(2,1)}) fusion(bf16[2,4,96,512]{3,2,1,0:T(8,128)(2,1)S(1)} %get-tuple-element.24, bf16[2,4,96,512]{3,2,1,0:T(8,128)(2,1)S(1)} %get-tuple-element.25), kind=kLoop, calls=%fused_computation.5 | loop fusion | flops 3145728 | bytes 3145728 | tf_op jit(solution)/shard_map/squeeze | solution.py:308
  41.8 2.5 %collective-permute-start.5 = (bf16[4,96,1024]{2,1,0:T(8,128)(2,1)}, bf16[4,96,1024]{2,1,0:T(8,128)(2,1)}, u32[]{:S(2)}, u32[]{:S(2)}) collective-permute-start(bf16[4,96,1024]{2,1,0:T(8,128)(2,1)} %get-tuple-element.23.refs_0_), channel_id=1, source_target_pairs={{0,8},{8,0},{16,24},{24,16},{1,9},{9,1},{17,25},{25,17},{2,10},{10... | collective-permute-start | bytes 2359304 | tf_op jit(solution)/shard_map/ppermute | solution.py:23
  44.3 1.6 %copy.18 = bf16[1024,768]{0,1:T(8,128)(2,1)} copy(bf16[1024,768]{1,0:T(8,128)(2,1)S(1)} %copy-done) | data formatting | bytes 3145728 | tf_op args[0]
  46.5 1.1 collective-permute-done.6.refs_3_
  47.7 11.4 %all-to-all-done.slots_hbm = bf16[8,128,768]{2,1,0:T(8,128)(2,1)S(1)} async-done(((bf16[8,128,768]{2,1,0:T(8,128)(2,1)}), bf16[8,128,768]{2,1,0:T(8,128)(2,1)S(1)}, u32[]{:S(2)}, u32[]{:S(2)}) %all-to-all-start) | async-done | bytes 1572896 | tf_op jit(solution)/shard_map/all_to_all | solution.py:295
  59.1 1.2 copy-done.1
  60.3 12.5 %shard_map.96 = (bf16[1024,768]{1,0:T(8,128)(2,1)}, bf16[1024,1024]{1,0:T(8,128)(2,1)}, bf16[768,512]{1,0:T(8,128)(2,1)}, bf16[768,512]{1,0:T(8,128)(2,1)}) custom-call(s32[1]{0:T(128)} %bitcast.core_ref, s32[1]{0:T(128)} %bitcast.2.flip_ref, s32[8]{0:T(128)} %into_ref.1, bf16[8,128,768]{2,1,0:T(8,128)(2,1)} %copy-done.1, bf16[1024,768]{1,0:T(8,128)(2,1)} %features_hbm.3, ...), custom_call_target="tpu_custom_call" | custom-call | flops 4831838208 | bytes 16777216 | tf_op jit(solution)/shard_map/pallas_call | solution.py:315
  72.8 1.8 %collective-permute-start.10 = (bf16[768,512]{1,0:T(8,128)(2,1)}, bf16[768,512]{1,0:T(8,128)(2,1)S(1)}, u32[]{:S(2)}, u32[]{:S(2)}) collective-permute-start(bf16[768,512]{1,0:T(8,128)(2,1)} %get-tuple-element.21), channel_id=1, source_target_pairs={{0,8},{8,0},{16,24},{24,16},{1,9},{9,1},{17,25},{25,17},{2,10},{10... | collective-permute-start | bytes 2359304 | tf_op jit(solution)/shard_map/ppermute | solution.py:23
  74.7 4.8 %shard_map.97 = (bf16[768,512]{1,0:T(8,128)(2,1)}, bf16[768,512]{1,0:T(8,128)(2,1)}) custom-call(s32[1]{0:T(128)} %bitcast.core_ref, bf16[768,1024]{1,0:T(8,128)(2,1)} %bitcast.71, bf16[1024,768]{1,0:T(8,128)(2,1)} %get-tuple-element.16.aggregate_hbm, bf16[1024,1024]{1,0:T(8,128)(2,1)} %get-tuple-element.17.grad_hbm), custom_call_target="tpu_custom_call" | custom-call | flops 1610612736 | bytes 6291456 | tf_op jit(solution)/shard_map/pallas_call | solution.py:345
  79.5 1.9 %add_convert_fusion.1 = bf16[8,96,256]{2,1,0:T(8,128)(2,1)} fusion(bf16[8,96,512]{2,1,0:T(8,128)(2,1)S(1)} %bitcast.76, s32[]{:T(128)S(6)} %select_n.163, bf16[8,96,512]{2,1,0:T(8,128)(2,1)} %bitcast.80), kind=kLoop, calls=%fused_computation.10 | loop fusion | flops 786432 | bytes 1179652 | tf_op jit(solution)/shard_map/convert_element_type | solution.py:233
  81.4 1.5 %collective-permute-start.11 = (bf16[8,96,256]{2,1,0:T(8,128)(2,1)}, bf16[8,96,256]{2,1,0:T(8,128)(2,1)S(1)}, u32[]{:S(2)}, u32[]{:S(2)}) collective-permute-start(bf16[8,96,256]{2,1,0:T(8,128)(2,1)} %add_convert_fusion.1), channel_id=1, source_target_pairs={{0,16},{8,24},{16,0},{24,8},{1,17},{9,25},{17,1},{25,9},{2,18},{10... | collective-permute-start | bytes 1179656 | tf_op jit(solution)/shard_map/ppermute | solution.py:23
  82.9 1.9 %fusion.4 = bf16[4,96,512]{2,1,0:T(8,128)(2,1)} fusion(bf16[4,2,96,512]{3,2,1,0:T(8,128)(2,1)S(1)} %bitcast.74, s32[]{:T(128)S(6)} %select_n.160, bf16[4,2,96,512]{3,2,1,0:T(8,128)(2,1)} %bitcast.78), kind=kLoop, calls=%fused_computation.22 | loop fusion | flops 786432 | bytes 1179652 | tf_op jit(solution)/shard_map/convert_element_type | solution.py:233
  85.7 7.3 %collective-permute-done.11 = bf16[8,96,256]{2,1,0:T(8,128)(2,1)S(1)} collective-permute-done((bf16[8,96,256]{2,1,0:T(8,128)(2,1)}, bf16[8,96,256]{2,1,0:T(8,128)(2,1)S(1)}, u32[]{:S(2)}, u32[]{:S(2)}) %collective-permute-start.11) | collective-permute-done | bytes 393248 | tf_op jit(solution)/shard_map/ppermute | solution.py:23
  94.2 2.6 %collective-permute-done.8 = bf16[4,96,512]{2,1,0:T(8,128)(2,1)} collective-permute-done((bf16[4,96,512]{2,1,0:T(8,128)(2,1)}, bf16[4,96,512]{2,1,0:T(8,128)(2,1)}, u32[]{:S(2)}, u32[]{:S(2)}) %collective-permute-start.8) | collective-permute-done | bytes 393248 | tf_op jit(solution)/shard_map/ppermute | solution.py:23
  96.8 1.1 fusion.3
  98.1 2.4 %collective-permute-done.12 = bf16[4,96,256]{2,1,0:T(8,128)(2,1)S(1)} collective-permute-done((bf16[4,96,256]{2,1,0:T(8,128)(2,1)S(1)}, bf16[4,96,256]{2,1,0:T(8,128)(2,1)S(1)}, u32[]{:S(2)}, u32[]{:S(2)}) %collective-permute-start.12) | collective-permute-done | bytes 196640 | tf_op jit(solution)/shard_map/ppermute | solution.py:23
  100.5 3.2 %collective-permute-done.9 = bf16[4,96,256]{2,1,0:T(8,128)(2,1)S(1)} collective-permute-done((bf16[4,96,256]{2,1,0:T(8,128)(2,1)S(1)}, bf16[4,96,256]{2,1,0:T(8,128)(2,1)S(1)}, u32[]{:S(2)}, u32[]{:S(2)}) %collective-permute-start.9) | collective-permute-done | bytes 196640 | tf_op jit(solution)/shard_map/ppermute | solution.py:23
  103.9 2.5 %collective-permute-start.14 = (bf16[96,512]{1,0:T(8,128)(2,1)S(1)}, bf16[96,512]{1,0:T(8,128)(2,1)S(1)}, u32[]{:S(2)}, u32[]{:S(2)}) collective-permute-start(bf16[96,512]{1,0:T(8,128)(2,1)S(1)} %get-tuple-element.33), channel_id=1, source_target_pairs={{0,4},{1,5},{2,6},{3,7},{4,0},{5,1},{6,2},{7,3},{8,12},{9,13},{10,... | collective-permute-start | bytes 294920 | tf_op jit(solution)/shard_map/ppermute | solution.py:23
  106.4 1.9 %collective-permute-start.15 = (bf16[96,512]{1,0:T(8,128)(2,1)S(1)}, bf16[96,512]{1,0:T(8,128)(2,1)S(1)}, u32[]{:S(2)}, u32[]{:S(2)}) collective-permute-start(bf16[96,512]{1,0:T(8,128)(2,1)S(1)} %get-tuple-element.34), channel_id=1, source_target_pairs={{0,6},{1,7},{2,4},{3,5},{4,2},{5,3},{6,0},{7,1},{8,14},{9,15},{10,... | collective-permute-start | bytes 294920 | tf_op jit(solution)/shard_map/ppermute | solution.py:23
  108.3 1.7 %collective-permute-done.13 = bf16[96,512]{1,0:T(8,128)(2,1)S(1)} collective-permute-done((bf16[96,512]{1,0:T(8,128)(2,1)S(1)}, bf16[96,512]{1,0:T(8,128)(2,1)S(1)}, u32[]{:S(2)}, u32[]{:S(2)}) %collective-permute-start.13) | collective-permute-done | bytes 98336 | tf_op jit(solution)/shard_map/ppermute | solution.py:23
  110.0 3.2 %collective-permute-done.14 = bf16[96,512]{1,0:T(8,128)(2,1)S(1)} collective-permute-done((bf16[96,512]{1,0:T(8,128)(2,1)S(1)}, bf16[96,512]{1,0:T(8,128)(2,1)S(1)}, u32[]{:S(2)}, u32[]{:S(2)}) %collective-permute-start.14) | collective-permute-done | bytes 98336 | tf_op jit(solution)/shard_map/ppermute | solution.py:23
  113.4 1.4 %collective-permute-start.16 = (bf16[2,96,256]{2,1,0:T(8,128)(2,1)S(1)}, bf16[2,96,256]{2,1,0:T(8,128)(2,1)S(1)}, u32[]{:S(2)}, u32[]{:S(2)}) collective-permute-start(bf16[2,96,256]{2,1,0:T(8,128)(2,1)S(1)} %pad_maximum_fusion.7), channel_id=1, source_target_pairs={{0,16},{8,24},{16,0},{24,8},{1,17},{9,25},{17,1},{25,9},{2,18},{10... | collective-permute-start | bytes 294920 | tf_op jit(solution)/shard_map/ppermute | solution.py:23
  114.8 3.3 %collective-permute-done.16 = bf16[2,96,256]{2,1,0:T(8,128)(2,1)S(1)} collective-permute-done((bf16[2,96,256]{2,1,0:T(8,128)(2,1)S(1)}, bf16[2,96,256]{2,1,0:T(8,128)(2,1)S(1)}, u32[]{:S(2)}, u32[]{:S(2)}) %collective-permute-start.16) | collective-permute-done | bytes 98336 | tf_op jit(solution)/shard_map/ppermute | solution.py:23
  118.2 1.4 %collective-permute-done.17 = bf16[96,1024]{1,0:T(8,128)(2,1)S(1)} collective-permute-done((bf16[96,1024]{1,0:T(8,128)(2,1)S(1)}, bf16[96,1024]{1,0:T(8,128)(2,1)S(1)}, u32[]{:S(2)}, u32[]{:S(2)}) %collective-permute-start.17) | collective-permute-done | bytes 196640 | tf_op jit(solution)/shard_map/ppermute | solution.py:23
  (42 shorter events, 6.2 us)
Async XLA Ops:
  1.6 17.0 %collective-permute-start = (bf16[2,96,512]{2,1,0:T(8,128)(2,1)S(1)}, bf16[2,96,512]{2,1,0:T(8,128)(2,1)S(1)}, u32[]{:S(2)}, u32[]{:S(2)}) collective-permute-start(bf16[2,96,512]{2,1,0:T(8,128)(2,1)S(1)} %pad_maximum_fusion.4), channel_id=1, source_target_pairs={{8,9},{9,8},{10,11},{11,10},{12,13},{13,12},{14,15},{15,14},{24,25... | collective-permute-start | bytes 589832 | tf_op jit(solution)/shard_map/ppermute | solution.py:31
  2.3 16.3 %collective-permute-start.1 = (bf16[2,96,512]{2,1,0:T(8,128)(2,1)S(1)}, bf16[2,96,512]{2,1,0:T(8,128)(2,1)S(1)}, u32[]{:S(2)}, u32[]{:S(2)}) collective-permute-start(bf16[2,96,512]{2,1,0:T(8,128)(2,1)S(1)} %pad_maximum_fusion.4), channel_id=1, source_target_pairs={{0,2},{1,3},{2,0},{3,1},{4,6},{5,7},{6,4},{7,5},{8,11},{9,10},{10,... | collective-permute-start | bytes 589832 | tf_op jit(solution)/shard_map/ppermute | solution.py:31
  5.4 13.2 %collective-permute-start.2 = (bf16[2,96,512]{2,1,0:T(8,128)(2,1)S(1)}, bf16[2,96,512]{2,1,0:T(8,128)(2,1)S(1)}, u32[]{:S(2)}, u32[]{:S(2)}) collective-permute-start(bf16[2,96,512]{2,1,0:T(8,128)(2,1)S(1)} %pad_maximum_fusion.4), channel_id=1, source_target_pairs={{0,4},{1,5},{2,6},{3,7},{4,0},{5,1},{6,2},{7,3},{8,13},{9,12},{10,... | collective-permute-start | bytes 589832 | tf_op jit(solution)/shard_map/ppermute | solution.py:31
  8.0 12.8 %collective-permute-start.3 = (bf16[2,96,512]{2,1,0:T(8,128)(2,1)S(1)}, bf16[2,96,512]{2,1,0:T(8,128)(2,1)S(1)}, u32[]{:S(2)}, u32[]{:S(2)}) collective-permute-start(bf16[2,96,512]{2,1,0:T(8,128)(2,1)S(1)} %pad_maximum_fusion.4), channel_id=1, source_target_pairs={{0,6},{1,7},{2,4},{3,5},{4,2},{5,3},{6,0},{7,1},{8,15},{9,14},{10,... | collective-permute-start | bytes 589832 | tf_op jit(solution)/shard_map/ppermute | solution.py:31
  12.6 46.6 %all-to-all-start = ((bf16[8,128,768]{2,1,0:T(8,128)(2,1)}), bf16[8,128,768]{2,1,0:T(8,128)(2,1)S(1)}, u32[]{:S(2)}, u32[]{:S(2)}) async-start(bf16[8,128,768]{2,1,0:T(8,128)(2,1)} %bitcast.69), calls=%async_computation | async-start | bytes 3145728 | tf_op jit(solution)/shard_map/all_to_all | solution.py:295
  21.1 18.1 %collective-permute-start.4 = (bf16[2,4,96,512]{3,2,1,0:T(8,128)(2,1)S(1)}, bf16[2,4,96,512]{3,2,1,0:T(8,128)(2,1)}, u32[]{:S(2)}, u32[]{:S(2)}) collective-permute-start(bf16[2,4,96,512]{3,2,1,0:T(8,128)(2,1)S(1)} %pad_maximum_fusion.1), channel_id=1, source_target_pairs={{0,16},{8,24},{16,0},{24,8},{1,17},{9,25},{17,1},{25,9},{2,18},{10... | collective-permute-start | bytes 2359304 | tf_op jit(solution)/shard_map/ppermute | solution.py:23
  40.4 3.9 %copy-start = (bf16[1024,768]{1,0:T(8,128)(2,1)S(1)}, bf16[1024,768]{1,0:T(8,128)(2,1)}, u32[]{:S(2)}) copy-start(bf16[1024,768]{1,0:T(8,128)(2,1)} %features_hbm.3) | copy-start | bytes 4718596
  41.8 4.8 %collective-permute-start.5 = (bf16[4,96,1024]{2,1,0:T(8,128)(2,1)}, bf16[4,96,1024]{2,1,0:T(8,128)(2,1)}, u32[]{:S(2)}, u32[]{:S(2)}) collective-permute-start(bf16[4,96,1024]{2,1,0:T(8,128)(2,1)} %get-tuple-element.23.refs_0_), channel_id=1, source_target_pairs={{0,8},{8,0},{16,24},{24,16},{1,9},{9,1},{17,25},{25,17},{2,10},{10... | collective-permute-start | bytes 2359304 | tf_op jit(solution)/shard_map/ppermute | solution.py:23
  44.3 3.4 %collective-permute-start.6 = (bf16[4,96,1024]{2,1,0:T(8,128)(2,1)}, bf16[4,96,1024]{2,1,0:T(8,128)(2,1)}, u32[]{:S(2)}, u32[]{:S(2)}) collective-permute-start(bf16[4,96,1024]{2,1,0:T(8,128)(2,1)} %get-tuple-element.22.refs_2_), channel_id=1, source_target_pairs={{0,8},{8,0},{16,24},{24,16},{1,9},{9,1},{17,25},{25,17},{2,10},{10... | collective-permute-start | bytes 2359304 | tf_op jit(solution)/shard_map/ppermute | solution.py:23
  59.1 1.2 copy-start.1
  72.8 6.6 %collective-permute-start.10 = (bf16[768,512]{1,0:T(8,128)(2,1)}, bf16[768,512]{1,0:T(8,128)(2,1)S(1)}, u32[]{:S(2)}, u32[]{:S(2)}) collective-permute-start(bf16[768,512]{1,0:T(8,128)(2,1)} %get-tuple-element.21), channel_id=1, source_target_pairs={{0,8},{8,0},{16,24},{24,16},{1,9},{9,1},{17,25},{25,17},{2,10},{10... | collective-permute-start | bytes 2359304 | tf_op jit(solution)/shard_map/ppermute | solution.py:23
  74.6 8.3 %collective-permute-start.7 = (bf16[768,512]{1,0:T(8,128)(2,1)}, bf16[768,512]{1,0:T(8,128)(2,1)S(1)}, u32[]{:S(2)}, u32[]{:S(2)}) collective-permute-start(bf16[768,512]{1,0:T(8,128)(2,1)} %get-tuple-element.19), channel_id=1, source_target_pairs={{0,8},{8,0},{16,24},{24,16},{1,9},{9,1},{17,25},{25,17},{2,10},{10... | collective-permute-start | bytes 2359304 | tf_op jit(solution)/shard_map/ppermute | solution.py:23
  79.4 13.6 %copy-start.3 = (bf16[768,512]{1,0:T(8,128)(2,1)S(1)}, bf16[768,512]{1,0:T(8,128)(2,1)}, u32[]{:S(2)}) copy-start(bf16[768,512]{1,0:T(8,128)(2,1)} %get-tuple-element.20) | copy-start | bytes 2359300
  81.4 11.7 %collective-permute-start.11 = (bf16[8,96,256]{2,1,0:T(8,128)(2,1)}, bf16[8,96,256]{2,1,0:T(8,128)(2,1)S(1)}, u32[]{:S(2)}, u32[]{:S(2)}) collective-permute-start(bf16[8,96,256]{2,1,0:T(8,128)(2,1)} %add_convert_fusion.1), channel_id=1, source_target_pairs={{0,16},{8,24},{16,0},{24,8},{1,17},{9,25},{17,1},{25,9},{2,18},{10... | collective-permute-start | bytes 1179656 | tf_op jit(solution)/shard_map/ppermute | solution.py:23
  82.9 13.9 %copy-start.2 = (bf16[768,512]{1,0:T(8,128)(2,1)S(1)}, bf16[768,512]{1,0:T(8,128)(2,1)}, u32[]{:S(2)}) copy-start(bf16[768,512]{1,0:T(8,128)(2,1)} %get-tuple-element.18) | copy-start | bytes 2359300
  84.8 12.0 %collective-permute-start.8 = (bf16[4,96,512]{2,1,0:T(8,128)(2,1)}, bf16[4,96,512]{2,1,0:T(8,128)(2,1)}, u32[]{:S(2)}, u32[]{:S(2)}) collective-permute-start(bf16[4,96,512]{2,1,0:T(8,128)(2,1)} %fusion.4), channel_id=1, source_target_pairs={{0,1},{1,0},{2,3},{3,2},{4,5},{5,4},{6,7},{7,6},{8,9},{9,8},{10,11... | collective-permute-start | bytes 1179656 | tf_op jit(solution)/shard_map/ppermute | solution.py:23
  93.3 7.2 %collective-permute-start.12 = (bf16[4,96,256]{2,1,0:T(8,128)(2,1)S(1)}, bf16[4,96,256]{2,1,0:T(8,128)(2,1)S(1)}, u32[]{:S(2)}, u32[]{:S(2)}) collective-permute-start(bf16[4,96,256]{2,1,0:T(8,128)(2,1)S(1)} %dynamic-slice_bitcast_fusion), channel_id=1, source_target_pairs={{0,1},{1,0},{2,3},{3,2},{4,5},{5,4},{6,7},{7,6},{8,9},{9,8},{10,11... | collective-permute-start | bytes 589832 | tf_op jit(solution)/shard_map/ppermute | solution.py:23
  98.0 5.8 %collective-permute-start.9 = (bf16[4,96,256]{2,1,0:T(8,128)(2,1)S(1)}, bf16[4,96,256]{2,1,0:T(8,128)(2,1)S(1)}, u32[]{:S(2)}, u32[]{:S(2)}) collective-permute-start(bf16[4,96,256]{2,1,0:T(8,128)(2,1)S(1)} %constant_dynamic-slice_fusion), channel_id=1, source_target_pairs={{0,16},{8,24},{16,0},{24,8},{1,17},{9,25},{17,1},{25,9},{2,18},{10... | collective-permute-start | bytes 589832 | tf_op jit(solution)/shard_map/ppermute | solution.py:23
  103.8 6.2 %collective-permute-start.13 = (bf16[96,512]{1,0:T(8,128)(2,1)S(1)}, bf16[96,512]{1,0:T(8,128)(2,1)S(1)}, u32[]{:S(2)}, u32[]{:S(2)}) collective-permute-start(bf16[96,512]{1,0:T(8,128)(2,1)S(1)} %get-tuple-element.32), channel_id=1, source_target_pairs={{0,2},{1,3},{2,0},{3,1},{4,6},{5,7},{6,4},{7,5},{8,10},{9,11},{10,... | collective-permute-start | bytes 294920 | tf_op jit(solution)/shard_map/ppermute | solution.py:23
  103.9 9.3 %collective-permute-start.14 = (bf16[96,512]{1,0:T(8,128)(2,1)S(1)}, bf16[96,512]{1,0:T(8,128)(2,1)S(1)}, u32[]{:S(2)}, u32[]{:S(2)}) collective-permute-start(bf16[96,512]{1,0:T(8,128)(2,1)S(1)} %get-tuple-element.33), channel_id=1, source_target_pairs={{0,4},{1,5},{2,6},{3,7},{4,0},{5,1},{6,2},{7,3},{8,12},{9,13},{10,... | collective-permute-start | bytes 294920 | tf_op jit(solution)/shard_map/ppermute | solution.py:23
  106.4 6.8 %collective-permute-start.15 = (bf16[96,512]{1,0:T(8,128)(2,1)S(1)}, bf16[96,512]{1,0:T(8,128)(2,1)S(1)}, u32[]{:S(2)}, u32[]{:S(2)}) collective-permute-start(bf16[96,512]{1,0:T(8,128)(2,1)S(1)} %get-tuple-element.34), channel_id=1, source_target_pairs={{0,6},{1,7},{2,4},{3,5},{4,2},{5,3},{6,0},{7,1},{8,14},{9,15},{10,... | collective-permute-start | bytes 294920 | tf_op jit(solution)/shard_map/ppermute | solution.py:23
  113.4 4.7 %collective-permute-start.16 = (bf16[2,96,256]{2,1,0:T(8,128)(2,1)S(1)}, bf16[2,96,256]{2,1,0:T(8,128)(2,1)S(1)}, u32[]{:S(2)}, u32[]{:S(2)}) collective-permute-start(bf16[2,96,256]{2,1,0:T(8,128)(2,1)S(1)} %pad_maximum_fusion.7), channel_id=1, source_target_pairs={{0,16},{8,24},{16,0},{24,8},{1,17},{9,25},{17,1},{25,9},{2,18},{10... | collective-permute-start | bytes 294920 | tf_op jit(solution)/shard_map/ppermute | solution.py:23
  118.1 1.5 %collective-permute-start.17 = (bf16[96,1024]{1,0:T(8,128)(2,1)S(1)}, bf16[96,1024]{1,0:T(8,128)(2,1)S(1)}, u32[]{:S(2)}, u32[]{:S(2)}) collective-permute-start(bf16[96,1024]{1,0:T(8,128)(2,1)S(1)} %pad_maximum_fusion.5), channel_id=1, source_target_pairs={{0,8},{8,0},{16,24},{24,16},{1,9},{9,1},{17,25},{25,17},{2,10},{10... | collective-permute-start | bytes 589832 | tf_op jit(solution)/shard_map/ppermute | solution.py:23

commit v11 on v10

v11 whole, which is shorter than its diff:
```python
import functools

import jax
import jax.numpy as jnp
from jax import lax
from jax.experimental import pallas as pl
from jax.experimental.pallas import tpu as pltpu
from jax.sharding import PartitionSpec as P

F32 = jnp.float32
BF16 = jnp.bfloat16
SCALE = 0.7978845608
CUBIC = 0.044715
MIB = 1 << 20
HBM = pl.BlockSpec(memory_space=pltpu.HBM)
SMEM = pl.BlockSpec(memory_space=pltpu.SMEM)
VMEM = pl.BlockSpec(memory_space=pltpu.VMEM)
DMA = pltpu.SemaphoreType.DMA


def swap(value, axis, step):
    size = lax.axis_size(axis)
    return lax.ppermute(value, axis, [(index, index ^ step) for index in range(size)])


def cross(value, step):
    reps, doms = lax.axis_size("rep"), lax.axis_size("dom")
    pairs = [
        (rep * doms + dom, rep * doms + (dom ^ step ^ (rep & 1))) for rep in range(reps) for dom in range(doms)
    ]
    return lax.ppermute(value, ("rep", "dom"), [(source, target) for source, target in pairs if source != target])


def split_copies(source, target, sems, count=4):
    size = source.shape[0] // count
    return [
        pltpu.make_async_copy(
            source.at[index * size : (index + 1) * size], target.at[index * size : (index + 1) * size], sems.at[index]
        )
        for index in range(count)
    ]


def slots_kernel(
    src_hbm, peer_hbm, tiles_hbm, features_hbm, out_hbm, src, peer, tiles, features, dense, out, in_sems, out_sems
):
    scalars = [
        pltpu.make_async_copy(src_hbm, src, in_sems.at[2, 0]),
        pltpu.make_async_copy(peer_hbm, peer, in_sems.at[2, 1]),
    ]
    tile_copies = split_copies(tiles_hbm, tiles, in_sems.at[0])
    feature_copies = split_copies(features_hbm, features, in_sems.at[1])
    for copy in scalars + tile_copies + feature_copies:
        copy.start()
    count, block, _ = tiles.shape
    dense[...] = jnp.zeros_like(dense)
    for copy in scalars + tile_copies:
        copy.wait()

    def place(tile, carry):
        row = pl.multiple_of(peer[tile] * block, block)
        column = pl.multiple_of(src[tile] * block, block)
        at = (pl.ds(row, block), pl.ds(column, block))
        dense[at] = dense[at] + tiles[tile].astype(F32)
        return carry

    lax.fori_loop(0, count, place, 0)
    for copy in feature_copies:
        copy.wait()
    chunk = 4 * block
    results = []
    for index in range(out.shape[0] // chunk):
        at = slice(index * chunk, (index + 1) * chunk)
        out[at, :] = jnp.dot(dense[at, :].astype(BF16), features[...], preferred_element_type=F32).astype(BF16)
        results.append(pltpu.make_async_copy(out.at[at, :], out_hbm.at[at, :], out_sems.at[index]))
        results[-1].start()
    for result in results:
        result.wait()


def weight_copies(flip, weight_hbms, weight, sems):
    sources = len(weight_hbms)
    copies = []
    for source, weight_hbm in enumerate(weight_hbms):
        for piece in range(weight_hbm.shape[0]):
            target = piece if sources == 1 else 2 * piece + (flip ^ source)
            copies.append(
                pltpu.make_async_copy(weight_hbm.at[piece], weight.at[target], sems.at[sources * piece + source])
            )
    return copies


def self_kernel(flip_ref, features_hbm, *refs):
    *weight_hbms, out_hbm, features, weight, out, feature_sems, weight_sems, out_sems = refs
    rows, width = features.shape
    hidden = out.shape[1]
    copies = weight_copies(flip_ref[0], weight_hbms, weight, weight_sems)
    copies += split_copies(features_hbm, features, feature_sems)
    for copy in copies:
        copy.start()
    for copy in copies:
        copy.wait()
    chunk = 256
    results = split_copies(out, out_hbm, out_sems, rows // chunk)
    for index, result in enumerate(results):
        at = slice(index * chunk, (index + 1) * chunk)
        out[at, :] = jnp.dot(
            features[at, :], weight[...].reshape(width, hidden), preferred_element_type=F32
        ).astype(BF16)
        result.start()
    for result in results:
        result.wait()


def layer_kernel(
    sources, pieces, places_ref, into_ref, slots_ref, total_hbm, turned_hbm, cotangent_hbm, *refs
):
    weight_hbms, out_hbms = refs[:sources], refs[sources:-15]
    total, turned, cotangent, weight, summed, values, aggregate, left, grad, first, second = refs[-15:-4]
    row_sems, weight_sems, turned_sems, out_sems = refs[-4:]
    senders, block, _ = slots_ref.shape
    rows, hidden = grad.shape
    width = aggregate.shape[1]
    core, flip, low, upper = [places_ref[index] for index in range(4)]
    chunk = 256
    parts = rows // chunk
    weights = weight_copies(flip, weight_hbms, weight, weight_sems)
    totals = split_copies(total_hbm, total, row_sems.at[0], parts)
    cotangents = split_copies(cotangent_hbm, cotangent, row_sems.at[1], parts)
    turnings = split_copies(turned_hbm, turned, turned_sems)
    for copy in weights + totals + cotangents + turnings:
        copy.start()

    summed[...] = jnp.zeros_like(summed)
    for sender in range(senders):
        at = pl.ds(pl.multiple_of(into_ref[sender] * block, block), block)
        summed[at, :] = summed[at, :] + slots_ref[sender].astype(F32)
    aggregate[...] = summed[...].astype(BF16)
    left[...] = aggregate[...].T
    for copy in weights:
        copy.wait()
    span = hidden // 2

    def multiply(index):
        at = slice(index * chunk, (index + 1) * chunk)
        for begin in range(0, hidden, span):
            columns = slice(begin, begin + span)
            values[index % 2, :, columns] = jnp.dot(
                aggregate[at, :], weight[:, :, columns].reshape(width, span), preferred_element_type=F32
            )

    multiply(0)
    for index in range(parts):
        if index + 1 < parts:
            multiply(index + 1)
        totals[index].wait()
        cotangents[index].wait()
        for row in range(0, chunk, 32):
            at = slice(index * chunk + row, index * chunk + row + 32)
            for begin in range(0, hidden, span):
                columns = slice(begin, begin + span)
                value = values[index % 2, row : row + 32, columns] + total[at, columns].astype(F32)
                value = value.astype(BF16)
                square = value * value
                bend = jnp.tanh(value * (square * (SCALE * CUBIC) + SCALE))
                inner = value * (square * (1.5 * SCALE * CUBIC) + 0.5 * SCALE)
                grad[at, columns] = cotangent[at, columns] * ((1.0 + bend) * (inner * (1.0 - bend) + 0.5))

    for copy in turnings:
        copy.wait()
    results = []

    def send(source, target):
        results.append(pltpu.make_async_copy(source, target, out_sems.at[len(results)]))
        results[-1].start()

    for index, operand in enumerate([turned, left]):
        product = jnp.dot(operand[...], grad[:, :span], preferred_element_type=F32).astype(BF16)
        first[index] = product.reshape(first.shape[1:])
    for term, which in enumerate([1 - core, core]):
        if pieces:
            for leave, bit in enumerate([1 - low, low]):
                for row in range(first.shape[1] // 2):
                    send(first.at[which, 2 * row + bit], out_hbms[4 * term + leave].at[row])
        else:
            send(first.at[which], out_hbms[4 * term])
    for index, operand in enumerate([turned, left]):
        for side in range(2):
            columns = slice(span + side * span // 2, span + (side + 1) * span // 2)
            second[index, side] = jnp.dot(operand[...], grad[:, columns], preferred_element_type=F32).astype(BF16)
    for term, which in enumerate([1 - core, core]):
        for leave, bit in enumerate([1 - upper, upper]):
            send(second.at[which, bit], out_hbms[4 * term + 2 + leave])
    for result in results:
        result.wait()


def call(kernel, outs, places, out_places, scratch=(), flops=0, moved=0, vmem=56):
    return pl.pallas_call(
        kernel,
        out_shape=outs,
        in_specs=places,
        out_specs=out_places,
        scratch_shapes=list(scratch),
        compiler_params=pltpu.CompilerParams(vmem_limit_bytes=vmem * MIB),
        cost_estimate=pl.CostEstimate(flops=flops, bytes_accessed=moved, transcendentals=0),
    )


def joined(held, other, upper, axis):
    return jnp.stack([jnp.where(upper, other, held), jnp.where(upper, held, other)], axis=axis)


def gather_high(held, high):
    step = 1
    while step < lax.axis_size("rep") // 2:
        other = swap(held, "rep", 2 * step)
        upper = (high & step) != 0
        held = jnp.concatenate([jnp.where(upper, other, held), jnp.where(upper, held, other)], axis=-1)
        step *= 2
    return held


def added(terms):
    return sum(term.astype(F32) for term in terms).astype(BF16)


def half_of(value, axis, which):
    size = value.shape[axis] // 2
    return lax.dynamic_slice_in_dim(value, which * size, size, axis)


def low_half(term, which):
    return lax.dynamic_index_in_dim(term.reshape(-1, 2, *term.shape[1:]), which, 1, keepdims=False)


def column_half(term, which):
    size = term.shape[-1] // 2
    return lax.dynamic_slice_in_dim(term, which * size, size, term.ndim - 1)


def exchanged(term, take, which, axis, step):
    return added([take(term, which), swap(take(term, 1 - which), axis, step)])


def reduce_high(term, high, step):
    while step:
        term = exchanged(term, column_half, (high // step) % 2, "rep", 2 * step)
        step //= 2
    return term


def shards(features, cotangent, w_self, w_neigh, tile_vals, tile_src, tile_peer, in_block):
    dom_size = lax.axis_size("dom")
    rows, width = features.shape
    hidden = w_self.shape[1]
    block = tile_vals.shape[1]
    me = lax.axis_index("dom")
    rep = lax.axis_index("rep")
    parts = lax.axis_size("rep") // 2
    core, high = rep & 1, rep >> 1
    low, place = me & 1, me >> 1

    share = hidden // parts
    held = jnp.stack([lax.dynamic_slice_in_dim(weight, high * share, share, 1) for weight in (w_self, w_neigh)])
    pieces = [cross(held, 2 * step) for step in range(dom_size // 2)]
    slots = call(
        slots_kernel,
        jax.ShapeDtypeStruct((dom_size * block, width), BF16),
        [HBM] * 4,
        HBM,
        [
            pltpu.SMEM(tile_src.shape, jnp.int32),
            pltpu.SMEM(tile_peer.shape, jnp.int32),
            pltpu.VMEM(tile_vals.shape, BF16),
            pltpu.VMEM(features.shape, BF16),
            pltpu.VMEM((dom_size * block, rows), F32),
            pltpu.VMEM((dom_size * block, width), BF16),
            DMA((3, 4)),
            DMA((dom_size // 4,)),
        ],
        flops=2 * dom_size * block * rows * width,
        moved=tile_vals.size * 2 + rows * width * 4,
    )(tile_src, tile_peer, tile_vals, features)
    *pieces, _ = lax.optimization_barrier((*pieces, slots))
    received = lax.all_to_all(slots.reshape(dom_size, block, width), "dom", split_axis=0, concat_axis=0, tiled=True)
    pieces[0] = jnp.where(core == 0, held, pieces[0])
    pieces = [piece[:, None] for piece in pieces]
    bit = 1
    while len(pieces) > 1:
        upper = (place & bit) != 0
        pieces = [
            jnp.concatenate([jnp.where(upper, b, a), jnp.where(upper, a, b)], axis=1)
            for a, b in zip(pieces[::2], pieces[1::2])
        ]
        bit *= 2
    mine = gather_high(pieces[0], high)
    depth = width // dom_size
    tiled = depth % 16 == 0
    flip = low ^ core
    weights = [[mine[index], swap(mine[index], "rep", 1)] for index in range(2)]
    if not tiled:
        weights = [[joined(*weight, flip != 0, 1).reshape(-1, 128, hidden)] for weight in weights]
    sources, count = len(weights[0]), sum(weight.shape[0] for weight in weights[0])
    weight_shape = pltpu.VMEM((count, width // count, hidden), BF16)
    total = call(
        self_kernel,
        jax.ShapeDtypeStruct((rows, hidden), BF16),
        [SMEM] + [HBM] * (1 + sources),
        HBM,
        [
            pltpu.VMEM((rows, width), BF16),
            weight_shape,
            pltpu.VMEM((rows, hidden), BF16),
            DMA((4,)),
            DMA((count,)),
            DMA((rows // 256,)),
        ],
    )(flip.astype(jnp.int32).reshape(1), features, *weights[0])
    turned = features.T

    span = hidden // 2
    upper = (high // (parts // 2)) % 2
    places = jnp.stack([core, flip, low, upper]).astype(jnp.int32)
    if tiled:
        first_shapes = [jax.ShapeDtypeStruct((dom_size // 2, depth, span), BF16)] * 2
        first_scratch = (2, dom_size, depth, span)
    else:
        first_shapes = [jax.ShapeDtypeStruct((width, span), BF16), jax.ShapeDtypeStruct((8, 128), BF16)]
        first_scratch = (2, width, span)
    out_shapes = (first_shapes + [jax.ShapeDtypeStruct((width, span // 2), BF16)] * 2) * 2
    outs = call(
        functools.partial(layer_kernel, sources, tiled),
        out_shapes,
        [SMEM, SMEM, VMEM] + [HBM] * (3 + sources),
        [HBM] * 8,
        [
            pltpu.VMEM((rows, hidden), BF16),
            pltpu.VMEM((width, rows), BF16),
            pltpu.VMEM((rows, hidden), BF16),
            weight_shape,
            pltpu.VMEM((rows, width), F32),
            pltpu.VMEM((2, 256, hidden), F32),
            pltpu.VMEM((rows, width), BF16),
            pltpu.VMEM((width, rows), BF16),
            pltpu.VMEM((rows, hidden), BF16),
            pltpu.VMEM(first_scratch, BF16),
            pltpu.VMEM((2, 2, width, span // 2), BF16),
            DMA((2, rows // 256)),
            DMA((count,)),
            DMA((4,)),
            DMA((2 * dom_size + 4,)),
        ],
        flops=6 * rows * width * hidden,
        moved=16 * rows * hidden,
    )(places, in_block, received, total, turned, cotangent, *weights[1])
    outs = list(outs)
    if not tiled:
        for at in (0, 4):
            term = outs[at].reshape(dom_size, depth, span)
            outs[at], outs[at + 1] = low_half(term, 1 - low), low_half(term, low)
    terms = [None] * 4
    for at in (0, 2, 1, 3):
        terms[at] = [outs[4 + at], swap(outs[at], "rep", 1)]
    first = added([*terms[1], swap(added(terms[0]), "dom", 1)])
    second = added([*terms[3], swap(added(terms[2]), "rep", parts)]).reshape(dom_size, depth, -1)
    first = reduce_high(first, high, parts // 2)
    second = exchanged(reduce_high(second, high, parts // 4), low_half, low, "dom", 1)
    both = jnp.concatenate([first, second], axis=2)
    summed = lax.dynamic_index_in_dim(both, place, 0, keepdims=False).astype(F32)
    for step in range(1, dom_size // 2):
        piece = lax.dynamic_index_in_dim(both, place ^ step, 0, keepdims=False)
        summed = summed + swap(piece, "dom", 2 * step).astype(F32)
    summed = summed.astype(BF16)
    size = summed.shape[1] // 2
    held = gather_high(jnp.stack([summed[:, :size], summed[:, size:]]), high)
    whole = jnp.concatenate([held[0], held[1]], axis=1)
    opposite = swap(whole, "rep", 1)
    return (
        jnp.where(core == 0, whole, opposite).astype(F32),
        jnp.where(core == 0, opposite, whole).astype(F32),
    )


def solution(mesh):
    in_specs = (
        P(("rep", "dom"), None),
        P(("rep", "dom"), None),
        P("dom", None),
        P("dom", None),
        P(("rep", "dom"), None, None),
        P(("rep", "dom")),
        P(("rep", "dom")),
        P(("rep", "dom")),
    )
    out_specs = (P("dom", None), P("dom", None))
    return jax.shard_map(shards, mesh=mesh, in_specs=in_specs, out_specs=out_specs, check_vma=False)
```

time: 121 us -> 119 us (0.983)
  other arithmetic: 9.22 us -> 4.91 us
  starting transfers between devices: 27.8 us -> 29.9 us
    convert_element_type x6, other arithmetic: 5.27 us -> 2.66 us  [added(): return sum((term.astype(F32) for term in terms)).astype(BF16)]
    ppermute x14 -> x16, starting transfers between devices: 15.4 us -> 17.5 us  [swap(): lax.ppermute(value, axis, [(index, index ^ step) for index in range(size)])]
    ppermute x14 -> x16, waiting for transfers between devices: 43.4 us -> 45.2 us  [swap(): lax.ppermute(value, axis, [(index, index ^ step) for index in range(size)])]
    all_to_all x1, waiting for transfers between devices: 11.4 us -> 10 us  [shards(): lax.all_to_all(slots.reshape(dom_size, block, width), 'dom', split_axis=0...]
    unnamed x9 -> x11, local copies, waits for them, and re-layouts: 2.84 us -> 1.66 us
  transfers between devices with their start and end apart: 19 -> 21, of which waited for: 13 -> 11; matrix products, arithmetic and copies ran while one was open for 8% -> 5% of each run, Pallas kernels for 8% -> 8%
where the time goes in v11:
time: 119 us; the launch traced here: 118 us
  waiting for transfers between devices  57.5 us (48%)
  starting transfers between devices  29.9 us (25%)
  Pallas kernels  22.4 us (19%)
  other arithmetic  4.91 us (4%)
  local copies, waits for them, and re-layouts  2.67 us (2%)
    ppermute x16, waiting for transfers between devices, swap(): lax.ppermute(value, axis, [(index, index ^ step) for index in range(size)])  45.2 us
    ppermute x16, starting transfers between devices, swap(): lax.ppermute(value, axis, [(index, index ^ step) for index in range(size)])  17.5 us
    pallas_call x1, Pallas kernels, shards(): call(functools.partial(layer_kernel, sources, tiled), out_shapes, [SMEM,...  13.1 us
    all_to_all x1, waiting for transfers between devices, shards(): lax.all_to_all(slots.reshape(dom_size, block, width), 'dom', split_axis=0...  10 us
    ppermute x4, starting transfers between devices, cross(): lax.ppermute(value, ('rep', 'dom'), [(source, target) for source, target...  6.35 us
    all_to_all x1, starting transfers between devices, shards(): lax.all_to_all(slots.reshape(dom_size, block, width), 'dom', split_axis=0...  6.03 us
    pallas_call x1, Pallas kernels, shards(): call(self_kernel, jax.ShapeDtypeStruct((rows, hidden), BF16), [SMEM] + [H...  4.68 us
    pallas_call x1, Pallas kernels, shards(): call(slots_kernel, jax.ShapeDtypeStruct((dom_size * block, width), BF16),...  4.57 us
  transfers between devices with their start and end apart: 21, of which 11 were waited for; matrix products, arithmetic and copies ran while one was open for 5% of the time, Pallas kernels for 8%

profile of v11, /device:TPU:0, one launch (start us, length us, event | category | flops | bytes accessed | tf_op | source)
XLA Modules:
  0.0 118.2 jit_solution(17652886496637177380)
XLA Ops:
  0.6 1.0 dynamic-slice_bitcast_fusion.1
  2.3 3.1 %collective-permute-start.1 = (bf16[2,96,512]{2,1,0:T(8,128)(2,1)S(1)}, bf16[2,96,512]{2,1,0:T(8,128)(2,1)S(1)}, u32[]{:S(2)}, u32[]{:S(2)}) collective-permute-start(bf16[2,96,512]{2,1,0:T(8,128)(2,1)S(1)} %pad_maximum_fusion.4), channel_id=1, source_target_pairs={{0,2},{1,3},{2,0},{3,1},{4,6},{5,7},{6,4},{7,5},{8,11},{9,10},{10,... | collective-permute-start | bytes 589832 | tf_op jit(solution)/shard_map/ppermute | solution.py:31
  5.4 2.6 %collective-permute-start.2 = (bf16[2,96,512]{2,1,0:T(8,128)(2,1)S(1)}, bf16[2,96,512]{2,1,0:T(8,128)(2,1)S(1)}, u32[]{:S(2)}, u32[]{:S(2)}) collective-permute-start(bf16[2,96,512]{2,1,0:T(8,128)(2,1)S(1)} %pad_maximum_fusion.4), channel_id=1, source_target_pairs={{0,4},{1,5},{2,6},{3,7},{4,0},{5,1},{6,2},{7,3},{8,13},{9,12},{10,... | collective-permute-start | bytes 589832 | tf_op jit(solution)/shard_map/ppermute | solution.py:31
  8.0 4.6 %shard_map.95 = bf16[1024,768]{1,0:T(8,128)(2,1)} custom-call(s32[32]{0:T(128)} %src_hbm.1, s32[32]{0:T(128)} %peer_hbm.1, bf16[32,128,128]{2,1,0:T(8,128)(2,1)} %tiles_hbm.1, bf16[1024,768]{1,0:T(8,128)(2,1)} %features_hbm.3), custom_call_target="tpu_custom_call" | custom-call | flops 1610612736 | bytes 4194304 | tf_op jit(solution)/shard_map/pallas_call | solution.py:267
  12.6 6.0 %all-to-all-start = ((bf16[8,128,768]{2,1,0:T(8,128)(2,1)}), bf16[8,128,768]{2,1,0:T(8,128)(2,1)}, u32[]{:S(2)}, u32[]{:S(2)}) async-start(bf16[8,128,768]{2,1,0:T(8,128)(2,1)} %bitcast.55), calls=%async_computation | async-start | bytes 3145728 | tf_op jit(solution)/shard_map/all_to_all | solution.py:286
  18.6 2.2 %collective-permute-done.3 = bf16[2,96,512]{2,1,0:T(8,128)(2,1)S(1)} collective-permute-done((bf16[2,96,512]{2,1,0:T(8,128)(2,1)S(1)}, bf16[2,96,512]{2,1,0:T(8,128)(2,1)S(1)}, u32[]{:S(2)}, u32[]{:S(2)}) %collective-permute-start.3) | collective-permute-done | bytes 196640 | tf_op jit(solution)/shard_map/ppermute | solution.py:31
  21.1 1.6 %collective-permute-start.4 = (bf16[2,4,96,512]{3,2,1,0:T(8,128)(2,1)S(1)}, bf16[2,4,96,512]{3,2,1,0:T(8,128)(2,1)S(1)}, u32[]{:S(2)}, u32[]{:S(2)}) collective-permute-start(bf16[2,4,96,512]{3,2,1,0:T(8,128)(2,1)S(1)} %pad_maximum_fusion.1), channel_id=1, source_target_pairs={{0,16},{8,24},{16,0},{24,8},{1,17},{9,25},{17,1},{25,9},{2,18},{10... | collective-permute-start | bytes 2359304 | tf_op jit(solution)/shard_map/ppermute | solution.py:23
  22.7 16.4 %collective-permute-done.4 = bf16[2,4,96,512]{3,2,1,0:T(8,128)(2,1)S(1)} collective-permute-done((bf16[2,4,96,512]{3,2,1,0:T(8,128)(2,1)S(1)}, bf16[2,4,96,512]{3,2,1,0:T(8,128)(2,1)S(1)}, u32[]{:S(2)}, u32[]{:S(2)}) %collective-permute-start.4) | collective-permute-done | bytes 786464 | tf_op jit(solution)/shard_map/ppermute | solution.py:23
  39.4 2.8 %collective-permute-start.5 = (bf16[4,96,1024]{2,1,0:T(8,128)(2,1)S(1)}, bf16[4,96,1024]{2,1,0:T(8,128)(2,1)}, u32[]{:S(2)}, u32[]{:S(2)}) collective-permute-start(bf16[4,96,1024]{2,1,0:T(8,128)(2,1)S(1)} %get-tuple-element.27.refs_0_), channel_id=1, source_target_pairs={{0,8},{8,0},{16,24},{24,16},{1,9},{9,1},{17,25},{25,17},{2,10},{10... | collective-permute-start | bytes 2359304 | tf_op jit(solution)/shard_map/ppermute | solution.py:23
  42.3 1.6 %copy.13 = bf16[1024,768]{0,1:T(8,128)(2,1)} copy(bf16[1024,768]{1,0:T(8,128)(2,1)S(1)} %copy-done) | data formatting | bytes 3145728 | tf_op args[0]
  44.5 4.7 %shard_map.96.total_hbm = bf16[1024,1024]{1,0:T(8,128)(2,1)} custom-call(s32[1]{0:T(128)} %bitcast.1.flip_ref, bf16[1024,768]{1,0:T(8,128)(2,1)} %features_hbm.3, bf16[4,96,1024]{2,1,0:T(8,128)(2,1)} %copy-done.1, bf16[4,96,1024]{2,1,0:T(8,128)(2,1)} %collective-permute-done.5.refs_1_), custom_call_target="tpu_custom_call" | custom-call | tf_op jit(solution)/shard_map/pallas_call | solution.py:306
  49.2 10.0 %all-to-all-done.slots_ref = bf16[8,128,768]{2,1,0:T(8,128)(2,1)} async-done(((bf16[8,128,768]{2,1,0:T(8,128)(2,1)}), bf16[8,128,768]{2,1,0:T(8,128)(2,1)}, u32[]{:S(2)}, u32[]{:S(2)}) %all-to-all-start) | async-done | bytes 1572896 | tf_op jit(solution)/shard_map/all_to_all | solution.py:286
  59.2 13.1 %shard_map.97 = (bf16[4,96,512]{2,1,0:T(8,128)(2,1)}, bf16[4,96,512]{2,1,0:T(8,128)(2,1)}, bf16[768,256]{1,0:T(8,128)(2,1)}, bf16[768,256]{1,0:T(8,128)(2,1)}, b...) custom-call(s32[4]{0:T(128)} %pad_add_fusion.places_ref, ...), custom_call_target="tpu_custom_call" | custom-call | flops 4831838208 | bytes 16777216 | tf_op jit(solution)/shard_map/pallas_call | solution.py:332
  72.4 1.8 %collective-permute-start.12 = (bf16[768,256]{1,0:T(8,128)(2,1)}, bf16[768,256]{1,0:T(8,128)(2,1)S(1)}, u32[]{:S(2)}, u32[]{:S(2)}) collective-permute-start(bf16[768,256]{1,0:T(8,128)(2,1)} %get-tuple-element.25), channel_id=1, source_target_pairs={{0,8},{8,0},{16,24},{24,16},{1,9},{9,1},{17,25},{25,17},{2,10},{10... | collective-permute-start | bytes 1179656 | tf_op jit(solution)/shard_map/ppermute | solution.py:23
  74.7 1.0 collective-permute-done.12
  75.8 1.1 add_convert_fusion.1
  76.9 1.6 %collective-permute-start.13 = (bf16[768,256]{1,0:T(8,128)(2,1)S(1)}, bf16[768,256]{1,0:T(8,128)(2,1)S(1)}, u32[]{:S(2)}, u32[]{:S(2)}) collective-permute-start(bf16[768,256]{1,0:T(8,128)(2,1)S(1)} %add_convert_fusion.1), channel_id=1, source_target_pairs={{0,16},{8,24},{16,0},{24,8},{1,17},{9,25},{17,1},{25,9},{2,18},{10... | collective-permute-start | bytes 1179656 | tf_op jit(solution)/shard_map/ppermute | solution.py:23
  78.6 1.1 add_convert_fusion.3
  79.7 1.0 collective-permute-start.9
  80.7 7.7 %collective-permute-done.13 = bf16[768,256]{1,0:T(8,128)(2,1)S(1)} collective-permute-done((bf16[768,256]{1,0:T(8,128)(2,1)S(1)}, bf16[768,256]{1,0:T(8,128)(2,1)S(1)}, u32[]{:S(2)}, u32[]{:S(2)}) %collective-permute-start.13) | collective-permute-done | bytes 393248 | tf_op jit(solution)/shard_map/ppermute | solution.py:23
  88.5 0.9 collective-permute-start.14
  89.5 2.2 %collective-permute-done.9 = bf16[4,96,512]{2,1,0:T(8,128)(2,1)S(1)} collective-permute-done((bf16[4,96,512]{2,1,0:T(8,128)(2,1)S(1)}, bf16[4,96,512]{2,1,0:T(8,128)(2,1)S(1)}, u32[]{:S(2)}, u32[]{:S(2)}) %collective-permute-start.9) | collective-permute-done | bytes 393248 | tf_op jit(solution)/shard_map/ppermute | solution.py:23
  92.0 3.5 %collective-permute-done.14 = bf16[4,96,256]{2,1,0:T(8,128)(2,1)S(1)} collective-permute-done((bf16[4,96,256]{2,1,0:T(8,128)(2,1)S(1)}, bf16[4,96,256]{2,1,0:T(8,128)(2,1)S(1)}, u32[]{:S(2)}, u32[]{:S(2)}) %collective-permute-start.14) | collective-permute-done | bytes 196640 | tf_op jit(solution)/shard_map/ppermute | solution.py:23
  95.5 2.4 %collective-permute-done.10 = bf16[4,96,256]{2,1,0:T(8,128)(2,1)S(1)} collective-permute-done((bf16[4,96,256]{2,1,0:T(8,128)(2,1)S(1)}, bf16[4,96,256]{2,1,0:T(8,128)(2,1)S(1)}, u32[]{:S(2)}, u32[]{:S(2)}) %collective-permute-start.10) | collective-permute-done | bytes 196640 | tf_op jit(solution)/shard_map/ppermute | solution.py:23
  98.1 2.4 %collective-permute-start.15 = (bf16[96,512]{1,0:T(8,128)(2,1)S(1)}, bf16[96,512]{1,0:T(8,128)(2,1)S(1)}, u32[]{:S(2)}, u32[]{:S(2)}) collective-permute-start(bf16[96,512]{1,0:T(8,128)(2,1)S(1)} %get-tuple-element.36), channel_id=1, source_target_pairs={{0,2},{1,3},{2,0},{3,1},{4,6},{5,7},{6,4},{7,5},{8,10},{9,11},{10,... | collective-permute-start | bytes 294920 | tf_op jit(solution)/shard_map/ppermute | solution.py:23
  100.5 2.4 %collective-permute-start.16 = (bf16[96,512]{1,0:T(8,128)(2,1)S(1)}, bf16[96,512]{1,0:T(8,128)(2,1)S(1)}, u32[]{:S(2)}, u32[]{:S(2)}) collective-permute-start(bf16[96,512]{1,0:T(8,128)(2,1)S(1)} %get-tuple-element.37), channel_id=1, source_target_pairs={{0,4},{1,5},{2,6},{3,7},{4,0},{5,1},{6,2},{7,3},{8,12},{9,13},{10,... | collective-permute-start | bytes 294920 | tf_op jit(solution)/shard_map/ppermute | solution.py:23
  102.9 1.4 %collective-permute-start.17 = (bf16[96,512]{1,0:T(8,128)(2,1)S(1)}, bf16[96,512]{1,0:T(8,128)(2,1)S(1)}, u32[]{:S(2)}, u32[]{:S(2)}) collective-permute-start(bf16[96,512]{1,0:T(8,128)(2,1)S(1)} %get-tuple-element.38), channel_id=1, source_target_pairs={{0,6},{1,7},{2,4},{3,5},{4,2},{5,3},{6,0},{7,1},{8,14},{9,15},{10,... | collective-permute-start | bytes 294920 | tf_op jit(solution)/shard_map/ppermute | solution.py:23
  104.3 6.6 %collective-permute-done.16 = bf16[96,512]{1,0:T(8,128)(2,1)S(1)} collective-permute-done((bf16[96,512]{1,0:T(8,128)(2,1)S(1)}, bf16[96,512]{1,0:T(8,128)(2,1)S(1)}, u32[]{:S(2)}, u32[]{:S(2)}) %collective-permute-start.16) | collective-permute-done | bytes 98336 | tf_op jit(solution)/shard_map/ppermute | solution.py:23
  111.0 0.7 collective-permute-start.18
  111.7 4.0 %collective-permute-done.18 = bf16[2,96,256]{2,1,0:T(8,128)(2,1)S(1)} collective-permute-done((bf16[2,96,256]{2,1,0:T(8,128)(2,1)S(1)}, bf16[2,96,256]{2,1,0:T(8,128)(2,1)S(1)}, u32[]{:S(2)}, u32[]{:S(2)}) %collective-permute-start.18) | collective-permute-done | bytes 98336 | tf_op jit(solution)/shard_map/ppermute | solution.py:23
  115.8 1.4 %collective-permute-done.19 = bf16[96,1024]{1,0:T(8,128)(2,1)S(1)} collective-permute-done((bf16[96,1024]{1,0:T(8,128)(2,1)S(1)}, bf16[96,1024]{1,0:T(8,128)(2,1)S(1)}, u32[]{:S(2)}, u32[]{:S(2)}) %collective-permute-start.19) | collective-permute-done | bytes 196640 | tf_op jit(solution)/shard_map/ppermute | solution.py:23
  117.2 1.0 select_convert_fusion
  (49 shorter events, 3.3 us)
Async XLA Ops:
  1.6 17.0 %collective-permute-start = (bf16[2,96,512]{2,1,0:T(8,128)(2,1)S(1)}, bf16[2,96,512]{2,1,0:T(8,128)(2,1)S(1)}, u32[]{:S(2)}, u32[]{:S(2)}) collective-permute-start(bf16[2,96,512]{2,1,0:T(8,128)(2,1)S(1)} %pad_maximum_fusion.4), channel_id=1, source_target_pairs={{8,9},{9,8},{10,11},{11,10},{12,13},{13,12},{14,15},{15,14},{24,25... | collective-permute-start | bytes 589832 | tf_op jit(solution)/shard_map/ppermute | solution.py:31
  2.3 16.3 %collective-permute-start.1 = (bf16[2,96,512]{2,1,0:T(8,128)(2,1)S(1)}, bf16[2,96,512]{2,1,0:T(8,128)(2,1)S(1)}, u32[]{:S(2)}, u32[]{:S(2)}) collective-permute-start(bf16[2,96,512]{2,1,0:T(8,128)(2,1)S(1)} %pad_maximum_fusion.4), channel_id=1, source_target_pairs={{0,2},{1,3},{2,0},{3,1},{4,6},{5,7},{6,4},{7,5},{8,11},{9,10},{10,... | collective-permute-start | bytes 589832 | tf_op jit(solution)/shard_map/ppermute | solution.py:31
  5.4 13.2 %collective-permute-start.2 = (bf16[2,96,512]{2,1,0:T(8,128)(2,1)S(1)}, bf16[2,96,512]{2,1,0:T(8,128)(2,1)S(1)}, u32[]{:S(2)}, u32[]{:S(2)}) collective-permute-start(bf16[2,96,512]{2,1,0:T(8,128)(2,1)S(1)} %pad_maximum_fusion.4), channel_id=1, source_target_pairs={{0,4},{1,5},{2,6},{3,7},{4,0},{5,1},{6,2},{7,3},{8,13},{9,12},{10,... | collective-permute-start | bytes 589832 | tf_op jit(solution)/shard_map/ppermute | solution.py:31
  8.0 12.8 %collective-permute-start.3 = (bf16[2,96,512]{2,1,0:T(8,128)(2,1)S(1)}, bf16[2,96,512]{2,1,0:T(8,128)(2,1)S(1)}, u32[]{:S(2)}, u32[]{:S(2)}) collective-permute-start(bf16[2,96,512]{2,1,0:T(8,128)(2,1)S(1)} %pad_maximum_fusion.4), channel_id=1, source_target_pairs={{0,6},{1,7},{2,4},{3,5},{4,2},{5,3},{6,0},{7,1},{8,15},{9,14},{10,... | collective-permute-start | bytes 589832 | tf_op jit(solution)/shard_map/ppermute | solution.py:31
  12.6 46.7 %all-to-all-start = ((bf16[8,128,768]{2,1,0:T(8,128)(2,1)}), bf16[8,128,768]{2,1,0:T(8,128)(2,1)}, u32[]{:S(2)}, u32[]{:S(2)}) async-start(bf16[8,128,768]{2,1,0:T(8,128)(2,1)} %bitcast.55), calls=%async_computation | async-start | bytes 3145728 | tf_op jit(solution)/shard_map/all_to_all | solution.py:286
  21.1 18.0 %collective-permute-start.4 = (bf16[2,4,96,512]{3,2,1,0:T(8,128)(2,1)S(1)}, bf16[2,4,96,512]{3,2,1,0:T(8,128)(2,1)S(1)}, u32[]{:S(2)}, u32[]{:S(2)}) collective-permute-start(bf16[2,4,96,512]{3,2,1,0:T(8,128)(2,1)S(1)} %pad_maximum_fusion.1), channel_id=1, source_target_pairs={{0,16},{8,24},{16,0},{24,8},{1,17},{9,25},{17,1},{25,9},{2,18},{10... | collective-permute-start | bytes 2359304 | tf_op jit(solution)/shard_map/ppermute | solution.py:23
  39.2 3.1 %copy-start = (bf16[1024,768]{1,0:T(8,128)(2,1)S(1)}, bf16[1024,768]{1,0:T(8,128)(2,1)}, u32[]{:S(2)}) copy-start(bf16[1024,768]{1,0:T(8,128)(2,1)} %features_hbm.3) | copy-start | bytes 4718596
  39.4 4.5 %copy-start.1 = (bf16[4,96,1024]{2,1,0:T(8,128)(2,1)}, bf16[4,96,1024]{2,1,0:T(8,128)(2,1)S(1)}, u32[]{:S(2)}) copy-start(bf16[4,96,1024]{2,1,0:T(8,128)(2,1)S(1)} %get-tuple-element.27.refs_0_) | copy-start | bytes 2359300
  39.4 4.5 %copy-start.2 = (bf16[4,96,1024]{2,1,0:T(8,128)(2,1)}, bf16[4,96,1024]{2,1,0:T(8,128)(2,1)S(1)}, u32[]{:S(2)}) copy-start(bf16[4,96,1024]{2,1,0:T(8,128)(2,1)S(1)} %get-tuple-element.26.refs_0_) | copy-start | bytes 2359300
  39.4 5.1 %collective-permute-start.5 = (bf16[4,96,1024]{2,1,0:T(8,128)(2,1)S(1)}, bf16[4,96,1024]{2,1,0:T(8,128)(2,1)}, u32[]{:S(2)}, u32[]{:S(2)}) collective-permute-start(bf16[4,96,1024]{2,1,0:T(8,128)(2,1)S(1)} %get-tuple-element.27.refs_0_), channel_id=1, source_target_pairs={{0,8},{8,0},{16,24},{24,16},{1,9},{9,1},{17,25},{25,17},{2,10},{10... | collective-permute-start | bytes 2359304 | tf_op jit(solution)/shard_map/ppermute | solution.py:23
  42.2 7.0 %collective-permute-start.6 = (bf16[4,96,1024]{2,1,0:T(8,128)(2,1)S(1)}, bf16[4,96,1024]{2,1,0:T(8,128)(2,1)}, u32[]{:S(2)}, u32[]{:S(2)}) collective-permute-start(bf16[4,96,1024]{2,1,0:T(8,128)(2,1)S(1)} %get-tuple-element.26.refs_0_), channel_id=1, source_target_pairs={{0,8},{8,0},{16,24},{24,16},{1,9},{9,1},{17,25},{25,17},{2,10},{10... | collective-permute-start | bytes 2359304 | tf_op jit(solution)/shard_map/ppermute | solution.py:23
  72.4 16.0 %copy-start.4 = (bf16[768,256]{1,0:T(8,128)(2,1)S(1)}, bf16[768,256]{1,0:T(8,128)(2,1)}, u32[]{:S(2)}) copy-start(bf16[768,256]{1,0:T(8,128)(2,1)} %get-tuple-element.22) | copy-start | bytes 1179652
  72.4 3.4 %collective-permute-start.12 = (bf16[768,256]{1,0:T(8,128)(2,1)}, bf16[768,256]{1,0:T(8,128)(2,1)S(1)}, u32[]{:S(2)}, u32[]{:S(2)}) collective-permute-start(bf16[768,256]{1,0:T(8,128)(2,1)} %get-tuple-element.25), channel_id=1, source_target_pairs={{0,8},{8,0},{16,24},{24,16},{1,9},{9,1},{17,25},{25,17},{2,10},{10... | collective-permute-start | bytes 1179656 | tf_op jit(solution)/shard_map/ppermute | solution.py:23
  74.2 4.3 %collective-permute-start.8 = (bf16[4,96,512]{2,1,0:T(8,128)(2,1)}, bf16[4,96,512]{2,1,0:T(8,128)(2,1)S(1)}, u32[]{:S(2)}, u32[]{:S(2)}) collective-permute-start(bf16[4,96,512]{2,1,0:T(8,128)(2,1)} %get-tuple-element.21), channel_id=1, source_target_pairs={{0,8},{8,0},{16,24},{24,16},{1,9},{9,1},{17,25},{25,17},{2,10},{10... | collective-permute-start | bytes 1179656 | tf_op jit(solution)/shard_map/ppermute | solution.py:23
  74.3 6.4 %collective-permute-start.11 = (bf16[768,256]{1,0:T(8,128)(2,1)}, bf16[768,256]{1,0:T(8,128)(2,1)S(1)}, u32[]{:S(2)}, u32[]{:S(2)}) collective-permute-start(bf16[768,256]{1,0:T(8,128)(2,1)} %get-tuple-element.23), channel_id=1, source_target_pairs={{0,8},{8,0},{16,24},{24,16},{1,9},{9,1},{17,25},{25,17},{2,10},{10... | collective-permute-start | bytes 1179656 | tf_op jit(solution)/shard_map/ppermute | solution.py:23
  76.9 11.5 %collective-permute-start.13 = (bf16[768,256]{1,0:T(8,128)(2,1)S(1)}, bf16[768,256]{1,0:T(8,128)(2,1)S(1)}, u32[]{:S(2)}, u32[]{:S(2)}) collective-permute-start(bf16[768,256]{1,0:T(8,128)(2,1)S(1)} %add_convert_fusion.1), channel_id=1, source_target_pairs={{0,16},{8,24},{16,0},{24,8},{1,17},{9,25},{17,1},{25,9},{2,18},{10... | collective-permute-start | bytes 1179656 | tf_op jit(solution)/shard_map/ppermute | solution.py:23
  78.5 11.0 %collective-permute-start.7 = (bf16[4,96,512]{2,1,0:T(8,128)(2,1)}, bf16[4,96,512]{2,1,0:T(8,128)(2,1)S(1)}, u32[]{:S(2)}, u32[]{:S(2)}) collective-permute-start(bf16[4,96,512]{2,1,0:T(8,128)(2,1)} %get-tuple-element.19), channel_id=1, source_target_pairs={{0,8},{8,0},{16,24},{24,16},{1,9},{9,1},{17,25},{25,17},{2,10},{10... | collective-permute-start | bytes 1179656 | tf_op jit(solution)/shard_map/ppermute | solution.py:23
  78.6 13.1 %copy-start.3 = (bf16[4,96,512]{2,1,0:T(8,128)(2,1)S(1)}, bf16[4,96,512]{2,1,0:T(8,128)(2,1)}, u32[]{:S(2)}) copy-start(bf16[4,96,512]{2,1,0:T(8,128)(2,1)} %get-tuple-element.18) | copy-start | bytes 1179652
  79.7 12.0 %collective-permute-start.9 = (bf16[4,96,512]{2,1,0:T(8,128)(2,1)S(1)}, bf16[4,96,512]{2,1,0:T(8,128)(2,1)S(1)}, u32[]{:S(2)}, u32[]{:S(2)}) collective-permute-start(bf16[4,96,512]{2,1,0:T(8,128)(2,1)S(1)} %add_convert_fusion.3), channel_id=1, source_target_pairs={{0,1},{1,0},{2,3},{3,2},{4,5},{5,4},{6,7},{7,6},{8,9},{9,8},{10,11... | collective-permute-start | bytes 1179656 | tf_op jit(solution)/shard_map/ppermute | solution.py:23
  88.5 6.9 %collective-permute-start.14 = (bf16[4,96,256]{2,1,0:T(8,128)(2,1)S(1)}, bf16[4,96,256]{2,1,0:T(8,128)(2,1)S(1)}, u32[]{:S(2)}, u32[]{:S(2)}) collective-permute-start(bf16[4,96,256]{2,1,0:T(8,128)(2,1)S(1)} %dynamic-slice_bitcast_fusion), channel_id=1, source_target_pairs={{0,1},{1,0},{2,3},{3,2},{4,5},{5,4},{6,7},{7,6},{8,9},{9,8},{10,11... | collective-permute-start | bytes 589832 | tf_op jit(solution)/shard_map/ppermute | solution.py:23
  91.9 6.1 %collective-permute-start.10 = (bf16[4,96,256]{2,1,0:T(8,128)(2,1)S(1)}, bf16[4,96,256]{2,1,0:T(8,128)(2,1)S(1)}, u32[]{:S(2)}, u32[]{:S(2)}) collective-permute-start(bf16[4,96,256]{2,1,0:T(8,128)(2,1)S(1)} %constant_dynamic-slice_fusion), channel_id=1, source_target_pairs={{0,16},{8,24},{16,0},{24,8},{1,17},{9,25},{17,1},{25,9},{2,18},{10... | collective-permute-start | bytes 589832 | tf_op jit(solution)/shard_map/ppermute | solution.py:23
  98.1 6.2 %collective-permute-start.15 = (bf16[96,512]{1,0:T(8,128)(2,1)S(1)}, bf16[96,512]{1,0:T(8,128)(2,1)S(1)}, u32[]{:S(2)}, u32[]{:S(2)}) collective-permute-start(bf16[96,512]{1,0:T(8,128)(2,1)S(1)} %get-tuple-element.36), channel_id=1, source_target_pairs={{0,2},{1,3},{2,0},{3,1},{4,6},{5,7},{6,4},{7,5},{8,10},{9,11},{10,... | collective-permute-start | bytes 294920 | tf_op jit(solution)/shard_map/ppermute | solution.py:23
  100.5 10.4 %collective-permute-start.16 = (bf16[96,512]{1,0:T(8,128)(2,1)S(1)}, bf16[96,512]{1,0:T(8,128)(2,1)S(1)}, u32[]{:S(2)}, u32[]{:S(2)}) collective-permute-start(bf16[96,512]{1,0:T(8,128)(2,1)S(1)} %get-tuple-element.37), channel_id=1, source_target_pairs={{0,4},{1,5},{2,6},{3,7},{4,0},{5,1},{6,2},{7,3},{8,12},{9,13},{10,... | collective-permute-start | bytes 294920 | tf_op jit(solution)/shard_map/ppermute | solution.py:23
  102.9 8.0 %collective-permute-start.17 = (bf16[96,512]{1,0:T(8,128)(2,1)S(1)}, bf16[96,512]{1,0:T(8,128)(2,1)S(1)}, u32[]{:S(2)}, u32[]{:S(2)}) collective-permute-start(bf16[96,512]{1,0:T(8,128)(2,1)S(1)} %get-tuple-element.38), channel_id=1, source_target_pairs={{0,6},{1,7},{2,4},{3,5},{4,2},{5,3},{6,0},{7,1},{8,14},{9,15},{10,... | collective-permute-start | bytes 294920 | tf_op jit(solution)/shard_map/ppermute | solution.py:23
  111.0 4.7 %collective-permute-start.18 = (bf16[2,96,256]{2,1,0:T(8,128)(2,1)S(1)}, bf16[2,96,256]{2,1,0:T(8,128)(2,1)S(1)}, u32[]{:S(2)}, u32[]{:S(2)}) collective-permute-start(bf16[2,96,256]{2,1,0:T(8,128)(2,1)S(1)} %pad_maximum_fusion.7), channel_id=1, source_target_pairs={{0,16},{8,24},{16,0},{24,8},{1,17},{9,25},{17,1},{25,9},{2,18},{10... | collective-permute-start | bytes 294920 | tf_op jit(solution)/shard_map/ppermute | solution.py:23
  115.7 1.5 %collective-permute-start.19 = (bf16[96,1024]{1,0:T(8,128)(2,1)S(1)}, bf16[96,1024]{1,0:T(8,128)(2,1)S(1)}, u32[]{:S(2)}, u32[]{:S(2)}) collective-permute-start(bf16[96,1024]{1,0:T(8,128)(2,1)S(1)} %pad_maximum_fusion.5), channel_id=1, source_target_pairs={{0,8},{8,0},{16,24},{24,16},{1,9},{9,1},{17,25},{25,17},{2,10},{10... | collective-permute-start | bytes 589832 | tf_op jit(solution)/shard_map/ppermute | solution.py:23

commit v12 on v11

--- a/solution.py
+++ b/solution.py
@@ -113,11 +113,11 @@
 
 
 def layer_kernel(
-    sources, pieces, places_ref, into_ref, slots_ref, total_hbm, turned_hbm, cotangent_hbm, *refs
+    sources, pieces, places_ref, into_ref, slots_ref, total_hbm, features_hbm, cotangent_hbm, *refs
 ):
-    weight_hbms, out_hbms = refs[:sources], refs[sources:-15]
-    total, turned, cotangent, weight, summed, values, aggregate, left, grad, first, second = refs[-15:-4]
-    row_sems, weight_sems, turned_sems, out_sems = refs[-4:]
+    weight_hbms, out_hbms = refs[:sources], refs[sources:-14]
+    total, features, cotangent, weight, summed, values, aggregate, grad, first, second = refs[-14:-4]
+    row_sems, weight_sems, feature_sems, out_sems = refs[-4:]
     senders, block, _ = slots_ref.shape
     rows, hidden = grad.shape
     width = aggregate.shape[1]
@@ -127,8 +127,8 @@
     weights = weight_copies(flip, weight_hbms, weight, weight_sems)
     totals = split_copies(total_hbm, total, row_sems.at[0], parts)
     cotangents = split_copies(cotangent_hbm, cotangent, row_sems.at[1], parts)
-    turnings = split_copies(turned_hbm, turned, turned_sems)
-    for copy in weights + totals + cotangents + turnings:
+    inputs = split_copies(features_hbm, features, feature_sems)
+    for copy in weights + totals + cotangents + inputs:
         copy.start()
 
     summed[...] = jnp.zeros_like(summed)
@@ -136,7 +136,6 @@
         at = pl.ds(pl.multiple_of(into_ref[sender] * block, block), block)
         summed[at, :] = summed[at, :] + slots_ref[sender].astype(F32)
     aggregate[...] = summed[...].astype(BF16)
-    left[...] = aggregate[...].T
     for copy in weights:
         copy.wait()
     span = hidden // 2
@@ -166,7 +165,7 @@
                 inner = value * (square * (1.5 * SCALE * CUBIC) + 0.5 * SCALE)
                 grad[at, columns] = cotangent[at, columns] * ((1.0 + bend) * (inner * (1.0 - bend) + 0.5))
 
-    for copy in turnings:
+    for copy in inputs:
         copy.wait()
     results = []
 
@@ -174,9 +173,10 @@
         results.append(pltpu.make_async_copy(source, target, out_sems.at[len(results)]))
         results[-1].start()
 
-    for index, operand in enumerate([turned, left]):
-        product = jnp.dot(operand[...], grad[:, :span], preferred_element_type=F32).astype(BF16)
-        first[index] = product.reshape(first.shape[1:])
+    contract = (((0,), (0,)), ((), ()))
+    for index, operand in enumerate([features, aggregate]):
+        product = lax.dot_general(operand[...], grad[:, :span], contract, preferred_element_type=F32)
+        first[index] = product.astype(BF16).reshape(first.shape[1:])
     for term, which in enumerate([1 - core, core]):
         if pieces:
             for leave, bit in enumerate([1 - low, low]):
@@ -184,10 +184,10 @@
                     send(first.at[which, 2 * row + bit], out_hbms[4 * term + leave].at[row])
         else:
             send(first.at[which], out_hbms[4 * term])
-    for index, operand in enumerate([turned, left]):
+    for index, operand in enumerate([features, aggregate]):
+        product = lax.dot_general(operand[...], grad[:, span:], contract, preferred_element_type=F32).astype(BF16)
         for side in range(2):
-            columns = slice(span + side * span // 2, span + (side + 1) * span // 2)
-            second[index, side] = jnp.dot(operand[...], grad[:, columns], preferred_element_type=F32).astype(BF16)
+            second[index, side] = product[:, side * span // 2 : (side + 1) * span // 2]
     for term, which in enumerate([1 - core, core]):
         for leave, bit in enumerate([1 - upper, upper]):
             send(second.at[which, bit], out_hbms[4 * term + 2 + leave])
@@ -262,8 +262,9 @@
     low, place = me & 1, me >> 1
 
     share = hidden // parts
+    top = dom_size // 2
     held = jnp.stack([lax.dynamic_slice_in_dim(weight, high * share, share, 1) for weight in (w_self, w_neigh)])
-    pieces = [cross(held, 2 * step) for step in range(dom_size // 2)]
+    near, far = cross(held, 0), cross(held, top)
     slots = call(
         slots_kernel,
         jax.ShapeDtypeStruct((dom_size * block, width), BF16),
@@ -282,19 +283,15 @@
         flops=2 * dom_size * block * rows * width,
         moved=tile_vals.size * 2 + rows * width * 4,
     )(tile_src, tile_peer, tile_vals, features)
-    *pieces, _ = lax.optimization_barrier((*pieces, slots))
+    near, far, slots = lax.optimization_barrier((near, far, slots))
+    held = joined(jnp.where(core == 0, held, near), far, (me & top) != 0, 1)
+    step = top // 2
+    while step > 1:
+        held = joined(held, swap(held, "dom", step), (me & step) != 0, 2)
+        held = held.reshape(2, -1, *held.shape[3:])
+        step //= 2
     received = lax.all_to_all(slots.reshape(dom_size, block, width), "dom", split_axis=0, concat_axis=0, tiled=True)
-    pieces[0] = jnp.where(core == 0, held, pieces[0])
-    pieces = [piece[:, None] for piece in pieces]
-    bit = 1
-    while len(pieces) > 1:
-        upper = (place & bit) != 0
-        pieces = [
-            jnp.concatenate([jnp.where(upper, b, a), jnp.where(upper, a, b)], axis=1)
-            for a, b in zip(pieces[::2], pieces[1::2])
-        ]
-        bit *= 2
-    mine = gather_high(pieces[0], high)
+    mine = gather_high(held, high)
     depth = width // dom_size
     tiled = depth % 16 == 0
     flip = low ^ core
@@ -316,9 +313,9 @@
             DMA((count,)),
             DMA((rows // 256,)),
         ],
+        flops=2 * rows * width * hidden,
+        moved=7 * rows * hidden,
     )(flip.astype(jnp.int32).reshape(1), features, *weights[0])
-    turned = features.T
-
     span = hidden // 2
     upper = (high // (parts // 2)) % 2
     places = jnp.stack([core, flip, low, upper]).astype(jnp.int32)
@@ -336,13 +333,12 @@
         [HBM] * 8,
         [
             pltpu.VMEM((rows, hidden), BF16),
-            pltpu.VMEM((width, rows), BF16),
+            pltpu.VMEM((rows, width), BF16),
             pltpu.VMEM((rows, hidden), BF16),
             weight_shape,
             pltpu.VMEM((rows, width), F32),
             pltpu.VMEM((2, 256, hidden), F32),
             pltpu.VMEM((rows, width), BF16),
-            pltpu.VMEM((width, rows), BF16),
             pltpu.VMEM((rows, hidden), BF16),
             pltpu.VMEM(first_scratch, BF16),
             pltpu.VMEM((2, 2, width, span // 2), BF16),
@@ -353,7 +349,7 @@
         ],
         flops=6 * rows * width * hidden,
         moved=16 * rows * hidden,
-    )(places, in_block, received, total, turned, cotangent, *weights[1])
+    )(places, in_block, received, total, features, cotangent, *weights[1])
     outs = list(outs)
     if not tiled:
         for at in (0, 4):

time: 119 us -> 117 us (0.983)
  starting transfers between devices: 29.9 us -> 26 us
  waiting for transfers between devices: 57.5 us -> 60.3 us
    ppermute x16 -> x17, waiting for transfers between devices: 45.2 us -> 51.3 us  [swap(): lax.ppermute(value, axis, [(index, index ^ step) for index in range(size)])]
    all_to_all x1, waiting for transfers between devices: 10 us -> 5.09 us  [shards(): lax.all_to_all(slots.reshape(dom_size, block, width), 'dom', split_axis=0...]
    ppermute x16 -> x17, starting transfers between devices: 17.5 us -> 15.7 us  [swap(): lax.ppermute(value, axis, [(index, index ^ step) for index in range(size)])]
    ppermute x4 -> x2, waiting for transfers between devices: 2.22 us -> 3.89 us  [cross(): lax.ppermute(value, ('rep', 'dom'), [(source, target) for source, target...]
    ppermute x4 -> x2, starting transfers between devices: 6.35 us -> 4.77 us  [cross(): lax.ppermute(value, ('rep', 'dom'), [(source, target) for source, target...]
  transfers between devices with their start and end apart: 21 -> 20, of which waited for: 11 -> 15; matrix products, arithmetic and copies ran while one was open for 5% -> 3% of each run, Pallas kernels for 8% -> 8%
where the time goes in v12:
time: 117 us; the launch traced here: 116 us
  waiting for transfers between devices  60.3 us (52%)
  starting transfers between devices  26 us (22%)
  Pallas kernels  22.1 us (19%)
  other arithmetic  4.86 us (4%)
  local copies, waits for them, and re-layouts  2.17 us (2%)
    ppermute x17, waiting for transfers between devices, swap(): lax.ppermute(value, axis, [(index, index ^ step) for index in range(size)])  51.3 us
    ppermute x17, starting transfers between devices, swap(): lax.ppermute(value, axis, [(index, index ^ step) for index in range(size)])  15.7 us
    pallas_call x1, Pallas kernels, shards(): call(functools.partial(layer_kernel, sources, tiled), out_shapes, [SMEM,...  12.8 us
    all_to_all x1, starting transfers between devices, shards(): lax.all_to_all(slots.reshape(dom_size, block, width), 'dom', split_axis=0...  5.58 us
    all_to_all x1, waiting for transfers between devices, shards(): lax.all_to_all(slots.reshape(dom_size, block, width), 'dom', split_axis=0...  5.09 us
    ppermute x2, starting transfers between devices, cross(): lax.ppermute(value, ('rep', 'dom'), [(source, target) for source, target...  4.77 us
    pallas_call x1, Pallas kernels, shards(): call(self_kernel, jax.ShapeDtypeStruct((rows, hidden), BF16), [SMEM] + [H...  4.67 us
    pallas_call x1, Pallas kernels, shards(): call(slots_kernel, jax.ShapeDtypeStruct((dom_size * block, width), BF16),...  4.55 us
  transfers between devices with their start and end apart: 20, of which 15 were waited for; matrix products, arithmetic and copies ran while one was open for 3% of the time, Pallas kernels for 8%

profile of v12, /device:TPU:0, one launch (start us, length us, event | category | flops | bytes accessed | tf_op | source)
XLA Modules:
  0.0 116.3 jit_solution(11986395758861762389)
XLA Ops:
  0.6 1.0 dynamic-slice_bitcast_fusion.1
  2.3 4.1 %collective-permute-start.1 = (bf16[2,96,512]{2,1,0:T(8,128)(2,1)S(1)}, bf16[2,96,512]{2,1,0:T(8,128)(2,1)S(1)}, u32[]{:S(2)}, u32[]{:S(2)}) collective-permute-start(bf16[2,96,512]{2,1,0:T(8,128)(2,1)S(1)} %pad_maximum_fusion.3), channel_id=1, source_target_pairs={{0,4},{1,5},{2,6},{3,7},{4,0},{5,1},{6,2},{7,3},{8,13},{9,12},{10,... | collective-permute-start | bytes 589832 | tf_op jit(solution)/shard_map/ppermute | solution.py:31
  6.4 4.6 %shard_map.95 = bf16[1024,768]{1,0:T(8,128)(2,1)} custom-call(s32[32]{0:T(128)} %src_hbm.1, s32[32]{0:T(128)} %peer_hbm.1, bf16[32,128,128]{2,1,0:T(8,128)(2,1)} %tiles_hbm.1, bf16[1024,768]{1,0:T(8,128)(2,1)} %features_hbm.5), custom_call_target="tpu_custom_call" | custom-call | flops 1610612736 | bytes 4194304 | tf_op jit(solution)/shard_map/pallas_call | solution.py:268
  11.0 3.9 %collective-permute-done.1 = bf16[2,96,512]{2,1,0:T(8,128)(2,1)S(1)} collective-permute-done((bf16[2,96,512]{2,1,0:T(8,128)(2,1)S(1)}, bf16[2,96,512]{2,1,0:T(8,128)(2,1)S(1)}, u32[]{:S(2)}, u32[]{:S(2)}) %collective-permute-start.1) | collective-permute-done | bytes 196640 | tf_op jit(solution)/shard_map/ppermute | solution.py:31
  15.0 2.5 %collective-permute-start.2 = (bf16[2,2,96,512]{3,2,1,0:T(8,128)(2,1)S(1)}, bf16[2,2,96,512]{3,2,1,0:T(8,128)(2,1)S(1)}, u32[]{:S(2)}, u32[]{:S(2)}) collective-permute-start(bf16[2,2,96,512]{3,2,1,0:T(8,128)(2,1)S(1)} %pad_maximum_fusion.2), channel_id=1, source_target_pairs={{0,2},{1,3},{2,0},{3,1},{4,6},{5,7},{6,4},{7,5},{8,10},{9,11},{10,... | collective-permute-start | bytes 1179656 | tf_op jit(solution)/shard_map/ppermute | solution.py:23
  17.4 5.6 %all-to-all-start = ((bf16[8,128,768]{2,1,0:T(8,128)(2,1)}), bf16[8,128,768]{2,1,0:T(8,128)(2,1)S(1)}, u32[]{:S(2)}, u32[]{:S(2)}) async-start(bf16[8,128,768]{2,1,0:T(8,128)(2,1)} %bitcast.6), calls=%async_computation | async-start | bytes 3145728 | tf_op jit(solution)/shard_map/all_to_all | solution.py:293
  23.0 3.8 %collective-permute-done.2 = bf16[2,2,96,512]{3,2,1,0:T(8,128)(2,1)S(1)} collective-permute-done((bf16[2,2,96,512]{3,2,1,0:T(8,128)(2,1)S(1)}, bf16[2,2,96,512]{3,2,1,0:T(8,128)(2,1)S(1)}, u32[]{:S(2)}, u32[]{:S(2)}) %collective-permute-start.2) | collective-permute-done | bytes 393248 | tf_op jit(solution)/shard_map/ppermute | solution.py:23
  27.0 1.6 %collective-permute-start.3 = (bf16[2,4,96,512]{3,2,1,0:T(8,128)(2,1)S(1)}, bf16[2,4,96,512]{3,2,1,0:T(8,128)(2,1)S(1)}, u32[]{:S(2)}, u32[]{:S(2)}) collective-permute-start(bf16[2,4,96,512]{3,2,1,0:T(8,128)(2,1)S(1)} %bitcast.53), channel_id=1, source_target_pairs={{0,16},{8,24},{16,0},{24,8},{1,17},{9,25},{17,1},{25,9},{2,18},{10... | collective-permute-start | bytes 2359304 | tf_op jit(solution)/shard_map/ppermute | solution.py:23
  28.6 18.4 %collective-permute-done.3 = bf16[2,4,96,512]{3,2,1,0:T(8,128)(2,1)S(1)} collective-permute-done((bf16[2,4,96,512]{3,2,1,0:T(8,128)(2,1)S(1)}, bf16[2,4,96,512]{3,2,1,0:T(8,128)(2,1)S(1)}, u32[]{:S(2)}, u32[]{:S(2)}) %collective-permute-start.3) | collective-permute-done | bytes 786464 | tf_op jit(solution)/shard_map/ppermute | solution.py:23
  48.6 1.4 %collective-permute-done.4.refs_1_ = bf16[4,96,1024]{2,1,0:T(8,128)(2,1)} collective-permute-done((bf16[4,96,1024]{2,1,0:T(8,128)(2,1)S(1)}, bf16[4,96,1024]{2,1,0:T(8,128)(2,1)}, u32[]{:S(2)}, u32[]{:S(2)}) %collective-permute-start.4) | collective-permute-done | bytes 786464 | tf_op jit(solution)/shard_map/ppermute | solution.py:23
  50.0 4.7 %shard_map.96.total_hbm = bf16[1024,1024]{1,0:T(8,128)(2,1)} custom-call(s32[1]{0:T(128)} %bitcast.1.flip_ref, bf16[1024,768]{1,0:T(8,128)(2,1)} %features_hbm.5, bf16[4,96,1024]{2,1,0:T(8,128)(2,1)} %copy-done.2, bf16[4,96,1024]{2,1,0:T(8,128)(2,1)} %collective-permute-done.4.refs_1_), custom_call_target="tpu_custom_call" | custom-call | flops 1610612736 | bytes 7340032 | tf_op jit(solution)/shard_map/pallas_call | solution.py:303
  54.7 5.1 %all-to-all-done.slots_ref = bf16[8,128,768]{2,1,0:T(8,128)(2,1)S(1)} async-done(((bf16[8,128,768]{2,1,0:T(8,128)(2,1)}), bf16[8,128,768]{2,1,0:T(8,128)(2,1)S(1)}, u32[]{:S(2)}, u32[]{:S(2)}) %all-to-all-start) | async-done | bytes 1572896 | tf_op jit(solution)/shard_map/all_to_all | solution.py:293
  59.8 1.1 copy-done
  61.0 12.8 %shard_map.97 = (bf16[4,96,512]{2,1,0:T(8,128)(2,1)}, bf16[4,96,512]{2,1,0:T(8,128)(2,1)}, bf16[768,256]{1,0:T(8,128)(2,1)}, bf16[768,256]{1,0:T(8,128)(2,1)}, b...) custom-call(s32[4]{0:T(128)} %pad_add_fusion.places_ref, ...), custom_call_target="tpu_custom_call" | custom-call | flops 4831838208 | bytes 16777216 | tf_op jit(solution)/shard_map/pallas_call | solution.py:329
  74.5 1.3 %collective-permute-done.11 = bf16[768,256]{1,0:T(8,128)(2,1)S(1)} collective-permute-done((bf16[768,256]{1,0:T(8,128)(2,1)}, bf16[768,256]{1,0:T(8,128)(2,1)S(1)}, u32[]{:S(2)}, u32[]{:S(2)}) %collective-permute-start.11) | collective-permute-done | bytes 393248 | tf_op jit(solution)/shard_map/ppermute | solution.py:23
  75.8 1.1 add_convert_fusion.1
  76.9 1.6 %collective-permute-start.12 = (bf16[768,256]{1,0:T(8,128)(2,1)S(1)}, bf16[768,256]{1,0:T(8,128)(2,1)S(1)}, u32[]{:S(2)}, u32[]{:S(2)}) collective-permute-start(bf16[768,256]{1,0:T(8,128)(2,1)S(1)} %add_convert_fusion.1), channel_id=1, source_target_pairs={{0,16},{8,24},{16,0},{24,8},{1,17},{9,25},{17,1},{25,9},{2,18},{10... | collective-permute-start | bytes 1179656 | tf_op jit(solution)/shard_map/ppermute | solution.py:23
  78.5 1.1 add_convert_fusion.3
  79.7 1.5 %collective-permute-start.8 = (bf16[4,96,512]{2,1,0:T(8,128)(2,1)S(1)}, bf16[4,96,512]{2,1,0:T(8,128)(2,1)S(1)}, u32[]{:S(2)}, u32[]{:S(2)}) collective-permute-start(bf16[4,96,512]{2,1,0:T(8,128)(2,1)S(1)} %add_convert_fusion.3), channel_id=1, source_target_pairs={{0,1},{1,0},{2,3},{3,2},{4,5},{5,4},{6,7},{7,6},{8,9},{9,8},{10,11... | collective-permute-start | bytes 1179656 | tf_op jit(solution)/shard_map/ppermute | solution.py:23
  81.2 6.9 %collective-permute-done.12 = bf16[768,256]{1,0:T(8,128)(2,1)S(1)} collective-permute-done((bf16[768,256]{1,0:T(8,128)(2,1)S(1)}, bf16[768,256]{1,0:T(8,128)(2,1)S(1)}, u32[]{:S(2)}, u32[]{:S(2)}) %collective-permute-start.12) | collective-permute-done | bytes 393248 | tf_op jit(solution)/shard_map/ppermute | solution.py:23
  88.3 1.5 %collective-permute-start.13 = (bf16[4,96,256]{2,1,0:T(8,128)(2,1)S(1)}, bf16[4,96,256]{2,1,0:T(8,128)(2,1)S(1)}, u32[]{:S(2)}, u32[]{:S(2)}) collective-permute-start(bf16[4,96,256]{2,1,0:T(8,128)(2,1)S(1)} %dynamic-slice_bitcast_fusion), channel_id=1, source_target_pairs={{0,1},{1,0},{2,3},{3,2},{4,5},{5,4},{6,7},{7,6},{8,9},{9,8},{10,11... | collective-permute-start | bytes 589832 | tf_op jit(solution)/shard_map/ppermute | solution.py:23
  89.9 1.8 %collective-permute-done.8 = bf16[4,96,512]{2,1,0:T(8,128)(2,1)S(1)} collective-permute-done((bf16[4,96,512]{2,1,0:T(8,128)(2,1)S(1)}, bf16[4,96,512]{2,1,0:T(8,128)(2,1)S(1)}, u32[]{:S(2)}, u32[]{:S(2)}) %collective-permute-start.8) | collective-permute-done | bytes 393248 | tf_op jit(solution)/shard_map/ppermute | solution.py:23
  92.0 3.5 %collective-permute-done.13 = bf16[4,96,256]{2,1,0:T(8,128)(2,1)S(1)} collective-permute-done((bf16[4,96,256]{2,1,0:T(8,128)(2,1)S(1)}, bf16[4,96,256]{2,1,0:T(8,128)(2,1)S(1)}, u32[]{:S(2)}, u32[]{:S(2)}) %collective-permute-start.13) | collective-permute-done | bytes 196640 | tf_op jit(solution)/shard_map/ppermute | solution.py:23
  95.5 2.5 %collective-permute-done.9 = bf16[4,96,256]{2,1,0:T(8,128)(2,1)S(1)} collective-permute-done((bf16[4,96,256]{2,1,0:T(8,128)(2,1)S(1)}, bf16[4,96,256]{2,1,0:T(8,128)(2,1)S(1)}, u32[]{:S(2)}, u32[]{:S(2)}) %collective-permute-start.9) | collective-permute-done | bytes 196640 | tf_op jit(solution)/shard_map/ppermute | solution.py:23
  98.2 4.2 %collective-permute-start.15 = (bf16[96,512]{1,0:T(8,128)(2,1)S(1)}, bf16[96,512]{1,0:T(8,128)(2,1)S(1)}, u32[]{:S(2)}, u32[]{:S(2)}) collective-permute-start(bf16[96,512]{1,0:T(8,128)(2,1)S(1)} %get-tuple-element.35), channel_id=1, source_target_pairs={{0,4},{1,5},{2,6},{3,7},{4,0},{5,1},{6,2},{7,3},{8,12},{9,13},{10,... | collective-permute-start | bytes 294920 | tf_op jit(solution)/shard_map/ppermute | solution.py:23
  102.6 0.8 collective-permute-done.14
  103.4 4.4 %collective-permute-done.15 = bf16[96,512]{1,0:T(8,128)(2,1)S(1)} collective-permute-done((bf16[96,512]{1,0:T(8,128)(2,1)S(1)}, bf16[96,512]{1,0:T(8,128)(2,1)S(1)}, u32[]{:S(2)}, u32[]{:S(2)}) %collective-permute-start.15) | collective-permute-done | bytes 98336 | tf_op jit(solution)/shard_map/ppermute | solution.py:23
  107.8 1.2 %collective-permute-done.16 = bf16[96,512]{1,0:T(8,128)(2,1)S(1)} collective-permute-done((bf16[96,512]{1,0:T(8,128)(2,1)S(1)}, bf16[96,512]{1,0:T(8,128)(2,1)S(1)}, u32[]{:S(2)}, u32[]{:S(2)}) %collective-permute-start.16) | collective-permute-done | bytes 98336 | tf_op jit(solution)/shard_map/ppermute | solution.py:23
  109.1 0.8 collective-permute-start.17
  109.9 3.8 %collective-permute-done.17 = bf16[2,96,256]{2,1,0:T(8,128)(2,1)S(1)} collective-permute-done((bf16[2,96,256]{2,1,0:T(8,128)(2,1)S(1)}, bf16[2,96,256]{2,1,0:T(8,128)(2,1)S(1)}, u32[]{:S(2)}, u32[]{:S(2)}) %collective-permute-start.17) | collective-permute-done | bytes 98336 | tf_op jit(solution)/shard_map/ppermute | solution.py:23
  113.9 1.4 %collective-permute-done.18 = bf16[96,1024]{1,0:T(8,128)(2,1)S(1)} collective-permute-done((bf16[96,1024]{1,0:T(8,128)(2,1)S(1)}, bf16[96,1024]{1,0:T(8,128)(2,1)S(1)}, u32[]{:S(2)}, u32[]{:S(2)}) %collective-permute-start.18) | collective-permute-done | bytes 196640 | tf_op jit(solution)/shard_map/ppermute | solution.py:23
  115.3 1.0 select_convert_fusion
  (46 shorter events, 4.4 us)
Async XLA Ops:
  1.6 9.3 %collective-permute-start = (bf16[2,96,512]{2,1,0:T(8,128)(2,1)S(1)}, bf16[2,96,512]{2,1,0:T(8,128)(2,1)S(1)}, u32[]{:S(2)}, u32[]{:S(2)}) collective-permute-start(bf16[2,96,512]{2,1,0:T(8,128)(2,1)S(1)} %pad_maximum_fusion.3), channel_id=1, source_target_pairs={{8,9},{9,8},{10,11},{11,10},{12,13},{13,12},{14,15},{15,14},{24,25... | collective-permute-start | bytes 589832 | tf_op jit(solution)/shard_map/ppermute | solution.py:31
  2.3 12.6 %collective-permute-start.1 = (bf16[2,96,512]{2,1,0:T(8,128)(2,1)S(1)}, bf16[2,96,512]{2,1,0:T(8,128)(2,1)S(1)}, u32[]{:S(2)}, u32[]{:S(2)}) collective-permute-start(bf16[2,96,512]{2,1,0:T(8,128)(2,1)S(1)} %pad_maximum_fusion.3), channel_id=1, source_target_pairs={{0,4},{1,5},{2,6},{3,7},{4,0},{5,1},{6,2},{7,3},{8,13},{9,12},{10,... | collective-permute-start | bytes 589832 | tf_op jit(solution)/shard_map/ppermute | solution.py:31
  15.0 11.9 %collective-permute-start.2 = (bf16[2,2,96,512]{3,2,1,0:T(8,128)(2,1)S(1)}, bf16[2,2,96,512]{3,2,1,0:T(8,128)(2,1)S(1)}, u32[]{:S(2)}, u32[]{:S(2)}) collective-permute-start(bf16[2,2,96,512]{3,2,1,0:T(8,128)(2,1)S(1)} %pad_maximum_fusion.2), channel_id=1, source_target_pairs={{0,2},{1,3},{2,0},{3,1},{4,6},{5,7},{6,4},{7,5},{8,10},{9,11},{10,... | collective-permute-start | bytes 1179656 | tf_op jit(solution)/shard_map/ppermute | solution.py:23
  17.4 42.4 %all-to-all-start = ((bf16[8,128,768]{2,1,0:T(8,128)(2,1)}), bf16[8,128,768]{2,1,0:T(8,128)(2,1)S(1)}, u32[]{:S(2)}, u32[]{:S(2)}) async-start(bf16[8,128,768]{2,1,0:T(8,128)(2,1)} %bitcast.6), calls=%async_computation | async-start | bytes 3145728 | tf_op jit(solution)/shard_map/all_to_all | solution.py:293
  27.0 19.9 %collective-permute-start.3 = (bf16[2,4,96,512]{3,2,1,0:T(8,128)(2,1)S(1)}, bf16[2,4,96,512]{3,2,1,0:T(8,128)(2,1)S(1)}, u32[]{:S(2)}, u32[]{:S(2)}) collective-permute-start(bf16[2,4,96,512]{3,2,1,0:T(8,128)(2,1)S(1)} %bitcast.53), channel_id=1, source_target_pairs={{0,16},{8,24},{16,0},{24,8},{1,17},{9,25},{17,1},{25,9},{2,18},{10... | collective-permute-start | bytes 2359304 | tf_op jit(solution)/shard_map/ppermute | solution.py:23
  47.3 2.8 %copy-start.2 = (bf16[4,96,1024]{2,1,0:T(8,128)(2,1)}, bf16[4,96,1024]{2,1,0:T(8,128)(2,1)S(1)}, u32[]{:S(2)}) copy-start(bf16[4,96,1024]{2,1,0:T(8,128)(2,1)S(1)} %get-tuple-element.25.refs_0_) | copy-start | bytes 2359300
  47.3 7.5 %copy-start.1 = (bf16[4,96,1024]{2,1,0:T(8,128)(2,1)}, bf16[4,96,1024]{2,1,0:T(8,128)(2,1)S(1)}, u32[]{:S(2)}) copy-start(bf16[4,96,1024]{2,1,0:T(8,128)(2,1)S(1)} %get-tuple-element.24.refs_0_) | copy-start | bytes 2359300
  47.3 2.8 %collective-permute-start.4 = (bf16[4,96,1024]{2,1,0:T(8,128)(2,1)S(1)}, bf16[4,96,1024]{2,1,0:T(8,128)(2,1)}, u32[]{:S(2)}, u32[]{:S(2)}) collective-permute-start(bf16[4,96,1024]{2,1,0:T(8,128)(2,1)S(1)} %get-tuple-element.25.refs_0_), channel_id=1, source_target_pairs={{0,8},{8,0},{16,24},{24,16},{1,9},{9,1},{17,25},{25,17},{2,10},{10... | collective-permute-start | bytes 2359304 | tf_op jit(solution)/shard_map/ppermute | solution.py:23
  48.0 6.7 %collective-permute-start.5 = (bf16[4,96,1024]{2,1,0:T(8,128)(2,1)S(1)}, bf16[4,96,1024]{2,1,0:T(8,128)(2,1)}, u32[]{:S(2)}, u32[]{:S(2)}) collective-permute-start(bf16[4,96,1024]{2,1,0:T(8,128)(2,1)S(1)} %get-tuple-element.24.refs_0_), channel_id=1, source_target_pairs={{0,8},{8,0},{16,24},{24,16},{1,9},{9,1},{17,25},{25,17},{2,10},{10... | collective-permute-start | bytes 2359304 | tf_op jit(solution)/shard_map/ppermute | solution.py:23
  59.8 1.1 copy-start
  73.8 14.3 %copy-start.4 = (bf16[768,256]{1,0:T(8,128)(2,1)S(1)}, bf16[768,256]{1,0:T(8,128)(2,1)}, u32[]{:S(2)}) copy-start(bf16[768,256]{1,0:T(8,128)(2,1)} %get-tuple-element.20) | copy-start | bytes 1179652
  73.8 2.0 %collective-permute-start.11 = (bf16[768,256]{1,0:T(8,128)(2,1)}, bf16[768,256]{1,0:T(8,128)(2,1)S(1)}, u32[]{:S(2)}, u32[]{:S(2)}) collective-permute-start(bf16[768,256]{1,0:T(8,128)(2,1)} %get-tuple-element.23), channel_id=1, source_target_pairs={{0,8},{8,0},{16,24},{24,16},{1,9},{9,1},{17,25},{25,17},{2,10},{10... | collective-permute-start | bytes 1179656 | tf_op jit(solution)/shard_map/ppermute | solution.py:23
  73.9 4.6 %collective-permute-start.7 = (bf16[4,96,512]{2,1,0:T(8,128)(2,1)}, bf16[4,96,512]{2,1,0:T(8,128)(2,1)S(1)}, u32[]{:S(2)}, u32[]{:S(2)}) collective-permute-start(bf16[4,96,512]{2,1,0:T(8,128)(2,1)} %get-tuple-element.19), channel_id=1, source_target_pairs={{0,8},{8,0},{16,24},{24,16},{1,9},{9,1},{17,25},{25,17},{2,10},{10... | collective-permute-start | bytes 1179656 | tf_op jit(solution)/shard_map/ppermute | solution.py:23
  74.4 6.8 %collective-permute-start.10 = (bf16[768,256]{1,0:T(8,128)(2,1)}, bf16[768,256]{1,0:T(8,128)(2,1)S(1)}, u32[]{:S(2)}, u32[]{:S(2)}) collective-permute-start(bf16[768,256]{1,0:T(8,128)(2,1)} %get-tuple-element.21), channel_id=1, source_target_pairs={{0,8},{8,0},{16,24},{24,16},{1,9},{9,1},{17,25},{25,17},{2,10},{10... | collective-permute-start | bytes 1179656 | tf_op jit(solution)/shard_map/ppermute | solution.py:23
  76.9 11.2 %collective-permute-start.12 = (bf16[768,256]{1,0:T(8,128)(2,1)S(1)}, bf16[768,256]{1,0:T(8,128)(2,1)S(1)}, u32[]{:S(2)}, u32[]{:S(2)}) collective-permute-start(bf16[768,256]{1,0:T(8,128)(2,1)S(1)} %add_convert_fusion.1), channel_id=1, source_target_pairs={{0,16},{8,24},{16,0},{24,8},{1,17},{9,25},{17,1},{25,9},{2,18},{10... | collective-permute-start | bytes 1179656 | tf_op jit(solution)/shard_map/ppermute | solution.py:23
  78.5 11.3 %collective-permute-start.6 = (bf16[4,96,512]{2,1,0:T(8,128)(2,1)}, bf16[4,96,512]{2,1,0:T(8,128)(2,1)S(1)}, u32[]{:S(2)}, u32[]{:S(2)}) collective-permute-start(bf16[4,96,512]{2,1,0:T(8,128)(2,1)} %get-tuple-element.17), channel_id=1, source_target_pairs={{0,8},{8,0},{16,24},{24,16},{1,9},{9,1},{17,25},{25,17},{2,10},{10... | collective-permute-start | bytes 1179656 | tf_op jit(solution)/shard_map/ppermute | solution.py:23
  78.5 13.1 %copy-start.3 = (bf16[4,96,512]{2,1,0:T(8,128)(2,1)S(1)}, bf16[4,96,512]{2,1,0:T(8,128)(2,1)}, u32[]{:S(2)}) copy-start(bf16[4,96,512]{2,1,0:T(8,128)(2,1)} %get-tuple-element.16) | copy-start | bytes 1179652
  79.7 12.0 %collective-permute-start.8 = (bf16[4,96,512]{2,1,0:T(8,128)(2,1)S(1)}, bf16[4,96,512]{2,1,0:T(8,128)(2,1)S(1)}, u32[]{:S(2)}, u32[]{:S(2)}) collective-permute-start(bf16[4,96,512]{2,1,0:T(8,128)(2,1)S(1)} %add_convert_fusion.3), channel_id=1, source_target_pairs={{0,1},{1,0},{2,3},{3,2},{4,5},{5,4},{6,7},{7,6},{8,9},{9,8},{10,11... | collective-permute-start | bytes 1179656 | tf_op jit(solution)/shard_map/ppermute | solution.py:23
  88.3 7.1 %collective-permute-start.13 = (bf16[4,96,256]{2,1,0:T(8,128)(2,1)S(1)}, bf16[4,96,256]{2,1,0:T(8,128)(2,1)S(1)}, u32[]{:S(2)}, u32[]{:S(2)}) collective-permute-start(bf16[4,96,256]{2,1,0:T(8,128)(2,1)S(1)} %dynamic-slice_bitcast_fusion), channel_id=1, source_target_pairs={{0,1},{1,0},{2,3},{3,2},{4,5},{5,4},{6,7},{7,6},{8,9},{9,8},{10,11... | collective-permute-start | bytes 589832 | tf_op jit(solution)/shard_map/ppermute | solution.py:23
  91.8 6.2 %collective-permute-start.9 = (bf16[4,96,256]{2,1,0:T(8,128)(2,1)S(1)}, bf16[4,96,256]{2,1,0:T(8,128)(2,1)S(1)}, u32[]{:S(2)}, u32[]{:S(2)}) collective-permute-start(bf16[4,96,256]{2,1,0:T(8,128)(2,1)S(1)} %constant_dynamic-slice_fusion), channel_id=1, source_target_pairs={{0,16},{8,24},{16,0},{24,8},{1,17},{9,25},{17,1},{25,9},{2,18},{10... | collective-permute-start | bytes 589832 | tf_op jit(solution)/shard_map/ppermute | solution.py:23
  98.1 5.2 %collective-permute-start.14 = (bf16[96,512]{1,0:T(8,128)(2,1)S(1)}, bf16[96,512]{1,0:T(8,128)(2,1)S(1)}, u32[]{:S(2)}, u32[]{:S(2)}) collective-permute-start(bf16[96,512]{1,0:T(8,128)(2,1)S(1)} %get-tuple-element.34), channel_id=1, source_target_pairs={{0,2},{1,3},{2,0},{3,1},{4,6},{5,7},{6,4},{7,5},{8,10},{9,11},{10,... | collective-permute-start | bytes 294920 | tf_op jit(solution)/shard_map/ppermute | solution.py:23
  98.2 9.5 %collective-permute-start.15 = (bf16[96,512]{1,0:T(8,128)(2,1)S(1)}, bf16[96,512]{1,0:T(8,128)(2,1)S(1)}, u32[]{:S(2)}, u32[]{:S(2)}) collective-permute-start(bf16[96,512]{1,0:T(8,128)(2,1)S(1)} %get-tuple-element.35), channel_id=1, source_target_pairs={{0,4},{1,5},{2,6},{3,7},{4,0},{5,1},{6,2},{7,3},{8,12},{9,13},{10,... | collective-permute-start | bytes 294920 | tf_op jit(solution)/shard_map/ppermute | solution.py:23
  102.4 6.5 %collective-permute-start.16 = (bf16[96,512]{1,0:T(8,128)(2,1)S(1)}, bf16[96,512]{1,0:T(8,128)(2,1)S(1)}, u32[]{:S(2)}, u32[]{:S(2)}) collective-permute-start(bf16[96,512]{1,0:T(8,128)(2,1)S(1)} %get-tuple-element.36), channel_id=1, source_target_pairs={{0,6},{1,7},{2,4},{3,5},{4,2},{5,3},{6,0},{7,1},{8,14},{9,15},{10,... | collective-permute-start | bytes 294920 | tf_op jit(solution)/shard_map/ppermute | solution.py:23
  109.1 4.7 %collective-permute-start.17 = (bf16[2,96,256]{2,1,0:T(8,128)(2,1)S(1)}, bf16[2,96,256]{2,1,0:T(8,128)(2,1)S(1)}, u32[]{:S(2)}, u32[]{:S(2)}) collective-permute-start(bf16[2,96,256]{2,1,0:T(8,128)(2,1)S(1)} %pad_maximum_fusion.6), channel_id=1, source_target_pairs={{0,16},{8,24},{16,0},{24,8},{1,17},{9,25},{17,1},{25,9},{2,18},{10... | collective-permute-start | bytes 294920 | tf_op jit(solution)/shard_map/ppermute | solution.py:23
  113.8 1.5 %collective-permute-start.18 = (bf16[96,1024]{1,0:T(8,128)(2,1)S(1)}, bf16[96,1024]{1,0:T(8,128)(2,1)S(1)}, u32[]{:S(2)}, u32[]{:S(2)}) collective-permute-start(bf16[96,1024]{1,0:T(8,128)(2,1)S(1)} %pad_maximum_fusion.4), channel_id=1, source_target_pairs={{0,8},{8,0},{16,24},{24,16},{1,9},{9,1},{17,25},{25,17},{2,10},{10... | collective-permute-start | bytes 589832 | tf_op jit(solution)/shard_map/ppermute | solution.py:23

commit v13 on v12

--- a/solution.py
+++ b/solution.py
@@ -115,8 +115,8 @@
 def layer_kernel(
     sources, pieces, places_ref, into_ref, slots_ref, total_hbm, features_hbm, cotangent_hbm, *refs
 ):
-    weight_hbms, out_hbms = refs[:sources], refs[sources:-14]
-    total, features, cotangent, weight, summed, values, aggregate, grad, first, second = refs[-14:-4]
+    weight_hbms, out_hbms = refs[:sources], refs[sources:-15]
+    total, features, cotangent, weight, summed, values, aggregate, grad, turned, first, second = refs[-15:-4]
     row_sems, weight_sems, feature_sems, out_sems = refs[-4:]
     senders, block, _ = slots_ref.shape
     rows, hidden = grad.shape
@@ -140,43 +140,60 @@
         copy.wait()
     span = hidden // 2
 
-    def multiply(index):
-        at = slice(index * chunk, (index + 1) * chunk)
-        for begin in range(0, hidden, span):
-            columns = slice(begin, begin + span)
-            values[index % 2, :, columns] = jnp.dot(
-                aggregate[at, :], weight[:, :, columns].reshape(width, span), preferred_element_type=F32
-            )
-
-    multiply(0)
+    contract = (((0,), (0,)), ((), ()))
+
+    def multiply(half, index):
+        at, columns = slice(index * chunk, (index + 1) * chunk), slice(half * span, (half + 1) * span)
+        values[at, columns] = jnp.dot(
+            aggregate[at, :], weight[:, :, columns].reshape(width, span), preferred_element_type=F32
+        )
+
+    def slope(half, row):
+        at, columns = slice(row, row + 32), slice(half * span, (half + 1) * span)
+        value = (values[at, columns] + total[at, columns].astype(F32)).astype(BF16)
+        square = value * value
+        bend = jnp.tanh(value * (square * (SCALE * CUBIC) + SCALE))
+        inner = value * (square * (1.5 * SCALE * CUBIC) + 0.5 * SCALE)
+        grad[at, columns] = cotangent[at, columns] * ((1.0 + bend) * (inner * (1.0 - bend) + 0.5))
+
+    def first_term(index, operand, begin):
+        product = lax.dot_general(
+            operand[:, begin : begin + chunk], grad[:, :span], contract, preferred_element_type=F32
+        )
+        turned[index, begin : begin + chunk, :] = product.astype(BF16)
+
+    def in_turn(steps, half):
+        done = 0
+        for index, step in enumerate(steps):
+            step()
+            until = (index + 1) * rows // len(steps) // 32 * 32
+            for row in range(done, until, 32):
+                slope(half, row)
+            done = until
+
     for index in range(parts):
-        if index + 1 < parts:
-            multiply(index + 1)
-        totals[index].wait()
-        cotangents[index].wait()
-        for row in range(0, chunk, 32):
-            at = slice(index * chunk + row, index * chunk + row + 32)
-            for begin in range(0, hidden, span):
-                columns = slice(begin, begin + span)
-                value = values[index % 2, row : row + 32, columns] + total[at, columns].astype(F32)
-                value = value.astype(BF16)
-                square = value * value
-                bend = jnp.tanh(value * (square * (SCALE * CUBIC) + SCALE))
-                inner = value * (square * (1.5 * SCALE * CUBIC) + 0.5 * SCALE)
-                grad[at, columns] = cotangent[at, columns] * ((1.0 + bend) * (inner * (1.0 - bend) + 0.5))
-
+        multiply(0, index)
+    for copy in totals + cotangents:
+        copy.wait()
+    in_turn([functools.partial(multiply, 1, index) for index in range(parts)], 0)
     for copy in inputs:
         copy.wait()
+    in_turn(
+        [
+            functools.partial(first_term, index, operand, begin)
+            for index, operand in enumerate([features, aggregate])
+            for begin in range(0, width, chunk)
+        ],
+        1,
+    )
     results = []
 
     def send(source, target):
         results.append(pltpu.make_async_copy(source, target, out_sems.at[len(results)]))
         results[-1].start()
 
-    contract = (((0,), (0,)), ((), ()))
-    for index, operand in enumerate([features, aggregate]):
-        product = lax.dot_general(operand[...], grad[:, :span], contract, preferred_element_type=F32)
-        first[index] = product.astype(BF16).reshape(first.shape[1:])
+    for index in range(2):
+        first[index] = turned[index].reshape(first.shape[1:])
     for term, which in enumerate([1 - core, core]):
         if pieces:
             for leave, bit in enumerate([1 - low, low]):
@@ -195,7 +212,7 @@
         result.wait()
 
 
-def call(kernel, outs, places, out_places, scratch=(), flops=0, moved=0, vmem=56):
+def call(kernel, outs, places, out_places, scratch=(), flops=0, moved=0, vmem=40):
     return pl.pallas_call(
         kernel,
         out_shape=outs,
@@ -282,6 +299,7 @@
         ],
         flops=2 * dom_size * block * rows * width,
         moved=tile_vals.size * 2 + rows * width * 4,
+        vmem=56,
     )(tile_src, tile_peer, tile_vals, features)
     near, far, slots = lax.optimization_barrier((near, far, slots))
     held = joined(jnp.where(core == 0, held, near), far, (me & top) != 0, 1)
@@ -337,9 +355,10 @@
             pltpu.VMEM((rows, hidden), BF16),
             weight_shape,
             pltpu.VMEM((rows, width), F32),
-            pltpu.VMEM((2, 256, hidden), F32),
+            pltpu.VMEM((rows, hidden), F32),
             pltpu.VMEM((rows, width), BF16),
             pltpu.VMEM((rows, hidden), BF16),
+            pltpu.VMEM((2, width, span), BF16),
             pltpu.VMEM(first_scratch, BF16),
             pltpu.VMEM((2, 2, width, span // 2), BF16),
             DMA((2, rows // 256)),
@@ -358,8 +377,9 @@
     terms = [None] * 4
     for at in (0, 2, 1, 3):
         terms[at] = [outs[4 + at], swap(outs[at], "rep", 1)]
-    first = added([*terms[1], swap(added(terms[0]), "dom", 1)])
-    second = added([*terms[3], swap(added(terms[2]), "rep", parts)]).reshape(dom_size, depth, -1)
+    first, second = lax.optimization_barrier((added(terms[0]), added(terms[2])))
+    first = added([*terms[1], swap(first, "dom", 1)])
+    second = added([*terms[3], swap(second, "rep", parts)]).reshape(dom_size, depth, -1)
     first = reduce_high(first, high, parts // 2)
     second = exchanged(reduce_high(second, high, parts // 4), low_half, low, "dom", 1)
     both = jnp.concatenate([first, second], axis=2)

time: 117 us -> 123 us (1.051)
  local copies, waits for them, and re-layouts: 2.17 us -> 8.36 us
  starting transfers between devices: 26 us -> 30.6 us
  waiting for transfers between devices: 60.3 us -> 56.2 us
  other arithmetic: 4.86 us -> 3.33 us
    unnamed x10 -> x12, local copies, waits for them, and re-layouts: 1.16 us -> 7.35 us
    ppermute x17, starting transfers between devices: 15.7 us -> 20.3 us  [swap(): lax.ppermute(value, axis, [(index, index ^ step) for index in range(size)])]
    all_to_all x1, waiting for transfers between devices: 5.09 us -> 2.23 us  [shards(): lax.all_to_all(slots.reshape(dom_size, block, width), 'dom', split_axis=0...]
    ppermute x17, waiting for transfers between devices: 51.3 us -> 50 us  [swap(): lax.ppermute(value, axis, [(index, index ^ step) for index in range(size)])]
  transfers between devices with their start and end apart: 20 -> 20, of which waited for: 15 -> 13; matrix products, arithmetic and copies ran while one was open for 3% -> 2% of each run, Pallas kernels for 8% -> 8%
where the time goes in v13:
time: 123 us; the launch traced here: 122 us
  waiting for transfers between devices  56.2 us (46%)
  starting transfers between devices  30.6 us (25%)
  Pallas kernels  23 us (19%)
  local copies, waits for them, and re-layouts  8.36 us (7%)
  other arithmetic  3.33 us (3%)
    ppermute x17, waiting for transfers between devices, swap(): lax.ppermute(value, axis, [(index, index ^ step) for index in range(size)])  50 us
    ppermute x17, starting transfers between devices, swap(): lax.ppermute(value, axis, [(index, index ^ step) for index in range(size)])  20.3 us
    pallas_call x1, Pallas kernels, shards(): call(functools.partial(layer_kernel, sources, tiled), out_shapes, [SMEM,...  13.7 us
    unnamed x12, local copies, waits for them, and re-layouts  7.35 us
    all_to_all x1, starting transfers between devices, shards(): lax.all_to_all(slots.reshape(dom_size, block, width), 'dom', split_axis=0...  5.58 us
    pallas_call x1, Pallas kernels, shards(): call(self_kernel, jax.ShapeDtypeStruct((rows, hidden), BF16), [SMEM] + [H...  4.8 us
    ppermute x2, starting transfers between devices, cross(): lax.ppermute(value, ('rep', 'dom'), [(source, target) for source, target...  4.77 us
    pallas_call x1, Pallas kernels, shards(): call(slots_kernel, jax.ShapeDtypeStruct((dom_size * block, width), BF16),...  4.54 us
  transfers between devices with their start and end apart: 20, of which 13 were waited for; matrix products, arithmetic and copies ran while one was open for 2% of the time, Pallas kernels for 8%

profile of v13, /device:TPU:0, one launch (start us, length us, event | category | flops | bytes accessed | tf_op | source)
XLA Modules:
  0.0 122.4 jit_solution(7065258304253945461)
XLA Ops:
  2.3 4.1 %collective-permute-start.1 = (bf16[2,96,512]{2,1,0:T(8,128)(2,1)S(1)}, bf16[2,96,512]{2,1,0:T(8,128)(2,1)S(1)}, u32[]{:S(2)}, u32[]{:S(2)}) collective-permute-start(bf16[2,96,512]{2,1,0:T(8,128)(2,1)S(1)} %pad_maximum_fusion.3), channel_id=1, source_target_pairs={{0,4},{1,5},{2,6},{3,7},{4,0},{5,1},{6,2},{7,3},{8,13},{9,12},{10,... | collective-permute-start | bytes 589832 | tf_op jit(solution)/shard_map/ppermute | solution.py:31
  6.4 4.5 %shard_map.95 = bf16[1024,768]{1,0:T(8,128)(2,1)} custom-call(s32[32]{0:T(128)} %src_hbm.1, s32[32]{0:T(128)} %peer_hbm.1, bf16[32,128,128]{2,1,0:T(8,128)(2,1)} %tiles_hbm.1, bf16[1024,768]{1,0:T(8,128)(2,1)} %features_hbm.5), custom_call_target="tpu_custom_call" | custom-call | flops 1610612736 | bytes 4194304 | tf_op jit(solution)/shard_map/pallas_call | solution.py:285
  11.0 3.9 %collective-permute-done.1 = bf16[2,96,512]{2,1,0:T(8,128)(2,1)S(1)} collective-permute-done((bf16[2,96,512]{2,1,0:T(8,128)(2,1)S(1)}, bf16[2,96,512]{2,1,0:T(8,128)(2,1)S(1)}, u32[]{:S(2)}, u32[]{:S(2)}) %collective-permute-start.1) | collective-permute-done | bytes 196640 | tf_op jit(solution)/shard_map/ppermute | solution.py:31
  15.0 2.5 %collective-permute-start.2 = (bf16[2,2,96,512]{3,2,1,0:T(8,128)(2,1)S(1)}, bf16[2,2,96,512]{3,2,1,0:T(8,128)(2,1)S(1)}, u32[]{:S(2)}, u32[]{:S(2)}) collective-permute-start(bf16[2,2,96,512]{3,2,1,0:T(8,128)(2,1)S(1)} %pad_maximum_fusion.2), channel_id=1, source_target_pairs={{0,2},{1,3},{2,0},{3,1},{4,6},{5,7},{6,4},{7,5},{8,10},{9,11},{10,... | collective-permute-start | bytes 1179656 | tf_op jit(solution)/shard_map/ppermute | solution.py:23
  17.4 5.6 %all-to-all-start = ((bf16[8,128,768]{2,1,0:T(8,128)(2,1)}), bf16[8,128,768]{2,1,0:T(8,128)(2,1)S(1)}, u32[]{:S(2)}, u32[]{:S(2)}) async-start(bf16[8,128,768]{2,1,0:T(8,128)(2,1)} %bitcast.6), calls=%async_computation | async-start | bytes 3145728 | tf_op jit(solution)/shard_map/all_to_all | solution.py:311
  23.0 3.8 %collective-permute-done.2 = bf16[2,2,96,512]{3,2,1,0:T(8,128)(2,1)S(1)} collective-permute-done((bf16[2,2,96,512]{3,2,1,0:T(8,128)(2,1)S(1)}, bf16[2,2,96,512]{3,2,1,0:T(8,128)(2,1)S(1)}, u32[]{:S(2)}, u32[]{:S(2)}) %collective-permute-start.2) | collective-permute-done | bytes 393248 | tf_op jit(solution)/shard_map/ppermute | solution.py:23
  27.0 1.6 %collective-permute-start.3 = (bf16[2,4,96,512]{3,2,1,0:T(8,128)(2,1)S(1)}, bf16[2,4,96,512]{3,2,1,0:T(8,128)(2,1)S(1)}, u32[]{:S(2)}, u32[]{:S(2)}) collective-permute-start(bf16[2,4,96,512]{3,2,1,0:T(8,128)(2,1)S(1)} %bitcast.53), channel_id=1, source_target_pairs={{0,16},{8,24},{16,0},{24,8},{1,17},{9,25},{17,1},{25,9},{2,18},{10... | collective-permute-start | bytes 2359304 | tf_op jit(solution)/shard_map/ppermute | solution.py:23
  28.6 18.4 %collective-permute-done.3 = bf16[2,4,96,512]{3,2,1,0:T(8,128)(2,1)S(1)} collective-permute-done((bf16[2,4,96,512]{3,2,1,0:T(8,128)(2,1)S(1)}, bf16[2,4,96,512]{3,2,1,0:T(8,128)(2,1)S(1)}, u32[]{:S(2)}, u32[]{:S(2)}) %collective-permute-start.3) | collective-permute-done | bytes 786464 | tf_op jit(solution)/shard_map/ppermute | solution.py:23
  48.1 1.9 %collective-permute-done.4.refs_1_ = bf16[4,96,1024]{2,1,0:T(8,128)(2,1)} collective-permute-done((bf16[4,96,1024]{2,1,0:T(8,128)(2,1)S(1)}, bf16[4,96,1024]{2,1,0:T(8,128)(2,1)}, u32[]{:S(2)}, u32[]{:S(2)}) %collective-permute-start.4) | collective-permute-done | bytes 786464 | tf_op jit(solution)/shard_map/ppermute | solution.py:23
  50.0 1.4 %copy-done.1 = bf16[1024,768]{1,0:T(8,128)(2,1)S(1)} copy-done((bf16[1024,768]{1,0:T(8,128)(2,1)S(1)}, bf16[1024,768]{1,0:T(8,128)(2,1)}, u32[]{:S(2)}) %copy-start.1) | copy-done | bytes 1572888
  51.4 4.8 %shard_map.96.total_hbm = bf16[1024,1024]{1,0:T(8,128)(2,1)S(1)} custom-call(s32[1]{0:T(128)} %bitcast.1.flip_ref, bf16[1024,768]{1,0:T(8,128)(2,1)S(1)} %copy-done.1, bf16[4,96,1024]{2,1,0:T(8,128)(2,1)S(1)} %get-tuple-element.29.refs_0_, bf16[4,96,1024]{2,1,0:T(8,128)(2,1)} %collective-permute-done.4.refs_1_), custom_call_target="tpu_custom_call" | custom-call | flops 1610612736 | bytes 7340032 | tf_op jit(solution)/shard_map/pallas_call | solution.py:321
  56.3 1.3 %copy-done.4 = bf16[1024,1024]{1,0:T(8,128)(2,1)} copy-done((bf16[1024,1024]{1,0:T(8,128)(2,1)}, bf16[1024,1024]{1,0:T(8,128)(2,1)S(1)}, u32[]{:S(2)}) %copy-start.4) | copy-done | bytes 2097176
  57.6 2.2 %all-to-all-done.slots_ref = bf16[8,128,768]{2,1,0:T(8,128)(2,1)S(1)} async-done(((bf16[8,128,768]{2,1,0:T(8,128)(2,1)}), bf16[8,128,768]{2,1,0:T(8,128)(2,1)S(1)}, u32[]{:S(2)}, u32[]{:S(2)}) %all-to-all-start) | async-done | bytes 1572896 | tf_op jit(solution)/shard_map/all_to_all | solution.py:311
  59.8 1.6 %copy-done = bf16[1024,1024]{1,0:T(8,128)(2,1)S(1)} copy-done((bf16[1024,1024]{1,0:T(8,128)(2,1)S(1)}, bf16[1024,1024]{1,0:T(8,128)(2,1)}, u32[]{:S(2)}) %copy-start) | copy-done | bytes 2097176
  61.4 1.4 %copy-done.2 = bf16[1024,768]{1,0:T(8,128)(2,1)S(1)} copy-done((bf16[1024,768]{1,0:T(8,128)(2,1)S(1)}, bf16[1024,768]{1,0:T(8,128)(2,1)}, u32[]{:S(2)}) %copy-start.2) | copy-done | bytes 1572888
  62.8 1.6 %copy-done.5 = bf16[1024,1024]{1,0:T(8,128)(2,1)S(1)} copy-done((bf16[1024,1024]{1,0:T(8,128)(2,1)S(1)}, bf16[1024,1024]{1,0:T(8,128)(2,1)}, u32[]{:S(2)}) %copy-start.5) | copy-done | bytes 2097176
  64.4 13.7 %shard_map.97 = (bf16[4,96,512]{2,1,0:T(8,128)(2,1)S(1)}, bf16[4,96,512]{2,1,0:T(8,128)(2,1)S(1)}, bf16[768,256]{1,0:T(8,128)(2,1)S(1)}, bf16[768,256]{1,0:T(8,1...) custom-call(s32[4]{0:T(128)S(1)} %pad_add_fusion.places_ref, ...), custom_call_target="tpu_custom_call" | custom-call | flops 4831838208 | bytes 16777216 | tf_op jit(solution)/shard_map/pallas_call | solution.py:347
  78.8 1.1 collective-permute-done.8
  80.0 1.0 collective-permute-done.7
  81.1 1.6 %collective-permute-start.12 = (bf16[768,256]{1,0:T(8,128)(2,1)S(1)}, bf16[768,256]{1,0:T(8,128)(2,1)}, u32[]{:S(2)}, u32[]{:S(2)}) collective-permute-start(bf16[768,256]{1,0:T(8,128)(2,1)S(1)} %add_convert_fusion.2), channel_id=1, source_target_pairs={{0,16},{8,24},{16,0},{24,8},{1,17},{9,25},{17,1},{25,9},{2,18},{10... | collective-permute-start | bytes 1179656 | tf_op jit(solution)/shard_map/ppermute | solution.py:23
  82.7 2.5 %collective-permute-start.9 = (bf16[4,96,512]{2,1,0:T(8,128)(2,1)S(1)}, bf16[4,96,512]{2,1,0:T(8,128)(2,1)S(1)}, u32[]{:S(2)}, u32[]{:S(2)}) collective-permute-start(bf16[4,96,512]{2,1,0:T(8,128)(2,1)S(1)} %add_convert_fusion.3), channel_id=1, source_target_pairs={{0,1},{1,0},{2,3},{3,2},{4,5},{5,4},{6,7},{7,6},{8,9},{9,8},{10,11... | collective-permute-start | bytes 1179656 | tf_op jit(solution)/shard_map/ppermute | solution.py:23
  85.2 7.3 %collective-permute-done.12 = bf16[768,256]{1,0:T(8,128)(2,1)} collective-permute-done((bf16[768,256]{1,0:T(8,128)(2,1)S(1)}, bf16[768,256]{1,0:T(8,128)(2,1)}, u32[]{:S(2)}, u32[]{:S(2)}) %collective-permute-start.12) | collective-permute-done | bytes 393248 | tf_op jit(solution)/shard_map/ppermute | solution.py:23
  92.5 1.1 add_convert_fusion
  93.6 2.3 %collective-permute-start.13 = (bf16[4,96,256]{2,1,0:T(8,128)(2,1)S(1)}, bf16[4,96,256]{2,1,0:T(8,128)(2,1)S(1)}, u32[]{:S(2)}, u32[]{:S(2)}) collective-permute-start(bf16[4,96,256]{2,1,0:T(8,128)(2,1)S(1)} %dynamic-slice_bitcast_fusion), channel_id=1, source_target_pairs={{0,1},{1,0},{2,3},{3,2},{4,5},{5,4},{6,7},{7,6},{8,9},{9,8},{10,11... | collective-permute-start | bytes 589832 | tf_op jit(solution)/shard_map/ppermute | solution.py:23
  96.1 1.8 %collective-permute-start.10 = (bf16[4,96,256]{2,1,0:T(8,128)(2,1)S(1)}, bf16[4,96,256]{2,1,0:T(8,128)(2,1)S(1)}, u32[]{:S(2)}, u32[]{:S(2)}) collective-permute-start(bf16[4,96,256]{2,1,0:T(8,128)(2,1)S(1)} %constant_dynamic-slice_fusion), channel_id=1, source_target_pairs={{0,16},{8,24},{16,0},{24,8},{1,17},{9,25},{17,1},{25,9},{2,18},{10... | collective-permute-start | bytes 589832 | tf_op jit(solution)/shard_map/ppermute | solution.py:23
  97.9 2.4 %collective-permute-done.13 = bf16[4,96,256]{2,1,0:T(8,128)(2,1)S(1)} collective-permute-done((bf16[4,96,256]{2,1,0:T(8,128)(2,1)S(1)}, bf16[4,96,256]{2,1,0:T(8,128)(2,1)S(1)}, u32[]{:S(2)}, u32[]{:S(2)}) %collective-permute-start.13) | collective-permute-done | bytes 196640 | tf_op jit(solution)/shard_map/ppermute | solution.py:23
  100.4 1.6 %collective-permute-done.10 = bf16[4,96,256]{2,1,0:T(8,128)(2,1)S(1)} collective-permute-done((bf16[4,96,256]{2,1,0:T(8,128)(2,1)S(1)}, bf16[4,96,256]{2,1,0:T(8,128)(2,1)S(1)}, u32[]{:S(2)}, u32[]{:S(2)}) %collective-permute-start.10) | collective-permute-done | bytes 196640 | tf_op jit(solution)/shard_map/ppermute | solution.py:23
  102.2 6.1 %collective-permute-start.15 = (bf16[96,512]{1,0:T(8,128)(2,1)S(1)}, bf16[96,512]{1,0:T(8,128)(2,1)S(1)}, u32[]{:S(2)}, u32[]{:S(2)}) collective-permute-start(bf16[96,512]{1,0:T(8,128)(2,1)S(1)} %get-tuple-element.39), channel_id=1, source_target_pairs={{0,4},{1,5},{2,6},{3,7},{4,0},{5,1},{6,2},{7,3},{8,12},{9,13},{10,... | collective-permute-start | bytes 294920 | tf_op jit(solution)/shard_map/ppermute | solution.py:23
  108.3 6.8 %collective-permute-done.15 = bf16[96,512]{1,0:T(8,128)(2,1)S(1)} collective-permute-done((bf16[96,512]{1,0:T(8,128)(2,1)S(1)}, bf16[96,512]{1,0:T(8,128)(2,1)S(1)}, u32[]{:S(2)}, u32[]{:S(2)}) %collective-permute-start.15) | collective-permute-done | bytes 98336 | tf_op jit(solution)/shard_map/ppermute | solution.py:23
  115.6 4.3 %collective-permute-done.17 = bf16[2,96,256]{2,1,0:T(8,128)(2,1)S(1)} collective-permute-done((bf16[2,96,256]{2,1,0:T(8,128)(2,1)S(1)}, bf16[2,96,256]{2,1,0:T(8,128)(2,1)S(1)}, u32[]{:S(2)}, u32[]{:S(2)}) %collective-permute-start.17) | collective-permute-done | bytes 98336 | tf_op jit(solution)/shard_map/ppermute | solution.py:23
  120.0 1.4 %collective-permute-done.18 = bf16[96,1024]{1,0:T(8,128)(2,1)S(1)} collective-permute-done((bf16[96,1024]{1,0:T(8,128)(2,1)S(1)}, bf16[96,1024]{1,0:T(8,128)(2,1)S(1)}, u32[]{:S(2)}, u32[]{:S(2)}) %collective-permute-start.18) | collective-permute-done | bytes 196640 | tf_op jit(solution)/shard_map/ppermute | solution.py:23
  121.4 1.0 select_convert_fusion
  (48 shorter events, 4.9 us)
Async XLA Ops:
  1.6 9.3 %collective-permute-start = (bf16[2,96,512]{2,1,0:T(8,128)(2,1)S(1)}, bf16[2,96,512]{2,1,0:T(8,128)(2,1)S(1)}, u32[]{:S(2)}, u32[]{:S(2)}) collective-permute-start(bf16[2,96,512]{2,1,0:T(8,128)(2,1)S(1)} %pad_maximum_fusion.3), channel_id=1, source_target_pairs={{8,9},{9,8},{10,11},{11,10},{12,13},{13,12},{14,15},{15,14},{24,25... | collective-permute-start | bytes 589832 | tf_op jit(solution)/shard_map/ppermute | solution.py:31
  2.3 12.6 %collective-permute-start.1 = (bf16[2,96,512]{2,1,0:T(8,128)(2,1)S(1)}, bf16[2,96,512]{2,1,0:T(8,128)(2,1)S(1)}, u32[]{:S(2)}, u32[]{:S(2)}) collective-permute-start(bf16[2,96,512]{2,1,0:T(8,128)(2,1)S(1)} %pad_maximum_fusion.3), channel_id=1, source_target_pairs={{0,4},{1,5},{2,6},{3,7},{4,0},{5,1},{6,2},{7,3},{8,13},{9,12},{10,... | collective-permute-start | bytes 589832 | tf_op jit(solution)/shard_map/ppermute | solution.py:31
  15.0 11.9 %collective-permute-start.2 = (bf16[2,2,96,512]{3,2,1,0:T(8,128)(2,1)S(1)}, bf16[2,2,96,512]{3,2,1,0:T(8,128)(2,1)S(1)}, u32[]{:S(2)}, u32[]{:S(2)}) collective-permute-start(bf16[2,2,96,512]{3,2,1,0:T(8,128)(2,1)S(1)} %pad_maximum_fusion.2), channel_id=1, source_target_pairs={{0,2},{1,3},{2,0},{3,1},{4,6},{5,7},{6,4},{7,5},{8,10},{9,11},{10,... | collective-permute-start | bytes 1179656 | tf_op jit(solution)/shard_map/ppermute | solution.py:23
  17.4 42.4 %all-to-all-start = ((bf16[8,128,768]{2,1,0:T(8,128)(2,1)}), bf16[8,128,768]{2,1,0:T(8,128)(2,1)S(1)}, u32[]{:S(2)}, u32[]{:S(2)}) async-start(bf16[8,128,768]{2,1,0:T(8,128)(2,1)} %bitcast.6), calls=%async_computation | async-start | bytes 3145728 | tf_op jit(solution)/shard_map/all_to_all | solution.py:311
  27.0 19.9 %collective-permute-start.3 = (bf16[2,4,96,512]{3,2,1,0:T(8,128)(2,1)S(1)}, bf16[2,4,96,512]{3,2,1,0:T(8,128)(2,1)S(1)}, u32[]{:S(2)}, u32[]{:S(2)}) collective-permute-start(bf16[2,4,96,512]{3,2,1,0:T(8,128)(2,1)S(1)} %bitcast.53), channel_id=1, source_target_pairs={{0,16},{8,24},{16,0},{24,8},{1,17},{9,25},{17,1},{25,9},{2,18},{10... | collective-permute-start | bytes 2359304 | tf_op jit(solution)/shard_map/ppermute | solution.py:23
  47.3 2.8 %collective-permute-start.4 = (bf16[4,96,1024]{2,1,0:T(8,128)(2,1)S(1)}, bf16[4,96,1024]{2,1,0:T(8,128)(2,1)}, u32[]{:S(2)}, u32[]{:S(2)}) collective-permute-start(bf16[4,96,1024]{2,1,0:T(8,128)(2,1)S(1)} %get-tuple-element.29.refs_0_), channel_id=1, source_target_pairs={{0,8},{8,0},{16,24},{24,16},{1,9},{9,1},{17,25},{25,17},{2,10},{10... | collective-permute-start | bytes 2359304 | tf_op jit(solution)/shard_map/ppermute | solution.py:23
  48.0 9.6 %collective-permute-start.5 = (bf16[4,96,1024]{2,1,0:T(8,128)(2,1)S(1)}, bf16[4,96,1024]{2,1,0:T(8,128)(2,1)}, u32[]{:S(2)}, u32[]{:S(2)}) collective-permute-start(bf16[4,96,1024]{2,1,0:T(8,128)(2,1)S(1)} %get-tuple-element.28.refs_0_), channel_id=1, source_target_pairs={{0,8},{8,0},{16,24},{24,16},{1,9},{9,1},{17,25},{25,17},{2,10},{10... | collective-permute-start | bytes 2359304 | tf_op jit(solution)/shard_map/ppermute | solution.py:23
  50.0 1.4 %copy-start.1 = (bf16[1024,768]{1,0:T(8,128)(2,1)S(1)}, bf16[1024,768]{1,0:T(8,128)(2,1)}, u32[]{:S(2)}) copy-start(bf16[1024,768]{1,0:T(8,128)(2,1)} %features_hbm.5) | copy-start | bytes 4718596
  51.4 8.4 %copy-start.3 = (s32[8]{0:T(128)S(1)}, s32[8]{0:T(128)}, u32[]{:S(2)}) copy-start(s32[8]{0:T(128)} %into_ref.1) | copy-start | bytes 100
  56.2 1.4 %copy-start.4 = (bf16[1024,1024]{1,0:T(8,128)(2,1)}, bf16[1024,1024]{1,0:T(8,128)(2,1)S(1)}, u32[]{:S(2)}) copy-start(bf16[1024,1024]{1,0:T(8,128)(2,1)S(1)} %shard_map.96.total_hbm) | copy-start | bytes 6291460
  59.8 1.6 %copy-start = (bf16[1024,1024]{1,0:T(8,128)(2,1)S(1)}, bf16[1024,1024]{1,0:T(8,128)(2,1)}, u32[]{:S(2)}) copy-start(bf16[1024,1024]{1,0:T(8,128)(2,1)} %cotangent_hbm.1) | copy-start | bytes 6291460
  61.4 1.4 %copy-start.2 = (bf16[1024,768]{1,0:T(8,128)(2,1)S(1)}, bf16[1024,768]{1,0:T(8,128)(2,1)}, u32[]{:S(2)}) copy-start(bf16[1024,768]{1,0:T(8,128)(2,1)} %features_hbm.5) | copy-start | bytes 4718596
  62.8 1.6 %copy-start.5 = (bf16[1024,1024]{1,0:T(8,128)(2,1)S(1)}, bf16[1024,1024]{1,0:T(8,128)(2,1)}, u32[]{:S(2)}) copy-start(bf16[1024,1024]{1,0:T(8,128)(2,1)} %copy-done.4) | copy-start | bytes 6291460
  78.1 1.8 %collective-permute-start.8 = (bf16[768,256]{1,0:T(8,128)(2,1)S(1)}, bf16[768,256]{1,0:T(8,128)(2,1)S(1)}, u32[]{:S(2)}, u32[]{:S(2)}) collective-permute-start(bf16[768,256]{1,0:T(8,128)(2,1)S(1)} %get-tuple-element.23), channel_id=1, source_target_pairs={{0,8},{8,0},{16,24},{24,16},{1,9},{9,1},{17,25},{25,17},{2,10},{10... | collective-permute-start | bytes 1179656 | tf_op jit(solution)/shard_map/ppermute | solution.py:23
  78.2 2.8 %collective-permute-start.7 = (bf16[4,96,512]{2,1,0:T(8,128)(2,1)S(1)}, bf16[4,96,512]{2,1,0:T(8,128)(2,1)S(1)}, u32[]{:S(2)}, u32[]{:S(2)}) collective-permute-start(bf16[4,96,512]{2,1,0:T(8,128)(2,1)S(1)} %get-tuple-element.21), channel_id=1, source_target_pairs={{0,8},{8,0},{16,24},{24,16},{1,9},{9,1},{17,25},{25,17},{2,10},{10... | collective-permute-start | bytes 1179656 | tf_op jit(solution)/shard_map/ppermute | solution.py:23
  78.7 6.5 %collective-permute-start.11 = (bf16[768,256]{1,0:T(8,128)(2,1)}, bf16[768,256]{1,0:T(8,128)(2,1)S(1)}, u32[]{:S(2)}, u32[]{:S(2)}) collective-permute-start(bf16[768,256]{1,0:T(8,128)(2,1)} %get-tuple-element.26), channel_id=1, source_target_pairs={{0,8},{8,0},{16,24},{24,16},{1,9},{9,1},{17,25},{25,17},{2,10},{10... | collective-permute-start | bytes 1179656 | tf_op jit(solution)/shard_map/ppermute | solution.py:23
  81.1 11.3 %collective-permute-start.12 = (bf16[768,256]{1,0:T(8,128)(2,1)S(1)}, bf16[768,256]{1,0:T(8,128)(2,1)}, u32[]{:S(2)}, u32[]{:S(2)}) collective-permute-start(bf16[768,256]{1,0:T(8,128)(2,1)S(1)} %add_convert_fusion.2), channel_id=1, source_target_pairs={{0,16},{8,24},{16,0},{24,8},{1,17},{9,25},{17,1},{25,9},{2,18},{10... | collective-permute-start | bytes 1179656 | tf_op jit(solution)/shard_map/ppermute | solution.py:23
  82.7 13.2 %collective-permute-start.6 = (bf16[4,96,512]{2,1,0:T(8,128)(2,1)S(1)}, bf16[4,96,512]{2,1,0:T(8,128)(2,1)S(1)}, u32[]{:S(2)}, u32[]{:S(2)}) collective-permute-start(bf16[4,96,512]{2,1,0:T(8,128)(2,1)S(1)} %get-tuple-element.19), channel_id=1, source_target_pairs={{0,8},{8,0},{16,24},{24,16},{1,9},{9,1},{17,25},{25,17},{2,10},{10... | collective-permute-start | bytes 1179656 | tf_op jit(solution)/shard_map/ppermute | solution.py:23
  82.7 13.2 %collective-permute-start.9 = (bf16[4,96,512]{2,1,0:T(8,128)(2,1)S(1)}, bf16[4,96,512]{2,1,0:T(8,128)(2,1)S(1)}, u32[]{:S(2)}, u32[]{:S(2)}) collective-permute-start(bf16[4,96,512]{2,1,0:T(8,128)(2,1)S(1)} %add_convert_fusion.3), channel_id=1, source_target_pairs={{0,1},{1,0},{2,3},{3,2},{4,5},{5,4},{6,7},{7,6},{8,9},{9,8},{10,11... | collective-permute-start | bytes 1179656 | tf_op jit(solution)/shard_map/ppermute | solution.py:23
  93.6 6.7 %collective-permute-start.13 = (bf16[4,96,256]{2,1,0:T(8,128)(2,1)S(1)}, bf16[4,96,256]{2,1,0:T(8,128)(2,1)S(1)}, u32[]{:S(2)}, u32[]{:S(2)}) collective-permute-start(bf16[4,96,256]{2,1,0:T(8,128)(2,1)S(1)} %dynamic-slice_bitcast_fusion), channel_id=1, source_target_pairs={{0,1},{1,0},{2,3},{3,2},{4,5},{5,4},{6,7},{7,6},{8,9},{9,8},{10,11... | collective-permute-start | bytes 589832 | tf_op jit(solution)/shard_map/ppermute | solution.py:23
  96.1 5.9 %collective-permute-start.10 = (bf16[4,96,256]{2,1,0:T(8,128)(2,1)S(1)}, bf16[4,96,256]{2,1,0:T(8,128)(2,1)S(1)}, u32[]{:S(2)}, u32[]{:S(2)}) collective-permute-start(bf16[4,96,256]{2,1,0:T(8,128)(2,1)S(1)} %constant_dynamic-slice_fusion), channel_id=1, source_target_pairs={{0,16},{8,24},{16,0},{24,8},{1,17},{9,25},{17,1},{25,9},{2,18},{10... | collective-permute-start | bytes 589832 | tf_op jit(solution)/shard_map/ppermute | solution.py:23
  102.1 6.2 %collective-permute-start.14 = (bf16[96,512]{1,0:T(8,128)(2,1)S(1)}, bf16[96,512]{1,0:T(8,128)(2,1)S(1)}, u32[]{:S(2)}, u32[]{:S(2)}) collective-permute-start(bf16[96,512]{1,0:T(8,128)(2,1)S(1)} %get-tuple-element.38), channel_id=1, source_target_pairs={{0,2},{1,3},{2,0},{3,1},{4,6},{5,7},{6,4},{7,5},{8,10},{9,11},{10,... | collective-permute-start | bytes 294920 | tf_op jit(solution)/shard_map/ppermute | solution.py:23
  102.2 12.8 %collective-permute-start.15 = (bf16[96,512]{1,0:T(8,128)(2,1)S(1)}, bf16[96,512]{1,0:T(8,128)(2,1)S(1)}, u32[]{:S(2)}, u32[]{:S(2)}) collective-permute-start(bf16[96,512]{1,0:T(8,128)(2,1)S(1)} %get-tuple-element.39), channel_id=1, source_target_pairs={{0,4},{1,5},{2,6},{3,7},{4,0},{5,1},{6,2},{7,3},{8,12},{9,13},{10,... | collective-permute-start | bytes 294920 | tf_op jit(solution)/shard_map/ppermute | solution.py:23
  108.3 6.8 %collective-permute-start.16 = (bf16[96,512]{1,0:T(8,128)(2,1)S(1)}, bf16[96,512]{1,0:T(8,128)(2,1)S(1)}, u32[]{:S(2)}, u32[]{:S(2)}) collective-permute-start(bf16[96,512]{1,0:T(8,128)(2,1)S(1)} %get-tuple-element.40), channel_id=1, source_target_pairs={{0,6},{1,7},{2,4},{3,5},{4,2},{5,3},{6,0},{7,1},{8,14},{9,15},{10,... | collective-permute-start | bytes 294920 | tf_op jit(solution)/shard_map/ppermute | solution.py:23
  115.2 4.7 %collective-permute-start.17 = (bf16[2,96,256]{2,1,0:T(8,128)(2,1)S(1)}, bf16[2,96,256]{2,1,0:T(8,128)(2,1)S(1)}, u32[]{:S(2)}, u32[]{:S(2)}) collective-permute-start(bf16[2,96,256]{2,1,0:T(8,128)(2,1)S(1)} %pad_maximum_fusion.6), channel_id=1, source_target_pairs={{0,16},{8,24},{16,0},{24,8},{1,17},{9,25},{17,1},{25,9},{2,18},{10... | collective-permute-start | bytes 294920 | tf_op jit(solution)/shard_map/ppermute | solution.py:23
  119.9 1.5 %collective-permute-start.18 = (bf16[96,1024]{1,0:T(8,128)(2,1)S(1)}, bf16[96,1024]{1,0:T(8,128)(2,1)S(1)}, u32[]{:S(2)}, u32[]{:S(2)}) collective-permute-start(bf16[96,1024]{1,0:T(8,128)(2,1)S(1)} %pad_maximum_fusion.4), channel_id=1, source_target_pairs={{0,8},{8,0},{16,24},{24,16},{1,9},{9,1},{17,25},{25,17},{2,10},{10... | collective-permute-start | bytes 589832 | tf_op jit(solution)/shard_map/ppermute | solution.py:23

commit v14 on v12

--- a/solution.py
+++ b/solution.py
@@ -115,8 +115,8 @@
 def layer_kernel(
     sources, pieces, places_ref, into_ref, slots_ref, total_hbm, features_hbm, cotangent_hbm, *refs
 ):
-    weight_hbms, out_hbms = refs[:sources], refs[sources:-14]
-    total, features, cotangent, weight, summed, values, aggregate, grad, first, second = refs[-14:-4]
+    weight_hbms, out_hbms = refs[:sources], refs[sources:-13]
+    total, features, cotangent, weight, summed, values, aggregate, grad, both = refs[-13:-4]
     row_sems, weight_sems, feature_sems, out_sems = refs[-4:]
     senders, block, _ = slots_ref.shape
     rows, hidden = grad.shape
@@ -167,30 +167,30 @@
 
     for copy in inputs:
         copy.wait()
-    results = []
-
-    def send(source, target):
-        results.append(pltpu.make_async_copy(source, target, out_sems.at[len(results)]))
-        results[-1].start()
-
+    moves = []
+    for term, which in enumerate([1 - core, core]):
+        for index, target in enumerate(out_hbms[2 * term : 2 * term + 2]):
+            if not pieces:
+                moves.append((index, both.at[index, which], target))
+                continue
+            row_bit, column_bit = (low, upper) if index else (1 - low, 1 - upper)
+            for row in range(target.shape[0]):
+                for side in range(2):
+                    half = jnp.where(which == 0, side, column_bit)
+                    place = 2 * row + jnp.where(which == 0, row_bit, side)
+                    columns = slice(side * span, (side + 1) * span)
+                    moves.append((half, both.at[half, which, place], target.at[row, :, columns]))
     contract = (((0,), (0,)), ((), ()))
-    for index, operand in enumerate([features, aggregate]):
-        product = lax.dot_general(operand[...], grad[:, :span], contract, preferred_element_type=F32)
-        first[index] = product.astype(BF16).reshape(first.shape[1:])
-    for term, which in enumerate([1 - core, core]):
-        if pieces:
-            for leave, bit in enumerate([1 - low, low]):
-                for row in range(first.shape[1] // 2):
-                    send(first.at[which, 2 * row + bit], out_hbms[4 * term + leave].at[row])
-        else:
-            send(first.at[which], out_hbms[4 * term])
-    for index, operand in enumerate([features, aggregate]):
-        product = lax.dot_general(operand[...], grad[:, span:], contract, preferred_element_type=F32).astype(BF16)
-        for side in range(2):
-            second[index, side] = product[:, side * span // 2 : (side + 1) * span // 2]
-    for term, which in enumerate([1 - core, core]):
-        for leave, bit in enumerate([1 - upper, upper]):
-            send(second.at[which, bit], out_hbms[4 * term + 2 + leave])
+    results = [
+        pltpu.make_async_copy(source, target, out_sems.at[index]) for index, (_, source, target) in enumerate(moves)
+    ]
+    for half in range(2):
+        columns = slice(half * span, (half + 1) * span)
+        for index, operand in enumerate([features, aggregate]):
+            product = lax.dot_general(operand[...], grad[:, columns], contract, preferred_element_type=F32)
+            both[half, index] = product.astype(BF16).reshape(both.shape[2:])
+        for move, result in zip(moves, results):
+            pl.when(move[0] == half)(result.start)
     for result in results:
         result.wait()
 
@@ -230,8 +230,24 @@
     return lax.dynamic_slice_in_dim(value, which * size, size, axis)
 
 
-def low_half(term, which):
-    return lax.dynamic_index_in_dim(term.reshape(-1, 2, *term.shape[1:]), which, 1, keepdims=False)
+def first_pieces(term, depth, core, low, upper):
+    term = term.reshape(-1, 2, depth, 2, term.shape[1] // 2)
+    pieces = []
+    for row_bit, column_bit in ((1 - low, 1 - upper), (low, upper)):
+        rows = lax.dynamic_index_in_dim(term, row_bit, 1, keepdims=False)
+        columns = lax.dynamic_index_in_dim(term, column_bit, 3, keepdims=False).swapaxes(1, 2)
+        pieces.append(jnp.where(core == 0, rows, columns).reshape(term.shape[0], depth, -1))
+    return pieces
+
+
+def turn_swap(value, turn):
+    reps, doms = lax.axis_size("rep"), lax.axis_size("dom")
+    pairs = []
+    for rep in range(reps):
+        for dom in range(doms):
+            target = rep * doms + (dom ^ 1) if rep % 2 == turn else (rep ^ (reps // 2)) * doms + dom
+            pairs.append((rep * doms + dom, target))
+    return lax.ppermute(value, ("rep", "dom"), pairs)
 
 
 def column_half(term, which):
@@ -320,17 +336,16 @@
     upper = (high // (parts // 2)) % 2
     places = jnp.stack([core, flip, low, upper]).astype(jnp.int32)
     if tiled:
-        first_shapes = [jax.ShapeDtypeStruct((dom_size // 2, depth, span), BF16)] * 2
-        first_scratch = (2, dom_size, depth, span)
+        out_shapes = [jax.ShapeDtypeStruct((dom_size // 2, depth, hidden), BF16)] * 4
+        product_shape = (2, 2, dom_size, depth, span)
     else:
-        first_shapes = [jax.ShapeDtypeStruct((width, span), BF16), jax.ShapeDtypeStruct((8, 128), BF16)]
-        first_scratch = (2, width, span)
-    out_shapes = (first_shapes + [jax.ShapeDtypeStruct((width, span // 2), BF16)] * 2) * 2
+        out_shapes = [jax.ShapeDtypeStruct((width, span), BF16)] * 4
+        product_shape = (2, 2, width, span)
     outs = call(
         functools.partial(layer_kernel, sources, tiled),
         out_shapes,
         [SMEM, SMEM, VMEM] + [HBM] * (3 + sources),
-        [HBM] * 8,
+        [HBM] * 4,
         [
             pltpu.VMEM((rows, hidden), BF16),
             pltpu.VMEM((rows, width), BF16),
@@ -340,37 +355,32 @@
             pltpu.VMEM((2, 256, hidden), F32),
             pltpu.VMEM((rows, width), BF16),
             pltpu.VMEM((rows, hidden), BF16),
-            pltpu.VMEM(first_scratch, BF16),
-            pltpu.VMEM((2, 2, width, span // 2), BF16),
+            pltpu.VMEM(product_shape, BF16),
             DMA((2, rows // 256)),
             DMA((count,)),
             DMA((4,)),
-            DMA((2 * dom_size + 4,)),
+            DMA((4 * dom_size,)),
         ],
         flops=6 * rows * width * hidden,
         moved=16 * rows * hidden,
     )(places, in_block, received, total, features, cotangent, *weights[1])
-    outs = list(outs)
+    sent, kept = outs[:2], outs[2:]
     if not tiled:
-        for at in (0, 4):
-            term = outs[at].reshape(dom_size, depth, span)
-            outs[at], outs[at + 1] = low_half(term, 1 - low), low_half(term, low)
-    terms = [None] * 4
-    for at in (0, 2, 1, 3):
-        terms[at] = [outs[4 + at], swap(outs[at], "rep", 1)]
-    first = added([*terms[1], swap(added(terms[0]), "dom", 1)])
-    second = added([*terms[3], swap(added(terms[2]), "rep", parts)]).reshape(dom_size, depth, -1)
-    first = reduce_high(first, high, parts // 2)
-    second = exchanged(reduce_high(second, high, parts // 4), low_half, low, "dom", 1)
-    both = jnp.concatenate([first, second], axis=2)
+        sent, kept = [
+            first_pieces(jnp.concatenate(pair, axis=1), depth, which, low, upper)
+            for pair, which in ((sent, 1 - core), (kept, core))
+        ]
+    leave, stay = [[own, swap(piece, "rep", 1)] for own, piece in zip(kept, sent)]
+    held = added([*stay, turn_swap(added(leave), 0)])
+    bit = jnp.where(core == 0, upper, low)
+    held = added([column_half(held, bit), turn_swap(column_half(held, 1 - bit), 1)])
+    both = reduce_high(held, high, parts // 4)
     summed = lax.dynamic_index_in_dim(both, place, 0, keepdims=False).astype(F32)
     for step in range(1, dom_size // 2):
         piece = lax.dynamic_index_in_dim(both, place ^ step, 0, keepdims=False)
         summed = summed + swap(piece, "dom", 2 * step).astype(F32)
     summed = summed.astype(BF16)
-    size = summed.shape[1] // 2
-    held = gather_high(jnp.stack([summed[:, :size], summed[:, size:]]), high)
-    whole = jnp.concatenate([held[0], held[1]], axis=1)
+    whole = gather_high(summed, high)
     opposite = swap(whole, "rep", 1)
     return (
         jnp.where(core == 0, whole, opposite).astype(F32),

time: 117 us -> 117 us (level)
  waiting for transfers between devices: 60.3 us -> 62.1 us
    ppermute x0 -> x2, waiting for transfers between devices: none -> 16.8 us  [turn_swap(): return lax.ppermute(value, ('rep', 'dom'), pairs)]
    ppermute x17 -> x11, waiting for transfers between devices: 51.3 us -> 36.4 us  [swap(): lax.ppermute(value, axis, [(index, index ^ step) for index in range(size)])]
    ppermute x17 -> x11, starting transfers between devices: 15.7 us -> 11.5 us  [swap(): lax.ppermute(value, axis, [(index, index ^ step) for index in range(size)])]
    ppermute x0 -> x2, starting transfers between devices: none -> 3.09 us  [turn_swap(): return lax.ppermute(value, ('rep', 'dom'), pairs)]
    convert_element_type x6 -> x3, other arithmetic: 2.66 us -> 1.99 us  [added(): return sum((term.astype(F32) for term in terms)).astype(BF16)]
  transfers between devices with their start and end apart: 20 -> 16, of which waited for: 15 -> 13; matrix products, arithmetic and copies ran while one was open for 3% -> 2% of each run, Pallas kernels for 8% -> 8%
where the time goes in v14:
time: 117 us
  waiting for transfers between devices  62.1 us (53%)
  starting transfers between devices  25 us (21%)
  Pallas kernels  22.2 us (19%)
  other arithmetic  4.24 us (4%)
  local copies, waits for them, and re-layouts  2.18 us (2%)
    ppermute x11, waiting for transfers between devices, swap(): lax.ppermute(value, axis, [(index, index ^ step) for index in range(size)])  36.4 us
    ppermute x2, waiting for transfers between devices, turn_swap(): return lax.ppermute(value, ('rep', 'dom'), pairs)  16.8 us
    pallas_call x1, Pallas kernels, shards(): call(functools.partial(layer_kernel, sources, tiled), out_shapes, [SMEM,...  13 us
    ppermute x11, starting transfers between devices, swap(): lax.ppermute(value, axis, [(index, index ^ step) for index in range(size)])  11.5 us
    all_to_all x1, starting transfers between devices, shards(): lax.all_to_all(slots.reshape(dom_size, block, width), 'dom', split_axis=0...  5.58 us
    all_to_all x1, waiting for transfers between devices, shards(): lax.all_to_all(slots.reshape(dom_size, block, width), 'dom', split_axis=0...  5.08 us
    ppermute x2, starting transfers between devices, cross(): lax.ppermute(value, ('rep', 'dom'), [(source, target) for source, target...  4.77 us
    pallas_call x1, Pallas kernels, shards(): call(self_kernel, jax.ShapeDtypeStruct((rows, hidden), BF16), [SMEM] + [H...  4.67 us
  transfers between devices with their start and end apart: 16, of which 13 were waited for; matrix products, arithmetic and copies ran while one was open for 2% of the time, Pallas kernels for 8%

profile of v14, /device:TPU:0, one launch (start us, length us, event | category | flops | bytes accessed | tf_op | source)
XLA Modules:
  0.0 116.6 jit_solution(4384714999754003396)
XLA Ops:
  0.6 1.0 dynamic-slice_bitcast_fusion.3
  1.6 0.7 collective-permute-start
  2.3 4.1 %collective-permute-start.1 = (bf16[2,96,512]{2,1,0:T(8,128)(2,1)S(1)}, bf16[2,96,512]{2,1,0:T(8,128)(2,1)S(1)}, u32[]{:S(2)}, u32[]{:S(2)}) collective-permute-start(bf16[2,96,512]{2,1,0:T(8,128)(2,1)S(1)} %pad_maximum_fusion.3), channel_id=1, source_target_pairs={{0,4},{1,5},{2,6},{3,7},{4,0},{5,1},{6,2},{7,3},{8,13},{9,12},{10,... | collective-permute-start | bytes 589832 | tf_op jit(solution)/shard_map/ppermute | solution.py:31
  6.4 4.6 %shard_map.95 = bf16[1024,768]{1,0:T(8,128)(2,1)} custom-call(s32[32]{0:T(128)} %src_hbm.1, s32[32]{0:T(128)} %peer_hbm.1, bf16[32,128,128]{2,1,0:T(8,128)(2,1)} %tiles_hbm.1, bf16[1024,768]{1,0:T(8,128)(2,1)} %features_hbm.5), custom_call_target="tpu_custom_call" | custom-call | flops 1610612736 | bytes 4194304 | tf_op jit(solution)/shard_map/pallas_call | solution.py:284
  11.0 3.9 %collective-permute-done.1 = bf16[2,96,512]{2,1,0:T(8,128)(2,1)S(1)} collective-permute-done((bf16[2,96,512]{2,1,0:T(8,128)(2,1)S(1)}, bf16[2,96,512]{2,1,0:T(8,128)(2,1)S(1)}, u32[]{:S(2)}, u32[]{:S(2)}) %collective-permute-start.1) | collective-permute-done | bytes 196640 | tf_op jit(solution)/shard_map/ppermute | solution.py:31
  15.0 2.5 %collective-permute-start.2 = (bf16[2,2,96,512]{3,2,1,0:T(8,128)(2,1)S(1)}, bf16[2,2,96,512]{3,2,1,0:T(8,128)(2,1)S(1)}, u32[]{:S(2)}, u32[]{:S(2)}) collective-permute-start(bf16[2,2,96,512]{3,2,1,0:T(8,128)(2,1)S(1)} %pad_maximum_fusion.2), channel_id=1, source_target_pairs={{0,2},{1,3},{2,0},{3,1},{4,6},{5,7},{6,4},{7,5},{8,10},{9,11},{10,... | collective-permute-start | bytes 1179656 | tf_op jit(solution)/shard_map/ppermute | solution.py:23
  17.4 5.6 %all-to-all-start = ((bf16[8,128,768]{2,1,0:T(8,128)(2,1)}), bf16[8,128,768]{2,1,0:T(8,128)(2,1)S(1)}, u32[]{:S(2)}, u32[]{:S(2)}) async-start(bf16[8,128,768]{2,1,0:T(8,128)(2,1)} %bitcast.6), calls=%async_computation | async-start | bytes 3145728 | tf_op jit(solution)/shard_map/all_to_all | solution.py:309
  23.0 3.8 %collective-permute-done.2 = bf16[2,2,96,512]{3,2,1,0:T(8,128)(2,1)S(1)} collective-permute-done((bf16[2,2,96,512]{3,2,1,0:T(8,128)(2,1)S(1)}, bf16[2,2,96,512]{3,2,1,0:T(8,128)(2,1)S(1)}, u32[]{:S(2)}, u32[]{:S(2)}) %collective-permute-start.2) | collective-permute-done | bytes 393248 | tf_op jit(solution)/shard_map/ppermute | solution.py:23
  27.0 1.6 %collective-permute-start.3 = (bf16[2,4,96,512]{3,2,1,0:T(8,128)(2,1)S(1)}, bf16[2,4,96,512]{3,2,1,0:T(8,128)(2,1)S(1)}, u32[]{:S(2)}, u32[]{:S(2)}) collective-permute-start(bf16[2,4,96,512]{3,2,1,0:T(8,128)(2,1)S(1)} %bitcast.35), channel_id=1, source_target_pairs={{0,16},{8,24},{16,0},{24,8},{1,17},{9,25},{17,1},{25,9},{2,18},{10... | collective-permute-start | bytes 2359304 | tf_op jit(solution)/shard_map/ppermute | solution.py:23
  28.6 18.4 %collective-permute-done.3 = bf16[2,4,96,512]{3,2,1,0:T(8,128)(2,1)S(1)} collective-permute-done((bf16[2,4,96,512]{3,2,1,0:T(8,128)(2,1)S(1)}, bf16[2,4,96,512]{3,2,1,0:T(8,128)(2,1)S(1)}, u32[]{:S(2)}, u32[]{:S(2)}) %collective-permute-start.3) | collective-permute-done | bytes 786464 | tf_op jit(solution)/shard_map/ppermute | solution.py:23
  47.3 0.7 collective-permute-start.4
  48.1 0.7 pad_add_fusion.places_ref
  48.7 1.3 %collective-permute-done.4.refs_1_ = bf16[4,96,1024]{2,1,0:T(8,128)(2,1)} collective-permute-done((bf16[4,96,1024]{2,1,0:T(8,128)(2,1)S(1)}, bf16[4,96,1024]{2,1,0:T(8,128)(2,1)}, u32[]{:S(2)}, u32[]{:S(2)}) %collective-permute-start.4) | collective-permute-done | bytes 786464 | tf_op jit(solution)/shard_map/ppermute | solution.py:23
  50.0 4.7 %shard_map.96.total_hbm = bf16[1024,1024]{1,0:T(8,128)(2,1)} custom-call(s32[1]{0:T(128)} %bitcast.1.flip_ref, bf16[1024,768]{1,0:T(8,128)(2,1)} %features_hbm.5, bf16[4,96,1024]{2,1,0:T(8,128)(2,1)} %copy-done.3, bf16[4,96,1024]{2,1,0:T(8,128)(2,1)} %collective-permute-done.4.refs_1_), custom_call_target="tpu_custom_call" | custom-call | flops 1610612736 | bytes 7340032 | tf_op jit(solution)/shard_map/pallas_call | solution.py:319
  54.7 5.1 %all-to-all-done.slots_ref = bf16[8,128,768]{2,1,0:T(8,128)(2,1)S(1)} async-done(((bf16[8,128,768]{2,1,0:T(8,128)(2,1)}), bf16[8,128,768]{2,1,0:T(8,128)(2,1)S(1)}, u32[]{:S(2)}, u32[]{:S(2)}) %all-to-all-start) | async-done | bytes 1572896 | tf_op jit(solution)/shard_map/all_to_all | solution.py:309
  59.8 1.1 copy-done
  61.0 13.0 %shard_map.97 = (bf16[4,96,1024]{2,1,0:T(8,128)(2,1)}, bf16[4,96,1024]{2,1,0:T(8,128)(2,1)}, bf16[4,96,1024]{2,1,0:T(8,128)(2,1)}, bf16[4,96,1024]{2,1,0:T(8,128)(2,1)}) custom-call(s32[4]{0:T(128)} %pad_add_fusion.places_ref, s32[8]{0:T(128)} %into_ref.1, bf16[8,128,768]{2,1,0:T(8,128)(2,1)} %copy-done, bf16[1024,1024]{1,0:T(8,128)(2,1)} %shard_map.96.total_hbm, ...), custom_call_target="tpu_custom_call" | custom-call | flops 4831838208 | bytes 16777216 | tf_op jit(solution)/shard_map/pallas_call | solution.py:344
  74.0 0.5 collective-permute-start.6
  74.5 2.0 %collective-permute-done.7 = bf16[4,96,1024]{2,1,0:T(8,128)(2,1)S(1)} collective-permute-done((bf16[4,96,1024]{2,1,0:T(8,128)(2,1)}, bf16[4,96,1024]{2,1,0:T(8,128)(2,1)S(1)}, u32[]{:S(2)}, u32[]{:S(2)}) %collective-permute-start.7) | collective-permute-done | bytes 786464 | tf_op jit(solution)/shard_map/ppermute | solution.py:23
  76.5 1.4 %add_convert_fusion.1 = bf16[4,96,1024]{2,1,0:T(8,128)(2,1)S(1)} fusion(bf16[4,96,1024]{2,1,0:T(8,128)(2,1)S(1)} %collective-permute-done.7, bf16[4,96,1024]{2,1,0:T(8,128)(2,1)} %get-tuple-element.14), kind=kLoop, calls=%fused_computation.3 | loop fusion | flops 1572864 | bytes 2359296 | tf_op jit(solution)/shard_map/convert_element_type | solution.py:225
  78.0 1.5 %collective-permute-start.8 = (bf16[4,96,1024]{2,1,0:T(8,128)(2,1)S(1)}, bf16[4,96,1024]{2,1,0:T(8,128)(2,1)S(1)}, u32[]{:S(2)}, u32[]{:S(2)}) collective-permute-start(bf16[4,96,1024]{2,1,0:T(8,128)(2,1)S(1)} %add_convert_fusion.1), channel_id=1, source_target_pairs={{0,1},{1,0},{2,3},{3,2},{4,5},{5,4},{6,7},{7,6},{8,24},{9,25},{10,... | collective-permute-start | bytes 2359304 | tf_op jit(solution)/shard_map/ppermute | solution.py:250
  79.5 10.5 %collective-permute-done.8 = bf16[4,96,1024]{2,1,0:T(8,128)(2,1)S(1)} collective-permute-done((bf16[4,96,1024]{2,1,0:T(8,128)(2,1)S(1)}, bf16[4,96,1024]{2,1,0:T(8,128)(2,1)S(1)}, u32[]{:S(2)}, u32[]{:S(2)}) %collective-permute-start.8) | collective-permute-done | bytes 786464 | tf_op jit(solution)/shard_map/ppermute | solution.py:250
  90.5 1.6 %collective-permute-start.9 = (bf16[4,96,512]{2,1,0:T(8,128)(2,1)S(1)}, bf16[4,96,512]{2,1,0:T(8,128)(2,1)S(1)}, u32[]{:S(2)}, u32[]{:S(2)}) collective-permute-start(bf16[4,96,512]{2,1,0:T(8,128)(2,1)S(1)} %constant_dynamic-slice_fusion), channel_id=1, source_target_pairs={{0,16},{1,17},{2,18},{3,19},{4,20},{5,21},{6,22},{7,23},{8,9},{9,8... | collective-permute-start | bytes 1179656 | tf_op jit(solution)/shard_map/ppermute | solution.py:250
  92.1 6.3 %collective-permute-done.9 = bf16[4,96,512]{2,1,0:T(8,128)(2,1)S(1)} collective-permute-done((bf16[4,96,512]{2,1,0:T(8,128)(2,1)S(1)}, bf16[4,96,512]{2,1,0:T(8,128)(2,1)S(1)}, u32[]{:S(2)}, u32[]{:S(2)}) %collective-permute-start.9) | collective-permute-done | bytes 393248 | tf_op jit(solution)/shard_map/ppermute | solution.py:250
  98.6 4.2 %collective-permute-start.11 = (bf16[96,512]{1,0:T(8,128)(2,1)S(1)}, bf16[96,512]{1,0:T(8,128)(2,1)S(1)}, u32[]{:S(2)}, u32[]{:S(2)}) collective-permute-start(bf16[96,512]{1,0:T(8,128)(2,1)S(1)} %get-tuple-element.28), channel_id=1, source_target_pairs={{0,4},{1,5},{2,6},{3,7},{4,0},{5,1},{6,2},{7,3},{8,12},{9,13},{10,... | collective-permute-start | bytes 294920 | tf_op jit(solution)/shard_map/ppermute | solution.py:23
  103.0 0.8 collective-permute-done.10
  103.7 4.4 %collective-permute-done.11 = bf16[96,512]{1,0:T(8,128)(2,1)S(1)} collective-permute-done((bf16[96,512]{1,0:T(8,128)(2,1)S(1)}, bf16[96,512]{1,0:T(8,128)(2,1)S(1)}, u32[]{:S(2)}, u32[]{:S(2)}) %collective-permute-start.11) | collective-permute-done | bytes 98336 | tf_op jit(solution)/shard_map/ppermute | solution.py:23
  108.1 1.2 %collective-permute-done.12 = bf16[96,512]{1,0:T(8,128)(2,1)S(1)} collective-permute-done((bf16[96,512]{1,0:T(8,128)(2,1)S(1)}, bf16[96,512]{1,0:T(8,128)(2,1)S(1)}, u32[]{:S(2)}, u32[]{:S(2)}) %collective-permute-start.12) | collective-permute-done | bytes 98336 | tf_op jit(solution)/shard_map/ppermute | solution.py:23
  109.4 1.6 %collective-permute-start.13 = (bf16[96,512]{1,0:T(8,128)(2,1)S(1)}, bf16[96,512]{1,0:T(8,128)(2,1)S(1)}, u32[]{:S(2)}, u32[]{:S(2)}) collective-permute-start(bf16[96,512]{1,0:T(8,128)(2,1)S(1)} %fusion.5), channel_id=1, source_target_pairs={{0,16},{8,24},{16,0},{24,8},{1,17},{9,25},{17,1},{25,9},{2,18},{10... | collective-permute-start | bytes 294920 | tf_op jit(solution)/shard_map/ppermute | solution.py:23
  111.0 3.1 %collective-permute-done.13 = bf16[96,512]{1,0:T(8,128)(2,1)S(1)} collective-permute-done((bf16[96,512]{1,0:T(8,128)(2,1)S(1)}, bf16[96,512]{1,0:T(8,128)(2,1)S(1)}, u32[]{:S(2)}, u32[]{:S(2)}) %collective-permute-start.13) | collective-permute-done | bytes 98336 | tf_op jit(solution)/shard_map/ppermute | solution.py:23
  114.2 1.4 %collective-permute-done.14 = bf16[96,1024]{1,0:T(8,128)(2,1)S(1)} collective-permute-done((bf16[96,1024]{1,0:T(8,128)(2,1)S(1)}, bf16[96,1024]{1,0:T(8,128)(2,1)S(1)}, u32[]{:S(2)}, u32[]{:S(2)}) %collective-permute-start.14) | collective-permute-done | bytes 196640 | tf_op jit(solution)/shard_map/ppermute | solution.py:23
  115.6 1.0 select_convert_fusion
  (29 shorter events, 1.7 us)
Async XLA Ops:
  1.6 9.3 %collective-permute-start = (bf16[2,96,512]{2,1,0:T(8,128)(2,1)S(1)}, bf16[2,96,512]{2,1,0:T(8,128)(2,1)S(1)}, u32[]{:S(2)}, u32[]{:S(2)}) collective-permute-start(bf16[2,96,512]{2,1,0:T(8,128)(2,1)S(1)} %pad_maximum_fusion.3), channel_id=1, source_target_pairs={{8,9},{9,8},{10,11},{11,10},{12,13},{13,12},{14,15},{15,14},{24,25... | collective-permute-start | bytes 589832 | tf_op jit(solution)/shard_map/ppermute | solution.py:31
  2.3 12.6 %collective-permute-start.1 = (bf16[2,96,512]{2,1,0:T(8,128)(2,1)S(1)}, bf16[2,96,512]{2,1,0:T(8,128)(2,1)S(1)}, u32[]{:S(2)}, u32[]{:S(2)}) collective-permute-start(bf16[2,96,512]{2,1,0:T(8,128)(2,1)S(1)} %pad_maximum_fusion.3), channel_id=1, source_target_pairs={{0,4},{1,5},{2,6},{3,7},{4,0},{5,1},{6,2},{7,3},{8,13},{9,12},{10,... | collective-permute-start | bytes 589832 | tf_op jit(solution)/shard_map/ppermute | solution.py:31
  15.0 11.9 %collective-permute-start.2 = (bf16[2,2,96,512]{3,2,1,0:T(8,128)(2,1)S(1)}, bf16[2,2,96,512]{3,2,1,0:T(8,128)(2,1)S(1)}, u32[]{:S(2)}, u32[]{:S(2)}) collective-permute-start(bf16[2,2,96,512]{3,2,1,0:T(8,128)(2,1)S(1)} %pad_maximum_fusion.2), channel_id=1, source_target_pairs={{0,2},{1,3},{2,0},{3,1},{4,6},{5,7},{6,4},{7,5},{8,10},{9,11},{10,... | collective-permute-start | bytes 1179656 | tf_op jit(solution)/shard_map/ppermute | solution.py:23
  17.4 42.4 %all-to-all-start = ((bf16[8,128,768]{2,1,0:T(8,128)(2,1)}), bf16[8,128,768]{2,1,0:T(8,128)(2,1)S(1)}, u32[]{:S(2)}, u32[]{:S(2)}) async-start(bf16[8,128,768]{2,1,0:T(8,128)(2,1)} %bitcast.6), calls=%async_computation | async-start | bytes 3145728 | tf_op jit(solution)/shard_map/all_to_all | solution.py:309
  27.0 19.9 %collective-permute-start.3 = (bf16[2,4,96,512]{3,2,1,0:T(8,128)(2,1)S(1)}, bf16[2,4,96,512]{3,2,1,0:T(8,128)(2,1)S(1)}, u32[]{:S(2)}, u32[]{:S(2)}) collective-permute-start(bf16[2,4,96,512]{3,2,1,0:T(8,128)(2,1)S(1)} %bitcast.35), channel_id=1, source_target_pairs={{0,16},{8,24},{16,0},{24,8},{1,17},{9,25},{17,1},{25,9},{2,18},{10... | collective-permute-start | bytes 2359304 | tf_op jit(solution)/shard_map/ppermute | solution.py:23
  47.3 2.8 %copy-start.3 = (bf16[4,96,1024]{2,1,0:T(8,128)(2,1)}, bf16[4,96,1024]{2,1,0:T(8,128)(2,1)S(1)}, u32[]{:S(2)}) copy-start(bf16[4,96,1024]{2,1,0:T(8,128)(2,1)S(1)} %get-tuple-element.17.refs_0_) | copy-start | bytes 2359300
  47.3 7.5 %copy-start.1 = (bf16[4,96,1024]{2,1,0:T(8,128)(2,1)}, bf16[4,96,1024]{2,1,0:T(8,128)(2,1)S(1)}, u32[]{:S(2)}) copy-start(bf16[4,96,1024]{2,1,0:T(8,128)(2,1)S(1)} %get-tuple-element.16.refs_0_) | copy-start | bytes 2359300
  47.3 2.8 %collective-permute-start.4 = (bf16[4,96,1024]{2,1,0:T(8,128)(2,1)S(1)}, bf16[4,96,1024]{2,1,0:T(8,128)(2,1)}, u32[]{:S(2)}, u32[]{:S(2)}) collective-permute-start(bf16[4,96,1024]{2,1,0:T(8,128)(2,1)S(1)} %get-tuple-element.17.refs_0_), channel_id=1, source_target_pairs={{0,8},{8,0},{16,24},{24,16},{1,9},{9,1},{17,25},{25,17},{2,10},{10... | collective-permute-start | bytes 2359304 | tf_op jit(solution)/shard_map/ppermute | solution.py:23
  48.0 6.7 %collective-permute-start.5 = (bf16[4,96,1024]{2,1,0:T(8,128)(2,1)S(1)}, bf16[4,96,1024]{2,1,0:T(8,128)(2,1)}, u32[]{:S(2)}, u32[]{:S(2)}) collective-permute-start(bf16[4,96,1024]{2,1,0:T(8,128)(2,1)S(1)} %get-tuple-element.16.refs_0_), channel_id=1, source_target_pairs={{0,8},{8,0},{16,24},{24,16},{1,9},{9,1},{17,25},{25,17},{2,10},{10... | collective-permute-start | bytes 2359304 | tf_op jit(solution)/shard_map/ppermute | solution.py:23
  59.8 1.1 copy-start
  73.9 16.1 %copy-start.2 = (bf16[4,96,1024]{2,1,0:T(8,128)(2,1)S(1)}, bf16[4,96,1024]{2,1,0:T(8,128)(2,1)}, u32[]{:S(2)}) copy-start(bf16[4,96,1024]{2,1,0:T(8,128)(2,1)} %get-tuple-element.12) | copy-start | bytes 2359300
  73.9 2.6 %collective-permute-start.7 = (bf16[4,96,1024]{2,1,0:T(8,128)(2,1)}, bf16[4,96,1024]{2,1,0:T(8,128)(2,1)S(1)}, u32[]{:S(2)}, u32[]{:S(2)}) collective-permute-start(bf16[4,96,1024]{2,1,0:T(8,128)(2,1)} %get-tuple-element.15), channel_id=1, source_target_pairs={{0,8},{8,0},{16,24},{24,16},{1,9},{9,1},{17,25},{25,17},{2,10},{10... | collective-permute-start | bytes 2359304 | tf_op jit(solution)/shard_map/ppermute | solution.py:23
  74.0 5.5 %collective-permute-start.6 = (bf16[4,96,1024]{2,1,0:T(8,128)(2,1)}, bf16[4,96,1024]{2,1,0:T(8,128)(2,1)S(1)}, u32[]{:S(2)}, u32[]{:S(2)}) collective-permute-start(bf16[4,96,1024]{2,1,0:T(8,128)(2,1)} %get-tuple-element.13), channel_id=1, source_target_pairs={{0,8},{8,0},{16,24},{24,16},{1,9},{9,1},{17,25},{25,17},{2,10},{10... | collective-permute-start | bytes 2359304 | tf_op jit(solution)/shard_map/ppermute | solution.py:23
  78.0 12.1 %collective-permute-start.8 = (bf16[4,96,1024]{2,1,0:T(8,128)(2,1)S(1)}, bf16[4,96,1024]{2,1,0:T(8,128)(2,1)S(1)}, u32[]{:S(2)}, u32[]{:S(2)}) collective-permute-start(bf16[4,96,1024]{2,1,0:T(8,128)(2,1)S(1)} %add_convert_fusion.1), channel_id=1, source_target_pairs={{0,1},{1,0},{2,3},{3,2},{4,5},{5,4},{6,7},{7,6},{8,24},{9,25},{10,... | collective-permute-start | bytes 2359304 | tf_op jit(solution)/shard_map/ppermute | solution.py:250
  90.5 7.8 %collective-permute-start.9 = (bf16[4,96,512]{2,1,0:T(8,128)(2,1)S(1)}, bf16[4,96,512]{2,1,0:T(8,128)(2,1)S(1)}, u32[]{:S(2)}, u32[]{:S(2)}) collective-permute-start(bf16[4,96,512]{2,1,0:T(8,128)(2,1)S(1)} %constant_dynamic-slice_fusion), channel_id=1, source_target_pairs={{0,16},{1,17},{2,18},{3,19},{4,20},{5,21},{6,22},{7,23},{8,9},{9,8... | collective-permute-start | bytes 1179656 | tf_op jit(solution)/shard_map/ppermute | solution.py:250
  98.5 5.2 %collective-permute-start.10 = (bf16[96,512]{1,0:T(8,128)(2,1)S(1)}, bf16[96,512]{1,0:T(8,128)(2,1)S(1)}, u32[]{:S(2)}, u32[]{:S(2)}) collective-permute-start(bf16[96,512]{1,0:T(8,128)(2,1)S(1)} %get-tuple-element.26), channel_id=1, source_target_pairs={{0,2},{1,3},{2,0},{3,1},{4,6},{5,7},{6,4},{7,5},{8,10},{9,11},{10,... | collective-permute-start | bytes 294920 | tf_op jit(solution)/shard_map/ppermute | solution.py:23
  98.6 9.5 %collective-permute-start.11 = (bf16[96,512]{1,0:T(8,128)(2,1)S(1)}, bf16[96,512]{1,0:T(8,128)(2,1)S(1)}, u32[]{:S(2)}, u32[]{:S(2)}) collective-permute-start(bf16[96,512]{1,0:T(8,128)(2,1)S(1)} %get-tuple-element.28), channel_id=1, source_target_pairs={{0,4},{1,5},{2,6},{3,7},{4,0},{5,1},{6,2},{7,3},{8,12},{9,13},{10,... | collective-permute-start | bytes 294920 | tf_op jit(solution)/shard_map/ppermute | solution.py:23
  102.8 6.5 %collective-permute-start.12 = (bf16[96,512]{1,0:T(8,128)(2,1)S(1)}, bf16[96,512]{1,0:T(8,128)(2,1)S(1)}, u32[]{:S(2)}, u32[]{:S(2)}) collective-permute-start(bf16[96,512]{1,0:T(8,128)(2,1)S(1)} %get-tuple-element.27), channel_id=1, source_target_pairs={{0,6},{1,7},{2,4},{3,5},{4,2},{5,3},{6,0},{7,1},{8,14},{9,15},{10,... | collective-permute-start | bytes 294920 | tf_op jit(solution)/shard_map/ppermute | solution.py:23
  109.4 4.7 %collective-permute-start.13 = (bf16[96,512]{1,0:T(8,128)(2,1)S(1)}, bf16[96,512]{1,0:T(8,128)(2,1)S(1)}, u32[]{:S(2)}, u32[]{:S(2)}) collective-permute-start(bf16[96,512]{1,0:T(8,128)(2,1)S(1)} %fusion.5), channel_id=1, source_target_pairs={{0,16},{8,24},{16,0},{24,8},{1,17},{9,25},{17,1},{25,9},{2,18},{10... | collective-permute-start | bytes 294920 | tf_op jit(solution)/shard_map/ppermute | solution.py:23
  114.1 1.5 %collective-permute-start.14 = (bf16[96,1024]{1,0:T(8,128)(2,1)S(1)}, bf16[96,1024]{1,0:T(8,128)(2,1)S(1)}, u32[]{:S(2)}, u32[]{:S(2)}) collective-permute-start(bf16[96,1024]{1,0:T(8,128)(2,1)S(1)} %pad_maximum_fusion.4), channel_id=1, source_target_pairs={{0,8},{8,0},{16,24},{24,16},{1,9},{9,1},{17,25},{25,17},{2,10},{10... | collective-permute-start | bytes 589832 | tf_op jit(solution)/shard_map/ppermute | solution.py:23

commit v15 on v14

--- a/solution.py
+++ b/solution.py
@@ -113,12 +113,13 @@
 
 
 def layer_kernel(
-    sources, pieces, places_ref, into_ref, slots_ref, total_hbm, features_hbm, cotangent_hbm, *refs
+    sources, pieces, places_ref, into_ref, slots_hbm, total_hbm, features_hbm, cotangent_hbm, *refs
 ):
-    weight_hbms, out_hbms = refs[:sources], refs[sources:-13]
+    weight_hbms, out_hbms = refs[:sources], refs[sources:-15]
+    slots, slot_sems = refs[-15:-13]
     total, features, cotangent, weight, summed, values, aggregate, grad, both = refs[-13:-4]
     row_sems, weight_sems, feature_sems, out_sems = refs[-4:]
-    senders, block, _ = slots_ref.shape
+    senders, block, _ = slots.shape
     rows, hidden = grad.shape
     width = aggregate.shape[1]
     core, flip, low, upper = [places_ref[index] for index in range(4)]
@@ -128,13 +129,37 @@
     totals = split_copies(total_hbm, total, row_sems.at[0], parts)
     cotangents = split_copies(cotangent_hbm, cotangent, row_sems.at[1], parts)
     inputs = split_copies(features_hbm, features, feature_sems)
-    for copy in weights + totals + cotangents + inputs:
+    arrivals = [
+        pltpu.make_async_copy(slots_hbm.at[sender], slots.at[sender], slot_sems.at[sender]) for sender in range(senders)
+    ]
+    for copy in arrivals + weights + totals + cotangents + inputs:
         copy.start()
 
-    summed[...] = jnp.zeros_like(summed)
+    def target(sender):
+        return pl.ds(pl.multiple_of(into_ref[sender] * block, block), block)
+
+    for index in range(rows // block):
+        reached = functools.reduce(jnp.logical_or, [into_ref[sender] == index for sender in range(senders)])
+
+        @pl.when(jnp.logical_not(reached))
+        def _():
+            summed[index * block : (index + 1) * block, :] = jnp.zeros((block, width), F32)
+
     for sender in range(senders):
-        at = pl.ds(pl.multiple_of(into_ref[sender] * block, block), block)
-        summed[at, :] = summed[at, :] + slots_ref[sender].astype(F32)
+        arrivals[sender].wait()
+        if sender == 0:
+            summed[target(0), :] = slots[0].astype(F32)
+            continue
+        again = functools.reduce(jnp.logical_or, [into_ref[sender] == into_ref[index] for index in range(sender)])
+
+        @pl.when(again)
+        def _():
+            summed[target(sender), :] = summed[target(sender), :] + slots[sender].astype(F32)
+
+        @pl.when(jnp.logical_not(again))
+        def _():
+            summed[target(sender), :] = slots[sender].astype(F32)
+
     aggregate[...] = summed[...].astype(BF16)
     for copy in weights:
         copy.wait()
@@ -171,7 +196,7 @@
     for term, which in enumerate([1 - core, core]):
         for index, target in enumerate(out_hbms[2 * term : 2 * term + 2]):
             if not pieces:
-                moves.append((index, both.at[index, which], target))
+                moves.append((index, which, both.at[index, which], target))
                 continue
             row_bit, column_bit = (low, upper) if index else (1 - low, 1 - upper)
             for row in range(target.shape[0]):
@@ -179,18 +204,18 @@
                     half = jnp.where(which == 0, side, column_bit)
                     place = 2 * row + jnp.where(which == 0, row_bit, side)
                     columns = slice(side * span, (side + 1) * span)
-                    moves.append((half, both.at[half, which, place], target.at[row, :, columns]))
+                    moves.append((half, which, both.at[half, which, place], target.at[row, :, columns]))
     contract = (((0,), (0,)), ((), ()))
     results = [
-        pltpu.make_async_copy(source, target, out_sems.at[index]) for index, (_, source, target) in enumerate(moves)
+        pltpu.make_async_copy(source, target, out_sems.at[index]) for index, (_, _, source, target) in enumerate(moves)
     ]
     for half in range(2):
         columns = slice(half * span, (half + 1) * span)
         for index, operand in enumerate([features, aggregate]):
             product = lax.dot_general(operand[...], grad[:, columns], contract, preferred_element_type=F32)
             both[half, index] = product.astype(BF16).reshape(both.shape[2:])
-        for move, result in zip(moves, results):
-            pl.when(move[0] == half)(result.start)
+            for move, result in zip(moves, results):
+                pl.when(jnp.logical_and(move[0] == half, move[1] == index))(result.start)
     for result in results:
         result.wait()
 
@@ -331,6 +356,7 @@
         ],
         flops=2 * rows * width * hidden,
         moved=7 * rows * hidden,
+        vmem=62,
     )(flip.astype(jnp.int32).reshape(1), features, *weights[0])
     span = hidden // 2
     upper = (high // (parts // 2)) % 2
@@ -344,9 +370,11 @@
     outs = call(
         functools.partial(layer_kernel, sources, tiled),
         out_shapes,
-        [SMEM, SMEM, VMEM] + [HBM] * (3 + sources),
+        [SMEM, SMEM] + [HBM] * (4 + sources),
         [HBM] * 4,
         [
+            pltpu.VMEM((dom_size, block, width), BF16),
+            DMA((dom_size,)),
             pltpu.VMEM((rows, hidden), BF16),
             pltpu.VMEM((rows, width), BF16),
             pltpu.VMEM((rows, hidden), BF16),

time: 117 us -> 121 us (1.034)
  starting transfers between devices: 25 us -> 29.4 us
  waiting for transfers between devices: 62.1 us -> 59 us
  other arithmetic: 4.24 us -> 6.21 us
    all_to_all x1, waiting for transfers between devices: 5.08 us -> 1.19 us  [shards(): lax.all_to_all(slots.reshape(dom_size, block, width), 'dom', split_axis=0...]
    ppermute x11, starting transfers between devices: 11.5 us -> 13.8 us  [swap(): lax.ppermute(value, axis, [(index, index ^ step) for index in range(size)])]
    ppermute x2, starting transfers between devices: 3.09 us -> 5.24 us  [turn_swap(): return lax.ppermute(value, ('rep', 'dom'), pairs)]
    ppermute x11, waiting for transfers between devices: 36.4 us -> 37.9 us  [swap(): lax.ppermute(value, axis, [(index, index ^ step) for index in range(size)])]
  transfers between devices with their start and end apart: 16 -> 16, of which waited for: 13 -> 12; matrix products, arithmetic and copies ran while one was open for 2% -> 4% of each run, Pallas kernels for 8% -> 8%
where the time goes in v15:
time: 121 us; the launch traced here: 120 us
  waiting for transfers between devices  59 us (49%)
  starting transfers between devices  29.4 us (24%)
  Pallas kernels  22 us (18%)
  other arithmetic  6.21 us (5%)
  local copies, waits for them, and re-layouts  3.05 us (3%)
    ppermute x11, waiting for transfers between devices, swap(): lax.ppermute(value, axis, [(index, index ^ step) for index in range(size)])  37.9 us
    ppermute x2, waiting for transfers between devices, turn_swap(): return lax.ppermute(value, ('rep', 'dom'), pairs)  16 us
    ppermute x11, starting transfers between devices, swap(): lax.ppermute(value, axis, [(index, index ^ step) for index in range(size)])  13.8 us
    pallas_call x1, Pallas kernels, shards(): call(functools.partial(layer_kernel, sources, tiled), out_shapes, [SMEM,...  12.8 us
    all_to_all x1, starting transfers between devices, shards(): lax.all_to_all(slots.reshape(dom_size, block, width), 'dom', split_axis=0...  5.58 us
    ppermute x2, starting transfers between devices, turn_swap(): return lax.ppermute(value, ('rep', 'dom'), pairs)  5.24 us
    ppermute x2, starting transfers between devices, cross(): lax.ppermute(value, ('rep', 'dom'), [(source, target) for source, target...  4.77 us
    pallas_call x1, Pallas kernels, shards(): call(self_kernel, jax.ShapeDtypeStruct((rows, hidden), BF16), [SMEM] + [H...  4.66 us
  transfers between devices with their start and end apart: 16, of which 12 were waited for; matrix products, arithmetic and copies ran while one was open for 4% of the time, Pallas kernels for 8%

profile of v15, /device:TPU:0, one launch (start us, length us, event | category | flops | bytes accessed | tf_op | source)
XLA Modules:
  0.0 120.4 jit_solution(14554256922539097356)
XLA Ops:
  0.6 1.0 dynamic-slice_bitcast_fusion.3
  1.6 0.7 collective-permute-start
  2.3 4.1 %collective-permute-start.1 = (bf16[2,96,512]{2,1,0:T(8,128)(2,1)S(1)}, bf16[2,96,512]{2,1,0:T(8,128)(2,1)S(1)}, u32[]{:S(2)}, u32[]{:S(2)}) collective-permute-start(bf16[2,96,512]{2,1,0:T(8,128)(2,1)S(1)} %pad_maximum_fusion.3), channel_id=1, source_target_pairs={{0,4},{1,5},{2,6},{3,7},{4,0},{5,1},{6,2},{7,3},{8,13},{9,12},{10,... | collective-permute-start | bytes 589832 | tf_op jit(solution)/shard_map/ppermute | solution.py:31
  6.4 4.6 %shard_map.95 = bf16[1024,768]{1,0:T(8,128)(2,1)} custom-call(s32[32]{0:T(128)} %src_hbm.1, s32[32]{0:T(128)} %peer_hbm.1, bf16[32,128,128]{2,1,0:T(8,128)(2,1)} %tiles_hbm.1, bf16[1024,768]{1,0:T(8,128)(2,1)} %features_hbm.5), custom_call_target="tpu_custom_call" | custom-call | flops 1610612736 | bytes 4194304 | tf_op jit(solution)/shard_map/pallas_call | solution.py:309
  11.0 3.9 %collective-permute-done.1 = bf16[2,96,512]{2,1,0:T(8,128)(2,1)S(1)} collective-permute-done((bf16[2,96,512]{2,1,0:T(8,128)(2,1)S(1)}, bf16[2,96,512]{2,1,0:T(8,128)(2,1)S(1)}, u32[]{:S(2)}, u32[]{:S(2)}) %collective-permute-start.1) | collective-permute-done | bytes 196640 | tf_op jit(solution)/shard_map/ppermute | solution.py:31
  15.0 2.5 %collective-permute-start.2 = (bf16[2,2,96,512]{3,2,1,0:T(8,128)(2,1)S(1)}, bf16[2,2,96,512]{3,2,1,0:T(8,128)(2,1)S(1)}, u32[]{:S(2)}, u32[]{:S(2)}) collective-permute-start(bf16[2,2,96,512]{3,2,1,0:T(8,128)(2,1)S(1)} %pad_maximum_fusion.2), channel_id=1, source_target_pairs={{0,2},{1,3},{2,0},{3,1},{4,6},{5,7},{6,4},{7,5},{8,10},{9,11},{10,... | collective-permute-start | bytes 1179656 | tf_op jit(solution)/shard_map/ppermute | solution.py:23
  17.4 5.6 %all-to-all-start = ((bf16[8,128,768]{2,1,0:T(8,128)(2,1)}), bf16[8,128,768]{2,1,0:T(8,128)(2,1)S(1)}, u32[]{:S(2)}, u32[]{:S(2)}) async-start(bf16[8,128,768]{2,1,0:T(8,128)(2,1)} %bitcast.6), calls=%async_computation | async-start | bytes 3145728 | tf_op jit(solution)/shard_map/all_to_all | solution.py:334
  23.0 3.8 %collective-permute-done.2 = bf16[2,2,96,512]{3,2,1,0:T(8,128)(2,1)S(1)} collective-permute-done((bf16[2,2,96,512]{3,2,1,0:T(8,128)(2,1)S(1)}, bf16[2,2,96,512]{3,2,1,0:T(8,128)(2,1)S(1)}, u32[]{:S(2)}, u32[]{:S(2)}) %collective-permute-start.2) | collective-permute-done | bytes 393248 | tf_op jit(solution)/shard_map/ppermute | solution.py:23
  27.0 1.6 %collective-permute-start.3 = (bf16[2,4,96,512]{3,2,1,0:T(8,128)(2,1)S(1)}, bf16[2,4,96,512]{3,2,1,0:T(8,128)(2,1)}, u32[]{:S(2)}, u32[]{:S(2)}) collective-permute-start(bf16[2,4,96,512]{3,2,1,0:T(8,128)(2,1)S(1)} %bitcast.35), channel_id=1, source_target_pairs={{0,16},{8,24},{16,0},{24,8},{1,17},{9,25},{17,1},{25,9},{2,18},{10... | collective-permute-start | bytes 2359304 | tf_op jit(solution)/shard_map/ppermute | solution.py:23
  28.6 18.5 %collective-permute-done.3 = bf16[2,4,96,512]{3,2,1,0:T(8,128)(2,1)} collective-permute-done((bf16[2,4,96,512]{3,2,1,0:T(8,128)(2,1)S(1)}, bf16[2,4,96,512]{3,2,1,0:T(8,128)(2,1)}, u32[]{:S(2)}, u32[]{:S(2)}) %collective-permute-start.3) | collective-permute-done | bytes 786464 | tf_op jit(solution)/shard_map/ppermute | solution.py:23
  47.1 1.2 %broadcast_select_fusion = (bf16[2,4,96,512]{3,2,1,0:T(8,128)(2,1)S(1)}, bf16[2,4,96,512]{3,2,1,0:T(8,128)(2,1)S(1)}) fusion(bf16[2,4,96,512]{3,2,1,0:T(8,128)(2,1)S(1)} %bitcast.36, bf16[2,4,96,512]{3,2,1,0:T(8,128)(2,1)} %collective-permute-done.3, pred[]{:T(512)S(6)} %ne.20), kind=kLoop, calls=%fused_computation.10 | loop fusion | flops 786432 | bytes 3145729 | tf_op jit(solution)/shard_map/jit(_where)/select_n | solution.py:244
  48.3 1.1 fusion.2
  49.4 0.9 copy-done.2
  50.8 0.6 pad_add_fusion.places_ref
  51.4 2.5 %collective-permute-done.4.refs_1_ = bf16[4,96,1024]{2,1,0:T(8,128)(2,1)} collective-permute-done((bf16[4,96,1024]{2,1,0:T(8,128)(2,1)S(1)}, bf16[4,96,1024]{2,1,0:T(8,128)(2,1)}, u32[]{:S(2)}, u32[]{:S(2)}) %collective-permute-start.4) | collective-permute-done | bytes 786464 | tf_op jit(solution)/shard_map/ppermute | solution.py:23
  54.0 4.7 %shard_map.96.total_hbm = bf16[1024,1024]{1,0:T(8,128)(2,1)} custom-call(s32[1]{0:T(128)} %bitcast.1.flip_ref, bf16[1024,768]{1,0:T(8,128)(2,1)} %features_hbm.5, bf16[4,96,1024]{2,1,0:T(8,128)(2,1)} %copy-done.2, bf16[4,96,1024]{2,1,0:T(8,128)(2,1)} %collective-permute-done.4.refs_1_), custom_call_target="tpu_custom_call" | custom-call | flops 1610612736 | bytes 7340032 | tf_op jit(solution)/shard_map/pallas_call | solution.py:344
  58.6 1.2 all-to-all-done.slots_hbm
  59.8 1.1 copy-done
  61.0 12.8 %shard_map.97 = (bf16[4,96,1024]{2,1,0:T(8,128)(2,1)}, bf16[4,96,1024]{2,1,0:T(8,128)(2,1)}, bf16[4,96,1024]{2,1,0:T(8,128)(2,1)}, bf16[4,96,1024]{2,1,0:T(8,128)(2,1)}) custom-call(s32[4]{0:T(128)} %pad_add_fusion.places_ref, s32[8]{0:T(128)} %into_ref.1, bf16[8,128,768]{2,1,0:T(8,128)(2,1)} %copy-done, bf16[1024,1024]{1,0:T(8,128)(2,1)} %shard_map.96.total_hbm, ...), custom_call_target="tpu_custom_call" | custom-call | flops 4831838208 | bytes 16777216 | tf_op jit(solution)/shard_map/pallas_call | solution.py:370
  74.3 2.0 %collective-permute-done.7 = bf16[4,96,1024]{2,1,0:T(8,128)(2,1)S(1)} collective-permute-done((bf16[4,96,1024]{2,1,0:T(8,128)(2,1)}, bf16[4,96,1024]{2,1,0:T(8,128)(2,1)S(1)}, u32[]{:S(2)}, u32[]{:S(2)}) %collective-permute-start.7) | collective-permute-done | bytes 786464 | tf_op jit(solution)/shard_map/ppermute | solution.py:23
  76.3 1.4 %add_convert_fusion.1 = bf16[4,96,1024]{2,1,0:T(8,128)(2,1)S(1)} fusion(bf16[4,96,1024]{2,1,0:T(8,128)(2,1)S(1)} %collective-permute-done.7, bf16[4,96,1024]{2,1,0:T(8,128)(2,1)} %get-tuple-element.14), kind=kLoop, calls=%fused_computation.3 | loop fusion | flops 1572864 | bytes 2359296 | tf_op jit(solution)/shard_map/convert_element_type | solution.py:250
  77.8 3.4 %collective-permute-start.8 = (bf16[4,96,1024]{2,1,0:T(8,128)(2,1)S(1)}, bf16[4,96,1024]{2,1,0:T(8,128)(2,1)S(1)}, u32[]{:S(2)}, u32[]{:S(2)}) collective-permute-start(bf16[4,96,1024]{2,1,0:T(8,128)(2,1)S(1)} %add_convert_fusion.1), channel_id=1, source_target_pairs={{0,1},{1,0},{2,3},{3,2},{4,5},{5,4},{6,7},{7,6},{8,24},{9,25},{10,... | collective-permute-start | bytes 2359304 | tf_op jit(solution)/shard_map/ppermute | solution.py:275
  81.2 10.0 %collective-permute-done.8 = bf16[4,96,1024]{2,1,0:T(8,128)(2,1)S(1)} collective-permute-done((bf16[4,96,1024]{2,1,0:T(8,128)(2,1)S(1)}, bf16[4,96,1024]{2,1,0:T(8,128)(2,1)S(1)}, u32[]{:S(2)}, u32[]{:S(2)}) %collective-permute-start.8) | collective-permute-done | bytes 786464 | tf_op jit(solution)/shard_map/ppermute | solution.py:275
  91.7 1.8 %collective-permute-start.9 = (bf16[4,96,512]{2,1,0:T(8,128)(2,1)S(1)}, bf16[4,96,512]{2,1,0:T(8,128)(2,1)S(1)}, u32[]{:S(2)}, u32[]{:S(2)}) collective-permute-start(bf16[4,96,512]{2,1,0:T(8,128)(2,1)S(1)} %constant_dynamic-slice_fusion), channel_id=1, source_target_pairs={{0,16},{1,17},{2,18},{3,19},{4,20},{5,21},{6,22},{7,23},{8,9},{9,8... | collective-permute-start | bytes 1179656 | tf_op jit(solution)/shard_map/ppermute | solution.py:275
  93.5 6.0 %collective-permute-done.9 = bf16[4,96,512]{2,1,0:T(8,128)(2,1)S(1)} collective-permute-done((bf16[4,96,512]{2,1,0:T(8,128)(2,1)S(1)}, bf16[4,96,512]{2,1,0:T(8,128)(2,1)S(1)}, u32[]{:S(2)}, u32[]{:S(2)}) %collective-permute-start.9) | collective-permute-done | bytes 393248 | tf_op jit(solution)/shard_map/ppermute | solution.py:275
  99.7 6.9 %collective-permute-start.11 = (bf16[96,512]{1,0:T(8,128)(2,1)S(1)}, bf16[96,512]{1,0:T(8,128)(2,1)S(1)}, u32[]{:S(2)}, u32[]{:S(2)}) collective-permute-start(bf16[96,512]{1,0:T(8,128)(2,1)S(1)} %get-tuple-element.28), channel_id=1, source_target_pairs={{0,4},{1,5},{2,6},{3,7},{4,0},{5,1},{6,2},{7,3},{8,12},{9,13},{10,... | collective-permute-start | bytes 294920 | tf_op jit(solution)/shard_map/ppermute | solution.py:23
  106.6 5.3 %collective-permute-done.11 = bf16[96,512]{1,0:T(8,128)(2,1)S(1)} collective-permute-done((bf16[96,512]{1,0:T(8,128)(2,1)S(1)}, bf16[96,512]{1,0:T(8,128)(2,1)S(1)}, u32[]{:S(2)}, u32[]{:S(2)}) %collective-permute-start.11) | collective-permute-done | bytes 98336 | tf_op jit(solution)/shard_map/ppermute | solution.py:23
  111.9 1.2 %collective-permute-done.12 = bf16[96,512]{1,0:T(8,128)(2,1)S(1)} collective-permute-done((bf16[96,512]{1,0:T(8,128)(2,1)S(1)}, bf16[96,512]{1,0:T(8,128)(2,1)S(1)}, u32[]{:S(2)}, u32[]{:S(2)}) %collective-permute-start.12) | collective-permute-done | bytes 98336 | tf_op jit(solution)/shard_map/ppermute | solution.py:23
  113.2 1.6 %collective-permute-start.13 = (bf16[96,512]{1,0:T(8,128)(2,1)S(1)}, bf16[96,512]{1,0:T(8,128)(2,1)S(1)}, u32[]{:S(2)}, u32[]{:S(2)}) collective-permute-start(bf16[96,512]{1,0:T(8,128)(2,1)S(1)} %fusion.5), channel_id=1, source_target_pairs={{0,16},{8,24},{16,0},{24,8},{1,17},{9,25},{17,1},{25,9},{2,18},{10... | collective-permute-start | bytes 294920 | tf_op jit(solution)/shard_map/ppermute | solution.py:23
  114.8 3.1 %collective-permute-done.13 = bf16[96,512]{1,0:T(8,128)(2,1)S(1)} collective-permute-done((bf16[96,512]{1,0:T(8,128)(2,1)S(1)}, bf16[96,512]{1,0:T(8,128)(2,1)S(1)}, u32[]{:S(2)}, u32[]{:S(2)}) %collective-permute-start.13) | collective-permute-done | bytes 98336 | tf_op jit(solution)/shard_map/ppermute | solution.py:23
  118.0 1.4 %collective-permute-done.14 = bf16[96,1024]{1,0:T(8,128)(2,1)S(1)} collective-permute-done((bf16[96,1024]{1,0:T(8,128)(2,1)S(1)}, bf16[96,1024]{1,0:T(8,128)(2,1)S(1)}, u32[]{:S(2)}, u32[]{:S(2)}) %collective-permute-start.14) | collective-permute-done | bytes 196640 | tf_op jit(solution)/shard_map/ppermute | solution.py:23
  119.4 1.0 select_convert_fusion
  (27 shorter events, 2.2 us)
Async XLA Ops:
  1.6 9.3 %collective-permute-start = (bf16[2,96,512]{2,1,0:T(8,128)(2,1)S(1)}, bf16[2,96,512]{2,1,0:T(8,128)(2,1)S(1)}, u32[]{:S(2)}, u32[]{:S(2)}) collective-permute-start(bf16[2,96,512]{2,1,0:T(8,128)(2,1)S(1)} %pad_maximum_fusion.3), channel_id=1, source_target_pairs={{8,9},{9,8},{10,11},{11,10},{12,13},{13,12},{14,15},{15,14},{24,25... | collective-permute-start | bytes 589832 | tf_op jit(solution)/shard_map/ppermute | solution.py:31
  2.3 12.6 %collective-permute-start.1 = (bf16[2,96,512]{2,1,0:T(8,128)(2,1)S(1)}, bf16[2,96,512]{2,1,0:T(8,128)(2,1)S(1)}, u32[]{:S(2)}, u32[]{:S(2)}) collective-permute-start(bf16[2,96,512]{2,1,0:T(8,128)(2,1)S(1)} %pad_maximum_fusion.3), channel_id=1, source_target_pairs={{0,4},{1,5},{2,6},{3,7},{4,0},{5,1},{6,2},{7,3},{8,13},{9,12},{10,... | collective-permute-start | bytes 589832 | tf_op jit(solution)/shard_map/ppermute | solution.py:31
  15.0 11.9 %collective-permute-start.2 = (bf16[2,2,96,512]{3,2,1,0:T(8,128)(2,1)S(1)}, bf16[2,2,96,512]{3,2,1,0:T(8,128)(2,1)S(1)}, u32[]{:S(2)}, u32[]{:S(2)}) collective-permute-start(bf16[2,2,96,512]{3,2,1,0:T(8,128)(2,1)S(1)} %pad_maximum_fusion.2), channel_id=1, source_target_pairs={{0,2},{1,3},{2,0},{3,1},{4,6},{5,7},{6,4},{7,5},{8,10},{9,11},{10,... | collective-permute-start | bytes 1179656 | tf_op jit(solution)/shard_map/ppermute | solution.py:23
  17.4 42.4 %all-to-all-start = ((bf16[8,128,768]{2,1,0:T(8,128)(2,1)}), bf16[8,128,768]{2,1,0:T(8,128)(2,1)S(1)}, u32[]{:S(2)}, u32[]{:S(2)}) async-start(bf16[8,128,768]{2,1,0:T(8,128)(2,1)} %bitcast.6), calls=%async_computation | async-start | bytes 3145728 | tf_op jit(solution)/shard_map/all_to_all | solution.py:334
  27.0 20.0 %collective-permute-start.3 = (bf16[2,4,96,512]{3,2,1,0:T(8,128)(2,1)S(1)}, bf16[2,4,96,512]{3,2,1,0:T(8,128)(2,1)}, u32[]{:S(2)}, u32[]{:S(2)}) collective-permute-start(bf16[2,4,96,512]{3,2,1,0:T(8,128)(2,1)S(1)} %bitcast.35), channel_id=1, source_target_pairs={{0,16},{8,24},{16,0},{24,8},{1,17},{9,25},{17,1},{25,9},{2,18},{10... | collective-permute-start | bytes 2359304 | tf_op jit(solution)/shard_map/ppermute | solution.py:23
  49.4 0.9 copy-start.2
  50.3 3.7 %collective-permute-start.4 = (bf16[4,96,1024]{2,1,0:T(8,128)(2,1)S(1)}, bf16[4,96,1024]{2,1,0:T(8,128)(2,1)}, u32[]{:S(2)}, u32[]{:S(2)}) collective-permute-start(bf16[4,96,1024]{2,1,0:T(8,128)(2,1)S(1)} %get-tuple-element.17.refs_0_), channel_id=1, source_target_pairs={{0,8},{8,0},{16,24},{24,16},{1,9},{9,1},{17,25},{25,17},{2,10},{10... | collective-permute-start | bytes 2359304 | tf_op jit(solution)/shard_map/ppermute | solution.py:23
  50.8 7.8 %collective-permute-start.5 = (bf16[4,96,1024]{2,1,0:T(8,128)(2,1)}, bf16[4,96,1024]{2,1,0:T(8,128)(2,1)}, u32[]{:S(2)}, u32[]{:S(2)}) collective-permute-start(bf16[4,96,1024]{2,1,0:T(8,128)(2,1)} %get-tuple-element.16.refs_0_), channel_id=1, source_target_pairs={{0,8},{8,0},{16,24},{24,16},{1,9},{9,1},{17,25},{25,17},{2,10},{10... | collective-permute-start | bytes 2359304 | tf_op jit(solution)/shard_map/ppermute | solution.py:23
  59.8 1.1 copy-start
  73.7 17.4 %copy-start.1 = (bf16[4,96,1024]{2,1,0:T(8,128)(2,1)S(1)}, bf16[4,96,1024]{2,1,0:T(8,128)(2,1)}, u32[]{:S(2)}) copy-start(bf16[4,96,1024]{2,1,0:T(8,128)(2,1)} %get-tuple-element.12) | copy-start | bytes 2359300
  73.8 2.6 %collective-permute-start.7 = (bf16[4,96,1024]{2,1,0:T(8,128)(2,1)}, bf16[4,96,1024]{2,1,0:T(8,128)(2,1)S(1)}, u32[]{:S(2)}, u32[]{:S(2)}) collective-permute-start(bf16[4,96,1024]{2,1,0:T(8,128)(2,1)} %get-tuple-element.15), channel_id=1, source_target_pairs={{0,8},{8,0},{16,24},{24,16},{1,9},{9,1},{17,25},{25,17},{2,10},{10... | collective-permute-start | bytes 2359304 | tf_op jit(solution)/shard_map/ppermute | solution.py:23
  73.8 7.4 %collective-permute-start.6 = (bf16[4,96,1024]{2,1,0:T(8,128)(2,1)}, bf16[4,96,1024]{2,1,0:T(8,128)(2,1)S(1)}, u32[]{:S(2)}, u32[]{:S(2)}) collective-permute-start(bf16[4,96,1024]{2,1,0:T(8,128)(2,1)} %get-tuple-element.13), channel_id=1, source_target_pairs={{0,8},{8,0},{16,24},{24,16},{1,9},{9,1},{17,25},{25,17},{2,10},{10... | collective-permute-start | bytes 2359304 | tf_op jit(solution)/shard_map/ppermute | solution.py:23
  77.8 13.4 %collective-permute-start.8 = (bf16[4,96,1024]{2,1,0:T(8,128)(2,1)S(1)}, bf16[4,96,1024]{2,1,0:T(8,128)(2,1)S(1)}, u32[]{:S(2)}, u32[]{:S(2)}) collective-permute-start(bf16[4,96,1024]{2,1,0:T(8,128)(2,1)S(1)} %add_convert_fusion.1), channel_id=1, source_target_pairs={{0,1},{1,0},{2,3},{3,2},{4,5},{5,4},{6,7},{7,6},{8,24},{9,25},{10,... | collective-permute-start | bytes 2359304 | tf_op jit(solution)/shard_map/ppermute | solution.py:275
  91.7 7.8 %collective-permute-start.9 = (bf16[4,96,512]{2,1,0:T(8,128)(2,1)S(1)}, bf16[4,96,512]{2,1,0:T(8,128)(2,1)S(1)}, u32[]{:S(2)}, u32[]{:S(2)}) collective-permute-start(bf16[4,96,512]{2,1,0:T(8,128)(2,1)S(1)} %constant_dynamic-slice_fusion), channel_id=1, source_target_pairs={{0,16},{1,17},{2,18},{3,19},{4,20},{5,21},{6,22},{7,23},{8,9},{9,8... | collective-permute-start | bytes 1179656 | tf_op jit(solution)/shard_map/ppermute | solution.py:275
  99.7 6.9 %collective-permute-start.10 = (bf16[96,512]{1,0:T(8,128)(2,1)S(1)}, bf16[96,512]{1,0:T(8,128)(2,1)S(1)}, u32[]{:S(2)}, u32[]{:S(2)}) collective-permute-start(bf16[96,512]{1,0:T(8,128)(2,1)S(1)} %get-tuple-element.26), channel_id=1, source_target_pairs={{0,2},{1,3},{2,0},{3,1},{4,6},{5,7},{6,4},{7,5},{8,10},{9,11},{10,... | collective-permute-start | bytes 294920 | tf_op jit(solution)/shard_map/ppermute | solution.py:23
  99.7 12.2 %collective-permute-start.11 = (bf16[96,512]{1,0:T(8,128)(2,1)S(1)}, bf16[96,512]{1,0:T(8,128)(2,1)S(1)}, u32[]{:S(2)}, u32[]{:S(2)}) collective-permute-start(bf16[96,512]{1,0:T(8,128)(2,1)S(1)} %get-tuple-element.28), channel_id=1, source_target_pairs={{0,4},{1,5},{2,6},{3,7},{4,0},{5,1},{6,2},{7,3},{8,12},{9,13},{10,... | collective-permute-start | bytes 294920 | tf_op jit(solution)/shard_map/ppermute | solution.py:23
  106.6 6.5 %collective-permute-start.12 = (bf16[96,512]{1,0:T(8,128)(2,1)S(1)}, bf16[96,512]{1,0:T(8,128)(2,1)S(1)}, u32[]{:S(2)}, u32[]{:S(2)}) collective-permute-start(bf16[96,512]{1,0:T(8,128)(2,1)S(1)} %get-tuple-element.27), channel_id=1, source_target_pairs={{0,6},{1,7},{2,4},{3,5},{4,2},{5,3},{6,0},{7,1},{8,14},{9,15},{10,... | collective-permute-start | bytes 294920 | tf_op jit(solution)/shard_map/ppermute | solution.py:23
  113.2 4.7 %collective-permute-start.13 = (bf16[96,512]{1,0:T(8,128)(2,1)S(1)}, bf16[96,512]{1,0:T(8,128)(2,1)S(1)}, u32[]{:S(2)}, u32[]{:S(2)}) collective-permute-start(bf16[96,512]{1,0:T(8,128)(2,1)S(1)} %fusion.5), channel_id=1, source_target_pairs={{0,16},{8,24},{16,0},{24,8},{1,17},{9,25},{17,1},{25,9},{2,18},{10... | collective-permute-start | bytes 294920 | tf_op jit(solution)/shard_map/ppermute | solution.py:23
  117.9 1.5 %collective-permute-start.14 = (bf16[96,1024]{1,0:T(8,128)(2,1)S(1)}, bf16[96,1024]{1,0:T(8,128)(2,1)S(1)}, u32[]{:S(2)}, u32[]{:S(2)}) collective-permute-start(bf16[96,1024]{1,0:T(8,128)(2,1)S(1)} %pad_maximum_fusion.4), channel_id=1, source_target_pairs={{0,8},{8,0},{16,24},{24,16},{1,9},{9,1},{17,25},{25,17},{2,10},{10... | collective-permute-start | bytes 589832 | tf_op jit(solution)/shard_map/ppermute | solution.py:23

commit v16 on v15

--- a/solution.py
+++ b/solution.py
@@ -132,7 +132,7 @@
     arrivals = [
         pltpu.make_async_copy(slots_hbm.at[sender], slots.at[sender], slot_sems.at[sender]) for sender in range(senders)
     ]
-    for copy in arrivals + weights + totals + cotangents + inputs:
+    for copy in arrivals + weights + totals[:1] + cotangents[:1]:
         copy.start()
 
     def target(sender):
@@ -145,8 +145,11 @@
         def _():
             summed[index * block : (index + 1) * block, :] = jnp.zeros((block, width), F32)
 
+    for copy in arrivals:
+        copy.wait()
+    for copy in [copy for pair in zip(totals[1:], cotangents[1:]) for copy in pair] + inputs:
+        copy.start()
     for sender in range(senders):
-        arrivals[sender].wait()
         if sender == 0:
             summed[target(0), :] = slots[0].astype(F32)
             continue
@@ -356,7 +359,6 @@
         ],
         flops=2 * rows * width * hidden,
         moved=7 * rows * hidden,
-        vmem=62,
     )(flip.astype(jnp.int32).reshape(1), features, *weights[0])
     span = hidden // 2
     upper = (high // (parts // 2)) % 2

time: 121 us -> 116 us (0.959)
  starting transfers between devices: 29.4 us -> 25 us
  waiting for transfers between devices: 59 us -> 62.1 us
  other arithmetic: 6.21 us -> 4.24 us
    all_to_all x1, waiting for transfers between devices: 1.19 us -> 5.08 us  [shards(): lax.all_to_all(slots.reshape(dom_size, block, width), 'dom', split_axis=0...]
    ppermute x11, starting transfers between devices: 13.8 us -> 11.5 us  [swap(): lax.ppermute(value, axis, [(index, index ^ step) for index in range(size)])]
    ppermute x2, starting transfers between devices: 5.24 us -> 3.11 us  [turn_swap(): return lax.ppermute(value, ('rep', 'dom'), pairs)]
    ppermute x11, waiting for transfers between devices: 37.9 us -> 36.4 us  [swap(): lax.ppermute(value, axis, [(index, index ^ step) for index in range(size)])]
  transfers between devices with their start and end apart: 16 -> 16, of which waited for: 12 -> 13; matrix products, arithmetic and copies ran while one was open for 4% -> 2% of each run, Pallas kernels for 8% -> 8%
where the time goes in v16:
time: 116 us; the launch traced here: 115 us
  waiting for transfers between devices  62.1 us (54%)
  starting transfers between devices  25 us (22%)
  Pallas kernels  21.1 us (18%)
  other arithmetic  4.24 us (4%)
  local copies, waits for them, and re-layouts  2.18 us (2%)
    ppermute x11, waiting for transfers between devices, swap(): lax.ppermute(value, axis, [(index, index ^ step) for index in range(size)])  36.4 us
    ppermute x2, waiting for transfers between devices, turn_swap(): return lax.ppermute(value, ('rep', 'dom'), pairs)  16.8 us
    pallas_call x1, Pallas kernels, shards(): call(functools.partial(layer_kernel, sources, tiled), out_shapes, [SMEM,...  11.9 us
    ppermute x11, starting transfers between devices, swap(): lax.ppermute(value, axis, [(index, index ^ step) for index in range(size)])  11.5 us
    all_to_all x1, starting transfers between devices, shards(): lax.all_to_all(slots.reshape(dom_size, block, width), 'dom', split_axis=0...  5.58 us
    all_to_all x1, waiting for transfers between devices, shards(): lax.all_to_all(slots.reshape(dom_size, block, width), 'dom', split_axis=0...  5.08 us
    ppermute x2, starting transfers between devices, cross(): lax.ppermute(value, ('rep', 'dom'), [(source, target) for source, target...  4.77 us
    pallas_call x1, Pallas kernels, shards(): call(self_kernel, jax.ShapeDtypeStruct((rows, hidden), BF16), [SMEM] + [H...  4.67 us
  transfers between devices with their start and end apart: 16, of which 13 were waited for; matrix products, arithmetic and copies ran while one was open for 2% of the time, Pallas kernels for 8%

profile of v16, /device:TPU:0, one launch (start us, length us, event | category | flops | bytes accessed | tf_op | source)
XLA Modules:
  0.0 115.5 jit_solution(3760389476704631369)
XLA Ops:
  0.6 1.0 dynamic-slice_bitcast_fusion.3
  1.6 0.7 collective-permute-start
  2.3 4.1 %collective-permute-start.1 = (bf16[2,96,512]{2,1,0:T(8,128)(2,1)S(1)}, bf16[2,96,512]{2,1,0:T(8,128)(2,1)S(1)}, u32[]{:S(2)}, u32[]{:S(2)}) collective-permute-start(bf16[2,96,512]{2,1,0:T(8,128)(2,1)S(1)} %pad_maximum_fusion.3), channel_id=1, source_target_pairs={{0,4},{1,5},{2,6},{3,7},{4,0},{5,1},{6,2},{7,3},{8,13},{9,12},{10,... | collective-permute-start | bytes 589832 | tf_op jit(solution)/shard_map/ppermute | solution.py:31
  6.4 4.6 %shard_map.95 = bf16[1024,768]{1,0:T(8,128)(2,1)} custom-call(s32[32]{0:T(128)} %src_hbm.1, s32[32]{0:T(128)} %peer_hbm.1, bf16[32,128,128]{2,1,0:T(8,128)(2,1)} %tiles_hbm.1, bf16[1024,768]{1,0:T(8,128)(2,1)} %features_hbm.5), custom_call_target="tpu_custom_call" | custom-call | flops 1610612736 | bytes 4194304 | tf_op jit(solution)/shard_map/pallas_call | solution.py:312
  11.0 3.9 %collective-permute-done.1 = bf16[2,96,512]{2,1,0:T(8,128)(2,1)S(1)} collective-permute-done((bf16[2,96,512]{2,1,0:T(8,128)(2,1)S(1)}, bf16[2,96,512]{2,1,0:T(8,128)(2,1)S(1)}, u32[]{:S(2)}, u32[]{:S(2)}) %collective-permute-start.1) | collective-permute-done | bytes 196640 | tf_op jit(solution)/shard_map/ppermute | solution.py:31
  15.0 2.5 %collective-permute-start.2 = (bf16[2,2,96,512]{3,2,1,0:T(8,128)(2,1)S(1)}, bf16[2,2,96,512]{3,2,1,0:T(8,128)(2,1)S(1)}, u32[]{:S(2)}, u32[]{:S(2)}) collective-permute-start(bf16[2,2,96,512]{3,2,1,0:T(8,128)(2,1)S(1)} %pad_maximum_fusion.2), channel_id=1, source_target_pairs={{0,2},{1,3},{2,0},{3,1},{4,6},{5,7},{6,4},{7,5},{8,10},{9,11},{10,... | collective-permute-start | bytes 1179656 | tf_op jit(solution)/shard_map/ppermute | solution.py:23
  17.4 5.6 %all-to-all-start = ((bf16[8,128,768]{2,1,0:T(8,128)(2,1)}), bf16[8,128,768]{2,1,0:T(8,128)(2,1)S(1)}, u32[]{:S(2)}, u32[]{:S(2)}) async-start(bf16[8,128,768]{2,1,0:T(8,128)(2,1)} %bitcast.6), calls=%async_computation | async-start | bytes 3145728 | tf_op jit(solution)/shard_map/all_to_all | solution.py:337
  23.0 3.8 %collective-permute-done.2 = bf16[2,2,96,512]{3,2,1,0:T(8,128)(2,1)S(1)} collective-permute-done((bf16[2,2,96,512]{3,2,1,0:T(8,128)(2,1)S(1)}, bf16[2,2,96,512]{3,2,1,0:T(8,128)(2,1)S(1)}, u32[]{:S(2)}, u32[]{:S(2)}) %collective-permute-start.2) | collective-permute-done | bytes 393248 | tf_op jit(solution)/shard_map/ppermute | solution.py:23
  27.0 1.6 %collective-permute-start.3 = (bf16[2,4,96,512]{3,2,1,0:T(8,128)(2,1)S(1)}, bf16[2,4,96,512]{3,2,1,0:T(8,128)(2,1)S(1)}, u32[]{:S(2)}, u32[]{:S(2)}) collective-permute-start(bf16[2,4,96,512]{3,2,1,0:T(8,128)(2,1)S(1)} %bitcast.35), channel_id=1, source_target_pairs={{0,16},{8,24},{16,0},{24,8},{1,17},{9,25},{17,1},{25,9},{2,18},{10... | collective-permute-start | bytes 2359304 | tf_op jit(solution)/shard_map/ppermute | solution.py:23
  28.6 18.4 %collective-permute-done.3 = bf16[2,4,96,512]{3,2,1,0:T(8,128)(2,1)S(1)} collective-permute-done((bf16[2,4,96,512]{3,2,1,0:T(8,128)(2,1)S(1)}, bf16[2,4,96,512]{3,2,1,0:T(8,128)(2,1)S(1)}, u32[]{:S(2)}, u32[]{:S(2)}) %collective-permute-start.3) | collective-permute-done | bytes 786464 | tf_op jit(solution)/shard_map/ppermute | solution.py:23
  47.3 0.7 collective-permute-start.4
  48.1 0.7 pad_add_fusion.places_ref
  48.7 1.3 %collective-permute-done.4.refs_1_ = bf16[4,96,1024]{2,1,0:T(8,128)(2,1)} collective-permute-done((bf16[4,96,1024]{2,1,0:T(8,128)(2,1)S(1)}, bf16[4,96,1024]{2,1,0:T(8,128)(2,1)}, u32[]{:S(2)}, u32[]{:S(2)}) %collective-permute-start.4) | collective-permute-done | bytes 786464 | tf_op jit(solution)/shard_map/ppermute | solution.py:23
  50.0 4.7 %shard_map.96.total_hbm = bf16[1024,1024]{1,0:T(8,128)(2,1)} custom-call(s32[1]{0:T(128)} %bitcast.1.flip_ref, bf16[1024,768]{1,0:T(8,128)(2,1)} %features_hbm.5, bf16[4,96,1024]{2,1,0:T(8,128)(2,1)} %copy-done.3, bf16[4,96,1024]{2,1,0:T(8,128)(2,1)} %collective-permute-done.4.refs_1_), custom_call_target="tpu_custom_call" | custom-call | flops 1610612736 | bytes 7340032 | tf_op jit(solution)/shard_map/pallas_call | solution.py:347
  54.7 5.1 %all-to-all-done.slots_hbm = bf16[8,128,768]{2,1,0:T(8,128)(2,1)S(1)} async-done(((bf16[8,128,768]{2,1,0:T(8,128)(2,1)}), bf16[8,128,768]{2,1,0:T(8,128)(2,1)S(1)}, u32[]{:S(2)}, u32[]{:S(2)}) %all-to-all-start) | async-done | bytes 1572896 | tf_op jit(solution)/shard_map/all_to_all | solution.py:337
  59.8 1.1 copy-done
  61.0 11.9 %shard_map.97 = (bf16[4,96,1024]{2,1,0:T(8,128)(2,1)}, bf16[4,96,1024]{2,1,0:T(8,128)(2,1)}, bf16[4,96,1024]{2,1,0:T(8,128)(2,1)}, bf16[4,96,1024]{2,1,0:T(8,128)(2,1)}) custom-call(s32[4]{0:T(128)} %pad_add_fusion.places_ref, s32[8]{0:T(128)} %into_ref.1, bf16[8,128,768]{2,1,0:T(8,128)(2,1)} %copy-done, bf16[1024,1024]{1,0:T(8,128)(2,1)} %shard_map.96.total_hbm, ...), custom_call_target="tpu_custom_call" | custom-call | flops 4831838208 | bytes 16777216 | tf_op jit(solution)/shard_map/pallas_call | solution.py:372
  72.9 0.5 collective-permute-start.6
  73.4 2.0 %collective-permute-done.7 = bf16[4,96,1024]{2,1,0:T(8,128)(2,1)S(1)} collective-permute-done((bf16[4,96,1024]{2,1,0:T(8,128)(2,1)}, bf16[4,96,1024]{2,1,0:T(8,128)(2,1)S(1)}, u32[]{:S(2)}, u32[]{:S(2)}) %collective-permute-start.7) | collective-permute-done | bytes 786464 | tf_op jit(solution)/shard_map/ppermute | solution.py:23
  75.4 1.4 %add_convert_fusion.1 = bf16[4,96,1024]{2,1,0:T(8,128)(2,1)S(1)} fusion(bf16[4,96,1024]{2,1,0:T(8,128)(2,1)S(1)} %collective-permute-done.7, bf16[4,96,1024]{2,1,0:T(8,128)(2,1)} %get-tuple-element.14), kind=kLoop, calls=%fused_computation.3 | loop fusion | flops 1572864 | bytes 2359296 | tf_op jit(solution)/shard_map/convert_element_type | solution.py:253
  76.9 1.5 %collective-permute-start.8 = (bf16[4,96,1024]{2,1,0:T(8,128)(2,1)S(1)}, bf16[4,96,1024]{2,1,0:T(8,128)(2,1)S(1)}, u32[]{:S(2)}, u32[]{:S(2)}) collective-permute-start(bf16[4,96,1024]{2,1,0:T(8,128)(2,1)S(1)} %add_convert_fusion.1), channel_id=1, source_target_pairs={{0,1},{1,0},{2,3},{3,2},{4,5},{5,4},{6,7},{7,6},{8,24},{9,25},{10,... | collective-permute-start | bytes 2359304 | tf_op jit(solution)/shard_map/ppermute | solution.py:278
  78.4 10.5 %collective-permute-done.8 = bf16[4,96,1024]{2,1,0:T(8,128)(2,1)S(1)} collective-permute-done((bf16[4,96,1024]{2,1,0:T(8,128)(2,1)S(1)}, bf16[4,96,1024]{2,1,0:T(8,128)(2,1)S(1)}, u32[]{:S(2)}, u32[]{:S(2)}) %collective-permute-start.8) | collective-permute-done | bytes 786464 | tf_op jit(solution)/shard_map/ppermute | solution.py:278
  89.4 1.6 %collective-permute-start.9 = (bf16[4,96,512]{2,1,0:T(8,128)(2,1)S(1)}, bf16[4,96,512]{2,1,0:T(8,128)(2,1)S(1)}, u32[]{:S(2)}, u32[]{:S(2)}) collective-permute-start(bf16[4,96,512]{2,1,0:T(8,128)(2,1)S(1)} %constant_dynamic-slice_fusion), channel_id=1, source_target_pairs={{0,16},{1,17},{2,18},{3,19},{4,20},{5,21},{6,22},{7,23},{8,9},{9,8... | collective-permute-start | bytes 1179656 | tf_op jit(solution)/shard_map/ppermute | solution.py:278
  91.0 6.3 %collective-permute-done.9 = bf16[4,96,512]{2,1,0:T(8,128)(2,1)S(1)} collective-permute-done((bf16[4,96,512]{2,1,0:T(8,128)(2,1)S(1)}, bf16[4,96,512]{2,1,0:T(8,128)(2,1)S(1)}, u32[]{:S(2)}, u32[]{:S(2)}) %collective-permute-start.9) | collective-permute-done | bytes 393248 | tf_op jit(solution)/shard_map/ppermute | solution.py:278
  97.5 4.2 %collective-permute-start.11 = (bf16[96,512]{1,0:T(8,128)(2,1)S(1)}, bf16[96,512]{1,0:T(8,128)(2,1)S(1)}, u32[]{:S(2)}, u32[]{:S(2)}) collective-permute-start(bf16[96,512]{1,0:T(8,128)(2,1)S(1)} %get-tuple-element.28), channel_id=1, source_target_pairs={{0,4},{1,5},{2,6},{3,7},{4,0},{5,1},{6,2},{7,3},{8,12},{9,13},{10,... | collective-permute-start | bytes 294920 | tf_op jit(solution)/shard_map/ppermute | solution.py:23
  101.9 0.8 collective-permute-done.10
  102.6 4.4 %collective-permute-done.11 = bf16[96,512]{1,0:T(8,128)(2,1)S(1)} collective-permute-done((bf16[96,512]{1,0:T(8,128)(2,1)S(1)}, bf16[96,512]{1,0:T(8,128)(2,1)S(1)}, u32[]{:S(2)}, u32[]{:S(2)}) %collective-permute-start.11) | collective-permute-done | bytes 98336 | tf_op jit(solution)/shard_map/ppermute | solution.py:23
  107.0 1.2 %collective-permute-done.12 = bf16[96,512]{1,0:T(8,128)(2,1)S(1)} collective-permute-done((bf16[96,512]{1,0:T(8,128)(2,1)S(1)}, bf16[96,512]{1,0:T(8,128)(2,1)S(1)}, u32[]{:S(2)}, u32[]{:S(2)}) %collective-permute-start.12) | collective-permute-done | bytes 98336 | tf_op jit(solution)/shard_map/ppermute | solution.py:23
  108.3 1.6 %collective-permute-start.13 = (bf16[96,512]{1,0:T(8,128)(2,1)S(1)}, bf16[96,512]{1,0:T(8,128)(2,1)S(1)}, u32[]{:S(2)}, u32[]{:S(2)}) collective-permute-start(bf16[96,512]{1,0:T(8,128)(2,1)S(1)} %fusion.5), channel_id=1, source_target_pairs={{0,16},{8,24},{16,0},{24,8},{1,17},{9,25},{17,1},{25,9},{2,18},{10... | collective-permute-start | bytes 294920 | tf_op jit(solution)/shard_map/ppermute | solution.py:23
  109.9 3.1 %collective-permute-done.13 = bf16[96,512]{1,0:T(8,128)(2,1)S(1)} collective-permute-done((bf16[96,512]{1,0:T(8,128)(2,1)S(1)}, bf16[96,512]{1,0:T(8,128)(2,1)S(1)}, u32[]{:S(2)}, u32[]{:S(2)}) %collective-permute-start.13) | collective-permute-done | bytes 98336 | tf_op jit(solution)/shard_map/ppermute | solution.py:23
  113.1 1.4 %collective-permute-done.14 = bf16[96,1024]{1,0:T(8,128)(2,1)S(1)} collective-permute-done((bf16[96,1024]{1,0:T(8,128)(2,1)S(1)}, bf16[96,1024]{1,0:T(8,128)(2,1)S(1)}, u32[]{:S(2)}, u32[]{:S(2)}) %collective-permute-start.14) | collective-permute-done | bytes 196640 | tf_op jit(solution)/shard_map/ppermute | solution.py:23
  114.5 1.0 select_convert_fusion
  (29 shorter events, 1.7 us)
Async XLA Ops:
  1.6 9.3 %collective-permute-start = (bf16[2,96,512]{2,1,0:T(8,128)(2,1)S(1)}, bf16[2,96,512]{2,1,0:T(8,128)(2,1)S(1)}, u32[]{:S(2)}, u32[]{:S(2)}) collective-permute-start(bf16[2,96,512]{2,1,0:T(8,128)(2,1)S(1)} %pad_maximum_fusion.3), channel_id=1, source_target_pairs={{8,9},{9,8},{10,11},{11,10},{12,13},{13,12},{14,15},{15,14},{24,25... | collective-permute-start | bytes 589832 | tf_op jit(solution)/shard_map/ppermute | solution.py:31
  2.3 12.6 %collective-permute-start.1 = (bf16[2,96,512]{2,1,0:T(8,128)(2,1)S(1)}, bf16[2,96,512]{2,1,0:T(8,128)(2,1)S(1)}, u32[]{:S(2)}, u32[]{:S(2)}) collective-permute-start(bf16[2,96,512]{2,1,0:T(8,128)(2,1)S(1)} %pad_maximum_fusion.3), channel_id=1, source_target_pairs={{0,4},{1,5},{2,6},{3,7},{4,0},{5,1},{6,2},{7,3},{8,13},{9,12},{10,... | collective-permute-start | bytes 589832 | tf_op jit(solution)/shard_map/ppermute | solution.py:31
  15.0 11.9 %collective-permute-start.2 = (bf16[2,2,96,512]{3,2,1,0:T(8,128)(2,1)S(1)}, bf16[2,2,96,512]{3,2,1,0:T(8,128)(2,1)S(1)}, u32[]{:S(2)}, u32[]{:S(2)}) collective-permute-start(bf16[2,2,96,512]{3,2,1,0:T(8,128)(2,1)S(1)} %pad_maximum_fusion.2), channel_id=1, source_target_pairs={{0,2},{1,3},{2,0},{3,1},{4,6},{5,7},{6,4},{7,5},{8,10},{9,11},{10,... | collective-permute-start | bytes 1179656 | tf_op jit(solution)/shard_map/ppermute | solution.py:23
  17.4 42.4 %all-to-all-start = ((bf16[8,128,768]{2,1,0:T(8,128)(2,1)}), bf16[8,128,768]{2,1,0:T(8,128)(2,1)S(1)}, u32[]{:S(2)}, u32[]{:S(2)}) async-start(bf16[8,128,768]{2,1,0:T(8,128)(2,1)} %bitcast.6), calls=%async_computation | async-start | bytes 3145728 | tf_op jit(solution)/shard_map/all_to_all | solution.py:337
  27.0 19.9 %collective-permute-start.3 = (bf16[2,4,96,512]{3,2,1,0:T(8,128)(2,1)S(1)}, bf16[2,4,96,512]{3,2,1,0:T(8,128)(2,1)S(1)}, u32[]{:S(2)}, u32[]{:S(2)}) collective-permute-start(bf16[2,4,96,512]{3,2,1,0:T(8,128)(2,1)S(1)} %bitcast.35), channel_id=1, source_target_pairs={{0,16},{8,24},{16,0},{24,8},{1,17},{9,25},{17,1},{25,9},{2,18},{10... | collective-permute-start | bytes 2359304 | tf_op jit(solution)/shard_map/ppermute | solution.py:23
  47.3 2.8 %copy-start.3 = (bf16[4,96,1024]{2,1,0:T(8,128)(2,1)}, bf16[4,96,1024]{2,1,0:T(8,128)(2,1)S(1)}, u32[]{:S(2)}) copy-start(bf16[4,96,1024]{2,1,0:T(8,128)(2,1)S(1)} %get-tuple-element.17.refs_0_) | copy-start | bytes 2359300
  47.3 7.5 %copy-start.1 = (bf16[4,96,1024]{2,1,0:T(8,128)(2,1)}, bf16[4,96,1024]{2,1,0:T(8,128)(2,1)S(1)}, u32[]{:S(2)}) copy-start(bf16[4,96,1024]{2,1,0:T(8,128)(2,1)S(1)} %get-tuple-element.16.refs_0_) | copy-start | bytes 2359300
  47.3 2.8 %collective-permute-start.4 = (bf16[4,96,1024]{2,1,0:T(8,128)(2,1)S(1)}, bf16[4,96,1024]{2,1,0:T(8,128)(2,1)}, u32[]{:S(2)}, u32[]{:S(2)}) collective-permute-start(bf16[4,96,1024]{2,1,0:T(8,128)(2,1)S(1)} %get-tuple-element.17.refs_0_), channel_id=1, source_target_pairs={{0,8},{8,0},{16,24},{24,16},{1,9},{9,1},{17,25},{25,17},{2,10},{10... | collective-permute-start | bytes 2359304 | tf_op jit(solution)/shard_map/ppermute | solution.py:23
  48.0 6.7 %collective-permute-start.5 = (bf16[4,96,1024]{2,1,0:T(8,128)(2,1)S(1)}, bf16[4,96,1024]{2,1,0:T(8,128)(2,1)}, u32[]{:S(2)}, u32[]{:S(2)}) collective-permute-start(bf16[4,96,1024]{2,1,0:T(8,128)(2,1)S(1)} %get-tuple-element.16.refs_0_), channel_id=1, source_target_pairs={{0,8},{8,0},{16,24},{24,16},{1,9},{9,1},{17,25},{25,17},{2,10},{10... | collective-permute-start | bytes 2359304 | tf_op jit(solution)/shard_map/ppermute | solution.py:23
  59.8 1.1 copy-start
  72.8 16.1 %copy-start.2 = (bf16[4,96,1024]{2,1,0:T(8,128)(2,1)S(1)}, bf16[4,96,1024]{2,1,0:T(8,128)(2,1)}, u32[]{:S(2)}) copy-start(bf16[4,96,1024]{2,1,0:T(8,128)(2,1)} %get-tuple-element.12) | copy-start | bytes 2359300
  72.9 2.6 %collective-permute-start.7 = (bf16[4,96,1024]{2,1,0:T(8,128)(2,1)}, bf16[4,96,1024]{2,1,0:T(8,128)(2,1)S(1)}, u32[]{:S(2)}, u32[]{:S(2)}) collective-permute-start(bf16[4,96,1024]{2,1,0:T(8,128)(2,1)} %get-tuple-element.15), channel_id=1, source_target_pairs={{0,8},{8,0},{16,24},{24,16},{1,9},{9,1},{17,25},{25,17},{2,10},{10... | collective-permute-start | bytes 2359304 | tf_op jit(solution)/shard_map/ppermute | solution.py:23
  72.9 5.5 %collective-permute-start.6 = (bf16[4,96,1024]{2,1,0:T(8,128)(2,1)}, bf16[4,96,1024]{2,1,0:T(8,128)(2,1)S(1)}, u32[]{:S(2)}, u32[]{:S(2)}) collective-permute-start(bf16[4,96,1024]{2,1,0:T(8,128)(2,1)} %get-tuple-element.13), channel_id=1, source_target_pairs={{0,8},{8,0},{16,24},{24,16},{1,9},{9,1},{17,25},{25,17},{2,10},{10... | collective-permute-start | bytes 2359304 | tf_op jit(solution)/shard_map/ppermute | solution.py:23
  76.9 12.1 %collective-permute-start.8 = (bf16[4,96,1024]{2,1,0:T(8,128)(2,1)S(1)}, bf16[4,96,1024]{2,1,0:T(8,128)(2,1)S(1)}, u32[]{:S(2)}, u32[]{:S(2)}) collective-permute-start(bf16[4,96,1024]{2,1,0:T(8,128)(2,1)S(1)} %add_convert_fusion.1), channel_id=1, source_target_pairs={{0,1},{1,0},{2,3},{3,2},{4,5},{5,4},{6,7},{7,6},{8,24},{9,25},{10,... | collective-permute-start | bytes 2359304 | tf_op jit(solution)/shard_map/ppermute | solution.py:278
  89.4 7.8 %collective-permute-start.9 = (bf16[4,96,512]{2,1,0:T(8,128)(2,1)S(1)}, bf16[4,96,512]{2,1,0:T(8,128)(2,1)S(1)}, u32[]{:S(2)}, u32[]{:S(2)}) collective-permute-start(bf16[4,96,512]{2,1,0:T(8,128)(2,1)S(1)} %constant_dynamic-slice_fusion), channel_id=1, source_target_pairs={{0,16},{1,17},{2,18},{3,19},{4,20},{5,21},{6,22},{7,23},{8,9},{9,8... | collective-permute-start | bytes 1179656 | tf_op jit(solution)/shard_map/ppermute | solution.py:278
  97.4 5.2 %collective-permute-start.10 = (bf16[96,512]{1,0:T(8,128)(2,1)S(1)}, bf16[96,512]{1,0:T(8,128)(2,1)S(1)}, u32[]{:S(2)}, u32[]{:S(2)}) collective-permute-start(bf16[96,512]{1,0:T(8,128)(2,1)S(1)} %get-tuple-element.26), channel_id=1, source_target_pairs={{0,2},{1,3},{2,0},{3,1},{4,6},{5,7},{6,4},{7,5},{8,10},{9,11},{10,... | collective-permute-start | bytes 294920 | tf_op jit(solution)/shard_map/ppermute | solution.py:23
  97.5 9.5 %collective-permute-start.11 = (bf16[96,512]{1,0:T(8,128)(2,1)S(1)}, bf16[96,512]{1,0:T(8,128)(2,1)S(1)}, u32[]{:S(2)}, u32[]{:S(2)}) collective-permute-start(bf16[96,512]{1,0:T(8,128)(2,1)S(1)} %get-tuple-element.28), channel_id=1, source_target_pairs={{0,4},{1,5},{2,6},{3,7},{4,0},{5,1},{6,2},{7,3},{8,12},{9,13},{10,... | collective-permute-start | bytes 294920 | tf_op jit(solution)/shard_map/ppermute | solution.py:23
  101.7 6.5 %collective-permute-start.12 = (bf16[96,512]{1,0:T(8,128)(2,1)S(1)}, bf16[96,512]{1,0:T(8,128)(2,1)S(1)}, u32[]{:S(2)}, u32[]{:S(2)}) collective-permute-start(bf16[96,512]{1,0:T(8,128)(2,1)S(1)} %get-tuple-element.27), channel_id=1, source_target_pairs={{0,6},{1,7},{2,4},{3,5},{4,2},{5,3},{6,0},{7,1},{8,14},{9,15},{10,... | collective-permute-start | bytes 294920 | tf_op jit(solution)/shard_map/ppermute | solution.py:23
  108.3 4.7 %collective-permute-start.13 = (bf16[96,512]{1,0:T(8,128)(2,1)S(1)}, bf16[96,512]{1,0:T(8,128)(2,1)S(1)}, u32[]{:S(2)}, u32[]{:S(2)}) collective-permute-start(bf16[96,512]{1,0:T(8,128)(2,1)S(1)} %fusion.5), channel_id=1, source_target_pairs={{0,16},{8,24},{16,0},{24,8},{1,17},{9,25},{17,1},{25,9},{2,18},{10... | collective-permute-start | bytes 294920 | tf_op jit(solution)/shard_map/ppermute | solution.py:23
  113.0 1.5 %collective-permute-start.14 = (bf16[96,1024]{1,0:T(8,128)(2,1)S(1)}, bf16[96,1024]{1,0:T(8,128)(2,1)S(1)}, u32[]{:S(2)}, u32[]{:S(2)}) collective-permute-start(bf16[96,1024]{1,0:T(8,128)(2,1)S(1)} %pad_maximum_fusion.4), channel_id=1, source_target_pairs={{0,8},{8,0},{16,24},{24,16},{1,9},{9,1},{17,25},{25,17},{2,10},{10... | collective-permute-start | bytes 589832 | tf_op jit(solution)/shard_map/ppermute | solution.py:23

commit v17 on v16

--- a/solution.py
+++ b/solution.py
@@ -401,9 +401,14 @@
             for pair, which in ((sent, 1 - core), (kept, core))
         ]
     leave, stay = [[own, swap(piece, "rep", 1)] for own, piece in zip(kept, sent)]
-    held = added([*stay, turn_swap(added(leave), 0)])
     bit = jnp.where(core == 0, upper, low)
-    held = added([column_half(held, bit), turn_swap(column_half(held, 1 - bit), 1)])
+    halves = []
+    size = dom_size // 4
+    for begin in (0, size):
+        gone, kept = [[term[begin : begin + size] for term in terms] for terms in (leave, stay)]
+        held = added([*kept, turn_swap(added(gone), 0)])
+        halves.append(added([column_half(held, bit), turn_swap(column_half(held, 1 - bit), 1)]))
+    held = jnp.concatenate(halves)
     both = reduce_high(held, high, parts // 4)
     summed = lax.dynamic_index_in_dim(both, place, 0, keepdims=False).astype(F32)
     for step in range(1, dom_size // 2):

time: 116 us -> 116 us (level)
    ppermute x2 -> x4, waiting for transfers between devices: 16.8 us -> 15.6 us  [turn_swap(): return lax.ppermute(value, ('rep', 'dom'), pairs)]
    ppermute x2 -> x4, starting transfers between devices: 3.11 us -> 4.25 us  [turn_swap(): return lax.ppermute(value, ('rep', 'dom'), pairs)]
  transfers between devices with their start and end apart: 16 -> 18, of which waited for: 13 -> 15; matrix products, arithmetic and copies ran while one was open for 2% -> 2% of each run, Pallas kernels for 8% -> 8%
where the time goes in v17:
time: 116 us
  waiting for transfers between devices  61 us (53%)
  starting transfers between devices  26.1 us (22%)
  Pallas kernels  21.1 us (18%)
  other arithmetic  4.3 us (4%)
  local copies, waits for them, and re-layouts  2.15 us (2%)
    ppermute x11, waiting for transfers between devices, swap(): lax.ppermute(value, axis, [(index, index ^ step) for index in range(size)])  36.4 us
    ppermute x4, waiting for transfers between devices, turn_swap(): return lax.ppermute(value, ('rep', 'dom'), pairs)  15.6 us
    pallas_call x1, Pallas kernels, shards(): call(functools.partial(layer_kernel, sources, tiled), out_shapes, [SMEM,...  11.9 us
    ppermute x11, starting transfers between devices, swap(): lax.ppermute(value, axis, [(index, index ^ step) for index in range(size)])  11.5 us
    all_to_all x1, starting transfers between devices, shards(): lax.all_to_all(slots.reshape(dom_size, block, width), 'dom', split_axis=0...  5.58 us
    all_to_all x1, waiting for transfers between devices, shards(): lax.all_to_all(slots.reshape(dom_size, block, width), 'dom', split_axis=0...  5.09 us
    ppermute x2, starting transfers between devices, cross(): lax.ppermute(value, ('rep', 'dom'), [(source, target) for source, target...  4.77 us
    pallas_call x1, Pallas kernels, shards(): call(self_kernel, jax.ShapeDtypeStruct((rows, hidden), BF16), [SMEM] + [H...  4.67 us
  transfers between devices with their start and end apart: 18, of which 15 were waited for; matrix products, arithmetic and copies ran while one was open for 2% of the time, Pallas kernels for 8%

profile of v17, /device:TPU:0, one launch (start us, length us, event | category | flops | bytes accessed | tf_op | source)
XLA Modules:
  0.0 115.5 jit_solution(12447903193117629443)
XLA Ops:
  0.6 1.0 dynamic-slice_bitcast_fusion
  1.6 0.7 collective-permute-start
  2.3 4.1 %collective-permute-start.1 = (bf16[2,96,512]{2,1,0:T(8,128)(2,1)S(1)}, bf16[2,96,512]{2,1,0:T(8,128)(2,1)S(1)}, u32[]{:S(2)}, u32[]{:S(2)}) collective-permute-start(bf16[2,96,512]{2,1,0:T(8,128)(2,1)S(1)} %pad_maximum_fusion.3), channel_id=1, source_target_pairs={{0,4},{1,5},{2,6},{3,7},{4,0},{5,1},{6,2},{7,3},{8,13},{9,12},{10,... | collective-permute-start | bytes 589832 | tf_op jit(solution)/shard_map/ppermute | solution.py:31
  6.4 4.6 %shard_map.95 = bf16[1024,768]{1,0:T(8,128)(2,1)} custom-call(s32[32]{0:T(128)} %src_hbm.1, s32[32]{0:T(128)} %peer_hbm.1, bf16[32,128,128]{2,1,0:T(8,128)(2,1)} %tiles_hbm.1, bf16[1024,768]{1,0:T(8,128)(2,1)} %features_hbm.5), custom_call_target="tpu_custom_call" | custom-call | flops 1610612736 | bytes 4194304 | tf_op jit(solution)/shard_map/pallas_call | solution.py:312
  11.0 3.9 %collective-permute-done.1 = bf16[2,96,512]{2,1,0:T(8,128)(2,1)S(1)} collective-permute-done((bf16[2,96,512]{2,1,0:T(8,128)(2,1)S(1)}, bf16[2,96,512]{2,1,0:T(8,128)(2,1)S(1)}, u32[]{:S(2)}, u32[]{:S(2)}) %collective-permute-start.1) | collective-permute-done | bytes 196640 | tf_op jit(solution)/shard_map/ppermute | solution.py:31
  15.0 2.5 %collective-permute-start.2 = (bf16[2,2,96,512]{3,2,1,0:T(8,128)(2,1)S(1)}, bf16[2,2,96,512]{3,2,1,0:T(8,128)(2,1)S(1)}, u32[]{:S(2)}, u32[]{:S(2)}) collective-permute-start(bf16[2,2,96,512]{3,2,1,0:T(8,128)(2,1)S(1)} %pad_maximum_fusion.2), channel_id=1, source_target_pairs={{0,2},{1,3},{2,0},{3,1},{4,6},{5,7},{6,4},{7,5},{8,10},{9,11},{10,... | collective-permute-start | bytes 1179656 | tf_op jit(solution)/shard_map/ppermute | solution.py:23
  17.4 5.6 %all-to-all-start = ((bf16[8,128,768]{2,1,0:T(8,128)(2,1)}), bf16[8,128,768]{2,1,0:T(8,128)(2,1)S(1)}, u32[]{:S(2)}, u32[]{:S(2)}) async-start(bf16[8,128,768]{2,1,0:T(8,128)(2,1)} %bitcast.6), calls=%async_computation | async-start | bytes 3145728 | tf_op jit(solution)/shard_map/all_to_all | solution.py:337
  23.0 3.8 %collective-permute-done.2 = bf16[2,2,96,512]{3,2,1,0:T(8,128)(2,1)S(1)} collective-permute-done((bf16[2,2,96,512]{3,2,1,0:T(8,128)(2,1)S(1)}, bf16[2,2,96,512]{3,2,1,0:T(8,128)(2,1)S(1)}, u32[]{:S(2)}, u32[]{:S(2)}) %collective-permute-start.2) | collective-permute-done | bytes 393248 | tf_op jit(solution)/shard_map/ppermute | solution.py:23
  27.0 1.6 %collective-permute-start.3 = (bf16[2,4,96,512]{3,2,1,0:T(8,128)(2,1)S(1)}, bf16[2,4,96,512]{3,2,1,0:T(8,128)(2,1)S(1)}, u32[]{:S(2)}, u32[]{:S(2)}) collective-permute-start(bf16[2,4,96,512]{3,2,1,0:T(8,128)(2,1)S(1)} %bitcast.37), channel_id=1, source_target_pairs={{0,16},{8,24},{16,0},{24,8},{1,17},{9,25},{17,1},{25,9},{2,18},{10... | collective-permute-start | bytes 2359304 | tf_op jit(solution)/shard_map/ppermute | solution.py:23
  28.6 18.4 %collective-permute-done.3 = bf16[2,4,96,512]{3,2,1,0:T(8,128)(2,1)S(1)} collective-permute-done((bf16[2,4,96,512]{3,2,1,0:T(8,128)(2,1)S(1)}, bf16[2,4,96,512]{3,2,1,0:T(8,128)(2,1)S(1)}, u32[]{:S(2)}, u32[]{:S(2)}) %collective-permute-start.3) | collective-permute-done | bytes 786464 | tf_op jit(solution)/shard_map/ppermute | solution.py:23
  47.3 0.7 collective-permute-start.4
  48.7 1.4 %collective-permute-done.4.refs_1_ = bf16[4,96,1024]{2,1,0:T(8,128)(2,1)} collective-permute-done((bf16[4,96,1024]{2,1,0:T(8,128)(2,1)S(1)}, bf16[4,96,1024]{2,1,0:T(8,128)(2,1)}, u32[]{:S(2)}, u32[]{:S(2)}) %collective-permute-start.4) | collective-permute-done | bytes 786464 | tf_op jit(solution)/shard_map/ppermute | solution.py:23
  50.0 4.7 %shard_map.96.total_hbm = bf16[1024,1024]{1,0:T(8,128)(2,1)} custom-call(s32[1]{0:T(128)} %bitcast.1.flip_ref, bf16[1024,768]{1,0:T(8,128)(2,1)} %features_hbm.5, bf16[4,96,1024]{2,1,0:T(8,128)(2,1)} %copy-done.3, bf16[4,96,1024]{2,1,0:T(8,128)(2,1)} %collective-permute-done.4.refs_1_), custom_call_target="tpu_custom_call" | custom-call | flops 1610612736 | bytes 7340032 | tf_op jit(solution)/shard_map/pallas_call | solution.py:347
  54.7 5.1 %all-to-all-done.slots_hbm = bf16[8,128,768]{2,1,0:T(8,128)(2,1)S(1)} async-done(((bf16[8,128,768]{2,1,0:T(8,128)(2,1)}), bf16[8,128,768]{2,1,0:T(8,128)(2,1)S(1)}, u32[]{:S(2)}, u32[]{:S(2)}) %all-to-all-start) | async-done | bytes 1572896 | tf_op jit(solution)/shard_map/all_to_all | solution.py:337
  59.8 1.1 copy-done
  61.0 11.9 %shard_map.97 = (bf16[4,96,1024]{2,1,0:T(8,128)(2,1)}, bf16[4,96,1024]{2,1,0:T(8,128)(2,1)}, bf16[4,96,1024]{2,1,0:T(8,128)(2,1)}, bf16[4,96,1024]{2,1,0:T(8,128)(2,1)}) custom-call(s32[4]{0:T(128)} %pad_add_fusion.places_ref, s32[8]{0:T(128)} %into_ref.1, bf16[8,128,768]{2,1,0:T(8,128)(2,1)} %copy-done, bf16[1024,1024]{1,0:T(8,128)(2,1)} %shard_map.96.total_hbm, ...), custom_call_target="tpu_custom_call" | custom-call | flops 4831838208 | bytes 16777216 | tf_op jit(solution)/shard_map/pallas_call | solution.py:372
  73.4 2.0 %collective-permute-done.7 = bf16[4,96,1024]{2,1,0:T(8,128)(2,1)S(1)} collective-permute-done((bf16[4,96,1024]{2,1,0:T(8,128)(2,1)}, bf16[4,96,1024]{2,1,0:T(8,128)(2,1)S(1)}, u32[]{:S(2)}, u32[]{:S(2)}) %collective-permute-start.7) | collective-permute-done | bytes 786464 | tf_op jit(solution)/shard_map/ppermute | solution.py:23
  75.4 1.4 %add_convert_fusion.1 = (bf16[2,96,1024]{2,1,0:T(8,128)(2,1)S(1)}, bf16[2,96,1024]{2,1,0:T(8,128)(2,1)S(1)}) fusion(bf16[4,96,1024]{2,1,0:T(8,128)(2,1)S(1)} %collective-permute-done.7, bf16[4,96,1024]{2,1,0:T(8,128)(2,1)} %get-tuple-element.14), kind=kLoop, calls=%fused_computation.8 | loop fusion | flops 1572864 | bytes 2359296 | tf_op jit(solution)/shard_map/convert_element_type | solution.py:253
  76.9 1.5 %collective-permute-start.10 = (bf16[2,96,1024]{2,1,0:T(8,128)(2,1)S(1)}, bf16[2,96,1024]{2,1,0:T(8,128)(2,1)S(1)}, u32[]{:S(2)}, u32[]{:S(2)}) collective-permute-start(bf16[2,96,1024]{2,1,0:T(8,128)(2,1)S(1)} %get-tuple-element.18), channel_id=1, source_target_pairs={{0,1},{1,0},{2,3},{3,2},{4,5},{5,4},{6,7},{7,6},{8,24},{9,25},{10,... | collective-permute-start | bytes 1179656 | tf_op jit(solution)/shard_map/ppermute | solution.py:278
  79.0 5.7 %collective-permute-done.10 = bf16[2,96,1024]{2,1,0:T(8,128)(2,1)S(1)} collective-permute-done((bf16[2,96,1024]{2,1,0:T(8,128)(2,1)S(1)}, bf16[2,96,1024]{2,1,0:T(8,128)(2,1)S(1)}, u32[]{:S(2)}, u32[]{:S(2)}) %collective-permute-start.10) | collective-permute-done | bytes 393248 | tf_op jit(solution)/shard_map/ppermute | solution.py:278
  84.7 4.2 %collective-permute-done.8 = bf16[2,96,1024]{2,1,0:T(8,128)(2,1)S(1)} collective-permute-done((bf16[2,96,1024]{2,1,0:T(8,128)(2,1)S(1)}, bf16[2,96,1024]{2,1,0:T(8,128)(2,1)S(1)}, u32[]{:S(2)}, u32[]{:S(2)}) %collective-permute-start.8) | collective-permute-done | bytes 393248 | tf_op jit(solution)/shard_map/ppermute | solution.py:278
  89.4 1.6 %collective-permute-start.11 = (bf16[2,96,512]{2,1,0:T(8,128)(2,1)S(1)}, bf16[2,96,512]{2,1,0:T(8,128)(2,1)S(1)}, u32[]{:S(2)}, u32[]{:S(2)}) collective-permute-start(bf16[2,96,512]{2,1,0:T(8,128)(2,1)S(1)} %constant_dynamic-slice_fusion), channel_id=1, source_target_pairs={{0,16},{1,17},{2,18},{3,19},{4,20},{5,21},{6,22},{7,23},{8,9},{9,8... | collective-permute-start | bytes 589832 | tf_op jit(solution)/shard_map/ppermute | solution.py:278
  91.6 3.6 %collective-permute-done.11 = bf16[2,96,512]{2,1,0:T(8,128)(2,1)S(1)} collective-permute-done((bf16[2,96,512]{2,1,0:T(8,128)(2,1)S(1)}, bf16[2,96,512]{2,1,0:T(8,128)(2,1)S(1)}, u32[]{:S(2)}, u32[]{:S(2)}) %collective-permute-start.11) | collective-permute-done | bytes 196640 | tf_op jit(solution)/shard_map/ppermute | solution.py:278
  95.2 2.0 %collective-permute-done.9 = bf16[2,96,512]{2,1,0:T(8,128)(2,1)S(1)} collective-permute-done((bf16[2,96,512]{2,1,0:T(8,128)(2,1)S(1)}, bf16[2,96,512]{2,1,0:T(8,128)(2,1)S(1)}, u32[]{:S(2)}, u32[]{:S(2)}) %collective-permute-start.9) | collective-permute-done | bytes 196640 | tf_op jit(solution)/shard_map/ppermute | solution.py:278
  97.5 4.2 %collective-permute-start.13 = (bf16[96,512]{1,0:T(8,128)(2,1)S(1)}, bf16[96,512]{1,0:T(8,128)(2,1)S(1)}, u32[]{:S(2)}, u32[]{:S(2)}) collective-permute-start(bf16[96,512]{1,0:T(8,128)(2,1)S(1)} %get-tuple-element.31), channel_id=1, source_target_pairs={{0,4},{1,5},{2,6},{3,7},{4,0},{5,1},{6,2},{7,3},{8,12},{9,13},{10,... | collective-permute-start | bytes 294920 | tf_op jit(solution)/shard_map/ppermute | solution.py:23
  101.9 0.8 collective-permute-done.12
  102.6 4.4 %collective-permute-done.13 = bf16[96,512]{1,0:T(8,128)(2,1)S(1)} collective-permute-done((bf16[96,512]{1,0:T(8,128)(2,1)S(1)}, bf16[96,512]{1,0:T(8,128)(2,1)S(1)}, u32[]{:S(2)}, u32[]{:S(2)}) %collective-permute-start.13) | collective-permute-done | bytes 98336 | tf_op jit(solution)/shard_map/ppermute | solution.py:23
  107.0 1.2 %collective-permute-done.14 = bf16[96,512]{1,0:T(8,128)(2,1)S(1)} collective-permute-done((bf16[96,512]{1,0:T(8,128)(2,1)S(1)}, bf16[96,512]{1,0:T(8,128)(2,1)S(1)}, u32[]{:S(2)}, u32[]{:S(2)}) %collective-permute-start.14) | collective-permute-done | bytes 98336 | tf_op jit(solution)/shard_map/ppermute | solution.py:23
  108.3 1.6 %collective-permute-start.15 = (bf16[96,512]{1,0:T(8,128)(2,1)S(1)}, bf16[96,512]{1,0:T(8,128)(2,1)S(1)}, u32[]{:S(2)}, u32[]{:S(2)}) collective-permute-start(bf16[96,512]{1,0:T(8,128)(2,1)S(1)} %fusion.5), channel_id=1, source_target_pairs={{0,16},{8,24},{16,0},{24,8},{1,17},{9,25},{17,1},{25,9},{2,18},{10... | collective-permute-start | bytes 294920 | tf_op jit(solution)/shard_map/ppermute | solution.py:23
  109.9 3.1 %collective-permute-done.15 = bf16[96,512]{1,0:T(8,128)(2,1)S(1)} collective-permute-done((bf16[96,512]{1,0:T(8,128)(2,1)S(1)}, bf16[96,512]{1,0:T(8,128)(2,1)S(1)}, u32[]{:S(2)}, u32[]{:S(2)}) %collective-permute-start.15) | collective-permute-done | bytes 98336 | tf_op jit(solution)/shard_map/ppermute | solution.py:23
  113.1 1.4 %collective-permute-done.16 = bf16[96,1024]{1,0:T(8,128)(2,1)S(1)} collective-permute-done((bf16[96,1024]{1,0:T(8,128)(2,1)S(1)}, bf16[96,1024]{1,0:T(8,128)(2,1)S(1)}, u32[]{:S(2)}, u32[]{:S(2)}) %collective-permute-start.16) | collective-permute-done | bytes 196640 | tf_op jit(solution)/shard_map/ppermute | solution.py:23
  114.6 1.0 select_convert_fusion
  (35 shorter events, 4.1 us)
Async XLA Ops:
  1.6 9.3 %collective-permute-start = (bf16[2,96,512]{2,1,0:T(8,128)(2,1)S(1)}, bf16[2,96,512]{2,1,0:T(8,128)(2,1)S(1)}, u32[]{:S(2)}, u32[]{:S(2)}) collective-permute-start(bf16[2,96,512]{2,1,0:T(8,128)(2,1)S(1)} %pad_maximum_fusion.3), channel_id=1, source_target_pairs={{8,9},{9,8},{10,11},{11,10},{12,13},{13,12},{14,15},{15,14},{24,25... | collective-permute-start | bytes 589832 | tf_op jit(solution)/shard_map/ppermute | solution.py:31
  2.3 12.6 %collective-permute-start.1 = (bf16[2,96,512]{2,1,0:T(8,128)(2,1)S(1)}, bf16[2,96,512]{2,1,0:T(8,128)(2,1)S(1)}, u32[]{:S(2)}, u32[]{:S(2)}) collective-permute-start(bf16[2,96,512]{2,1,0:T(8,128)(2,1)S(1)} %pad_maximum_fusion.3), channel_id=1, source_target_pairs={{0,4},{1,5},{2,6},{3,7},{4,0},{5,1},{6,2},{7,3},{8,13},{9,12},{10,... | collective-permute-start | bytes 589832 | tf_op jit(solution)/shard_map/ppermute | solution.py:31
  15.0 11.9 %collective-permute-start.2 = (bf16[2,2,96,512]{3,2,1,0:T(8,128)(2,1)S(1)}, bf16[2,2,96,512]{3,2,1,0:T(8,128)(2,1)S(1)}, u32[]{:S(2)}, u32[]{:S(2)}) collective-permute-start(bf16[2,2,96,512]{3,2,1,0:T(8,128)(2,1)S(1)} %pad_maximum_fusion.2), channel_id=1, source_target_pairs={{0,2},{1,3},{2,0},{3,1},{4,6},{5,7},{6,4},{7,5},{8,10},{9,11},{10,... | collective-permute-start | bytes 1179656 | tf_op jit(solution)/shard_map/ppermute | solution.py:23
  17.4 42.4 %all-to-all-start = ((bf16[8,128,768]{2,1,0:T(8,128)(2,1)}), bf16[8,128,768]{2,1,0:T(8,128)(2,1)S(1)}, u32[]{:S(2)}, u32[]{:S(2)}) async-start(bf16[8,128,768]{2,1,0:T(8,128)(2,1)} %bitcast.6), calls=%async_computation | async-start | bytes 3145728 | tf_op jit(solution)/shard_map/all_to_all | solution.py:337
  27.0 19.9 %collective-permute-start.3 = (bf16[2,4,96,512]{3,2,1,0:T(8,128)(2,1)S(1)}, bf16[2,4,96,512]{3,2,1,0:T(8,128)(2,1)S(1)}, u32[]{:S(2)}, u32[]{:S(2)}) collective-permute-start(bf16[2,4,96,512]{3,2,1,0:T(8,128)(2,1)S(1)} %bitcast.37), channel_id=1, source_target_pairs={{0,16},{8,24},{16,0},{24,8},{1,17},{9,25},{17,1},{25,9},{2,18},{10... | collective-permute-start | bytes 2359304 | tf_op jit(solution)/shard_map/ppermute | solution.py:23
  47.3 2.8 %copy-start.3 = (bf16[4,96,1024]{2,1,0:T(8,128)(2,1)}, bf16[4,96,1024]{2,1,0:T(8,128)(2,1)S(1)}, u32[]{:S(2)}) copy-start(bf16[4,96,1024]{2,1,0:T(8,128)(2,1)S(1)} %get-tuple-element.21.refs_0_) | copy-start | bytes 2359300
  47.3 7.5 %copy-start.2 = (bf16[4,96,1024]{2,1,0:T(8,128)(2,1)}, bf16[4,96,1024]{2,1,0:T(8,128)(2,1)S(1)}, u32[]{:S(2)}) copy-start(bf16[4,96,1024]{2,1,0:T(8,128)(2,1)S(1)} %get-tuple-element.20.refs_0_) | copy-start | bytes 2359300
  47.3 2.8 %collective-permute-start.4 = (bf16[4,96,1024]{2,1,0:T(8,128)(2,1)S(1)}, bf16[4,96,1024]{2,1,0:T(8,128)(2,1)}, u32[]{:S(2)}, u32[]{:S(2)}) collective-permute-start(bf16[4,96,1024]{2,1,0:T(8,128)(2,1)S(1)} %get-tuple-element.21.refs_0_), channel_id=1, source_target_pairs={{0,8},{8,0},{16,24},{24,16},{1,9},{9,1},{17,25},{25,17},{2,10},{10... | collective-permute-start | bytes 2359304 | tf_op jit(solution)/shard_map/ppermute | solution.py:23
  48.0 6.7 %collective-permute-start.5 = (bf16[4,96,1024]{2,1,0:T(8,128)(2,1)S(1)}, bf16[4,96,1024]{2,1,0:T(8,128)(2,1)}, u32[]{:S(2)}, u32[]{:S(2)}) collective-permute-start(bf16[4,96,1024]{2,1,0:T(8,128)(2,1)S(1)} %get-tuple-element.20.refs_0_), channel_id=1, source_target_pairs={{0,8},{8,0},{16,24},{24,16},{1,9},{9,1},{17,25},{25,17},{2,10},{10... | collective-permute-start | bytes 2359304 | tf_op jit(solution)/shard_map/ppermute | solution.py:23
  59.8 1.1 copy-start
  72.9 16.1 %copy-start.1 = (bf16[4,96,1024]{2,1,0:T(8,128)(2,1)S(1)}, bf16[4,96,1024]{2,1,0:T(8,128)(2,1)}, u32[]{:S(2)}) copy-start(bf16[4,96,1024]{2,1,0:T(8,128)(2,1)} %get-tuple-element.12) | copy-start | bytes 2359300
  72.9 2.6 %collective-permute-start.7 = (bf16[4,96,1024]{2,1,0:T(8,128)(2,1)}, bf16[4,96,1024]{2,1,0:T(8,128)(2,1)S(1)}, u32[]{:S(2)}, u32[]{:S(2)}) collective-permute-start(bf16[4,96,1024]{2,1,0:T(8,128)(2,1)} %get-tuple-element.15), channel_id=1, source_target_pairs={{0,8},{8,0},{16,24},{24,16},{1,9},{9,1},{17,25},{25,17},{2,10},{10... | collective-permute-start | bytes 2359304 | tf_op jit(solution)/shard_map/ppermute | solution.py:23
  72.9 6.0 %collective-permute-start.6 = (bf16[4,96,1024]{2,1,0:T(8,128)(2,1)}, bf16[4,96,1024]{2,1,0:T(8,128)(2,1)S(1)}, u32[]{:S(2)}, u32[]{:S(2)}) collective-permute-start(bf16[4,96,1024]{2,1,0:T(8,128)(2,1)} %get-tuple-element.13), channel_id=1, source_target_pairs={{0,8},{8,0},{16,24},{24,16},{1,9},{9,1},{17,25},{25,17},{2,10},{10... | collective-permute-start | bytes 2359304 | tf_op jit(solution)/shard_map/ppermute | solution.py:23
  76.9 7.8 %collective-permute-start.10 = (bf16[2,96,1024]{2,1,0:T(8,128)(2,1)S(1)}, bf16[2,96,1024]{2,1,0:T(8,128)(2,1)S(1)}, u32[]{:S(2)}, u32[]{:S(2)}) collective-permute-start(bf16[2,96,1024]{2,1,0:T(8,128)(2,1)S(1)} %get-tuple-element.18), channel_id=1, source_target_pairs={{0,1},{1,0},{2,3},{3,2},{4,5},{5,4},{6,7},{7,6},{8,24},{9,25},{10,... | collective-permute-start | bytes 1179656 | tf_op jit(solution)/shard_map/ppermute | solution.py:278
  78.4 10.5 %collective-permute-start.8 = (bf16[2,96,1024]{2,1,0:T(8,128)(2,1)S(1)}, bf16[2,96,1024]{2,1,0:T(8,128)(2,1)S(1)}, u32[]{:S(2)}, u32[]{:S(2)}) collective-permute-start(bf16[2,96,1024]{2,1,0:T(8,128)(2,1)S(1)} %get-tuple-element.19), channel_id=1, source_target_pairs={{0,1},{1,0},{2,3},{3,2},{4,5},{5,4},{6,7},{7,6},{8,24},{9,25},{10,... | collective-permute-start | bytes 1179656 | tf_op jit(solution)/shard_map/ppermute | solution.py:278
  89.4 5.7 %collective-permute-start.11 = (bf16[2,96,512]{2,1,0:T(8,128)(2,1)S(1)}, bf16[2,96,512]{2,1,0:T(8,128)(2,1)S(1)}, u32[]{:S(2)}, u32[]{:S(2)}) collective-permute-start(bf16[2,96,512]{2,1,0:T(8,128)(2,1)S(1)} %constant_dynamic-slice_fusion), channel_id=1, source_target_pairs={{0,16},{1,17},{2,18},{3,19},{4,20},{5,21},{6,22},{7,23},{8,9},{9,8... | collective-permute-start | bytes 589832 | tf_op jit(solution)/shard_map/ppermute | solution.py:278
  91.0 6.2 %collective-permute-start.9 = (bf16[2,96,512]{2,1,0:T(8,128)(2,1)S(1)}, bf16[2,96,512]{2,1,0:T(8,128)(2,1)S(1)}, u32[]{:S(2)}, u32[]{:S(2)}) collective-permute-start(bf16[2,96,512]{2,1,0:T(8,128)(2,1)S(1)} %constant_dynamic-slice_fusion.1), channel_id=1, source_target_pairs={{0,16},{1,17},{2,18},{3,19},{4,20},{5,21},{6,22},{7,23},{8,9},{9,8... | collective-permute-start | bytes 589832 | tf_op jit(solution)/shard_map/ppermute | solution.py:278
  97.4 5.2 %collective-permute-start.12 = (bf16[96,512]{1,0:T(8,128)(2,1)S(1)}, bf16[96,512]{1,0:T(8,128)(2,1)S(1)}, u32[]{:S(2)}, u32[]{:S(2)}) collective-permute-start(bf16[96,512]{1,0:T(8,128)(2,1)S(1)} %get-tuple-element.30), channel_id=1, source_target_pairs={{0,2},{1,3},{2,0},{3,1},{4,6},{5,7},{6,4},{7,5},{8,10},{9,11},{10,... | collective-permute-start | bytes 294920 | tf_op jit(solution)/shard_map/ppermute | solution.py:23
  97.5 9.5 %collective-permute-start.13 = (bf16[96,512]{1,0:T(8,128)(2,1)S(1)}, bf16[96,512]{1,0:T(8,128)(2,1)S(1)}, u32[]{:S(2)}, u32[]{:S(2)}) collective-permute-start(bf16[96,512]{1,0:T(8,128)(2,1)S(1)} %get-tuple-element.31), channel_id=1, source_target_pairs={{0,4},{1,5},{2,6},{3,7},{4,0},{5,1},{6,2},{7,3},{8,12},{9,13},{10,... | collective-permute-start | bytes 294920 | tf_op jit(solution)/shard_map/ppermute | solution.py:23
  101.7 6.5 %collective-permute-start.14 = (bf16[96,512]{1,0:T(8,128)(2,1)S(1)}, bf16[96,512]{1,0:T(8,128)(2,1)S(1)}, u32[]{:S(2)}, u32[]{:S(2)}) collective-permute-start(bf16[96,512]{1,0:T(8,128)(2,1)S(1)} %get-tuple-element.32), channel_id=1, source_target_pairs={{0,6},{1,7},{2,4},{3,5},{4,2},{5,3},{6,0},{7,1},{8,14},{9,15},{10,... | collective-permute-start | bytes 294920 | tf_op jit(solution)/shard_map/ppermute | solution.py:23
  108.3 4.7 %collective-permute-start.15 = (bf16[96,512]{1,0:T(8,128)(2,1)S(1)}, bf16[96,512]{1,0:T(8,128)(2,1)S(1)}, u32[]{:S(2)}, u32[]{:S(2)}) collective-permute-start(bf16[96,512]{1,0:T(8,128)(2,1)S(1)} %fusion.5), channel_id=1, source_target_pairs={{0,16},{8,24},{16,0},{24,8},{1,17},{9,25},{17,1},{25,9},{2,18},{10... | collective-permute-start | bytes 294920 | tf_op jit(solution)/shard_map/ppermute | solution.py:23
  113.1 1.5 %collective-permute-start.16 = (bf16[96,1024]{1,0:T(8,128)(2,1)S(1)}, bf16[96,1024]{1,0:T(8,128)(2,1)S(1)}, u32[]{:S(2)}, u32[]{:S(2)}) collective-permute-start(bf16[96,1024]{1,0:T(8,128)(2,1)S(1)} %pad_maximum_fusion.4), channel_id=1, source_target_pairs={{0,8},{8,0},{16,24},{24,16},{1,9},{9,1},{17,25},{25,17},{2,10},{10... | collective-permute-start | bytes 589832 | tf_op jit(solution)/shard_map/ppermute | solution.py:23

commit v18 on v17

--- a/solution.py
+++ b/solution.py
@@ -12,6 +12,7 @@
 SCALE = 0.7978845608
 CUBIC = 0.044715
 MIB = 1 << 20
+ANY = pl.BlockSpec(memory_space=pl.ANY)
 HBM = pl.BlockSpec(memory_space=pltpu.HBM)
 SMEM = pl.BlockSpec(memory_space=pltpu.SMEM)
 VMEM = pl.BlockSpec(memory_space=pltpu.VMEM)
@@ -372,7 +373,7 @@
     outs = call(
         functools.partial(layer_kernel, sources, tiled),
         out_shapes,
-        [SMEM, SMEM] + [HBM] * (4 + sources),
+        [SMEM, SMEM, ANY] + [HBM] * (3 + sources),
         [HBM] * 4,
         [
             pltpu.VMEM((dom_size, block, width), BF16),
@@ -393,6 +394,7 @@
         ],
         flops=6 * rows * width * hidden,
         moved=16 * rows * hidden,
+        vmem=54,
     )(places, in_block, received, total, features, cotangent, *weights[1])
     sent, kept = outs[:2], outs[2:]
     if not tiled:
@@ -406,7 +408,8 @@
     size = dom_size // 4
     for begin in (0, size):
         gone, kept = [[term[begin : begin + size] for term in terms] for terms in (leave, stay)]
-        held = added([*kept, turn_swap(added(gone), 0)])
+        gone, *leave = lax.optimization_barrier((added(gone), *leave))
+        held = added([*kept, turn_swap(gone, 0)])
         halves.append(added([column_half(held, bit), turn_swap(column_half(held, 1 - bit), 1)]))
     held = jnp.concatenate(halves)
     both = reduce_high(held, high, parts // 4)

time: 116 us -> 117 us (level)
    convert_element_type x4 -> x5, other arithmetic: 1.97 us -> 2.8 us  [added(): return sum((term.astype(F32) for term in terms)).astype(BF16)]
  transfers between devices with their start and end apart: 18 -> 18, of which waited for: 15 -> 15; matrix products, arithmetic and copies ran while one was open for 2% -> 3% of each run, Pallas kernels for 8% -> 8%
where the time goes in v18:
time: 117 us; the launch traced here: 116 us
  waiting for transfers between devices  60.9 us (52%)
  starting transfers between devices  26.1 us (22%)
  Pallas kernels  21.1 us (18%)
  other arithmetic  5.18 us (4%)
  local copies, waits for them, and re-layouts  2.15 us (2%)
    ppermute x11, waiting for transfers between devices, swap(): lax.ppermute(value, axis, [(index, index ^ step) for index in range(size)])  36.4 us
    ppermute x4, waiting for transfers between devices, turn_swap(): return lax.ppermute(value, ('rep', 'dom'), pairs)  15.6 us
    pallas_call x1, Pallas kernels, shards(): call(functools.partial(layer_kernel, sources, tiled), out_shapes, [SMEM,...  11.9 us
    ppermute x11, starting transfers between devices, swap(): lax.ppermute(value, axis, [(index, index ^ step) for index in range(size)])  11.5 us
    all_to_all x1, starting transfers between devices, shards(): lax.all_to_all(slots.reshape(dom_size, block, width), 'dom', split_axis=0...  5.58 us
    all_to_all x1, waiting for transfers between devices, shards(): lax.all_to_all(slots.reshape(dom_size, block, width), 'dom', split_axis=0...  5.08 us
    ppermute x2, starting transfers between devices, cross(): lax.ppermute(value, ('rep', 'dom'), [(source, target) for source, target...  4.77 us
    pallas_call x1, Pallas kernels, shards(): call(self_kernel, jax.ShapeDtypeStruct((rows, hidden), BF16), [SMEM] + [H...  4.67 us
  transfers between devices with their start and end apart: 18, of which 15 were waited for; matrix products, arithmetic and copies ran while one was open for 3% of the time, Pallas kernels for 8%

profile of v18, /device:TPU:0, one launch (start us, length us, event | category | flops | bytes accessed | tf_op | source)
XLA Modules:
  0.0 116.4 jit_solution(16112409912484966574)
XLA Ops:
  0.6 1.0 dynamic-slice_bitcast_fusion
  2.3 4.1 %collective-permute-start.1 = (bf16[2,96,512]{2,1,0:T(8,128)(2,1)S(1)}, bf16[2,96,512]{2,1,0:T(8,128)(2,1)S(1)}, u32[]{:S(2)}, u32[]{:S(2)}) collective-permute-start(bf16[2,96,512]{2,1,0:T(8,128)(2,1)S(1)} %pad_maximum_fusion.3), channel_id=1, source_target_pairs={{0,4},{1,5},{2,6},{3,7},{4,0},{5,1},{6,2},{7,3},{8,13},{9,12},{10,... | collective-permute-start | bytes 589832 | tf_op jit(solution)/shard_map/ppermute | solution.py:32
  6.4 4.6 %shard_map.95 = bf16[1024,768]{1,0:T(8,128)(2,1)} custom-call(s32[32]{0:T(128)} %src_hbm.1, s32[32]{0:T(128)} %peer_hbm.1, bf16[32,128,128]{2,1,0:T(8,128)(2,1)} %tiles_hbm.1, bf16[1024,768]{1,0:T(8,128)(2,1)} %features_hbm.5), custom_call_target="tpu_custom_call" | custom-call | flops 1610612736 | bytes 4194304 | tf_op jit(solution)/shard_map/pallas_call | solution.py:313
  11.0 3.9 %collective-permute-done.1 = bf16[2,96,512]{2,1,0:T(8,128)(2,1)S(1)} collective-permute-done((bf16[2,96,512]{2,1,0:T(8,128)(2,1)S(1)}, bf16[2,96,512]{2,1,0:T(8,128)(2,1)S(1)}, u32[]{:S(2)}, u32[]{:S(2)}) %collective-permute-start.1) | collective-permute-done | bytes 196640 | tf_op jit(solution)/shard_map/ppermute | solution.py:32
  15.0 2.5 %collective-permute-start.2 = (bf16[2,2,96,512]{3,2,1,0:T(8,128)(2,1)S(1)}, bf16[2,2,96,512]{3,2,1,0:T(8,128)(2,1)S(1)}, u32[]{:S(2)}, u32[]{:S(2)}) collective-permute-start(bf16[2,2,96,512]{3,2,1,0:T(8,128)(2,1)S(1)} %pad_maximum_fusion.2), channel_id=1, source_target_pairs={{0,2},{1,3},{2,0},{3,1},{4,6},{5,7},{6,4},{7,5},{8,10},{9,11},{10,... | collective-permute-start | bytes 1179656 | tf_op jit(solution)/shard_map/ppermute | solution.py:24
  17.4 5.6 %all-to-all-start = ((bf16[8,128,768]{2,1,0:T(8,128)(2,1)}), bf16[8,128,768]{2,1,0:T(8,128)(2,1)S(1)}, u32[]{:S(2)}, u32[]{:S(2)}) async-start(bf16[8,128,768]{2,1,0:T(8,128)(2,1)} %bitcast.6), calls=%async_computation | async-start | bytes 3145728 | tf_op jit(solution)/shard_map/all_to_all | solution.py:338
  23.0 3.8 %collective-permute-done.2 = bf16[2,2,96,512]{3,2,1,0:T(8,128)(2,1)S(1)} collective-permute-done((bf16[2,2,96,512]{3,2,1,0:T(8,128)(2,1)S(1)}, bf16[2,2,96,512]{3,2,1,0:T(8,128)(2,1)S(1)}, u32[]{:S(2)}, u32[]{:S(2)}) %collective-permute-start.2) | collective-permute-done | bytes 393248 | tf_op jit(solution)/shard_map/ppermute | solution.py:24
  27.0 1.6 %collective-permute-start.3 = (bf16[2,4,96,512]{3,2,1,0:T(8,128)(2,1)S(1)}, bf16[2,4,96,512]{3,2,1,0:T(8,128)(2,1)S(1)}, u32[]{:S(2)}, u32[]{:S(2)}) collective-permute-start(bf16[2,4,96,512]{3,2,1,0:T(8,128)(2,1)S(1)} %bitcast.37), channel_id=1, source_target_pairs={{0,16},{8,24},{16,0},{24,8},{1,17},{9,25},{17,1},{25,9},{2,18},{10... | collective-permute-start | bytes 2359304 | tf_op jit(solution)/shard_map/ppermute | solution.py:24
  28.6 18.4 %collective-permute-done.3 = bf16[2,4,96,512]{3,2,1,0:T(8,128)(2,1)S(1)} collective-permute-done((bf16[2,4,96,512]{3,2,1,0:T(8,128)(2,1)S(1)}, bf16[2,4,96,512]{3,2,1,0:T(8,128)(2,1)S(1)}, u32[]{:S(2)}, u32[]{:S(2)}) %collective-permute-start.3) | collective-permute-done | bytes 786464 | tf_op jit(solution)/shard_map/ppermute | solution.py:24
  47.3 0.7 collective-permute-start.4
  48.7 1.3 %collective-permute-done.4.refs_1_ = bf16[4,96,1024]{2,1,0:T(8,128)(2,1)} collective-permute-done((bf16[4,96,1024]{2,1,0:T(8,128)(2,1)S(1)}, bf16[4,96,1024]{2,1,0:T(8,128)(2,1)}, u32[]{:S(2)}, u32[]{:S(2)}) %collective-permute-start.4) | collective-permute-done | bytes 786464 | tf_op jit(solution)/shard_map/ppermute | solution.py:24
  50.0 4.7 %shard_map.96.total_hbm = bf16[1024,1024]{1,0:T(8,128)(2,1)} custom-call(s32[1]{0:T(128)} %bitcast.1.flip_ref, bf16[1024,768]{1,0:T(8,128)(2,1)} %features_hbm.5, bf16[4,96,1024]{2,1,0:T(8,128)(2,1)} %copy-done.3, bf16[4,96,1024]{2,1,0:T(8,128)(2,1)} %collective-permute-done.4.refs_1_), custom_call_target="tpu_custom_call" | custom-call | flops 1610612736 | bytes 7340032 | tf_op jit(solution)/shard_map/pallas_call | solution.py:348
  54.7 5.1 %all-to-all-done.slots_hbm = bf16[8,128,768]{2,1,0:T(8,128)(2,1)S(1)} async-done(((bf16[8,128,768]{2,1,0:T(8,128)(2,1)}), bf16[8,128,768]{2,1,0:T(8,128)(2,1)S(1)}, u32[]{:S(2)}, u32[]{:S(2)}) %all-to-all-start) | async-done | bytes 1572896 | tf_op jit(solution)/shard_map/all_to_all | solution.py:338
  59.8 1.1 copy-done
  61.0 11.9 %shard_map.97 = (bf16[4,96,1024]{2,1,0:T(8,128)(2,1)}, bf16[4,96,1024]{2,1,0:T(8,128)(2,1)}, bf16[4,96,1024]{2,1,0:T(8,128)(2,1)}, bf16[4,96,1024]{2,1,0:T(8,128)(2,1)}) custom-call(s32[4]{0:T(128)} %pad_add_fusion.places_ref, s32[8]{0:T(128)} %into_ref.1, bf16[8,128,768]{2,1,0:T(8,128)(2,1)} %copy-done, bf16[1024,1024]{1,0:T(8,128)(2,1)} %shard_map.96.total_hbm, ...), custom_call_target="tpu_custom_call" | custom-call | flops 4831838208 | bytes 16777216 | tf_op jit(solution)/shard_map/pallas_call | solution.py:373
  73.5 2.0 %collective-permute-done.7 = bf16[4,96,1024]{2,1,0:T(8,128)(2,1)S(1)} collective-permute-done((bf16[4,96,1024]{2,1,0:T(8,128)(2,1)}, bf16[4,96,1024]{2,1,0:T(8,128)(2,1)S(1)}, u32[]{:S(2)}, u32[]{:S(2)}) %collective-permute-start.7) | collective-permute-done | bytes 786464 | tf_op jit(solution)/shard_map/ppermute | solution.py:24
  75.4 1.1 add_convert_fusion.3
  76.6 1.1 add_convert_fusion.1
  77.7 1.5 %collective-permute-start.10 = (bf16[2,96,1024]{2,1,0:T(8,128)(2,1)S(1)}, bf16[2,96,1024]{2,1,0:T(8,128)(2,1)S(1)}, u32[]{:S(2)}, u32[]{:S(2)}) collective-permute-start(bf16[2,96,1024]{2,1,0:T(8,128)(2,1)S(1)} %add_convert_fusion.1), channel_id=1, source_target_pairs={{0,1},{1,0},{2,3},{3,2},{4,5},{5,4},{6,7},{7,6},{8,24},{9,25},{10,... | collective-permute-start | bytes 1179656 | tf_op jit(solution)/shard_map/ppermute | solution.py:279
  79.8 5.7 %collective-permute-done.10 = bf16[2,96,1024]{2,1,0:T(8,128)(2,1)S(1)} collective-permute-done((bf16[2,96,1024]{2,1,0:T(8,128)(2,1)S(1)}, bf16[2,96,1024]{2,1,0:T(8,128)(2,1)S(1)}, u32[]{:S(2)}, u32[]{:S(2)}) %collective-permute-start.10) | collective-permute-done | bytes 393248 | tf_op jit(solution)/shard_map/ppermute | solution.py:279
  85.5 4.2 %collective-permute-done.8 = bf16[2,96,1024]{2,1,0:T(8,128)(2,1)S(1)} collective-permute-done((bf16[2,96,1024]{2,1,0:T(8,128)(2,1)S(1)}, bf16[2,96,1024]{2,1,0:T(8,128)(2,1)S(1)}, u32[]{:S(2)}, u32[]{:S(2)}) %collective-permute-start.8) | collective-permute-done | bytes 393248 | tf_op jit(solution)/shard_map/ppermute | solution.py:279
  90.2 1.6 %collective-permute-start.11 = (bf16[2,96,512]{2,1,0:T(8,128)(2,1)S(1)}, bf16[2,96,512]{2,1,0:T(8,128)(2,1)S(1)}, u32[]{:S(2)}, u32[]{:S(2)}) collective-permute-start(bf16[2,96,512]{2,1,0:T(8,128)(2,1)S(1)} %constant_dynamic-slice_fusion), channel_id=1, source_target_pairs={{0,16},{1,17},{2,18},{3,19},{4,20},{5,21},{6,22},{7,23},{8,9},{9,8... | collective-permute-start | bytes 589832 | tf_op jit(solution)/shard_map/ppermute | solution.py:279
  92.4 3.6 %collective-permute-done.11 = bf16[2,96,512]{2,1,0:T(8,128)(2,1)S(1)} collective-permute-done((bf16[2,96,512]{2,1,0:T(8,128)(2,1)S(1)}, bf16[2,96,512]{2,1,0:T(8,128)(2,1)S(1)}, u32[]{:S(2)}, u32[]{:S(2)}) %collective-permute-start.11) | collective-permute-done | bytes 196640 | tf_op jit(solution)/shard_map/ppermute | solution.py:279
  96.0 2.0 %collective-permute-done.9 = bf16[2,96,512]{2,1,0:T(8,128)(2,1)S(1)} collective-permute-done((bf16[2,96,512]{2,1,0:T(8,128)(2,1)S(1)}, bf16[2,96,512]{2,1,0:T(8,128)(2,1)S(1)}, u32[]{:S(2)}, u32[]{:S(2)}) %collective-permute-start.9) | collective-permute-done | bytes 196640 | tf_op jit(solution)/shard_map/ppermute | solution.py:279
  98.4 4.2 %collective-permute-start.13 = (bf16[96,512]{1,0:T(8,128)(2,1)S(1)}, bf16[96,512]{1,0:T(8,128)(2,1)S(1)}, u32[]{:S(2)}, u32[]{:S(2)}) collective-permute-start(bf16[96,512]{1,0:T(8,128)(2,1)S(1)} %get-tuple-element.37), channel_id=1, source_target_pairs={{0,4},{1,5},{2,6},{3,7},{4,0},{5,1},{6,2},{7,3},{8,12},{9,13},{10,... | collective-permute-start | bytes 294920 | tf_op jit(solution)/shard_map/ppermute | solution.py:24
  102.7 0.8 collective-permute-done.12
  103.5 4.4 %collective-permute-done.13 = bf16[96,512]{1,0:T(8,128)(2,1)S(1)} collective-permute-done((bf16[96,512]{1,0:T(8,128)(2,1)S(1)}, bf16[96,512]{1,0:T(8,128)(2,1)S(1)}, u32[]{:S(2)}, u32[]{:S(2)}) %collective-permute-start.13) | collective-permute-done | bytes 98336 | tf_op jit(solution)/shard_map/ppermute | solution.py:24
  107.9 1.2 %collective-permute-done.14 = bf16[96,512]{1,0:T(8,128)(2,1)S(1)} collective-permute-done((bf16[96,512]{1,0:T(8,128)(2,1)S(1)}, bf16[96,512]{1,0:T(8,128)(2,1)S(1)}, u32[]{:S(2)}, u32[]{:S(2)}) %collective-permute-start.14) | collective-permute-done | bytes 98336 | tf_op jit(solution)/shard_map/ppermute | solution.py:24
  109.2 1.6 %collective-permute-start.15 = (bf16[96,512]{1,0:T(8,128)(2,1)S(1)}, bf16[96,512]{1,0:T(8,128)(2,1)S(1)}, u32[]{:S(2)}, u32[]{:S(2)}) collective-permute-start(bf16[96,512]{1,0:T(8,128)(2,1)S(1)} %fusion.5), channel_id=1, source_target_pairs={{0,16},{8,24},{16,0},{24,8},{1,17},{9,25},{17,1},{25,9},{2,18},{10... | collective-permute-start | bytes 294920 | tf_op jit(solution)/shard_map/ppermute | solution.py:24
  110.8 3.1 %collective-permute-done.15 = bf16[96,512]{1,0:T(8,128)(2,1)S(1)} collective-permute-done((bf16[96,512]{1,0:T(8,128)(2,1)S(1)}, bf16[96,512]{1,0:T(8,128)(2,1)S(1)}, u32[]{:S(2)}, u32[]{:S(2)}) %collective-permute-start.15) | collective-permute-done | bytes 98336 | tf_op jit(solution)/shard_map/ppermute | solution.py:24
  114.0 1.4 %collective-permute-done.16 = bf16[96,1024]{1,0:T(8,128)(2,1)S(1)} collective-permute-done((bf16[96,1024]{1,0:T(8,128)(2,1)S(1)}, bf16[96,1024]{1,0:T(8,128)(2,1)S(1)}, u32[]{:S(2)}, u32[]{:S(2)}) %collective-permute-start.16) | collective-permute-done | bytes 196640 | tf_op jit(solution)/shard_map/ppermute | solution.py:24
  115.4 1.0 select_convert_fusion
  (36 shorter events, 4.8 us)
Async XLA Ops:
  1.6 9.4 %collective-permute-start = (bf16[2,96,512]{2,1,0:T(8,128)(2,1)S(1)}, bf16[2,96,512]{2,1,0:T(8,128)(2,1)S(1)}, u32[]{:S(2)}, u32[]{:S(2)}) collective-permute-start(bf16[2,96,512]{2,1,0:T(8,128)(2,1)S(1)} %pad_maximum_fusion.3), channel_id=1, source_target_pairs={{8,9},{9,8},{10,11},{11,10},{12,13},{13,12},{14,15},{15,14},{24,25... | collective-permute-start | bytes 589832 | tf_op jit(solution)/shard_map/ppermute | solution.py:32
  2.3 12.6 %collective-permute-start.1 = (bf16[2,96,512]{2,1,0:T(8,128)(2,1)S(1)}, bf16[2,96,512]{2,1,0:T(8,128)(2,1)S(1)}, u32[]{:S(2)}, u32[]{:S(2)}) collective-permute-start(bf16[2,96,512]{2,1,0:T(8,128)(2,1)S(1)} %pad_maximum_fusion.3), channel_id=1, source_target_pairs={{0,4},{1,5},{2,6},{3,7},{4,0},{5,1},{6,2},{7,3},{8,13},{9,12},{10,... | collective-permute-start | bytes 589832 | tf_op jit(solution)/shard_map/ppermute | solution.py:32
  15.0 11.9 %collective-permute-start.2 = (bf16[2,2,96,512]{3,2,1,0:T(8,128)(2,1)S(1)}, bf16[2,2,96,512]{3,2,1,0:T(8,128)(2,1)S(1)}, u32[]{:S(2)}, u32[]{:S(2)}) collective-permute-start(bf16[2,2,96,512]{3,2,1,0:T(8,128)(2,1)S(1)} %pad_maximum_fusion.2), channel_id=1, source_target_pairs={{0,2},{1,3},{2,0},{3,1},{4,6},{5,7},{6,4},{7,5},{8,10},{9,11},{10,... | collective-permute-start | bytes 1179656 | tf_op jit(solution)/shard_map/ppermute | solution.py:24
  17.4 42.4 %all-to-all-start = ((bf16[8,128,768]{2,1,0:T(8,128)(2,1)}), bf16[8,128,768]{2,1,0:T(8,128)(2,1)S(1)}, u32[]{:S(2)}, u32[]{:S(2)}) async-start(bf16[8,128,768]{2,1,0:T(8,128)(2,1)} %bitcast.6), calls=%async_computation | async-start | bytes 3145728 | tf_op jit(solution)/shard_map/all_to_all | solution.py:338
  27.0 19.9 %collective-permute-start.3 = (bf16[2,4,96,512]{3,2,1,0:T(8,128)(2,1)S(1)}, bf16[2,4,96,512]{3,2,1,0:T(8,128)(2,1)S(1)}, u32[]{:S(2)}, u32[]{:S(2)}) collective-permute-start(bf16[2,4,96,512]{3,2,1,0:T(8,128)(2,1)S(1)} %bitcast.37), channel_id=1, source_target_pairs={{0,16},{8,24},{16,0},{24,8},{1,17},{9,25},{17,1},{25,9},{2,18},{10... | collective-permute-start | bytes 2359304 | tf_op jit(solution)/shard_map/ppermute | solution.py:24
  47.3 2.8 %copy-start.3 = (bf16[4,96,1024]{2,1,0:T(8,128)(2,1)}, bf16[4,96,1024]{2,1,0:T(8,128)(2,1)S(1)}, u32[]{:S(2)}) copy-start(bf16[4,96,1024]{2,1,0:T(8,128)(2,1)S(1)} %get-tuple-element.27.refs_0_) | copy-start | bytes 2359300
  47.3 7.5 %copy-start.1 = (bf16[4,96,1024]{2,1,0:T(8,128)(2,1)}, bf16[4,96,1024]{2,1,0:T(8,128)(2,1)S(1)}, u32[]{:S(2)}) copy-start(bf16[4,96,1024]{2,1,0:T(8,128)(2,1)S(1)} %get-tuple-element.26.refs_0_) | copy-start | bytes 2359300
  47.3 2.8 %collective-permute-start.4 = (bf16[4,96,1024]{2,1,0:T(8,128)(2,1)S(1)}, bf16[4,96,1024]{2,1,0:T(8,128)(2,1)}, u32[]{:S(2)}, u32[]{:S(2)}) collective-permute-start(bf16[4,96,1024]{2,1,0:T(8,128)(2,1)S(1)} %get-tuple-element.27.refs_0_), channel_id=1, source_target_pairs={{0,8},{8,0},{16,24},{24,16},{1,9},{9,1},{17,25},{25,17},{2,10},{10... | collective-permute-start | bytes 2359304 | tf_op jit(solution)/shard_map/ppermute | solution.py:24
  48.0 6.7 %collective-permute-start.5 = (bf16[4,96,1024]{2,1,0:T(8,128)(2,1)S(1)}, bf16[4,96,1024]{2,1,0:T(8,128)(2,1)}, u32[]{:S(2)}, u32[]{:S(2)}) collective-permute-start(bf16[4,96,1024]{2,1,0:T(8,128)(2,1)S(1)} %get-tuple-element.26.refs_0_), channel_id=1, source_target_pairs={{0,8},{8,0},{16,24},{24,16},{1,9},{9,1},{17,25},{25,17},{2,10},{10... | collective-permute-start | bytes 2359304 | tf_op jit(solution)/shard_map/ppermute | solution.py:24
  59.8 1.1 copy-start
  72.9 16.9 %copy-start.2 = (bf16[4,96,1024]{2,1,0:T(8,128)(2,1)S(1)}, bf16[4,96,1024]{2,1,0:T(8,128)(2,1)}, u32[]{:S(2)}) copy-start(bf16[4,96,1024]{2,1,0:T(8,128)(2,1)} %get-tuple-element.16) | copy-start | bytes 2359300
  72.9 2.6 %collective-permute-start.7 = (bf16[4,96,1024]{2,1,0:T(8,128)(2,1)}, bf16[4,96,1024]{2,1,0:T(8,128)(2,1)S(1)}, u32[]{:S(2)}, u32[]{:S(2)}) collective-permute-start(bf16[4,96,1024]{2,1,0:T(8,128)(2,1)} %get-tuple-element.19), channel_id=1, source_target_pairs={{0,8},{8,0},{16,24},{24,16},{1,9},{9,1},{17,25},{25,17},{2,10},{10... | collective-permute-start | bytes 2359304 | tf_op jit(solution)/shard_map/ppermute | solution.py:24
  73.0 6.8 %collective-permute-start.6 = (bf16[4,96,1024]{2,1,0:T(8,128)(2,1)}, bf16[4,96,1024]{2,1,0:T(8,128)(2,1)S(1)}, u32[]{:S(2)}, u32[]{:S(2)}) collective-permute-start(bf16[4,96,1024]{2,1,0:T(8,128)(2,1)} %get-tuple-element.17), channel_id=1, source_target_pairs={{0,8},{8,0},{16,24},{24,16},{1,9},{9,1},{17,25},{25,17},{2,10},{10... | collective-permute-start | bytes 2359304 | tf_op jit(solution)/shard_map/ppermute | solution.py:24
  77.7 7.8 %collective-permute-start.10 = (bf16[2,96,1024]{2,1,0:T(8,128)(2,1)S(1)}, bf16[2,96,1024]{2,1,0:T(8,128)(2,1)S(1)}, u32[]{:S(2)}, u32[]{:S(2)}) collective-permute-start(bf16[2,96,1024]{2,1,0:T(8,128)(2,1)S(1)} %add_convert_fusion.1), channel_id=1, source_target_pairs={{0,1},{1,0},{2,3},{3,2},{4,5},{5,4},{6,7},{7,6},{8,24},{9,25},{10,... | collective-permute-start | bytes 1179656 | tf_op jit(solution)/shard_map/ppermute | solution.py:279
  79.2 10.5 %collective-permute-start.8 = (bf16[2,96,1024]{2,1,0:T(8,128)(2,1)S(1)}, bf16[2,96,1024]{2,1,0:T(8,128)(2,1)S(1)}, u32[]{:S(2)}, u32[]{:S(2)}) collective-permute-start(bf16[2,96,1024]{2,1,0:T(8,128)(2,1)S(1)} %add_convert_fusion.3), channel_id=1, source_target_pairs={{0,1},{1,0},{2,3},{3,2},{4,5},{5,4},{6,7},{7,6},{8,24},{9,25},{10,... | collective-permute-start | bytes 1179656 | tf_op jit(solution)/shard_map/ppermute | solution.py:279
  90.2 5.7 %collective-permute-start.11 = (bf16[2,96,512]{2,1,0:T(8,128)(2,1)S(1)}, bf16[2,96,512]{2,1,0:T(8,128)(2,1)S(1)}, u32[]{:S(2)}, u32[]{:S(2)}) collective-permute-start(bf16[2,96,512]{2,1,0:T(8,128)(2,1)S(1)} %constant_dynamic-slice_fusion), channel_id=1, source_target_pairs={{0,16},{1,17},{2,18},{3,19},{4,20},{5,21},{6,22},{7,23},{8,9},{9,8... | collective-permute-start | bytes 589832 | tf_op jit(solution)/shard_map/ppermute | solution.py:279
  91.8 6.3 %collective-permute-start.9 = (bf16[2,96,512]{2,1,0:T(8,128)(2,1)S(1)}, bf16[2,96,512]{2,1,0:T(8,128)(2,1)S(1)}, u32[]{:S(2)}, u32[]{:S(2)}) collective-permute-start(bf16[2,96,512]{2,1,0:T(8,128)(2,1)S(1)} %constant_dynamic-slice_fusion.1), channel_id=1, source_target_pairs={{0,16},{1,17},{2,18},{3,19},{4,20},{5,21},{6,22},{7,23},{8,9},{9,8... | collective-permute-start | bytes 589832 | tf_op jit(solution)/shard_map/ppermute | solution.py:279
  98.3 5.2 %collective-permute-start.12 = (bf16[96,512]{1,0:T(8,128)(2,1)S(1)}, bf16[96,512]{1,0:T(8,128)(2,1)S(1)}, u32[]{:S(2)}, u32[]{:S(2)}) collective-permute-start(bf16[96,512]{1,0:T(8,128)(2,1)S(1)} %get-tuple-element.36), channel_id=1, source_target_pairs={{0,2},{1,3},{2,0},{3,1},{4,6},{5,7},{6,4},{7,5},{8,10},{9,11},{10,... | collective-permute-start | bytes 294920 | tf_op jit(solution)/shard_map/ppermute | solution.py:24
  98.4 9.5 %collective-permute-start.13 = (bf16[96,512]{1,0:T(8,128)(2,1)S(1)}, bf16[96,512]{1,0:T(8,128)(2,1)S(1)}, u32[]{:S(2)}, u32[]{:S(2)}) collective-permute-start(bf16[96,512]{1,0:T(8,128)(2,1)S(1)} %get-tuple-element.37), channel_id=1, source_target_pairs={{0,4},{1,5},{2,6},{3,7},{4,0},{5,1},{6,2},{7,3},{8,12},{9,13},{10,... | collective-permute-start | bytes 294920 | tf_op jit(solution)/shard_map/ppermute | solution.py:24
  102.6 6.5 %collective-permute-start.14 = (bf16[96,512]{1,0:T(8,128)(2,1)S(1)}, bf16[96,512]{1,0:T(8,128)(2,1)S(1)}, u32[]{:S(2)}, u32[]{:S(2)}) collective-permute-start(bf16[96,512]{1,0:T(8,128)(2,1)S(1)} %get-tuple-element.38), channel_id=1, source_target_pairs={{0,6},{1,7},{2,4},{3,5},{4,2},{5,3},{6,0},{7,1},{8,14},{9,15},{10,... | collective-permute-start | bytes 294920 | tf_op jit(solution)/shard_map/ppermute | solution.py:24
  109.2 4.7 %collective-permute-start.15 = (bf16[96,512]{1,0:T(8,128)(2,1)S(1)}, bf16[96,512]{1,0:T(8,128)(2,1)S(1)}, u32[]{:S(2)}, u32[]{:S(2)}) collective-permute-start(bf16[96,512]{1,0:T(8,128)(2,1)S(1)} %fusion.5), channel_id=1, source_target_pairs={{0,16},{8,24},{16,0},{24,8},{1,17},{9,25},{17,1},{25,9},{2,18},{10... | collective-permute-start | bytes 294920 | tf_op jit(solution)/shard_map/ppermute | solution.py:24
  113.9 1.5 %collective-permute-start.16 = (bf16[96,1024]{1,0:T(8,128)(2,1)S(1)}, bf16[96,1024]{1,0:T(8,128)(2,1)S(1)}, u32[]{:S(2)}, u32[]{:S(2)}) collective-permute-start(bf16[96,1024]{1,0:T(8,128)(2,1)S(1)} %pad_maximum_fusion.4), channel_id=1, source_target_pairs={{0,8},{8,0},{16,24},{24,16},{1,9},{9,1},{17,25},{25,17},{2,10},{10... | collective-permute-start | bytes 589832 | tf_op jit(solution)/shard_map/ppermute | solution.py:24

commit v19 on v17

--- a/solution.py
+++ b/solution.py
@@ -182,16 +182,16 @@
             multiply(index + 1)
         totals[index].wait()
         cotangents[index].wait()
-        for row in range(0, chunk, 32):
-            at = slice(index * chunk + row, index * chunk + row + 32)
+        for row in range(0, chunk, 16):
+            at = slice(index * chunk + row, index * chunk + row + 16)
             for begin in range(0, hidden, span):
                 columns = slice(begin, begin + span)
-                value = values[index % 2, row : row + 32, columns] + total[at, columns].astype(F32)
-                value = value.astype(BF16)
+                value = values[index % 2, row : row + 16, columns] + total[at, columns].astype(F32)
                 square = value * value
                 bend = jnp.tanh(value * (square * (SCALE * CUBIC) + SCALE))
                 inner = value * (square * (1.5 * SCALE * CUBIC) + 0.5 * SCALE)
-                grad[at, columns] = cotangent[at, columns] * ((1.0 + bend) * (inner * (1.0 - bend) + 0.5))
+                slope = (1.0 + bend) * (inner * (1.0 - bend) + 0.5)
+                grad[at, columns] = (cotangent[at, columns].astype(F32) * slope).astype(BF16)
 
     for copy in inputs:
         copy.wait()

time: 116 us -> 117 us (level)
  no operation moved by 1% of the time
where the time goes in v19:
time: 117 us
  waiting for transfers between devices  61 us (52%)
  starting transfers between devices  26.1 us (22%)
  Pallas kernels  22.1 us (19%)
  other arithmetic  4.3 us (4%)
  local copies, waits for them, and re-layouts  2.15 us (2%)
    ppermute x11, waiting for transfers between devices, swap(): lax.ppermute(value, axis, [(index, index ^ step) for index in range(size)])  36.5 us
    ppermute x4, waiting for transfers between devices, turn_swap(): return lax.ppermute(value, ('rep', 'dom'), pairs)  15.6 us
    pallas_call x1, Pallas kernels, shards(): call(functools.partial(layer_kernel, sources, tiled), out_shapes, [SMEM,...  12.9 us
    ppermute x11, starting transfers between devices, swap(): lax.ppermute(value, axis, [(index, index ^ step) for index in range(size)])  11.5 us
    all_to_all x1, starting transfers between devices, shards(): lax.all_to_all(slots.reshape(dom_size, block, width), 'dom', split_axis=0...  5.58 us
    all_to_all x1, waiting for transfers between devices, shards(): lax.all_to_all(slots.reshape(dom_size, block, width), 'dom', split_axis=0...  5.09 us
    ppermute x2, starting transfers between devices, cross(): lax.ppermute(value, ('rep', 'dom'), [(source, target) for source, target...  4.77 us
    pallas_call x1, Pallas kernels, shards(): call(self_kernel, jax.ShapeDtypeStruct((rows, hidden), BF16), [SMEM] + [H...  4.67 us
  transfers between devices with their start and end apart: 18, of which 15 were waited for; matrix products, arithmetic and copies ran while one was open for 2% of the time, Pallas kernels for 8%

profile of v19, /device:TPU:0, one launch (start us, length us, event | category | flops | bytes accessed | tf_op | source)
XLA Modules:
  0.0 116.5 jit_solution(6854684433744584811)
XLA Ops:
  0.6 1.0 dynamic-slice_bitcast_fusion
  1.6 0.7 collective-permute-start
  2.3 4.1 %collective-permute-start.1 = (bf16[2,96,512]{2,1,0:T(8,128)(2,1)S(1)}, bf16[2,96,512]{2,1,0:T(8,128)(2,1)S(1)}, u32[]{:S(2)}, u32[]{:S(2)}) collective-permute-start(bf16[2,96,512]{2,1,0:T(8,128)(2,1)S(1)} %pad_maximum_fusion.3), channel_id=1, source_target_pairs={{0,4},{1,5},{2,6},{3,7},{4,0},{5,1},{6,2},{7,3},{8,13},{9,12},{10,... | collective-permute-start | bytes 589832 | tf_op jit(solution)/shard_map/ppermute | solution.py:31
  6.4 4.6 %shard_map.95 = bf16[1024,768]{1,0:T(8,128)(2,1)} custom-call(s32[32]{0:T(128)} %src_hbm.1, s32[32]{0:T(128)} %peer_hbm.1, bf16[32,128,128]{2,1,0:T(8,128)(2,1)} %tiles_hbm.1, bf16[1024,768]{1,0:T(8,128)(2,1)} %features_hbm.5), custom_call_target="tpu_custom_call" | custom-call | flops 1610612736 | bytes 4194304 | tf_op jit(solution)/shard_map/pallas_call | solution.py:312
  11.0 3.9 %collective-permute-done.1 = bf16[2,96,512]{2,1,0:T(8,128)(2,1)S(1)} collective-permute-done((bf16[2,96,512]{2,1,0:T(8,128)(2,1)S(1)}, bf16[2,96,512]{2,1,0:T(8,128)(2,1)S(1)}, u32[]{:S(2)}, u32[]{:S(2)}) %collective-permute-start.1) | collective-permute-done | bytes 196640 | tf_op jit(solution)/shard_map/ppermute | solution.py:31
  15.0 2.5 %collective-permute-start.2 = (bf16[2,2,96,512]{3,2,1,0:T(8,128)(2,1)S(1)}, bf16[2,2,96,512]{3,2,1,0:T(8,128)(2,1)S(1)}, u32[]{:S(2)}, u32[]{:S(2)}) collective-permute-start(bf16[2,2,96,512]{3,2,1,0:T(8,128)(2,1)S(1)} %pad_maximum_fusion.2), channel_id=1, source_target_pairs={{0,2},{1,3},{2,0},{3,1},{4,6},{5,7},{6,4},{7,5},{8,10},{9,11},{10,... | collective-permute-start | bytes 1179656 | tf_op jit(solution)/shard_map/ppermute | solution.py:23
  17.4 5.6 %all-to-all-start = ((bf16[8,128,768]{2,1,0:T(8,128)(2,1)}), bf16[8,128,768]{2,1,0:T(8,128)(2,1)S(1)}, u32[]{:S(2)}, u32[]{:S(2)}) async-start(bf16[8,128,768]{2,1,0:T(8,128)(2,1)} %bitcast.6), calls=%async_computation | async-start | bytes 3145728 | tf_op jit(solution)/shard_map/all_to_all | solution.py:337
  23.0 3.8 %collective-permute-done.2 = bf16[2,2,96,512]{3,2,1,0:T(8,128)(2,1)S(1)} collective-permute-done((bf16[2,2,96,512]{3,2,1,0:T(8,128)(2,1)S(1)}, bf16[2,2,96,512]{3,2,1,0:T(8,128)(2,1)S(1)}, u32[]{:S(2)}, u32[]{:S(2)}) %collective-permute-start.2) | collective-permute-done | bytes 393248 | tf_op jit(solution)/shard_map/ppermute | solution.py:23
  27.0 1.6 %collective-permute-start.3 = (bf16[2,4,96,512]{3,2,1,0:T(8,128)(2,1)S(1)}, bf16[2,4,96,512]{3,2,1,0:T(8,128)(2,1)S(1)}, u32[]{:S(2)}, u32[]{:S(2)}) collective-permute-start(bf16[2,4,96,512]{3,2,1,0:T(8,128)(2,1)S(1)} %bitcast.37), channel_id=1, source_target_pairs={{0,16},{8,24},{16,0},{24,8},{1,17},{9,25},{17,1},{25,9},{2,18},{10... | collective-permute-start | bytes 2359304 | tf_op jit(solution)/shard_map/ppermute | solution.py:23
  28.6 18.4 %collective-permute-done.3 = bf16[2,4,96,512]{3,2,1,0:T(8,128)(2,1)S(1)} collective-permute-done((bf16[2,4,96,512]{3,2,1,0:T(8,128)(2,1)S(1)}, bf16[2,4,96,512]{3,2,1,0:T(8,128)(2,1)S(1)}, u32[]{:S(2)}, u32[]{:S(2)}) %collective-permute-start.3) | collective-permute-done | bytes 786464 | tf_op jit(solution)/shard_map/ppermute | solution.py:23
  47.3 0.7 collective-permute-start.4
  48.7 1.4 %collective-permute-done.4.refs_1_ = bf16[4,96,1024]{2,1,0:T(8,128)(2,1)} collective-permute-done((bf16[4,96,1024]{2,1,0:T(8,128)(2,1)S(1)}, bf16[4,96,1024]{2,1,0:T(8,128)(2,1)}, u32[]{:S(2)}, u32[]{:S(2)}) %collective-permute-start.4) | collective-permute-done | bytes 786464 | tf_op jit(solution)/shard_map/ppermute | solution.py:23
  50.0 4.7 %shard_map.96.total_hbm = bf16[1024,1024]{1,0:T(8,128)(2,1)} custom-call(s32[1]{0:T(128)} %bitcast.1.flip_ref, bf16[1024,768]{1,0:T(8,128)(2,1)} %features_hbm.5, bf16[4,96,1024]{2,1,0:T(8,128)(2,1)} %copy-done.3, bf16[4,96,1024]{2,1,0:T(8,128)(2,1)} %collective-permute-done.4.refs_1_), custom_call_target="tpu_custom_call" | custom-call | flops 1610612736 | bytes 7340032 | tf_op jit(solution)/shard_map/pallas_call | solution.py:347
  54.7 5.1 %all-to-all-done.slots_hbm = bf16[8,128,768]{2,1,0:T(8,128)(2,1)S(1)} async-done(((bf16[8,128,768]{2,1,0:T(8,128)(2,1)}), bf16[8,128,768]{2,1,0:T(8,128)(2,1)S(1)}, u32[]{:S(2)}, u32[]{:S(2)}) %all-to-all-start) | async-done | bytes 1572896 | tf_op jit(solution)/shard_map/all_to_all | solution.py:337
  59.8 1.1 copy-done
  61.0 12.9 %shard_map.97 = (bf16[4,96,1024]{2,1,0:T(8,128)(2,1)}, bf16[4,96,1024]{2,1,0:T(8,128)(2,1)}, bf16[4,96,1024]{2,1,0:T(8,128)(2,1)}, bf16[4,96,1024]{2,1,0:T(8,128)(2,1)}) custom-call(s32[4]{0:T(128)} %pad_add_fusion.places_ref, s32[8]{0:T(128)} %into_ref.1, bf16[8,128,768]{2,1,0:T(8,128)(2,1)} %copy-done, bf16[1024,1024]{1,0:T(8,128)(2,1)} %shard_map.96.total_hbm, ...), custom_call_target="tpu_custom_call" | custom-call | flops 4831838208 | bytes 16777216 | tf_op jit(solution)/shard_map/pallas_call | solution.py:372
  74.4 2.0 %collective-permute-done.7 = bf16[4,96,1024]{2,1,0:T(8,128)(2,1)S(1)} collective-permute-done((bf16[4,96,1024]{2,1,0:T(8,128)(2,1)}, bf16[4,96,1024]{2,1,0:T(8,128)(2,1)S(1)}, u32[]{:S(2)}, u32[]{:S(2)}) %collective-permute-start.7) | collective-permute-done | bytes 786464 | tf_op jit(solution)/shard_map/ppermute | solution.py:23
  76.4 1.4 %add_convert_fusion.1 = (bf16[2,96,1024]{2,1,0:T(8,128)(2,1)S(1)}, bf16[2,96,1024]{2,1,0:T(8,128)(2,1)S(1)}) fusion(bf16[4,96,1024]{2,1,0:T(8,128)(2,1)S(1)} %collective-permute-done.7, bf16[4,96,1024]{2,1,0:T(8,128)(2,1)} %get-tuple-element.14), kind=kLoop, calls=%fused_computation.8 | loop fusion | flops 1572864 | bytes 2359296 | tf_op jit(solution)/shard_map/convert_element_type | solution.py:253
  77.8 1.5 %collective-permute-start.10 = (bf16[2,96,1024]{2,1,0:T(8,128)(2,1)S(1)}, bf16[2,96,1024]{2,1,0:T(8,128)(2,1)S(1)}, u32[]{:S(2)}, u32[]{:S(2)}) collective-permute-start(bf16[2,96,1024]{2,1,0:T(8,128)(2,1)S(1)} %get-tuple-element.18), channel_id=1, source_target_pairs={{0,1},{1,0},{2,3},{3,2},{4,5},{5,4},{6,7},{7,6},{8,24},{9,25},{10,... | collective-permute-start | bytes 1179656 | tf_op jit(solution)/shard_map/ppermute | solution.py:278
  79.9 5.7 %collective-permute-done.10 = bf16[2,96,1024]{2,1,0:T(8,128)(2,1)S(1)} collective-permute-done((bf16[2,96,1024]{2,1,0:T(8,128)(2,1)S(1)}, bf16[2,96,1024]{2,1,0:T(8,128)(2,1)S(1)}, u32[]{:S(2)}, u32[]{:S(2)}) %collective-permute-start.10) | collective-permute-done | bytes 393248 | tf_op jit(solution)/shard_map/ppermute | solution.py:278
  85.7 4.2 %collective-permute-done.8 = bf16[2,96,1024]{2,1,0:T(8,128)(2,1)S(1)} collective-permute-done((bf16[2,96,1024]{2,1,0:T(8,128)(2,1)S(1)}, bf16[2,96,1024]{2,1,0:T(8,128)(2,1)S(1)}, u32[]{:S(2)}, u32[]{:S(2)}) %collective-permute-start.8) | collective-permute-done | bytes 393248 | tf_op jit(solution)/shard_map/ppermute | solution.py:278
  90.3 1.6 %collective-permute-start.11 = (bf16[2,96,512]{2,1,0:T(8,128)(2,1)S(1)}, bf16[2,96,512]{2,1,0:T(8,128)(2,1)S(1)}, u32[]{:S(2)}, u32[]{:S(2)}) collective-permute-start(bf16[2,96,512]{2,1,0:T(8,128)(2,1)S(1)} %constant_dynamic-slice_fusion), channel_id=1, source_target_pairs={{0,16},{1,17},{2,18},{3,19},{4,20},{5,21},{6,22},{7,23},{8,9},{9,8... | collective-permute-start | bytes 589832 | tf_op jit(solution)/shard_map/ppermute | solution.py:278
  92.5 3.6 %collective-permute-done.11 = bf16[2,96,512]{2,1,0:T(8,128)(2,1)S(1)} collective-permute-done((bf16[2,96,512]{2,1,0:T(8,128)(2,1)S(1)}, bf16[2,96,512]{2,1,0:T(8,128)(2,1)S(1)}, u32[]{:S(2)}, u32[]{:S(2)}) %collective-permute-start.11) | collective-permute-done | bytes 196640 | tf_op jit(solution)/shard_map/ppermute | solution.py:278
  96.1 2.0 %collective-permute-done.9 = bf16[2,96,512]{2,1,0:T(8,128)(2,1)S(1)} collective-permute-done((bf16[2,96,512]{2,1,0:T(8,128)(2,1)S(1)}, bf16[2,96,512]{2,1,0:T(8,128)(2,1)S(1)}, u32[]{:S(2)}, u32[]{:S(2)}) %collective-permute-start.9) | collective-permute-done | bytes 196640 | tf_op jit(solution)/shard_map/ppermute | solution.py:278
  98.5 4.2 %collective-permute-start.13 = (bf16[96,512]{1,0:T(8,128)(2,1)S(1)}, bf16[96,512]{1,0:T(8,128)(2,1)S(1)}, u32[]{:S(2)}, u32[]{:S(2)}) collective-permute-start(bf16[96,512]{1,0:T(8,128)(2,1)S(1)} %get-tuple-element.31), channel_id=1, source_target_pairs={{0,4},{1,5},{2,6},{3,7},{4,0},{5,1},{6,2},{7,3},{8,12},{9,13},{10,... | collective-permute-start | bytes 294920 | tf_op jit(solution)/shard_map/ppermute | solution.py:23
  102.8 0.8 collective-permute-done.12
  103.6 4.4 %collective-permute-done.13 = bf16[96,512]{1,0:T(8,128)(2,1)S(1)} collective-permute-done((bf16[96,512]{1,0:T(8,128)(2,1)S(1)}, bf16[96,512]{1,0:T(8,128)(2,1)S(1)}, u32[]{:S(2)}, u32[]{:S(2)}) %collective-permute-start.13) | collective-permute-done | bytes 98336 | tf_op jit(solution)/shard_map/ppermute | solution.py:23
  108.0 1.2 %collective-permute-done.14 = bf16[96,512]{1,0:T(8,128)(2,1)S(1)} collective-permute-done((bf16[96,512]{1,0:T(8,128)(2,1)S(1)}, bf16[96,512]{1,0:T(8,128)(2,1)S(1)}, u32[]{:S(2)}, u32[]{:S(2)}) %collective-permute-start.14) | collective-permute-done | bytes 98336 | tf_op jit(solution)/shard_map/ppermute | solution.py:23
  109.3 1.6 %collective-permute-start.15 = (bf16[96,512]{1,0:T(8,128)(2,1)S(1)}, bf16[96,512]{1,0:T(8,128)(2,1)S(1)}, u32[]{:S(2)}, u32[]{:S(2)}) collective-permute-start(bf16[96,512]{1,0:T(8,128)(2,1)S(1)} %fusion.5), channel_id=1, source_target_pairs={{0,16},{8,24},{16,0},{24,8},{1,17},{9,25},{17,1},{25,9},{2,18},{10... | collective-permute-start | bytes 294920 | tf_op jit(solution)/shard_map/ppermute | solution.py:23
  110.9 3.1 %collective-permute-done.15 = bf16[96,512]{1,0:T(8,128)(2,1)S(1)} collective-permute-done((bf16[96,512]{1,0:T(8,128)(2,1)S(1)}, bf16[96,512]{1,0:T(8,128)(2,1)S(1)}, u32[]{:S(2)}, u32[]{:S(2)}) %collective-permute-start.15) | collective-permute-done | bytes 98336 | tf_op jit(solution)/shard_map/ppermute | solution.py:23
  114.1 1.4 %collective-permute-done.16 = bf16[96,1024]{1,0:T(8,128)(2,1)S(1)} collective-permute-done((bf16[96,1024]{1,0:T(8,128)(2,1)S(1)}, bf16[96,1024]{1,0:T(8,128)(2,1)S(1)}, u32[]{:S(2)}, u32[]{:S(2)}) %collective-permute-start.16) | collective-permute-done | bytes 196640 | tf_op jit(solution)/shard_map/ppermute | solution.py:23
  115.5 1.0 select_convert_fusion
  (35 shorter events, 4.0 us)
Async XLA Ops:
  1.6 9.3 %collective-permute-start = (bf16[2,96,512]{2,1,0:T(8,128)(2,1)S(1)}, bf16[2,96,512]{2,1,0:T(8,128)(2,1)S(1)}, u32[]{:S(2)}, u32[]{:S(2)}) collective-permute-start(bf16[2,96,512]{2,1,0:T(8,128)(2,1)S(1)} %pad_maximum_fusion.3), channel_id=1, source_target_pairs={{8,9},{9,8},{10,11},{11,10},{12,13},{13,12},{14,15},{15,14},{24,25... | collective-permute-start | bytes 589832 | tf_op jit(solution)/shard_map/ppermute | solution.py:31
  2.3 12.6 %collective-permute-start.1 = (bf16[2,96,512]{2,1,0:T(8,128)(2,1)S(1)}, bf16[2,96,512]{2,1,0:T(8,128)(2,1)S(1)}, u32[]{:S(2)}, u32[]{:S(2)}) collective-permute-start(bf16[2,96,512]{2,1,0:T(8,128)(2,1)S(1)} %pad_maximum_fusion.3), channel_id=1, source_target_pairs={{0,4},{1,5},{2,6},{3,7},{4,0},{5,1},{6,2},{7,3},{8,13},{9,12},{10,... | collective-permute-start | bytes 589832 | tf_op jit(solution)/shard_map/ppermute | solution.py:31
  15.0 11.9 %collective-permute-start.2 = (bf16[2,2,96,512]{3,2,1,0:T(8,128)(2,1)S(1)}, bf16[2,2,96,512]{3,2,1,0:T(8,128)(2,1)S(1)}, u32[]{:S(2)}, u32[]{:S(2)}) collective-permute-start(bf16[2,2,96,512]{3,2,1,0:T(8,128)(2,1)S(1)} %pad_maximum_fusion.2), channel_id=1, source_target_pairs={{0,2},{1,3},{2,0},{3,1},{4,6},{5,7},{6,4},{7,5},{8,10},{9,11},{10,... | collective-permute-start | bytes 1179656 | tf_op jit(solution)/shard_map/ppermute | solution.py:23
  17.4 42.4 %all-to-all-start = ((bf16[8,128,768]{2,1,0:T(8,128)(2,1)}), bf16[8,128,768]{2,1,0:T(8,128)(2,1)S(1)}, u32[]{:S(2)}, u32[]{:S(2)}) async-start(bf16[8,128,768]{2,1,0:T(8,128)(2,1)} %bitcast.6), calls=%async_computation | async-start | bytes 3145728 | tf_op jit(solution)/shard_map/all_to_all | solution.py:337
  27.0 19.9 %collective-permute-start.3 = (bf16[2,4,96,512]{3,2,1,0:T(8,128)(2,1)S(1)}, bf16[2,4,96,512]{3,2,1,0:T(8,128)(2,1)S(1)}, u32[]{:S(2)}, u32[]{:S(2)}) collective-permute-start(bf16[2,4,96,512]{3,2,1,0:T(8,128)(2,1)S(1)} %bitcast.37), channel_id=1, source_target_pairs={{0,16},{8,24},{16,0},{24,8},{1,17},{9,25},{17,1},{25,9},{2,18},{10... | collective-permute-start | bytes 2359304 | tf_op jit(solution)/shard_map/ppermute | solution.py:23
  47.3 2.8 %copy-start.3 = (bf16[4,96,1024]{2,1,0:T(8,128)(2,1)}, bf16[4,96,1024]{2,1,0:T(8,128)(2,1)S(1)}, u32[]{:S(2)}) copy-start(bf16[4,96,1024]{2,1,0:T(8,128)(2,1)S(1)} %get-tuple-element.21.refs_0_) | copy-start | bytes 2359300
  47.3 7.5 %copy-start.2 = (bf16[4,96,1024]{2,1,0:T(8,128)(2,1)}, bf16[4,96,1024]{2,1,0:T(8,128)(2,1)S(1)}, u32[]{:S(2)}) copy-start(bf16[4,96,1024]{2,1,0:T(8,128)(2,1)S(1)} %get-tuple-element.20.refs_0_) | copy-start | bytes 2359300
  47.3 2.8 %collective-permute-start.4 = (bf16[4,96,1024]{2,1,0:T(8,128)(2,1)S(1)}, bf16[4,96,1024]{2,1,0:T(8,128)(2,1)}, u32[]{:S(2)}, u32[]{:S(2)}) collective-permute-start(bf16[4,96,1024]{2,1,0:T(8,128)(2,1)S(1)} %get-tuple-element.21.refs_0_), channel_id=1, source_target_pairs={{0,8},{8,0},{16,24},{24,16},{1,9},{9,1},{17,25},{25,17},{2,10},{10... | collective-permute-start | bytes 2359304 | tf_op jit(solution)/shard_map/ppermute | solution.py:23
  48.0 6.7 %collective-permute-start.5 = (bf16[4,96,1024]{2,1,0:T(8,128)(2,1)S(1)}, bf16[4,96,1024]{2,1,0:T(8,128)(2,1)}, u32[]{:S(2)}, u32[]{:S(2)}) collective-permute-start(bf16[4,96,1024]{2,1,0:T(8,128)(2,1)S(1)} %get-tuple-element.20.refs_0_), channel_id=1, source_target_pairs={{0,8},{8,0},{16,24},{24,16},{1,9},{9,1},{17,25},{25,17},{2,10},{10... | collective-permute-start | bytes 2359304 | tf_op jit(solution)/shard_map/ppermute | solution.py:23
  59.8 1.1 copy-start
  73.8 16.1 %copy-start.1 = (bf16[4,96,1024]{2,1,0:T(8,128)(2,1)S(1)}, bf16[4,96,1024]{2,1,0:T(8,128)(2,1)}, u32[]{:S(2)}) copy-start(bf16[4,96,1024]{2,1,0:T(8,128)(2,1)} %get-tuple-element.12) | copy-start | bytes 2359300
  73.8 2.6 %collective-permute-start.7 = (bf16[4,96,1024]{2,1,0:T(8,128)(2,1)}, bf16[4,96,1024]{2,1,0:T(8,128)(2,1)S(1)}, u32[]{:S(2)}, u32[]{:S(2)}) collective-permute-start(bf16[4,96,1024]{2,1,0:T(8,128)(2,1)} %get-tuple-element.15), channel_id=1, source_target_pairs={{0,8},{8,0},{16,24},{24,16},{1,9},{9,1},{17,25},{25,17},{2,10},{10... | collective-permute-start | bytes 2359304 | tf_op jit(solution)/shard_map/ppermute | solution.py:23
  73.9 6.0 %collective-permute-start.6 = (bf16[4,96,1024]{2,1,0:T(8,128)(2,1)}, bf16[4,96,1024]{2,1,0:T(8,128)(2,1)S(1)}, u32[]{:S(2)}, u32[]{:S(2)}) collective-permute-start(bf16[4,96,1024]{2,1,0:T(8,128)(2,1)} %get-tuple-element.13), channel_id=1, source_target_pairs={{0,8},{8,0},{16,24},{24,16},{1,9},{9,1},{17,25},{25,17},{2,10},{10... | collective-permute-start | bytes 2359304 | tf_op jit(solution)/shard_map/ppermute | solution.py:23
  77.8 7.8 %collective-permute-start.10 = (bf16[2,96,1024]{2,1,0:T(8,128)(2,1)S(1)}, bf16[2,96,1024]{2,1,0:T(8,128)(2,1)S(1)}, u32[]{:S(2)}, u32[]{:S(2)}) collective-permute-start(bf16[2,96,1024]{2,1,0:T(8,128)(2,1)S(1)} %get-tuple-element.18), channel_id=1, source_target_pairs={{0,1},{1,0},{2,3},{3,2},{4,5},{5,4},{6,7},{7,6},{8,24},{9,25},{10,... | collective-permute-start | bytes 1179656 | tf_op jit(solution)/shard_map/ppermute | solution.py:278
  79.4 10.5 %collective-permute-start.8 = (bf16[2,96,1024]{2,1,0:T(8,128)(2,1)S(1)}, bf16[2,96,1024]{2,1,0:T(8,128)(2,1)S(1)}, u32[]{:S(2)}, u32[]{:S(2)}) collective-permute-start(bf16[2,96,1024]{2,1,0:T(8,128)(2,1)S(1)} %get-tuple-element.19), channel_id=1, source_target_pairs={{0,1},{1,0},{2,3},{3,2},{4,5},{5,4},{6,7},{7,6},{8,24},{9,25},{10,... | collective-permute-start | bytes 1179656 | tf_op jit(solution)/shard_map/ppermute | solution.py:278
  90.3 5.7 %collective-permute-start.11 = (bf16[2,96,512]{2,1,0:T(8,128)(2,1)S(1)}, bf16[2,96,512]{2,1,0:T(8,128)(2,1)S(1)}, u32[]{:S(2)}, u32[]{:S(2)}) collective-permute-start(bf16[2,96,512]{2,1,0:T(8,128)(2,1)S(1)} %constant_dynamic-slice_fusion), channel_id=1, source_target_pairs={{0,16},{1,17},{2,18},{3,19},{4,20},{5,21},{6,22},{7,23},{8,9},{9,8... | collective-permute-start | bytes 589832 | tf_op jit(solution)/shard_map/ppermute | solution.py:278
  92.0 6.2 %collective-permute-start.9 = (bf16[2,96,512]{2,1,0:T(8,128)(2,1)S(1)}, bf16[2,96,512]{2,1,0:T(8,128)(2,1)S(1)}, u32[]{:S(2)}, u32[]{:S(2)}) collective-permute-start(bf16[2,96,512]{2,1,0:T(8,128)(2,1)S(1)} %constant_dynamic-slice_fusion.1), channel_id=1, source_target_pairs={{0,16},{1,17},{2,18},{3,19},{4,20},{5,21},{6,22},{7,23},{8,9},{9,8... | collective-permute-start | bytes 589832 | tf_op jit(solution)/shard_map/ppermute | solution.py:278
  98.4 5.2 %collective-permute-start.12 = (bf16[96,512]{1,0:T(8,128)(2,1)S(1)}, bf16[96,512]{1,0:T(8,128)(2,1)S(1)}, u32[]{:S(2)}, u32[]{:S(2)}) collective-permute-start(bf16[96,512]{1,0:T(8,128)(2,1)S(1)} %get-tuple-element.30), channel_id=1, source_target_pairs={{0,2},{1,3},{2,0},{3,1},{4,6},{5,7},{6,4},{7,5},{8,10},{9,11},{10,... | collective-permute-start | bytes 294920 | tf_op jit(solution)/shard_map/ppermute | solution.py:23
  98.5 9.5 %collective-permute-start.13 = (bf16[96,512]{1,0:T(8,128)(2,1)S(1)}, bf16[96,512]{1,0:T(8,128)(2,1)S(1)}, u32[]{:S(2)}, u32[]{:S(2)}) collective-permute-start(bf16[96,512]{1,0:T(8,128)(2,1)S(1)} %get-tuple-element.31), channel_id=1, source_target_pairs={{0,4},{1,5},{2,6},{3,7},{4,0},{5,1},{6,2},{7,3},{8,12},{9,13},{10,... | collective-permute-start | bytes 294920 | tf_op jit(solution)/shard_map/ppermute | solution.py:23
  102.7 6.5 %collective-permute-start.14 = (bf16[96,512]{1,0:T(8,128)(2,1)S(1)}, bf16[96,512]{1,0:T(8,128)(2,1)S(1)}, u32[]{:S(2)}, u32[]{:S(2)}) collective-permute-start(bf16[96,512]{1,0:T(8,128)(2,1)S(1)} %get-tuple-element.32), channel_id=1, source_target_pairs={{0,6},{1,7},{2,4},{3,5},{4,2},{5,3},{6,0},{7,1},{8,14},{9,15},{10,... | collective-permute-start | bytes 294920 | tf_op jit(solution)/shard_map/ppermute | solution.py:23
  109.3 4.7 %collective-permute-start.15 = (bf16[96,512]{1,0:T(8,128)(2,1)S(1)}, bf16[96,512]{1,0:T(8,128)(2,1)S(1)}, u32[]{:S(2)}, u32[]{:S(2)}) collective-permute-start(bf16[96,512]{1,0:T(8,128)(2,1)S(1)} %fusion.5), channel_id=1, source_target_pairs={{0,16},{8,24},{16,0},{24,8},{1,17},{9,25},{17,1},{25,9},{2,18},{10... | collective-permute-start | bytes 294920 | tf_op jit(solution)/shard_map/ppermute | solution.py:23
  114.0 1.5 %collective-permute-start.16 = (bf16[96,1024]{1,0:T(8,128)(2,1)S(1)}, bf16[96,1024]{1,0:T(8,128)(2,1)S(1)}, u32[]{:S(2)}, u32[]{:S(2)}) collective-permute-start(bf16[96,1024]{1,0:T(8,128)(2,1)S(1)} %pad_maximum_fusion.4), channel_id=1, source_target_pairs={{0,8},{8,0},{16,24},{24,16},{1,9},{9,1},{17,25},{25,17},{2,10},{10... | collective-permute-start | bytes 589832 | tf_op jit(solution)/shard_map/ppermute | solution.py:23

commit v20 on v19

--- a/solution.py
+++ b/solution.py
@@ -147,7 +147,7 @@
 
     for copy in arrivals:
         copy.wait()
-    for copy in [copy for pair in zip(totals[1:], cotangents[1:]) for copy in pair] + inputs:
+    for copy in [copy for pair in zip(totals[1:], cotangents[1:]) for copy in pair]:
         copy.start()
     for sender in range(senders):
         if sender == 0:
@@ -182,6 +182,9 @@
             multiply(index + 1)
         totals[index].wait()
         cotangents[index].wait()
+        if index == 0:
+            for copy in inputs:
+                copy.start()
         for row in range(0, chunk, 16):
             at = slice(index * chunk + row, index * chunk + row + 16)
             for begin in range(0, hidden, span):

time: 117 us -> 117 us (level)
  no operation moved by 1% of the time
where the time goes in v20:
time: 117 us; the launch traced here: 116 us
  waiting for transfers between devices  61 us (52%)
  starting transfers between devices  26.1 us (22%)
  Pallas kernels  22.1 us (19%)
  other arithmetic  4.3 us (4%)
  local copies, waits for them, and re-layouts  2.15 us (2%)
    ppermute x11, waiting for transfers between devices, swap(): lax.ppermute(value, axis, [(index, index ^ step) for index in range(size)])  36.4 us
    ppermute x4, waiting for transfers between devices, turn_swap(): return lax.ppermute(value, ('rep', 'dom'), pairs)  15.6 us
    pallas_call x1, Pallas kernels, shards(): call(functools.partial(layer_kernel, sources, tiled), out_shapes, [SMEM,...  12.8 us
    ppermute x11, starting transfers between devices, swap(): lax.ppermute(value, axis, [(index, index ^ step) for index in range(size)])  11.5 us
    all_to_all x1, starting transfers between devices, shards(): lax.all_to_all(slots.reshape(dom_size, block, width), 'dom', split_axis=0...  5.58 us
    all_to_all x1, waiting for transfers between devices, shards(): lax.all_to_all(slots.reshape(dom_size, block, width), 'dom', split_axis=0...  5.09 us
    ppermute x2, starting transfers between devices, cross(): lax.ppermute(value, ('rep', 'dom'), [(source, target) for source, target...  4.77 us
    pallas_call x1, Pallas kernels, shards(): call(self_kernel, jax.ShapeDtypeStruct((rows, hidden), BF16), [SMEM] + [H...  4.67 us
  transfers between devices with their start and end apart: 18, of which 15 were waited for; matrix products, arithmetic and copies ran while one was open for 2% of the time, Pallas kernels for 8%

profile of v20, /device:TPU:0, one launch (start us, length us, event | category | flops | bytes accessed | tf_op | source)
XLA Modules:
  0.0 116.5 jit_solution(13363508957760348865)
XLA Ops:
  0.6 1.0 dynamic-slice_bitcast_fusion
  1.6 0.7 collective-permute-start
  2.3 4.1 %collective-permute-start.1 = (bf16[2,96,512]{2,1,0:T(8,128)(2,1)S(1)}, bf16[2,96,512]{2,1,0:T(8,128)(2,1)S(1)}, u32[]{:S(2)}, u32[]{:S(2)}) collective-permute-start(bf16[2,96,512]{2,1,0:T(8,128)(2,1)S(1)} %pad_maximum_fusion.3), channel_id=1, source_target_pairs={{0,4},{1,5},{2,6},{3,7},{4,0},{5,1},{6,2},{7,3},{8,13},{9,12},{10,... | collective-permute-start | bytes 589832 | tf_op jit(solution)/shard_map/ppermute | solution.py:31
  6.4 4.6 %shard_map.95 = bf16[1024,768]{1,0:T(8,128)(2,1)} custom-call(s32[32]{0:T(128)} %src_hbm.1, s32[32]{0:T(128)} %peer_hbm.1, bf16[32,128,128]{2,1,0:T(8,128)(2,1)} %tiles_hbm.1, bf16[1024,768]{1,0:T(8,128)(2,1)} %features_hbm.5), custom_call_target="tpu_custom_call" | custom-call | flops 1610612736 | bytes 4194304 | tf_op jit(solution)/shard_map/pallas_call | solution.py:315
  11.0 3.9 %collective-permute-done.1 = bf16[2,96,512]{2,1,0:T(8,128)(2,1)S(1)} collective-permute-done((bf16[2,96,512]{2,1,0:T(8,128)(2,1)S(1)}, bf16[2,96,512]{2,1,0:T(8,128)(2,1)S(1)}, u32[]{:S(2)}, u32[]{:S(2)}) %collective-permute-start.1) | collective-permute-done | bytes 196640 | tf_op jit(solution)/shard_map/ppermute | solution.py:31
  15.0 2.5 %collective-permute-start.2 = (bf16[2,2,96,512]{3,2,1,0:T(8,128)(2,1)S(1)}, bf16[2,2,96,512]{3,2,1,0:T(8,128)(2,1)S(1)}, u32[]{:S(2)}, u32[]{:S(2)}) collective-permute-start(bf16[2,2,96,512]{3,2,1,0:T(8,128)(2,1)S(1)} %pad_maximum_fusion.2), channel_id=1, source_target_pairs={{0,2},{1,3},{2,0},{3,1},{4,6},{5,7},{6,4},{7,5},{8,10},{9,11},{10,... | collective-permute-start | bytes 1179656 | tf_op jit(solution)/shard_map/ppermute | solution.py:23
  17.4 5.6 %all-to-all-start = ((bf16[8,128,768]{2,1,0:T(8,128)(2,1)}), bf16[8,128,768]{2,1,0:T(8,128)(2,1)S(1)}, u32[]{:S(2)}, u32[]{:S(2)}) async-start(bf16[8,128,768]{2,1,0:T(8,128)(2,1)} %bitcast.6), calls=%async_computation | async-start | bytes 3145728 | tf_op jit(solution)/shard_map/all_to_all | solution.py:340
  23.0 3.8 %collective-permute-done.2 = bf16[2,2,96,512]{3,2,1,0:T(8,128)(2,1)S(1)} collective-permute-done((bf16[2,2,96,512]{3,2,1,0:T(8,128)(2,1)S(1)}, bf16[2,2,96,512]{3,2,1,0:T(8,128)(2,1)S(1)}, u32[]{:S(2)}, u32[]{:S(2)}) %collective-permute-start.2) | collective-permute-done | bytes 393248 | tf_op jit(solution)/shard_map/ppermute | solution.py:23
  27.0 1.6 %collective-permute-start.3 = (bf16[2,4,96,512]{3,2,1,0:T(8,128)(2,1)S(1)}, bf16[2,4,96,512]{3,2,1,0:T(8,128)(2,1)S(1)}, u32[]{:S(2)}, u32[]{:S(2)}) collective-permute-start(bf16[2,4,96,512]{3,2,1,0:T(8,128)(2,1)S(1)} %bitcast.37), channel_id=1, source_target_pairs={{0,16},{8,24},{16,0},{24,8},{1,17},{9,25},{17,1},{25,9},{2,18},{10... | collective-permute-start | bytes 2359304 | tf_op jit(solution)/shard_map/ppermute | solution.py:23
  28.6 18.4 %collective-permute-done.3 = bf16[2,4,96,512]{3,2,1,0:T(8,128)(2,1)S(1)} collective-permute-done((bf16[2,4,96,512]{3,2,1,0:T(8,128)(2,1)S(1)}, bf16[2,4,96,512]{3,2,1,0:T(8,128)(2,1)S(1)}, u32[]{:S(2)}, u32[]{:S(2)}) %collective-permute-start.3) | collective-permute-done | bytes 786464 | tf_op jit(solution)/shard_map/ppermute | solution.py:23
  47.3 0.7 collective-permute-start.4
  48.7 1.4 %collective-permute-done.4.refs_1_ = bf16[4,96,1024]{2,1,0:T(8,128)(2,1)} collective-permute-done((bf16[4,96,1024]{2,1,0:T(8,128)(2,1)S(1)}, bf16[4,96,1024]{2,1,0:T(8,128)(2,1)}, u32[]{:S(2)}, u32[]{:S(2)}) %collective-permute-start.4) | collective-permute-done | bytes 786464 | tf_op jit(solution)/shard_map/ppermute | solution.py:23
  50.0 4.7 %shard_map.96.total_hbm = bf16[1024,1024]{1,0:T(8,128)(2,1)} custom-call(s32[1]{0:T(128)} %bitcast.1.flip_ref, bf16[1024,768]{1,0:T(8,128)(2,1)} %features_hbm.5, bf16[4,96,1024]{2,1,0:T(8,128)(2,1)} %copy-done.3, bf16[4,96,1024]{2,1,0:T(8,128)(2,1)} %collective-permute-done.4.refs_1_), custom_call_target="tpu_custom_call" | custom-call | flops 1610612736 | bytes 7340032 | tf_op jit(solution)/shard_map/pallas_call | solution.py:350
  54.7 5.1 %all-to-all-done.slots_hbm = bf16[8,128,768]{2,1,0:T(8,128)(2,1)S(1)} async-done(((bf16[8,128,768]{2,1,0:T(8,128)(2,1)}), bf16[8,128,768]{2,1,0:T(8,128)(2,1)S(1)}, u32[]{:S(2)}, u32[]{:S(2)}) %all-to-all-start) | async-done | bytes 1572896 | tf_op jit(solution)/shard_map/all_to_all | solution.py:340
  59.8 1.1 copy-done
  61.0 12.8 %shard_map.97 = (bf16[4,96,1024]{2,1,0:T(8,128)(2,1)}, bf16[4,96,1024]{2,1,0:T(8,128)(2,1)}, bf16[4,96,1024]{2,1,0:T(8,128)(2,1)}, bf16[4,96,1024]{2,1,0:T(8,128)(2,1)}) custom-call(s32[4]{0:T(128)} %pad_add_fusion.places_ref, s32[8]{0:T(128)} %into_ref.1, bf16[8,128,768]{2,1,0:T(8,128)(2,1)} %copy-done, bf16[1024,1024]{1,0:T(8,128)(2,1)} %shard_map.96.total_hbm, ...), custom_call_target="tpu_custom_call" | custom-call | flops 4831838208 | bytes 16777216 | tf_op jit(solution)/shard_map/pallas_call | solution.py:375
  74.4 2.0 %collective-permute-done.7 = bf16[4,96,1024]{2,1,0:T(8,128)(2,1)S(1)} collective-permute-done((bf16[4,96,1024]{2,1,0:T(8,128)(2,1)}, bf16[4,96,1024]{2,1,0:T(8,128)(2,1)S(1)}, u32[]{:S(2)}, u32[]{:S(2)}) %collective-permute-start.7) | collective-permute-done | bytes 786464 | tf_op jit(solution)/shard_map/ppermute | solution.py:23
  76.4 1.4 %add_convert_fusion.1 = (bf16[2,96,1024]{2,1,0:T(8,128)(2,1)S(1)}, bf16[2,96,1024]{2,1,0:T(8,128)(2,1)S(1)}) fusion(bf16[4,96,1024]{2,1,0:T(8,128)(2,1)S(1)} %collective-permute-done.7, bf16[4,96,1024]{2,1,0:T(8,128)(2,1)} %get-tuple-element.14), kind=kLoop, calls=%fused_computation.8 | loop fusion | flops 1572864 | bytes 2359296 | tf_op jit(solution)/shard_map/convert_element_type | solution.py:256
  77.8 1.5 %collective-permute-start.10 = (bf16[2,96,1024]{2,1,0:T(8,128)(2,1)S(1)}, bf16[2,96,1024]{2,1,0:T(8,128)(2,1)S(1)}, u32[]{:S(2)}, u32[]{:S(2)}) collective-permute-start(bf16[2,96,1024]{2,1,0:T(8,128)(2,1)S(1)} %get-tuple-element.18), channel_id=1, source_target_pairs={{0,1},{1,0},{2,3},{3,2},{4,5},{5,4},{6,7},{7,6},{8,24},{9,25},{10,... | collective-permute-start | bytes 1179656 | tf_op jit(solution)/shard_map/ppermute | solution.py:281
  79.9 5.7 %collective-permute-done.10 = bf16[2,96,1024]{2,1,0:T(8,128)(2,1)S(1)} collective-permute-done((bf16[2,96,1024]{2,1,0:T(8,128)(2,1)S(1)}, bf16[2,96,1024]{2,1,0:T(8,128)(2,1)S(1)}, u32[]{:S(2)}, u32[]{:S(2)}) %collective-permute-start.10) | collective-permute-done | bytes 393248 | tf_op jit(solution)/shard_map/ppermute | solution.py:281
  85.7 4.2 %collective-permute-done.8 = bf16[2,96,1024]{2,1,0:T(8,128)(2,1)S(1)} collective-permute-done((bf16[2,96,1024]{2,1,0:T(8,128)(2,1)S(1)}, bf16[2,96,1024]{2,1,0:T(8,128)(2,1)S(1)}, u32[]{:S(2)}, u32[]{:S(2)}) %collective-permute-start.8) | collective-permute-done | bytes 393248 | tf_op jit(solution)/shard_map/ppermute | solution.py:281
  90.3 1.6 %collective-permute-start.11 = (bf16[2,96,512]{2,1,0:T(8,128)(2,1)S(1)}, bf16[2,96,512]{2,1,0:T(8,128)(2,1)S(1)}, u32[]{:S(2)}, u32[]{:S(2)}) collective-permute-start(bf16[2,96,512]{2,1,0:T(8,128)(2,1)S(1)} %constant_dynamic-slice_fusion), channel_id=1, source_target_pairs={{0,16},{1,17},{2,18},{3,19},{4,20},{5,21},{6,22},{7,23},{8,9},{9,8... | collective-permute-start | bytes 589832 | tf_op jit(solution)/shard_map/ppermute | solution.py:281
  92.5 3.6 %collective-permute-done.11 = bf16[2,96,512]{2,1,0:T(8,128)(2,1)S(1)} collective-permute-done((bf16[2,96,512]{2,1,0:T(8,128)(2,1)S(1)}, bf16[2,96,512]{2,1,0:T(8,128)(2,1)S(1)}, u32[]{:S(2)}, u32[]{:S(2)}) %collective-permute-start.11) | collective-permute-done | bytes 196640 | tf_op jit(solution)/shard_map/ppermute | solution.py:281
  96.1 2.0 %collective-permute-done.9 = bf16[2,96,512]{2,1,0:T(8,128)(2,1)S(1)} collective-permute-done((bf16[2,96,512]{2,1,0:T(8,128)(2,1)S(1)}, bf16[2,96,512]{2,1,0:T(8,128)(2,1)S(1)}, u32[]{:S(2)}, u32[]{:S(2)}) %collective-permute-start.9) | collective-permute-done | bytes 196640 | tf_op jit(solution)/shard_map/ppermute | solution.py:281
  98.5 4.2 %collective-permute-start.13 = (bf16[96,512]{1,0:T(8,128)(2,1)S(1)}, bf16[96,512]{1,0:T(8,128)(2,1)S(1)}, u32[]{:S(2)}, u32[]{:S(2)}) collective-permute-start(bf16[96,512]{1,0:T(8,128)(2,1)S(1)} %get-tuple-element.31), channel_id=1, source_target_pairs={{0,4},{1,5},{2,6},{3,7},{4,0},{5,1},{6,2},{7,3},{8,12},{9,13},{10,... | collective-permute-start | bytes 294920 | tf_op jit(solution)/shard_map/ppermute | solution.py:23
  102.8 0.8 collective-permute-done.12
  103.6 4.4 %collective-permute-done.13 = bf16[96,512]{1,0:T(8,128)(2,1)S(1)} collective-permute-done((bf16[96,512]{1,0:T(8,128)(2,1)S(1)}, bf16[96,512]{1,0:T(8,128)(2,1)S(1)}, u32[]{:S(2)}, u32[]{:S(2)}) %collective-permute-start.13) | collective-permute-done | bytes 98336 | tf_op jit(solution)/shard_map/ppermute | solution.py:23
  108.0 1.2 %collective-permute-done.14 = bf16[96,512]{1,0:T(8,128)(2,1)S(1)} collective-permute-done((bf16[96,512]{1,0:T(8,128)(2,1)S(1)}, bf16[96,512]{1,0:T(8,128)(2,1)S(1)}, u32[]{:S(2)}, u32[]{:S(2)}) %collective-permute-start.14) | collective-permute-done | bytes 98336 | tf_op jit(solution)/shard_map/ppermute | solution.py:23
  109.3 1.6 %collective-permute-start.15 = (bf16[96,512]{1,0:T(8,128)(2,1)S(1)}, bf16[96,512]{1,0:T(8,128)(2,1)S(1)}, u32[]{:S(2)}, u32[]{:S(2)}) collective-permute-start(bf16[96,512]{1,0:T(8,128)(2,1)S(1)} %fusion.5), channel_id=1, source_target_pairs={{0,16},{8,24},{16,0},{24,8},{1,17},{9,25},{17,1},{25,9},{2,18},{10... | collective-permute-start | bytes 294920 | tf_op jit(solution)/shard_map/ppermute | solution.py:23
  110.9 3.1 %collective-permute-done.15 = bf16[96,512]{1,0:T(8,128)(2,1)S(1)} collective-permute-done((bf16[96,512]{1,0:T(8,128)(2,1)S(1)}, bf16[96,512]{1,0:T(8,128)(2,1)S(1)}, u32[]{:S(2)}, u32[]{:S(2)}) %collective-permute-start.15) | collective-permute-done | bytes 98336 | tf_op jit(solution)/shard_map/ppermute | solution.py:23
  114.1 1.4 %collective-permute-done.16 = bf16[96,1024]{1,0:T(8,128)(2,1)S(1)} collective-permute-done((bf16[96,1024]{1,0:T(8,128)(2,1)S(1)}, bf16[96,1024]{1,0:T(8,128)(2,1)S(1)}, u32[]{:S(2)}, u32[]{:S(2)}) %collective-permute-start.16) | collective-permute-done | bytes 196640 | tf_op jit(solution)/shard_map/ppermute | solution.py:23
  115.5 1.0 select_convert_fusion
  (35 shorter events, 4.1 us)
Async XLA Ops:
  1.6 9.3 %collective-permute-start = (bf16[2,96,512]{2,1,0:T(8,128)(2,1)S(1)}, bf16[2,96,512]{2,1,0:T(8,128)(2,1)S(1)}, u32[]{:S(2)}, u32[]{:S(2)}) collective-permute-start(bf16[2,96,512]{2,1,0:T(8,128)(2,1)S(1)} %pad_maximum_fusion.3), channel_id=1, source_target_pairs={{8,9},{9,8},{10,11},{11,10},{12,13},{13,12},{14,15},{15,14},{24,25... | collective-permute-start | bytes 589832 | tf_op jit(solution)/shard_map/ppermute | solution.py:31
  2.3 12.6 %collective-permute-start.1 = (bf16[2,96,512]{2,1,0:T(8,128)(2,1)S(1)}, bf16[2,96,512]{2,1,0:T(8,128)(2,1)S(1)}, u32[]{:S(2)}, u32[]{:S(2)}) collective-permute-start(bf16[2,96,512]{2,1,0:T(8,128)(2,1)S(1)} %pad_maximum_fusion.3), channel_id=1, source_target_pairs={{0,4},{1,5},{2,6},{3,7},{4,0},{5,1},{6,2},{7,3},{8,13},{9,12},{10,... | collective-permute-start | bytes 589832 | tf_op jit(solution)/shard_map/ppermute | solution.py:31
  15.0 11.9 %collective-permute-start.2 = (bf16[2,2,96,512]{3,2,1,0:T(8,128)(2,1)S(1)}, bf16[2,2,96,512]{3,2,1,0:T(8,128)(2,1)S(1)}, u32[]{:S(2)}, u32[]{:S(2)}) collective-permute-start(bf16[2,2,96,512]{3,2,1,0:T(8,128)(2,1)S(1)} %pad_maximum_fusion.2), channel_id=1, source_target_pairs={{0,2},{1,3},{2,0},{3,1},{4,6},{5,7},{6,4},{7,5},{8,10},{9,11},{10,... | collective-permute-start | bytes 1179656 | tf_op jit(solution)/shard_map/ppermute | solution.py:23
  17.4 42.4 %all-to-all-start = ((bf16[8,128,768]{2,1,0:T(8,128)(2,1)}), bf16[8,128,768]{2,1,0:T(8,128)(2,1)S(1)}, u32[]{:S(2)}, u32[]{:S(2)}) async-start(bf16[8,128,768]{2,1,0:T(8,128)(2,1)} %bitcast.6), calls=%async_computation | async-start | bytes 3145728 | tf_op jit(solution)/shard_map/all_to_all | solution.py:340
  27.0 19.9 %collective-permute-start.3 = (bf16[2,4,96,512]{3,2,1,0:T(8,128)(2,1)S(1)}, bf16[2,4,96,512]{3,2,1,0:T(8,128)(2,1)S(1)}, u32[]{:S(2)}, u32[]{:S(2)}) collective-permute-start(bf16[2,4,96,512]{3,2,1,0:T(8,128)(2,1)S(1)} %bitcast.37), channel_id=1, source_target_pairs={{0,16},{8,24},{16,0},{24,8},{1,17},{9,25},{17,1},{25,9},{2,18},{10... | collective-permute-start | bytes 2359304 | tf_op jit(solution)/shard_map/ppermute | solution.py:23
  47.3 2.8 %copy-start.3 = (bf16[4,96,1024]{2,1,0:T(8,128)(2,1)}, bf16[4,96,1024]{2,1,0:T(8,128)(2,1)S(1)}, u32[]{:S(2)}) copy-start(bf16[4,96,1024]{2,1,0:T(8,128)(2,1)S(1)} %get-tuple-element.21.refs_0_) | copy-start | bytes 2359300
  47.3 7.5 %copy-start.2 = (bf16[4,96,1024]{2,1,0:T(8,128)(2,1)}, bf16[4,96,1024]{2,1,0:T(8,128)(2,1)S(1)}, u32[]{:S(2)}) copy-start(bf16[4,96,1024]{2,1,0:T(8,128)(2,1)S(1)} %get-tuple-element.20.refs_0_) | copy-start | bytes 2359300
  47.3 2.8 %collective-permute-start.4 = (bf16[4,96,1024]{2,1,0:T(8,128)(2,1)S(1)}, bf16[4,96,1024]{2,1,0:T(8,128)(2,1)}, u32[]{:S(2)}, u32[]{:S(2)}) collective-permute-start(bf16[4,96,1024]{2,1,0:T(8,128)(2,1)S(1)} %get-tuple-element.21.refs_0_), channel_id=1, source_target_pairs={{0,8},{8,0},{16,24},{24,16},{1,9},{9,1},{17,25},{25,17},{2,10},{10... | collective-permute-start | bytes 2359304 | tf_op jit(solution)/shard_map/ppermute | solution.py:23
  48.0 6.7 %collective-permute-start.5 = (bf16[4,96,1024]{2,1,0:T(8,128)(2,1)S(1)}, bf16[4,96,1024]{2,1,0:T(8,128)(2,1)}, u32[]{:S(2)}, u32[]{:S(2)}) collective-permute-start(bf16[4,96,1024]{2,1,0:T(8,128)(2,1)S(1)} %get-tuple-element.20.refs_0_), channel_id=1, source_target_pairs={{0,8},{8,0},{16,24},{24,16},{1,9},{9,1},{17,25},{25,17},{2,10},{10... | collective-permute-start | bytes 2359304 | tf_op jit(solution)/shard_map/ppermute | solution.py:23
  59.8 1.1 copy-start
  73.8 16.1 %copy-start.1 = (bf16[4,96,1024]{2,1,0:T(8,128)(2,1)S(1)}, bf16[4,96,1024]{2,1,0:T(8,128)(2,1)}, u32[]{:S(2)}) copy-start(bf16[4,96,1024]{2,1,0:T(8,128)(2,1)} %get-tuple-element.12) | copy-start | bytes 2359300
  73.8 2.6 %collective-permute-start.7 = (bf16[4,96,1024]{2,1,0:T(8,128)(2,1)}, bf16[4,96,1024]{2,1,0:T(8,128)(2,1)S(1)}, u32[]{:S(2)}, u32[]{:S(2)}) collective-permute-start(bf16[4,96,1024]{2,1,0:T(8,128)(2,1)} %get-tuple-element.15), channel_id=1, source_target_pairs={{0,8},{8,0},{16,24},{24,16},{1,9},{9,1},{17,25},{25,17},{2,10},{10... | collective-permute-start | bytes 2359304 | tf_op jit(solution)/shard_map/ppermute | solution.py:23
  73.9 6.0 %collective-permute-start.6 = (bf16[4,96,1024]{2,1,0:T(8,128)(2,1)}, bf16[4,96,1024]{2,1,0:T(8,128)(2,1)S(1)}, u32[]{:S(2)}, u32[]{:S(2)}) collective-permute-start(bf16[4,96,1024]{2,1,0:T(8,128)(2,1)} %get-tuple-element.13), channel_id=1, source_target_pairs={{0,8},{8,0},{16,24},{24,16},{1,9},{9,1},{17,25},{25,17},{2,10},{10... | collective-permute-start | bytes 2359304 | tf_op jit(solution)/shard_map/ppermute | solution.py:23
  77.8 7.8 %collective-permute-start.10 = (bf16[2,96,1024]{2,1,0:T(8,128)(2,1)S(1)}, bf16[2,96,1024]{2,1,0:T(8,128)(2,1)S(1)}, u32[]{:S(2)}, u32[]{:S(2)}) collective-permute-start(bf16[2,96,1024]{2,1,0:T(8,128)(2,1)S(1)} %get-tuple-element.18), channel_id=1, source_target_pairs={{0,1},{1,0},{2,3},{3,2},{4,5},{5,4},{6,7},{7,6},{8,24},{9,25},{10,... | collective-permute-start | bytes 1179656 | tf_op jit(solution)/shard_map/ppermute | solution.py:281
  79.3 10.5 %collective-permute-start.8 = (bf16[2,96,1024]{2,1,0:T(8,128)(2,1)S(1)}, bf16[2,96,1024]{2,1,0:T(8,128)(2,1)S(1)}, u32[]{:S(2)}, u32[]{:S(2)}) collective-permute-start(bf16[2,96,1024]{2,1,0:T(8,128)(2,1)S(1)} %get-tuple-element.19), channel_id=1, source_target_pairs={{0,1},{1,0},{2,3},{3,2},{4,5},{5,4},{6,7},{7,6},{8,24},{9,25},{10,... | collective-permute-start | bytes 1179656 | tf_op jit(solution)/shard_map/ppermute | solution.py:281
  90.3 5.7 %collective-permute-start.11 = (bf16[2,96,512]{2,1,0:T(8,128)(2,1)S(1)}, bf16[2,96,512]{2,1,0:T(8,128)(2,1)S(1)}, u32[]{:S(2)}, u32[]{:S(2)}) collective-permute-start(bf16[2,96,512]{2,1,0:T(8,128)(2,1)S(1)} %constant_dynamic-slice_fusion), channel_id=1, source_target_pairs={{0,16},{1,17},{2,18},{3,19},{4,20},{5,21},{6,22},{7,23},{8,9},{9,8... | collective-permute-start | bytes 589832 | tf_op jit(solution)/shard_map/ppermute | solution.py:281
  91.9 6.2 %collective-permute-start.9 = (bf16[2,96,512]{2,1,0:T(8,128)(2,1)S(1)}, bf16[2,96,512]{2,1,0:T(8,128)(2,1)S(1)}, u32[]{:S(2)}, u32[]{:S(2)}) collective-permute-start(bf16[2,96,512]{2,1,0:T(8,128)(2,1)S(1)} %constant_dynamic-slice_fusion.1), channel_id=1, source_target_pairs={{0,16},{1,17},{2,18},{3,19},{4,20},{5,21},{6,22},{7,23},{8,9},{9,8... | collective-permute-start | bytes 589832 | tf_op jit(solution)/shard_map/ppermute | solution.py:281
  98.4 5.2 %collective-permute-start.12 = (bf16[96,512]{1,0:T(8,128)(2,1)S(1)}, bf16[96,512]{1,0:T(8,128)(2,1)S(1)}, u32[]{:S(2)}, u32[]{:S(2)}) collective-permute-start(bf16[96,512]{1,0:T(8,128)(2,1)S(1)} %get-tuple-element.30), channel_id=1, source_target_pairs={{0,2},{1,3},{2,0},{3,1},{4,6},{5,7},{6,4},{7,5},{8,10},{9,11},{10,... | collective-permute-start | bytes 294920 | tf_op jit(solution)/shard_map/ppermute | solution.py:23
  98.5 9.5 %collective-permute-start.13 = (bf16[96,512]{1,0:T(8,128)(2,1)S(1)}, bf16[96,512]{1,0:T(8,128)(2,1)S(1)}, u32[]{:S(2)}, u32[]{:S(2)}) collective-permute-start(bf16[96,512]{1,0:T(8,128)(2,1)S(1)} %get-tuple-element.31), channel_id=1, source_target_pairs={{0,4},{1,5},{2,6},{3,7},{4,0},{5,1},{6,2},{7,3},{8,12},{9,13},{10,... | collective-permute-start | bytes 294920 | tf_op jit(solution)/shard_map/ppermute | solution.py:23
  102.7 6.5 %collective-permute-start.14 = (bf16[96,512]{1,0:T(8,128)(2,1)S(1)}, bf16[96,512]{1,0:T(8,128)(2,1)S(1)}, u32[]{:S(2)}, u32[]{:S(2)}) collective-permute-start(bf16[96,512]{1,0:T(8,128)(2,1)S(1)} %get-tuple-element.32), channel_id=1, source_target_pairs={{0,6},{1,7},{2,4},{3,5},{4,2},{5,3},{6,0},{7,1},{8,14},{9,15},{10,... | collective-permute-start | bytes 294920 | tf_op jit(solution)/shard_map/ppermute | solution.py:23
  109.3 4.7 %collective-permute-start.15 = (bf16[96,512]{1,0:T(8,128)(2,1)S(1)}, bf16[96,512]{1,0:T(8,128)(2,1)S(1)}, u32[]{:S(2)}, u32[]{:S(2)}) collective-permute-start(bf16[96,512]{1,0:T(8,128)(2,1)S(1)} %fusion.5), channel_id=1, source_target_pairs={{0,16},{8,24},{16,0},{24,8},{1,17},{9,25},{17,1},{25,9},{2,18},{10... | collective-permute-start | bytes 294920 | tf_op jit(solution)/shard_map/ppermute | solution.py:23
  114.0 1.5 %collective-permute-start.16 = (bf16[96,1024]{1,0:T(8,128)(2,1)S(1)}, bf16[96,1024]{1,0:T(8,128)(2,1)S(1)}, u32[]{:S(2)}, u32[]{:S(2)}) collective-permute-start(bf16[96,1024]{1,0:T(8,128)(2,1)S(1)} %pad_maximum_fusion.4), channel_id=1, source_target_pairs={{0,8},{8,0},{16,24},{24,16},{1,9},{9,1},{17,25},{25,17},{2,10},{10... | collective-permute-start | bytes 589832 | tf_op jit(solution)/shard_map/ppermute | solution.py:23

commit v21 on v19

--- a/solution.py
+++ b/solution.py
@@ -184,8 +184,8 @@
         cotangents[index].wait()
         for row in range(0, chunk, 16):
             at = slice(index * chunk + row, index * chunk + row + 16)
-            for begin in range(0, hidden, span):
-                columns = slice(begin, begin + span)
+            for begin in range(0, hidden, 256):
+                columns = slice(begin, begin + 256)
                 value = values[index % 2, row : row + 16, columns] + total[at, columns].astype(F32)
                 square = value * value
                 bend = jnp.tanh(value * (square * (SCALE * CUBIC) + SCALE))

time: 117 us -> 117 us (level)
  no operation moved by 1% of the time
where the time goes in v21:
time: 117 us; the launch traced here: 116 us
  waiting for transfers between devices  61 us (52%)
  starting transfers between devices  26.1 us (22%)
  Pallas kernels  22 us (19%)
  other arithmetic  4.3 us (4%)
  local copies, waits for them, and re-layouts  2.15 us (2%)
    ppermute x11, waiting for transfers between devices, swap(): lax.ppermute(value, axis, [(index, index ^ step) for index in range(size)])  36.5 us
    ppermute x4, waiting for transfers between devices, turn_swap(): return lax.ppermute(value, ('rep', 'dom'), pairs)  15.6 us
    pallas_call x1, Pallas kernels, shards(): call(functools.partial(layer_kernel, sources, tiled), out_shapes, [SMEM,...  12.8 us
    ppermute x11, starting transfers between devices, swap(): lax.ppermute(value, axis, [(index, index ^ step) for index in range(size)])  11.5 us
    all_to_all x1, starting transfers between devices, shards(): lax.all_to_all(slots.reshape(dom_size, block, width), 'dom', split_axis=0...  5.58 us
    all_to_all x1, waiting for transfers between devices, shards(): lax.all_to_all(slots.reshape(dom_size, block, width), 'dom', split_axis=0...  5.09 us
    ppermute x2, starting transfers between devices, cross(): lax.ppermute(value, ('rep', 'dom'), [(source, target) for source, target...  4.77 us
    pallas_call x1, Pallas kernels, shards(): call(self_kernel, jax.ShapeDtypeStruct((rows, hidden), BF16), [SMEM] + [H...  4.67 us
  transfers between devices with their start and end apart: 18, of which 15 were waited for; matrix products, arithmetic and copies ran while one was open for 2% of the time, Pallas kernels for 8%

profile of v21, /device:TPU:0, one launch (start us, length us, event | category | flops | bytes accessed | tf_op | source)
XLA Modules:
  0.0 116.5 jit_solution(3867819766692818589)
XLA Ops:
  0.6 1.0 dynamic-slice_bitcast_fusion
  1.6 0.7 collective-permute-start
  2.3 4.1 %collective-permute-start.1 = (bf16[2,96,512]{2,1,0:T(8,128)(2,1)S(1)}, bf16[2,96,512]{2,1,0:T(8,128)(2,1)S(1)}, u32[]{:S(2)}, u32[]{:S(2)}) collective-permute-start(bf16[2,96,512]{2,1,0:T(8,128)(2,1)S(1)} %pad_maximum_fusion.3), channel_id=1, source_target_pairs={{0,4},{1,5},{2,6},{3,7},{4,0},{5,1},{6,2},{7,3},{8,13},{9,12},{10,... | collective-permute-start | bytes 589832 | tf_op jit(solution)/shard_map/ppermute | solution.py:31
  6.4 4.6 %shard_map.95 = bf16[1024,768]{1,0:T(8,128)(2,1)} custom-call(s32[32]{0:T(128)} %src_hbm.1, s32[32]{0:T(128)} %peer_hbm.1, bf16[32,128,128]{2,1,0:T(8,128)(2,1)} %tiles_hbm.1, bf16[1024,768]{1,0:T(8,128)(2,1)} %features_hbm.5), custom_call_target="tpu_custom_call" | custom-call | flops 1610612736 | bytes 4194304 | tf_op jit(solution)/shard_map/pallas_call | solution.py:312
  11.0 3.9 %collective-permute-done.1 = bf16[2,96,512]{2,1,0:T(8,128)(2,1)S(1)} collective-permute-done((bf16[2,96,512]{2,1,0:T(8,128)(2,1)S(1)}, bf16[2,96,512]{2,1,0:T(8,128)(2,1)S(1)}, u32[]{:S(2)}, u32[]{:S(2)}) %collective-permute-start.1) | collective-permute-done | bytes 196640 | tf_op jit(solution)/shard_map/ppermute | solution.py:31
  15.0 2.5 %collective-permute-start.2 = (bf16[2,2,96,512]{3,2,1,0:T(8,128)(2,1)S(1)}, bf16[2,2,96,512]{3,2,1,0:T(8,128)(2,1)S(1)}, u32[]{:S(2)}, u32[]{:S(2)}) collective-permute-start(bf16[2,2,96,512]{3,2,1,0:T(8,128)(2,1)S(1)} %pad_maximum_fusion.2), channel_id=1, source_target_pairs={{0,2},{1,3},{2,0},{3,1},{4,6},{5,7},{6,4},{7,5},{8,10},{9,11},{10,... | collective-permute-start | bytes 1179656 | tf_op jit(solution)/shard_map/ppermute | solution.py:23
  17.4 5.6 %all-to-all-start = ((bf16[8,128,768]{2,1,0:T(8,128)(2,1)}), bf16[8,128,768]{2,1,0:T(8,128)(2,1)S(1)}, u32[]{:S(2)}, u32[]{:S(2)}) async-start(bf16[8,128,768]{2,1,0:T(8,128)(2,1)} %bitcast.6), calls=%async_computation | async-start | bytes 3145728 | tf_op jit(solution)/shard_map/all_to_all | solution.py:337
  23.0 3.8 %collective-permute-done.2 = bf16[2,2,96,512]{3,2,1,0:T(8,128)(2,1)S(1)} collective-permute-done((bf16[2,2,96,512]{3,2,1,0:T(8,128)(2,1)S(1)}, bf16[2,2,96,512]{3,2,1,0:T(8,128)(2,1)S(1)}, u32[]{:S(2)}, u32[]{:S(2)}) %collective-permute-start.2) | collective-permute-done | bytes 393248 | tf_op jit(solution)/shard_map/ppermute | solution.py:23
  27.0 1.6 %collective-permute-start.3 = (bf16[2,4,96,512]{3,2,1,0:T(8,128)(2,1)S(1)}, bf16[2,4,96,512]{3,2,1,0:T(8,128)(2,1)S(1)}, u32[]{:S(2)}, u32[]{:S(2)}) collective-permute-start(bf16[2,4,96,512]{3,2,1,0:T(8,128)(2,1)S(1)} %bitcast.37), channel_id=1, source_target_pairs={{0,16},{8,24},{16,0},{24,8},{1,17},{9,25},{17,1},{25,9},{2,18},{10... | collective-permute-start | bytes 2359304 | tf_op jit(solution)/shard_map/ppermute | solution.py:23
  28.6 18.4 %collective-permute-done.3 = bf16[2,4,96,512]{3,2,1,0:T(8,128)(2,1)S(1)} collective-permute-done((bf16[2,4,96,512]{3,2,1,0:T(8,128)(2,1)S(1)}, bf16[2,4,96,512]{3,2,1,0:T(8,128)(2,1)S(1)}, u32[]{:S(2)}, u32[]{:S(2)}) %collective-permute-start.3) | collective-permute-done | bytes 786464 | tf_op jit(solution)/shard_map/ppermute | solution.py:23
  47.3 0.7 collective-permute-start.4
  48.7 1.4 %collective-permute-done.4.refs_1_ = bf16[4,96,1024]{2,1,0:T(8,128)(2,1)} collective-permute-done((bf16[4,96,1024]{2,1,0:T(8,128)(2,1)S(1)}, bf16[4,96,1024]{2,1,0:T(8,128)(2,1)}, u32[]{:S(2)}, u32[]{:S(2)}) %collective-permute-start.4) | collective-permute-done | bytes 786464 | tf_op jit(solution)/shard_map/ppermute | solution.py:23
  50.0 4.7 %shard_map.96.total_hbm = bf16[1024,1024]{1,0:T(8,128)(2,1)} custom-call(s32[1]{0:T(128)} %bitcast.1.flip_ref, bf16[1024,768]{1,0:T(8,128)(2,1)} %features_hbm.5, bf16[4,96,1024]{2,1,0:T(8,128)(2,1)} %copy-done.3, bf16[4,96,1024]{2,1,0:T(8,128)(2,1)} %collective-permute-done.4.refs_1_), custom_call_target="tpu_custom_call" | custom-call | flops 1610612736 | bytes 7340032 | tf_op jit(solution)/shard_map/pallas_call | solution.py:347
  54.7 5.1 %all-to-all-done.slots_hbm = bf16[8,128,768]{2,1,0:T(8,128)(2,1)S(1)} async-done(((bf16[8,128,768]{2,1,0:T(8,128)(2,1)}), bf16[8,128,768]{2,1,0:T(8,128)(2,1)S(1)}, u32[]{:S(2)}, u32[]{:S(2)}) %all-to-all-start) | async-done | bytes 1572896 | tf_op jit(solution)/shard_map/all_to_all | solution.py:337
  59.8 1.1 copy-done
  61.0 12.8 %shard_map.97 = (bf16[4,96,1024]{2,1,0:T(8,128)(2,1)}, bf16[4,96,1024]{2,1,0:T(8,128)(2,1)}, bf16[4,96,1024]{2,1,0:T(8,128)(2,1)}, bf16[4,96,1024]{2,1,0:T(8,128)(2,1)}) custom-call(s32[4]{0:T(128)} %pad_add_fusion.places_ref, s32[8]{0:T(128)} %into_ref.1, bf16[8,128,768]{2,1,0:T(8,128)(2,1)} %copy-done, bf16[1024,1024]{1,0:T(8,128)(2,1)} %shard_map.96.total_hbm, ...), custom_call_target="tpu_custom_call" | custom-call | flops 4831838208 | bytes 16777216 | tf_op jit(solution)/shard_map/pallas_call | solution.py:372
  74.4 2.0 %collective-permute-done.7 = bf16[4,96,1024]{2,1,0:T(8,128)(2,1)S(1)} collective-permute-done((bf16[4,96,1024]{2,1,0:T(8,128)(2,1)}, bf16[4,96,1024]{2,1,0:T(8,128)(2,1)S(1)}, u32[]{:S(2)}, u32[]{:S(2)}) %collective-permute-start.7) | collective-permute-done | bytes 786464 | tf_op jit(solution)/shard_map/ppermute | solution.py:23
  76.4 1.4 %add_convert_fusion.1 = (bf16[2,96,1024]{2,1,0:T(8,128)(2,1)S(1)}, bf16[2,96,1024]{2,1,0:T(8,128)(2,1)S(1)}) fusion(bf16[4,96,1024]{2,1,0:T(8,128)(2,1)S(1)} %collective-permute-done.7, bf16[4,96,1024]{2,1,0:T(8,128)(2,1)} %get-tuple-element.14), kind=kLoop, calls=%fused_computation.8 | loop fusion | flops 1572864 | bytes 2359296 | tf_op jit(solution)/shard_map/convert_element_type | solution.py:253
  77.8 1.5 %collective-permute-start.10 = (bf16[2,96,1024]{2,1,0:T(8,128)(2,1)S(1)}, bf16[2,96,1024]{2,1,0:T(8,128)(2,1)S(1)}, u32[]{:S(2)}, u32[]{:S(2)}) collective-permute-start(bf16[2,96,1024]{2,1,0:T(8,128)(2,1)S(1)} %get-tuple-element.18), channel_id=1, source_target_pairs={{0,1},{1,0},{2,3},{3,2},{4,5},{5,4},{6,7},{7,6},{8,24},{9,25},{10,... | collective-permute-start | bytes 1179656 | tf_op jit(solution)/shard_map/ppermute | solution.py:278
  79.9 5.7 %collective-permute-done.10 = bf16[2,96,1024]{2,1,0:T(8,128)(2,1)S(1)} collective-permute-done((bf16[2,96,1024]{2,1,0:T(8,128)(2,1)S(1)}, bf16[2,96,1024]{2,1,0:T(8,128)(2,1)S(1)}, u32[]{:S(2)}, u32[]{:S(2)}) %collective-permute-start.10) | collective-permute-done | bytes 393248 | tf_op jit(solution)/shard_map/ppermute | solution.py:278
  85.6 4.2 %collective-permute-done.8 = bf16[2,96,1024]{2,1,0:T(8,128)(2,1)S(1)} collective-permute-done((bf16[2,96,1024]{2,1,0:T(8,128)(2,1)S(1)}, bf16[2,96,1024]{2,1,0:T(8,128)(2,1)S(1)}, u32[]{:S(2)}, u32[]{:S(2)}) %collective-permute-start.8) | collective-permute-done | bytes 393248 | tf_op jit(solution)/shard_map/ppermute | solution.py:278
  90.3 1.6 %collective-permute-start.11 = (bf16[2,96,512]{2,1,0:T(8,128)(2,1)S(1)}, bf16[2,96,512]{2,1,0:T(8,128)(2,1)S(1)}, u32[]{:S(2)}, u32[]{:S(2)}) collective-permute-start(bf16[2,96,512]{2,1,0:T(8,128)(2,1)S(1)} %constant_dynamic-slice_fusion), channel_id=1, source_target_pairs={{0,16},{1,17},{2,18},{3,19},{4,20},{5,21},{6,22},{7,23},{8,9},{9,8... | collective-permute-start | bytes 589832 | tf_op jit(solution)/shard_map/ppermute | solution.py:278
  92.5 3.6 %collective-permute-done.11 = bf16[2,96,512]{2,1,0:T(8,128)(2,1)S(1)} collective-permute-done((bf16[2,96,512]{2,1,0:T(8,128)(2,1)S(1)}, bf16[2,96,512]{2,1,0:T(8,128)(2,1)S(1)}, u32[]{:S(2)}, u32[]{:S(2)}) %collective-permute-start.11) | collective-permute-done | bytes 196640 | tf_op jit(solution)/shard_map/ppermute | solution.py:278
  96.1 2.0 %collective-permute-done.9 = bf16[2,96,512]{2,1,0:T(8,128)(2,1)S(1)} collective-permute-done((bf16[2,96,512]{2,1,0:T(8,128)(2,1)S(1)}, bf16[2,96,512]{2,1,0:T(8,128)(2,1)S(1)}, u32[]{:S(2)}, u32[]{:S(2)}) %collective-permute-start.9) | collective-permute-done | bytes 196640 | tf_op jit(solution)/shard_map/ppermute | solution.py:278
  98.4 4.2 %collective-permute-start.13 = (bf16[96,512]{1,0:T(8,128)(2,1)S(1)}, bf16[96,512]{1,0:T(8,128)(2,1)S(1)}, u32[]{:S(2)}, u32[]{:S(2)}) collective-permute-start(bf16[96,512]{1,0:T(8,128)(2,1)S(1)} %get-tuple-element.31), channel_id=1, source_target_pairs={{0,4},{1,5},{2,6},{3,7},{4,0},{5,1},{6,2},{7,3},{8,12},{9,13},{10,... | collective-permute-start | bytes 294920 | tf_op jit(solution)/shard_map/ppermute | solution.py:23
  102.8 0.8 collective-permute-done.12
  103.6 4.4 %collective-permute-done.13 = bf16[96,512]{1,0:T(8,128)(2,1)S(1)} collective-permute-done((bf16[96,512]{1,0:T(8,128)(2,1)S(1)}, bf16[96,512]{1,0:T(8,128)(2,1)S(1)}, u32[]{:S(2)}, u32[]{:S(2)}) %collective-permute-start.13) | collective-permute-done | bytes 98336 | tf_op jit(solution)/shard_map/ppermute | solution.py:23
  108.0 1.2 %collective-permute-done.14 = bf16[96,512]{1,0:T(8,128)(2,1)S(1)} collective-permute-done((bf16[96,512]{1,0:T(8,128)(2,1)S(1)}, bf16[96,512]{1,0:T(8,128)(2,1)S(1)}, u32[]{:S(2)}, u32[]{:S(2)}) %collective-permute-start.14) | collective-permute-done | bytes 98336 | tf_op jit(solution)/shard_map/ppermute | solution.py:23
  109.3 1.6 %collective-permute-start.15 = (bf16[96,512]{1,0:T(8,128)(2,1)S(1)}, bf16[96,512]{1,0:T(8,128)(2,1)S(1)}, u32[]{:S(2)}, u32[]{:S(2)}) collective-permute-start(bf16[96,512]{1,0:T(8,128)(2,1)S(1)} %fusion.5), channel_id=1, source_target_pairs={{0,16},{8,24},{16,0},{24,8},{1,17},{9,25},{17,1},{25,9},{2,18},{10... | collective-permute-start | bytes 294920 | tf_op jit(solution)/shard_map/ppermute | solution.py:23
  110.8 3.1 %collective-permute-done.15 = bf16[96,512]{1,0:T(8,128)(2,1)S(1)} collective-permute-done((bf16[96,512]{1,0:T(8,128)(2,1)S(1)}, bf16[96,512]{1,0:T(8,128)(2,1)S(1)}, u32[]{:S(2)}, u32[]{:S(2)}) %collective-permute-start.15) | collective-permute-done | bytes 98336 | tf_op jit(solution)/shard_map/ppermute | solution.py:23
  114.1 1.4 %collective-permute-done.16 = bf16[96,1024]{1,0:T(8,128)(2,1)S(1)} collective-permute-done((bf16[96,1024]{1,0:T(8,128)(2,1)S(1)}, bf16[96,1024]{1,0:T(8,128)(2,1)S(1)}, u32[]{:S(2)}, u32[]{:S(2)}) %collective-permute-start.16) | collective-permute-done | bytes 196640 | tf_op jit(solution)/shard_map/ppermute | solution.py:23
  115.5 1.0 select_convert_fusion
  (35 shorter events, 4.1 us)
Async XLA Ops:
  1.6 9.3 %collective-permute-start = (bf16[2,96,512]{2,1,0:T(8,128)(2,1)S(1)}, bf16[2,96,512]{2,1,0:T(8,128)(2,1)S(1)}, u32[]{:S(2)}, u32[]{:S(2)}) collective-permute-start(bf16[2,96,512]{2,1,0:T(8,128)(2,1)S(1)} %pad_maximum_fusion.3), channel_id=1, source_target_pairs={{8,9},{9,8},{10,11},{11,10},{12,13},{13,12},{14,15},{15,14},{24,25... | collective-permute-start | bytes 589832 | tf_op jit(solution)/shard_map/ppermute | solution.py:31
  2.3 12.6 %collective-permute-start.1 = (bf16[2,96,512]{2,1,0:T(8,128)(2,1)S(1)}, bf16[2,96,512]{2,1,0:T(8,128)(2,1)S(1)}, u32[]{:S(2)}, u32[]{:S(2)}) collective-permute-start(bf16[2,96,512]{2,1,0:T(8,128)(2,1)S(1)} %pad_maximum_fusion.3), channel_id=1, source_target_pairs={{0,4},{1,5},{2,6},{3,7},{4,0},{5,1},{6,2},{7,3},{8,13},{9,12},{10,... | collective-permute-start | bytes 589832 | tf_op jit(solution)/shard_map/ppermute | solution.py:31
  15.0 11.9 %collective-permute-start.2 = (bf16[2,2,96,512]{3,2,1,0:T(8,128)(2,1)S(1)}, bf16[2,2,96,512]{3,2,1,0:T(8,128)(2,1)S(1)}, u32[]{:S(2)}, u32[]{:S(2)}) collective-permute-start(bf16[2,2,96,512]{3,2,1,0:T(8,128)(2,1)S(1)} %pad_maximum_fusion.2), channel_id=1, source_target_pairs={{0,2},{1,3},{2,0},{3,1},{4,6},{5,7},{6,4},{7,5},{8,10},{9,11},{10,... | collective-permute-start | bytes 1179656 | tf_op jit(solution)/shard_map/ppermute | solution.py:23
  17.4 42.4 %all-to-all-start = ((bf16[8,128,768]{2,1,0:T(8,128)(2,1)}), bf16[8,128,768]{2,1,0:T(8,128)(2,1)S(1)}, u32[]{:S(2)}, u32[]{:S(2)}) async-start(bf16[8,128,768]{2,1,0:T(8,128)(2,1)} %bitcast.6), calls=%async_computation | async-start | bytes 3145728 | tf_op jit(solution)/shard_map/all_to_all | solution.py:337
  27.0 19.9 %collective-permute-start.3 = (bf16[2,4,96,512]{3,2,1,0:T(8,128)(2,1)S(1)}, bf16[2,4,96,512]{3,2,1,0:T(8,128)(2,1)S(1)}, u32[]{:S(2)}, u32[]{:S(2)}) collective-permute-start(bf16[2,4,96,512]{3,2,1,0:T(8,128)(2,1)S(1)} %bitcast.37), channel_id=1, source_target_pairs={{0,16},{8,24},{16,0},{24,8},{1,17},{9,25},{17,1},{25,9},{2,18},{10... | collective-permute-start | bytes 2359304 | tf_op jit(solution)/shard_map/ppermute | solution.py:23
  47.3 2.8 %copy-start.3 = (bf16[4,96,1024]{2,1,0:T(8,128)(2,1)}, bf16[4,96,1024]{2,1,0:T(8,128)(2,1)S(1)}, u32[]{:S(2)}) copy-start(bf16[4,96,1024]{2,1,0:T(8,128)(2,1)S(1)} %get-tuple-element.21.refs_0_) | copy-start | bytes 2359300
  47.3 7.5 %copy-start.2 = (bf16[4,96,1024]{2,1,0:T(8,128)(2,1)}, bf16[4,96,1024]{2,1,0:T(8,128)(2,1)S(1)}, u32[]{:S(2)}) copy-start(bf16[4,96,1024]{2,1,0:T(8,128)(2,1)S(1)} %get-tuple-element.20.refs_0_) | copy-start | bytes 2359300
  47.3 2.8 %collective-permute-start.4 = (bf16[4,96,1024]{2,1,0:T(8,128)(2,1)S(1)}, bf16[4,96,1024]{2,1,0:T(8,128)(2,1)}, u32[]{:S(2)}, u32[]{:S(2)}) collective-permute-start(bf16[4,96,1024]{2,1,0:T(8,128)(2,1)S(1)} %get-tuple-element.21.refs_0_), channel_id=1, source_target_pairs={{0,8},{8,0},{16,24},{24,16},{1,9},{9,1},{17,25},{25,17},{2,10},{10... | collective-permute-start | bytes 2359304 | tf_op jit(solution)/shard_map/ppermute | solution.py:23
  48.0 6.7 %collective-permute-start.5 = (bf16[4,96,1024]{2,1,0:T(8,128)(2,1)S(1)}, bf16[4,96,1024]{2,1,0:T(8,128)(2,1)}, u32[]{:S(2)}, u32[]{:S(2)}) collective-permute-start(bf16[4,96,1024]{2,1,0:T(8,128)(2,1)S(1)} %get-tuple-element.20.refs_0_), channel_id=1, source_target_pairs={{0,8},{8,0},{16,24},{24,16},{1,9},{9,1},{17,25},{25,17},{2,10},{10... | collective-permute-start | bytes 2359304 | tf_op jit(solution)/shard_map/ppermute | solution.py:23
  59.8 1.1 copy-start
  73.8 16.1 %copy-start.1 = (bf16[4,96,1024]{2,1,0:T(8,128)(2,1)S(1)}, bf16[4,96,1024]{2,1,0:T(8,128)(2,1)}, u32[]{:S(2)}) copy-start(bf16[4,96,1024]{2,1,0:T(8,128)(2,1)} %get-tuple-element.12) | copy-start | bytes 2359300
  73.8 2.6 %collective-permute-start.7 = (bf16[4,96,1024]{2,1,0:T(8,128)(2,1)}, bf16[4,96,1024]{2,1,0:T(8,128)(2,1)S(1)}, u32[]{:S(2)}, u32[]{:S(2)}) collective-permute-start(bf16[4,96,1024]{2,1,0:T(8,128)(2,1)} %get-tuple-element.15), channel_id=1, source_target_pairs={{0,8},{8,0},{16,24},{24,16},{1,9},{9,1},{17,25},{25,17},{2,10},{10... | collective-permute-start | bytes 2359304 | tf_op jit(solution)/shard_map/ppermute | solution.py:23
  73.9 6.0 %collective-permute-start.6 = (bf16[4,96,1024]{2,1,0:T(8,128)(2,1)}, bf16[4,96,1024]{2,1,0:T(8,128)(2,1)S(1)}, u32[]{:S(2)}, u32[]{:S(2)}) collective-permute-start(bf16[4,96,1024]{2,1,0:T(8,128)(2,1)} %get-tuple-element.13), channel_id=1, source_target_pairs={{0,8},{8,0},{16,24},{24,16},{1,9},{9,1},{17,25},{25,17},{2,10},{10... | collective-permute-start | bytes 2359304 | tf_op jit(solution)/shard_map/ppermute | solution.py:23
  77.8 7.8 %collective-permute-start.10 = (bf16[2,96,1024]{2,1,0:T(8,128)(2,1)S(1)}, bf16[2,96,1024]{2,1,0:T(8,128)(2,1)S(1)}, u32[]{:S(2)}, u32[]{:S(2)}) collective-permute-start(bf16[2,96,1024]{2,1,0:T(8,128)(2,1)S(1)} %get-tuple-element.18), channel_id=1, source_target_pairs={{0,1},{1,0},{2,3},{3,2},{4,5},{5,4},{6,7},{7,6},{8,24},{9,25},{10,... | collective-permute-start | bytes 1179656 | tf_op jit(solution)/shard_map/ppermute | solution.py:278
  79.3 10.5 %collective-permute-start.8 = (bf16[2,96,1024]{2,1,0:T(8,128)(2,1)S(1)}, bf16[2,96,1024]{2,1,0:T(8,128)(2,1)S(1)}, u32[]{:S(2)}, u32[]{:S(2)}) collective-permute-start(bf16[2,96,1024]{2,1,0:T(8,128)(2,1)S(1)} %get-tuple-element.19), channel_id=1, source_target_pairs={{0,1},{1,0},{2,3},{3,2},{4,5},{5,4},{6,7},{7,6},{8,24},{9,25},{10,... | collective-permute-start | bytes 1179656 | tf_op jit(solution)/shard_map/ppermute | solution.py:278
  90.3 5.7 %collective-permute-start.11 = (bf16[2,96,512]{2,1,0:T(8,128)(2,1)S(1)}, bf16[2,96,512]{2,1,0:T(8,128)(2,1)S(1)}, u32[]{:S(2)}, u32[]{:S(2)}) collective-permute-start(bf16[2,96,512]{2,1,0:T(8,128)(2,1)S(1)} %constant_dynamic-slice_fusion), channel_id=1, source_target_pairs={{0,16},{1,17},{2,18},{3,19},{4,20},{5,21},{6,22},{7,23},{8,9},{9,8... | collective-permute-start | bytes 589832 | tf_op jit(solution)/shard_map/ppermute | solution.py:278
  91.9 6.2 %collective-permute-start.9 = (bf16[2,96,512]{2,1,0:T(8,128)(2,1)S(1)}, bf16[2,96,512]{2,1,0:T(8,128)(2,1)S(1)}, u32[]{:S(2)}, u32[]{:S(2)}) collective-permute-start(bf16[2,96,512]{2,1,0:T(8,128)(2,1)S(1)} %constant_dynamic-slice_fusion.1), channel_id=1, source_target_pairs={{0,16},{1,17},{2,18},{3,19},{4,20},{5,21},{6,22},{7,23},{8,9},{9,8... | collective-permute-start | bytes 589832 | tf_op jit(solution)/shard_map/ppermute | solution.py:278
  98.4 5.2 %collective-permute-start.12 = (bf16[96,512]{1,0:T(8,128)(2,1)S(1)}, bf16[96,512]{1,0:T(8,128)(2,1)S(1)}, u32[]{:S(2)}, u32[]{:S(2)}) collective-permute-start(bf16[96,512]{1,0:T(8,128)(2,1)S(1)} %get-tuple-element.30), channel_id=1, source_target_pairs={{0,2},{1,3},{2,0},{3,1},{4,6},{5,7},{6,4},{7,5},{8,10},{9,11},{10,... | collective-permute-start | bytes 294920 | tf_op jit(solution)/shard_map/ppermute | solution.py:23
  98.4 9.5 %collective-permute-start.13 = (bf16[96,512]{1,0:T(8,128)(2,1)S(1)}, bf16[96,512]{1,0:T(8,128)(2,1)S(1)}, u32[]{:S(2)}, u32[]{:S(2)}) collective-permute-start(bf16[96,512]{1,0:T(8,128)(2,1)S(1)} %get-tuple-element.31), channel_id=1, source_target_pairs={{0,4},{1,5},{2,6},{3,7},{4,0},{5,1},{6,2},{7,3},{8,12},{9,13},{10,... | collective-permute-start | bytes 294920 | tf_op jit(solution)/shard_map/ppermute | solution.py:23
  102.6 6.5 %collective-permute-start.14 = (bf16[96,512]{1,0:T(8,128)(2,1)S(1)}, bf16[96,512]{1,0:T(8,128)(2,1)S(1)}, u32[]{:S(2)}, u32[]{:S(2)}) collective-permute-start(bf16[96,512]{1,0:T(8,128)(2,1)S(1)} %get-tuple-element.32), channel_id=1, source_target_pairs={{0,6},{1,7},{2,4},{3,5},{4,2},{5,3},{6,0},{7,1},{8,14},{9,15},{10,... | collective-permute-start | bytes 294920 | tf_op jit(solution)/shard_map/ppermute | solution.py:23
  109.3 4.7 %collective-permute-start.15 = (bf16[96,512]{1,0:T(8,128)(2,1)S(1)}, bf16[96,512]{1,0:T(8,128)(2,1)S(1)}, u32[]{:S(2)}, u32[]{:S(2)}) collective-permute-start(bf16[96,512]{1,0:T(8,128)(2,1)S(1)} %fusion.5), channel_id=1, source_target_pairs={{0,16},{8,24},{16,0},{24,8},{1,17},{9,25},{17,1},{25,9},{2,18},{10... | collective-permute-start | bytes 294920 | tf_op jit(solution)/shard_map/ppermute | solution.py:23
  114.0 1.5 %collective-permute-start.16 = (bf16[96,1024]{1,0:T(8,128)(2,1)S(1)}, bf16[96,1024]{1,0:T(8,128)(2,1)S(1)}, u32[]{:S(2)}, u32[]{:S(2)}) collective-permute-start(bf16[96,1024]{1,0:T(8,128)(2,1)S(1)} %pad_maximum_fusion.4), channel_id=1, source_target_pairs={{0,8},{8,0},{16,24},{24,16},{1,9},{9,1},{17,25},{25,17},{2,10},{10... | collective-permute-start | bytes 589832 | tf_op jit(solution)/shard_map/ppermute | solution.py:23
